TPU v7x, 32 devices: a whole 2x2x4 slice. The times are simulated.
32 devices in a mesh: fsdp: 4 (over z), ctx: 2 (over x), tp: 4 (over y, core).
Axes of the slice: x: 2, y: 2, z: 4, core: 2. Of those that a mesh axis runs over, the one named last changes fastest.
Arguments:
- tokens: bfloat16 [8192, 2048], P(('fsdp', 'ctx')), may hold values from -6 to 6
- q_weight: bfloat16 [2048, 2048], P('fsdp', 'tp'), may hold values from -0.25 to 0.25
- k_weight: bfloat16 [2048, 512], P('fsdp', 'tp'), may hold values from -0.125 to 0.125
- v_weight: bfloat16 [2048, 512], P('fsdp', 'tp'), may hold values from -0.125 to 0.125
- o_weight: bfloat16 [2048, 2048], P('fsdp', 'tp'), may hold values from -0.5 to 0.5
- attn_gain: bfloat16 [2048], P('fsdp'), may hold values from 0.099609375 to 1.8984375
- gate_weight: bfloat16 [2048, 8192], P('fsdp', 'tp'), may hold values from -0.125 to 0.125
- up_weight: bfloat16 [2048, 8192], P('fsdp', 'tp'), may hold values from -0.125 to 0.125
- down_weight: bfloat16 [2048, 8192], P('fsdp', 'tp'), may hold values from -0.125 to 0.125
- ffn_gain: bfloat16 [2048], P('fsdp'), may hold values from 0.099609375 to 1.8984375
- lengths: int32 [4, 6], P('fsdp'), may hold values from 1 to 1024, as said below
- deal: int32 [4, 4], P('fsdp'), may hold values from 0 to 3, as said below
- cotangent: bfloat16 [8192, 2048], P(('fsdp', 'ctx')), may hold values from -6 to 6
Outputs:
- output: bfloat16 [8192, 2048], P(('fsdp', 'ctx'))
- tokens_grad: bfloat16 [8192, 2048], P(('fsdp', 'ctx'))
- q_grad: float32 [2048, 2048], P('fsdp', 'tp')
- k_grad: float32 [2048, 512], P('fsdp', 'tp')
- v_grad: float32 [2048, 512], P('fsdp', 'tp')
- o_grad: float32 [2048, 2048], P('fsdp', 'tp')
- attn_gain_grad: float32 [2048], P('fsdp')
- gate_grad: float32 [2048, 8192], P('fsdp', 'tp')
- up_grad: float32 [2048, 8192], P('fsdp', 'tp')
- down_grad: float32 [2048, 8192], P('fsdp', 'tp')
- ffn_gain_grad: float32 [2048], P('fsdp')
Inputs may be any that keep to these rules, and one draw needn't show every extreme that they name: Each group's lengths add up to 2048, so that no row is padding; exactly one of them equals 1024, and it is the first or the last of the group's list. `deal`: each row is a permutation of the group's 4 spans; for each c, places 2c and 2c+1 hold one span of the first half and one of the second half of the packed order.
All inputs are finite; a program needn't handle non-finite values.
Results may differ from a plain program's by a relative error of at most 0.025.
Values may be sent and summed in bfloat16 or wider, within the bound.
No kernel may reach another device: no remote copies, remote signals or barrier semaphores. Data moves between devices by JAX's collectives and lax.ppermute only.
A program may use at most 448 MiB of HBM per device.

v0:
```python
import math

import jax
import jax.numpy as jnp
from jax import lax
from jax.sharding import PartitionSpec as P

HEAD_DIM = 64


EPSILON = 1e-05
ROPE_BASE = 500000.0
MASKED = -1e30


def rms_scale(hidden, gain_row):
    mean_square = jnp.mean(hidden * hidden, axis=-1, keepdims=True)
    return hidden * lax.rsqrt(mean_square + EPSILON) * gain_row


def rotate(values, cos_table, sin_table):
    half_dim = values.shape[-1] // 2
    turned = jnp.concatenate([-values[..., half_dim:], values[..., :half_dim]], axis=-1)
    return values * cos_table + turned * sin_table


def angle_tables(position, head_dim):
    half_dim = head_dim // 2
    inverse = jnp.exp(
        jnp.arange(half_dim, dtype=jnp.float32) * (-2.0 * math.log(ROPE_BASE) / head_dim)
    )
    angles = position.astype(jnp.float32)[:, None] * inverse[None, :]
    both_halves = jnp.concatenate([angles, angles], axis=-1)[:, None, :]
    return (jnp.cos(both_halves), jnp.sin(both_halves))


def token_places(length_row, deal_row, span_size):
    natural = (
        deal_row[:, None] * span_size + jnp.arange(span_size, dtype=jnp.int32)[None, :]
    ).reshape(-1)
    seq_ends = jnp.cumsum(length_row, dtype=jnp.int32)
    seq_starts = seq_ends - length_row
    segment = jnp.sum(
        (natural[None, :] >= seq_ends[:, None]).astype(jnp.int32), axis=0, dtype=jnp.int32
    )
    member = segment[None, :] == jnp.arange(length_row.shape[0], dtype=jnp.int32)[:, None]
    position = natural - jnp.sum(jnp.where(member, seq_starts[:, None], 0), axis=0, dtype=jnp.int32)
    return (natural, segment, position)


def block_mask(segment_rows, natural_rows, segment_all, natural_all):
    return (segment_rows[:, None] == segment_all[None, :]) & (
        natural_all[None, :] <= natural_rows[:, None]
    )


def masked_scores(query_block, key_head, allowed, score_scale):
    raw_scores = (
        jnp.einsum("qgd,kd->gqk", query_block, key_head, preferred_element_type=jnp.float32)
        * score_scale
    )
    return jnp.where(allowed[None], raw_scores, MASKED)


def spread_shards(grads):
    return (
        lax.psum_scatter(
            grads[0].astype(jnp.bfloat16), "fsdp", scatter_dimension=0, tiled=True
        ).astype(jnp.float32),
        lax.psum_scatter(
            grads[1].astype(jnp.bfloat16), "fsdp", scatter_dimension=0, tiled=True
        ).astype(jnp.float32),
        lax.psum_scatter(
            grads[2].astype(jnp.bfloat16), "fsdp", scatter_dimension=0, tiled=True
        ).astype(jnp.float32),
        lax.psum_scatter(
            grads[3].astype(jnp.bfloat16), "fsdp", scatter_dimension=0, tiled=True
        ).astype(jnp.float32),
        lax.psum_scatter(
            grads[4].astype(jnp.bfloat16), "fsdp", scatter_dimension=0, tiled=True
        ).astype(jnp.float32),
        lax.psum_scatter(
            grads[5].astype(jnp.bfloat16), "fsdp", scatter_dimension=0, tiled=True
        ).astype(jnp.float32),
        lax.psum_scatter(
            grads[6].astype(jnp.bfloat16), "fsdp", scatter_dimension=0, tiled=True
        ).astype(jnp.float32),
        lax.psum_scatter(
            grads[7].astype(jnp.bfloat16), "fsdp", scatter_dimension=0, tiled=True
        ).astype(jnp.float32),
        lax.psum_scatter(
            grads[8].astype(jnp.bfloat16), "fsdp", scatter_dimension=0, tiled=True
        ).astype(jnp.float32),
    )


def shards(
    tokens,
    q_weight,
    k_weight,
    v_weight,
    o_weight,
    attn_gain,
    gate_weight,
    up_weight,
    down_weight,
    ffn_gain,
    lengths,
    deal,
    cotangent,
):
    q_full, k_full, v_full, o_full, gain_one = (
        lax.all_gather(q_weight, "fsdp", axis=0, tiled=True),
        lax.all_gather(k_weight, "fsdp", axis=0, tiled=True),
        lax.all_gather(v_weight, "fsdp", axis=0, tiled=True),
        lax.all_gather(o_weight, "fsdp", axis=0, tiled=True),
        lax.all_gather(attn_gain, "fsdp", axis=0, tiled=True),
    )
    gate_full, up_full, down_full, gain_two = (
        lax.all_gather(gate_weight, "fsdp", axis=0, tiled=True),
        lax.all_gather(up_weight, "fsdp", axis=0, tiled=True),
        lax.all_gather(down_weight, "fsdp", axis=0, tiled=True),
        lax.all_gather(ffn_gain, "fsdp", axis=0, tiled=True),
    )
    gain_one = gain_one.astype(jnp.float32)
    gain_two = gain_two.astype(jnp.float32)
    row_count = tokens.shape[0]
    ctx_count = lax.axis_size("ctx")
    group_size = row_count * ctx_count
    natural_all, segment_all, position_all = token_places(lengths[0], deal[0], row_count // 2)
    row_start = lax.axis_index("ctx") * row_count
    natural_own = lax.dynamic_slice_in_dim(natural_all, row_start, row_count, 0)
    segment_own = lax.dynamic_slice_in_dim(segment_all, row_start, row_count, 0)
    position_own = lax.dynamic_slice_in_dim(position_all, row_start, row_count, 0)
    head_dim = HEAD_DIM
    kv_local = k_full.shape[1] // head_dim
    q_local = q_full.shape[1] // head_dim
    per_kv = q_local // kv_local
    score_scale = head_dim ** (-0.5)
    cos_table, sin_table = angle_tables(position_own, head_dim)
    inputs = tokens.astype(jnp.float32)
    normed, norm_pull = jax.vjp(rms_scale, inputs, gain_one)
    normed_low = normed.astype(jnp.bfloat16)
    q_raw = jnp.dot(normed_low, q_full, preferred_element_type=jnp.float32).reshape(
        row_count, q_local, head_dim
    )
    k_raw = jnp.dot(normed_low, k_full, preferred_element_type=jnp.float32).reshape(
        row_count, kv_local, head_dim
    )
    v_raw = jnp.dot(normed_low, v_full, preferred_element_type=jnp.float32)
    q_turned, q_pull = jax.vjp(lambda values: rotate(values, cos_table, sin_table), q_raw)
    k_turned, k_pull = jax.vjp(lambda values: rotate(values, cos_table, sin_table), k_raw)
    q_low = q_turned.astype(jnp.bfloat16).reshape(row_count, kv_local, per_kv, head_dim)
    k_low = k_turned.astype(jnp.bfloat16).reshape(row_count, kv_local * head_dim)
    v_low = v_raw.astype(jnp.bfloat16)
    k_group, v_group = (
        lax.all_gather(k_low, "ctx", axis=0, tiled=True),
        lax.all_gather(v_low, "ctx", axis=0, tiled=True),
    )
    k_group = k_group.reshape(group_size, kv_local, head_dim)
    v_group = v_group.reshape(group_size, kv_local, head_dim)
    block_rows = min(512, row_count)
    block_count = row_count // block_rows
    outputs = []
    kept = []
    for block_index in range(block_count):
        first_row = block_index * block_rows
        allowed = block_mask(
            segment_own[first_row : first_row + block_rows],
            natural_own[first_row : first_row + block_rows],
            segment_all,
            natural_all,
        )
        head_outs = []
        for kv_index in range(kv_local):
            query_block = q_low[first_row : first_row + block_rows, kv_index]
            scores = masked_scores(query_block, k_group[:, kv_index], allowed, score_scale)
            row_top = jnp.max(scores, axis=-1, keepdims=True)
            exp_scores = jnp.exp(scores - row_top)
            row_total = jnp.sum(exp_scores, axis=-1, keepdims=True)
            probs_low = (exp_scores / row_total).astype(jnp.bfloat16)
            head_outs.append(
                jnp.einsum(
                    "gqk,kd->qgd",
                    probs_low,
                    v_group[:, kv_index],
                    preferred_element_type=jnp.float32,
                )
            )
            kept.append((row_top, row_total))
        outputs.append(jnp.stack(head_outs, axis=1))
    heads_low = (
        jnp.concatenate(outputs, axis=0).reshape(row_count, q_local * head_dim).astype(jnp.bfloat16)
    )
    attn_part = jnp.einsum("re,de->rd", heads_low, o_full, preferred_element_type=jnp.float32)
    attn_total = lax.psum(attn_part.astype(jnp.bfloat16), "tp").astype(jnp.float32)
    hidden_one = inputs + attn_total
    normed_two, norm_two_pull = jax.vjp(rms_scale, hidden_one, gain_two)
    normed_two_low = normed_two.astype(jnp.bfloat16)
    gate_raw = jnp.dot(normed_two_low, gate_full, preferred_element_type=jnp.float32)
    up_raw = jnp.dot(normed_two_low, up_full, preferred_element_type=jnp.float32)
    mixed, glu_pull = jax.vjp(
        lambda gate_val, up_val: jax.nn.silu(gate_val) * up_val, gate_raw, up_raw
    )
    mixed_low = mixed.astype(jnp.bfloat16)
    ffn_part = jnp.einsum("rf,df->rd", mixed_low, down_full, preferred_element_type=jnp.float32)
    ffn_total = lax.psum(ffn_part.astype(jnp.bfloat16), "tp").astype(jnp.float32)
    result = (hidden_one + ffn_total).astype(jnp.bfloat16)
    cot_float = cotangent.astype(jnp.float32)
    d_mixed = jnp.dot(cotangent, down_full, preferred_element_type=jnp.float32)
    grad_down = jnp.einsum("rd,rf->df", cotangent, mixed_low, preferred_element_type=jnp.float32)
    d_gate, d_up = glu_pull(d_mixed)
    d_gate_low = d_gate.astype(jnp.bfloat16)
    d_up_low = d_up.astype(jnp.bfloat16)
    grad_gate = jnp.einsum(
        "rd,rf->df", normed_two_low, d_gate_low, preferred_element_type=jnp.float32
    )
    grad_up = jnp.einsum("rd,rf->df", normed_two_low, d_up_low, preferred_element_type=jnp.float32)
    d_norm_part = jnp.einsum("rf,df->rd", d_gate_low, gate_full, preferred_element_type=jnp.float32)
    d_norm_part = d_norm_part + jnp.einsum(
        "rf,df->rd", d_up_low, up_full, preferred_element_type=jnp.float32
    )
    d_normed_two = lax.psum(d_norm_part.astype(jnp.bfloat16), "tp").astype(jnp.float32)
    d_hidden_part, grad_gain_two = norm_two_pull(d_normed_two)
    d_hidden_one = cot_float + d_hidden_part
    d_attn_low = d_hidden_one.astype(jnp.bfloat16)
    grad_out = jnp.einsum("rd,re->de", d_attn_low, heads_low, preferred_element_type=jnp.float32)
    d_heads_low = jnp.dot(d_attn_low, o_full, preferred_element_type=jnp.float32).astype(
        jnp.bfloat16
    )
    d_heads_low = d_heads_low.reshape(row_count, kv_local, per_kv, head_dim)
    q_grad_parts = [[None] * kv_local for block_index in range(block_count)]
    key_sums = []
    value_sums = []
    for kv_index in range(kv_local):
        key_acc = jnp.zeros((group_size, head_dim), jnp.float32)
        value_acc = jnp.zeros((group_size, head_dim), jnp.float32)
        for block_index in range(block_count):
            first_row = block_index * block_rows
            allowed = block_mask(
                segment_own[first_row : first_row + block_rows],
                natural_own[first_row : first_row + block_rows],
                segment_all,
                natural_all,
            )
            query_block = q_low[first_row : first_row + block_rows, kv_index]
            scores = masked_scores(query_block, k_group[:, kv_index], allowed, score_scale)
            row_top, row_total = kept[block_index * kv_local + kv_index]
            probs = jnp.exp(scores - row_top) / row_total
            probs_low = probs.astype(jnp.bfloat16)
            d_out_block = d_heads_low[first_row : first_row + block_rows, kv_index]
            d_probs = jnp.einsum(
                "qgd,kd->gqk", d_out_block, v_group[:, kv_index], preferred_element_type=jnp.float32
            )
            d_scores = probs * (d_probs - jnp.sum(probs * d_probs, axis=-1, keepdims=True))
            d_scores_low = d_scores.astype(jnp.bfloat16)
            q_grad_parts[block_index][kv_index] = (
                jnp.einsum(
                    "gqk,kd->qgd",
                    d_scores_low,
                    k_group[:, kv_index],
                    preferred_element_type=jnp.float32,
                )
                * score_scale
            )
            key_acc = (
                key_acc
                + jnp.einsum(
                    "gqk,qgd->kd", d_scores_low, query_block, preferred_element_type=jnp.float32
                )
                * score_scale
            )
            value_acc = value_acc + jnp.einsum(
                "gqk,qgd->kd", probs_low, d_out_block, preferred_element_type=jnp.float32
            )
        key_sums.append(key_acc)
        value_sums.append(value_acc)
    key_grad_all = jnp.stack(key_sums, axis=1).reshape(group_size, kv_local * head_dim)
    value_grad_all = jnp.stack(value_sums, axis=1).reshape(group_size, kv_local * head_dim)
    key_own, value_own = (
        lax.psum_scatter(
            key_grad_all.astype(jnp.bfloat16), "ctx", scatter_dimension=0, tiled=True
        ).astype(jnp.float32),
        lax.psum_scatter(
            value_grad_all.astype(jnp.bfloat16), "ctx", scatter_dimension=0, tiled=True
        ).astype(jnp.float32),
    )
    q_turn_grad = jnp.concatenate(
        [jnp.stack(parts, axis=1) for parts in q_grad_parts], axis=0
    ).reshape(row_count, q_local, head_dim)
    d_q_low = q_pull(q_turn_grad)[0].reshape(row_count, q_local * head_dim).astype(jnp.bfloat16)
    d_k_low = (
        k_pull(key_own.reshape(row_count, kv_local, head_dim))[0]
        .reshape(row_count, kv_local * head_dim)
        .astype(jnp.bfloat16)
    )
    d_v_low = value_own.astype(jnp.bfloat16)
    grad_q = jnp.einsum("rd,re->de", normed_low, d_q_low, preferred_element_type=jnp.float32)
    grad_k = jnp.einsum("rd,re->de", normed_low, d_k_low, preferred_element_type=jnp.float32)
    grad_v = jnp.einsum("rd,re->de", normed_low, d_v_low, preferred_element_type=jnp.float32)
    d_in_part = jnp.einsum("re,de->rd", d_q_low, q_full, preferred_element_type=jnp.float32)
    d_in_part = d_in_part + jnp.einsum(
        "re,de->rd", d_k_low, k_full, preferred_element_type=jnp.float32
    )
    d_in_part = d_in_part + jnp.einsum(
        "re,de->rd", d_v_low, v_full, preferred_element_type=jnp.float32
    )
    d_normed = lax.psum(d_in_part.astype(jnp.bfloat16), "tp").astype(jnp.float32)
    d_input_part, grad_gain_one = norm_pull(d_normed)
    tokens_grad = (d_hidden_one + d_input_part).astype(jnp.bfloat16)
    grads = (
        grad_q,
        grad_k,
        grad_v,
        grad_out,
        grad_gain_one,
        grad_gate,
        grad_up,
        grad_down,
        grad_gain_two,
    )
    shares = spread_shards(grads)
    final = (
        lax.psum(shares[0].astype(jnp.bfloat16), "ctx").astype(jnp.float32),
        lax.psum(shares[1].astype(jnp.bfloat16), "ctx").astype(jnp.float32),
        lax.psum(shares[2].astype(jnp.bfloat16), "ctx").astype(jnp.float32),
        lax.psum(shares[3].astype(jnp.bfloat16), "ctx").astype(jnp.float32),
        lax.psum(shares[4].astype(jnp.bfloat16), "ctx").astype(jnp.float32),
        lax.psum(shares[5].astype(jnp.bfloat16), "ctx").astype(jnp.float32),
        lax.psum(shares[6].astype(jnp.bfloat16), "ctx").astype(jnp.float32),
        lax.psum(shares[7].astype(jnp.bfloat16), "ctx").astype(jnp.float32),
        lax.psum(shares[8].astype(jnp.bfloat16), "ctx").astype(jnp.float32),
    )
    return (
        result,
        tokens_grad,
        final[0],
        final[1],
        final[2],
        final[3],
        final[4],
        final[5],
        final[6],
        final[7],
        final[8],
    )


def solution(mesh):
    placed = (
        P(("fsdp", "ctx"), None),
        P("fsdp", "tp"),
        P("fsdp", "tp"),
        P("fsdp", "tp"),
        P("fsdp", "tp"),
        P("fsdp"),
        P("fsdp", "tp"),
        P("fsdp", "tp"),
        P("fsdp", "tp"),
        P("fsdp"),
        P("fsdp", None),
        P("fsdp", None),
        P(("fsdp", "ctx"), None),
    )
    return jax.shard_map(
        shards,
        mesh=mesh,
        in_specs=placed,
        out_specs=(
            P(("fsdp", "ctx"), None),
            P(("fsdp", "ctx"), None),
            P("fsdp", "tp"),
            P("fsdp", "tp"),
            P("fsdp", "tp"),
            P("fsdp", "tp"),
            P("fsdp"),
            P("fsdp", "tp"),
            P("fsdp", "tp"),
            P("fsdp", "tp"),
            P("fsdp"),
        ),
        check_vma=False,
    )
```

profile of v0, /device:TPU:0, one launch (start us, length us, event | category | flops | bytes accessed | tf_op | source)
XLA Modules:
  0.0 1954.1 jit_solution(14107071406199729156)
XLA Ops:
  16.2 13.8 all-gather
  30.0 21.6 %all_gather.36 = bf16[2048,128]{1,0:T(8,128)(2,1)S(1)} all-gather(bf16[512,128]{1,0:T(8,128)(2,1)} %param.15), channel_id=1, replica_groups=mesh['fsdp'=4,'ctx'=2,'tp'=4] {'fsdp'}, dimensions={0}, use_global_device_ids=true | all-gather | bytes 655360 | tf_op jit(solution)/shard_map/all_gather | solution.py:114
  54.5 7.0 all_gather.37
  61.6 16.9 all_gather.34
  80.5 7.6 all_gather.35
  98.3 10.6 fusion.182
  108.9 10.2 fusion.181
  119.2 9.3 fusion.180
  128.5 7.5 fusion.147
  136.0 8.2 fusion.144
  146.8 9.3 fusion.179
  156.1 7.4 fusion.138
  171.9 11.9 all-gather.1
  183.8 70.5 %all-reduce.15.cloned.1.call-done = bf16[1024,2048]{1,0:T(8,128)(2,1)} async-done(((bf16[1024,2048]{1,0:T(8,128)(2,1)}), bf16[1024,2048]{1,0:T(8,128)(2,1)}) %all-reduce.15.cloned.1.call-update) | async-done | bytes 4194320 | tf_op jit(solution)/shard_map/psum | solution.py:196
  264.5 141.1 %all-gather.12.cloned.1.call-done = bf16[2048,2048]{1,0:T(8,128)(2,1)} async-done(((bf16[512,2048]{1,0:T(8,128)(2,1)}), bf16[2048,2048]{1,0:T(8,128)(2,1)}) %all-gather.12.cloned.1.call-update) | async-done | bytes 8388624 | tf_op jit(solution)/shard_map/all_gather | solution.py:120
  405.6 14.5 fusion.185
  420.2 134.8 %all-gather.14.cloned.1.call-done = bf16[2048,2048]{1,0:T(8,128)(2,1)} async-done(((bf16[512,2048]{1,0:T(8,128)(2,1)}), bf16[2048,2048]{1,0:T(8,128)(2,1)}) %all-gather.14.cloned.1.call-update) | async-done | bytes 8388624 | tf_op jit(solution)/shard_map/all_gather | solution.py:121
  555.0 14.6 fusion.186
  569.6 134.8 %all-gather.16.cloned.1.call-done = bf16[2048,2048]{1,0:T(8,128)(2,1)} async-done(((bf16[512,2048]{1,0:T(8,128)(2,1)}), bf16[2048,2048]{1,0:T(8,128)(2,1)}) %all-gather.16.cloned.1.call-update) | async-done | bytes 8388624 | tf_op jit(solution)/shard_map/all_gather | solution.py:122
  704.4 21.6 %multiply_convert_fusion = (bf16[1024,2048]{1,0:T(8,128)(2,1)S(1)}, bf16[1024,2048]{1,0:T(8,128)(2,1)}, bf16[1024,2048]{1,0:T(8,128)(2,1)}) fusion(f32[1024,2048]{1,0:T(8,128)} %fusion.185, f32[1024,2048]{1,0:T(8,128)} %fusion.186, bf16[1024,2048]{1,0:T(8,128)(2,1)} %param.25, bf16[2048,2048]{1,0:T(8,128)(2,1)} %all-gather.16.cloned.1.call-done), kind=kOutput, calls=%fused_computation.67 | convolution fusion | flops 8623489024 | bytes 41943040 | tf_op jit(solution)/shard_map/dot_general | solution.py:210
  726.1 16.2 fusion.187
  742.3 12.3 add_convert_fusion.1
  754.6 83.8 %all-reduce.17.cloned.1.call-done = bf16[1024,2048]{1,0:T(8,128)(2,1)} async-done(((bf16[1024,2048]{1,0:T(8,128)(2,1)}), bf16[1024,2048]{1,0:T(8,128)(2,1)}) %all-reduce.17.cloned.1.call-update) | async-done | bytes 4194320 | tf_op jit(solution)/shard_map/psum | solution.py:223
  838.4 8.6 fusion.26
  857.2 9.2 fusion.69
  866.4 9.4 fusion.72
  875.8 13.1 fusion.13
  889.8 7.4 fusion.7
  897.2 10.6 fusion.10
  907.7 10.6 fusion.4
  918.4 11.6 fusion.15
  937.1 8.4 fusion.97
  946.4 12.2 fusion.12
  961.2 11.6 fusion.9
  975.4 11.6 fusion.6
  1024.1 7.3 convolution_convert_fusion.4
  1031.5 14.1 convolution_convert_fusion.1
  1045.9 14.1 convolution_convert_fusion
  1060.0 14.1 convert_bitcast_fusion
  1074.5 14.0 convolution_convert_fusion.2
  1101.5 45.6 %reduce-scatter.20.cloned.1.call-done = bf16[512,512]{1,0:T(8,128)(2,1)} async-done(((bf16[2048,512]{1,0:T(8,128)(2,1)}), bf16[512,512]{1,0:T(8,128)(2,1)}) %reduce-scatter.20.cloned.1.call-update) | async-done | bytes 524304 | tf_op jit(solution)/shard_map/reduce_scatter | solution.py:76
  1147.1 146.1 %reduce-scatter.22.cloned.1.call-done = bf16[512,2048]{1,0:T(8,128)(2,1)} async-done(((bf16[2048,2048]{1,0:T(8,128)(2,1)}), bf16[512,2048]{1,0:T(8,128)(2,1)}) %reduce-scatter.22.cloned.1.call-update) | async-done | bytes 2097168 | tf_op jit(solution)/shard_map/reduce_scatter | solution.py:82
  1293.2 147.4 %reduce-scatter.24.cloned.1.call-done = bf16[512,2048]{1,0:T(8,128)(2,1)} async-done(((bf16[2048,2048]{1,0:T(8,128)(2,1)}), bf16[512,2048]{1,0:T(8,128)(2,1)}) %reduce-scatter.24.cloned.1.call-update) | async-done | bytes 2097168 | tf_op jit(solution)/shard_map/reduce_scatter | solution.py:85
  1440.6 147.4 %reduce-scatter.26.cloned.1.call-done = bf16[512,2048]{0,1:T(8,128)(2,1)} async-done(((bf16[2048,2048]{0,1:T(8,128)(2,1)}), bf16[512,2048]{0,1:T(8,128)(2,1)}) %reduce-scatter.26.cloned.1.call-update) | async-done | bytes 2097168 | tf_op jit(solution)/shard_map/reduce_scatter | solution.py:88
  1589.3 155.7 %all-reduce.19.cloned.1.call-done = (bf16[1024,2048]{1,0:T(8,128)(2,1)}, bf16[1024,2048]{1,0:T(8,128)(2,1)}) async-done(((bf16[1024,2048]{1,0:T(8,128)(2,1)}, bf16[1024,2048]{1,0:T(8,128)(2,1)}), (bf16[1024,2048]{1,0:T(8,128)(2,1)}, bf16[1024,2048]{1,0:T(8,128)(2,1)})) %all-reduce.19.cloned.1.call-update) | async-done | bytes 8388624 | tf_op jit(solution)/shard_map/psum | solution.py:207
  1751.0 11.9 all-reduce.7
  1769.5 13.2 fusion.33
  1782.8 149.0 %all-reduce.21.cloned.1.call-done = (bf16[512,2048]{0,1:T(8,128)(2,1)}, bf16[512,512]{1,0:T(8,128)(2,1)}, bf16[512,128]{1,0:T(8,128)(2,1)}, bf16[512,128]{1,0:T(...) async-done(((bf16[512,2048]{0,1:T(8,128)(2,1)}, bf16[512,512]{1,0:T(8,128)(2,1)}, bf16[512,128]{1,0:T(8,128)(2,1)}, ...) | async-done | bytes 7602192 | tf_op jit(solution)/shard_map/psum | solution.py:331
  (268 shorter events, 147.8 us)
Async XLA Ops:
  7.2 85.1 %all-gather.8.cloned.1.call-start = ((), (), s32[]{:S(2)}) async-start(), calls=%async_computation.9 | async-start | bytes 2621440 | tf_op jit(solution)/shard_map/all_gather | solution.py:113
  7.9 155.8 %all-gather.10.cloned.1.call-start = ((), (), s32[]{:S(2)}) async-start(), calls=%async_computation.10 | async-start | bytes 2621440 | tf_op jit(solution)/shard_map/all_gather | solution.py:116
  8.7 245.7 %all-reduce.15.cloned.1.call-start = ((), (), s32[]{:S(2)}) async-start(), calls=%async_computation.11 | async-start | bytes 8388608 | tf_op jit(solution)/shard_map/psum | solution.py:196
  11.0 40.7 %copy-start = (bf16[1024,2048]{1,0:T(8,128)(2,1)S(1)}, bf16[1024,2048]{1,0:T(8,128)(2,1)}, u32[]{:S(2)}) copy-start(bf16[1024,2048]{1,0:T(8,128)(2,1)} %param.13) | copy-start | bytes 12582916
  11.1 43.2 %copy-start.41 = (s32[2048]{0:T(1024)}, s32[2048]{0:T(1024)S(1)}, u32[]{:S(2)}) copy-start(s32[2048]{0:T(1024)S(1)} %convert_reduce_fusion) | copy-start | bytes 24580
  12.2 85.5 %copy-start.10 = (f32[1024,64]{0,1:T(8,128)}, f32[1024,64]{0,1:T(8,128)S(1)}, u32[]{:S(2)}) copy-start(f32[1024,64]{0,1:T(8,128)S(1)} %get-tuple-element.88) | copy-start | bytes 786436
  12.2 85.5 %copy-start.12 = (f32[1024,64]{0,1:T(8,128)}, f32[1024,64]{0,1:T(8,128)S(1)}, u32[]{:S(2)}) copy-start(f32[1024,64]{0,1:T(8,128)S(1)} %get-tuple-element.87) | copy-start | bytes 786436
  15.5 38.8 %copy-start.45 = (f32[1024]{0:T(1024)}, f32[1024]{0:T(1024)S(1)}, u32[]{:S(2)}) copy-start(f32[1024]{0:T(1024)S(1)} %fusion.34) | copy-start | bytes 12292
  15.5 38.8 %copy-start.43 = (f32[1024]{0:T(1024)}, f32[1024]{0:T(1024)S(1)}, u32[]{:S(2)}) copy-start(f32[1024]{0:T(1024)S(1)} %fusion.165) | copy-start | bytes 12292
  30.0 24.5 %copy-start.39 = (f32[4,1,512]{2,1,0:T(1,128)}, f32[4,1,512]{2,1,0:T(1,128)S(1)}, u32[]{:S(2)}) copy-start(f32[4,1,512]{2,1,0:T(1,128)S(1)} %convert_element_type.270) | copy-start | bytes 24580
  52.7 27.9 %copy-start.7 = (bf16[1024,2048]{1,0:T(8,128)(2,1)}, bf16[1024,2048]{1,0:T(8,128)(2,1)S(1)}, u32[]{:S(2)}) copy-start(bf16[1024,2048]{1,0:T(8,128)(2,1)S(1)} %fusion.24) | copy-start | bytes 12582916
  54.2 34.9 %dynamic-slice-start = ((s32[2048]{0:T(1024)}, s32[]{:T(128)}), s32[1024]{0:T(1024)S(1)}, s32[]{:S(2)}) async-start(s32[2048]{0:T(1024)} %copy-done.41, s32[]{:T(128)} %select_n.26), calls=%async_computation.35 | async-start | bytes 8704 | tf_op jit(solution)/shard_map/dynamic_slice | solution.py:133
  54.2 34.9 %copy-start.42 = (s32[2048]{0:T(1024)S(1)}, s32[2048]{0:T(1024)}, u32[]{:S(2)}) copy-start(s32[2048]{0:T(1024)} %copy-done.41) | copy-start | bytes 24580
  61.6 85.2 %copy-start.16 = (bf16[2048,128]{0,1:T(8,128)(2,1)}, bf16[2048,128]{0,1:T(8,128)(2,1)S(1)}, u32[]{:S(2)}) copy-start(bf16[2048,128]{0,1:T(8,128)(2,1)S(1)} %all_gather.37) | copy-start | bytes 1572868
  98.3 48.4 %copy-start.18 = (bf16[1024,2,4,64]{0,3,2,1:T(8,128)(2,1)}, bf16[1024,2,4,64]{0,3,2,1:T(8,128)(2,1)S(1)}, u32[]{:S(2)}) copy-start(bf16[1024,2,4,64]{0,3,2,1:T(8,128)(2,1)S(1)} %fusion.104) | copy-start | bytes 3145732
  108.9 19.5 %copy-start.54 = (f32[4,512]{1,0:T(4,128)}, f32[4,512]{1,0:T(4,128)S(1)}, u32[]{:S(2)}) copy-start(f32[4,512]{1,0:T(4,128)S(1)} %get-tuple-element.101) | copy-start | bytes 24580
  119.1 16.9 copy-start.52
  128.5 15.8 copy-start.48
  128.5 15.8 slice-start
  128.5 15.7 slice-start.1
  170.1 235.5 %all-gather.12.cloned.1.call-start = ((), (), s32[]{:S(2)}) async-start(), calls=%async_computation.12 | async-start | bytes 10485760 | tf_op jit(solution)/shard_map/all_gather | solution.py:120
  170.7 384.3 %all-gather.14.cloned.1.call-start = ((), (), s32[]{:S(2)}) async-start(), calls=%async_computation.13 | async-start | bytes 10485760 | tf_op jit(solution)/shard_map/all_gather | solution.py:121
  171.3 533.2 %all-gather.16.cloned.1.call-start = ((), (), s32[]{:S(2)}) async-start(), calls=%async_computation.14 | async-start | bytes 10485760 | tf_op jit(solution)/shard_map/all_gather | solution.py:122
  171.9 666.6 %all-reduce.17.cloned.1.call-start = ((), (), s32[]{:S(2)}) async-start(), calls=%async_computation.15 | async-start | bytes 8388608 | tf_op jit(solution)/shard_map/psum | solution.py:223
  726.1 16.2 copy-start.61
  726.1 16.2 copy-start.57
  754.6 247.5 %reduce-scatter.12.cloned.1.call-start = ((), (), s32[]{:S(2)}) async-start(), calls=%async_computation.17 | async-start | bytes 786432 | tf_op jit(solution)/shard_map/reduce_scatter | solution.py:284
  866.4 22.5 %slice-start.4 = ((s8[16777216]{0:T(1024)(128)(4,1)}), s8[4194304]{0:T(1024)(128)(4,1)S(1)}, s32[]{:S(2)}) async-start(s8[16777216]{0:T(1024)(128)(4,1)} %bitcast.401), calls=%async_computation.31 | async-start | bytes 8388608
  866.4 22.5 %slice-start.5 = ((s8[16777216]{0:T(1024)(128)(4,1)}), s8[4194304]{0:T(1024)(128)(4,1)S(1)}, s32[]{:S(2)}) async-start(s8[16777216]{0:T(1024)(128)(4,1)} %bitcast.401), calls=%async_computation.32 | async-start | bytes 8388608
  875.8 14.0 slice-start.7
  875.8 14.0 copy-start.49
  946.4 63.7 %reduce-scatter.10.cloned.1.call-start = ((), (), s32[]{:S(2)}) async-start(), calls=%async_computation.16 | async-start | bytes 786432 | tf_op jit(solution)/shard_map/reduce_scatter | solution.py:281
  995.2 100.5 %reduce-scatter.18.cloned.1.call-start = ((), (), s32[]{:S(2)}) async-start(), calls=%async_computation.20 | async-start | bytes 655360 | tf_op jit(solution)/shard_map/reduce_scatter | solution.py:73
  1006.4 89.3 %reduce-scatter.16.cloned.1.call-start = ((), (), s32[]{:S(2)}) async-start(), calls=%async_computation.19 | async-start | bytes 655360 | tf_op jit(solution)/shard_map/reduce_scatter | solution.py:70
  1016.5 85.1 %reduce-scatter.14.cloned.1.call-start = ((), (), s32[]{:S(2)}) async-start(), calls=%async_computation.18 | async-start | bytes 2621440 | tf_op jit(solution)/shard_map/reduce_scatter | solution.py:67
  1024.1 123.0 %reduce-scatter.20.cloned.1.call-start = ((), (), s32[]{:S(2)}) async-start(), calls=%async_computation.21 | async-start | bytes 2621440 | tf_op jit(solution)/shard_map/reduce_scatter | solution.py:76
  1031.4 261.8 %reduce-scatter.22.cloned.1.call-start = ((), (), s32[]{:S(2)}) async-start(), calls=%async_computation.22 | async-start | bytes 10485760 | tf_op jit(solution)/shard_map/reduce_scatter | solution.py:82
  1045.6 394.9 %reduce-scatter.24.cloned.1.call-start = ((), (), s32[]{:S(2)}) async-start(), calls=%async_computation.23 | async-start | bytes 10485760 | tf_op jit(solution)/shard_map/reduce_scatter | solution.py:85
  1060.0 528.0 %reduce-scatter.26.cloned.1.call-start = ((), (), s32[]{:S(2)}) async-start(), calls=%async_computation.24 | async-start | bytes 10485760 | tf_op jit(solution)/shard_map/reduce_scatter | solution.py:88
  1074.2 14.4 copy-start.28
  1074.2 670.9 %all-reduce.19.cloned.1.call-start = ((), (), s32[]{:S(2)}) async-start(), calls=%async_computation.25 | async-start | bytes 16777216 | tf_op jit(solution)/shard_map/psum | solution.py:207
  1074.5 14.1 copy-start.58
  1095.6 492.5 %copy-start.60 = (u32[32]{0:T(128)S(1)}, u32[32]{0:T(128)}, u32[]{:S(2)}) copy-start(u32[32]{0:T(128)} %constant.54) | copy-start | bytes 388
  1095.6 649.5 %copy-start.40 = (f32[4,1,512]{2,1,0:T(1,128)S(1)}, f32[4,1,512]{2,1,0:T(1,128)}, u32[]{:S(2)}) copy-start(f32[4,1,512]{2,1,0:T(1,128)} %copy-done.39) | copy-start | bytes 24580
  1095.6 649.5 %copy-start.44 = (f32[1024]{0:T(1024)S(1)}, f32[1024]{0:T(1024)}, u32[]{:S(2)}) copy-start(f32[1024]{0:T(1024)} %copy-done.43) | copy-start | bytes 12292
  1095.6 655.3 %copy-start.47 = (bf16[2048]{0:T(1024)(128)(2,1)S(1)}, bf16[2048]{0:T(1024)(128)(2,1)}, u32[]{:S(2)}) copy-start(bf16[2048]{0:T(1024)(128)(2,1)} %get-tuple-element.55) | copy-start | bytes 12292
  1095.6 673.9 %copy-start.46 = (f32[1024]{0:T(1024)S(1)}, f32[1024]{0:T(1024)}, u32[]{:S(2)}) copy-start(f32[1024]{0:T(1024)} %copy-done.45) | copy-start | bytes 12292
  1095.6 836.2 %all-reduce.21.cloned.1.call-start = ((), (), s32[]{:S(2)}) async-start(), calls=%async_computation.26 | async-start | bytes 15204352 | tf_op jit(solution)/shard_map/psum | solution.py:331
  (43 other events, 276.5 us)
Sparse Core Ops, SparseCore 0:
  9.6 60.1 all-gather.7
  71.3 44.2 all-gather.9
  170.2 84.0 all-reduce.14
  255.8 149.7 all-gather.11
  407.1 147.8 all-gather.13
  556.5 147.8 all-gather.15
  754.7 83.7 all-reduce.16
  946.5 14.6 reduce-scatter.11
  995.3 14.7 reduce-scatter.9
  1012.2 21.6 reduce-scatter.17
  1036.7 19.8 reduce-scatter.15
  1059.4 42.1 reduce-scatter.13
  1103.9 43.1 reduce-scatter.19
  1149.3 143.8 reduce-scatter.21
  1295.4 145.1 reduce-scatter.23
  1442.8 145.1 reduce-scatter.25
  1591.0 153.9 all-reduce.18
  1747.9 183.8 all-reduce.20
where the time goes:
time: 1960 us; the launch traced here: 1950 us
  waiting for transfers between devices  1370 us (70%)
  matrix products  337 us (17%)
  other arithmetic  124 us (6%)
  blocking collectives  96 us (5%)
    psum x1, waiting for transfers between devices, shards(): lax.psum(ffn_part.astype(jnp.bfloat16), 'tp').astype(jnp.float32)  156 us
    psum x1, waiting for transfers between devices, shards(): lax.psum(shares[7].astype(jnp.bfloat16), 'ctx').astype(jnp.float32)  149 us
    reduce_scatter x1, waiting for transfers between devices, spread_shards(): lax.psum_scatter(grads[7].astype(jnp.bfloat16), 'fsdp', scatter_dimension...  147 us
    reduce_scatter x1, waiting for transfers between devices, spread_shards(): lax.psum_scatter(grads[6].astype(jnp.bfloat16), 'fsdp', scatter_dimension...  147 us
    reduce_scatter x1, waiting for transfers between devices, spread_shards(): lax.psum_scatter(grads[5].astype(jnp.bfloat16), 'fsdp', scatter_dimension...  146 us
    all_gather x1, waiting for transfers between devices, shards(): lax.all_gather(gate_weight, 'fsdp', axis=0, tiled=True)  141 us
    all_gather x1, waiting for transfers between devices, shards(): lax.all_gather(up_weight, 'fsdp', axis=0, tiled=True)  135 us
    all_gather x1, waiting for transfers between devices, shards(): lax.all_gather(down_weight, 'fsdp', axis=0, tiled=True)  135 us
  transfers between devices with their start and end apart: 18, of which 13 were waited for; matrix products, arithmetic and copies ran while one was open for 15% of the time, Pallas kernels for 0%

commit v1 on v0

v1 whole, which is shorter than its diff:
```python
import functools
import math

import jax
import jax.numpy as jnp
from jax import lax
from jax.experimental import pallas as pl
from jax.experimental.pallas import tpu as pltpu
from jax.sharding import PartitionSpec as P

HEAD_DIM = 64
EPSILON = 1e-05
ROPE_BASE = 500000.0
MASKED = -1e30
LOG2_E = 1.4426950408889634
BLOCK = 256
CHUNKS = 2
VMEM = 56 * 2**20

F32 = jnp.float32
BF16 = jnp.bfloat16

PAIR = [(0, 1), (1, 0)]
CORE = [(0, 1), (1, 0), (2, 3), (3, 2)]
ACROSS = [(0, 2), (2, 0), (1, 3), (3, 1)]


def joint_pairs(x_core):
    pairs = []
    for ctx in range(2):
        for tp in range(4):
            there = (1 - ctx) * 4 + tp if tp % 2 == x_core else ctx * 4 + (tp ^ 2)
            pairs.append((ctx * 4 + tp, there))
    return pairs


FIRST = joint_pairs(0)
SECOND = joint_pairs(1)


def swap_core(v):
    return lax.ppermute(v, "tp", CORE)


def swap_y(v):
    return lax.ppermute(v, "tp", ACROSS)


def swap_x(v):
    return lax.ppermute(v, "ctx", PAIR)


def swap_first(v):
    return lax.ppermute(v, ("ctx", "tp"), FIRST)


def swap_second(v):
    return lax.ppermute(v, ("ctx", "tp"), SECOND)


def after(value, *others):
    return lax.optimization_barrier((value,) + others)[0]


def params(*semantics):
    return pltpu.CompilerParams(vmem_limit_bytes=VMEM)


def cost(flops, read, exps=0):
    return pl.CostEstimate(flops=int(flops), bytes_accessed=int(read), transcendentals=int(exps))


def inv_rms(hidden):
    return lax.rsqrt(jnp.mean(hidden * hidden, axis=-1, keepdims=True) + EPSILON)


def rms_back(hidden, gain, grad):
    scale = inv_rms(hidden)
    weighted = grad * gain
    inner = jnp.mean(weighted * hidden, axis=-1, keepdims=True)
    return scale * weighted - hidden * (scale * scale * scale) * inner


def turn_lanes(u, first):
    return jnp.where(first, pltpu.roll(u, 96, 1), pltpu.roll(u, 32, 1))


def two_halves(step, width, halves):
    return [
        pl.BlockSpec((step, width), lambda i: (jnp.minimum(i, halves - 1), 0)),
        pl.BlockSpec((step, width), lambda i: (jnp.maximum(i - halves, 0), 0)),
    ]


def either(halves, body, low_refs, high_refs):
    @pl.when(pl.program_id(0) < halves)
    def _():
        body(*low_refs)

    @pl.when(pl.program_id(0) >= halves)
    def _():
        body(*high_refs)


def qkv_kernel(halves, low_ref, high_ref, wq_ref, wkv_ref, cos_ref, sin_ref, o_ref):
    cos, sin = cos_ref[...], sin_ref[...]
    lane = lax.broadcasted_iota(jnp.int32, cos.shape, 1)
    first = (lane % 64) < 32

    def body(x_ref):
        x = x_ref[...]
        raw = jnp.dot(x, wq_ref[...], preferred_element_type=F32)
        tiles = raw.shape[1] // 128
        for tile in range(tiles):
            u = raw[:, tile * 128 : (tile + 1) * 128]
            turned = u * cos + turn_lanes(u, first) * sin
            o_ref[:, tile * 128 : (tile + 1) * 128] = turned.astype(BF16)
        u = jnp.dot(x, wkv_ref[...], preferred_element_type=F32)
        turned = u * cos + turn_lanes(u, first) * sin
        o_ref[:, tiles * 128 :] = jnp.where(lane < 64, turned, u).astype(BF16)

    either(halves, body, (low_ref,), (high_ref,))


def project_qkv(x, w, q_width, cos, sin):
    half_rows, depth = x[0].shape
    rows = 2 * half_rows
    width = q_width + 128
    step = min(512, half_rows)
    return pl.pallas_call(
        functools.partial(qkv_kernel, half_rows // step),
        out_shape=jax.ShapeDtypeStruct((rows, width), BF16),
        grid=(rows // step,),
        in_specs=two_halves(step, depth, half_rows // step)
        + [
            pl.BlockSpec((depth, q_width), lambda i: (0, 1)),
            pl.BlockSpec((depth, 128), lambda i: (0, 2 * q_width // 128)),
            pl.BlockSpec((step, 128), lambda i: (i, 0)),
            pl.BlockSpec((step, 128), lambda i: (i, 0)),
        ],
        out_specs=pl.BlockSpec((step, width), lambda i: (i, 0)),
        compiler_params=params(),
        cost_estimate=cost(2 * rows * depth * width, 2 * (rows * depth + depth * width)),
        name="qkv",
    )(*x, w, w, cos, sin)


def ffn_kernel(halves, xl_ref, xh_ref, cl_ref, ch_ref, w_ref, o_ref):
    n = w_ref.shape[1] // 3

    def body(x_ref, c_ref):
        x = x_ref[...]
        gate = jnp.dot(x, w_ref[:, :n], preferred_element_type=F32)
        up = jnp.dot(x, w_ref[:, n : 2 * n], preferred_element_type=F32)
        d_mixed = jnp.dot(c_ref[...], w_ref[:, 2 * n :], preferred_element_type=F32)
        sig = 1.0 / (1.0 + jnp.exp(-gate))
        silu = gate * sig
        o_ref[:, :n] = (d_mixed * up * (sig * (1.0 + gate * (1.0 - sig)))).astype(BF16)
        o_ref[:, n : 2 * n] = (d_mixed * silu).astype(BF16)
        o_ref[:, 2 * n :] = (silu * up).astype(BF16)

    either(halves, body, (xl_ref, cl_ref), (xh_ref, ch_ref))


def ffn_chunk(x, cot, w):
    half_rows, depth = x[0].shape
    rows = 2 * half_rows
    width = w.shape[1]
    step = min(512, half_rows)
    halves = half_rows // step
    return pl.pallas_call(
        functools.partial(ffn_kernel, halves),
        out_shape=jax.ShapeDtypeStruct((rows, width), BF16),
        grid=(rows // step,),
        in_specs=two_halves(step, depth, halves)
        + two_halves(step, depth, halves)
        + [pl.BlockSpec((depth, width), lambda i: (0, 0))],
        out_specs=pl.BlockSpec((step, width), lambda i: (i, 0)),
        compiler_params=params(),
        cost_estimate=cost(2 * rows * depth * width, 4 * rows * depth + 4 * depth * width),
        name="ffn",
    )(*x, *cot, w)


DOWN = (((0,), (0,)), ((), ()))


def grads_kernel(split, xl_ref, xh_ref, yl_ref, yh_ref, a_ref, b_ref, o_ref):
    half_rows = xl_ref.shape[0]

    def both(low_ref, high_ref, right_ref, columns):
        low = right_ref[:half_rows, columns].astype(BF16)
        high = right_ref[half_rows:, columns].astype(BF16)
        total = lax.dot_general(low_ref[...], low, DOWN, preferred_element_type=F32)
        return total + lax.dot_general(high_ref[...], high, DOWN, preferred_element_type=F32)

    o_ref[:, :split] = both(xl_ref, xh_ref, a_ref, slice(None)).astype(BF16)
    o_ref[:, split:] = both(yl_ref, yh_ref, b_ref, slice(None)).astype(BF16)


def weight_grads(x, a, a_width, a_column, y, b, b_width, b_column):
    half_rows, depth = x[0].shape
    rows = 2 * half_rows
    width = a_width + b_width
    step = 512
    tall = pl.BlockSpec((half_rows, step), lambda i: (0, i))
    return pl.pallas_call(
        functools.partial(grads_kernel, a_width),
        out_shape=jax.ShapeDtypeStruct((depth, width), BF16),
        grid=(depth // step,),
        in_specs=[tall] * 4
        + [
            pl.BlockSpec((rows, a_width), lambda i: (0, a_column)),
            pl.BlockSpec((rows, b_width), lambda i: (0, b_column)),
        ],
        out_specs=pl.BlockSpec((step, width), lambda i: (i, 0)),
        compiler_params=params(),
        cost_estimate=cost(2 * rows * depth * width, 4 * rows * depth + 4 * depth * width),
        name="weight_grads",
    )(*x, *y, a, b)


def back_kernel(*refs):
    o_ref = refs[-1]
    count = (len(refs) - 1) // 2
    total = None
    for part in range(count):
        term = lax.dot_general(
            refs[part][...].astype(BF16),
            refs[count + part][...],
            (((1,), (1,)), ((), ())),
            preferred_element_type=F32,
        )
        total = term if total is None else total + term
    o_ref[...] = total.astype(BF16)


def back_product(terms):
    rows = terms[0][0].shape[0]
    depth = terms[0][2].shape[0]
    step = 512
    total = sum(term[4] for term in terms)
    return pl.pallas_call(
        back_kernel,
        out_shape=jax.ShapeDtypeStruct((rows, depth), BF16),
        grid=(rows // step,),
        in_specs=[
            pl.BlockSpec((step, term[4]), lambda i, column=term[1]: (i, column)) for term in terms
        ]
        + [pl.BlockSpec((depth, term[4]), lambda i, column=term[3]: (0, column)) for term in terms],
        out_specs=pl.BlockSpec((step, depth), lambda i: (i, 0)),
        compiler_params=params(),
        cost_estimate=cost(2 * rows * depth * total, 2 * rows * depth),
        name="back",
    )(*[term[0] for term in terms], *[term[2] for term in terms])


def front_kernel(halves, low_ref, high_ref, w_ref, o_ref):
    def body(x_ref):
        o_ref[...] = jnp.dot(x_ref[...], w_ref[...], preferred_element_type=F32).astype(BF16)

    either(halves, body, (low_ref,), (high_ref,))


def front_product(x, w, width, column):
    half_rows, depth = x[0].shape
    rows = 2 * half_rows
    step = min(512, half_rows)
    halves = half_rows // step
    return pl.pallas_call(
        functools.partial(front_kernel, halves),
        out_shape=jax.ShapeDtypeStruct((rows, width), BF16),
        grid=(rows // step,),
        in_specs=two_halves(step, depth, halves)
        + [pl.BlockSpec((depth, width), lambda i: (0, column))],
        out_specs=pl.BlockSpec((step, width), lambda i: (i, 0)),
        compiler_params=params(),
        cost_estimate=cost(2 * rows * depth * width, 2 * rows * depth),
        name="front",
    )(*x, w)


def stack_heads(block):
    count = block.shape[1] // HEAD_DIM
    return jnp.concatenate(
        [block[:, h * HEAD_DIM : (h + 1) * HEAD_DIM] for h in range(count)], axis=0
    )


def unstack_heads(stacked):
    count = stacked.shape[0] // BLOCK
    return jnp.concatenate([stacked[h * BLOCK : (h + 1) * BLOCK] for h in range(count)], axis=1)


def allowed_of(i, j, start):
    row = i * BLOCK + lax.broadcasted_iota(jnp.int32, (BLOCK, BLOCK), 0)
    col = j * BLOCK + lax.broadcasted_iota(jnp.int32, (BLOCK, BLOCK), 1)
    return (col <= row) & (col >= start)


def attend_kernel(place, first, q_ref, kv_ref, start_ref, o_ref):
    i = pl.program_id(0)
    q = stack_heads(q_ref[...])
    heads = q.shape[0] // BLOCK
    start = start_ref[...]

    def step(j, carry):
        top, total, acc = carry
        at = pl.multiple_of(place[j] * BLOCK, BLOCK)
        kv = kv_ref[pl.ds(at, BLOCK), :]
        raw = lax.dot_general(
            q, kv[:, :HEAD_DIM], (((1,), (1,)), ((), ())), preferred_element_type=F32
        ) * (HEAD_DIM**-0.5 * LOG2_E)
        allowed = allowed_of(i, j, start)
        scores = jnp.where(allowed[None], raw.reshape(heads, BLOCK, BLOCK), MASKED).reshape(
            heads * BLOCK, BLOCK
        )
        new_top = jnp.maximum(top, jnp.max(scores, axis=-1, keepdims=True))
        keep = jnp.exp2(top - new_top)
        probs = jnp.exp2(scores - new_top)
        total = total * keep + jnp.sum(probs, axis=-1, keepdims=True)
        acc = acc * keep + jnp.dot(probs.astype(BF16), kv, preferred_element_type=F32)
        return (new_top, total, acc)

    size = heads * BLOCK
    top, total, acc = lax.fori_loop(
        first[i],
        i + 1,
        step,
        (
            jnp.full((size, 1), MASKED, F32),
            jnp.zeros((size, 1), F32),
            jnp.zeros((size, 2 * HEAD_DIM), F32),
        ),
    )
    out = acc[:, HEAD_DIM:] / total
    q_width = q_ref.shape[1]
    o_ref[:, :q_width] = unstack_heads(out)
    lse = top + jnp.log2(total)
    lane = lax.broadcasted_iota(jnp.int32, (BLOCK, 128), 1)
    packed = jnp.zeros((BLOCK, 128), F32)
    for h in range(heads):
        packed = jnp.where(lane == h, lse[h * BLOCK : (h + 1) * BLOCK], packed)
    o_ref[:, q_width:] = packed


def attend(qkv, place, first, start, q_width):
    rows = qkv.shape[0]
    blocks = rows // BLOCK
    return pl.pallas_call(
        attend_kernel,
        out_shape=jax.ShapeDtypeStruct((rows, q_width + 128), F32),
        grid_spec=pltpu.PrefetchScalarGridSpec(
            num_scalar_prefetch=2,
            grid=(blocks,),
            in_specs=[
                pl.BlockSpec((BLOCK, q_width), lambda i, place, first: (place[i], 0)),
                pl.BlockSpec((rows, 128), lambda i, place, first: (0, q_width // 128)),
                pl.BlockSpec((BLOCK, 1), lambda i, place, first: (i, 0)),
            ],
            out_specs=pl.BlockSpec((BLOCK, q_width + 128), lambda i, place, first: (place[i], 0)),
        ),
        compiler_params=params(),
        cost_estimate=cost(16e9, 4e6, rows * 1024 * 4),
        name="attend",
    )(place, first, qkv, qkv, start)


def attend_back_kernel(
    place,
    first,
    q_ref,
    d_ref,
    h_ref,
    kv_ref,
    start_ref,
    cos_ref,
    sin_ref,
    o_ref,
    dkv_ref,
):
    i = pl.program_id(0)
    blocks = pl.num_programs(0)
    score_scale = HEAD_DIM**-0.5
    q_width = q_ref.shape[1]

    @pl.when(i == 0)
    def _():
        dkv_ref[...] = jnp.zeros_like(dkv_ref)

    q = stack_heads(q_ref[...])
    d_out = stack_heads(d_ref[...])
    heads = q.shape[0] // BLOCK
    out = stack_heads(h_ref[:, :q_width])
    delta = jnp.sum(d_out.astype(F32) * out, axis=-1, keepdims=True)
    lse_block = h_ref[:, q_width:]
    lse = jnp.concatenate([lse_block[:, h : h + 1] for h in range(heads)], axis=0)
    start = start_ref[...]

    def step(j, d_q):
        at = pl.multiple_of(place[j] * BLOCK, BLOCK)
        kv = kv_ref[pl.ds(at, BLOCK), :]
        k, v = kv[:, :HEAD_DIM], kv[:, HEAD_DIM:]
        across = (((1,), (1,)), ((), ()))
        down = (((0,), (0,)), ((), ()))
        raw = lax.dot_general(q, k, across, preferred_element_type=F32) * (score_scale * LOG2_E)
        allowed = allowed_of(i, j, start)
        scores = jnp.where(allowed[None], raw.reshape(heads, BLOCK, BLOCK), MASKED).reshape(
            heads * BLOCK, BLOCK
        )
        probs = jnp.exp2(scores - lse)
        d_probs = lax.dot_general(d_out, v, across, preferred_element_type=F32)
        d_scores = (probs * (d_probs - delta)).astype(BF16)
        d_k = lax.dot_general(d_scores, q, down, preferred_element_type=F32) * score_scale
        d_v = lax.dot_general(probs.astype(BF16), d_out, down, preferred_element_type=F32)
        here = pl.ds(pl.multiple_of(j * BLOCK, BLOCK), BLOCK)
        dkv_ref[here, :] += jnp.concatenate([d_k, d_v], axis=1)
        return d_q + jnp.dot(d_scores, k, preferred_element_type=F32)

    d_q = lax.fori_loop(first[i], i + 1, step, jnp.zeros((heads * BLOCK, HEAD_DIM), F32))
    d_q = unstack_heads(d_q * score_scale)
    lane = lax.broadcasted_iota(jnp.int32, (BLOCK, 128), 1)
    front = (lane % 64) < 32
    mine = pl.ds(pl.multiple_of(place[i] * BLOCK, BLOCK), BLOCK)
    cos, sin = cos_ref[mine, :], sin_ref[mine, :]
    for tile in range(q_width // 128):
        u = d_q[:, tile * 128 : (tile + 1) * 128]
        o_ref[mine, tile * 128 : (tile + 1) * 128] = (u * cos - turn_lanes(u, front) * sin).astype(
            BF16
        )

    @pl.when(i == blocks - 1)
    def _():
        for b in range(dkv_ref.shape[0] // BLOCK):
            there = pl.ds(pl.multiple_of(place[b] * BLOCK, BLOCK), BLOCK)
            u = dkv_ref[b * BLOCK : (b + 1) * BLOCK, :]
            turned = u * cos_ref[there, :] - turn_lanes(u, front) * sin_ref[there, :]
            o_ref[there, q_width:] = jnp.where(lane < HEAD_DIM, turned, u).astype(BF16)


def attend_back(qkv, d_heads, heads, place, first, start, cos, sin):
    rows, width = qkv.shape
    q_width = d_heads.shape[1]
    blocks = rows // BLOCK
    by_place = lambda i, place, first: (place[i], 0)
    whole = lambda i, place, first: (0, 0)
    return pl.pallas_call(
        attend_back_kernel,
        out_shape=jax.ShapeDtypeStruct((rows, width), BF16),
        grid_spec=pltpu.PrefetchScalarGridSpec(
            num_scalar_prefetch=2,
            grid=(blocks,),
            in_specs=[
                pl.BlockSpec((BLOCK, q_width), by_place),
                pl.BlockSpec((BLOCK, q_width), by_place),
                pl.BlockSpec((BLOCK, q_width + 128), by_place),
                pl.BlockSpec((rows, 128), lambda i, place, first: (0, q_width // 128)),
                pl.BlockSpec((BLOCK, 1), lambda i, place, first: (i, 0)),
                pl.BlockSpec((rows, 128), whole),
                pl.BlockSpec((rows, 128), whole),
            ],
            out_specs=pl.BlockSpec((rows, width), whole),
            scratch_shapes=[pltpu.VMEM((rows, 128), F32)],
        ),
        compiler_params=params(),
        cost_estimate=cost(40e9, 6e6, rows * 1024 * 4),
        name="attend_back",
    )(place, first, qkv, d_heads, heads, qkv, start, cos, sin)


def sum_to_owner(part):
    rows = part.shape[0] // 8
    arrived = swap_core(part[4 * rows :])
    arrived = part[2 * rows : 4 * rows] + arrived[2 * rows :], part[: 2 * rows] + arrived[: 2 * rows]
    pair = arrived[1] + swap_second(arrived[0])
    return pair[:rows].astype(F32) + swap_first(pair[rows:]).astype(F32)


def share_rows(own):
    two = jnp.concatenate([own, swap_first(own)])
    four = jnp.concatenate([two, swap_second(two)])
    return four, swap_core(four)


def share_in_ctx(own, y, core):
    pair = jnp.stack([own, swap_y(own)])
    four = jnp.stack([pair, swap_core(pair)])
    four = jnp.where(y == 1, four[:, ::-1], four)
    four = jnp.where(core == 1, four[::-1], four)
    return four.transpose(1, 0, 2, 3).reshape(-1, own.shape[1])


def sum_all(v):
    v = v + swap_core(v)
    v = v + swap_y(v)
    return v + swap_x(v)


def both_halves(own, other, ctx):
    low = jnp.where(ctx == 0, own, other).astype(F32)
    high = jnp.where(ctx == 0, other, own).astype(F32)
    return low, high


def shards(
    tokens,
    q_weight,
    k_weight,
    v_weight,
    o_weight,
    attn_gain,
    gate_weight,
    up_weight,
    down_weight,
    ffn_gain,
    lengths,
    deal,
    cotangent,
):
    ctx = lax.axis_index("ctx")
    tp = lax.axis_index("tp")
    y, core = tp // 2, tp % 2
    row_count, depth = tokens.shape
    group_rows = row_count * lax.axis_size("ctx")
    own_rows = row_count // lax.axis_size("tp")

    def half(weight):
        width = weight.shape[1] // 2
        return lax.dynamic_slice_in_dim(weight, ctx * width, width, 1)

    q_half, k_half, v_half, o_half = map(half, (q_weight, k_weight, v_weight, o_weight))
    q_width, kv_width = q_half.shape[1], k_half.shape[1]
    attn_shard = jnp.concatenate([o_half, q_half, k_half, v_half], axis=1)
    attn_full = lax.all_gather(attn_shard, "fsdp", axis=0, tiled=True)
    gains = lax.all_gather(jnp.stack([attn_gain, ffn_gain]), "fsdp", axis=1, tiled=True)
    gain_one = gains[0].astype(F32)[None]
    gain_two = gains[1].astype(F32)[None]
    ff_half = gate_weight.shape[1] // 2
    chunk = ff_half // CHUNKS
    ffn_shards = []
    for part in range(CHUNKS):
        at = ctx * ff_half + part * chunk
        ffn_shards.append(
            jnp.concatenate(
                [
                    lax.dynamic_slice_in_dim(weight, at, chunk, 1)
                    for weight in (gate_weight, up_weight, down_weight)
                ],
                axis=1,
            )
        )
    ffn_full = []
    before = attn_full
    for part in range(CHUNKS):
        before = lax.all_gather(after(ffn_shards[part], before), "fsdp", axis=0, tiled=True)
        ffn_full.append(before)

    length_row, deal_row = lengths[0], deal[0]
    spans = deal_row.shape[0]
    span_rows = group_rows // spans
    ends = jnp.cumsum(length_row, dtype=jnp.int32)
    starts = ends - length_row
    natural = jnp.arange(group_rows, dtype=jnp.int32)
    inside = (natural[:, None] >= starts[None]) & (natural[:, None] < ends[None])
    start_of = jnp.sum(jnp.where(inside, starts[None], 0), axis=1, dtype=jnp.int32)
    first = start_of[::BLOCK] // BLOCK
    rel = jnp.arange(group_rows // own_rows, dtype=jnp.int32)
    rel_core = core ^ (rel // 4)
    by_first, by_second = rel % 2, (rel // 2) % 2
    rel_ctx = ctx ^ jnp.where(rel_core == 0, by_first, by_second)
    rel_y = y ^ jnp.where(rel_core == 0, by_second, by_first)
    dealt_block = rel_ctx * (row_count // own_rows) + rel_y * 2 + rel_core
    per_span = span_rows // own_rows
    span_of = jnp.sum(
        jnp.where(
            (dealt_block // per_span)[:, None] == jnp.arange(spans, dtype=jnp.int32)[None],
            deal_row[None],
            0,
        ),
        axis=1,
        dtype=jnp.int32,
    )
    natural_block = span_of * per_span + dealt_block % per_span
    place = jnp.sum(
        jnp.where(natural_block[None, :] == rel[:, None], rel[None, :], 0), axis=1, dtype=jnp.int32
    )
    natural_rel = (
        natural_block[:, None] * own_rows + jnp.arange(own_rows, dtype=jnp.int32)[None]
    ).reshape(-1)
    inside_rel = (natural_rel[:, None] >= starts[None]) & (natural_rel[:, None] < ends[None])
    position = natural_rel - jnp.sum(
        jnp.where(inside_rel, starts[None], 0), axis=1, dtype=jnp.int32
    )
    lane = jnp.arange(128, dtype=jnp.int32)
    inverse = jnp.exp((lane % 32).astype(F32) * (-2.0 * math.log(ROPE_BASE) / HEAD_DIM))
    angles = position.astype(F32)[:, None] * inverse[None]
    cos = jnp.cos(angles)
    sin = jnp.where((lane % 64 < 32)[None], -jnp.sin(angles), jnp.sin(angles))
    start_column = start_of[:, None]

    tokens_own = lax.dynamic_slice_in_dim(tokens, tp * own_rows, own_rows, 0).astype(F32)
    cot_low = lax.dynamic_slice_in_dim(cotangent, tp * own_rows, own_rows, 0)
    cot_own = cot_low.astype(F32)
    normed = share_rows((tokens_own * inv_rms(tokens_own) * gain_one).astype(BF16))
    cot = share_rows(after(cot_low, normed[0]))
    qkv = project_qkv(normed, attn_full, q_width, cos, sin)
    heads = attend(qkv, place, first, start_column, q_width)
    heads = after(heads, *cot)
    attn_part = back_product([(heads, 0, attn_full, 0, q_width)])
    hidden = tokens_own + sum_to_owner(attn_part)
    normed_two = share_rows((hidden * inv_rms(hidden) * gain_two).astype(BF16))

    acts = []
    grad_parts = []
    for part in range(CHUNKS):
        acts.append(ffn_chunk(normed_two, cot, ffn_full[part]))
        grad_parts.append(
            weight_grads(normed_two, acts[part], 2 * chunk, 0, cot, acts[part], chunk, 2)
        )
    d_norm_part = back_product(
        [(acts[part], 0, ffn_full[part], 0, 2 * chunk) for part in range(CHUNKS)]
    )
    ffn_part = back_product([(acts[part], 2, ffn_full[part], 2, chunk) for part in range(CHUNKS)])
    d_normed_two = sum_to_owner(d_norm_part)
    d_hidden = cot_own + rms_back(hidden, gain_two, d_normed_two)
    d_attn = share_rows(d_hidden.astype(BF16))
    result_own = (hidden + sum_to_owner(ffn_part)).astype(BF16)
    result = share_in_ctx(result_own, y, core)

    d_heads = front_product(d_attn, attn_full, q_width, 0)
    d_qkv = attend_back(qkv, d_heads, heads, place, first, start_column, cos, sin)
    d_normed_part = back_product(
        [
            (d_qkv, 0, attn_full, 1, q_width),
            (d_qkv, q_width // 128, attn_full, 2 * q_width // 128, 128),
        ]
    )
    attn_grad = weight_grads(
        d_attn, heads, q_width, 0, normed, d_qkv, q_width + 128, 0
    )
    d_normed = sum_to_owner(d_normed_part)
    tokens_grad_own = (d_hidden + rms_back(tokens_own, gain_one, d_normed)).astype(BF16)
    tokens_grad = share_in_ctx(tokens_grad_own, y, core)

    reduced = [
        lax.psum_scatter(part, "fsdp", scatter_dimension=0, tiled=True) for part in grad_parts
    ]
    attn_reduced = lax.psum_scatter(attn_grad, "fsdp", scatter_dimension=0, tiled=True)

    def gain_grad(pairs, gain):
        products = sum(
            jnp.sum(mine.astype(F32) * grad.astype(F32), axis=1) for mine, grad in pairs
        )
        return sum_all(products) / gain.astype(F32)

    attn_gain_grad = gain_grad([(attn_shard[:, q_width:], attn_reduced[:, q_width:])], attn_gain)
    ffn_gain_grad = gain_grad(
        [
            (ffn_shards[part][:, : 2 * chunk], reduced[part][:, : 2 * chunk])
            for part in range(CHUNKS)
        ],
        ffn_gain,
    )

    other_reduced = [swap_x(part) for part in reduced]
    halves = [both_halves(mine, other, ctx) for mine, other in zip(reduced, other_reduced)]

    def ffn_out(which):
        return jnp.concatenate(
            [
                halves[part][side][:, which * chunk : (which + 1) * chunk]
                for side in range(2)
                for part in range(CHUNKS)
            ],
            axis=1,
        )

    attn_low, attn_high = both_halves(attn_reduced, swap_x(attn_reduced), ctx)

    def attn_out(begin, end):
        return jnp.concatenate([attn_low[:, begin:end], attn_high[:, begin:end]], axis=1)

    q_end, k_end = 2 * q_width, 2 * q_width + kv_width
    return (
        result,
        tokens_grad,
        attn_out(q_width, q_end),
        attn_out(q_end, k_end),
        attn_out(k_end, k_end + kv_width),
        attn_out(0, q_width),
        attn_gain_grad,
        ffn_out(0),
        ffn_out(1),
        ffn_out(2),
        ffn_gain_grad,
    )


def solution(mesh):
    rows = P(("fsdp", "ctx"), None)
    matrix = P("fsdp", "tp")
    vector = P("fsdp")
    return jax.shard_map(
        shards,
        mesh=mesh,
        in_specs=(
            rows,
            matrix,
            matrix,
            matrix,
            matrix,
            vector,
            matrix,
            matrix,
            matrix,
            vector,
            P("fsdp", None),
            P("fsdp", None),
            rows,
        ),
        out_specs=(
            rows,
            rows,
            matrix,
            matrix,
            matrix,
            matrix,
            vector,
            matrix,
            matrix,
            matrix,
            vector,
        ),
        check_vma=False,
    )
```

time: 1960 us -> 891 us (0.45)
  waiting for transfers between devices: 1370 us -> 453 us
  matrix products: 337 us -> 0 us
  Pallas kernels: 0 us -> 218 us
  blocking collectives: 96 us -> 13.5 us
  starting transfers between devices: 1.37 us -> 52.2 us
  other arithmetic: 124 us -> 86 us
  local copies, waits for them, and re-layouts: 10.1 us -> 46 us
    reduce_scatter x9 -> x3, waiting for transfers between devices: 496 us -> 32.9 us  [the longest x2 32.9 us: shards(): lax.psum_scatter(part, 'fsdp', scatter_dimension=0, tiled=True)]
    psum x4 -> x0, waiting for transfers between devices: 459 us -> none  [the longest x1 156 us: shards(): lax.psum(ffn_part.astype(jnp.bfloat16), 'tp').astype(jnp.float32)]
    ppermute x0 -> x37, waiting for transfers between devices: none -> 300 us  [the longest x8 148 us: swap_second(): return lax.ppermute(v, ('ctx', 'tp'), SECOND)]
    dot_general x41 -> x0, matrix products: 298 us -> none  [the longest x4 41.6 us: shards(): jnp.einsum('qgd,kd->gqk', d_out_block, v_group[:, kv_index], preferred_el...]
    all_gather x5 -> x3, waiting for transfers between devices: 411 us -> 119 us  [the longest x2 101 us: shards(): lax.all_gather(after(ffn_shards[part], before), 'fsdp', axis=0, tiled=True)]
    pallas_call x0 -> x13, Pallas kernels: none -> 218 us  [the longest x4 52.4 us: back_product(): pl.pallas_call(back_kernel, out_shape=jax.ShapeDtypeStruct((rows, depth),...]
    convert_element_type x22 -> x8, other arithmetic: 81 us -> 9.96 us  [the longest x1 3.98 us: shards(): d_attn = share_rows(d_hidden.astype(BF16))]
    all_gather x6 -> x1, blocking collectives: 78.7 us -> 13.5 us  [shards(): lax.all_gather(jnp.stack([attn_gain, ffn_gain]), 'fsdp', axis=1, tiled=True)]
  transfers between devices with their start and end apart: 18 -> 43, of which waited for: 13 -> 25; matrix products, arithmetic and copies ran while one was open for 15% -> 13% of each run, Pallas kernels for 0% -> 24%
where the time goes in v1:
time: 891 us; the launch traced here: 884 us
  waiting for transfers between devices  453 us (51%)
  Pallas kernels  218 us (24%)
  other arithmetic  86 us (10%)
  starting transfers between devices  52.2 us (6%)
  local copies, waits for them, and re-layouts  46 us (5%)
  between operations  15 us (2%)
  blocking collectives  13.5 us (2%)
    ppermute x8, waiting for transfers between devices, swap_second(): return lax.ppermute(v, ('ctx', 'tp'), SECOND)  148 us
    all_gather x2, waiting for transfers between devices, shards(): lax.all_gather(after(ffn_shards[part], before), 'fsdp', axis=0, tiled=True)  101 us
    ppermute x8, waiting for transfers between devices, swap_first(): return lax.ppermute(v, ('ctx', 'tp'), FIRST)  87.8 us
    pallas_call x4, Pallas kernels, back_product(): pl.pallas_call(back_kernel, out_shape=jax.ShapeDtypeStruct((rows, depth),...  52.4 us
    pallas_call x3, Pallas kernels, weight_grads(): pl.pallas_call(functools.partial(grads_kernel, a_width), out_shape=jax.Sh...  51.7 us
    ppermute x5, waiting for transfers between devices, swap_x(): return lax.ppermute(v, 'ctx', PAIR)  46.6 us
    pallas_call x2, Pallas kernels, ffn_chunk(): pl.pallas_call(functools.partial(ffn_kernel, halves), out_shape=jax.Shape...  41.2 us
    pallas_call x1, Pallas kernels, attend_back(): pl.pallas_call(attend_back_kernel, out_shape=jax.ShapeDtypeStruct((rows,...  33.7 us
  transfers between devices with their start and end apart: 43, of which 25 were waited for; matrix products, arithmetic and copies ran while one was open for 13% of the time, Pallas kernels for 24%

profile of v1, /device:TPU:0, one launch (start us, length us, event | category | flops | bytes accessed | tf_op | source)
XLA Modules:
  0.0 883.6 jit_solution(4093534275216609738)
XLA Ops:
  10.8 13.5 %all_gather.12 = bf16[2,2048]{1,0:T(2,128)(2,1)S(1)} all-gather(bf16[2,512]{1,0:T(2,128)(2,1)S(1)} %pad_maximum_fusion.21), channel_id=1, replica_groups=mesh['fsdp'=4,'ctx'=2,'tp'=4] {'fsdp'}, dimensions={1}, use_global_device_ids=true | all-gather | bytes 10240 | tf_op jit(solution)/shard_map/all_gather | solution.py:535
  27.4 13.9 %collective-permute-done = bf16[256,2048]{1,0:T(8,128)(2,1)S(1)} collective-permute-done((bf16[256,2048]{1,0:T(8,128)(2,1)S(1)}, bf16[256,2048]{1,0:T(8,128)(2,1)S(1)}, u32[]{:S(2)}, u32[]{:S(2)}) %collective-permute-start) | collective-permute-done | bytes 1048608 | tf_op jit(solution)/shard_map/ppermute | solution.py:54
  44.5 23.2 %collective-permute-done.1 = bf16[512,2048]{1,0:T(8,128)(2,1)S(1)} collective-permute-done((bf16[512,2048]{1,0:T(8,128)(2,1)S(1)}, bf16[512,2048]{1,0:T(8,128)(2,1)S(1)}, u32[]{:S(2)}, u32[]{:S(2)}) %collective-permute-start.1) | collective-permute-done | bytes 2097184 | tf_op jit(solution)/shard_map/ppermute | solution.py:58
  71.5 14.2 %collective-permute-done.3 = bf16[256,2048]{1,0:T(8,128)(2,1)S(1)} collective-permute-done((bf16[256,2048]{1,0:T(8,128)(2,1)S(1)}, bf16[256,2048]{1,0:T(8,128)(2,1)S(1)}, u32[]{:S(2)}, u32[]{:S(2)}) %collective-permute-start.3) | collective-permute-done | bytes 1048608 | tf_op jit(solution)/shard_map/ppermute | solution.py:54
  93.1 20.4 %collective-permute-done.4 = bf16[512,2048]{1,0:T(8,128)(2,1)} collective-permute-done((bf16[512,2048]{1,0:T(8,128)(2,1)}, bf16[512,2048]{1,0:T(8,128)(2,1)}, u32[]{:S(2)}, u32[]{:S(2)}) %collective-permute-start.4) | collective-permute-done | bytes 2097184 | tf_op jit(solution)/shard_map/ppermute | solution.py:58
  113.5 3.2 constant_dynamic-update-slice_fusion.cl_ref.yl_ref
  119.9 5.5 negate_select_fusion
  125.5 18.8 %all-gather.4.cloned.1.call-done.wq_ref.wkv_ref.refs_1_.w_ref.refs_2_.refs_3_ = bf16[2048,640]{1,0:T(8,128)(2,1)} async-done(((bf16[512,640]{1,0:T(8,128)(2,1)}), bf16[2048,640]{1,0:T(8,128)(2,1)}) %all-gather.4.cloned.1.call-update) | async-done | bytes 2621456 | tf_op jit(solution)/shard_map/all_gather | solution.py:534
  144.3 10.3 %qkv.1.q_ref.kv_ref = bf16[2048,384]{1,0:T(8,128)(2,1)} custom-call(bf16[1024,2048]{1,0:T(8,128)(2,1)} %pad_maximum_fusion.low_ref.yl_ref, bf16[1024,2048]{1,0:T(8,128)(2,1)} %collective-permute-done.2.high_ref.yh_ref, bf16[2048,640]{1,0:T(8,128)(2,1)} %all-gather.4.cloned.1.call-done.wq_ref.wkv_ref.refs_1_.w_ref.refs_2_.refs_3_, ...), custom_call_target="tpu_custom_call" | custom-call | flops 3221225472 | bytes 9961472 | tf_op jit(solution)/shard_map/qkv/pallas_call | solution.py:130
  154.6 21.8 %attend.1.refs_0_.h_ref.a_ref = f32[2048,384]{1,0:T(8,128)} custom-call(s32[8]{0:T(128)} %select_reduce_fusion.2.place, s32[8]{0:T(128)} %and_select_fusion.2.first, bf16[2048,384]{1,0:T(8,128)(2,1)} %qkv.1.q_ref.kv_ref, bf16[2048,384]{1,0:T(8,128)(2,1)} %qkv.1.q_ref.kv_ref, s32[2048,1]{1,0:T(8,128)} %copy.28.start_ref), custom_call_target="tpu_custom_call" | custom-call | flops 16000000000 | bytes 4000000 | tf_op jit(solution)/shard_map/attend/pallas_call | solution.py:350
  176.4 7.0 back.4
  183.4 4.8 slice.224
  199.7 24.6 %collective-permute-done.7 = bf16[512,2048]{1,0:T(8,128)(2,1)S(1)} collective-permute-done((bf16[512,2048]{1,0:T(8,128)(2,1)S(1)}, bf16[512,2048]{1,0:T(8,128)(2,1)S(1)}, u32[]{:S(2)}, u32[]{:S(2)}) %collective-permute-start.7) | collective-permute-done | bytes 2097184 | tf_op jit(solution)/shard_map/ppermute | solution.py:58
  228.4 13.3 %collective-permute-done.8 = bf16[256,2048]{1,0:T(8,128)(2,1)S(1)} collective-permute-done((bf16[256,2048]{1,0:T(8,128)(2,1)S(1)}, bf16[256,2048]{1,0:T(8,128)(2,1)S(1)}, u32[]{:S(2)}, u32[]{:S(2)}) %collective-permute-start.8) | collective-permute-done | bytes 1048608 | tf_op jit(solution)/shard_map/ppermute | solution.py:54
  247.4 63.5 %all-gather.6.cloned.1.call-done.w_ref.refs_2_ = bf16[2048,1536]{1,0:T(8,128)(2,1)} async-done(((bf16[512,1536]{1,0:T(8,128)(2,1)}), bf16[2048,1536]{1,0:T(8,128)(2,1)}) %all-gather.6.cloned.1.call-update) | async-done | bytes 6291472 | tf_op jit(solution)/shard_map/all_gather | solution.py:555
  314.9 24.6 %collective-permute-done.10 = bf16[512,2048]{1,0:T(8,128)(2,1)S(1)} collective-permute-done((bf16[512,2048]{1,0:T(8,128)(2,1)S(1)}, bf16[512,2048]{1,0:T(8,128)(2,1)S(1)}, u32[]{:S(2)}, u32[]{:S(2)}) %collective-permute-start.10) | collective-permute-done | bytes 2097184 | tf_op jit(solution)/shard_map/ppermute | solution.py:58
  341.4 7.3 collective-permute-done.11.xh_ref
  348.7 20.6 %ffn.2.refs_0_.a_ref.b_ref = bf16[2048,1536]{1,0:T(8,128)(2,1)} custom-call(bf16[1024,2048]{1,0:T(8,128)(2,1)} %copy-done.17, bf16[1024,2048]{1,0:T(8,128)(2,1)} %collective-permute-done.11.xh_ref, bf16[1024,2048]{1,0:T(8,128)(2,1)} %constant_dynamic-update-slice_fusion.cl_ref.yl_ref, bf16[1024,2048]{1,0:T(8,128)(2,1)} %collective-permute-done.5.ch_ref.yh_ref, ...), custom_call_target="tpu_custom_call" | custom-call | flops 12884901888 | bytes 29360128 | tf_op jit(solution)/shard_map/ffn/pallas_call | solution.py:171
  369.3 19.6 %weight_grads.4 = bf16[2048,1536]{1,0:T(8,128)(2,1)} custom-call(bf16[1024,2048]{1,0:T(8,128)(2,1)} %copy-done.17, bf16[1024,2048]{1,0:T(8,128)(2,1)} %collective-permute-done.11.xh_ref, bf16[1024,2048]{1,0:T(8,128)(2,1)} %constant_dynamic-update-slice_fusion.cl_ref.yl_ref, bf16[1024,2048]{1,0:T(8,128)(2,1)} %collective-permute-done.5.ch_ref.yh_ref, ...), custom_call_target="tpu_custom_call" | custom-call | flops 12884901888 | bytes 29360128 | tf_op jit(solution)/shard_map/weight_grads/pallas_call | solution.py:207
  389.1 37.1 %all-gather.8.cloned.1.call-done.w_ref.refs_3_ = bf16[2048,1536]{1,0:T(8,128)(2,1)} async-done(((bf16[512,1536]{1,0:T(8,128)(2,1)}), bf16[2048,1536]{1,0:T(8,128)(2,1)}) %all-gather.8.cloned.1.call-update) | async-done | bytes 6291472 | tf_op jit(solution)/shard_map/all_gather | solution.py:555
  426.2 20.6 %ffn.3.refs_1_.a_ref.b_ref = bf16[2048,1536]{1,0:T(8,128)(2,1)} custom-call(bf16[1024,2048]{1,0:T(8,128)(2,1)} %copy-done.17, bf16[1024,2048]{1,0:T(8,128)(2,1)} %collective-permute-done.11.xh_ref, bf16[1024,2048]{1,0:T(8,128)(2,1)} %constant_dynamic-update-slice_fusion.cl_ref.yl_ref, bf16[1024,2048]{1,0:T(8,128)(2,1)} %collective-permute-done.5.ch_ref.yh_ref, ...), custom_call_target="tpu_custom_call" | custom-call | flops 12884901888 | bytes 29360128 | tf_op jit(solution)/shard_map/ffn/pallas_call | solution.py:171
  446.8 23.7 %back.6 = bf16[2048,2048]{1,0:T(8,128)(2,1)} custom-call(bf16[2048,1536]{1,0:T(8,128)(2,1)} %ffn.2.refs_0_.a_ref.b_ref, bf16[2048,1536]{1,0:T(8,128)(2,1)} %ffn.3.refs_1_.a_ref.b_ref, bf16[2048,1536]{1,0:T(8,128)(2,1)} %all-gather.6.cloned.1.call-done.w_ref.refs_2_, bf16[2048,1536]{1,0:T(8,128)(2,1)} %all-gather.8.cloned.1.call-done.w_ref.refs_3_), custom_call_target="tpu_custom_call" | custom-call | flops 17179869184 | bytes 8388608 | tf_op jit(solution)/shard_map/back/pallas_call | solution.py:243
  470.5 4.8 slice.239
  475.3 13.7 %back.5 = bf16[2048,2048]{1,0:T(8,128)(2,1)} custom-call(bf16[2048,1536]{1,0:T(8,128)(2,1)} %ffn.2.refs_0_.a_ref.b_ref, bf16[2048,1536]{1,0:T(8,128)(2,1)} %ffn.3.refs_1_.a_ref.b_ref, bf16[2048,1536]{1,0:T(8,128)(2,1)} %all-gather.6.cloned.1.call-done.w_ref.refs_2_, bf16[2048,1536]{1,0:T(8,128)(2,1)} %all-gather.8.cloned.1.call-done.w_ref.refs_3_), custom_call_target="tpu_custom_call" | custom-call | flops 8589934592 | bytes 8388608 | tf_op jit(solution)/shard_map/back/pallas_call | solution.py:243
  489.0 2.7 slice.232
  496.2 2.8 collective-permute-done.12
  500.7 20.0 %collective-permute-done.18 = bf16[512,2048]{1,0:T(8,128)(2,1)S(1)} collective-permute-done((bf16[512,2048]{1,0:T(8,128)(2,1)S(1)}, bf16[512,2048]{1,0:T(8,128)(2,1)S(1)}, u32[]{:S(2)}, u32[]{:S(2)}) %collective-permute-start.18) | collective-permute-done | bytes 2097184 | tf_op jit(solution)/shard_map/ppermute | solution.py:58
  524.4 30.1 %collective-permute-done.13 = bf16[512,2048]{1,0:T(8,128)(2,1)S(1)} collective-permute-done((bf16[512,2048]{1,0:T(8,128)(2,1)S(1)}, bf16[512,2048]{1,0:T(8,128)(2,1)S(1)}, u32[]{:S(2)}, u32[]{:S(2)}) %collective-permute-start.13) | collective-permute-done | bytes 2097184 | tf_op jit(solution)/shard_map/ppermute | solution.py:58
  557.1 12.7 %collective-permute-done.14 = bf16[256,2048]{1,0:T(8,128)(2,1)S(1)} collective-permute-done((bf16[256,2048]{1,0:T(8,128)(2,1)S(1)}, bf16[256,2048]{1,0:T(8,128)(2,1)S(1)}, u32[]{:S(2)}, u32[]{:S(2)}) %collective-permute-start.14) | collective-permute-done | bytes 1048608 | tf_op jit(solution)/shard_map/ppermute | solution.py:54
  569.8 4.0 fusion.27
  575.3 13.3 %collective-permute-done.20 = bf16[256,2048]{1,0:T(8,128)(2,1)S(1)} collective-permute-done((bf16[256,2048]{1,0:T(8,128)(2,1)S(1)}, bf16[256,2048]{1,0:T(8,128)(2,1)S(1)}, u32[]{:S(2)}, u32[]{:S(2)}) %collective-permute-start.20) | collective-permute-done | bytes 1048608 | tf_op jit(solution)/shard_map/ppermute | solution.py:54
  591.8 19.4 %weight_grads.5 = bf16[2048,1536]{1,0:T(8,128)(2,1)} custom-call(bf16[1024,2048]{1,0:T(8,128)(2,1)} %copy-done.17, bf16[1024,2048]{1,0:T(8,128)(2,1)} %collective-permute-done.11.xh_ref, bf16[1024,2048]{1,0:T(8,128)(2,1)} %constant_dynamic-update-slice_fusion.cl_ref.yl_ref, bf16[1024,2048]{1,0:T(8,128)(2,1)} %collective-permute-done.5.ch_ref.yh_ref, ...), custom_call_target="tpu_custom_call" | custom-call | flops 12884901888 | bytes 29360128 | tf_op jit(solution)/shard_map/weight_grads/pallas_call | solution.py:207
  611.3 5.3 collective-permute-done.21
  620.8 5.7 collective-permute-done.22.high_ref.xh_ref
  626.4 7.1 front.1.d_ref
  633.6 33.7 %attend_back.1.refs_0_.refs_1_.b_ref = bf16[2048,384]{1,0:T(8,128)(2,1)} custom-call(s32[8]{0:T(128)} %select_reduce_fusion.2.place, s32[8]{0:T(128)} %and_select_fusion.2.first, bf16[2048,384]{1,0:T(8,128)(2,1)} %qkv.1.q_ref.kv_ref, bf16[2048,256]{1,0:T(8,128)(2,1)} %front.1.d_ref, f32[2048,384]{1,0:T(8,128)} %attend.1.refs_0_.h_ref.a_ref, ...), custom_call_target="tpu_custom_call" | custom-call | flops 40000000000 | bytes 6000000 | tf_op jit(solution)/shard_map/attend_back/pallas_call | solution.py:447
  667.3 8.1 back.7
  675.4 4.9 slice.246
  681.3 2.8 fusion.26
  686.5 32.9 %reduce-scatter.8.cloned.1.call-done = bf16[512,1536]{1,0:T(8,128)(2,1)} async-done(((bf16[2048,1536]{1,0:T(8,128)(2,1)}), bf16[512,1536]{1,0:T(8,128)(2,1)}) %reduce-scatter.8.cloned.1.call-update) | async-done | bytes 1572880 | tf_op jit(solution)/shard_map/reduce_scatter | solution.py:646
  724.6 3.2 reverse_select_fusion.3
  729.8 12.7 %weight_grads.3 = bf16[2048,640]{1,0:T(8,128)(2,1)} custom-call(bf16[1024,2048]{1,0:T(8,128)(2,1)} %copy-done.2, bf16[1024,2048]{1,0:T(8,128)(2,1)} %collective-permute-done.22.high_ref.xh_ref, bf16[1024,2048]{1,0:T(8,128)(2,1)} %pad_maximum_fusion.low_ref.yl_ref, bf16[1024,2048]{1,0:T(8,128)(2,1)} %collective-permute-done.2.high_ref.yh_ref, ...), custom_call_target="tpu_custom_call" | custom-call | flops 5368709120 | bytes 22020096 | tf_op jit(solution)/shard_map/weight_grads/pallas_call | solution.py:207
  751.2 13.9 %collective-permute-done.36 = f32[512]{0:T(512)S(1)} collective-permute-done((f32[512]{0:T(512)S(1)}, f32[512]{0:T(512)S(1)}, u32[]{:S(2)}, u32[]{:S(2)}) %collective-permute-start.36) | collective-permute-done | bytes 2080 | tf_op jit(solution)/shard_map/ppermute | solution.py:50
  775.5 23.2 %collective-permute-done.33 = bf16[512,1536]{1,0:T(8,128)(2,1)S(1)} collective-permute-done((bf16[512,1536]{1,0:T(8,128)(2,1)S(1)}, bf16[512,1536]{1,0:T(8,128)(2,1)S(1)}, u32[]{:S(2)}, u32[]{:S(2)}) %collective-permute-start.33) | collective-permute-done | bytes 1572896 | tf_op jit(solution)/shard_map/ppermute | solution.py:50
  800.9 20.3 %collective-permute-done.25 = bf16[256,2048]{1,0:T(8,128)(2,1)S(1)} collective-permute-done((bf16[256,2048]{1,0:T(8,128)(2,1)S(1)}, bf16[256,2048]{1,0:T(8,128)(2,1)S(1)}, u32[]{:S(2)}, u32[]{:S(2)}) %collective-permute-start.25) | collective-permute-done | bytes 1048608 | tf_op jit(solution)/shard_map/ppermute | solution.py:54
  826.3 14.5 %collective-permute-start.29 = (f32[512]{0:T(512)S(1)}, f32[512]{0:T(512)S(1)}, u32[]{:S(2)}, u32[]{:S(2)}) collective-permute-start(f32[512]{0:T(512)S(1)} %multiply_reduce_fusion.4), channel_id=1, source_target_pairs={{0,1},{1,0},{2,3},{3,2},{4,5},{5,4},{6,7},{7,6},{8,9},{9,8},{10,11... | collective-permute-start | bytes 6152 | tf_op jit(solution)/shard_map/ppermute | solution.py:42
  840.8 4.8 pad_maximum_fusion.7
  856.5 9.4 %collective-permute-done.31 = f32[512]{0:T(512)S(1)} collective-permute-done((f32[512]{0:T(512)S(1)}, f32[512]{0:T(512)S(1)}, u32[]{:S(2)}, u32[]{:S(2)}) %collective-permute-start.31) | collective-permute-done | bytes 2080 | tf_op jit(solution)/shard_map/ppermute | solution.py:50
  (261 shorter events, 131.0 us)
Async XLA Ops:
  7.2 81.5 %copy-start = (bf16[512,512]{1,0:T(8,128)(2,1)S(1)}, bf16[512,512]{1,0:T(8,128)(2,1)}, u32[]{:S(2)}) copy-start(bf16[512,512]{1,0:T(8,128)(2,1)} %param.14) | copy-start | bytes 1572868
  7.2 137.1 %all-gather.4.cloned.1.call-start = ((), (), s32[]{:S(2)}) async-start(), calls=%async_computation.3 | async-start | bytes 3276800 | tf_op jit(solution)/shard_map/all_gather | solution.py:534
  25.9 15.5 %collective-permute-start = (bf16[256,2048]{1,0:T(8,128)(2,1)S(1)}, bf16[256,2048]{1,0:T(8,128)(2,1)S(1)}, u32[]{:S(2)}, u32[]{:S(2)}) collective-permute-start(bf16[256,2048]{1,0:T(8,128)(2,1)S(1)} %fusion.4), channel_id=1, source_target_pairs={{0,4},{1,3},{2,6},{3,1},{4,0},{5,7},{6,2},{7,5},{8,12},{9,11},{10,... | collective-permute-start | bytes 3145736 | tf_op jit(solution)/shard_map/ppermute | solution.py:54
  41.6 26.1 %collective-permute-start.1 = (bf16[512,2048]{1,0:T(8,128)(2,1)S(1)}, bf16[512,2048]{1,0:T(8,128)(2,1)S(1)}, u32[]{:S(2)}, u32[]{:S(2)}) collective-permute-start(bf16[512,2048]{1,0:T(8,128)(2,1)S(1)} %pad_maximum_fusion.8), channel_id=1, source_target_pairs={{0,2},{1,5},{2,0},{3,7},{4,6},{5,1},{6,4},{7,3},{8,10},{9,13},{10,... | collective-permute-start | bytes 6291464 | tf_op jit(solution)/shard_map/ppermute | solution.py:58
  70.0 15.7 %collective-permute-start.3 = (bf16[256,2048]{1,0:T(8,128)(2,1)S(1)}, bf16[256,2048]{1,0:T(8,128)(2,1)S(1)}, u32[]{:S(2)}, u32[]{:S(2)}) collective-permute-start(bf16[256,2048]{1,0:T(8,128)(2,1)S(1)} %constant_dynamic-slice_fusion.6), channel_id=1, source_target_pairs={{0,4},{1,3},{2,6},{3,1},{4,0},{5,7},{6,2},{7,5},{8,12},{9,11},{10,... | collective-permute-start | bytes 3145736 | tf_op jit(solution)/shard_map/ppermute | solution.py:54
  87.1 26.4 %collective-permute-start.4 = (bf16[512,2048]{1,0:T(8,128)(2,1)}, bf16[512,2048]{1,0:T(8,128)(2,1)}, u32[]{:S(2)}, u32[]{:S(2)}) collective-permute-start(bf16[512,2048]{1,0:T(8,128)(2,1)} %pad_maximum_fusion.9), channel_id=1, source_target_pairs={{0,2},{1,5},{2,0},{3,7},{4,6},{5,1},{6,4},{7,3},{8,10},{9,13},{10,... | collective-permute-start | bytes 6291464 | tf_op jit(solution)/shard_map/ppermute | solution.py:58
  88.7 55.6 %collective-permute-start.2 = (bf16[1024,2048]{1,0:T(8,128)(2,1)}, bf16[1024,2048]{1,0:T(8,128)(2,1)}, u32[]{:S(2)}, u32[]{:S(2)}) collective-permute-start(bf16[1024,2048]{1,0:T(8,128)(2,1)} %pad_maximum_fusion.low_ref.yl_ref), channel_id=1, source_target_pairs={{0,1},{1,0},{2,3},{3,2},{4,5},{5,4},{6,7},{7,6},{8,9},{9,8},{10,11... | collective-permute-start | bytes 12582920 | tf_op jit(solution)/shard_map/ppermute | solution.py:42
  90.9 220.0 %all-gather.6.cloned.1.call-start = ((), (), s32[]{:S(2)}) async-start(), calls=%async_computation.4 | async-start | bytes 7864320 | tf_op jit(solution)/shard_map/all_gather | solution.py:555
  116.7 59.8 %collective-permute-start.5 = (bf16[1024,2048]{1,0:T(8,128)(2,1)}, bf16[1024,2048]{1,0:T(8,128)(2,1)}, u32[]{:S(2)}, u32[]{:S(2)}) collective-permute-start(bf16[1024,2048]{1,0:T(8,128)(2,1)} %constant_dynamic-update-slice_fusion.cl_ref.yl_ref), channel_id=1, source_target_pairs={{0,1},{1,0},{2,3},{3,2},{4,5},{5,4},{6,7},{7,6},{8,9},{9,8},{10,11... | collective-permute-start | bytes 12582920 | tf_op jit(solution)/shard_map/ppermute | solution.py:42
  188.2 7.5 collective-permute-start.6
  191.8 54.4 %copy-start.9 = (bf16[512,512]{1,0:T(8,128)(2,1)}, bf16[512,512]{1,0:T(8,128)(2,1)S(1)}, u32[]{:S(2)}) copy-start(bf16[512,512]{1,0:T(8,128)(2,1)S(1)} %get-tuple-element.50) | copy-start | bytes 1572868
  191.8 54.4 %copy-start.11 = (bf16[512,512]{1,0:T(8,128)(2,1)}, bf16[512,512]{1,0:T(8,128)(2,1)S(1)}, u32[]{:S(2)}) copy-start(bf16[512,512]{1,0:T(8,128)(2,1)S(1)} %get-tuple-element.75) | copy-start | bytes 1572868
  194.1 232.1 %all-gather.8.cloned.1.call-start = ((), (), s32[]{:S(2)}) async-start(), calls=%async_computation.5 | async-start | bytes 7864320 | tf_op jit(solution)/shard_map/all_gather | solution.py:555
  198.1 26.1 %collective-permute-start.7 = (bf16[512,2048]{1,0:T(8,128)(2,1)S(1)}, bf16[512,2048]{1,0:T(8,128)(2,1)S(1)}, u32[]{:S(2)}, u32[]{:S(2)}) collective-permute-start(bf16[512,2048]{1,0:T(8,128)(2,1)S(1)} %slice_add_fusion.6), channel_id=1, source_target_pairs={{0,2},{1,5},{2,0},{3,7},{4,6},{5,1},{6,4},{7,3},{8,10},{9,13},{10,... | collective-permute-start | bytes 6291464 | tf_op jit(solution)/shard_map/ppermute | solution.py:58
  226.8 14.9 %collective-permute-start.8 = (bf16[256,2048]{1,0:T(8,128)(2,1)S(1)}, bf16[256,2048]{1,0:T(8,128)(2,1)S(1)}, u32[]{:S(2)}, u32[]{:S(2)}) collective-permute-start(bf16[256,2048]{1,0:T(8,128)(2,1)S(1)} %slice.229), channel_id=1, source_target_pairs={{0,4},{1,3},{2,6},{3,1},{4,0},{5,7},{6,2},{7,5},{8,12},{9,11},{10,... | collective-permute-start | bytes 3145736 | tf_op jit(solution)/shard_map/ppermute | solution.py:54
  244.7 66.8 %collective-permute-start.9 = (bf16[256,2048]{1,0:T(8,128)(2,1)}, bf16[256,2048]{1,0:T(8,128)(2,1)}, u32[]{:S(2)}, u32[]{:S(2)}) collective-permute-start(bf16[256,2048]{1,0:T(8,128)(2,1)} %multiply_convert_fusion), channel_id=1, source_target_pairs={{0,4},{1,3},{2,6},{3,1},{4,0},{5,7},{6,2},{7,5},{8,12},{9,11},{10,... | collective-permute-start | bytes 3145736 | tf_op jit(solution)/shard_map/ppermute | solution.py:54
  311.0 373.6 %reduce-scatter.6.cloned.1.call-start = ((), (), s32[]{:S(2)}) async-start(), calls=%async_computation.7 | async-start | bytes 7864320 | tf_op jit(solution)/shard_map/reduce_scatter | solution.py:646
  313.3 26.1 %collective-permute-start.10 = (bf16[512,2048]{1,0:T(8,128)(2,1)S(1)}, bf16[512,2048]{1,0:T(8,128)(2,1)S(1)}, u32[]{:S(2)}, u32[]{:S(2)}) collective-permute-start(bf16[512,2048]{1,0:T(8,128)(2,1)S(1)} %pad_maximum_fusion.10), channel_id=1, source_target_pairs={{0,2},{1,5},{2,0},{3,7},{4,6},{5,1},{6,4},{7,3},{8,10},{9,13},{10,... | collective-permute-start | bytes 6291464 | tf_op jit(solution)/shard_map/ppermute | solution.py:58
  341.3 7.4 collective-permute-start.11
  388.8 330.6 %reduce-scatter.8.cloned.1.call-start = ((), (), s32[]{:S(2)}) async-start(), calls=%async_computation.8 | async-start | bytes 7864320 | tf_op jit(solution)/shard_map/reduce_scatter | solution.py:646
  475.3 16.9 %collective-permute-start.17 = (bf16[1024,2048]{1,0:T(8,128)(2,1)}, bf16[1024,2048]{1,0:T(8,128)(2,1)S(1)}, u32[]{:S(2)}, u32[]{:S(2)}) collective-permute-start(bf16[1024,2048]{1,0:T(8,128)(2,1)} %slice.239), channel_id=1, source_target_pairs={{0,1},{1,0},{2,3},{3,2},{4,5},{5,4},{6,7},{7,6},{8,9},{9,8},{10,11... | collective-permute-start | bytes 12582920 | tf_op jit(solution)/shard_map/ppermute | solution.py:42
  491.7 7.3 collective-permute-start.12
  494.6 26.1 %collective-permute-start.18 = (bf16[512,2048]{1,0:T(8,128)(2,1)S(1)}, bf16[512,2048]{1,0:T(8,128)(2,1)S(1)}, u32[]{:S(2)}, u32[]{:S(2)}) collective-permute-start(bf16[512,2048]{1,0:T(8,128)(2,1)S(1)} %slice_add_fusion.2), channel_id=1, source_target_pairs={{0,2},{1,5},{2,0},{3,7},{4,6},{5,1},{6,4},{7,3},{8,10},{9,13},{10,... | collective-permute-start | bytes 6291464 | tf_op jit(solution)/shard_map/ppermute | solution.py:58
  499.2 55.2 %collective-permute-start.13 = (bf16[512,2048]{1,0:T(8,128)(2,1)S(1)}, bf16[512,2048]{1,0:T(8,128)(2,1)S(1)}, u32[]{:S(2)}, u32[]{:S(2)}) collective-permute-start(bf16[512,2048]{1,0:T(8,128)(2,1)S(1)} %slice_add_fusion.4), channel_id=1, source_target_pairs={{0,2},{1,5},{2,0},{3,7},{4,6},{5,1},{6,4},{7,3},{8,10},{9,13},{10,... | collective-permute-start | bytes 6291464 | tf_op jit(solution)/shard_map/ppermute | solution.py:58
  522.8 33.7 %collective-permute-start.19 = (bf16[256,2048]{1,0:T(8,128)(2,1)S(1)}, bf16[256,2048]{1,0:T(8,128)(2,1)S(1)}, u32[]{:S(2)}, u32[]{:S(2)}) collective-permute-start(bf16[256,2048]{1,0:T(8,128)(2,1)S(1)} %slice.244), channel_id=1, source_target_pairs={{0,4},{1,3},{2,6},{3,1},{4,0},{5,7},{6,2},{7,5},{8,12},{9,11},{10,... | collective-permute-start | bytes 3145736 | tf_op jit(solution)/shard_map/ppermute | solution.py:54
  554.9 14.9 %collective-permute-start.14 = (bf16[256,2048]{1,0:T(8,128)(2,1)S(1)}, bf16[256,2048]{1,0:T(8,128)(2,1)S(1)}, u32[]{:S(2)}, u32[]{:S(2)}) collective-permute-start(bf16[256,2048]{1,0:T(8,128)(2,1)S(1)} %slice.237), channel_id=1, source_target_pairs={{0,4},{1,3},{2,6},{3,1},{4,0},{5,7},{6,2},{7,5},{8,12},{9,11},{10,... | collective-permute-start | bytes 3145736 | tf_op jit(solution)/shard_map/ppermute | solution.py:54
  573.8 14.8 %collective-permute-start.20 = (bf16[256,2048]{1,0:T(8,128)(2,1)S(1)}, bf16[256,2048]{1,0:T(8,128)(2,1)S(1)}, u32[]{:S(2)}, u32[]{:S(2)}) collective-permute-start(bf16[256,2048]{1,0:T(8,128)(2,1)S(1)} %get-tuple-element.21), channel_id=1, source_target_pairs={{0,4},{1,3},{2,6},{3,1},{4,0},{5,7},{6,2},{7,5},{8,12},{9,11},{10,... | collective-permute-start | bytes 3145736 | tf_op jit(solution)/shard_map/ppermute | solution.py:54
  590.2 26.4 %collective-permute-start.21 = (bf16[512,2048]{1,0:T(8,128)(2,1)}, bf16[512,2048]{1,0:T(8,128)(2,1)}, u32[]{:S(2)}, u32[]{:S(2)}) collective-permute-start(bf16[512,2048]{1,0:T(8,128)(2,1)} %pad_maximum_fusion.12), channel_id=1, source_target_pairs={{0,2},{1,5},{2,0},{3,7},{4,6},{5,1},{6,4},{7,3},{8,10},{9,13},{10,... | collective-permute-start | bytes 6291464 | tf_op jit(solution)/shard_map/ppermute | solution.py:58
  611.2 213.8 %reduce-scatter.4.cloned.1.call-start = ((), (), s32[]{:S(2)}) async-start(), calls=%async_computation.6 | async-start | bytes 3276800 | tf_op jit(solution)/shard_map/reduce_scatter | solution.py:648
  619.1 7.4 collective-permute-start.22
  619.2 61.2 %collective-permute-start.15 = (bf16[256,2048]{1,0:T(8,128)(2,1)S(1)}, bf16[256,2048]{1,0:T(8,128)(2,1)S(1)}, u32[]{:S(2)}, u32[]{:S(2)}) collective-permute-start(bf16[256,2048]{1,0:T(8,128)(2,1)S(1)} %copy-done.18), channel_id=1, source_target_pairs={{0,2},{2,0},{1,3},{3,1},{4,6},{6,4},{5,7},{7,5},{8,10},{10,8},{9,1... | collective-permute-start | bytes 3145736 | tf_op jit(solution)/shard_map/ppermute | solution.py:46
  680.3 62.3 %collective-permute-start.23 = (bf16[1024,2048]{1,0:T(8,128)(2,1)}, bf16[1024,2048]{1,0:T(8,128)(2,1)}, u32[]{:S(2)}, u32[]{:S(2)}) collective-permute-start(bf16[1024,2048]{1,0:T(8,128)(2,1)} %slice.246), channel_id=1, source_target_pairs={{0,1},{1,0},{2,3},{3,2},{4,5},{5,4},{6,7},{7,6},{8,9},{9,8},{10,11... | collective-permute-start | bytes 12582920 | tf_op jit(solution)/shard_map/ppermute | solution.py:42
  684.1 35.3 %copy-start.10 = (bf16[512,512]{1,0:T(8,128)(2,1)S(1)}, bf16[512,512]{1,0:T(8,128)(2,1)}, u32[]{:S(2)}) copy-start(bf16[512,512]{1,0:T(8,128)(2,1)} %copy-done.9) | copy-start | bytes 1572868
  684.1 35.3 %copy-start.12 = (bf16[512,512]{1,0:T(8,128)(2,1)S(1)}, bf16[512,512]{1,0:T(8,128)(2,1)}, u32[]{:S(2)}) copy-start(bf16[512,512]{1,0:T(8,128)(2,1)} %copy-done.11) | copy-start | bytes 1572868
  684.1 36.9 %collective-permute-start.16 = (bf16[2,256,2048]{2,1,0:T(8,128)(2,1)}, bf16[2,256,2048]{2,1,0:T(8,128)(2,1)}, u32[]{:S(2)}, u32[]{:S(2)}) collective-permute-start(bf16[2,256,2048]{2,1,0:T(8,128)(2,1)} %get-tuple-element.47), channel_id=1, source_target_pairs={{0,1},{1,0},{2,3},{3,2},{4,5},{5,4},{6,7},{7,6},{8,9},{9,8},{10,11... | collective-permute-start | bytes 6291464 | tf_op jit(solution)/shard_map/ppermute | solution.py:42
  721.0 2.1 collective-permute-start.34
  723.1 6.2 collective-permute-start.35
  727.8 37.9 %collective-permute-start.32 = (bf16[512,1536]{1,0:T(8,128)(2,1)S(1)}, bf16[512,1536]{1,0:T(8,128)(2,1)}, u32[]{:S(2)}, u32[]{:S(2)}) collective-permute-start(bf16[512,1536]{1,0:T(8,128)(2,1)S(1)} %copy-done.15), channel_id=1, source_target_pairs={{0,4},{4,0},{1,5},{5,1},{2,6},{6,2},{3,7},{7,3},{8,12},{12,8},{9,1... | collective-permute-start | bytes 4718600 | tf_op jit(solution)/shard_map/ppermute | solution.py:50
  729.3 35.9 %collective-permute-start.36 = (f32[512]{0:T(512)S(1)}, f32[512]{0:T(512)S(1)}, u32[]{:S(2)}, u32[]{:S(2)}) collective-permute-start(f32[512]{0:T(512)S(1)} %add.348), channel_id=1, source_target_pairs={{0,4},{4,0},{1,5},{5,1},{2,6},{6,2},{3,7},{7,3},{8,12},{12,8},{9,1... | collective-permute-start | bytes 6152 | tf_op jit(solution)/shard_map/ppermute | solution.py:50
  745.2 26.1 %collective-permute-start.24 = (bf16[512,2048]{1,0:T(8,128)(2,1)S(1)}, bf16[512,2048]{1,0:T(8,128)(2,1)S(1)}, u32[]{:S(2)}, u32[]{:S(2)}) collective-permute-start(bf16[512,2048]{1,0:T(8,128)(2,1)S(1)} %slice_add_fusion), channel_id=1, source_target_pairs={{0,2},{1,5},{2,0},{3,7},{4,6},{5,1},{6,4},{7,3},{8,10},{9,13},{10,... | collective-permute-start | bytes 6291464 | tf_op jit(solution)/shard_map/ppermute | solution.py:58
  749.8 49.0 %collective-permute-start.33 = (bf16[512,1536]{1,0:T(8,128)(2,1)S(1)}, bf16[512,1536]{1,0:T(8,128)(2,1)S(1)}, u32[]{:S(2)}, u32[]{:S(2)}) collective-permute-start(bf16[512,1536]{1,0:T(8,128)(2,1)S(1)} %copy-done.16), channel_id=1, source_target_pairs={{0,4},{4,0},{1,5},{5,1},{2,6},{6,2},{3,7},{7,3},{8,12},{12,8},{9,1... | collective-permute-start | bytes 4718600 | tf_op jit(solution)/shard_map/ppermute | solution.py:50
  774.0 47.2 %collective-permute-start.25 = (bf16[256,2048]{1,0:T(8,128)(2,1)S(1)}, bf16[256,2048]{1,0:T(8,128)(2,1)S(1)}, u32[]{:S(2)}, u32[]{:S(2)}) collective-permute-start(bf16[256,2048]{1,0:T(8,128)(2,1)S(1)} %slice.251), channel_id=1, source_target_pairs={{0,4},{1,3},{2,6},{3,1},{4,0},{5,7},{6,2},{7,5},{8,12},{9,11},{10,... | collective-permute-start | bytes 3145736 | tf_op jit(solution)/shard_map/ppermute | solution.py:54
  822.7 28.9 %collective-permute-start.26 = (bf16[256,2048]{1,0:T(8,128)(2,1)S(1)}, bf16[256,2048]{1,0:T(8,128)(2,1)}, u32[]{:S(2)}, u32[]{:S(2)}) collective-permute-start(bf16[256,2048]{1,0:T(8,128)(2,1)S(1)} %fusion.8), channel_id=1, source_target_pairs={{0,2},{2,0},{1,3},{3,1},{4,6},{6,4},{5,7},{7,5},{8,10},{10,8},{9,1... | collective-permute-start | bytes 3145736 | tf_op jit(solution)/shard_map/ppermute | solution.py:46
  826.3 19.3 %collective-permute-start.29 = (f32[512]{0:T(512)S(1)}, f32[512]{0:T(512)S(1)}, u32[]{:S(2)}, u32[]{:S(2)}) collective-permute-start(f32[512]{0:T(512)S(1)} %multiply_reduce_fusion.4), channel_id=1, source_target_pairs={{0,1},{1,0},{2,3},{3,2},{4,5},{5,4},{6,7},{7,6},{8,9},{9,8},{10,11... | collective-permute-start | bytes 6152 | tf_op jit(solution)/shard_map/ppermute | solution.py:42
  845.6 5.4 collective-permute-start.30
  849.5 17.0 %collective-permute-start.28 = (bf16[512,640]{1,0:T(8,128)(2,1)S(1)}, bf16[512,640]{1,0:T(8,128)(2,1)S(1)}, u32[]{:S(2)}, u32[]{:S(2)}) collective-permute-start(bf16[512,640]{1,0:T(8,128)(2,1)S(1)} %copy-done.31), channel_id=1, source_target_pairs={{0,4},{4,0},{1,5},{5,1},{2,6},{6,2},{3,7},{7,3},{8,12},{12,8},{9,1... | collective-permute-start | bytes 1966088 | tf_op jit(solution)/shard_map/ppermute | solution.py:50
  851.0 15.0 %collective-permute-start.31 = (f32[512]{0:T(512)S(1)}, f32[512]{0:T(512)S(1)}, u32[]{:S(2)}, u32[]{:S(2)}) collective-permute-start(f32[512]{0:T(512)S(1)} %add.344), channel_id=1, source_target_pairs={{0,4},{4,0},{1,5},{5,1},{2,6},{6,2},{3,7},{7,3},{8,12},{12,8},{9,1... | collective-permute-start | bytes 6152 | tf_op jit(solution)/shard_map/ppermute | solution.py:50
  853.2 17.9 %collective-permute-start.27 = (bf16[2,256,2048]{2,1,0:T(8,128)(2,1)S(1)}, bf16[2,256,2048]{2,1,0:T(8,128)(2,1)S(1)}, u32[]{:S(2)}, u32[]{:S(2)}) collective-permute-start(bf16[2,256,2048]{2,1,0:T(8,128)(2,1)S(1)} %get-tuple-element.44), channel_id=1, source_target_pairs={{0,1},{1,0},{2,3},{3,2},{4,5},{5,4},{6,7},{7,6},{8,9},{9,8},{10,11... | collective-permute-start | bytes 6291464 | tf_op jit(solution)/shard_map/ppermute | solution.py:42
  (44 other events, 375.5 us)
Sparse Core Ops, SparseCore 0:
  91.1 53.1 all-gather.3
  194.2 116.7 all-gather.5
  312.6 113.5 all-gather.7
  428.3 108.9 reduce-scatter.5
  611.4 107.9 reduce-scatter.7
  742.7 51.7 reduce-scatter.3

commit v2 on v1

--- a/solution.py
+++ b/solution.py
@@ -38,8 +38,13 @@
 SECOND = joint_pairs(1)
 
 
-def swap_core(v):
-    return lax.ppermute(v, "tp", CORE)
+def swap_core(v, pieces=1):
+    if pieces == 1:
+        return lax.ppermute(v, "tp", CORE)
+    rows = v.shape[0] // pieces
+    return jnp.concatenate(
+        [lax.ppermute(v[at * rows : (at + 1) * rows], "tp", CORE) for at in range(pieces)]
+    )
 
 
 def swap_y(v):
@@ -66,8 +71,8 @@
     return pltpu.CompilerParams(vmem_limit_bytes=VMEM)
 
 
-def cost(flops, read, exps=0):
-    return pl.CostEstimate(flops=int(flops), bytes_accessed=int(read), transcendentals=int(exps))
+def cost(gigaflops=0):
+    return pl.CostEstimate(flops=int(gigaflops * 1e9) + 1, bytes_accessed=1, transcendentals=0)
 
 
 def inv_rms(hidden):
@@ -140,7 +145,7 @@
         ],
         out_specs=pl.BlockSpec((step, width), lambda i: (i, 0)),
         compiler_params=params(),
-        cost_estimate=cost(2 * rows * depth * width, 2 * (rows * depth + depth * width)),
+        cost_estimate=cost(),
         name="qkv",
     )(*x, w, w, cos, sin)
 
@@ -177,7 +182,7 @@
         + [pl.BlockSpec((depth, width), lambda i: (0, 0))],
         out_specs=pl.BlockSpec((step, width), lambda i: (i, 0)),
         compiler_params=params(),
-        cost_estimate=cost(2 * rows * depth * width, 4 * rows * depth + 4 * depth * width),
+        cost_estimate=cost(),
         name="ffn",
     )(*x, *cot, w)
 
@@ -215,7 +220,7 @@
         ],
         out_specs=pl.BlockSpec((step, width), lambda i: (i, 0)),
         compiler_params=params(),
-        cost_estimate=cost(2 * rows * depth * width, 4 * rows * depth + 4 * depth * width),
+        cost_estimate=cost(),
         name="weight_grads",
     )(*x, *y, a, b)
 
@@ -250,7 +255,7 @@
         + [pl.BlockSpec((depth, term[4]), lambda i, column=term[3]: (0, column)) for term in terms],
         out_specs=pl.BlockSpec((step, depth), lambda i: (i, 0)),
         compiler_params=params(),
-        cost_estimate=cost(2 * rows * depth * total, 2 * rows * depth),
+        cost_estimate=cost(),
         name="back",
     )(*[term[0] for term in terms], *[term[2] for term in terms])
 
@@ -275,7 +280,7 @@
         + [pl.BlockSpec((depth, width), lambda i: (0, column))],
         out_specs=pl.BlockSpec((step, width), lambda i: (i, 0)),
         compiler_params=params(),
-        cost_estimate=cost(2 * rows * depth * width, 2 * rows * depth),
+        cost_estimate=cost(),
         name="front",
     )(*x, w)
 
@@ -361,7 +366,7 @@
             out_specs=pl.BlockSpec((BLOCK, q_width + 128), lambda i, place, first: (place[i], 0)),
         ),
         compiler_params=params(),
-        cost_estimate=cost(16e9, 4e6, rows * 1024 * 4),
+        cost_estimate=cost(),
         name="attend",
     )(place, first, qkv, qkv, start)
 
@@ -463,23 +468,62 @@
             scratch_shapes=[pltpu.VMEM((rows, 128), F32)],
         ),
         compiler_params=params(),
-        cost_estimate=cost(40e9, 6e6, rows * 1024 * 4),
+        cost_estimate=cost(),
         name="attend_back",
     )(place, first, qkv, d_heads, heads, qkv, start, cos, sin)
 
 
-def sum_to_owner(part):
+def sum_cores(part):
     rows = part.shape[0] // 8
-    arrived = swap_core(part[4 * rows :])
-    arrived = part[2 * rows : 4 * rows] + arrived[2 * rows :], part[: 2 * rows] + arrived[: 2 * rows]
-    pair = arrived[1] + swap_second(arrived[0])
-    return pair[:rows].astype(F32) + swap_first(pair[rows:]).astype(F32)
-
-
-def share_rows(own):
-    two = jnp.concatenate([own, swap_first(own)])
-    four = jnp.concatenate([two, swap_second(two)])
-    return four, swap_core(four)
+    arrived = [lax.ppermute(part[at * rows : (at + 1) * rows], "tp", CORE) for at in range(4, 8)]
+    far = part[2 * rows : 4 * rows] + jnp.concatenate(arrived[2:])
+    near = part[: 2 * rows] + jnp.concatenate(arrived[:2])
+    return far, near
+
+
+def sum_chips(far, near, behind=(), beside=()):
+    rows = near.shape[0] // 2
+    near = near + after(swap_second(far), *behind)
+    near = after(near, *beside)
+    return near[:rows].astype(F32) + swap_first(near[rows:]).astype(F32)
+
+
+def sum_to_owner(part, beside=()):
+    return sum_chips(*sum_cores(part), beside=beside)
+
+
+def share_rows(own, beside=()):
+    beside = list(beside) + [()] * (2 - len(beside))
+    two = jnp.concatenate([own, after(swap_first(own), *beside[0])])
+    four = jnp.concatenate([two, after(swap_second(two), *beside[1])])
+    return four, swap_core(four, 4)
+
+
+def ring_over(shard, count):
+    cycle = [(at, (at + 1) % count) for at in range(count)]
+    pieces = [shard]
+    for _ in range(count - 1):
+        pieces.append(lax.ppermute(pieces[-1], "fsdp", cycle))
+    return pieces
+
+
+def in_place(pieces, axis):
+    count, size = len(pieces), pieces[0].shape[axis]
+    here = lax.axis_index("fsdp")
+    shape = list(pieces[0].shape)
+    shape[axis] *= count
+    whole = jnp.zeros(shape, pieces[0].dtype)
+    for back, piece in enumerate(pieces):
+        owner = lax.rem(here + count - back, count)
+        whole = lax.dynamic_update_slice_in_dim(whole, piece, owner * size, axis)
+    return whole
+
+
+def shifts_over(shard, count):
+    return [shard] + [
+        lax.ppermute(shard, "fsdp", [(at, (at + by) % count) for at in range(count)])
+        for by in range(1, count)
+    ]
 
 
 def share_in_ctx(own, y, core):
@@ -531,8 +575,10 @@
     q_half, k_half, v_half, o_half = map(half, (q_weight, k_weight, v_weight, o_weight))
     q_width, kv_width = q_half.shape[1], k_half.shape[1]
     attn_shard = jnp.concatenate([o_half, q_half, k_half, v_half], axis=1)
-    attn_full = lax.all_gather(attn_shard, "fsdp", axis=0, tiled=True)
-    gains = lax.all_gather(jnp.stack([attn_gain, ffn_gain]), "fsdp", axis=1, tiled=True)
+    fsdp = lax.axis_size("fsdp")
+    attn_ring = ring_over(attn_shard, fsdp)
+    attn_full = in_place(attn_ring, 0)
+    gains = in_place(shifts_over(jnp.stack([attn_gain, ffn_gain]), fsdp), 1)
     gain_one = gains[0].astype(F32)[None]
     gain_two = gains[1].astype(F32)[None]
     ff_half = gate_weight.shape[1] // 2
@@ -549,12 +595,6 @@
                 axis=1,
             )
         )
-    ffn_full = []
-    before = attn_full
-    for part in range(CHUNKS):
-        before = lax.all_gather(after(ffn_shards[part], before), "fsdp", axis=0, tiled=True)
-        ffn_full.append(before)
-
     length_row, deal_row = lengths[0], deal[0]
     spans = deal_row.shape[0]
     span_rows = group_rows // spans
@@ -601,33 +641,46 @@
     tokens_own = lax.dynamic_slice_in_dim(tokens, tp * own_rows, own_rows, 0).astype(F32)
     cot_low = lax.dynamic_slice_in_dim(cotangent, tp * own_rows, own_rows, 0)
     cot_own = cot_low.astype(F32)
-    normed = share_rows((tokens_own * inv_rms(tokens_own) * gain_one).astype(BF16))
-    cot = share_rows(after(cot_low, normed[0]))
+    normed = share_rows(
+        (tokens_own * inv_rms(tokens_own) * gain_one).astype(BF16), [[piece] for piece in attn_ring[1:3]]
+    )
+    attn_full, first_shard, cot_low, cos, sin, *normed = lax.optimization_barrier(
+        (attn_full, after(ffn_shards[0], attn_ring[-1]), cot_low, cos, sin, *normed)
+    )
     qkv = project_qkv(normed, attn_full, q_width, cos, sin)
     heads = attend(qkv, place, first, start_column, q_width)
+    cot = share_rows(cot_low, [[qkv], [heads]])
+    ffn_full = [
+        lax.all_gather(shard, "fsdp", axis=0, tiled=True)
+        for shard in (first_shard, after(ffn_shards[1], heads))
+    ]
     heads = after(heads, *cot)
     attn_part = back_product([(heads, 0, attn_full, 0, q_width)])
-    hidden = tokens_own + sum_to_owner(attn_part)
+    hidden = tokens_own + sum_to_owner(attn_part, ffn_full[:1])
     normed_two = share_rows((hidden * inv_rms(hidden) * gain_two).astype(BF16))
 
     acts = []
     grad_parts = []
     for part in range(CHUNKS):
-        acts.append(ffn_chunk(normed_two, cot, ffn_full[part]))
+        acts.append(ffn_chunk(after(normed_two, *grad_parts), cot, ffn_full[part]))
         grad_parts.append(
             weight_grads(normed_two, acts[part], 2 * chunk, 0, cot, acts[part], chunk, 2)
         )
+    reduced = [
+        lax.psum_scatter(part, "fsdp", scatter_dimension=0, tiled=True) for part in grad_parts
+    ]
     d_norm_part = back_product(
         [(acts[part], 0, ffn_full[part], 0, 2 * chunk) for part in range(CHUNKS)]
     )
     ffn_part = back_product([(acts[part], 2, ffn_full[part], 2, chunk) for part in range(CHUNKS)])
-    d_normed_two = sum_to_owner(d_norm_part)
+    d_normed_two = sum_to_owner(d_norm_part, grad_parts)
     d_hidden = cot_own + rms_back(hidden, gain_two, d_normed_two)
-    d_attn = share_rows(d_hidden.astype(BF16))
-    result_own = (hidden + sum_to_owner(ffn_part)).astype(BF16)
-    result = share_in_ctx(result_own, y, core)
+    d_attn = share_rows(d_hidden.astype(BF16), [[ffn_part, reduced[0]]])
 
     d_heads = front_product(d_attn, attn_full, q_width, 0)
+    ffn_far, ffn_near = sum_cores(after(ffn_part, d_attn[1]))
+    d_heads, ffn_far, reduced[0] = lax.optimization_barrier((d_heads, ffn_far, reduced[0]))
+    other_reduced = [swap_x(reduced[0])]
     d_qkv = attend_back(qkv, d_heads, heads, place, first, start_column, cos, sin)
     d_normed_part = back_product(
         [
@@ -638,14 +691,20 @@
     attn_grad = weight_grads(
         d_attn, heads, q_width, 0, normed, d_qkv, q_width + 128, 0
     )
-    d_normed = sum_to_owner(d_normed_part)
+    normed_far, normed_near = sum_cores(d_normed_part)
+    for part in range(1, CHUNKS):
+        reduced[part] = after(reduced[part], attn_grad)
+    d_normed = sum_chips(normed_far, normed_near, beside=[attn_grad, *reduced[1:]])
+    for part in range(1, CHUNKS):
+        reduced[part] = after(reduced[part], d_normed)
+        other_reduced.append(swap_x(reduced[part]))
+    result_own = (hidden + sum_chips(ffn_far, ffn_near, behind=[normed_far])).astype(BF16)
+    result = share_in_ctx(result_own, y, core)
     tokens_grad_own = (d_hidden + rms_back(tokens_own, gain_one, d_normed)).astype(BF16)
     tokens_grad = share_in_ctx(tokens_grad_own, y, core)
 
-    reduced = [
-        lax.psum_scatter(part, "fsdp", scatter_dimension=0, tiled=True) for part in grad_parts
-    ]
     attn_reduced = lax.psum_scatter(attn_grad, "fsdp", scatter_dimension=0, tiled=True)
+    attn_reduced = after(attn_reduced, tokens_grad)
 
     def gain_grad(pairs, gain):
         products = sum(
@@ -662,7 +721,6 @@
         ffn_gain,
     )
 
-    other_reduced = [swap_x(part) for part in reduced]
     halves = [both_halves(mine, other, ctx) for mine, other in zip(reduced, other_reduced)]
 
     def ffn_out(which):

time: 891 us -> 771 us (0.87)
  waiting for transfers between devices: 453 us -> 305 us
  other arithmetic: 86 us -> 104 us
  starting transfers between devices: 52.2 us -> 66.1 us
  blocking collectives: 13.5 us -> 0 us
    all_gather x3 -> x2, waiting for transfers between devices: 119 us -> 20.1 us  [shards(): lax.all_gather(shard, 'fsdp', axis=0, tiled=True)]
    ppermute x8, waiting for transfers between devices: 148 us -> 82.2 us  [swap_second(): return lax.ppermute(v, ('ctx', 'tp'), SECOND)]
    ppermute x0 -> x38, waiting for transfers between devices: none -> 46 us  [the longest x3 30.5 us: ring_over(): pieces.append(lax.ppermute(pieces[-1], 'fsdp', cycle))]
    ppermute x4, waiting for transfers between devices: 0.01 us -> 42.8 us  [swap_y(): return lax.ppermute(v, 'tp', ACROSS)]
    ppermute x0 -> x38, starting transfers between devices: none -> 36 us  [the longest x16 23.8 us: sum_cores(): lax.ppermute(part[at * rows:(at + 1) * rows], 'tp', CORE)]
    reduce_scatter x2, waiting for transfers between devices: 32.9 us -> 0.03 us  [shards(): lax.psum_scatter(part, 'fsdp', scatter_dimension=0, tiled=True)]
    ppermute x5, waiting for transfers between devices: 46.6 us -> 22.7 us  [swap_x(): return lax.ppermute(v, 'ctx', PAIR)]
    ppermute x12 -> x4, waiting for transfers between devices: 17.3 us -> 1.15 us  [swap_core(): return lax.ppermute(v, 'tp', CORE)]
  transfers between devices with their start and end apart: 43 -> 72, of which waited for: 25 -> 31; matrix products, arithmetic and copies ran while one was open for 13% -> 18% of each run, Pallas kernels for 24% -> 29%
where the time goes in v2:
time: 771 us; the launch traced here: 765 us
  waiting for transfers between devices  305 us (40%)
  Pallas kernels  219 us (28%)
  other arithmetic  104 us (13%)
  starting transfers between devices  66.1 us (9%)
  local copies, waits for them, and re-layouts  54.8 us (7%)
  between operations  15.1 us (2%)
    ppermute x8, waiting for transfers between devices, swap_first(): return lax.ppermute(v, ('ctx', 'tp'), FIRST)  90.2 us
    ppermute x8, waiting for transfers between devices, swap_second(): return lax.ppermute(v, ('ctx', 'tp'), SECOND)  82.2 us
    pallas_call x4, Pallas kernels, back_product(): pl.pallas_call(back_kernel, out_shape=jax.ShapeDtypeStruct((rows, depth),...  52.4 us
    pallas_call x3, Pallas kernels, weight_grads(): pl.pallas_call(functools.partial(grads_kernel, a_width), out_shape=jax.Sh...  51.7 us
    ppermute x4, waiting for transfers between devices, swap_y(): return lax.ppermute(v, 'tp', ACROSS)  42.8 us
    pallas_call x2, Pallas kernels, ffn_chunk(): pl.pallas_call(functools.partial(ffn_kernel, halves), out_shape=jax.Shape...  41.1 us
    pallas_call x1, Pallas kernels, attend_back(): pl.pallas_call(attend_back_kernel, out_shape=jax.ShapeDtypeStruct((rows,...  33.7 us
    ppermute x3, waiting for transfers between devices, ring_over(): pieces.append(lax.ppermute(pieces[-1], 'fsdp', cycle))  30.5 us
  transfers between devices with their start and end apart: 72, of which 31 were waited for; matrix products, arithmetic and copies ran while one was open for 18% of the time, Pallas kernels for 29%

profile of v2, /device:TPU:0, one launch (start us, length us, event | category | flops | bytes accessed | tf_op | source)
XLA Modules:
  0.0 764.5 jit_solution(5000306243571890173)
XLA Ops:
  8.8 4.1 collective-permute-start.4
  24.8 17.0 %collective-permute-done = bf16[512,640]{1,0:T(8,128)(2,1)} collective-permute-done((bf16[512,640]{1,0:T(8,128)(2,1)S(1)}, bf16[512,640]{1,0:T(8,128)(2,1)}, u32[]{:S(2)}, u32[]{:S(2)}) %collective-permute-start) | collective-permute-done | bytes 655392 | tf_op jit(solution)/shard_map/ppermute | solution.py:506
  50.6 5.6 negate_select_fusion
  56.7 9.4 %collective-permute-done.1 = bf16[512,640]{1,0:T(8,128)(2,1)S(1)} collective-permute-done((bf16[512,640]{1,0:T(8,128)(2,1)}, bf16[512,640]{1,0:T(8,128)(2,1)S(1)}, u32[]{:S(2)}, u32[]{:S(2)}) %collective-permute-start.1) | collective-permute-done | bytes 655392 | tf_op jit(solution)/shard_map/ppermute | solution.py:506
  66.1 5.1 collective-permute-done.7
  79.1 4.2 collective-permute-done.2
  84.4 4.7 pad_maximum_fusion.low_ref.yl_ref
  89.1 3.8 pad_maximum_fusion.1.high_ref.yh_ref
  93.3 10.8 %qkv.1.q_ref.kv_ref = bf16[2048,384]{1,0:T(8,128)(2,1)} custom-call(bf16[1024,2048]{1,0:T(8,128)(2,1)} %pad_maximum_fusion.low_ref.yl_ref, bf16[1024,2048]{1,0:T(8,128)(2,1)} %pad_maximum_fusion.1.high_ref.yh_ref, bf16[2048,640]{1,0:T(8,128)(2,1)} %copy-done, bf16[2048,640]{1,0:T(8,128)(2,1)} %copy-done, f32[2048,128]{1,0:T(8,128)} %get-tuple-element.47.cos_ref, ...), custom_call_target="tpu_custom_call" | custom-call | flops 1 | bytes 1 | tf_op jit(solution)/shard_map/qkv/pallas_call | solution.py:135
  104.1 4.0 collective-permute-done.12
  113.2 22.0 %attend.1.refs_0_.h_ref.a_ref = f32[2048,384]{1,0:T(8,128)} custom-call(s32[8]{0:T(128)} %select_reduce_fusion.2.place, s32[8]{0:T(128)} %and_select_fusion.2.first, bf16[2048,384]{1,0:T(8,128)(2,1)} %qkv.1.q_ref.kv_ref, bf16[2048,384]{1,0:T(8,128)(2,1)} %qkv.1.q_ref.kv_ref, s32[2048,1]{1,0:T(8,128)} %copy.28.start_ref), custom_call_target="tpu_custom_call" | custom-call | flops 1 | bytes 1 | tf_op jit(solution)/shard_map/attend/pallas_call | solution.py:355
  146.7 7.0 back.4
  153.6 3.7 fusion.32
  167.0 23.1 %collective-permute-done.22 = bf16[512,2048]{1,0:T(8,128)(2,1)} collective-permute-done((bf16[512,2048]{1,0:T(8,128)(2,1)S(1)}, bf16[512,2048]{1,0:T(8,128)(2,1)}, u32[]{:S(2)}, u32[]{:S(2)}) %collective-permute-start.22) | collective-permute-done | bytes 2097184 | tf_op jit(solution)/shard_map/ppermute | solution.py:63
  193.7 10.7 %all-gather.3.cloned.1.call-done.w_ref.refs_2_ = bf16[2048,1536]{1,0:T(8,128)(2,1)} async-done(((bf16[512,1536]{1,0:T(8,128)(2,1)}), bf16[2048,1536]{1,0:T(8,128)(2,1)}) %all-gather.3.cloned.1.call-update) | async-done | bytes 6291472 | tf_op jit(solution)/shard_map/all_gather | solution.py:654
  206.0 13.3 %collective-permute-done.23 = bf16[256,2048]{1,0:T(8,128)(2,1)S(1)} collective-permute-done((bf16[256,2048]{1,0:T(8,128)(2,1)S(1)}, bf16[256,2048]{1,0:T(8,128)(2,1)S(1)}, u32[]{:S(2)}, u32[]{:S(2)}) %collective-permute-start.23) | collective-permute-done | bytes 1048608 | tf_op jit(solution)/shard_map/ppermute | solution.py:59
  223.2 13.3 %collective-permute-done.24 = bf16[256,2048]{1,0:T(8,128)(2,1)S(1)} collective-permute-done((bf16[256,2048]{1,0:T(8,128)(2,1)S(1)}, bf16[256,2048]{1,0:T(8,128)(2,1)S(1)}, u32[]{:S(2)}, u32[]{:S(2)}) %collective-permute-start.24) | collective-permute-done | bytes 1048608 | tf_op jit(solution)/shard_map/ppermute | solution.py:59
  238.8 24.0 %collective-permute-done.25 = bf16[512,2048]{1,0:T(8,128)(2,1)S(1)} collective-permute-done((bf16[512,2048]{1,0:T(8,128)(2,1)S(1)}, bf16[512,2048]{1,0:T(8,128)(2,1)S(1)}, u32[]{:S(2)}, u32[]{:S(2)}) %collective-permute-start.25) | collective-permute-done | bytes 2097184 | tf_op jit(solution)/shard_map/ppermute | solution.py:63
  269.5 20.6 %ffn.2.a_ref.b_ref.refs_0_ = bf16[2048,1536]{1,0:T(8,128)(2,1)} custom-call(bf16[1024,2048]{1,0:T(8,128)(2,1)} %pad_maximum_fusion.2.xl_ref, bf16[1024,2048]{1,0:T(8,128)(2,1)} %copy-done.1, bf16[1024,2048]{1,0:T(8,128)(2,1)} %constant_dynamic-update-slice_fusion.cl_ref.yl_ref, bf16[1024,2048]{1,0:T(8,128)(2,1)} %constant_dynamic-update-slice_fusion.3.ch_ref.yh_ref, ...), custom_call_target="tpu_custom_call" | custom-call | flops 1 | bytes 1 | tf_op jit(solution)/shard_map/ffn/pallas_call | solution.py:176
  290.1 19.5 %weight_grads.3 = bf16[2048,1536]{1,0:T(8,128)(2,1)} custom-call(bf16[1024,2048]{1,0:T(8,128)(2,1)} %pad_maximum_fusion.2.xl_ref, bf16[1024,2048]{1,0:T(8,128)(2,1)} %copy-done.1, bf16[1024,2048]{1,0:T(8,128)(2,1)} %constant_dynamic-update-slice_fusion.cl_ref.yl_ref, bf16[1024,2048]{1,0:T(8,128)(2,1)} %constant_dynamic-update-slice_fusion.3.ch_ref.yh_ref, ...), custom_call_target="tpu_custom_call" | custom-call | flops 1 | bytes 1 | tf_op jit(solution)/shard_map/weight_grads/pallas_call | solution.py:212
  310.1 9.4 %all-gather.5.cloned.1.call-done.w_ref.refs_3_ = bf16[2048,1536]{1,0:T(8,128)(2,1)} async-done(((bf16[512,1536]{1,0:T(8,128)(2,1)}), bf16[2048,1536]{1,0:T(8,128)(2,1)}) %all-gather.5.cloned.1.call-update) | async-done | bytes 6291472 | tf_op jit(solution)/shard_map/all_gather | solution.py:654
  319.5 20.5 %ffn.3.refs_1_.a_ref.b_ref = bf16[2048,1536]{1,0:T(8,128)(2,1)} custom-call(bf16[1024,2048]{1,0:T(8,128)(2,1)} %pad_maximum_fusion.2.xl_ref, bf16[1024,2048]{1,0:T(8,128)(2,1)} %copy-done.1, bf16[1024,2048]{1,0:T(8,128)(2,1)} %constant_dynamic-update-slice_fusion.cl_ref.yl_ref, bf16[1024,2048]{1,0:T(8,128)(2,1)} %constant_dynamic-update-slice_fusion.3.ch_ref.yh_ref, ...), custom_call_target="tpu_custom_call" | custom-call | flops 1 | bytes 1 | tf_op jit(solution)/shard_map/ffn/pallas_call | solution.py:176
  340.0 23.7 %back.6 = bf16[2048,2048]{1,0:T(8,128)(2,1)} custom-call(bf16[2048,1536]{1,0:T(8,128)(2,1)} %ffn.2.a_ref.b_ref.refs_0_, bf16[2048,1536]{1,0:T(8,128)(2,1)} %ffn.3.refs_1_.a_ref.b_ref, bf16[2048,1536]{1,0:T(8,128)(2,1)} %all-gather.3.cloned.1.call-done.w_ref.refs_2_, bf16[2048,1536]{1,0:T(8,128)(2,1)} %all-gather.5.cloned.1.call-done.w_ref.refs_3_), custom_call_target="tpu_custom_call" | custom-call | flops 1 | bytes 1 | tf_op jit(solution)/shard_map/back/pallas_call | solution.py:248
  363.7 3.7 fusion.31
  371.5 3.9 slice_add_fusion.2
  377.4 19.5 %weight_grads.4 = bf16[2048,1536]{1,0:T(8,128)(2,1)} custom-call(bf16[1024,2048]{1,0:T(8,128)(2,1)} %pad_maximum_fusion.2.xl_ref, bf16[1024,2048]{1,0:T(8,128)(2,1)} %copy-done.1, bf16[1024,2048]{1,0:T(8,128)(2,1)} %constant_dynamic-update-slice_fusion.cl_ref.yl_ref, bf16[1024,2048]{1,0:T(8,128)(2,1)} %constant_dynamic-update-slice_fusion.3.ch_ref.yh_ref, ...), custom_call_target="tpu_custom_call" | custom-call | flops 1 | bytes 1 | tf_op jit(solution)/shard_map/weight_grads/pallas_call | solution.py:212
  396.8 4.9 collective-permute-done.34
  401.7 4.1 fusion.11
  409.7 13.5 %collective-permute-done.35 = bf16[256,2048]{1,0:T(8,128)(2,1)S(1)} collective-permute-done((bf16[256,2048]{1,0:T(8,128)(2,1)}, bf16[256,2048]{1,0:T(8,128)(2,1)S(1)}, u32[]{:S(2)}, u32[]{:S(2)}) %collective-permute-start.35) | collective-permute-done | bytes 1048608 | tf_op jit(solution)/shard_map/ppermute | solution.py:59
  425.3 3.6 fusion.27
  430.4 13.7 %back.5 = bf16[2048,2048]{1,0:T(8,128)(2,1)} custom-call(bf16[2048,1536]{1,0:T(8,128)(2,1)} %ffn.2.a_ref.b_ref.refs_0_, bf16[2048,1536]{1,0:T(8,128)(2,1)} %ffn.3.refs_1_.a_ref.b_ref, bf16[2048,1536]{1,0:T(8,128)(2,1)} %all-gather.3.cloned.1.call-done.w_ref.refs_2_, bf16[2048,1536]{1,0:T(8,128)(2,1)} %all-gather.5.cloned.1.call-done.w_ref.refs_3_), custom_call_target="tpu_custom_call" | custom-call | flops 1 | bytes 1 | tf_op jit(solution)/shard_map/back/pallas_call | solution.py:248
  447.8 24.0 %collective-permute-done.39 = bf16[512,2048]{1,0:T(8,128)(2,1)S(1)} collective-permute-done((bf16[512,2048]{1,0:T(8,128)(2,1)S(1)}, bf16[512,2048]{1,0:T(8,128)(2,1)S(1)}, u32[]{:S(2)}, u32[]{:S(2)}) %collective-permute-start.39) | collective-permute-done | bytes 2097184 | tf_op jit(solution)/shard_map/ppermute | solution.py:63
  483.4 7.1 front.1.d_ref
  490.5 4.0 maximum_add_fusion.1
  494.5 33.7 %attend_back.1.refs_0_.refs_1_.b_ref = bf16[2048,384]{1,0:T(8,128)(2,1)} custom-call(s32[8]{0:T(128)} %select_reduce_fusion.2.place, s32[8]{0:T(128)} %and_select_fusion.2.first, bf16[2048,384]{1,0:T(8,128)(2,1)} %qkv.1.q_ref.kv_ref, bf16[2048,256]{1,0:T(8,128)(2,1)} %front.1.d_ref, f32[2048,384]{1,0:T(8,128)} %attend.1.refs_0_.h_ref.a_ref, ...), custom_call_target="tpu_custom_call" | custom-call | flops 1 | bytes 1 | tf_op jit(solution)/shard_map/attend_back/pallas_call | solution.py:452
  528.2 8.0 %back.7 = bf16[2048,2048]{1,0:T(8,128)(2,1)} custom-call(bf16[2048,384]{1,0:T(8,128)(2,1)} %attend_back.1.refs_0_.refs_1_.b_ref, bf16[2048,384]{1,0:T(8,128)(2,1)} %attend_back.1.refs_0_.refs_1_.b_ref, bf16[2048,640]{1,0:T(8,128)(2,1)} %copy-done, bf16[2048,640]{1,0:T(8,128)(2,1)} %copy-done), custom_call_target="tpu_custom_call" | custom-call | flops 1 | bytes 1 | tf_op jit(solution)/shard_map/back/pallas_call | solution.py:248
  536.2 4.1 fusion.29
  544.5 3.8 slice_add_fusion.1
  551.4 12.8 %weight_grads.5 = bf16[2048,640]{1,0:T(8,128)(2,1)} custom-call(bf16[1024,2048]{1,0:T(8,128)(2,1)} %pad_maximum_fusion.3.low_ref.xl_ref, bf16[1024,2048]{1,0:T(8,128)(2,1)} %copy-done.2, bf16[1024,2048]{1,0:T(8,128)(2,1)} %pad_maximum_fusion.low_ref.yl_ref, bf16[1024,2048]{1,0:T(8,128)(2,1)} %pad_maximum_fusion.1.high_ref.yh_ref, ...), custom_call_target="tpu_custom_call" | custom-call | flops 1 | bytes 1 | tf_op jit(solution)/shard_map/weight_grads/pallas_call | solution.py:212
  569.5 5.2 collective-permute-done.65
  575.8 12.1 %collective-permute-done.66 = f32[512]{0:T(512)S(1)} collective-permute-done((f32[512]{0:T(512)S(1)}, f32[512]{0:T(512)S(1)}, u32[]{:S(2)}, u32[]{:S(2)}) %collective-permute-start.66) | collective-permute-done | bytes 2080 | tf_op jit(solution)/shard_map/ppermute | solution.py:55
  589.1 20.1 %collective-permute-start.42 = (bf16[256,2048]{1,0:T(8,128)(2,1)}, bf16[256,2048]{1,0:T(8,128)(2,1)S(1)}, u32[]{:S(2)}, u32[]{:S(2)}) collective-permute-start(bf16[256,2048]{1,0:T(8,128)(2,1)} %get-tuple-element.87), channel_id=1, source_target_pairs={{0,1},{1,0},{2,3},{3,2},{4,5},{5,4},{6,7},{7,6},{8,9},{9,8},{10,11... | collective-permute-start | bytes 3145736 | tf_op jit(solution)/shard_map/ppermute | solution.py:478
  610.1 4.1 fusion.10
  618.3 3.9 fusion.13
  623.2 46.1 %collective-permute-done.55 = bf16[256,2048]{1,0:T(8,128)(2,1)S(1)} collective-permute-done((bf16[256,2048]{1,0:T(8,128)(2,1)S(1)}, bf16[256,2048]{1,0:T(8,128)(2,1)S(1)}, u32[]{:S(2)}, u32[]{:S(2)}) %collective-permute-start.55) | collective-permute-done | bytes 1048608 | tf_op jit(solution)/shard_map/ppermute | solution.py:59
  674.1 19.1 %collective-permute-done.56 = bf16[256,2048]{1,0:T(8,128)(2,1)S(1)} collective-permute-done((bf16[256,2048]{1,0:T(8,128)(2,1)S(1)}, bf16[256,2048]{1,0:T(8,128)(2,1)S(1)}, u32[]{:S(2)}, u32[]{:S(2)}) %collective-permute-start.56) | collective-permute-done | bytes 1048608 | tf_op jit(solution)/shard_map/ppermute | solution.py:51
  701.2 18.5 %collective-permute-done.50 = bf16[256,2048]{1,0:T(8,128)(2,1)S(1)} collective-permute-done((bf16[256,2048]{1,0:T(8,128)(2,1)S(1)}, bf16[256,2048]{1,0:T(8,128)(2,1)S(1)}, u32[]{:S(2)}, u32[]{:S(2)}) %collective-permute-start.50) | collective-permute-done | bytes 1048608 | tf_op jit(solution)/shard_map/ppermute | solution.py:51
  742.0 10.6 %collective-permute-done.61 = f32[512]{0:T(512)S(1)} collective-permute-done((f32[512]{0:T(512)S(1)}, f32[512]{0:T(512)S(1)}, u32[]{:S(2)}, u32[]{:S(2)}) %collective-permute-start.61) | collective-permute-done | bytes 2080 | tf_op jit(solution)/shard_map/ppermute | solution.py:55
  (331 shorter events, 166.2 us)
Async XLA Ops:
  7.2 197.1 %all-gather.3.cloned.1.call-start = ((), (), s32[]{:S(2)}) async-start(), calls=%async_computation.3 | async-start | bytes 7864320 | tf_op jit(solution)/shard_map/all_gather | solution.py:654
  22.0 19.8 %collective-permute-start.6 = (bf16[256,2048]{1,0:T(8,128)(2,1)}, bf16[256,2048]{1,0:T(8,128)(2,1)}, u32[]{:S(2)}, u32[]{:S(2)}) collective-permute-start(bf16[256,2048]{1,0:T(8,128)(2,1)} %fusion.4), channel_id=1, source_target_pairs={{0,4},{1,3},{2,6},{3,1},{4,0},{5,7},{6,2},{7,5},{8,12},{9,11},{10,... | collective-permute-start | bytes 3145736 | tf_op jit(solution)/shard_map/ppermute | solution.py:59
  24.4 17.3 %collective-permute-start = (bf16[512,640]{1,0:T(8,128)(2,1)S(1)}, bf16[512,640]{1,0:T(8,128)(2,1)}, u32[]{:S(2)}, u32[]{:S(2)}) collective-permute-start(bf16[512,640]{1,0:T(8,128)(2,1)S(1)} %get-tuple-element.80), channel_id=1, source_target_pairs={{0,8},{8,16},{16,24},{24,0},{1,9},{9,17},{17,25},{25,1},{2,10},{10... | collective-permute-start | bytes 1966088 | tf_op jit(solution)/shard_map/ppermute | solution.py:506
  44.8 26.4 %collective-permute-start.7 = (bf16[512,2048]{1,0:T(8,128)(2,1)}, bf16[512,2048]{1,0:T(8,128)(2,1)}, u32[]{:S(2)}, u32[]{:S(2)}) collective-permute-start(bf16[512,2048]{1,0:T(8,128)(2,1)} %pad_maximum_fusion.9), channel_id=1, source_target_pairs={{0,2},{1,5},{2,0},{3,7},{4,6},{5,1},{6,4},{7,3},{8,10},{9,13},{10,... | collective-permute-start | bytes 6291464 | tf_op jit(solution)/shard_map/ppermute | solution.py:63
  47.9 18.2 %collective-permute-start.1 = (bf16[512,640]{1,0:T(8,128)(2,1)}, bf16[512,640]{1,0:T(8,128)(2,1)S(1)}, u32[]{:S(2)}, u32[]{:S(2)}) collective-permute-start(bf16[512,640]{1,0:T(8,128)(2,1)} %collective-permute-done), channel_id=1, source_target_pairs={{0,8},{8,16},{16,24},{24,0},{1,9},{9,17},{17,25},{25,1},{2,10},{10... | collective-permute-start | bytes 1966088 | tf_op jit(solution)/shard_map/ppermute | solution.py:506
  56.2 32.9 %collective-permute-start.8 = (bf16[256,2048]{1,0:T(8,128)(2,1)}, bf16[256,2048]{1,0:T(8,128)(2,1)}, u32[]{:S(2)}, u32[]{:S(2)}) collective-permute-start(bf16[256,2048]{1,0:T(8,128)(2,1)} %fusion.4), channel_id=1, source_target_pairs={{0,1},{1,0},{2,3},{3,2},{4,5},{5,4},{6,7},{7,6},{8,9},{9,8},{10,11... | collective-permute-start | bytes 3145736 | tf_op jit(solution)/shard_map/ppermute | solution.py:46
  56.2 32.9 %collective-permute-start.9 = (bf16[256,2048]{1,0:T(8,128)(2,1)}, bf16[256,2048]{1,0:T(8,128)(2,1)}, u32[]{:S(2)}, u32[]{:S(2)}) collective-permute-start(bf16[256,2048]{1,0:T(8,128)(2,1)} %collective-permute-done.6), channel_id=1, source_target_pairs={{0,1},{1,0},{2,3},{3,2},{4,5},{5,4},{6,7},{7,6},{8,9},{9,8},{10,11... | collective-permute-start | bytes 3145736 | tf_op jit(solution)/shard_map/ppermute | solution.py:46
  66.1 17.1 %collective-permute-start.2 = (bf16[512,640]{1,0:T(8,128)(2,1)S(1)}, bf16[512,640]{1,0:T(8,128)(2,1)}, u32[]{:S(2)}, u32[]{:S(2)}) collective-permute-start(bf16[512,640]{1,0:T(8,128)(2,1)S(1)} %collective-permute-done.1), channel_id=1, source_target_pairs={{0,8},{8,16},{16,24},{24,0},{1,9},{9,17},{17,25},{25,1},{2,10},{10... | collective-permute-start | bytes 1966088 | tf_op jit(solution)/shard_map/ppermute | solution.py:506
  74.3 14.8 %collective-permute-start.10 = (bf16[256,2048]{1,0:T(8,128)(2,1)}, bf16[256,2048]{1,0:T(8,128)(2,1)}, u32[]{:S(2)}, u32[]{:S(2)}) collective-permute-start(bf16[256,2048]{1,0:T(8,128)(2,1)} %get-tuple-element.131), channel_id=1, source_target_pairs={{0,1},{1,0},{2,3},{3,2},{4,5},{5,4},{6,7},{7,6},{8,9},{9,8},{10,11... | collective-permute-start | bytes 3145736 | tf_op jit(solution)/shard_map/ppermute | solution.py:46
  74.3 14.8 %collective-permute-start.11 = (bf16[256,2048]{1,0:T(8,128)(2,1)}, bf16[256,2048]{1,0:T(8,128)(2,1)}, u32[]{:S(2)}, u32[]{:S(2)}) collective-permute-start(bf16[256,2048]{1,0:T(8,128)(2,1)} %get-tuple-element.132), channel_id=1, source_target_pairs={{0,1},{1,0},{2,3},{3,2},{4,5},{5,4},{6,7},{7,6},{8,9},{9,8},{10,11... | collective-permute-start | bytes 3145736 | tf_op jit(solution)/shard_map/ppermute | solution.py:46
  92.9 226.6 %all-gather.5.cloned.1.call-start = ((), (), s32[]{:S(2)}) async-start(), calls=%async_computation.4 | async-start | bytes 7864320 | tf_op jit(solution)/shard_map/all_gather | solution.py:654
  93.2 14.9 %collective-permute-start.12 = (bf16[256,2048]{1,0:T(8,128)(2,1)S(1)}, bf16[256,2048]{1,0:T(8,128)(2,1)S(1)}, u32[]{:S(2)}, u32[]{:S(2)}) collective-permute-start(bf16[256,2048]{1,0:T(8,128)(2,1)S(1)} %copy-done.5), channel_id=1, source_target_pairs={{0,4},{1,3},{2,6},{3,1},{4,0},{5,7},{6,2},{7,5},{8,12},{9,11},{10,... | collective-permute-start | bytes 3145736 | tf_op jit(solution)/shard_map/ppermute | solution.py:59
  110.5 26.2 %collective-permute-start.13 = (bf16[512,2048]{1,0:T(8,128)(2,1)}, bf16[512,2048]{1,0:T(8,128)(2,1)S(1)}, u32[]{:S(2)}, u32[]{:S(2)}) collective-permute-start(bf16[512,2048]{1,0:T(8,128)(2,1)} %pad_maximum_fusion.10), channel_id=1, source_target_pairs={{0,2},{1,5},{2,0},{3,7},{4,6},{5,1},{6,4},{7,3},{8,10},{9,13},{10,... | collective-permute-start | bytes 6291464 | tf_op jit(solution)/shard_map/ppermute | solution.py:63
  111.2 28.4 %collective-permute-start.14 = (bf16[256,2048]{1,0:T(8,128)(2,1)S(1)}, bf16[256,2048]{1,0:T(8,128)(2,1)}, u32[]{:S(2)}, u32[]{:S(2)}) collective-permute-start(bf16[256,2048]{1,0:T(8,128)(2,1)S(1)} %copy-done.5), channel_id=1, source_target_pairs={{0,1},{1,0},{2,3},{3,2},{4,5},{5,4},{6,7},{7,6},{8,9},{9,8},{10,11... | collective-permute-start | bytes 3145736 | tf_op jit(solution)/shard_map/ppermute | solution.py:46
  163.9 26.2 %collective-permute-start.22 = (bf16[512,2048]{1,0:T(8,128)(2,1)S(1)}, bf16[512,2048]{1,0:T(8,128)(2,1)}, u32[]{:S(2)}, u32[]{:S(2)}) collective-permute-start(bf16[512,2048]{1,0:T(8,128)(2,1)S(1)} %slice_add_fusion.4), channel_id=1, source_target_pairs={{0,2},{1,5},{2,0},{3,7},{4,6},{5,1},{6,4},{7,3},{8,10},{9,13},{10,... | collective-permute-start | bytes 6291464 | tf_op jit(solution)/shard_map/ppermute | solution.py:63
  166.2 278.0 %reduce-scatter.4.cloned.1.call-start = ((), (), s32[]{:S(2)}) async-start(), calls=%async_computation.5 | async-start | bytes 7864320 | tf_op jit(solution)/shard_map/reduce_scatter | solution.py:670
  166.5 23.6 %collective-permute-start.18 = (bf16[256,2048]{1,0:T(8,128)(2,1)}, bf16[256,2048]{1,0:T(8,128)(2,1)S(1)}, u32[]{:S(2)}, u32[]{:S(2)}) collective-permute-start(bf16[256,2048]{1,0:T(8,128)(2,1)} %get-tuple-element.95), channel_id=1, source_target_pairs={{0,1},{1,0},{2,3},{3,2},{4,5},{5,4},{6,7},{7,6},{8,9},{9,8},{10,11... | collective-permute-start | bytes 3145736 | tf_op jit(solution)/shard_map/ppermute | solution.py:478
  166.5 23.6 %collective-permute-start.19 = (bf16[256,2048]{1,0:T(8,128)(2,1)S(1)}, bf16[256,2048]{1,0:T(8,128)(2,1)S(1)}, u32[]{:S(2)}, u32[]{:S(2)}) collective-permute-start(bf16[256,2048]{1,0:T(8,128)(2,1)S(1)} %get-tuple-element.98), channel_id=1, source_target_pairs={{0,1},{1,0},{2,3},{3,2},{4,5},{5,4},{6,7},{7,6},{8,9},{9,8},{10,11... | collective-permute-start | bytes 3145736 | tf_op jit(solution)/shard_map/ppermute | solution.py:478
  204.4 14.9 %collective-permute-start.23 = (bf16[256,2048]{1,0:T(8,128)(2,1)S(1)}, bf16[256,2048]{1,0:T(8,128)(2,1)S(1)}, u32[]{:S(2)}, u32[]{:S(2)}) collective-permute-start(bf16[256,2048]{1,0:T(8,128)(2,1)S(1)} %slice.217), channel_id=1, source_target_pairs={{0,4},{1,3},{2,6},{3,1},{4,0},{5,7},{6,2},{7,5},{8,12},{9,11},{10,... | collective-permute-start | bytes 3145736 | tf_op jit(solution)/shard_map/ppermute | solution.py:59
  221.7 14.9 %collective-permute-start.24 = (bf16[256,2048]{1,0:T(8,128)(2,1)S(1)}, bf16[256,2048]{1,0:T(8,128)(2,1)S(1)}, u32[]{:S(2)}, u32[]{:S(2)}) collective-permute-start(bf16[256,2048]{1,0:T(8,128)(2,1)S(1)} %multiply_convert_fusion), channel_id=1, source_target_pairs={{0,4},{1,3},{2,6},{3,1},{4,0},{5,7},{6,2},{7,5},{8,12},{9,11},{10,... | collective-permute-start | bytes 3145736 | tf_op jit(solution)/shard_map/ppermute | solution.py:59
  236.8 26.1 %collective-permute-start.25 = (bf16[512,2048]{1,0:T(8,128)(2,1)S(1)}, bf16[512,2048]{1,0:T(8,128)(2,1)S(1)}, u32[]{:S(2)}, u32[]{:S(2)}) collective-permute-start(bf16[512,2048]{1,0:T(8,128)(2,1)S(1)} %pad_maximum_fusion.11), channel_id=1, source_target_pairs={{0,2},{1,5},{2,0},{3,7},{4,6},{5,1},{6,4},{7,3},{8,10},{9,13},{10,... | collective-permute-start | bytes 6291464 | tf_op jit(solution)/shard_map/ppermute | solution.py:63
  238.3 25.4 %collective-permute-start.26 = (bf16[256,2048]{1,0:T(8,128)(2,1)S(1)}, bf16[256,2048]{1,0:T(8,128)(2,1)S(1)}, u32[]{:S(2)}, u32[]{:S(2)}) collective-permute-start(bf16[256,2048]{1,0:T(8,128)(2,1)S(1)} %multiply_convert_fusion), channel_id=1, source_target_pairs={{0,1},{1,0},{2,3},{3,2},{4,5},{5,4},{6,7},{7,6},{8,9},{9,8},{10,11... | collective-permute-start | bytes 3145736 | tf_op jit(solution)/shard_map/ppermute | solution.py:46
  238.3 25.5 %collective-permute-start.27 = (bf16[256,2048]{1,0:T(8,128)(2,1)S(1)}, bf16[256,2048]{1,0:T(8,128)(2,1)S(1)}, u32[]{:S(2)}, u32[]{:S(2)}) collective-permute-start(bf16[256,2048]{1,0:T(8,128)(2,1)S(1)} %collective-permute-done.24), channel_id=1, source_target_pairs={{0,1},{1,0},{2,3},{3,2},{4,5},{5,4},{6,7},{7,6},{8,9},{9,8},{10,11... | collective-permute-start | bytes 3145736 | tf_op jit(solution)/shard_map/ppermute | solution.py:46
  309.6 254.6 %reduce-scatter.6.cloned.1.call-start = ((), (), s32[]{:S(2)}) async-start(), calls=%async_computation.6 | async-start | bytes 7864320 | tf_op jit(solution)/shard_map/reduce_scatter | solution.py:670
  375.4 26.4 %collective-permute-start.34 = (bf16[512,2048]{1,0:T(8,128)(2,1)}, bf16[512,2048]{1,0:T(8,128)(2,1)}, u32[]{:S(2)}, u32[]{:S(2)}) collective-permute-start(bf16[512,2048]{1,0:T(8,128)(2,1)} %slice_add_fusion.2), channel_id=1, source_target_pairs={{0,2},{1,5},{2,0},{3,7},{4,6},{5,1},{6,4},{7,3},{8,10},{9,13},{10,... | collective-permute-start | bytes 6291464 | tf_op jit(solution)/shard_map/ppermute | solution.py:63
  376.8 24.9 %collective-permute-start.30 = (bf16[256,2048]{1,0:T(8,128)(2,1)}, bf16[256,2048]{1,0:T(8,128)(2,1)}, u32[]{:S(2)}, u32[]{:S(2)}) collective-permute-start(bf16[256,2048]{1,0:T(8,128)(2,1)} %get-tuple-element.91), channel_id=1, source_target_pairs={{0,1},{1,0},{2,3},{3,2},{4,5},{5,4},{6,7},{7,6},{8,9},{9,8},{10,11... | collective-permute-start | bytes 3145736 | tf_op jit(solution)/shard_map/ppermute | solution.py:478
  376.8 24.9 %collective-permute-start.31 = (bf16[256,2048]{1,0:T(8,128)(2,1)S(1)}, bf16[256,2048]{1,0:T(8,128)(2,1)}, u32[]{:S(2)}, u32[]{:S(2)}) collective-permute-start(bf16[256,2048]{1,0:T(8,128)(2,1)S(1)} %get-tuple-element.94), channel_id=1, source_target_pairs={{0,1},{1,0},{2,3},{3,2},{4,5},{5,4},{6,7},{7,6},{8,9},{9,8},{10,11... | collective-permute-start | bytes 3145736 | tf_op jit(solution)/shard_map/ppermute | solution.py:478
  408.2 15.0 %collective-permute-start.35 = (bf16[256,2048]{1,0:T(8,128)(2,1)}, bf16[256,2048]{1,0:T(8,128)(2,1)S(1)}, u32[]{:S(2)}, u32[]{:S(2)}) collective-permute-start(bf16[256,2048]{1,0:T(8,128)(2,1)} %slice.228), channel_id=1, source_target_pairs={{0,4},{1,3},{2,6},{3,1},{4,0},{5,7},{6,2},{7,5},{8,12},{9,11},{10,... | collective-permute-start | bytes 3145736 | tf_op jit(solution)/shard_map/ppermute | solution.py:59
  409.7 319.7 %reduce-scatter.8.cloned.1.call-start = ((), (), s32[]{:S(2)}) async-start(), calls=%async_computation.7 | async-start | bytes 3276800 | tf_op jit(solution)/shard_map/reduce_scatter | solution.py:706
  429.0 15.2 %collective-permute-start.37 = (bf16[256,2048]{1,0:T(8,128)(2,1)S(1)}, bf16[256,2048]{1,0:T(8,128)(2,1)}, u32[]{:S(2)}, u32[]{:S(2)}) collective-permute-start(bf16[256,2048]{1,0:T(8,128)(2,1)S(1)} %get-tuple-element.73), channel_id=1, source_target_pairs={{0,4},{1,3},{2,6},{3,1},{4,0},{5,7},{6,2},{7,5},{8,12},{9,11},{10,... | collective-permute-start | bytes 3145736 | tf_op jit(solution)/shard_map/ppermute | solution.py:59
  445.7 26.1 %collective-permute-start.39 = (bf16[512,2048]{1,0:T(8,128)(2,1)S(1)}, bf16[512,2048]{1,0:T(8,128)(2,1)S(1)}, u32[]{:S(2)}, u32[]{:S(2)}) collective-permute-start(bf16[512,2048]{1,0:T(8,128)(2,1)S(1)} %pad_maximum_fusion.12), channel_id=1, source_target_pairs={{0,2},{1,5},{2,0},{3,7},{4,6},{5,1},{6,4},{7,3},{8,10},{9,13},{10,... | collective-permute-start | bytes 6291464 | tf_op jit(solution)/shard_map/ppermute | solution.py:63
  447.3 25.3 %collective-permute-start.36 = (bf16[256,2048]{1,0:T(8,128)(2,1)S(1)}, bf16[256,2048]{1,0:T(8,128)(2,1)S(1)}, u32[]{:S(2)}, u32[]{:S(2)}) collective-permute-start(bf16[256,2048]{1,0:T(8,128)(2,1)S(1)} %get-tuple-element.73), channel_id=1, source_target_pairs={{0,1},{1,0},{2,3},{3,2},{4,5},{5,4},{6,7},{7,6},{8,9},{9,8},{10,11... | collective-permute-start | bytes 3145736 | tf_op jit(solution)/shard_map/ppermute | solution.py:46
  447.3 25.4 %collective-permute-start.38 = (bf16[256,2048]{1,0:T(8,128)(2,1)}, bf16[256,2048]{1,0:T(8,128)(2,1)S(1)}, u32[]{:S(2)}, u32[]{:S(2)}) collective-permute-start(bf16[256,2048]{1,0:T(8,128)(2,1)} %collective-permute-done.37), channel_id=1, source_target_pairs={{0,1},{1,0},{2,3},{3,2},{4,5},{5,4},{6,7},{7,6},{8,9},{9,8},{10,11... | collective-permute-start | bytes 3145736 | tf_op jit(solution)/shard_map/ppermute | solution.py:46
  548.3 40.8 %collective-permute-start.54 = (bf16[512,2048]{1,0:T(8,128)(2,1)}, bf16[512,2048]{1,0:T(8,128)(2,1)}, u32[]{:S(2)}, u32[]{:S(2)}) collective-permute-start(bf16[512,2048]{1,0:T(8,128)(2,1)} %slice_add_fusion.1), channel_id=1, source_target_pairs={{0,2},{1,5},{2,0},{3,7},{4,6},{5,1},{6,4},{7,3},{8,10},{9,13},{10,... | collective-permute-start | bytes 6291464 | tf_op jit(solution)/shard_map/ppermute | solution.py:63
  549.8 59.4 %collective-permute-start.52 = (bf16[256,2048]{1,0:T(8,128)(2,1)}, bf16[256,2048]{1,0:T(8,128)(2,1)}, u32[]{:S(2)}, u32[]{:S(2)}) collective-permute-start(bf16[256,2048]{1,0:T(8,128)(2,1)} %get-tuple-element.83), channel_id=1, source_target_pairs={{0,1},{1,0},{2,3},{3,2},{4,5},{5,4},{6,7},{7,6},{8,9},{9,8},{10,11... | collective-permute-start | bytes 3145736 | tf_op jit(solution)/shard_map/ppermute | solution.py:478
  549.8 59.5 %collective-permute-start.53 = (bf16[256,2048]{1,0:T(8,128)(2,1)}, bf16[256,2048]{1,0:T(8,128)(2,1)}, u32[]{:S(2)}, u32[]{:S(2)}) collective-permute-start(bf16[256,2048]{1,0:T(8,128)(2,1)} %get-tuple-element.84), channel_id=1, source_target_pairs={{0,1},{1,0},{2,3},{3,2},{4,5},{5,4},{6,7},{7,6},{8,9},{9,8},{10,11... | collective-permute-start | bytes 3145736 | tf_op jit(solution)/shard_map/ppermute | solution.py:478
  550.3 64.0 %collective-permute-start.62 = (bf16[512,1536]{1,0:T(8,128)(2,1)}, bf16[512,1536]{1,0:T(8,128)(2,1)}, u32[]{:S(2)}, u32[]{:S(2)}) collective-permute-start(bf16[512,1536]{1,0:T(8,128)(2,1)} %reduce-scatter.4.cloned.1.call-done), channel_id=1, source_target_pairs={{0,4},{4,0},{1,5},{5,1},{2,6},{6,2},{3,7},{7,3},{8,12},{12,8},{9,1... | collective-permute-start | bytes 4718600 | tf_op jit(solution)/shard_map/ppermute | solution.py:55
  574.7 13.3 %collective-permute-start.66 = (f32[512]{0:T(512)S(1)}, f32[512]{0:T(512)S(1)}, u32[]{:S(2)}, u32[]{:S(2)}) collective-permute-start(f32[512]{0:T(512)S(1)} %add.388), channel_id=1, source_target_pairs={{0,4},{4,0},{1,5},{5,1},{2,6},{6,2},{3,7},{7,3},{8,12},{12,8},{9,1... | collective-permute-start | bytes 6152 | tf_op jit(solution)/shard_map/ppermute | solution.py:55
  587.9 30.3 %collective-permute-start.46 = (bf16[512,2048]{1,0:T(8,128)(2,1)}, bf16[512,2048]{1,0:T(8,128)(2,1)}, u32[]{:S(2)}, u32[]{:S(2)}) collective-permute-start(bf16[512,2048]{1,0:T(8,128)(2,1)} %maximum_add_fusion.1), channel_id=1, source_target_pairs={{0,2},{1,5},{2,0},{3,7},{4,6},{5,1},{6,4},{7,3},{8,10},{9,13},{10,... | collective-permute-start | bytes 6291464 | tf_op jit(solution)/shard_map/ppermute | solution.py:63
  589.1 29.2 %collective-permute-start.42 = (bf16[256,2048]{1,0:T(8,128)(2,1)}, bf16[256,2048]{1,0:T(8,128)(2,1)S(1)}, u32[]{:S(2)}, u32[]{:S(2)}) collective-permute-start(bf16[256,2048]{1,0:T(8,128)(2,1)} %get-tuple-element.87), channel_id=1, source_target_pairs={{0,1},{1,0},{2,3},{3,2},{4,5},{5,4},{6,7},{7,6},{8,9},{9,8},{10,11... | collective-permute-start | bytes 3145736 | tf_op jit(solution)/shard_map/ppermute | solution.py:478
  609.3 63.3 %collective-permute-start.63 = (bf16[512,1536]{1,0:T(8,128)(2,1)}, bf16[512,1536]{1,0:T(8,128)(2,1)S(1)}, u32[]{:S(2)}, u32[]{:S(2)}) collective-permute-start(bf16[512,1536]{1,0:T(8,128)(2,1)} %reduce-scatter.6.cloned.1.call-done), channel_id=1, source_target_pairs={{0,4},{4,0},{1,5},{5,1},{2,6},{6,2},{3,7},{7,3},{8,12},{12,8},{9,1... | collective-permute-start | bytes 4718600 | tf_op jit(solution)/shard_map/ppermute | solution.py:55
  614.3 55.0 %collective-permute-start.55 = (bf16[256,2048]{1,0:T(8,128)(2,1)S(1)}, bf16[256,2048]{1,0:T(8,128)(2,1)S(1)}, u32[]{:S(2)}, u32[]{:S(2)}) collective-permute-start(bf16[256,2048]{1,0:T(8,128)(2,1)S(1)} %slice.246), channel_id=1, source_target_pairs={{0,4},{1,3},{2,6},{3,1},{4,0},{5,7},{6,2},{7,5},{8,12},{9,11},{10,... | collective-permute-start | bytes 3145736 | tf_op jit(solution)/shard_map/ppermute | solution.py:59
  622.3 71.3 %collective-permute-start.49 = (bf16[256,2048]{1,0:T(8,128)(2,1)S(1)}, bf16[256,2048]{1,0:T(8,128)(2,1)S(1)}, u32[]{:S(2)}, u32[]{:S(2)}) collective-permute-start(bf16[256,2048]{1,0:T(8,128)(2,1)S(1)} %slice.292), channel_id=1, source_target_pairs={{0,4},{1,3},{2,6},{3,1},{4,0},{5,7},{6,2},{7,5},{8,12},{9,11},{10,... | collective-permute-start | bytes 3145736 | tf_op jit(solution)/shard_map/ppermute | solution.py:59
  670.7 22.5 %collective-permute-start.56 = (bf16[256,2048]{1,0:T(8,128)(2,1)S(1)}, bf16[256,2048]{1,0:T(8,128)(2,1)S(1)}, u32[]{:S(2)}, u32[]{:S(2)}) collective-permute-start(bf16[256,2048]{1,0:T(8,128)(2,1)S(1)} %fusion.8), channel_id=1, source_target_pairs={{0,2},{2,0},{1,3},{3,1},{4,6},{6,4},{5,7},{7,5},{8,10},{10,8},{9,1... | collective-permute-start | bytes 3145736 | tf_op jit(solution)/shard_map/ppermute | solution.py:51
  693.5 30.2 %collective-permute-start.57 = (bf16[2,256,2048]{2,1,0:T(8,128)(2,1)S(1)}, bf16[2,256,2048]{2,1,0:T(8,128)(2,1)S(1)}, u32[]{:S(2)}, u32[]{:S(2)}) collective-permute-start(bf16[2,256,2048]{2,1,0:T(8,128)(2,1)S(1)} %get-tuple-element.116), channel_id=1, source_target_pairs={{0,1},{1,0},{2,3},{3,2},{4,5},{5,4},{6,7},{7,6},{8,9},{9,8},{10,11... | collective-permute-start | bytes 6291464 | tf_op jit(solution)/shard_map/ppermute | solution.py:43
  694.1 25.6 %collective-permute-start.50 = (bf16[256,2048]{1,0:T(8,128)(2,1)S(1)}, bf16[256,2048]{1,0:T(8,128)(2,1)S(1)}, u32[]{:S(2)}, u32[]{:S(2)}) collective-permute-start(bf16[256,2048]{1,0:T(8,128)(2,1)S(1)} %add_convert_fusion), channel_id=1, source_target_pairs={{0,2},{2,0},{1,3},{3,1},{4,6},{6,4},{5,7},{7,5},{8,10},{10,8},{9,1... | collective-permute-start | bytes 3145736 | tf_op jit(solution)/shard_map/ppermute | solution.py:51
  736.1 17.1 %collective-permute-start.58 = (bf16[512,640]{1,0:T(8,128)(2,1)S(1)}, bf16[512,640]{1,0:T(8,128)(2,1)S(1)}, u32[]{:S(2)}, u32[]{:S(2)}) collective-permute-start(bf16[512,640]{1,0:T(8,128)(2,1)S(1)} %copy-done.22), channel_id=1, source_target_pairs={{0,4},{4,0},{1,5},{5,1},{2,6},{6,2},{3,7},{7,3},{8,12},{12,8},{9,1... | collective-permute-start | bytes 1966088 | tf_op jit(solution)/shard_map/ppermute | solution.py:55
  737.7 14.9 %collective-permute-start.61 = (f32[512]{0:T(512)S(1)}, f32[512]{0:T(512)S(1)}, u32[]{:S(2)}, u32[]{:S(2)}) collective-permute-start(f32[512]{0:T(512)S(1)} %add.384), channel_id=1, source_target_pairs={{0,4},{4,0},{1,5},{5,1},{2,6},{6,2},{3,7},{7,3},{8,12},{12,8},{9,1... | collective-permute-start | bytes 6152 | tf_op jit(solution)/shard_map/ppermute | solution.py:55
  (67 other events, 708.6 us)
Sparse Core Ops, SparseCore 0:
  93.1 111.2 all-gather.2
  205.9 113.5 all-gather.4
  321.8 108.9 reduce-scatter.3
  433.0 111.2 reduce-scatter.5
  588.6 70.9 reduce-scatter.7

commit v3 on v2

--- a/solution.py
+++ b/solution.py
@@ -38,13 +38,8 @@
 SECOND = joint_pairs(1)
 
 
-def swap_core(v, pieces=1):
-    if pieces == 1:
-        return lax.ppermute(v, "tp", CORE)
-    rows = v.shape[0] // pieces
-    return jnp.concatenate(
-        [lax.ppermute(v[at * rows : (at + 1) * rows], "tp", CORE) for at in range(pieces)]
-    )
+def swap_core(v):
+    return lax.ppermute(v, "tp", CORE)
 
 
 def swap_y(v):
@@ -107,13 +102,14 @@
         body(*high_refs)
 
 
-def qkv_kernel(halves, low_ref, high_ref, wq_ref, wkv_ref, cos_ref, sin_ref, o_ref):
+def qkv_kernel(halves, low_ref, high_ref, gain_ref, wq_ref, wkv_ref, cos_ref, sin_ref, o_ref):
     cos, sin = cos_ref[...], sin_ref[...]
     lane = lax.broadcasted_iota(jnp.int32, cos.shape, 1)
     first = (lane % 64) < 32
 
     def body(x_ref):
-        x = x_ref[...]
+        x = x_ref[...].astype(F32)
+        x = (x * inv_rms(x) * gain_ref[...]).astype(BF16)
         raw = jnp.dot(x, wq_ref[...], preferred_element_type=F32)
         tiles = raw.shape[1] // 128
         for tile in range(tiles):
@@ -127,7 +123,7 @@
     either(halves, body, (low_ref,), (high_ref,))
 
 
-def project_qkv(x, w, q_width, cos, sin):
+def project_qkv(x, gain, w, q_width, cos, sin):
     half_rows, depth = x[0].shape
     rows = 2 * half_rows
     width = q_width + 128
@@ -138,6 +134,7 @@
         grid=(rows // step,),
         in_specs=two_halves(step, depth, half_rows // step)
         + [
+            pl.BlockSpec((1, depth), lambda i: (0, 0)),
             pl.BlockSpec((depth, q_width), lambda i: (0, 1)),
             pl.BlockSpec((depth, 128), lambda i: (0, 2 * q_width // 128)),
             pl.BlockSpec((step, 128), lambda i: (i, 0)),
@@ -147,7 +144,7 @@
         compiler_params=params(),
         cost_estimate=cost(),
         name="qkv",
-    )(*x, w, w, cos, sin)
+    )(*x, gain, w, w, cos, sin)
 
 
 def ffn_kernel(halves, xl_ref, xh_ref, cl_ref, ch_ref, w_ref, o_ref):
@@ -240,17 +237,18 @@
     o_ref[...] = total.astype(BF16)
 
 
-def back_product(terms):
-    rows = terms[0][0].shape[0]
+def back_product(terms, part, parts):
+    rows = terms[0][0].shape[0] // parts
     depth = terms[0][2].shape[0]
-    step = 512
-    total = sum(term[4] for term in terms)
+    step = min(512, rows)
+    ahead = part * (rows // step)
     return pl.pallas_call(
         back_kernel,
         out_shape=jax.ShapeDtypeStruct((rows, depth), BF16),
         grid=(rows // step,),
         in_specs=[
-            pl.BlockSpec((step, term[4]), lambda i, column=term[1]: (i, column)) for term in terms
+            pl.BlockSpec((step, term[4]), lambda i, column=term[1]: (i + ahead, column))
+            for term in terms
         ]
         + [pl.BlockSpec((depth, term[4]), lambda i, column=term[3]: (0, column)) for term in terms],
         out_specs=pl.BlockSpec((step, depth), lambda i: (i, 0)),
@@ -473,30 +471,40 @@
     )(place, first, qkv, d_heads, heads, qkv, start, cos, sin)
 
 
-def sum_cores(part):
-    rows = part.shape[0] // 8
-    arrived = [lax.ppermute(part[at * rows : (at + 1) * rows], "tp", CORE) for at in range(4, 8)]
-    far = part[2 * rows : 4 * rows] + jnp.concatenate(arrived[2:])
-    near = part[: 2 * rows] + jnp.concatenate(arrived[:2])
-    return far, near
-
-
-def sum_chips(far, near, behind=(), beside=()):
+def sum_cores(terms, pieces=2, *held):
+    sent = [back_product(terms, 2 * pieces - 1 - at, 2 * pieces) for at in range(pieces)]
+    arrived = [swap_core(after(piece, *held)) for piece in sent]
+    mine = back_product(terms, 0, 2)
+    rows = mine.shape[0] // 2
+    if pieces == 1:
+        return mine[rows:] + arrived[0][rows:], mine[:rows] + arrived[0][:rows]
+    return mine[rows:] + arrived[0], mine[:rows] + arrived[1]
+
+
+def y_first(far, near, core):
     rows = near.shape[0] // 2
-    near = near + after(swap_second(far), *behind)
+    first, second = near[rows:], far[:rows]
+    return (
+        jnp.concatenate([jnp.where(core == 0, second, first), far[rows:]]),
+        jnp.concatenate([near[:rows], jnp.where(core == 0, first, second)]),
+    )
+
+
+def sum_pairs(far, near, *behind):
+    return near + after(swap_second(far), *behind)
+
+
+def sum_last(near, *beside):
+    rows = near.shape[0] // 2
     near = after(near, *beside)
     return near[:rows].astype(F32) + swap_first(near[rows:]).astype(F32)
 
 
-def sum_to_owner(part, beside=()):
-    return sum_chips(*sum_cores(part), beside=beside)
-
-
 def share_rows(own, beside=()):
     beside = list(beside) + [()] * (2 - len(beside))
-    two = jnp.concatenate([own, after(swap_first(own), *beside[0])])
-    four = jnp.concatenate([two, after(swap_second(two), *beside[1])])
-    return four, swap_core(four, 4)
+    one = after(swap_first(own), *beside[0])
+    parts = (own, one, swap_second(own), after(swap_second(one), *beside[1]))
+    return jnp.concatenate(parts), jnp.concatenate([swap_core(part) for part in parts])
 
 
 def ring_over(shard, count):
@@ -526,9 +534,10 @@
     ]
 
 
-def share_in_ctx(own, y, core):
-    pair = jnp.stack([own, swap_y(own)])
-    four = jnp.stack([pair, swap_core(pair)])
+def share_in_ctx(own, beside, y, core):
+    pair = jnp.stack([own, beside])
+    other = jnp.stack([swap_core(own), swap_core(beside)])
+    four = jnp.stack([pair, other])
     four = jnp.where(y == 1, four[:, ::-1], four)
     four = jnp.where(core == 1, four[::-1], four)
     return four.transpose(1, 0, 2, 3).reshape(-1, own.shape[1])
@@ -638,16 +647,14 @@
     sin = jnp.where((lane % 64 < 32)[None], -jnp.sin(angles), jnp.sin(angles))
     start_column = start_of[:, None]
 
-    tokens_own = lax.dynamic_slice_in_dim(tokens, tp * own_rows, own_rows, 0).astype(F32)
+    tokens_low = lax.dynamic_slice_in_dim(tokens, tp * own_rows, own_rows, 0)
     cot_low = lax.dynamic_slice_in_dim(cotangent, tp * own_rows, own_rows, 0)
-    cot_own = cot_low.astype(F32)
-    normed = share_rows(
-        (tokens_own * inv_rms(tokens_own) * gain_one).astype(BF16), [[piece] for piece in attn_ring[1:3]]
-    )
-    attn_full, first_shard, cot_low, cos, sin, *normed = lax.optimization_barrier(
-        (attn_full, after(ffn_shards[0], attn_ring[-1]), cot_low, cos, sin, *normed)
-    )
-    qkv = project_qkv(normed, attn_full, q_width, cos, sin)
+    tokens_own, cot_own = tokens_low.astype(F32), cot_low.astype(F32)
+    group_tokens = share_rows(tokens_low, [[piece] for piece in attn_ring[1:3]])
+    attn_full, first_shard, cot_low, cos, sin, gain_one, *group_tokens = lax.optimization_barrier(
+        (attn_full, ffn_shards[0], cot_low, cos, sin, gain_one, *group_tokens)
+    )
+    qkv = project_qkv(group_tokens, gain_one, attn_full, q_width, cos, sin)
     heads = attend(qkv, place, first, start_column, q_width)
     cot = share_rows(cot_low, [[qkv], [heads]])
     ffn_full = [
@@ -655,8 +662,10 @@
         for shard in (first_shard, after(ffn_shards[1], heads))
     ]
     heads = after(heads, *cot)
-    attn_part = back_product([(heads, 0, attn_full, 0, q_width)])
-    hidden = tokens_own + sum_to_owner(attn_part, ffn_full[:1])
+    attn_sum = sum_last(
+        sum_pairs(*sum_cores([(heads, 0, attn_full, 0, q_width)])), ffn_full[0]
+    )
+    hidden = tokens_own + attn_sum
     normed_two = share_rows((hidden * inv_rms(hidden) * gain_two).astype(BF16))
 
     acts = []
@@ -669,20 +678,30 @@
     reduced = [
         lax.psum_scatter(part, "fsdp", scatter_dimension=0, tiled=True) for part in grad_parts
     ]
-    d_norm_part = back_product(
-        [(acts[part], 0, ffn_full[part], 0, 2 * chunk) for part in range(CHUNKS)]
-    )
-    ffn_part = back_product([(acts[part], 2, ffn_full[part], 2, chunk) for part in range(CHUNKS)])
-    d_normed_two = sum_to_owner(d_norm_part, grad_parts)
+    d_norm_terms = [(acts[part], 0, ffn_full[part], 0, 2 * chunk) for part in range(CHUNKS)]
+    ffn_terms = [(acts[part], 2, ffn_full[part], 2, chunk) for part in range(CHUNKS)]
+    d_normed_two = sum_last(sum_pairs(*sum_cores(d_norm_terms, 1)), *grad_parts)
     d_hidden = cot_own + rms_back(hidden, gain_two, d_normed_two)
-    d_attn = share_rows(d_hidden.astype(BF16), [[ffn_part, reduced[0]]])
+    ffn_sent = [back_product(ffn_terms, at, 4) for at in (3, 2)]
+    ffn_mine = back_product(ffn_terms, 0, 2)
+    d_attn = share_rows(d_hidden.astype(BF16), [[reduced[0]], [*ffn_sent, ffn_mine]])
 
     d_heads = front_product(d_attn, attn_full, q_width, 0)
-    ffn_far, ffn_near = sum_cores(after(ffn_part, d_attn[1]))
+    arrived = [swap_core(after(piece, d_attn[1])) for piece in ffn_sent]
+    half_rows = ffn_mine.shape[0] // 2
+    ffn_far, ffn_near = y_first(
+        ffn_mine[half_rows:] + arrived[0], ffn_mine[:half_rows] + arrived[1], core
+    )
     d_heads, ffn_far, reduced[0] = lax.optimization_barrier((d_heads, ffn_far, reduced[0]))
     other_reduced = [swap_x(reduced[0])]
     d_qkv = attend_back(qkv, d_heads, heads, place, first, start_column, cos, sin)
-    d_normed_part = back_product(
+    ffn_near = ffn_near + after(swap_y(ffn_far), d_qkv)
+    d_qkv = after(d_qkv, ffn_near, other_reduced[0])
+    normed = []
+    for part in group_tokens:
+        wide = part.astype(F32)
+        normed.append((wide * inv_rms(wide) * gain_one).astype(BF16))
+    normed_far, normed_near = sum_cores(
         [
             (d_qkv, 0, attn_full, 1, q_width),
             (d_qkv, q_width // 128, attn_full, 2 * q_width // 128, 128),
@@ -691,35 +710,41 @@
     attn_grad = weight_grads(
         d_attn, heads, q_width, 0, normed, d_qkv, q_width + 128, 0
     )
-    normed_far, normed_near = sum_cores(d_normed_part)
     for part in range(1, CHUNKS):
         reduced[part] = after(reduced[part], attn_grad)
-    d_normed = sum_chips(normed_far, normed_near, beside=[attn_grad, *reduced[1:]])
+    d_normed = sum_last(sum_pairs(normed_far, normed_near), attn_grad, *reduced[1:])
     for part in range(1, CHUNKS):
         reduced[part] = after(reduced[part], d_normed)
         other_reduced.append(swap_x(reduced[part]))
-    result_own = (hidden + sum_chips(ffn_far, ffn_near, behind=[normed_far])).astype(BF16)
-    result = share_in_ctx(result_own, y, core)
+    ffn_near = after(ffn_near, normed_far)
+    ffn_sum = ffn_near[:own_rows].astype(F32) + swap_x(ffn_near[own_rows:]).astype(F32)
+    result_own = (hidden + ffn_sum).astype(BF16)
+    result = share_in_ctx(result_own, swap_y(result_own), y, core)
     tokens_grad_own = (d_hidden + rms_back(tokens_own, gain_one, d_normed)).astype(BF16)
-    tokens_grad = share_in_ctx(tokens_grad_own, y, core)
+    tokens_grad_beside = swap_y(tokens_grad_own)
+    tokens_grad = share_in_ctx(tokens_grad_own, tokens_grad_beside, y, core)
 
     attn_reduced = lax.psum_scatter(attn_grad, "fsdp", scatter_dimension=0, tiled=True)
-    attn_reduced = after(attn_reduced, tokens_grad)
-
-    def gain_grad(pairs, gain):
-        products = sum(
-            jnp.sum(mine.astype(F32) * grad.astype(F32), axis=1) for mine, grad in pairs
+    attn_reduced = after(attn_reduced, tokens_grad_beside)
+
+    def gain_part(pairs):
+        return sum(jnp.sum(mine.astype(F32) * grad.astype(F32), axis=1) for mine, grad in pairs)
+
+    gain_sums = sum_all(
+        jnp.stack(
+            [
+                gain_part([(attn_shard[:, q_width:], attn_reduced[:, q_width:])]),
+                gain_part(
+                    [
+                        (ffn_shards[part][:, : 2 * chunk], reduced[part][:, : 2 * chunk])
+                        for part in range(CHUNKS)
+                    ]
+                ),
+            ]
         )
-        return sum_all(products) / gain.astype(F32)
-
-    attn_gain_grad = gain_grad([(attn_shard[:, q_width:], attn_reduced[:, q_width:])], attn_gain)
-    ffn_gain_grad = gain_grad(
-        [
-            (ffn_shards[part][:, : 2 * chunk], reduced[part][:, : 2 * chunk])
-            for part in range(CHUNKS)
-        ],
-        ffn_gain,
-    )
+    )
+    attn_gain_grad = gain_sums[0] / attn_gain.astype(F32)
+    ffn_gain_grad = gain_sums[1] / ffn_gain.astype(F32)
 
     halves = [both_halves(mine, other, ctx) for mine, other in zip(reduced, other_reduced)]
 

time: 771 us -> 740 us (0.960)
  waiting for transfers between devices: 305 us -> 277 us
  Pallas kernels: 219 us -> 246 us
  local copies, waits for them, and re-layouts: 54.8 us -> 42.8 us
  starting transfers between devices: 66.1 us -> 55.7 us
    ppermute x8 -> x11, waiting for transfers between devices: 82.2 us -> 45.8 us  [swap_second(): return lax.ppermute(v, ('ctx', 'tp'), SECOND)]
    ppermute x32 -> x0, starting transfers between devices: 28 us -> none  [the longest x16 23.8 us: sum_cores(): lax.ppermute(part[at * rows:(at + 1) * rows], 'tp', CORE)]
    pallas_call x4 -> x11, Pallas kernels: 52.4 us -> 75.4 us  [back_product(): pl.pallas_call(back_kernel, out_shape=jax.ShapeDtypeStruct((rows, depth),...]
    slice x12 -> x5, local copies, waits for them, and re-layouts: 18.9 us -> 0.37 us  [the longest x3 0.27 us: sum_last(): return near[:rows].astype(F32) + swap_first(near[rows:]).astype(F32)]
    ppermute x8 -> x7, waiting for transfers between devices: 90.2 us -> 108 us  [swap_first(): return lax.ppermute(v, ('ctx', 'tp'), FIRST)]
    ppermute x5, waiting for transfers between devices: 22.7 us -> 40.4 us  [swap_x(): return lax.ppermute(v, 'ctx', PAIR)]
    ppermute x32 -> x0, waiting for transfers between devices: 15.5 us -> none  [the longest x16 11 us: sum_cores(): lax.ppermute(part[at * rows:(at + 1) * rows], 'tp', CORE)]
    ppermute x4, waiting for transfers between devices: 42.8 us -> 30.7 us  [swap_y(): return lax.ppermute(v, 'tp', ACROSS)]
  transfers between devices with their start and end apart: 72 -> 66, of which waited for: 31 -> 24; matrix products, arithmetic and copies ran while one was open for 18% -> 17% of each run, Pallas kernels for 29% -> 33%
where the time goes in v3:
time: 740 us; the launch traced here: 735 us
  waiting for transfers between devices  277 us (37%)
  Pallas kernels  246 us (33%)
  other arithmetic  99.7 us (13%)
  starting transfers between devices  55.7 us (8%)
  local copies, waits for them, and re-layouts  42.8 us (6%)
  between operations  14.9 us (2%)
    ppermute x7, waiting for transfers between devices, swap_first(): return lax.ppermute(v, ('ctx', 'tp'), FIRST)  108 us
    pallas_call x11, Pallas kernels, back_product(): pl.pallas_call(back_kernel, out_shape=jax.ShapeDtypeStruct((rows, depth),...  75.4 us
    pallas_call x3, Pallas kernels, weight_grads(): pl.pallas_call(functools.partial(grads_kernel, a_width), out_shape=jax.Sh...  51.7 us
    ppermute x11, waiting for transfers between devices, swap_second(): return lax.ppermute(v, ('ctx', 'tp'), SECOND)  45.8 us
    pallas_call x2, Pallas kernels, ffn_chunk(): pl.pallas_call(functools.partial(ffn_kernel, halves), out_shape=jax.Shape...  41.2 us
    ppermute x5, waiting for transfers between devices, swap_x(): return lax.ppermute(v, 'ctx', PAIR)  40.4 us
    pallas_call x1, Pallas kernels, attend_back(): pl.pallas_call(attend_back_kernel, out_shape=jax.ShapeDtypeStruct((rows,...  35.4 us
    ppermute x4, waiting for transfers between devices, swap_y(): return lax.ppermute(v, 'tp', ACROSS)  30.7 us
  transfers between devices with their start and end apart: 66, of which 24 were waited for; matrix products, arithmetic and copies ran while one was open for 17% of the time, Pallas kernels for 33%

profile of v3, /device:TPU:0, one launch (start us, length us, event | category | flops | bytes accessed | tf_op | source)
XLA Modules:
  0.0 735.4 jit_solution(13108653231147415092)
XLA Ops:
  19.9 5.6 negate_select_fusion
  25.5 9.7 %collective-permute-done = bf16[512,640]{1,0:T(8,128)(2,1)} collective-permute-done((bf16[512,640]{1,0:T(8,128)(2,1)S(1)}, bf16[512,640]{1,0:T(8,128)(2,1)}, u32[]{:S(2)}, u32[]{:S(2)}) %collective-permute-start) | collective-permute-done | bytes 655392 | tf_op jit(solution)/shard_map/ppermute | solution.py:514
  48.9 6.2 collective-permute-done.4
  55.1 4.4 collective-permute-start.5
  65.9 14.7 %collective-permute-done.2 = bf16[512,640]{1,0:T(8,128)(2,1)S(1)} collective-permute-done((bf16[512,640]{1,0:T(8,128)(2,1)}, bf16[512,640]{1,0:T(8,128)(2,1)S(1)}, u32[]{:S(2)}, u32[]{:S(2)}) %collective-permute-start.2) | collective-permute-done | bytes 655392 | tf_op jit(solution)/shard_map/ppermute | solution.py:514
  80.7 4.7 pad_maximum_fusion.low_ref
  91.3 12.0 %qkv.1.q_ref.kv_ref = bf16[2048,384]{1,0:T(8,128)(2,1)} custom-call(bf16[1024,2048]{1,0:T(8,128)(2,1)} %pad_maximum_fusion.low_ref, bf16[1024,2048]{1,0:T(8,128)(2,1)} %pad_maximum_fusion.1.high_ref, f32[1,2048]{1,0:T(1,128)} %get-tuple-element.49.gain_ref, bf16[2048,640]{1,0:T(8,128)(2,1)} %copy-done, bf16[2048,640]{1,0:T(8,128)(2,1)} %copy-done, ...), custom_call_target="tpu_custom_call" | custom-call | flops 1 | bytes 1 | tf_op jit(solution)/shard_map/qkv/pallas_call | solution.py:131
  103.3 12.1 %collective-permute-done.13 = bf16[256,2048]{1,0:T(8,128)(2,1)} collective-permute-done((bf16[256,2048]{1,0:T(8,128)(2,1)S(1)}, bf16[256,2048]{1,0:T(8,128)(2,1)}, u32[]{:S(2)}, u32[]{:S(2)}) %collective-permute-start.13) | collective-permute-done | bytes 1048608 | tf_op jit(solution)/shard_map/ppermute | solution.py:54
  119.1 22.7 %attend.1.refs_0_.h_ref.a_ref = f32[2048,384]{1,0:T(8,128)} custom-call(s32[8]{0:T(128)} %select_reduce_fusion.2.place, s32[8]{0:T(128)} %and_select_fusion.2.first, bf16[2048,384]{1,0:T(8,128)(2,1)} %qkv.1.q_ref.kv_ref, bf16[2048,384]{1,0:T(8,128)(2,1)} %qkv.1.q_ref.kv_ref, s32[2048,1]{1,0:T(8,128)} %copy.28.start_ref), custom_call_target="tpu_custom_call" | custom-call | flops 1 | bytes 1 | tf_op jit(solution)/shard_map/attend/pallas_call | solution.py:353
  152.7 3.5 back.13
  161.3 4.2 back.11
  169.1 24.5 %collective-permute-done.22 = bf16[512,2048]{1,0:T(8,128)(2,1)S(1)} collective-permute-done((bf16[512,2048]{1,0:T(8,128)(2,1)S(1)}, bf16[512,2048]{1,0:T(8,128)(2,1)S(1)}, u32[]{:S(2)}, u32[]{:S(2)}) %collective-permute-start.22) | collective-permute-done | bytes 2097184 | tf_op jit(solution)/shard_map/ppermute | solution.py:58
  193.9 8.9 %all-gather.3.cloned.1.call-done.w_ref.refs_2_ = bf16[2048,1536]{1,0:T(8,128)(2,1)} async-done(((bf16[512,1536]{1,0:T(8,128)(2,1)}), bf16[2048,1536]{1,0:T(8,128)(2,1)}) %all-gather.3.cloned.1.call-update) | async-done | bytes 6291472 | tf_op jit(solution)/shard_map/all_gather | solution.py:661
  204.4 13.3 %collective-permute-done.23 = bf16[256,2048]{1,0:T(8,128)(2,1)S(1)} collective-permute-done((bf16[256,2048]{1,0:T(8,128)(2,1)S(1)}, bf16[256,2048]{1,0:T(8,128)(2,1)S(1)}, u32[]{:S(2)}, u32[]{:S(2)}) %collective-permute-start.23) | collective-permute-done | bytes 1048608 | tf_op jit(solution)/shard_map/ppermute | solution.py:54
  224.4 23.0 %collective-permute-done.24 = bf16[256,2048]{1,0:T(8,128)(2,1)S(1)} collective-permute-done((bf16[256,2048]{1,0:T(8,128)(2,1)S(1)}, bf16[256,2048]{1,0:T(8,128)(2,1)S(1)}, u32[]{:S(2)}, u32[]{:S(2)}) %collective-permute-start.24) | collective-permute-done | bytes 1048608 | tf_op jit(solution)/shard_map/ppermute | solution.py:54
  248.1 14.1 %collective-permute-done.26 = bf16[256,2048]{1,0:T(8,128)(2,1)S(1)} collective-permute-done((bf16[256,2048]{1,0:T(8,128)(2,1)S(1)}, bf16[256,2048]{1,0:T(8,128)(2,1)S(1)}, u32[]{:S(2)}, u32[]{:S(2)}) %collective-permute-start.26) | collective-permute-done | bytes 1048608 | tf_op jit(solution)/shard_map/ppermute | solution.py:58
  267.0 20.7 %ffn.2.a_ref.b_ref.refs_0_ = bf16[2048,1536]{1,0:T(8,128)(2,1)} custom-call(bf16[1024,2048]{1,0:T(8,128)(2,1)} %pad_maximum_fusion.2.xl_ref, bf16[1024,2048]{1,0:T(8,128)(2,1)} %copy-done.2, bf16[1024,2048]{1,0:T(8,128)(2,1)} %copy-done.1, bf16[1024,2048]{1,0:T(8,128)(2,1)} %constant_dynamic-update-slice_fusion.4.ch_ref.yh_ref, ...), custom_call_target="tpu_custom_call" | custom-call | flops 1 | bytes 1 | tf_op jit(solution)/shard_map/ffn/pallas_call | solution.py:173
  287.7 19.4 %weight_grads.3 = bf16[2048,1536]{1,0:T(8,128)(2,1)} custom-call(bf16[1024,2048]{1,0:T(8,128)(2,1)} %pad_maximum_fusion.2.xl_ref, bf16[1024,2048]{1,0:T(8,128)(2,1)} %copy-done.2, bf16[1024,2048]{1,0:T(8,128)(2,1)} %copy-done.1, bf16[1024,2048]{1,0:T(8,128)(2,1)} %constant_dynamic-update-slice_fusion.4.ch_ref.yh_ref, ...), custom_call_target="tpu_custom_call" | custom-call | flops 1 | bytes 1 | tf_op jit(solution)/shard_map/weight_grads/pallas_call | solution.py:209
  307.6 10.3 %all-gather.5.cloned.1.call-done.w_ref.refs_3_ = bf16[2048,1536]{1,0:T(8,128)(2,1)} async-done(((bf16[512,1536]{1,0:T(8,128)(2,1)}), bf16[2048,1536]{1,0:T(8,128)(2,1)}) %all-gather.5.cloned.1.call-update) | async-done | bytes 6291472 | tf_op jit(solution)/shard_map/all_gather | solution.py:661
  318.0 20.5 %ffn.3.refs_1_.a_ref.b_ref = bf16[2048,1536]{1,0:T(8,128)(2,1)} custom-call(bf16[1024,2048]{1,0:T(8,128)(2,1)} %pad_maximum_fusion.2.xl_ref, bf16[1024,2048]{1,0:T(8,128)(2,1)} %copy-done.2, bf16[1024,2048]{1,0:T(8,128)(2,1)} %copy-done.1, bf16[1024,2048]{1,0:T(8,128)(2,1)} %constant_dynamic-update-slice_fusion.4.ch_ref.yh_ref, ...), custom_call_target="tpu_custom_call" | custom-call | flops 1 | bytes 1 | tf_op jit(solution)/shard_map/ffn/pallas_call | solution.py:173
  338.5 14.5 %back.17 = bf16[1024,2048]{1,0:T(8,128)(2,1)} custom-call(bf16[2048,1536]{1,0:T(8,128)(2,1)} %ffn.2.a_ref.b_ref.refs_0_, bf16[2048,1536]{1,0:T(8,128)(2,1)} %ffn.3.refs_1_.a_ref.b_ref, bf16[2048,1536]{1,0:T(8,128)(2,1)} %all-gather.3.cloned.1.call-done.w_ref.refs_2_, bf16[2048,1536]{1,0:T(8,128)(2,1)} %all-gather.5.cloned.1.call-done.w_ref.refs_3_), custom_call_target="tpu_custom_call" | custom-call | flops 1 | bytes 1 | tf_op jit(solution)/shard_map/back/pallas_call | solution.py:245
  353.1 14.7 %back.16 = bf16[1024,2048]{1,0:T(8,128)(2,1)} custom-call(bf16[2048,1536]{1,0:T(8,128)(2,1)} %ffn.2.a_ref.b_ref.refs_0_, bf16[2048,1536]{1,0:T(8,128)(2,1)} %ffn.3.refs_1_.a_ref.b_ref, bf16[2048,1536]{1,0:T(8,128)(2,1)} %all-gather.3.cloned.1.call-done.w_ref.refs_2_, bf16[2048,1536]{1,0:T(8,128)(2,1)} %all-gather.5.cloned.1.call-done.w_ref.refs_3_), custom_call_target="tpu_custom_call" | custom-call | flops 1 | bytes 1 | tf_op jit(solution)/shard_map/back/pallas_call | solution.py:245
  367.8 4.7 slice_add_fusion.3
  374.0 19.6 %weight_grads.4 = bf16[2048,1536]{1,0:T(8,128)(2,1)} custom-call(bf16[1024,2048]{1,0:T(8,128)(2,1)} %pad_maximum_fusion.2.xl_ref, bf16[1024,2048]{1,0:T(8,128)(2,1)} %copy-done.2, bf16[1024,2048]{1,0:T(8,128)(2,1)} %copy-done.1, bf16[1024,2048]{1,0:T(8,128)(2,1)} %constant_dynamic-update-slice_fusion.4.ch_ref.yh_ref, ...), custom_call_target="tpu_custom_call" | custom-call | flops 1 | bytes 1 | tf_op jit(solution)/shard_map/weight_grads/pallas_call | solution.py:209
  393.5 5.3 collective-permute-done.32
  403.7 13.3 %collective-permute-done.33 = bf16[256,2048]{1,0:T(8,128)(2,1)S(1)} collective-permute-done((bf16[256,2048]{1,0:T(8,128)(2,1)S(1)}, bf16[256,2048]{1,0:T(8,128)(2,1)S(1)}, u32[]{:S(2)}, u32[]{:S(2)}) %collective-permute-start.33) | collective-permute-done | bytes 1048608 | tf_op jit(solution)/shard_map/ppermute | solution.py:54
  418.1 4.1 fusion.29
  425.1 23.4 %collective-permute-done.35 = bf16[256,2048]{1,0:T(8,128)(2,1)} collective-permute-done((bf16[256,2048]{1,0:T(8,128)(2,1)}, bf16[256,2048]{1,0:T(8,128)(2,1)}, u32[]{:S(2)}, u32[]{:S(2)}) %collective-permute-start.35) | collective-permute-done | bytes 1048608 | tf_op jit(solution)/shard_map/ppermute | solution.py:54
  449.3 8.7 %back.14 = bf16[1024,2048]{1,0:T(8,128)(2,1)} custom-call(bf16[2048,1536]{1,0:T(8,128)(2,1)} %ffn.2.a_ref.b_ref.refs_0_, bf16[2048,1536]{1,0:T(8,128)(2,1)} %ffn.3.refs_1_.a_ref.b_ref, bf16[2048,1536]{1,0:T(8,128)(2,1)} %all-gather.3.cloned.1.call-done.w_ref.refs_2_, bf16[2048,1536]{1,0:T(8,128)(2,1)} %all-gather.5.cloned.1.call-done.w_ref.refs_3_), custom_call_target="tpu_custom_call" | custom-call | flops 1 | bytes 1 | tf_op jit(solution)/shard_map/back/pallas_call | solution.py:245
  457.9 6.2 back.15
  464.2 6.4 back.18
  475.8 3.7 pad_maximum_fusion.3.low_ref.xl_ref
  479.5 7.2 front.1.d_ref
  494.7 35.4 %attend_back.1.refs_0_.refs_1_.b_ref = bf16[2048,384]{1,0:T(8,128)(2,1)} custom-call(s32[8]{0:T(128)} %select_reduce_fusion.2.place, s32[8]{0:T(128)} %and_select_fusion.2.first, bf16[2048,384]{1,0:T(8,128)(2,1)} %qkv.1.q_ref.kv_ref, bf16[2048,256]{1,0:T(8,128)(2,1)} %front.1.d_ref, f32[2048,384]{1,0:T(8,128)} %attend.1.refs_0_.h_ref.a_ref, ...), custom_call_target="tpu_custom_call" | custom-call | flops 1 | bytes 1 | tf_op jit(solution)/shard_map/attend_back/pallas_call | solution.py:450
  530.1 9.5 %collective-permute-done.43 = bf16[512,2048]{1,0:T(8,128)(2,1)} collective-permute-done((bf16[512,2048]{1,0:T(8,128)(2,1)}, bf16[512,2048]{1,0:T(8,128)(2,1)}, u32[]{:S(2)}, u32[]{:S(2)}) %collective-permute-start.43) | collective-permute-done | bytes 2097184 | tf_op jit(solution)/shard_map/ppermute | solution.py:46
  539.6 3.9 maximum_add_fusion
  543.5 4.1 back.20
  552.1 5.4 back.19
  557.5 4.1 back.21
  562.1 3.9 slice_add_fusion.1
  567.8 4.4 fusion.5
  572.6 12.7 %weight_grads.5 = bf16[2048,640]{1,0:T(8,128)(2,1)} custom-call(bf16[1024,2048]{1,0:T(8,128)(2,1)} %pad_maximum_fusion.3.low_ref.xl_ref, bf16[1024,2048]{1,0:T(8,128)(2,1)} %constant_dynamic-update-slice_fusion.12.high_ref.xh_ref, bf16[1024,2048]{1,0:T(8,128)(2,1)} %get-tuple-element.134.yl_ref, bf16[1024,2048]{1,0:T(8,128)(2,1)} %get-tuple-element.133.yh_ref, ...), custom_call_target="tpu_custom_call" | custom-call | flops 1 | bytes 1 | tf_op jit(solution)/shard_map/weight_grads/pallas_call | solution.py:209
  601.1 21.9 %collective-permute-done.60 = bf16[512,1536]{1,0:T(8,128)(2,1)S(1)} collective-permute-done((bf16[512,1536]{1,0:T(8,128)(2,1)}, bf16[512,1536]{1,0:T(8,128)(2,1)S(1)}, u32[]{:S(2)}, u32[]{:S(2)}) %collective-permute-start.60) | collective-permute-done | bytes 1572896 | tf_op jit(solution)/shard_map/ppermute | solution.py:50
  623.4 22.0 %collective-permute-done.52 = bf16[256,2048]{1,0:T(8,128)(2,1)S(1)} collective-permute-done((bf16[256,2048]{1,0:T(8,128)(2,1)S(1)}, bf16[256,2048]{1,0:T(8,128)(2,1)S(1)}, u32[]{:S(2)}, u32[]{:S(2)}) %collective-permute-start.52) | collective-permute-done | bytes 1048608 | tf_op jit(solution)/shard_map/ppermute | solution.py:54
  646.0 12.7 %collective-permute-done.46 = bf16[256,2048]{1,0:T(8,128)(2,1)S(1)} collective-permute-done((bf16[256,2048]{1,0:T(8,128)(2,1)S(1)}, bf16[256,2048]{1,0:T(8,128)(2,1)S(1)}, u32[]{:S(2)}, u32[]{:S(2)}) %collective-permute-start.46) | collective-permute-done | bytes 1048608 | tf_op jit(solution)/shard_map/ppermute | solution.py:50
  670.6 18.0 %collective-permute-done.53 = bf16[256,2048]{1,0:T(8,128)(2,1)} collective-permute-done((bf16[256,2048]{1,0:T(8,128)(2,1)}, bf16[256,2048]{1,0:T(8,128)(2,1)}, u32[]{:S(2)}, u32[]{:S(2)}) %collective-permute-start.53) | collective-permute-done | bytes 1048608 | tf_op jit(solution)/shard_map/ppermute | solution.py:46
  690.0 3.7 pad_maximum_fusion.6
  705.6 5.8 collective-permute-done.59
  (328 shorter events, 166.5 us)
Async XLA Ops:
  7.2 195.6 %all-gather.3.cloned.1.call-start = ((), (), s32[]{:S(2)}) async-start(), calls=%async_computation.3 | async-start | bytes 7864320 | tf_op jit(solution)/shard_map/all_gather | solution.py:661
  9.6 26.7 %collective-permute-start.6 = (bf16[256,2048]{1,0:T(8,128)(2,1)}, bf16[256,2048]{1,0:T(8,128)(2,1)}, u32[]{:S(2)}, u32[]{:S(2)}) collective-permute-start(bf16[256,2048]{1,0:T(8,128)(2,1)} %constant_dynamic-slice_fusion.11), channel_id=1, source_target_pairs={{0,4},{1,3},{2,6},{3,1},{4,0},{5,7},{6,2},{7,5},{8,12},{9,11},{10,... | collective-permute-start | bytes 3145736 | tf_op jit(solution)/shard_map/ppermute | solution.py:54
  12.5 48.3 %collective-permute-start.7 = (bf16[256,2048]{1,0:T(8,128)(2,1)}, bf16[256,2048]{1,0:T(8,128)(2,1)}, u32[]{:S(2)}, u32[]{:S(2)}) collective-permute-start(bf16[256,2048]{1,0:T(8,128)(2,1)} %constant_dynamic-slice_fusion.11), channel_id=1, source_target_pairs={{0,2},{1,5},{2,0},{3,7},{4,6},{5,1},{6,4},{7,3},{8,10},{9,13},{10,... | collective-permute-start | bytes 3145736 | tf_op jit(solution)/shard_map/ppermute | solution.py:58
  14.1 71.3 %collective-permute-start.9 = (bf16[256,2048]{1,0:T(8,128)(2,1)}, bf16[256,2048]{1,0:T(8,128)(2,1)}, u32[]{:S(2)}, u32[]{:S(2)}) collective-permute-start(bf16[256,2048]{1,0:T(8,128)(2,1)} %constant_dynamic-slice_fusion.11), channel_id=1, source_target_pairs={{0,1},{1,0},{2,3},{3,2},{4,5},{5,4},{6,7},{7,6},{8,9},{9,8},{10,11... | collective-permute-start | bytes 3145736 | tf_op jit(solution)/shard_map/ppermute | solution.py:42
  16.0 19.1 %collective-permute-start = (bf16[512,640]{1,0:T(8,128)(2,1)S(1)}, bf16[512,640]{1,0:T(8,128)(2,1)}, u32[]{:S(2)}, u32[]{:S(2)}) collective-permute-start(bf16[512,640]{1,0:T(8,128)(2,1)S(1)} %get-tuple-element.86), channel_id=1, source_target_pairs={{0,8},{8,16},{16,24},{24,0},{1,9},{9,17},{17,25},{25,1},{2,10},{10... | collective-permute-start | bytes 1966088 | tf_op jit(solution)/shard_map/ppermute | solution.py:514
  17.7 28.6 %collective-permute-start.3 = (bf16[2,512]{1,0:T(2,128)(2,1)S(1)}, bf16[2,512]{1,0:T(2,128)(2,1)S(1)}, u32[]{:S(2)}, u32[]{:S(2)}) collective-permute-start(bf16[2,512]{1,0:T(2,128)(2,1)S(1)} %get-tuple-element.90), channel_id=1, source_target_pairs={{0,8},{8,16},{16,24},{24,0},{1,9},{9,17},{17,25},{25,1},{2,10},{10... | collective-permute-start | bytes 6152 | tf_op jit(solution)/shard_map/ppermute | solution.py:532
  36.3 26.6 %collective-permute-start.8 = (bf16[256,2048]{1,0:T(8,128)(2,1)}, bf16[256,2048]{1,0:T(8,128)(2,1)}, u32[]{:S(2)}, u32[]{:S(2)}) collective-permute-start(bf16[256,2048]{1,0:T(8,128)(2,1)} %collective-permute-done.6), channel_id=1, source_target_pairs={{0,2},{1,5},{2,0},{3,7},{4,6},{5,1},{6,4},{7,3},{8,10},{9,13},{10,... | collective-permute-start | bytes 3145736 | tf_op jit(solution)/shard_map/ppermute | solution.py:58
  40.9 20.4 %collective-permute-start.1 = (bf16[512,640]{1,0:T(8,128)(2,1)}, bf16[512,640]{1,0:T(8,128)(2,1)}, u32[]{:S(2)}, u32[]{:S(2)}) collective-permute-start(bf16[512,640]{1,0:T(8,128)(2,1)} %collective-permute-done), channel_id=1, source_target_pairs={{0,8},{8,16},{16,24},{24,0},{1,9},{9,17},{17,25},{25,1},{2,10},{10... | collective-permute-start | bytes 1966088 | tf_op jit(solution)/shard_map/ppermute | solution.py:514
  60.8 24.6 %collective-permute-start.10 = (bf16[256,2048]{1,0:T(8,128)(2,1)}, bf16[256,2048]{1,0:T(8,128)(2,1)S(1)}, u32[]{:S(2)}, u32[]{:S(2)}) collective-permute-start(bf16[256,2048]{1,0:T(8,128)(2,1)} %collective-permute-done.6), channel_id=1, source_target_pairs={{0,1},{1,0},{2,3},{3,2},{4,5},{5,4},{6,7},{7,6},{8,9},{9,8},{10,11... | collective-permute-start | bytes 3145736 | tf_op jit(solution)/shard_map/ppermute | solution.py:42
  60.8 24.6 %collective-permute-start.11 = (bf16[256,2048]{1,0:T(8,128)(2,1)}, bf16[256,2048]{1,0:T(8,128)(2,1)S(1)}, u32[]{:S(2)}, u32[]{:S(2)}) collective-permute-start(bf16[256,2048]{1,0:T(8,128)(2,1)} %collective-permute-done.7), channel_id=1, source_target_pairs={{0,1},{1,0},{2,3},{3,2},{4,5},{5,4},{6,7},{7,6},{8,9},{9,8},{10,11... | collective-permute-start | bytes 3145736 | tf_op jit(solution)/shard_map/ppermute | solution.py:42
  61.3 19.3 %collective-permute-start.2 = (bf16[512,640]{1,0:T(8,128)(2,1)}, bf16[512,640]{1,0:T(8,128)(2,1)S(1)}, u32[]{:S(2)}, u32[]{:S(2)}) collective-permute-start(bf16[512,640]{1,0:T(8,128)(2,1)} %collective-permute-done.1), channel_id=1, source_target_pairs={{0,8},{8,16},{16,24},{24,0},{1,9},{9,17},{17,25},{25,1},{2,10},{10... | collective-permute-start | bytes 1966088 | tf_op jit(solution)/shard_map/ppermute | solution.py:514
  62.9 22.5 %collective-permute-start.12 = (bf16[256,2048]{1,0:T(8,128)(2,1)}, bf16[256,2048]{1,0:T(8,128)(2,1)S(1)}, u32[]{:S(2)}, u32[]{:S(2)}) collective-permute-start(bf16[256,2048]{1,0:T(8,128)(2,1)} %collective-permute-done.8), channel_id=1, source_target_pairs={{0,1},{1,0},{2,3},{3,2},{4,5},{5,4},{6,7},{7,6},{8,9},{9,8},{10,11... | collective-permute-start | bytes 3145736 | tf_op jit(solution)/shard_map/ppermute | solution.py:42
  88.8 229.2 %all-gather.5.cloned.1.call-start = ((), (), s32[]{:S(2)}) async-start(), calls=%async_computation.4 | async-start | bytes 7864320 | tf_op jit(solution)/shard_map/all_gather | solution.py:661
  89.4 26.0 %collective-permute-start.13 = (bf16[256,2048]{1,0:T(8,128)(2,1)S(1)}, bf16[256,2048]{1,0:T(8,128)(2,1)}, u32[]{:S(2)}, u32[]{:S(2)}) collective-permute-start(bf16[256,2048]{1,0:T(8,128)(2,1)S(1)} %copy-done.23), channel_id=1, source_target_pairs={{0,4},{1,3},{2,6},{3,1},{4,0},{5,7},{6,2},{7,5},{8,12},{9,11},{10,... | collective-permute-start | bytes 3145736 | tf_op jit(solution)/shard_map/ppermute | solution.py:54
  89.8 52.1 %collective-permute-start.14 = (bf16[256,2048]{1,0:T(8,128)(2,1)S(1)}, bf16[256,2048]{1,0:T(8,128)(2,1)S(1)}, u32[]{:S(2)}, u32[]{:S(2)}) collective-permute-start(bf16[256,2048]{1,0:T(8,128)(2,1)S(1)} %copy-done.23), channel_id=1, source_target_pairs={{0,2},{1,5},{2,0},{3,7},{4,6},{5,1},{6,4},{7,3},{8,10},{9,13},{10,... | collective-permute-start | bytes 3145736 | tf_op jit(solution)/shard_map/ppermute | solution.py:58
  115.4 27.7 %collective-permute-start.15 = (bf16[256,2048]{1,0:T(8,128)(2,1)}, bf16[256,2048]{1,0:T(8,128)(2,1)}, u32[]{:S(2)}, u32[]{:S(2)}) collective-permute-start(bf16[256,2048]{1,0:T(8,128)(2,1)} %collective-permute-done.13), channel_id=1, source_target_pairs={{0,2},{1,5},{2,0},{3,7},{4,6},{5,1},{6,4},{7,3},{8,10},{9,13},{10,... | collective-permute-start | bytes 3145736 | tf_op jit(solution)/shard_map/ppermute | solution.py:58
  115.9 27.8 %collective-permute-start.16 = (bf16[256,2048]{1,0:T(8,128)(2,1)S(1)}, bf16[256,2048]{1,0:T(8,128)(2,1)}, u32[]{:S(2)}, u32[]{:S(2)}) collective-permute-start(bf16[256,2048]{1,0:T(8,128)(2,1)S(1)} %copy-done.23), channel_id=1, source_target_pairs={{0,1},{1,0},{2,3},{3,2},{4,5},{5,4},{6,7},{7,6},{8,9},{9,8},{10,11... | collective-permute-start | bytes 3145736 | tf_op jit(solution)/shard_map/ppermute | solution.py:42
  118.5 29.0 %collective-permute-start.17 = (bf16[256,2048]{1,0:T(8,128)(2,1)}, bf16[256,2048]{1,0:T(8,128)(2,1)}, u32[]{:S(2)}, u32[]{:S(2)}) collective-permute-start(bf16[256,2048]{1,0:T(8,128)(2,1)} %collective-permute-done.13), channel_id=1, source_target_pairs={{0,1},{1,0},{2,3},{3,2},{4,5},{5,4},{6,7},{7,6},{8,9},{9,8},{10,11... | collective-permute-start | bytes 3145736 | tf_op jit(solution)/shard_map/ppermute | solution.py:42
  157.6 290.9 %reduce-scatter.4.cloned.1.call-start = ((), (), s32[]{:S(2)}) async-start(), calls=%async_computation.5 | async-start | bytes 7864320 | tf_op jit(solution)/shard_map/reduce_scatter | solution.py:679
  167.5 26.1 %collective-permute-start.22 = (bf16[512,2048]{1,0:T(8,128)(2,1)S(1)}, bf16[512,2048]{1,0:T(8,128)(2,1)S(1)}, u32[]{:S(2)}, u32[]{:S(2)}) collective-permute-start(bf16[512,2048]{1,0:T(8,128)(2,1)S(1)} %slice_add_fusion.6), channel_id=1, source_target_pairs={{0,2},{1,5},{2,0},{3,7},{4,6},{5,1},{6,4},{7,3},{8,10},{9,13},{10,... | collective-permute-start | bytes 6291464 | tf_op jit(solution)/shard_map/ppermute | solution.py:58
  169.1 24.5 %collective-permute-start.20 = (bf16[512,2048]{1,0:T(8,128)(2,1)S(1)}, bf16[512,2048]{1,0:T(8,128)(2,1)S(1)}, u32[]{:S(2)}, u32[]{:S(2)}) collective-permute-start(bf16[512,2048]{1,0:T(8,128)(2,1)S(1)} %copy-done.30), channel_id=1, source_target_pairs={{0,1},{1,0},{2,3},{3,2},{4,5},{5,4},{6,7},{7,6},{8,9},{9,8},{10,11... | collective-permute-start | bytes 6291464 | tf_op jit(solution)/shard_map/ppermute | solution.py:42
  202.9 14.9 %collective-permute-start.23 = (bf16[256,2048]{1,0:T(8,128)(2,1)S(1)}, bf16[256,2048]{1,0:T(8,128)(2,1)S(1)}, u32[]{:S(2)}, u32[]{:S(2)}) collective-permute-start(bf16[256,2048]{1,0:T(8,128)(2,1)S(1)} %slice.161), channel_id=1, source_target_pairs={{0,4},{1,3},{2,6},{3,1},{4,0},{5,7},{6,2},{7,5},{8,12},{9,11},{10,... | collective-permute-start | bytes 3145736 | tf_op jit(solution)/shard_map/ppermute | solution.py:54
  221.4 26.0 %collective-permute-start.24 = (bf16[256,2048]{1,0:T(8,128)(2,1)S(1)}, bf16[256,2048]{1,0:T(8,128)(2,1)S(1)}, u32[]{:S(2)}, u32[]{:S(2)}) collective-permute-start(bf16[256,2048]{1,0:T(8,128)(2,1)S(1)} %multiply_convert_fusion), channel_id=1, source_target_pairs={{0,4},{1,3},{2,6},{3,1},{4,0},{5,7},{6,2},{7,5},{8,12},{9,11},{10,... | collective-permute-start | bytes 3145736 | tf_op jit(solution)/shard_map/ppermute | solution.py:54
  222.9 25.2 %collective-permute-start.25 = (bf16[256,2048]{1,0:T(8,128)(2,1)S(1)}, bf16[256,2048]{1,0:T(8,128)(2,1)S(1)}, u32[]{:S(2)}, u32[]{:S(2)}) collective-permute-start(bf16[256,2048]{1,0:T(8,128)(2,1)S(1)} %multiply_convert_fusion), channel_id=1, source_target_pairs={{0,2},{1,5},{2,0},{3,7},{4,6},{5,1},{6,4},{7,3},{8,10},{9,13},{10,... | collective-permute-start | bytes 3145736 | tf_op jit(solution)/shard_map/ppermute | solution.py:58
  247.4 14.8 %collective-permute-start.26 = (bf16[256,2048]{1,0:T(8,128)(2,1)S(1)}, bf16[256,2048]{1,0:T(8,128)(2,1)S(1)}, u32[]{:S(2)}, u32[]{:S(2)}) collective-permute-start(bf16[256,2048]{1,0:T(8,128)(2,1)S(1)} %collective-permute-done.24), channel_id=1, source_target_pairs={{0,2},{1,5},{2,0},{3,7},{4,6},{5,1},{6,4},{7,3},{8,10},{9,13},{10,... | collective-permute-start | bytes 3145736 | tf_op jit(solution)/shard_map/ppermute | solution.py:58
  307.2 278.2 %reduce-scatter.6.cloned.1.call-start = ((), (), s32[]{:S(2)}) async-start(), calls=%async_computation.6 | async-start | bytes 7864320 | tf_op jit(solution)/shard_map/reduce_scatter | solution.py:679
  353.0 14.8 %collective-permute-start.31 = (bf16[1024,2048]{1,0:T(8,128)(2,1)}, bf16[1024,2048]{1,0:T(8,128)(2,1)S(1)}, u32[]{:S(2)}, u32[]{:S(2)}) collective-permute-start(bf16[1024,2048]{1,0:T(8,128)(2,1)} %back.17), channel_id=1, source_target_pairs={{0,1},{1,0},{2,3},{3,2},{4,5},{5,4},{6,7},{7,6},{8,9},{9,8},{10,11... | collective-permute-start | bytes 12582920 | tf_op jit(solution)/shard_map/ppermute | solution.py:42
  372.5 26.4 %collective-permute-start.32 = (bf16[512,2048]{1,0:T(8,128)(2,1)}, bf16[512,2048]{1,0:T(8,128)(2,1)}, u32[]{:S(2)}, u32[]{:S(2)}) collective-permute-start(bf16[512,2048]{1,0:T(8,128)(2,1)} %slice_add_fusion.3), channel_id=1, source_target_pairs={{0,2},{1,5},{2,0},{3,7},{4,6},{5,1},{6,4},{7,3},{8,10},{9,13},{10,... | collective-permute-start | bytes 6291464 | tf_op jit(solution)/shard_map/ppermute | solution.py:58
  402.2 14.9 %collective-permute-start.33 = (bf16[256,2048]{1,0:T(8,128)(2,1)S(1)}, bf16[256,2048]{1,0:T(8,128)(2,1)S(1)}, u32[]{:S(2)}, u32[]{:S(2)}) collective-permute-start(bf16[256,2048]{1,0:T(8,128)(2,1)S(1)} %slice.169), channel_id=1, source_target_pairs={{0,4},{1,3},{2,6},{3,1},{4,0},{5,7},{6,2},{7,5},{8,12},{9,11},{10,... | collective-permute-start | bytes 3145736 | tf_op jit(solution)/shard_map/ppermute | solution.py:54
  422.2 26.3 %collective-permute-start.35 = (bf16[256,2048]{1,0:T(8,128)(2,1)}, bf16[256,2048]{1,0:T(8,128)(2,1)}, u32[]{:S(2)}, u32[]{:S(2)}) collective-permute-start(bf16[256,2048]{1,0:T(8,128)(2,1)} %get-tuple-element.83), channel_id=1, source_target_pairs={{0,4},{1,3},{2,6},{3,1},{4,0},{5,7},{6,2},{7,5},{8,12},{9,11},{10,... | collective-permute-start | bytes 3145736 | tf_op jit(solution)/shard_map/ppermute | solution.py:54
  423.7 25.5 %collective-permute-start.37 = (bf16[256,2048]{1,0:T(8,128)(2,1)}, bf16[256,2048]{1,0:T(8,128)(2,1)}, u32[]{:S(2)}, u32[]{:S(2)}) collective-permute-start(bf16[256,2048]{1,0:T(8,128)(2,1)} %get-tuple-element.83), channel_id=1, source_target_pairs={{0,2},{1,5},{2,0},{3,7},{4,6},{5,1},{6,4},{7,3},{8,10},{9,13},{10,... | collective-permute-start | bytes 3145736 | tf_op jit(solution)/shard_map/ppermute | solution.py:58
  448.5 22.0 %collective-permute-start.39 = (bf16[256,2048]{1,0:T(8,128)(2,1)}, bf16[256,2048]{1,0:T(8,128)(2,1)}, u32[]{:S(2)}, u32[]{:S(2)}) collective-permute-start(bf16[256,2048]{1,0:T(8,128)(2,1)} %collective-permute-done.35), channel_id=1, source_target_pairs={{0,2},{1,5},{2,0},{3,7},{4,6},{5,1},{6,4},{7,3},{8,10},{9,13},{10,... | collective-permute-start | bytes 3145736 | tf_op jit(solution)/shard_map/ppermute | solution.py:58
  448.6 222.0 %reduce-scatter.8.cloned.1.call-start = ((), (), s32[]{:S(2)}) async-start(), calls=%async_computation.7 | async-start | bytes 3276800 | tf_op jit(solution)/shard_map/reduce_scatter | solution.py:727
  448.6 22.4 %collective-permute-start.34 = (bf16[256,2048]{1,0:T(8,128)(2,1)}, bf16[256,2048]{1,0:T(8,128)(2,1)S(1)}, u32[]{:S(2)}, u32[]{:S(2)}) collective-permute-start(bf16[256,2048]{1,0:T(8,128)(2,1)} %get-tuple-element.83), channel_id=1, source_target_pairs={{0,1},{1,0},{2,3},{3,2},{4,5},{5,4},{6,7},{7,6},{8,9},{9,8},{10,11... | collective-permute-start | bytes 3145736 | tf_op jit(solution)/shard_map/ppermute | solution.py:42
  448.7 23.4 %collective-permute-start.36 = (bf16[256,2048]{1,0:T(8,128)(2,1)}, bf16[256,2048]{1,0:T(8,128)(2,1)S(1)}, u32[]{:S(2)}, u32[]{:S(2)}) collective-permute-start(bf16[256,2048]{1,0:T(8,128)(2,1)} %collective-permute-done.35), channel_id=1, source_target_pairs={{0,1},{1,0},{2,3},{3,2},{4,5},{5,4},{6,7},{7,6},{8,9},{9,8},{10,11... | collective-permute-start | bytes 3145736 | tf_op jit(solution)/shard_map/ppermute | solution.py:42
  449.2 24.0 %collective-permute-start.38 = (bf16[256,2048]{1,0:T(8,128)(2,1)}, bf16[256,2048]{1,0:T(8,128)(2,1)S(1)}, u32[]{:S(2)}, u32[]{:S(2)}) collective-permute-start(bf16[256,2048]{1,0:T(8,128)(2,1)} %collective-permute-done.37), channel_id=1, source_target_pairs={{0,1},{1,0},{2,3},{3,2},{4,5},{5,4},{6,7},{7,6},{8,9},{9,8},{10,11... | collective-permute-start | bytes 3145736 | tf_op jit(solution)/shard_map/ppermute | solution.py:42
  491.3 48.3 %collective-permute-start.43 = (bf16[512,2048]{1,0:T(8,128)(2,1)}, bf16[512,2048]{1,0:T(8,128)(2,1)}, u32[]{:S(2)}, u32[]{:S(2)}) collective-permute-start(bf16[512,2048]{1,0:T(8,128)(2,1)} %pad_maximum_fusion.9), channel_id=1, source_target_pairs={{0,2},{2,0},{1,3},{3,1},{4,6},{6,4},{5,7},{7,5},{8,10},{10,8},{9,1... | collective-permute-start | bytes 6291464 | tf_op jit(solution)/shard_map/ppermute | solution.py:46
  493.3 50.2 %collective-permute-start.44 = (bf16[512,1536]{1,0:T(8,128)(2,1)S(1)}, bf16[512,1536]{1,0:T(8,128)(2,1)}, u32[]{:S(2)}, u32[]{:S(2)}) collective-permute-start(bf16[512,1536]{1,0:T(8,128)(2,1)S(1)} %copy-done.20), channel_id=1, source_target_pairs={{0,4},{4,0},{1,5},{5,1},{2,6},{6,2},{3,7},{7,3},{8,12},{12,8},{9,1... | collective-permute-start | bytes 4718600 | tf_op jit(solution)/shard_map/ppermute | solution.py:50
  561.6 30.7 %collective-permute-start.50 = (bf16[512,2048]{1,0:T(8,128)(2,1)}, bf16[512,2048]{1,0:T(8,128)(2,1)}, u32[]{:S(2)}, u32[]{:S(2)}) collective-permute-start(bf16[512,2048]{1,0:T(8,128)(2,1)} %back.21), channel_id=1, source_target_pairs={{0,1},{1,0},{2,3},{3,2},{4,5},{5,4},{6,7},{7,6},{8,9},{9,8},{10,11... | collective-permute-start | bytes 6291464 | tf_op jit(solution)/shard_map/ppermute | solution.py:42
  566.0 26.4 %collective-permute-start.51 = (bf16[512,2048]{1,0:T(8,128)(2,1)}, bf16[512,2048]{1,0:T(8,128)(2,1)}, u32[]{:S(2)}, u32[]{:S(2)}) collective-permute-start(bf16[512,2048]{1,0:T(8,128)(2,1)} %slice_add_fusion.1), channel_id=1, source_target_pairs={{0,2},{1,5},{2,0},{3,7},{4,6},{5,1},{6,4},{7,3},{8,10},{9,13},{10,... | collective-permute-start | bytes 6291464 | tf_op jit(solution)/shard_map/ppermute | solution.py:58
  585.4 37.6 %collective-permute-start.60 = (bf16[512,1536]{1,0:T(8,128)(2,1)}, bf16[512,1536]{1,0:T(8,128)(2,1)S(1)}, u32[]{:S(2)}, u32[]{:S(2)}) collective-permute-start(bf16[512,1536]{1,0:T(8,128)(2,1)} %reduce-scatter.6.cloned.1.call-done), channel_id=1, source_target_pairs={{0,4},{4,0},{1,5},{5,1},{2,6},{6,2},{3,7},{7,3},{8,12},{12,8},{9,1... | collective-permute-start | bytes 4718600 | tf_op jit(solution)/shard_map/ppermute | solution.py:50
  595.1 50.4 %collective-permute-start.52 = (bf16[256,2048]{1,0:T(8,128)(2,1)S(1)}, bf16[256,2048]{1,0:T(8,128)(2,1)S(1)}, u32[]{:S(2)}, u32[]{:S(2)}) collective-permute-start(bf16[256,2048]{1,0:T(8,128)(2,1)S(1)} %slice.180), channel_id=1, source_target_pairs={{0,4},{1,3},{2,6},{3,1},{4,0},{5,7},{6,2},{7,5},{8,12},{9,11},{10,... | collective-permute-start | bytes 3145736 | tf_op jit(solution)/shard_map/ppermute | solution.py:54
  600.4 58.3 %collective-permute-start.46 = (bf16[256,2048]{1,0:T(8,128)(2,1)S(1)}, bf16[256,2048]{1,0:T(8,128)(2,1)S(1)}, u32[]{:S(2)}, u32[]{:S(2)}) collective-permute-start(bf16[256,2048]{1,0:T(8,128)(2,1)S(1)} %slice.177), channel_id=1, source_target_pairs={{0,4},{4,0},{1,5},{5,1},{2,6},{6,2},{3,7},{7,3},{8,12},{12,8},{9,1... | collective-permute-start | bytes 3145736 | tf_op jit(solution)/shard_map/ppermute | solution.py:50
  662.1 26.4 %collective-permute-start.53 = (bf16[256,2048]{1,0:T(8,128)(2,1)}, bf16[256,2048]{1,0:T(8,128)(2,1)}, u32[]{:S(2)}, u32[]{:S(2)}) collective-permute-start(bf16[256,2048]{1,0:T(8,128)(2,1)} %get-tuple-element.129), channel_id=1, source_target_pairs={{0,2},{2,0},{1,3},{3,1},{4,6},{6,4},{5,7},{7,5},{8,10},{10,8},{9,1... | collective-permute-start | bytes 3145736 | tf_op jit(solution)/shard_map/ppermute | solution.py:46
  670.2 33.5 %collective-permute-start.47 = (bf16[256,2048]{1,0:T(8,128)(2,1)}, bf16[256,2048]{1,0:T(8,128)(2,1)}, u32[]{:S(2)}, u32[]{:S(2)}) collective-permute-start(bf16[256,2048]{1,0:T(8,128)(2,1)} %get-tuple-element.130), channel_id=1, source_target_pairs={{0,2},{2,0},{1,3},{3,1},{4,6},{6,4},{5,7},{7,5},{8,10},{10,8},{9,1... | collective-permute-start | bytes 3145736 | tf_op jit(solution)/shard_map/ppermute | solution.py:46
  693.7 23.5 %collective-permute-start.54 = (bf16[256,2048]{1,0:T(8,128)(2,1)}, bf16[256,2048]{1,0:T(8,128)(2,1)S(1)}, u32[]{:S(2)}, u32[]{:S(2)}) collective-permute-start(bf16[256,2048]{1,0:T(8,128)(2,1)} %get-tuple-element.129), channel_id=1, source_target_pairs={{0,1},{1,0},{2,3},{3,2},{4,5},{5,4},{6,7},{7,6},{8,9},{9,8},{10,11... | collective-permute-start | bytes 3145736 | tf_op jit(solution)/shard_map/ppermute | solution.py:42
  694.2 28.9 %collective-permute-start.48 = (bf16[256,2048]{1,0:T(8,128)(2,1)}, bf16[256,2048]{1,0:T(8,128)(2,1)S(1)}, u32[]{:S(2)}, u32[]{:S(2)}) collective-permute-start(bf16[256,2048]{1,0:T(8,128)(2,1)} %get-tuple-element.130), channel_id=1, source_target_pairs={{0,1},{1,0},{2,3},{3,2},{4,5},{5,4},{6,7},{7,6},{8,9},{9,8},{10,11... | collective-permute-start | bytes 3145736 | tf_op jit(solution)/shard_map/ppermute | solution.py:42
  694.2 18.4 %collective-permute-start.56 = (bf16[512,640]{1,0:T(8,128)(2,1)S(1)}, bf16[512,640]{1,0:T(8,128)(2,1)S(1)}, u32[]{:S(2)}, u32[]{:S(2)}) collective-permute-start(bf16[512,640]{1,0:T(8,128)(2,1)S(1)} %copy-done.31), channel_id=1, source_target_pairs={{0,4},{4,0},{1,5},{5,1},{2,6},{6,2},{3,7},{7,3},{8,12},{12,8},{9,1... | collective-permute-start | bytes 1966088 | tf_op jit(solution)/shard_map/ppermute | solution.py:50
  (64 other events, 688.6 us)
Sparse Core Ops, SparseCore 0:
  88.9 113.8 all-gather.2
  204.4 113.5 all-gather.4
  320.3 108.9 reduce-scatter.3
  448.7 109.5 reduce-scatter.5
  585.5 49.2 reduce-scatter.7

commit v4 on v3

--- a/solution.py
+++ b/solution.py
@@ -85,54 +85,64 @@
     return jnp.where(first, pltpu.roll(u, 96, 1), pltpu.roll(u, 32, 1))
 
 
-def two_halves(step, width, halves):
-    return [
-        pl.BlockSpec((step, width), lambda i: (jnp.minimum(i, halves - 1), 0)),
-        pl.BlockSpec((step, width), lambda i: (jnp.maximum(i - halves, 0), 0)),
-    ]
-
-
-def either(halves, body, low_refs, high_refs):
-    @pl.when(pl.program_id(0) < halves)
+def stream_scratch(count, rows, depth):
+    return [pltpu.VMEM((2, rows, depth), BF16), pltpu.SemaphoreType.DMA((2,))] * count
+
+
+def next_piece(refs, buffer, sems):
+    i = pl.program_id(0)
+
+    def copy_of(piece):
+        return pltpu.make_async_copy(refs[piece], buffer.at[piece % 2], sems.at[piece % 2])
+
+    @pl.when(i == 0)
     def _():
-        body(*low_refs)
-
-    @pl.when(pl.program_id(0) >= halves)
-    def _():
-        body(*high_refs)
-
-
-def qkv_kernel(halves, low_ref, high_ref, gain_ref, wq_ref, wkv_ref, cos_ref, sin_ref, o_ref):
+        copy_of(0).start()
+
+    for piece in range(1, len(refs)):
+
+        @pl.when(i == piece - 1)
+        def _(piece=piece):
+            copy_of(piece).start()
+
+    for piece in range(len(refs)):
+
+        @pl.when(i == piece)
+        def _(piece=piece):
+            copy_of(piece).wait()
+
+    return buffer[lax.rem(i, 2)]
+
+
+def qkv_kernel(count, *refs):
+    gain_ref, wq_ref, wkv_ref, cos_ref, sin_ref, o_ref, buffer, sems = refs[count:]
     cos, sin = cos_ref[...], sin_ref[...]
+    depth = gain_ref.shape[1]
     lane = lax.broadcasted_iota(jnp.int32, cos.shape, 1)
     first = (lane % 64) < 32
-
-    def body(x_ref):
-        x = x_ref[...].astype(F32)
-        x = (x * inv_rms(x) * gain_ref[...]).astype(BF16)
-        raw = jnp.dot(x, wq_ref[...], preferred_element_type=F32)
-        tiles = raw.shape[1] // 128
-        for tile in range(tiles):
-            u = raw[:, tile * 128 : (tile + 1) * 128]
-            turned = u * cos + turn_lanes(u, first) * sin
-            o_ref[:, tile * 128 : (tile + 1) * 128] = turned.astype(BF16)
-        u = jnp.dot(x, wkv_ref[...], preferred_element_type=F32)
+    x = next_piece(refs[:count], buffer, sems).astype(F32)
+    x = (x * inv_rms(x) * gain_ref[...]).astype(BF16)
+    o_ref[:, :depth] = x
+    raw = jnp.dot(x, wq_ref[...], preferred_element_type=F32)
+    tiles = raw.shape[1] // 128
+    for tile in range(tiles):
+        u = raw[:, tile * 128 : (tile + 1) * 128]
         turned = u * cos + turn_lanes(u, first) * sin
-        o_ref[:, tiles * 128 :] = jnp.where(lane < 64, turned, u).astype(BF16)
-
-    either(halves, body, (low_ref,), (high_ref,))
+        o_ref[:, depth + tile * 128 : depth + (tile + 1) * 128] = turned.astype(BF16)
+    u = jnp.dot(x, wkv_ref[...], preferred_element_type=F32)
+    turned = u * cos + turn_lanes(u, first) * sin
+    o_ref[:, depth + tiles * 128 :] = jnp.where(lane < 64, turned, u).astype(BF16)
 
 
 def project_qkv(x, gain, w, q_width, cos, sin):
-    half_rows, depth = x[0].shape
-    rows = 2 * half_rows
-    width = q_width + 128
-    step = min(512, half_rows)
+    step, depth = x[0].shape
+    rows = len(x) * step
+    width = depth + q_width + 128
     return pl.pallas_call(
-        functools.partial(qkv_kernel, half_rows // step),
+        functools.partial(qkv_kernel, len(x)),
         out_shape=jax.ShapeDtypeStruct((rows, width), BF16),
-        grid=(rows // step,),
-        in_specs=two_halves(step, depth, half_rows // step)
+        grid=(len(x),),
+        in_specs=[pl.BlockSpec(memory_space=pl.ANY)] * len(x)
         + [
             pl.BlockSpec((1, depth), lambda i: (0, 0)),
             pl.BlockSpec((depth, q_width), lambda i: (0, 1)),
@@ -141,43 +151,40 @@
             pl.BlockSpec((step, 128), lambda i: (i, 0)),
         ],
         out_specs=pl.BlockSpec((step, width), lambda i: (i, 0)),
+        scratch_shapes=stream_scratch(1, step, depth),
         compiler_params=params(),
         cost_estimate=cost(),
         name="qkv",
     )(*x, gain, w, w, cos, sin)
 
 
-def ffn_kernel(halves, xl_ref, xh_ref, cl_ref, ch_ref, w_ref, o_ref):
+def ffn_kernel(count, *refs):
+    w_ref, o_ref, x_buffer, x_sems, c_buffer, c_sems = refs[2 * count :]
     n = w_ref.shape[1] // 3
-
-    def body(x_ref, c_ref):
-        x = x_ref[...]
-        gate = jnp.dot(x, w_ref[:, :n], preferred_element_type=F32)
-        up = jnp.dot(x, w_ref[:, n : 2 * n], preferred_element_type=F32)
-        d_mixed = jnp.dot(c_ref[...], w_ref[:, 2 * n :], preferred_element_type=F32)
-        sig = 1.0 / (1.0 + jnp.exp(-gate))
-        silu = gate * sig
-        o_ref[:, :n] = (d_mixed * up * (sig * (1.0 + gate * (1.0 - sig)))).astype(BF16)
-        o_ref[:, n : 2 * n] = (d_mixed * silu).astype(BF16)
-        o_ref[:, 2 * n :] = (silu * up).astype(BF16)
-
-    either(halves, body, (xl_ref, cl_ref), (xh_ref, ch_ref))
+    x = next_piece(refs[:count], x_buffer, x_sems)
+    c = next_piece(refs[count : 2 * count], c_buffer, c_sems)
+    gate = jnp.dot(x, w_ref[:, :n], preferred_element_type=F32)
+    up = jnp.dot(x, w_ref[:, n : 2 * n], preferred_element_type=F32)
+    d_mixed = jnp.dot(c, w_ref[:, 2 * n :], preferred_element_type=F32)
+    sig = 1.0 / (1.0 + jnp.exp(-gate))
+    silu = gate * sig
+    o_ref[:, :n] = (d_mixed * up * (sig * (1.0 + gate * (1.0 - sig)))).astype(BF16)
+    o_ref[:, n : 2 * n] = (d_mixed * silu).astype(BF16)
+    o_ref[:, 2 * n :] = (silu * up).astype(BF16)
 
 
 def ffn_chunk(x, cot, w):
-    half_rows, depth = x[0].shape
-    rows = 2 * half_rows
+    step, depth = x[0].shape
+    rows = len(x) * step
     width = w.shape[1]
-    step = min(512, half_rows)
-    halves = half_rows // step
     return pl.pallas_call(
-        functools.partial(ffn_kernel, halves),
+        functools.partial(ffn_kernel, len(x)),
         out_shape=jax.ShapeDtypeStruct((rows, width), BF16),
-        grid=(rows // step,),
-        in_specs=two_halves(step, depth, halves)
-        + two_halves(step, depth, halves)
+        grid=(len(x),),
+        in_specs=[pl.BlockSpec(memory_space=pl.ANY)] * (2 * len(x))
         + [pl.BlockSpec((depth, width), lambda i: (0, 0))],
         out_specs=pl.BlockSpec((step, width), lambda i: (i, 0)),
+        scratch_shapes=stream_scratch(2, step, depth),
         compiler_params=params(),
         cost_estimate=cost(),
         name="ffn",
@@ -187,30 +194,30 @@
 DOWN = (((0,), (0,)), ((), ()))
 
 
-def grads_kernel(split, xl_ref, xh_ref, yl_ref, yh_ref, a_ref, b_ref, o_ref):
-    half_rows = xl_ref.shape[0]
-
-    def both(low_ref, high_ref, right_ref, columns):
-        low = right_ref[:half_rows, columns].astype(BF16)
-        high = right_ref[half_rows:, columns].astype(BF16)
-        total = lax.dot_general(low_ref[...], low, DOWN, preferred_element_type=F32)
-        return total + lax.dot_general(high_ref[...], high, DOWN, preferred_element_type=F32)
-
-    o_ref[:, :split] = both(xl_ref, xh_ref, a_ref, slice(None)).astype(BF16)
-    o_ref[:, split:] = both(yl_ref, yh_ref, b_ref, slice(None)).astype(BF16)
+def grads_kernel(x_count, y_count, *refs):
+    a_ref, b_ref, o_ref = refs[x_count + y_count :]
+    split = a_ref.shape[1]
+
+    def product(tall_refs, right_ref):
+        tall = jnp.concatenate([ref[...] for ref in tall_refs], axis=0)
+        return lax.dot_general(
+            tall, right_ref[...].astype(BF16), DOWN, preferred_element_type=F32
+        ).astype(BF16)
+
+    o_ref[:, :split] = product(refs[:x_count], a_ref)
+    o_ref[:, split:] = product(refs[x_count : x_count + y_count], b_ref)
 
 
 def weight_grads(x, a, a_width, a_column, y, b, b_width, b_column):
-    half_rows, depth = x[0].shape
-    rows = 2 * half_rows
+    depth = x[0].shape[1]
+    rows = a.shape[0]
     width = a_width + b_width
     step = 512
-    tall = pl.BlockSpec((half_rows, step), lambda i: (0, i))
     return pl.pallas_call(
-        functools.partial(grads_kernel, a_width),
+        functools.partial(grads_kernel, len(x), len(y)),
         out_shape=jax.ShapeDtypeStruct((depth, width), BF16),
         grid=(depth // step,),
-        in_specs=[tall] * 4
+        in_specs=[pl.BlockSpec((piece.shape[0], step), lambda i: (0, i)) for piece in (*x, *y)]
         + [
             pl.BlockSpec((rows, a_width), lambda i: (0, a_column)),
             pl.BlockSpec((rows, b_width), lambda i: (0, b_column)),
@@ -258,25 +265,23 @@
     )(*[term[0] for term in terms], *[term[2] for term in terms])
 
 
-def front_kernel(halves, low_ref, high_ref, w_ref, o_ref):
-    def body(x_ref):
-        o_ref[...] = jnp.dot(x_ref[...], w_ref[...], preferred_element_type=F32).astype(BF16)
-
-    either(halves, body, (low_ref,), (high_ref,))
+def front_kernel(count, *refs):
+    w_ref, o_ref, buffer, sems = refs[count:]
+    x = next_piece(refs[:count], buffer, sems)
+    o_ref[...] = jnp.dot(x, w_ref[...], preferred_element_type=F32).astype(BF16)
 
 
 def front_product(x, w, width, column):
-    half_rows, depth = x[0].shape
-    rows = 2 * half_rows
-    step = min(512, half_rows)
-    halves = half_rows // step
+    step, depth = x[0].shape
+    rows = len(x) * step
     return pl.pallas_call(
-        functools.partial(front_kernel, halves),
+        functools.partial(front_kernel, len(x)),
         out_shape=jax.ShapeDtypeStruct((rows, width), BF16),
-        grid=(rows // step,),
-        in_specs=two_halves(step, depth, halves)
+        grid=(len(x),),
+        in_specs=[pl.BlockSpec(memory_space=pl.ANY)] * len(x)
         + [pl.BlockSpec((depth, width), lambda i: (0, column))],
         out_specs=pl.BlockSpec((step, width), lambda i: (i, 0)),
+        scratch_shapes=stream_scratch(1, step, depth),
         compiler_params=params(),
         cost_estimate=cost(),
         name="front",
@@ -347,7 +352,7 @@
     o_ref[:, q_width:] = packed
 
 
-def attend(qkv, place, first, start, q_width):
+def attend(qkv, depth, place, first, start, q_width):
     rows = qkv.shape[0]
     blocks = rows // BLOCK
     return pl.pallas_call(
@@ -357,8 +362,8 @@
             num_scalar_prefetch=2,
             grid=(blocks,),
             in_specs=[
-                pl.BlockSpec((BLOCK, q_width), lambda i, place, first: (place[i], 0)),
-                pl.BlockSpec((rows, 128), lambda i, place, first: (0, q_width // 128)),
+                pl.BlockSpec((BLOCK, q_width), lambda i, place, first: (place[i], depth // q_width)),
+                pl.BlockSpec((rows, 128), lambda i, place, first: (0, (depth + q_width) // 128)),
                 pl.BlockSpec((BLOCK, 1), lambda i, place, first: (i, 0)),
             ],
             out_specs=pl.BlockSpec((BLOCK, q_width + 128), lambda i, place, first: (place[i], 0)),
@@ -441,9 +446,9 @@
             o_ref[there, q_width:] = jnp.where(lane < HEAD_DIM, turned, u).astype(BF16)
 
 
-def attend_back(qkv, d_heads, heads, place, first, start, cos, sin):
-    rows, width = qkv.shape
-    q_width = d_heads.shape[1]
+def attend_back(qkv, depth, d_heads, heads, place, first, start, cos, sin):
+    rows, q_width = d_heads.shape
+    width = q_width + 128
     blocks = rows // BLOCK
     by_place = lambda i, place, first: (place[i], 0)
     whole = lambda i, place, first: (0, 0)
@@ -454,10 +459,10 @@
             num_scalar_prefetch=2,
             grid=(blocks,),
             in_specs=[
-                pl.BlockSpec((BLOCK, q_width), by_place),
+                pl.BlockSpec((BLOCK, q_width), lambda i, place, first: (place[i], depth // q_width)),
                 pl.BlockSpec((BLOCK, q_width), by_place),
                 pl.BlockSpec((BLOCK, q_width + 128), by_place),
-                pl.BlockSpec((rows, 128), lambda i, place, first: (0, q_width // 128)),
+                pl.BlockSpec((rows, 128), lambda i, place, first: (0, (depth + q_width) // 128)),
                 pl.BlockSpec((BLOCK, 1), lambda i, place, first: (i, 0)),
                 pl.BlockSpec((rows, 128), whole),
                 pl.BlockSpec((rows, 128), whole),
@@ -502,16 +507,18 @@
 
 def share_rows(own, beside=()):
     beside = list(beside) + [()] * (2 - len(beside))
-    one = after(swap_first(own), *beside[0])
-    parts = (own, one, swap_second(own), after(swap_second(one), *beside[1]))
-    return jnp.concatenate(parts), jnp.concatenate([swap_core(part) for part in parts])
-
-
-def ring_over(shard, count):
+    one, two, *_ = lax.optimization_barrier((swap_first(own), swap_second(own), *beside[0]))
+    early = tuple(swap_core(part) for part in (own, one, two))
+    last = after(swap_second(one), *early, *beside[1])
+    return (own, one, two, last, *early, swap_core(last))
+
+
+def ring_over(shard, count, held):
     cycle = [(at, (at + 1) % count) for at in range(count)]
     pieces = [shard]
-    for _ in range(count - 1):
-        pieces.append(lax.ppermute(pieces[-1], "fsdp", cycle))
+    for step in range(count - 1):
+        sent = after(pieces[-1], held) if step == 1 else pieces[-1]
+        pieces.append(lax.ppermute(sent, "fsdp", cycle))
     return pieces
 
 
@@ -525,13 +532,6 @@
         owner = lax.rem(here + count - back, count)
         whole = lax.dynamic_update_slice_in_dim(whole, piece, owner * size, axis)
     return whole
-
-
-def shifts_over(shard, count):
-    return [shard] + [
-        lax.ppermute(shard, "fsdp", [(at, (at + by) % count) for at in range(count)])
-        for by in range(1, count)
-    ]
 
 
 def share_in_ctx(own, beside, y, core):
@@ -585,9 +585,15 @@
     q_width, kv_width = q_half.shape[1], k_half.shape[1]
     attn_shard = jnp.concatenate([o_half, q_half, k_half, v_half], axis=1)
     fsdp = lax.axis_size("fsdp")
-    attn_ring = ring_over(attn_shard, fsdp)
-    attn_full = in_place(attn_ring, 0)
-    gains = in_place(shifts_over(jnp.stack([attn_gain, ffn_gain]), fsdp), 1)
+    gain_rows = jnp.stack([attn_gain, ffn_gain])
+    gain_width = attn_gain.shape[0]
+    extra = ((0, 14), (0, attn_shard.shape[1] - gain_width))
+    tokens_low = lax.dynamic_slice_in_dim(tokens, tp * own_rows, own_rows, 0)
+    tokens_one = swap_first(tokens_low)
+    attn_ring = ring_over(jnp.concatenate([attn_shard, jnp.pad(gain_rows, extra)]), fsdp, tokens_one)
+    own_depth = attn_shard.shape[0]
+    attn_full = in_place([piece[:own_depth] for piece in attn_ring], 0)
+    gains = in_place([piece[own_depth : own_depth + 2, :gain_width] for piece in attn_ring], 1)
     gain_one = gains[0].astype(F32)[None]
     gain_two = gains[1].astype(F32)[None]
     ff_half = gate_weight.shape[1] // 2
@@ -647,15 +653,16 @@
     sin = jnp.where((lane % 64 < 32)[None], -jnp.sin(angles), jnp.sin(angles))
     start_column = start_of[:, None]
 
-    tokens_low = lax.dynamic_slice_in_dim(tokens, tp * own_rows, own_rows, 0)
     cot_low = lax.dynamic_slice_in_dim(cotangent, tp * own_rows, own_rows, 0)
     tokens_own, cot_own = tokens_low.astype(F32), cot_low.astype(F32)
-    group_tokens = share_rows(tokens_low, [[piece] for piece in attn_ring[1:3]])
-    attn_full, first_shard, cot_low, cos, sin, gain_one, *group_tokens = lax.optimization_barrier(
-        (attn_full, ffn_shards[0], cot_low, cos, sin, gain_one, *group_tokens)
+    group_tokens = (tokens_low, tokens_one, swap_second(tokens_low), swap_second(tokens_one))
+    first_shard = after(ffn_shards[0], attn_ring[-1], *group_tokens[2:])
+    group_tokens = group_tokens + tuple(swap_core(part) for part in group_tokens)
+    attn_full, cot_low, cos, sin, gain_one, *group_tokens = lax.optimization_barrier(
+        (attn_full, cot_low, cos, sin, gain_one, *group_tokens)
     )
     qkv = project_qkv(group_tokens, gain_one, attn_full, q_width, cos, sin)
-    heads = attend(qkv, place, first, start_column, q_width)
+    heads = attend(qkv, depth, place, first, start_column, q_width)
     cot = share_rows(cot_low, [[qkv], [heads]])
     ffn_full = [
         lax.all_gather(shard, "fsdp", axis=0, tiled=True)
@@ -671,7 +678,8 @@
     acts = []
     grad_parts = []
     for part in range(CHUNKS):
-        acts.append(ffn_chunk(after(normed_two, *grad_parts), cot, ffn_full[part]))
+        normed_two = (after(normed_two[0], *grad_parts), *normed_two[1:])
+        acts.append(ffn_chunk(normed_two, cot, ffn_full[part]))
         grad_parts.append(
             weight_grads(normed_two, acts[part], 2 * chunk, 0, cot, acts[part], chunk, 2)
         )
@@ -684,48 +692,43 @@
     d_hidden = cot_own + rms_back(hidden, gain_two, d_normed_two)
     ffn_sent = [back_product(ffn_terms, at, 4) for at in (3, 2)]
     ffn_mine = back_product(ffn_terms, 0, 2)
-    d_attn = share_rows(d_hidden.astype(BF16), [[reduced[0]], [*ffn_sent, ffn_mine]])
+    d_attn = share_rows(d_hidden.astype(BF16), [[*ffn_sent, ffn_mine], [reduced[0]]])
 
     d_heads = front_product(d_attn, attn_full, q_width, 0)
-    arrived = [swap_core(after(piece, d_attn[1])) for piece in ffn_sent]
+    arrived = [swap_core(after(piece, *d_attn[4:])) for piece in ffn_sent]
     half_rows = ffn_mine.shape[0] // 2
     ffn_far, ffn_near = y_first(
         ffn_mine[half_rows:] + arrived[0], ffn_mine[:half_rows] + arrived[1], core
     )
     d_heads, ffn_far, reduced[0] = lax.optimization_barrier((d_heads, ffn_far, reduced[0]))
     other_reduced = [swap_x(reduced[0])]
-    d_qkv = attend_back(qkv, d_heads, heads, place, first, start_column, cos, sin)
+    d_qkv = attend_back(qkv, depth, d_heads, heads, place, first, start_column, cos, sin)
     ffn_near = ffn_near + after(swap_y(ffn_far), d_qkv)
-    d_qkv = after(d_qkv, ffn_near, other_reduced[0])
-    normed = []
-    for part in group_tokens:
-        wide = part.astype(F32)
-        normed.append((wide * inv_rms(wide) * gain_one).astype(BF16))
+    d_qkv = after(d_qkv, ffn_near, other_reduced[0], *reduced[1:])
+    ffn_sum = ffn_near[:own_rows].astype(F32) + swap_x(ffn_near[own_rows:]).astype(F32)
+    result_own = (hidden + ffn_sum).astype(BF16)
     normed_far, normed_near = sum_cores(
         [
             (d_qkv, 0, attn_full, 1, q_width),
             (d_qkv, q_width // 128, attn_full, 2 * q_width // 128, 128),
         ]
     )
+    normed_far = after(normed_far, result_own)
     attn_grad = weight_grads(
-        d_attn, heads, q_width, 0, normed, d_qkv, q_width + 128, 0
-    )
+        d_attn, heads, q_width, 0, (qkv,), d_qkv, q_width + 128, 0
+    )
+    d_normed = sum_last(sum_pairs(normed_far, normed_near), attn_grad)
+    tokens_grad_own = (d_hidden + rms_back(tokens_own, gain_one, d_normed)).astype(BF16)
     for part in range(1, CHUNKS):
-        reduced[part] = after(reduced[part], attn_grad)
-    d_normed = sum_last(sum_pairs(normed_far, normed_near), attn_grad, *reduced[1:])
-    for part in range(1, CHUNKS):
-        reduced[part] = after(reduced[part], d_normed)
+        reduced[part] = after(reduced[part], attn_grad, tokens_grad_own)
         other_reduced.append(swap_x(reduced[part]))
-    ffn_near = after(ffn_near, normed_far)
-    ffn_sum = ffn_near[:own_rows].astype(F32) + swap_x(ffn_near[own_rows:]).astype(F32)
-    result_own = (hidden + ffn_sum).astype(BF16)
-    result = share_in_ctx(result_own, swap_y(result_own), y, core)
-    tokens_grad_own = (d_hidden + rms_back(tokens_own, gain_one, d_normed)).astype(BF16)
     tokens_grad_beside = swap_y(tokens_grad_own)
     tokens_grad = share_in_ctx(tokens_grad_own, tokens_grad_beside, y, core)
+    result_own = after(result_own, tokens_grad_own)
+    result = share_in_ctx(result_own, swap_y(result_own), y, core)
 
     attn_reduced = lax.psum_scatter(attn_grad, "fsdp", scatter_dimension=0, tiled=True)
-    attn_reduced = after(attn_reduced, tokens_grad_beside)
+    attn_reduced = after(attn_reduced, tokens_grad_beside, *other_reduced)
 
     def gain_part(pairs):
         return sum(jnp.sum(mine.astype(F32) * grad.astype(F32), axis=1) for mine, grad in pairs)

time: 740 us -> 713 us (0.964)
  other arithmetic: 99.7 us -> 86.3 us
  local copies, waits for them, and re-layouts: 42.8 us -> 32.3 us
  starting transfers between devices: 55.7 us -> 46.8 us
    ppermute x7, waiting for transfers between devices: 108 us -> 43.5 us  [swap_first(): return lax.ppermute(v, ('ctx', 'tp'), FIRST)]
    ppermute x11, waiting for transfers between devices: 45.8 us -> 94.1 us  [swap_second(): return lax.ppermute(v, ('ctx', 'tp'), SECOND)]
    ppermute x5, waiting for transfers between devices: 40.4 us -> 15 us  [swap_x(): return lax.ppermute(v, 'ctx', PAIR)]
    ppermute x4, waiting for transfers between devices: 30.7 us -> 46.5 us  [swap_y(): return lax.ppermute(v, 'tp', ACROSS)]
    concatenate x4 -> x1, other arithmetic: 14 us -> 0.12 us  [shards(): jnp.concatenate([attn_shard, jnp.pad(gain_rows, extra)])]
    ppermute x6 -> x3, starting transfers between devices: 13.6 us -> 1.69 us  [ring_over(): pieces.append(lax.ppermute(sent, 'fsdp', cycle))]
    ppermute x28, waiting for transfers between devices: 0.19 us -> 12.1 us  [swap_core(): return lax.ppermute(v, 'tp', CORE)]
    unnamed x105 -> x133, local copies, waits for them, and re-layouts: 16.2 us -> 5.21 us
  transfers between devices with their start and end apart: 66 -> 63, of which waited for: 24 -> 30; matrix products, arithmetic and copies ran while one was open for 17% -> 15% of each run, Pallas kernels for 33% -> 35%
where the time goes in v4:
time: 713 us; the launch traced here: 705 us
  waiting for transfers between devices  274 us (38%)
  Pallas kernels  251 us (35%)
  other arithmetic  86.3 us (12%)
  starting transfers between devices  46.8 us (7%)
  local copies, waits for them, and re-layouts  32.3 us (5%)
  between operations  15.1 us (2%)
    ppermute x11, waiting for transfers between devices, swap_second(): return lax.ppermute(v, ('ctx', 'tp'), SECOND)  94.1 us
    pallas_call x11, Pallas kernels, back_product(): pl.pallas_call(back_kernel, out_shape=jax.ShapeDtypeStruct((rows, depth),...  75.5 us
    pallas_call x3, Pallas kernels, weight_grads(): pl.pallas_call(functools.partial(grads_kernel, len(x), len(y)), out_shape...  51.1 us
    ppermute x4, waiting for transfers between devices, swap_y(): return lax.ppermute(v, 'tp', ACROSS)  46.5 us
    ppermute x7, waiting for transfers between devices, swap_first(): return lax.ppermute(v, ('ctx', 'tp'), FIRST)  43.5 us
    pallas_call x2, Pallas kernels, ffn_chunk(): pl.pallas_call(functools.partial(ffn_kernel, len(x)), out_shape=jax.Shape...  43.5 us
    ppermute x3, waiting for transfers between devices, ring_over(): pieces.append(lax.ppermute(sent, 'fsdp', cycle))  39.7 us
    pallas_call x1, Pallas kernels, attend_back(): pl.pallas_call(attend_back_kernel, out_shape=jax.ShapeDtypeStruct((rows,...  33.7 us
  transfers between devices with their start and end apart: 63, of which 30 were waited for; matrix products, arithmetic and copies ran while one was open for 15% of the time, Pallas kernels for 35%

profile of v4, /device:TPU:0, one launch (start us, length us, event | category | flops | bytes accessed | tf_op | source)
XLA Modules:
  0.0 704.9 jit_solution(12766979528453611270)
XLA Ops:
  8.7 3.0 collective-permute-start.1
  14.8 16.9 %collective-permute-done = bf16[528,640]{1,0:T(8,128)(2,1)S(1)} collective-permute-done((bf16[528,640]{1,0:T(8,128)(2,1)S(1)}, bf16[528,640]{1,0:T(8,128)(2,1)S(1)}, u32[]{:S(2)}, u32[]{:S(2)}) %collective-permute-start) | collective-permute-done | bytes 675872 | tf_op jit(solution)/shard_map/ppermute | solution.py:521
  34.6 14.9 %collective-permute-done.2 = bf16[528,640]{1,0:T(8,128)(2,1)} collective-permute-done((bf16[528,640]{1,0:T(8,128)(2,1)S(1)}, bf16[528,640]{1,0:T(8,128)(2,1)}, u32[]{:S(2)}, u32[]{:S(2)}) %collective-permute-start.2) | collective-permute-done | bytes 675872 | tf_op jit(solution)/shard_map/ppermute | solution.py:521
  58.7 7.8 %collective-permute-done.3 = bf16[528,640]{1,0:T(8,128)(2,1)} collective-permute-done((bf16[528,640]{1,0:T(8,128)(2,1)}, bf16[528,640]{1,0:T(8,128)(2,1)}, u32[]{:S(2)}, u32[]{:S(2)}) %collective-permute-start.3) | collective-permute-done | bytes 675872 | tf_op jit(solution)/shard_map/ppermute | solution.py:521
  70.1 5.6 negate_select_fusion
  82.0 4.0 collective-permute-start.10
  86.1 15.3 %qkv.1.q_ref.kv_ref.refs_8_ = bf16[2048,2432]{1,0:T(8,128)(2,1)} custom-call(bf16[256,2048]{1,0:T(8,128)(2,1)} %copy-done.32, bf16[256,2048]{1,0:T(8,128)(2,1)} %copy-done.50, bf16[256,2048]{1,0:T(8,128)(2,1)} %collective-permute-done.4.refs_2_, bf16[256,2048]{1,0:T(8,128)(2,1)} %collective-permute-done.5.refs_3_, ...), custom_call_target="tpu_custom_call" | custom-call | flops 1 | bytes 1 | tf_op jit(solution)/shard_map/qkv/pallas_call | solution.py:141
  101.5 3.7 collective-permute-done.11.refs_10_
  105.2 4.9 collective-permute-done.10.refs_9_
  113.1 21.8 %attend.1.refs_0_.h_ref.refs_9_ = f32[2048,384]{1,0:T(8,128)} custom-call(s32[8]{0:T(128)} %select_reduce_fusion.2.place, s32[8]{0:T(128)} %and_select_fusion.2.first, bf16[2048,2432]{1,0:T(8,128)(2,1)} %qkv.1.q_ref.kv_ref.refs_8_, bf16[2048,2432]{1,0:T(8,128)(2,1)} %qkv.1.q_ref.kv_ref.refs_8_, s32[2048,1]{1,0:T(8,128)} %copy.28.start_ref), custom_call_target="tpu_custom_call" | custom-call | flops 1 | bytes 1 | tf_op jit(solution)/shard_map/attend/pallas_call | solution.py:358
  139.0 3.4 back.13
  144.5 3.5 back.12
  147.9 4.2 back.11
  155.7 25.2 %collective-permute-done.19 = bf16[512,2048]{1,0:T(8,128)(2,1)S(1)} collective-permute-done((bf16[512,2048]{1,0:T(8,128)(2,1)S(1)}, bf16[512,2048]{1,0:T(8,128)(2,1)S(1)}, u32[]{:S(2)}, u32[]{:S(2)}) %collective-permute-start.19) | collective-permute-done | bytes 2097184 | tf_op jit(solution)/shard_map/ppermute | solution.py:58
  183.5 13.3 %collective-permute-done.20 = bf16[256,2048]{1,0:T(8,128)(2,1)S(1)} collective-permute-done((bf16[256,2048]{1,0:T(8,128)(2,1)S(1)}, bf16[256,2048]{1,0:T(8,128)(2,1)S(1)}, u32[]{:S(2)}, u32[]{:S(2)}) %collective-permute-start.20) | collective-permute-done | bytes 1048608 | tf_op jit(solution)/shard_map/ppermute | solution.py:54
  203.5 22.6 %collective-permute-done.22.refs_2_ = bf16[256,2048]{1,0:T(8,128)(2,1)S(1)} collective-permute-done((bf16[256,2048]{1,0:T(8,128)(2,1)S(1)}, bf16[256,2048]{1,0:T(8,128)(2,1)S(1)}, u32[]{:S(2)}, u32[]{:S(2)}) %collective-permute-start.22) | collective-permute-done | bytes 1048608 | tf_op jit(solution)/shard_map/ppermute | solution.py:58
  230.3 11.1 %collective-permute-done.23.refs_3_ = bf16[256,2048]{1,0:T(8,128)(2,1)S(1)} collective-permute-done((bf16[256,2048]{1,0:T(8,128)(2,1)S(1)}, bf16[256,2048]{1,0:T(8,128)(2,1)S(1)}, u32[]{:S(2)}, u32[]{:S(2)}) %collective-permute-start.23) | collective-permute-done | bytes 1048608 | tf_op jit(solution)/shard_map/ppermute | solution.py:58
  244.3 21.8 %ffn.2.refs_16_.refs_17_.refs_0_ = bf16[2048,1536]{1,0:T(8,128)(2,1)} custom-call(bf16[256,2048]{1,0:T(8,128)(2,1)} %copy-done.1, bf16[256,2048]{1,0:T(8,128)(2,1)} %copy-done.7, bf16[256,2048]{1,0:T(8,128)(2,1)} %copy-done.6, bf16[256,2048]{1,0:T(8,128)(2,1)} %copy-done.11, bf16[256,2048]{1,0:T(8,128)(2,1)} %copy-done.8, bf16[256,2048]{1,0:T(8,128)(2,1)} %copy-done.10, ...), custom_call_target="tpu_custom_call" | custom-call | flops 1 | bytes 1 | tf_op jit(solution)/shard_map/ffn/pallas_call | solution.py:180
  266.1 19.2 %weight_grads.3 = bf16[2048,1536]{1,0:T(8,128)(2,1)} custom-call(bf16[256,2048]{1,0:T(8,128)(2,1)} %copy-done.1, bf16[256,2048]{1,0:T(8,128)(2,1)} %copy-done.7, bf16[256,2048]{1,0:T(8,128)(2,1)} %copy-done.6, bf16[256,2048]{1,0:T(8,128)(2,1)} %copy-done.11, bf16[256,2048]{1,0:T(8,128)(2,1)} %copy-done.8, bf16[256,2048]{1,0:T(8,128)(2,1)} %copy-done.10, ...), custom_call_target="tpu_custom_call" | custom-call | flops 1 | bytes 1 | tf_op jit(solution)/shard_map/weight_grads/pallas_call | solution.py:216
  285.9 11.2 %all-gather.5.cloned.1.call-done.refs_16_.refs_3_ = bf16[2048,1536]{1,0:T(8,128)(2,1)} async-done(((bf16[512,1536]{1,0:T(8,128)(2,1)}), bf16[2048,1536]{1,0:T(8,128)(2,1)}) %all-gather.5.cloned.1.call-update) | async-done | bytes 6291472 | tf_op jit(solution)/shard_map/all_gather | solution.py:668
  297.0 21.7 %ffn.3.refs_1_.refs_16_.refs_17_ = bf16[2048,1536]{1,0:T(8,128)(2,1)} custom-call(bf16[256,2048]{1,0:T(8,128)(2,1)} %copy-done.1, bf16[256,2048]{1,0:T(8,128)(2,1)} %copy-done.7, bf16[256,2048]{1,0:T(8,128)(2,1)} %copy-done.6, bf16[256,2048]{1,0:T(8,128)(2,1)} %copy-done.11, bf16[256,2048]{1,0:T(8,128)(2,1)} %copy-done.8, bf16[256,2048]{1,0:T(8,128)(2,1)} %copy-done.10, ...), custom_call_target="tpu_custom_call" | custom-call | flops 1 | bytes 1 | tf_op jit(solution)/shard_map/ffn/pallas_call | solution.py:180
  318.8 14.5 %back.17 = bf16[1024,2048]{1,0:T(8,128)(2,1)} custom-call(bf16[2048,1536]{1,0:T(8,128)(2,1)} %ffn.2.refs_16_.refs_17_.refs_0_, bf16[2048,1536]{1,0:T(8,128)(2,1)} %ffn.3.refs_1_.refs_16_.refs_17_, bf16[2048,1536]{1,0:T(8,128)(2,1)} %all-gather.3.cloned.1.call-done.refs_16_.refs_2_, bf16[2048,1536]{1,0:T(8,128)(2,1)} %all-gather.5.cloned.1.call-done.refs_16_.refs_3_), custom_call_target="tpu_custom_call" | custom-call | flops 1 | bytes 1 | tf_op jit(solution)/shard_map/back/pallas_call | solution.py:252
  333.3 14.5 %back.16 = bf16[1024,2048]{1,0:T(8,128)(2,1)} custom-call(bf16[2048,1536]{1,0:T(8,128)(2,1)} %ffn.2.refs_16_.refs_17_.refs_0_, bf16[2048,1536]{1,0:T(8,128)(2,1)} %ffn.3.refs_1_.refs_16_.refs_17_, bf16[2048,1536]{1,0:T(8,128)(2,1)} %all-gather.3.cloned.1.call-done.refs_16_.refs_2_, bf16[2048,1536]{1,0:T(8,128)(2,1)} %all-gather.5.cloned.1.call-done.refs_16_.refs_3_), custom_call_target="tpu_custom_call" | custom-call | flops 1 | bytes 1 | tf_op jit(solution)/shard_map/back/pallas_call | solution.py:252
  347.8 4.6 slice_add_fusion.3
  354.0 19.4 %weight_grads.4 = bf16[2048,1536]{1,0:T(8,128)(2,1)} custom-call(bf16[256,2048]{1,0:T(8,128)(2,1)} %copy-done.1, bf16[256,2048]{1,0:T(8,128)(2,1)} %copy-done.7, bf16[256,2048]{1,0:T(8,128)(2,1)} %copy-done.6, bf16[256,2048]{1,0:T(8,128)(2,1)} %copy-done.11, bf16[256,2048]{1,0:T(8,128)(2,1)} %copy-done.8, bf16[256,2048]{1,0:T(8,128)(2,1)} %copy-done.10, ...), custom_call_target="tpu_custom_call" | custom-call | flops 1 | bytes 1 | tf_op jit(solution)/shard_map/weight_grads/pallas_call | solution.py:216
  373.6 5.2 collective-permute-done.29
  378.8 3.3 fusion.9
  383.8 13.2 %collective-permute-done.30 = bf16[256,2048]{1,0:T(8,128)(2,1)S(1)} collective-permute-done((bf16[256,2048]{1,0:T(8,128)(2,1)S(1)}, bf16[256,2048]{1,0:T(8,128)(2,1)S(1)}, u32[]{:S(2)}, u32[]{:S(2)}) %collective-permute-start.30) | collective-permute-done | bytes 1048608 | tf_op jit(solution)/shard_map/ppermute | solution.py:54
  398.1 3.7 fusion.25
  404.8 6.3 back.18
  411.1 6.3 back.15
  417.4 9.1 %back.14 = bf16[1024,2048]{1,0:T(8,128)(2,1)} custom-call(bf16[2048,1536]{1,0:T(8,128)(2,1)} %ffn.2.refs_16_.refs_17_.refs_0_, bf16[2048,1536]{1,0:T(8,128)(2,1)} %ffn.3.refs_1_.refs_16_.refs_17_, bf16[2048,1536]{1,0:T(8,128)(2,1)} %all-gather.3.cloned.1.call-done.refs_16_.refs_2_, bf16[2048,1536]{1,0:T(8,128)(2,1)} %all-gather.5.cloned.1.call-done.refs_16_.refs_3_), custom_call_target="tpu_custom_call" | custom-call | flops 1 | bytes 1 | tf_op jit(solution)/shard_map/back/pallas_call | solution.py:252
  430.7 11.2 %collective-permute-done.36.refs_3_ = bf16[256,2048]{1,0:T(8,128)(2,1)S(1)} collective-permute-done((bf16[256,2048]{1,0:T(8,128)(2,1)S(1)}, bf16[256,2048]{1,0:T(8,128)(2,1)S(1)}, u32[]{:S(2)}, u32[]{:S(2)}) %collective-permute-start.36) | collective-permute-done | bytes 1048608 | tf_op jit(solution)/shard_map/ppermute | solution.py:58
  446.4 9.9 %front.1.d_ref = bf16[2048,256]{1,0:T(8,128)(2,1)} custom-call(bf16[256,2048]{1,0:T(8,128)(2,1)} %copy-done.15, bf16[256,2048]{1,0:T(8,128)(2,1)} %copy-done.28, bf16[256,2048]{1,0:T(8,128)(2,1)} %copy-done.27, bf16[256,2048]{1,0:T(8,128)(2,1)} %copy-done.31, bf16[256,2048]{1,0:T(8,128)(2,1)} %copy-done.29, ...), custom_call_target="tpu_custom_call" | custom-call | flops 1 | bytes 1 | tf_op jit(solution)/shard_map/front/pallas_call | solution.py:277
  463.0 33.7 %attend_back.1.refs_0_.refs_1_.refs_10_ = bf16[2048,384]{1,0:T(8,128)(2,1)} custom-call(s32[8]{0:T(128)} %select_reduce_fusion.2.place, s32[8]{0:T(128)} %and_select_fusion.2.first, bf16[2048,2432]{1,0:T(8,128)(2,1)} %qkv.1.q_ref.kv_ref.refs_8_, bf16[2048,256]{1,0:T(8,128)(2,1)} %front.1.d_ref, f32[2048,384]{1,0:T(8,128)} %attend.1.refs_0_.h_ref.refs_9_, ...), custom_call_target="tpu_custom_call" | custom-call | flops 1 | bytes 1 | tf_op jit(solution)/shard_map/attend_back/pallas_call | solution.py:455
  496.7 12.1 %collective-permute-done.40 = bf16[512,2048]{1,0:T(8,128)(2,1)S(1)} collective-permute-done((bf16[512,2048]{1,0:T(8,128)(2,1)}, bf16[512,2048]{1,0:T(8,128)(2,1)S(1)}, u32[]{:S(2)}, u32[]{:S(2)}) %collective-permute-start.40) | collective-permute-done | bytes 2097184 | tf_op jit(solution)/shard_map/ppermute | solution.py:46
  511.0 10.8 %reduce-scatter.6.cloned.1.call-done = bf16[512,1536]{1,0:T(8,128)(2,1)} async-done(((bf16[2048,1536]{1,0:T(8,128)(2,1)}), bf16[512,1536]{1,0:T(8,128)(2,1)}) %reduce-scatter.6.cloned.1.call-update) | async-done | bytes 1572880 | tf_op jit(solution)/shard_map/reduce_scatter | solution.py:687
  521.8 4.2 back.21
  528.6 4.1 back.20
  532.7 5.4 back.19
  538.1 15.0 %collective-permute-done.41 = bf16[256,2048]{1,0:T(8,128)(2,1)} collective-permute-done((bf16[256,2048]{1,0:T(8,128)(2,1)}, bf16[256,2048]{1,0:T(8,128)(2,1)}, u32[]{:S(2)}, u32[]{:S(2)}) %collective-permute-start.41) | collective-permute-done | bytes 1048608 | tf_op jit(solution)/shard_map/ppermute | solution.py:50
  553.0 3.4 add_convert_fusion
  559.5 12.6 %weight_grads.5 = bf16[2048,640]{1,0:T(8,128)(2,1)} custom-call(bf16[256,2048]{1,0:T(8,128)(2,1)} %copy-done.15, bf16[256,2048]{1,0:T(8,128)(2,1)} %copy-done.28, bf16[256,2048]{1,0:T(8,128)(2,1)} %copy-done.27, bf16[256,2048]{1,0:T(8,128)(2,1)} %copy-done.31, bf16[256,2048]{1,0:T(8,128)(2,1)} %copy-done.29, ...), custom_call_target="tpu_custom_call" | custom-call | flops 1 | bytes 1 | tf_op jit(solution)/shard_map/weight_grads/pallas_call | solution.py:216
  572.0 12.3 %collective-permute-done.45 = bf16[512,2048]{1,0:T(8,128)(2,1)} collective-permute-done((bf16[512,2048]{1,0:T(8,128)(2,1)}, bf16[512,2048]{1,0:T(8,128)(2,1)}, u32[]{:S(2)}, u32[]{:S(2)}) %collective-permute-start.45) | collective-permute-done | bytes 2097184 | tf_op jit(solution)/shard_map/ppermute | solution.py:58
  584.3 3.2 fusion.8
  591.7 12.1 %collective-permute-done.46 = bf16[256,2048]{1,0:T(8,128)(2,1)} collective-permute-done((bf16[256,2048]{1,0:T(8,128)(2,1)}, bf16[256,2048]{1,0:T(8,128)(2,1)}, u32[]{:S(2)}, u32[]{:S(2)}) %collective-permute-start.46) | collective-permute-done | bytes 1048608 | tf_op jit(solution)/shard_map/ppermute | solution.py:54
  605.9 3.4 fusion.6
  620.7 34.4 %collective-permute-done.47 = bf16[256,2048]{1,0:T(8,128)(2,1)} collective-permute-done((bf16[256,2048]{1,0:T(8,128)(2,1)S(1)}, bf16[256,2048]{1,0:T(8,128)(2,1)}, u32[]{:S(2)}, u32[]{:S(2)}) %collective-permute-start.47) | collective-permute-done | bytes 1048608 | tf_op jit(solution)/shard_map/ppermute | solution.py:46
  (339 shorter events, 146.7 us)
Async XLA Ops:
  7.2 174.6 %all-gather.3.cloned.1.call-start = ((), (), s32[]{:S(2)}) async-start(), calls=%async_computation.3 | async-start | bytes 7864320 | tf_op jit(solution)/shard_map/all_gather | solution.py:668
  8.7 23.1 %collective-permute-start.1 = (bf16[256,2048]{1,0:T(8,128)(2,1)S(1)}, bf16[256,2048]{1,0:T(8,128)(2,1)S(1)}, u32[]{:S(2)}, u32[]{:S(2)}) collective-permute-start(bf16[256,2048]{1,0:T(8,128)(2,1)S(1)} %constant_dynamic-slice_fusion.11.refs_0_), channel_id=1, source_target_pairs={{0,4},{1,3},{2,6},{3,1},{4,0},{5,7},{6,2},{7,5},{8,12},{9,11},{10,... | collective-permute-start | bytes 3145736 | tf_op jit(solution)/shard_map/ppermute | solution.py:54
  13.2 18.6 %collective-permute-start = (bf16[528,640]{1,0:T(8,128)(2,1)S(1)}, bf16[528,640]{1,0:T(8,128)(2,1)S(1)}, u32[]{:S(2)}, u32[]{:S(2)}) collective-permute-start(bf16[528,640]{1,0:T(8,128)(2,1)S(1)} %fusion.12), channel_id=1, source_target_pairs={{0,8},{8,16},{16,24},{24,0},{1,9},{9,17},{17,25},{25,1},{2,10},{10... | collective-permute-start | bytes 2027528 | tf_op jit(solution)/shard_map/ppermute | solution.py:521
  31.8 17.8 %collective-permute-start.2 = (bf16[528,640]{1,0:T(8,128)(2,1)S(1)}, bf16[528,640]{1,0:T(8,128)(2,1)}, u32[]{:S(2)}, u32[]{:S(2)}) collective-permute-start(bf16[528,640]{1,0:T(8,128)(2,1)S(1)} %collective-permute-done), channel_id=1, source_target_pairs={{0,8},{8,16},{16,24},{24,0},{1,9},{9,17},{17,25},{25,1},{2,10},{10... | collective-permute-start | bytes 2027528 | tf_op jit(solution)/shard_map/ppermute | solution.py:521
  32.6 23.8 %collective-permute-start.4 = (bf16[256,2048]{1,0:T(8,128)(2,1)S(1)}, bf16[256,2048]{1,0:T(8,128)(2,1)}, u32[]{:S(2)}, u32[]{:S(2)}) collective-permute-start(bf16[256,2048]{1,0:T(8,128)(2,1)S(1)} %constant_dynamic-slice_fusion.11.refs_0_), channel_id=1, source_target_pairs={{0,2},{1,5},{2,0},{3,7},{4,6},{5,1},{6,4},{7,3},{8,10},{9,13},{10,... | collective-permute-start | bytes 3145736 | tf_op jit(solution)/shard_map/ppermute | solution.py:58
  33.1 25.6 %collective-permute-start.5 = (bf16[256,2048]{1,0:T(8,128)(2,1)S(1)}, bf16[256,2048]{1,0:T(8,128)(2,1)}, u32[]{:S(2)}, u32[]{:S(2)}) collective-permute-start(bf16[256,2048]{1,0:T(8,128)(2,1)S(1)} %collective-permute-done.1.refs_1_), channel_id=1, source_target_pairs={{0,2},{1,5},{2,0},{3,7},{4,6},{5,1},{6,4},{7,3},{8,10},{9,13},{10,... | collective-permute-start | bytes 3145736 | tf_op jit(solution)/shard_map/ppermute | solution.py:58
  49.5 17.0 %collective-permute-start.3 = (bf16[528,640]{1,0:T(8,128)(2,1)}, bf16[528,640]{1,0:T(8,128)(2,1)}, u32[]{:S(2)}, u32[]{:S(2)}) collective-permute-start(bf16[528,640]{1,0:T(8,128)(2,1)} %collective-permute-done.2), channel_id=1, source_target_pairs={{0,8},{8,16},{16,24},{24,0},{1,9},{9,17},{17,25},{25,1},{2,10},{10... | collective-permute-start | bytes 2027528 | tf_op jit(solution)/shard_map/ppermute | solution.py:521
  66.6 230.5 %all-gather.5.cloned.1.call-start = ((), (), s32[]{:S(2)}) async-start(), calls=%async_computation.4 | async-start | bytes 7864320 | tf_op jit(solution)/shard_map/all_gather | solution.py:668
  66.6 14.9 %collective-permute-start.6 = (bf16[256,2048]{1,0:T(8,128)(2,1)S(1)}, bf16[256,2048]{1,0:T(8,128)(2,1)}, u32[]{:S(2)}, u32[]{:S(2)}) collective-permute-start(bf16[256,2048]{1,0:T(8,128)(2,1)S(1)} %constant_dynamic-slice_fusion.11.refs_0_), channel_id=1, source_target_pairs={{0,1},{1,0},{2,3},{3,2},{4,5},{5,4},{6,7},{7,6},{8,9},{9,8},{10,11... | collective-permute-start | bytes 3145736 | tf_op jit(solution)/shard_map/ppermute | solution.py:42
  82.0 23.2 %collective-permute-start.11 = (bf16[256,2048]{1,0:T(8,128)(2,1)}, bf16[256,2048]{1,0:T(8,128)(2,1)}, u32[]{:S(2)}, u32[]{:S(2)}) collective-permute-start(bf16[256,2048]{1,0:T(8,128)(2,1)} %constant_dynamic-slice_fusion.6.refs_8_), channel_id=1, source_target_pairs={{0,2},{1,5},{2,0},{3,7},{4,6},{5,1},{6,4},{7,3},{8,10},{9,13},{10,... | collective-permute-start | bytes 3145736 | tf_op jit(solution)/shard_map/ppermute | solution.py:58
  82.0 28.0 %collective-permute-start.10 = (bf16[256,2048]{1,0:T(8,128)(2,1)}, bf16[256,2048]{1,0:T(8,128)(2,1)}, u32[]{:S(2)}, u32[]{:S(2)}) collective-permute-start(bf16[256,2048]{1,0:T(8,128)(2,1)} %constant_dynamic-slice_fusion.6.refs_8_), channel_id=1, source_target_pairs={{0,4},{1,3},{2,6},{3,1},{4,0},{5,7},{6,2},{7,5},{8,12},{9,11},{10,... | collective-permute-start | bytes 3145736 | tf_op jit(solution)/shard_map/ppermute | solution.py:54
  86.0 48.9 %collective-permute-start.13 = (bf16[256,2048]{1,0:T(8,128)(2,1)}, bf16[256,2048]{1,0:T(8,128)(2,1)}, u32[]{:S(2)}, u32[]{:S(2)}) collective-permute-start(bf16[256,2048]{1,0:T(8,128)(2,1)} %constant_dynamic-slice_fusion.6.refs_8_), channel_id=1, source_target_pairs={{0,1},{1,0},{2,3},{3,2},{4,5},{5,4},{6,7},{7,6},{8,9},{9,8},{10,11... | collective-permute-start | bytes 3145736 | tf_op jit(solution)/shard_map/ppermute | solution.py:42
  110.0 25.0 %collective-permute-start.15 = (bf16[256,2048]{1,0:T(8,128)(2,1)}, bf16[256,2048]{1,0:T(8,128)(2,1)S(1)}, u32[]{:S(2)}, u32[]{:S(2)}) collective-permute-start(bf16[256,2048]{1,0:T(8,128)(2,1)} %collective-permute-done.11.refs_10_), channel_id=1, source_target_pairs={{0,1},{1,0},{2,3},{3,2},{4,5},{5,4},{6,7},{7,6},{8,9},{9,8},{10,11... | collective-permute-start | bytes 3145736 | tf_op jit(solution)/shard_map/ppermute | solution.py:42
  110.0 25.0 %collective-permute-start.14 = (bf16[256,2048]{1,0:T(8,128)(2,1)}, bf16[256,2048]{1,0:T(8,128)(2,1)S(1)}, u32[]{:S(2)}, u32[]{:S(2)}) collective-permute-start(bf16[256,2048]{1,0:T(8,128)(2,1)} %collective-permute-done.10.refs_9_), channel_id=1, source_target_pairs={{0,1},{1,0},{2,3},{3,2},{4,5},{5,4},{6,7},{7,6},{8,9},{9,8},{10,11... | collective-permute-start | bytes 3145736 | tf_op jit(solution)/shard_map/ppermute | solution.py:42
  110.5 24.5 %collective-permute-start.12 = (bf16[256,2048]{1,0:T(8,128)(2,1)}, bf16[256,2048]{1,0:T(8,128)(2,1)S(1)}, u32[]{:S(2)}, u32[]{:S(2)}) collective-permute-start(bf16[256,2048]{1,0:T(8,128)(2,1)} %collective-permute-done.10.refs_9_), channel_id=1, source_target_pairs={{0,2},{1,5},{2,0},{3,7},{4,6},{5,1},{6,4},{7,3},{8,10},{9,13},{10,... | collective-permute-start | bytes 3145736 | tf_op jit(solution)/shard_map/ppermute | solution.py:58
  144.2 298.7 %reduce-scatter.4.cloned.1.call-start = ((), (), s32[]{:S(2)}) async-start(), calls=%async_computation.5 | async-start | bytes 7864320 | tf_op jit(solution)/shard_map/reduce_scatter | solution.py:687
  154.8 26.1 %collective-permute-start.19 = (bf16[512,2048]{1,0:T(8,128)(2,1)S(1)}, bf16[512,2048]{1,0:T(8,128)(2,1)S(1)}, u32[]{:S(2)}, u32[]{:S(2)}) collective-permute-start(bf16[512,2048]{1,0:T(8,128)(2,1)S(1)} %slice_add_fusion.6), channel_id=1, source_target_pairs={{0,2},{1,5},{2,0},{3,7},{4,6},{5,1},{6,4},{7,3},{8,10},{9,13},{10,... | collective-permute-start | bytes 6291464 | tf_op jit(solution)/shard_map/ppermute | solution.py:58
  155.5 25.3 %collective-permute-start.17 = (bf16[512,2048]{1,0:T(8,128)(2,1)S(1)}, bf16[512,2048]{1,0:T(8,128)(2,1)S(1)}, u32[]{:S(2)}, u32[]{:S(2)}) collective-permute-start(bf16[512,2048]{1,0:T(8,128)(2,1)S(1)} %copy-done.48), channel_id=1, source_target_pairs={{0,1},{1,0},{2,3},{3,2},{4,5},{5,4},{6,7},{7,6},{8,9},{9,8},{10,11... | collective-permute-start | bytes 6291464 | tf_op jit(solution)/shard_map/ppermute | solution.py:42
  182.0 14.9 %collective-permute-start.20 = (bf16[256,2048]{1,0:T(8,128)(2,1)S(1)}, bf16[256,2048]{1,0:T(8,128)(2,1)S(1)}, u32[]{:S(2)}, u32[]{:S(2)}) collective-permute-start(bf16[256,2048]{1,0:T(8,128)(2,1)S(1)} %slice.186), channel_id=1, source_target_pairs={{0,4},{1,3},{2,6},{3,1},{4,0},{5,7},{6,2},{7,5},{8,12},{9,11},{10,... | collective-permute-start | bytes 3145736 | tf_op jit(solution)/shard_map/ppermute | solution.py:54
  200.5 25.6 %collective-permute-start.22 = (bf16[256,2048]{1,0:T(8,128)(2,1)S(1)}, bf16[256,2048]{1,0:T(8,128)(2,1)S(1)}, u32[]{:S(2)}, u32[]{:S(2)}) collective-permute-start(bf16[256,2048]{1,0:T(8,128)(2,1)S(1)} %multiply_convert_fusion.refs_0_), channel_id=1, source_target_pairs={{0,2},{1,5},{2,0},{3,7},{4,6},{5,1},{6,4},{7,3},{8,10},{9,13},{10,... | collective-permute-start | bytes 3145736 | tf_op jit(solution)/shard_map/ppermute | solution.py:58
  202.0 24.1 %collective-permute-start.21 = (bf16[256,2048]{1,0:T(8,128)(2,1)S(1)}, bf16[256,2048]{1,0:T(8,128)(2,1)S(1)}, u32[]{:S(2)}, u32[]{:S(2)}) collective-permute-start(bf16[256,2048]{1,0:T(8,128)(2,1)S(1)} %multiply_convert_fusion.refs_0_), channel_id=1, source_target_pairs={{0,4},{1,3},{2,6},{3,1},{4,0},{5,7},{6,2},{7,5},{8,12},{9,11},{10,... | collective-permute-start | bytes 3145736 | tf_op jit(solution)/shard_map/ppermute | solution.py:54
  203.5 24.7 %collective-permute-start.24 = (bf16[256,2048]{1,0:T(8,128)(2,1)S(1)}, bf16[256,2048]{1,0:T(8,128)(2,1)S(1)}, u32[]{:S(2)}, u32[]{:S(2)}) collective-permute-start(bf16[256,2048]{1,0:T(8,128)(2,1)S(1)} %multiply_convert_fusion.refs_0_), channel_id=1, source_target_pairs={{0,1},{1,0},{2,3},{3,2},{4,5},{5,4},{6,7},{7,6},{8,9},{9,8},{10,11... | collective-permute-start | bytes 3145736 | tf_op jit(solution)/shard_map/ppermute | solution.py:42
  226.7 14.8 %collective-permute-start.23 = (bf16[256,2048]{1,0:T(8,128)(2,1)S(1)}, bf16[256,2048]{1,0:T(8,128)(2,1)S(1)}, u32[]{:S(2)}, u32[]{:S(2)}) collective-permute-start(bf16[256,2048]{1,0:T(8,128)(2,1)S(1)} %collective-permute-done.21.refs_1_), channel_id=1, source_target_pairs={{0,2},{1,5},{2,0},{3,7},{4,6},{5,1},{6,4},{7,3},{8,10},{9,13},{10,... | collective-permute-start | bytes 3145736 | tf_op jit(solution)/shard_map/ppermute | solution.py:58
  285.3 236.5 %reduce-scatter.6.cloned.1.call-start = ((), (), s32[]{:S(2)}) async-start(), calls=%async_computation.6 | async-start | bytes 7864320 | tf_op jit(solution)/shard_map/reduce_scatter | solution.py:687
  333.2 14.5 %collective-permute-start.28 = (bf16[1024,2048]{1,0:T(8,128)(2,1)}, bf16[1024,2048]{1,0:T(8,128)(2,1)S(1)}, u32[]{:S(2)}, u32[]{:S(2)}) collective-permute-start(bf16[1024,2048]{1,0:T(8,128)(2,1)} %back.17), channel_id=1, source_target_pairs={{0,1},{1,0},{2,3},{3,2},{4,5},{5,4},{6,7},{7,6},{8,9},{9,8},{10,11... | collective-permute-start | bytes 12582920 | tf_op jit(solution)/shard_map/ppermute | solution.py:42
  352.4 26.4 %collective-permute-start.29 = (bf16[512,2048]{1,0:T(8,128)(2,1)}, bf16[512,2048]{1,0:T(8,128)(2,1)}, u32[]{:S(2)}, u32[]{:S(2)}) collective-permute-start(bf16[512,2048]{1,0:T(8,128)(2,1)} %slice_add_fusion.3), channel_id=1, source_target_pairs={{0,2},{1,5},{2,0},{3,7},{4,6},{5,1},{6,4},{7,3},{8,10},{9,13},{10,... | collective-permute-start | bytes 6291464 | tf_op jit(solution)/shard_map/ppermute | solution.py:58
  373.4 286.8 %reduce-scatter.8.cloned.1.call-start = ((), (), s32[]{:S(2)}) async-start(), calls=%async_computation.7 | async-start | bytes 3276800 | tf_op jit(solution)/shard_map/reduce_scatter | solution.py:730
  382.2 14.9 %collective-permute-start.30 = (bf16[256,2048]{1,0:T(8,128)(2,1)S(1)}, bf16[256,2048]{1,0:T(8,128)(2,1)S(1)}, u32[]{:S(2)}, u32[]{:S(2)}) collective-permute-start(bf16[256,2048]{1,0:T(8,128)(2,1)S(1)} %slice.194), channel_id=1, source_target_pairs={{0,4},{1,3},{2,6},{3,1},{4,0},{5,7},{6,2},{7,5},{8,12},{9,11},{10,... | collective-permute-start | bytes 3145736 | tf_op jit(solution)/shard_map/ppermute | solution.py:54
  401.8 25.1 %collective-permute-start.33 = (bf16[256,2048]{1,0:T(8,128)(2,1)S(1)}, bf16[256,2048]{1,0:T(8,128)(2,1)S(1)}, u32[]{:S(2)}, u32[]{:S(2)}) collective-permute-start(bf16[256,2048]{1,0:T(8,128)(2,1)S(1)} %get-tuple-element.97.refs_0_), channel_id=1, source_target_pairs={{0,2},{1,5},{2,0},{3,7},{4,6},{5,1},{6,4},{7,3},{8,10},{9,13},{10,... | collective-permute-start | bytes 3145736 | tf_op jit(solution)/shard_map/ppermute | solution.py:58
  403.3 23.6 %collective-permute-start.32 = (bf16[256,2048]{1,0:T(8,128)(2,1)S(1)}, bf16[256,2048]{1,0:T(8,128)(2,1)S(1)}, u32[]{:S(2)}, u32[]{:S(2)}) collective-permute-start(bf16[256,2048]{1,0:T(8,128)(2,1)S(1)} %get-tuple-element.97.refs_0_), channel_id=1, source_target_pairs={{0,4},{1,3},{2,6},{3,1},{4,0},{5,7},{6,2},{7,5},{8,12},{9,11},{10,... | collective-permute-start | bytes 3145736 | tf_op jit(solution)/shard_map/ppermute | solution.py:54
  427.1 14.8 %collective-permute-start.36 = (bf16[256,2048]{1,0:T(8,128)(2,1)S(1)}, bf16[256,2048]{1,0:T(8,128)(2,1)S(1)}, u32[]{:S(2)}, u32[]{:S(2)}) collective-permute-start(bf16[256,2048]{1,0:T(8,128)(2,1)S(1)} %collective-permute-done.32.refs_1_), channel_id=1, source_target_pairs={{0,2},{1,5},{2,0},{3,7},{4,6},{5,1},{6,4},{7,3},{8,10},{9,13},{10,... | collective-permute-start | bytes 3145736 | tf_op jit(solution)/shard_map/ppermute | solution.py:58
  428.5 14.4 %collective-permute-start.34 = (bf16[256,2048]{1,0:T(8,128)(2,1)S(1)}, bf16[256,2048]{1,0:T(8,128)(2,1)}, u32[]{:S(2)}, u32[]{:S(2)}) collective-permute-start(bf16[256,2048]{1,0:T(8,128)(2,1)S(1)} %collective-permute-done.32.refs_1_), channel_id=1, source_target_pairs={{0,1},{1,0},{2,3},{3,2},{4,5},{5,4},{6,7},{7,6},{8,9},{9,8},{10,11... | collective-permute-start | bytes 3145736 | tf_op jit(solution)/shard_map/ppermute | solution.py:42
  445.9 10.4 %collective-permute-start.38 = (bf16[512,2048]{1,0:T(8,128)(2,1)}, bf16[512,2048]{1,0:T(8,128)(2,1)}, u32[]{:S(2)}, u32[]{:S(2)}) collective-permute-start(bf16[512,2048]{1,0:T(8,128)(2,1)} %back.15), channel_id=1, source_target_pairs={{0,1},{1,0},{2,3},{3,2},{4,5},{5,4},{6,7},{7,6},{8,9},{9,8},{10,11... | collective-permute-start | bytes 6291464 | tf_op jit(solution)/shard_map/ppermute | solution.py:42
  460.9 47.9 %collective-permute-start.40 = (bf16[512,2048]{1,0:T(8,128)(2,1)}, bf16[512,2048]{1,0:T(8,128)(2,1)S(1)}, u32[]{:S(2)}, u32[]{:S(2)}) collective-permute-start(bf16[512,2048]{1,0:T(8,128)(2,1)} %pad_maximum_fusion.5), channel_id=1, source_target_pairs={{0,2},{2,0},{1,3},{3,1},{4,6},{6,4},{5,7},{7,5},{8,10},{10,8},{9,1... | collective-permute-start | bytes 6291464 | tf_op jit(solution)/shard_map/ppermute | solution.py:46
  462.3 59.5 %collective-permute-start.42 = (bf16[512,1536]{1,0:T(8,128)(2,1)}, bf16[512,1536]{1,0:T(8,128)(2,1)}, u32[]{:S(2)}, u32[]{:S(2)}) collective-permute-start(bf16[512,1536]{1,0:T(8,128)(2,1)} %reduce-scatter.4.cloned.1.call-done), channel_id=1, source_target_pairs={{0,4},{4,0},{1,5},{5,1},{2,6},{6,2},{3,7},{7,3},{8,12},{12,8},{9,1... | collective-permute-start | bytes 4718600 | tf_op jit(solution)/shard_map/ppermute | solution.py:50
  526.1 30.4 %collective-permute-start.44 = (bf16[512,2048]{1,0:T(8,128)(2,1)}, bf16[512,2048]{1,0:T(8,128)(2,1)S(1)}, u32[]{:S(2)}, u32[]{:S(2)}) collective-permute-start(bf16[512,2048]{1,0:T(8,128)(2,1)} %back.21), channel_id=1, source_target_pairs={{0,1},{1,0},{2,3},{3,2},{4,5},{5,4},{6,7},{7,6},{8,9},{9,8},{10,11... | collective-permute-start | bytes 6291464 | tf_op jit(solution)/shard_map/ppermute | solution.py:42
  527.2 25.9 %collective-permute-start.41 = (bf16[256,2048]{1,0:T(8,128)(2,1)}, bf16[256,2048]{1,0:T(8,128)(2,1)}, u32[]{:S(2)}, u32[]{:S(2)}) collective-permute-start(bf16[256,2048]{1,0:T(8,128)(2,1)} %slice.252), channel_id=1, source_target_pairs={{0,4},{4,0},{1,5},{5,1},{2,6},{6,2},{3,7},{7,3},{8,12},{12,8},{9,1... | collective-permute-start | bytes 3145736 | tf_op jit(solution)/shard_map/ppermute | solution.py:50
  558.0 26.4 %collective-permute-start.45 = (bf16[512,2048]{1,0:T(8,128)(2,1)}, bf16[512,2048]{1,0:T(8,128)(2,1)}, u32[]{:S(2)}, u32[]{:S(2)}) collective-permute-start(bf16[512,2048]{1,0:T(8,128)(2,1)} %slice_add_fusion), channel_id=1, source_target_pairs={{0,2},{1,5},{2,0},{3,7},{4,6},{5,1},{6,4},{7,3},{8,10},{9,13},{10,... | collective-permute-start | bytes 6291464 | tf_op jit(solution)/shard_map/ppermute | solution.py:58
  559.5 24.9 %collective-permute-start.43 = (bf16[512,2048]{1,0:T(8,128)(2,1)S(1)}, bf16[512,2048]{1,0:T(8,128)(2,1)}, u32[]{:S(2)}, u32[]{:S(2)}) collective-permute-start(bf16[512,2048]{1,0:T(8,128)(2,1)S(1)} %copy-done.43), channel_id=1, source_target_pairs={{0,1},{1,0},{2,3},{3,2},{4,5},{5,4},{6,7},{7,6},{8,9},{9,8},{10,11... | collective-permute-start | bytes 6291464 | tf_op jit(solution)/shard_map/ppermute | solution.py:42
  588.6 15.1 %collective-permute-start.46 = (bf16[256,2048]{1,0:T(8,128)(2,1)}, bf16[256,2048]{1,0:T(8,128)(2,1)}, u32[]{:S(2)}, u32[]{:S(2)}) collective-permute-start(bf16[256,2048]{1,0:T(8,128)(2,1)} %slice.205), channel_id=1, source_target_pairs={{0,4},{1,3},{2,6},{3,1},{4,0},{5,7},{6,2},{7,5},{8,12},{9,11},{10,... | collective-permute-start | bytes 3145736 | tf_op jit(solution)/shard_map/ppermute | solution.py:54
  609.3 45.9 %collective-permute-start.50 = (bf16[256,2048]{1,0:T(8,128)(2,1)}, bf16[256,2048]{1,0:T(8,128)(2,1)}, u32[]{:S(2)}, u32[]{:S(2)}) collective-permute-start(bf16[256,2048]{1,0:T(8,128)(2,1)} %fusion.6), channel_id=1, source_target_pairs={{0,2},{2,0},{1,3},{3,1},{4,6},{6,4},{5,7},{7,5},{8,10},{10,8},{9,1... | collective-permute-start | bytes 3145736 | tf_op jit(solution)/shard_map/ppermute | solution.py:46
  610.8 44.4 %collective-permute-start.47 = (bf16[256,2048]{1,0:T(8,128)(2,1)S(1)}, bf16[256,2048]{1,0:T(8,128)(2,1)}, u32[]{:S(2)}, u32[]{:S(2)}) collective-permute-start(bf16[256,2048]{1,0:T(8,128)(2,1)S(1)} %copy-done.34), channel_id=1, source_target_pairs={{0,2},{2,0},{1,3},{3,1},{4,6},{6,4},{5,7},{7,5},{8,10},{10,8},{9,1... | collective-permute-start | bytes 3145736 | tf_op jit(solution)/shard_map/ppermute | solution.py:46
  611.3 48.9 %collective-permute-start.53 = (bf16[512,1536]{1,0:T(8,128)(2,1)}, bf16[512,1536]{1,0:T(8,128)(2,1)}, u32[]{:S(2)}, u32[]{:S(2)}) collective-permute-start(bf16[512,1536]{1,0:T(8,128)(2,1)} %reduce-scatter.6.cloned.1.call-done), channel_id=1, source_target_pairs={{0,4},{4,0},{1,5},{5,1},{2,6},{6,2},{3,7},{7,3},{8,12},{12,8},{9,1... | collective-permute-start | bytes 4718600 | tf_op jit(solution)/shard_map/ppermute | solution.py:50
  618.6 60.0 %collective-permute-start.48 = (bf16[256,2048]{1,0:T(8,128)(2,1)S(1)}, bf16[256,2048]{1,0:T(8,128)(2,1)}, u32[]{:S(2)}, u32[]{:S(2)}) collective-permute-start(bf16[256,2048]{1,0:T(8,128)(2,1)S(1)} %copy-done.34), channel_id=1, source_target_pairs={{0,1},{1,0},{2,3},{3,2},{4,5},{5,4},{6,7},{7,6},{8,9},{9,8},{10,11... | collective-permute-start | bytes 3145736 | tf_op jit(solution)/shard_map/ppermute | solution.py:42
  618.6 67.6 %collective-permute-start.51 = (bf16[256,2048]{1,0:T(8,128)(2,1)}, bf16[256,2048]{1,0:T(8,128)(2,1)}, u32[]{:S(2)}, u32[]{:S(2)}) collective-permute-start(bf16[256,2048]{1,0:T(8,128)(2,1)} %fusion.6), channel_id=1, source_target_pairs={{0,1},{1,0},{2,3},{3,2},{4,5},{5,4},{6,7},{7,6},{8,9},{9,8},{10,11... | collective-permute-start | bytes 3145736 | tf_op jit(solution)/shard_map/ppermute | solution.py:42
  655.1 23.5 %collective-permute-start.49 = (bf16[256,2048]{1,0:T(8,128)(2,1)}, bf16[256,2048]{1,0:T(8,128)(2,1)}, u32[]{:S(2)}, u32[]{:S(2)}) collective-permute-start(bf16[256,2048]{1,0:T(8,128)(2,1)} %collective-permute-done.47), channel_id=1, source_target_pairs={{0,1},{1,0},{2,3},{3,2},{4,5},{5,4},{6,7},{7,6},{8,9},{9,8},{10,11... | collective-permute-start | bytes 3145736 | tf_op jit(solution)/shard_map/ppermute | solution.py:42
  655.1 31.1 %collective-permute-start.52 = (bf16[256,2048]{1,0:T(8,128)(2,1)}, bf16[256,2048]{1,0:T(8,128)(2,1)}, u32[]{:S(2)}, u32[]{:S(2)}) collective-permute-start(bf16[256,2048]{1,0:T(8,128)(2,1)} %collective-permute-done.50), channel_id=1, source_target_pairs={{0,1},{1,0},{2,3},{3,2},{4,5},{5,4},{6,7},{7,6},{8,9},{9,8},{10,11... | collective-permute-start | bytes 3145736 | tf_op jit(solution)/shard_map/ppermute | solution.py:42
  676.2 17.2 %collective-permute-start.54 = (bf16[512,640]{1,0:T(8,128)(2,1)S(1)}, bf16[512,640]{1,0:T(8,128)(2,1)S(1)}, u32[]{:S(2)}, u32[]{:S(2)}) collective-permute-start(bf16[512,640]{1,0:T(8,128)(2,1)S(1)} %copy-done.49), channel_id=1, source_target_pairs={{0,4},{4,0},{1,5},{5,1},{2,6},{6,2},{3,7},{7,3},{8,12},{12,8},{9,1... | collective-permute-start | bytes 1966088 | tf_op jit(solution)/shard_map/ppermute | solution.py:50
  (81 other events, 809.3 us)
Sparse Core Ops, SparseCore 0:
  66.7 115.1 all-gather.2
  183.4 113.5 all-gather.4
  299.4 108.9 reduce-scatter.3
  410.5 111.2 reduce-scatter.5
  572.2 52.0 reduce-scatter.7

commit v5 on v4

--- a/solution.py
+++ b/solution.py
@@ -14,7 +14,7 @@
 MASKED = -1e30
 LOG2_E = 1.4426950408889634
 BLOCK = 256
-CHUNKS = 2
+SPLIT = (5, 3)
 VMEM = 56 * 2**20
 
 F32 = jnp.float32
@@ -517,7 +517,7 @@
     cycle = [(at, (at + 1) % count) for at in range(count)]
     pieces = [shard]
     for step in range(count - 1):
-        sent = after(pieces[-1], held) if step == 1 else pieces[-1]
+        sent = after(pieces[-1], *held) if step == 1 else pieces[-1]
         pieces.append(lax.ppermute(sent, "fsdp", cycle))
     return pieces
 
@@ -581,35 +581,6 @@
         width = weight.shape[1] // 2
         return lax.dynamic_slice_in_dim(weight, ctx * width, width, 1)
 
-    q_half, k_half, v_half, o_half = map(half, (q_weight, k_weight, v_weight, o_weight))
-    q_width, kv_width = q_half.shape[1], k_half.shape[1]
-    attn_shard = jnp.concatenate([o_half, q_half, k_half, v_half], axis=1)
-    fsdp = lax.axis_size("fsdp")
-    gain_rows = jnp.stack([attn_gain, ffn_gain])
-    gain_width = attn_gain.shape[0]
-    extra = ((0, 14), (0, attn_shard.shape[1] - gain_width))
-    tokens_low = lax.dynamic_slice_in_dim(tokens, tp * own_rows, own_rows, 0)
-    tokens_one = swap_first(tokens_low)
-    attn_ring = ring_over(jnp.concatenate([attn_shard, jnp.pad(gain_rows, extra)]), fsdp, tokens_one)
-    own_depth = attn_shard.shape[0]
-    attn_full = in_place([piece[:own_depth] for piece in attn_ring], 0)
-    gains = in_place([piece[own_depth : own_depth + 2, :gain_width] for piece in attn_ring], 1)
-    gain_one = gains[0].astype(F32)[None]
-    gain_two = gains[1].astype(F32)[None]
-    ff_half = gate_weight.shape[1] // 2
-    chunk = ff_half // CHUNKS
-    ffn_shards = []
-    for part in range(CHUNKS):
-        at = ctx * ff_half + part * chunk
-        ffn_shards.append(
-            jnp.concatenate(
-                [
-                    lax.dynamic_slice_in_dim(weight, at, chunk, 1)
-                    for weight in (gate_weight, up_weight, down_weight)
-                ],
-                axis=1,
-            )
-        )
     length_row, deal_row = lengths[0], deal[0]
     spans = deal_row.shape[0]
     span_rows = group_rows // spans
@@ -653,7 +624,40 @@
     sin = jnp.where((lane % 64 < 32)[None], -jnp.sin(angles), jnp.sin(angles))
     start_column = start_of[:, None]
 
+    q_half, k_half, v_half, o_half = map(half, (q_weight, k_weight, v_weight, o_weight))
+    q_width, kv_width = q_half.shape[1], k_half.shape[1]
+    attn_shard = jnp.concatenate([o_half, q_half, k_half, v_half], axis=1)
+    fsdp = lax.axis_size("fsdp")
+    gain_rows = jnp.stack([attn_gain, ffn_gain])
+    gain_width = attn_gain.shape[0]
+    extra = ((0, 14), (0, attn_shard.shape[1] - gain_width))
+    tokens_low = lax.dynamic_slice_in_dim(tokens, tp * own_rows, own_rows, 0)
     cot_low = lax.dynamic_slice_in_dim(cotangent, tp * own_rows, own_rows, 0)
+    tokens_one = swap_first(tokens_low)
+    attn_ring = ring_over(
+        jnp.concatenate([attn_shard, jnp.pad(gain_rows, extra)]),
+        fsdp,
+        (tokens_one, cos, sin, cot_low, place, first, start_column),
+    )
+    own_depth = attn_shard.shape[0]
+    attn_full = in_place([piece[:own_depth] for piece in attn_ring], 0)
+    gains = in_place([piece[own_depth : own_depth + 2, :gain_width] for piece in attn_ring], 1)
+    gain_one = gains[0].astype(F32)[None]
+    gain_two = gains[1].astype(F32)[None]
+    ff_half = gate_weight.shape[1] // 2
+    chunks = [ff_half * share // sum(SPLIT) for share in SPLIT]
+    ffn_shards = []
+    for part, chunk in enumerate(chunks):
+        at = ctx * ff_half + sum(chunks[:part])
+        ffn_shards.append(
+            jnp.concatenate(
+                [
+                    lax.dynamic_slice_in_dim(weight, at, chunk, 1)
+                    for weight in (gate_weight, up_weight, down_weight)
+                ],
+                axis=1,
+            )
+        )
     tokens_own, cot_own = tokens_low.astype(F32), cot_low.astype(F32)
     group_tokens = (tokens_low, tokens_one, swap_second(tokens_low), swap_second(tokens_one))
     first_shard = after(ffn_shards[0], attn_ring[-1], *group_tokens[2:])
@@ -677,7 +681,7 @@
 
     acts = []
     grad_parts = []
-    for part in range(CHUNKS):
+    for part, chunk in enumerate(chunks):
         normed_two = (after(normed_two[0], *grad_parts), *normed_two[1:])
         acts.append(ffn_chunk(normed_two, cot, ffn_full[part]))
         grad_parts.append(
@@ -686,25 +690,34 @@
     reduced = [
         lax.psum_scatter(part, "fsdp", scatter_dimension=0, tiled=True) for part in grad_parts
     ]
-    d_norm_terms = [(acts[part], 0, ffn_full[part], 0, 2 * chunk) for part in range(CHUNKS)]
-    ffn_terms = [(acts[part], 2, ffn_full[part], 2, chunk) for part in range(CHUNKS)]
+    d_norm_terms = [
+        (acts[part], 0, ffn_full[part], 0, 2 * chunk) for part, chunk in enumerate(chunks)
+    ]
+    ffn_terms = [
+        (acts[part], 2, ffn_full[part], 2, chunk) for part, chunk in enumerate(chunks)
+    ]
     d_normed_two = sum_last(sum_pairs(*sum_cores(d_norm_terms, 1)), *grad_parts)
     d_hidden = cot_own + rms_back(hidden, gain_two, d_normed_two)
     ffn_sent = [back_product(ffn_terms, at, 4) for at in (3, 2)]
     ffn_mine = back_product(ffn_terms, 0, 2)
-    d_attn = share_rows(d_hidden.astype(BF16), [[*ffn_sent, ffn_mine], [reduced[0]]])
-
-    d_heads = front_product(d_attn, attn_full, q_width, 0)
-    arrived = [swap_core(after(piece, *d_attn[4:])) for piece in ffn_sent]
+    d_own = d_hidden.astype(BF16)
+    d_one, d_two, ffn_mine, *ffn_sent = lax.optimization_barrier(
+        (swap_first(d_own), swap_second(d_own), ffn_mine, *ffn_sent)
+    )
+    d_early = [swap_core(part) for part in (d_own, d_one, d_two)]
+    arrived = [swap_core(piece) for piece in ffn_sent]
     half_rows = ffn_mine.shape[0] // 2
     ffn_far, ffn_near = y_first(
         ffn_mine[half_rows:] + arrived[0], ffn_mine[:half_rows] + arrived[1], core
     )
-    d_heads, ffn_far, reduced[0] = lax.optimization_barrier((d_heads, ffn_far, reduced[0]))
+    d_last = after(swap_second(d_one), *d_early, ffn_far, ffn_near, reduced[0])
+    d_attn = (d_own, d_one, d_two, d_last, *d_early, swap_core(d_last))
+
+    d_heads = front_product(d_attn, attn_full, q_width, 0)
     other_reduced = [swap_x(reduced[0])]
     d_qkv = attend_back(qkv, depth, d_heads, heads, place, first, start_column, cos, sin)
     ffn_near = ffn_near + after(swap_y(ffn_far), d_qkv)
-    d_qkv = after(d_qkv, ffn_near, other_reduced[0], *reduced[1:])
+    d_qkv = after(d_qkv, ffn_near, other_reduced[0])
     ffn_sum = ffn_near[:own_rows].astype(F32) + swap_x(ffn_near[own_rows:]).astype(F32)
     result_own = (hidden + ffn_sum).astype(BF16)
     normed_far, normed_near = sum_cores(
@@ -713,13 +726,13 @@
             (d_qkv, q_width // 128, attn_full, 2 * q_width // 128, 128),
         ]
     )
-    normed_far = after(normed_far, result_own)
+    normed_far = after(normed_far, *reduced[1:])
     attn_grad = weight_grads(
         d_attn, heads, q_width, 0, (qkv,), d_qkv, q_width + 128, 0
     )
-    d_normed = sum_last(sum_pairs(normed_far, normed_near), attn_grad)
+    d_normed = sum_last(sum_pairs(normed_far, normed_near), attn_grad, result_own)
     tokens_grad_own = (d_hidden + rms_back(tokens_own, gain_one, d_normed)).astype(BF16)
-    for part in range(1, CHUNKS):
+    for part in range(1, len(chunks)):
         reduced[part] = after(reduced[part], attn_grad, tokens_grad_own)
         other_reduced.append(swap_x(reduced[part]))
     tokens_grad_beside = swap_y(tokens_grad_own)
@@ -740,7 +753,7 @@
                 gain_part(
                     [
                         (ffn_shards[part][:, : 2 * chunk], reduced[part][:, : 2 * chunk])
-                        for part in range(CHUNKS)
+                        for part, chunk in enumerate(chunks)
                     ]
                 ),
             ]
@@ -756,7 +769,7 @@
             [
                 halves[part][side][:, which * chunk : (which + 1) * chunk]
                 for side in range(2)
-                for part in range(CHUNKS)
+                for part, chunk in enumerate(chunks)
             ],
             axis=1,
         )

time: 713 us -> 741 us (1.039)
  waiting for transfers between devices: 274 us -> 233 us
  starting transfers between devices: 46.8 us -> 83.6 us
  Pallas kernels: 251 us -> 265 us
  other arithmetic: 86.3 us -> 97 us
    ppermute x4, waiting for transfers between devices: 46.5 us -> 6.46 us  [swap_y(): return lax.ppermute(v, 'tp', ACROSS)]
    ppermute x28, starting transfers between devices: 6.33 us -> 45.2 us  [swap_core(): return lax.ppermute(v, 'tp', CORE)]
    all_gather x2, waiting for transfers between devices: 11.9 us -> 31.3 us  [shards(): lax.all_gather(shard, 'fsdp', axis=0, tiled=True)]
    ppermute x11, waiting for transfers between devices: 94.1 us -> 76.7 us  [swap_second(): return lax.ppermute(v, ('ctx', 'tp'), SECOND)]
    ppermute x3, waiting for transfers between devices: 39.7 us -> 26.5 us  [ring_over(): pieces.append(lax.ppermute(sent, 'fsdp', cycle))]
    ppermute x5, waiting for transfers between devices: 15 us -> 26.2 us  [swap_x(): return lax.ppermute(v, 'ctx', PAIR)]
  transfers between devices with their start and end apart: 63 -> 63, of which waited for: 30 -> 25; matrix products, arithmetic and copies ran while one was open for 15% -> 16% of each run, Pallas kernels for 35% -> 36%
where the time goes in v5:
time: 741 us; the launch traced here: 731 us
  Pallas kernels  265 us (36%)
  waiting for transfers between devices  233 us (31%)
  other arithmetic  97 us (13%)
  starting transfers between devices  83.6 us (11%)
  local copies, waits for them, and re-layouts  37.5 us (5%)
  between operations  15.1 us (2%)
    pallas_call x11, Pallas kernels, back_product(): pl.pallas_call(back_kernel, out_shape=jax.ShapeDtypeStruct((rows, depth),...  78.1 us
    ppermute x11, waiting for transfers between devices, swap_second(): return lax.ppermute(v, ('ctx', 'tp'), SECOND)  76.7 us
    pallas_call x3, Pallas kernels, weight_grads(): pl.pallas_call(functools.partial(grads_kernel, len(x), len(y)), out_shape...  53.6 us
    pallas_call x2, Pallas kernels, ffn_chunk(): pl.pallas_call(functools.partial(ffn_kernel, len(x)), out_shape=jax.Shape...  50.8 us
    ppermute x7, waiting for transfers between devices, swap_first(): return lax.ppermute(v, ('ctx', 'tp'), FIRST)  46 us
    ppermute x28, starting transfers between devices, swap_core(): return lax.ppermute(v, 'tp', CORE)  45.2 us
    pallas_call x1, Pallas kernels, attend_back(): pl.pallas_call(attend_back_kernel, out_shape=jax.ShapeDtypeStruct((rows,...  35.1 us
    all_gather x2, waiting for transfers between devices, shards(): lax.all_gather(shard, 'fsdp', axis=0, tiled=True)  31.3 us
  transfers between devices with their start and end apart: 63, of which 25 were waited for; matrix products, arithmetic and copies ran while one was open for 16% of the time, Pallas kernels for 36%

profile of v5, /device:TPU:0, one launch (start us, length us, event | category | flops | bytes accessed | tf_op | source)
XLA Modules:
  0.0 731.2 jit_solution(626381492907246342)
XLA Ops:
  24.4 5.6 negate_select_fusion
  30.0 3.3 collective-permute-done
  36.8 15.0 %collective-permute-done.2 = bf16[528,640]{1,0:T(8,128)(2,1)} collective-permute-done((bf16[528,640]{1,0:T(8,128)(2,1)}, bf16[528,640]{1,0:T(8,128)(2,1)}, u32[]{:S(2)}, u32[]{:S(2)}) %collective-permute-start.2) | collective-permute-done | bytes 675872 | tf_op jit(solution)/shard_map/ppermute | solution.py:521
  55.8 5.3 collective-permute-done.5.refs_3_
  61.1 8.2 %collective-permute-done.3 = bf16[528,640]{1,0:T(8,128)(2,1)} collective-permute-done((bf16[528,640]{1,0:T(8,128)(2,1)}, bf16[528,640]{1,0:T(8,128)(2,1)}, u32[]{:S(2)}, u32[]{:S(2)}) %collective-permute-start.3) | collective-permute-done | bytes 675872 | tf_op jit(solution)/shard_map/ppermute | solution.py:521
  81.1 15.3 %qkv.1.q_ref.kv_ref.refs_8_ = bf16[2048,2432]{1,0:T(8,128)(2,1)} custom-call(bf16[256,2048]{1,0:T(8,128)(2,1)} %constant_dynamic-slice_fusion.11.refs_0_, bf16[256,2048]{1,0:T(8,128)(2,1)} %collective-permute-done.1.refs_1_, bf16[256,2048]{1,0:T(8,128)(2,1)} %collective-permute-done.4.refs_2_, bf16[256,2048]{1,0:T(8,128)(2,1)} %collective-permute-done.5.refs_3_, ...), custom_call_target="tpu_custom_call" | custom-call | flops 1 | bytes 1 | tf_op jit(solution)/shard_map/qkv/pallas_call | solution.py:141
  96.4 7.7 %collective-permute-done.11.refs_10_ = bf16[256,2048]{1,0:T(8,128)(2,1)} collective-permute-done((bf16[256,2048]{1,0:T(8,128)(2,1)S(1)}, bf16[256,2048]{1,0:T(8,128)(2,1)}, u32[]{:S(2)}, u32[]{:S(2)}) %collective-permute-start.11) | collective-permute-done | bytes 1048608 | tf_op jit(solution)/shard_map/ppermute | solution.py:58
  107.2 22.7 %attend.1.refs_0_.h_ref.refs_9_ = f32[2048,384]{1,0:T(8,128)} custom-call(s32[8]{0:T(128)} %select_reduce_fusion.2.place, s32[8]{0:T(128)} %and_select_fusion.2.first, bf16[2048,2432]{1,0:T(8,128)(2,1)} %qkv.1.q_ref.kv_ref.refs_8_, bf16[2048,2432]{1,0:T(8,128)(2,1)} %qkv.1.q_ref.kv_ref.refs_8_, s32[2048,1]{1,0:T(8,128)} %copy.28.start_ref), custom_call_target="tpu_custom_call" | custom-call | flops 1 | bytes 1 | tf_op jit(solution)/shard_map/attend/pallas_call | solution.py:358
  133.0 3.5 back.13
  136.6 3.5 back.12
  140.1 4.2 back.11
  151.7 22.1 %collective-permute-done.19 = bf16[512,2048]{1,0:T(8,128)(2,1)} collective-permute-done((bf16[512,2048]{1,0:T(8,128)(2,1)}, bf16[512,2048]{1,0:T(8,128)(2,1)}, u32[]{:S(2)}, u32[]{:S(2)}) %collective-permute-start.19) | collective-permute-done | bytes 2097184 | tf_op jit(solution)/shard_map/ppermute | solution.py:58
  177.0 31.3 %all-gather.3.cloned.1.call-done.refs_16_.refs_2_ = bf16[2048,1920]{1,0:T(8,128)(2,1)} async-done(((bf16[512,1920]{1,0:T(8,128)(2,1)}), bf16[2048,1920]{1,0:T(8,128)(2,1)}) %all-gather.3.cloned.1.call-update) | async-done | bytes 7864336 | tf_op jit(solution)/shard_map/all_gather | solution.py:672
  209.9 13.3 %collective-permute-done.20 = bf16[256,2048]{1,0:T(8,128)(2,1)S(1)} collective-permute-done((bf16[256,2048]{1,0:T(8,128)(2,1)S(1)}, bf16[256,2048]{1,0:T(8,128)(2,1)S(1)}, u32[]{:S(2)}, u32[]{:S(2)}) %collective-permute-start.20) | collective-permute-done | bytes 1048608 | tf_op jit(solution)/shard_map/ppermute | solution.py:54
  229.9 22.6 %collective-permute-done.22.refs_2_ = bf16[256,2048]{1,0:T(8,128)(2,1)S(1)} collective-permute-done((bf16[256,2048]{1,0:T(8,128)(2,1)S(1)}, bf16[256,2048]{1,0:T(8,128)(2,1)S(1)}, u32[]{:S(2)}, u32[]{:S(2)}) %collective-permute-start.22) | collective-permute-done | bytes 1048608 | tf_op jit(solution)/shard_map/ppermute | solution.py:58
  256.7 11.1 %collective-permute-done.23.refs_3_ = bf16[256,2048]{1,0:T(8,128)(2,1)S(1)} collective-permute-done((bf16[256,2048]{1,0:T(8,128)(2,1)S(1)}, bf16[256,2048]{1,0:T(8,128)(2,1)S(1)}, u32[]{:S(2)}, u32[]{:S(2)}) %collective-permute-start.23) | collective-permute-done | bytes 1048608 | tf_op jit(solution)/shard_map/ppermute | solution.py:58
  270.7 29.2 %ffn.2.refs_16_.refs_17_.refs_0_ = bf16[2048,1920]{1,0:T(8,128)(2,1)} custom-call(bf16[256,2048]{1,0:T(8,128)(2,1)} %copy-done.4, bf16[256,2048]{1,0:T(8,128)(2,1)} %copy-done.8, bf16[256,2048]{1,0:T(8,128)(2,1)} %copy-done.7, bf16[256,2048]{1,0:T(8,128)(2,1)} %copy-done.12, bf16[256,2048]{1,0:T(8,128)(2,1)} %copy-done.9, bf16[256,2048]{1,0:T(8,128)(2,1)} %copy-done.11, ...), custom_call_target="tpu_custom_call" | custom-call | flops 1 | bytes 1 | tf_op jit(solution)/shard_map/ffn/pallas_call | solution.py:180
  299.9 24.2 %weight_grads.3 = bf16[2048,1920]{1,0:T(8,128)(2,1)} custom-call(bf16[256,2048]{1,0:T(8,128)(2,1)} %copy-done.4, bf16[256,2048]{1,0:T(8,128)(2,1)} %copy-done.8, bf16[256,2048]{1,0:T(8,128)(2,1)} %copy-done.7, bf16[256,2048]{1,0:T(8,128)(2,1)} %copy-done.12, bf16[256,2048]{1,0:T(8,128)(2,1)} %copy-done.9, bf16[256,2048]{1,0:T(8,128)(2,1)} %copy-done.11, ...), custom_call_target="tpu_custom_call" | custom-call | flops 1 | bytes 1 | tf_op jit(solution)/shard_map/weight_grads/pallas_call | solution.py:216
  324.5 21.6 %ffn.3.refs_1_.refs_16_.refs_17_ = bf16[2048,1152]{1,0:T(8,128)(2,1)} custom-call(bf16[256,2048]{1,0:T(8,128)(2,1)} %copy-done.4, bf16[256,2048]{1,0:T(8,128)(2,1)} %copy-done.8, bf16[256,2048]{1,0:T(8,128)(2,1)} %copy-done.7, bf16[256,2048]{1,0:T(8,128)(2,1)} %copy-done.12, bf16[256,2048]{1,0:T(8,128)(2,1)} %copy-done.9, bf16[256,2048]{1,0:T(8,128)(2,1)} %copy-done.11, ...), custom_call_target="tpu_custom_call" | custom-call | flops 1 | bytes 1 | tf_op jit(solution)/shard_map/ffn/pallas_call | solution.py:180
  346.0 14.5 %back.15 = bf16[1024,2048]{1,0:T(8,128)(2,1)} custom-call(bf16[2048,1920]{1,0:T(8,128)(2,1)} %ffn.2.refs_16_.refs_17_.refs_0_, bf16[2048,1152]{1,0:T(8,128)(2,1)} %ffn.3.refs_1_.refs_16_.refs_17_, bf16[2048,1920]{1,0:T(8,128)(2,1)} %all-gather.3.cloned.1.call-done.refs_16_.refs_2_, bf16[2048,1152]{1,0:T(8,128)(2,1)} %all-gather.5.cloned.1.call-done.refs_16_.refs_3_), custom_call_target="tpu_custom_call" | custom-call | flops 1 | bytes 1 | tf_op jit(solution)/shard_map/back/pallas_call | solution.py:252
  360.7 14.6 %back.14 = bf16[1024,2048]{1,0:T(8,128)(2,1)} custom-call(bf16[2048,1920]{1,0:T(8,128)(2,1)} %ffn.2.refs_16_.refs_17_.refs_0_, bf16[2048,1152]{1,0:T(8,128)(2,1)} %ffn.3.refs_1_.refs_16_.refs_17_, bf16[2048,1920]{1,0:T(8,128)(2,1)} %all-gather.3.cloned.1.call-done.refs_16_.refs_2_, bf16[2048,1152]{1,0:T(8,128)(2,1)} %all-gather.5.cloned.1.call-done.refs_16_.refs_3_), custom_call_target="tpu_custom_call" | custom-call | flops 1 | bytes 1 | tf_op jit(solution)/shard_map/back/pallas_call | solution.py:252
  375.3 4.6 slice_add_fusion.2
  381.4 16.9 %weight_grads.4 = bf16[2048,1152]{1,0:T(8,128)(2,1)} custom-call(bf16[256,2048]{1,0:T(8,128)(2,1)} %copy-done.4, bf16[256,2048]{1,0:T(8,128)(2,1)} %copy-done.8, bf16[256,2048]{1,0:T(8,128)(2,1)} %copy-done.7, bf16[256,2048]{1,0:T(8,128)(2,1)} %copy-done.12, bf16[256,2048]{1,0:T(8,128)(2,1)} %copy-done.9, bf16[256,2048]{1,0:T(8,128)(2,1)} %copy-done.11, ...), custom_call_target="tpu_custom_call" | custom-call | flops 1 | bytes 1 | tf_op jit(solution)/shard_map/weight_grads/pallas_call | solution.py:216
  398.3 8.0 %collective-permute-done.29 = bf16[512,2048]{1,0:T(8,128)(2,1)} collective-permute-done((bf16[512,2048]{1,0:T(8,128)(2,1)}, bf16[512,2048]{1,0:T(8,128)(2,1)}, u32[]{:S(2)}, u32[]{:S(2)}) %collective-permute-start.29) | collective-permute-done | bytes 2097184 | tf_op jit(solution)/shard_map/ppermute | solution.py:58
  406.3 3.3 fusion.9
  410.0 14.6 %collective-permute-done.30 = bf16[256,2048]{1,0:T(8,128)(2,1)S(1)} collective-permute-done((bf16[256,2048]{1,0:T(8,128)(2,1)S(1)}, bf16[256,2048]{1,0:T(8,128)(2,1)S(1)}, u32[]{:S(2)}, u32[]{:S(2)}) %collective-permute-start.30) | collective-permute-done | bytes 1048608 | tf_op jit(solution)/shard_map/ppermute | solution.py:54
  425.6 4.2 fusion.26
  431.4 6.8 back.18
  438.2 6.8 back.17
  445.0 10.0 %back.16 = bf16[1024,2048]{1,0:T(8,128)(2,1)} custom-call(bf16[2048,1920]{1,0:T(8,128)(2,1)} %ffn.2.refs_16_.refs_17_.refs_0_, bf16[2048,1152]{1,0:T(8,128)(2,1)} %ffn.3.refs_1_.refs_16_.refs_17_, bf16[2048,1920]{1,0:T(8,128)(2,1)} %all-gather.3.cloned.1.call-done.refs_16_.refs_2_, bf16[2048,1152]{1,0:T(8,128)(2,1)} %all-gather.5.cloned.1.call-done.refs_16_.refs_3_), custom_call_target="tpu_custom_call" | custom-call | flops 1 | bytes 1 | tf_op jit(solution)/shard_map/back/pallas_call | solution.py:252
  462.6 3.9 slice_add_fusion.7
  475.9 9.6 %front.1.d_ref = bf16[2048,256]{1,0:T(8,128)(2,1)} custom-call(bf16[256,2048]{1,0:T(8,128)(2,1)} %get-tuple-element.93.refs_0_, bf16[256,2048]{1,0:T(8,128)(2,1)} %collective-permute-done.31.refs_1_, bf16[256,2048]{1,0:T(8,128)(2,1)} %collective-permute-done.32.refs_2_, bf16[256,2048]{1,0:T(8,128)(2,1)} %collective-permute-done.36.refs_3_, ...), custom_call_target="tpu_custom_call" | custom-call | flops 1 | bytes 1 | tf_op jit(solution)/shard_map/front/pallas_call | solution.py:277
  485.6 35.1 %attend_back.1.refs_0_.refs_1_.refs_10_ = bf16[2048,384]{1,0:T(8,128)(2,1)} custom-call(s32[8]{0:T(128)} %select_reduce_fusion.2.place, s32[8]{0:T(128)} %and_select_fusion.2.first, bf16[2048,2432]{1,0:T(8,128)(2,1)} %qkv.1.q_ref.kv_ref.refs_8_, bf16[2048,256]{1,0:T(8,128)(2,1)} %front.1.d_ref, f32[2048,384]{1,0:T(8,128)} %attend.1.refs_0_.h_ref.refs_9_, ...), custom_call_target="tpu_custom_call" | custom-call | flops 1 | bytes 1 | tf_op jit(solution)/shard_map/attend_back/pallas_call | solution.py:455
  520.7 3.9 fusion.25
  524.5 4.8 back.21
  529.5 4.1 back.20
  533.6 5.4 back.19
  538.9 3.2 slice_add_fusion
  542.1 3.6 reduce-scatter.6.cloned.1.call-done
  551.0 12.5 %weight_grads.5 = bf16[2048,640]{1,0:T(8,128)(2,1)} custom-call(bf16[256,2048]{1,0:T(8,128)(2,1)} %get-tuple-element.93.refs_0_, bf16[256,2048]{1,0:T(8,128)(2,1)} %collective-permute-done.31.refs_1_, bf16[256,2048]{1,0:T(8,128)(2,1)} %collective-permute-done.32.refs_2_, bf16[256,2048]{1,0:T(8,128)(2,1)} %collective-permute-done.36.refs_3_, ...), custom_call_target="tpu_custom_call" | custom-call | flops 1 | bytes 1 | tf_op jit(solution)/shard_map/weight_grads/pallas_call | solution.py:216
  563.5 12.4 %collective-permute-done.41 = bf16[256,2048]{1,0:T(8,128)(2,1)} collective-permute-done((bf16[256,2048]{1,0:T(8,128)(2,1)}, bf16[256,2048]{1,0:T(8,128)(2,1)}, u32[]{:S(2)}, u32[]{:S(2)}) %collective-permute-start.41) | collective-permute-done | bytes 1048608 | tf_op jit(solution)/shard_map/ppermute | solution.py:50
  575.9 3.8 add_convert_fusion
  586.6 18.0 %collective-permute-done.46 = bf16[256,2048]{1,0:T(8,128)(2,1)} collective-permute-done((bf16[256,2048]{1,0:T(8,128)(2,1)}, bf16[256,2048]{1,0:T(8,128)(2,1)}, u32[]{:S(2)}, u32[]{:S(2)}) %collective-permute-start.46) | collective-permute-done | bytes 1048608 | tf_op jit(solution)/shard_map/ppermute | solution.py:54
  606.8 3.5 fusion.6
  618.2 24.2 %collective-permute-start.48 = (bf16[256,2048]{1,0:T(8,128)(2,1)}, bf16[256,2048]{1,0:T(8,128)(2,1)}, u32[]{:S(2)}, u32[]{:S(2)}) collective-permute-start(bf16[256,2048]{1,0:T(8,128)(2,1)} %add_convert_fusion), channel_id=1, source_target_pairs={{0,1},{1,0},{2,3},{3,2},{4,5},{5,4},{6,7},{7,6},{8,9},{9,8},{10,11... | collective-permute-start | bytes 3145736 | tf_op jit(solution)/shard_map/ppermute | solution.py:42
  643.8 6.5 collective-permute-done.47
  650.3 15.9 %collective-permute-start.49 = (bf16[256,2048]{1,0:T(8,128)(2,1)}, bf16[256,2048]{1,0:T(8,128)(2,1)}, u32[]{:S(2)}, u32[]{:S(2)}) collective-permute-start(bf16[256,2048]{1,0:T(8,128)(2,1)} %collective-permute-done.47), channel_id=1, source_target_pairs={{0,1},{1,0},{2,3},{3,2},{4,5},{5,4},{6,7},{7,6},{8,9},{9,8},{10,11... | collective-permute-start | bytes 3145736 | tf_op jit(solution)/shard_map/ppermute | solution.py:42
  690.6 13.9 %collective-permute-done.54 = bf16[512,640]{1,0:T(8,128)(2,1)S(1)} collective-permute-done((bf16[512,640]{1,0:T(8,128)(2,1)S(1)}, bf16[512,640]{1,0:T(8,128)(2,1)S(1)}, u32[]{:S(2)}, u32[]{:S(2)}) %collective-permute-start.54) | collective-permute-done | bytes 655392 | tf_op jit(solution)/shard_map/ppermute | solution.py:50
  (317 shorter events, 158.1 us)
Async XLA Ops:
  7.2 201.1 %all-gather.3.cloned.1.call-start = ((), (), s32[]{:S(2)}) async-start(), calls=%async_computation.3 | async-start | bytes 9830400 | tf_op jit(solution)/shard_map/all_gather | solution.py:672
  12.7 20.5 %collective-permute-start = (bf16[528,640]{1,0:T(8,128)(2,1)}, bf16[528,640]{1,0:T(8,128)(2,1)}, u32[]{:S(2)}, u32[]{:S(2)}) collective-permute-start(bf16[528,640]{1,0:T(8,128)(2,1)} %fusion.12), channel_id=1, source_target_pairs={{0,8},{8,16},{16,24},{24,0},{1,9},{9,17},{17,25},{25,1},{2,10},{10... | collective-permute-start | bytes 2027528 | tf_op jit(solution)/shard_map/ppermute | solution.py:521
  18.1 15.2 %collective-permute-start.1 = (bf16[256,2048]{1,0:T(8,128)(2,1)}, bf16[256,2048]{1,0:T(8,128)(2,1)}, u32[]{:S(2)}, u32[]{:S(2)}) collective-permute-start(bf16[256,2048]{1,0:T(8,128)(2,1)} %constant_dynamic-slice_fusion.11.refs_0_), channel_id=1, source_target_pairs={{0,4},{1,3},{2,6},{3,1},{4,0},{5,7},{6,2},{7,5},{8,12},{9,11},{10,... | collective-permute-start | bytes 3145736 | tf_op jit(solution)/shard_map/ppermute | solution.py:54
  33.3 18.5 %collective-permute-start.2 = (bf16[528,640]{1,0:T(8,128)(2,1)}, bf16[528,640]{1,0:T(8,128)(2,1)}, u32[]{:S(2)}, u32[]{:S(2)}) collective-permute-start(bf16[528,640]{1,0:T(8,128)(2,1)} %collective-permute-done), channel_id=1, source_target_pairs={{0,8},{8,16},{16,24},{24,0},{1,9},{9,17},{17,25},{25,1},{2,10},{10... | collective-permute-start | bytes 2027528 | tf_op jit(solution)/shard_map/ppermute | solution.py:521
  34.8 21.1 %collective-permute-start.4 = (bf16[256,2048]{1,0:T(8,128)(2,1)}, bf16[256,2048]{1,0:T(8,128)(2,1)}, u32[]{:S(2)}, u32[]{:S(2)}) collective-permute-start(bf16[256,2048]{1,0:T(8,128)(2,1)} %constant_dynamic-slice_fusion.11.refs_0_), channel_id=1, source_target_pairs={{0,2},{1,5},{2,0},{3,7},{4,6},{5,1},{6,4},{7,3},{8,10},{9,13},{10,... | collective-permute-start | bytes 3145736 | tf_op jit(solution)/shard_map/ppermute | solution.py:58
  36.3 24.8 %collective-permute-start.5 = (bf16[256,2048]{1,0:T(8,128)(2,1)}, bf16[256,2048]{1,0:T(8,128)(2,1)}, u32[]{:S(2)}, u32[]{:S(2)}) collective-permute-start(bf16[256,2048]{1,0:T(8,128)(2,1)} %collective-permute-done.1.refs_1_), channel_id=1, source_target_pairs={{0,2},{1,5},{2,0},{3,7},{4,6},{5,1},{6,4},{7,3},{8,10},{9,13},{10,... | collective-permute-start | bytes 3145736 | tf_op jit(solution)/shard_map/ppermute | solution.py:58
  51.7 17.6 %collective-permute-start.3 = (bf16[528,640]{1,0:T(8,128)(2,1)}, bf16[528,640]{1,0:T(8,128)(2,1)}, u32[]{:S(2)}, u32[]{:S(2)}) collective-permute-start(bf16[528,640]{1,0:T(8,128)(2,1)} %collective-permute-done.2), channel_id=1, source_target_pairs={{0,8},{8,16},{16,24},{24,0},{1,9},{9,17},{17,25},{25,1},{2,10},{10... | collective-permute-start | bytes 2027528 | tf_op jit(solution)/shard_map/ppermute | solution.py:521
  69.3 255.1 %all-gather.5.cloned.1.call-start = ((), (), s32[]{:S(2)}) async-start(), calls=%async_computation.4 | async-start | bytes 5898240 | tf_op jit(solution)/shard_map/all_gather | solution.py:672
  78.5 25.6 %collective-permute-start.11 = (bf16[256,2048]{1,0:T(8,128)(2,1)S(1)}, bf16[256,2048]{1,0:T(8,128)(2,1)}, u32[]{:S(2)}, u32[]{:S(2)}) collective-permute-start(bf16[256,2048]{1,0:T(8,128)(2,1)S(1)} %constant_dynamic-slice_fusion.6.refs_8_), channel_id=1, source_target_pairs={{0,2},{1,5},{2,0},{3,7},{4,6},{5,1},{6,4},{7,3},{8,10},{9,13},{10,... | collective-permute-start | bytes 3145736 | tf_op jit(solution)/shard_map/ppermute | solution.py:58
  79.9 24.2 %collective-permute-start.10 = (bf16[256,2048]{1,0:T(8,128)(2,1)S(1)}, bf16[256,2048]{1,0:T(8,128)(2,1)}, u32[]{:S(2)}, u32[]{:S(2)}) collective-permute-start(bf16[256,2048]{1,0:T(8,128)(2,1)S(1)} %constant_dynamic-slice_fusion.6.refs_8_), channel_id=1, source_target_pairs={{0,4},{1,3},{2,6},{3,1},{4,0},{5,7},{6,2},{7,5},{8,12},{9,11},{10,... | collective-permute-start | bytes 3145736 | tf_op jit(solution)/shard_map/ppermute | solution.py:54
  81.1 48.8 %collective-permute-start.13 = (bf16[256,2048]{1,0:T(8,128)(2,1)S(1)}, bf16[256,2048]{1,0:T(8,128)(2,1)}, u32[]{:S(2)}, u32[]{:S(2)}) collective-permute-start(bf16[256,2048]{1,0:T(8,128)(2,1)S(1)} %constant_dynamic-slice_fusion.6.refs_8_), channel_id=1, source_target_pairs={{0,1},{1,0},{2,3},{3,2},{4,5},{5,4},{6,7},{7,6},{8,9},{9,8},{10,11... | collective-permute-start | bytes 3145736 | tf_op jit(solution)/shard_map/ppermute | solution.py:42
  104.1 25.8 %collective-permute-start.15 = (bf16[256,2048]{1,0:T(8,128)(2,1)}, bf16[256,2048]{1,0:T(8,128)(2,1)}, u32[]{:S(2)}, u32[]{:S(2)}) collective-permute-start(bf16[256,2048]{1,0:T(8,128)(2,1)} %collective-permute-done.11.refs_10_), channel_id=1, source_target_pairs={{0,1},{1,0},{2,3},{3,2},{4,5},{5,4},{6,7},{7,6},{8,9},{9,8},{10,11... | collective-permute-start | bytes 3145736 | tf_op jit(solution)/shard_map/ppermute | solution.py:42
  104.8 25.1 %collective-permute-start.14 = (bf16[256,2048]{1,0:T(8,128)(2,1)}, bf16[256,2048]{1,0:T(8,128)(2,1)}, u32[]{:S(2)}, u32[]{:S(2)}) collective-permute-start(bf16[256,2048]{1,0:T(8,128)(2,1)} %collective-permute-done.10.refs_9_), channel_id=1, source_target_pairs={{0,1},{1,0},{2,3},{3,2},{4,5},{5,4},{6,7},{7,6},{8,9},{9,8},{10,11... | collective-permute-start | bytes 3145736 | tf_op jit(solution)/shard_map/ppermute | solution.py:42
  104.8 25.1 %collective-permute-start.12 = (bf16[256,2048]{1,0:T(8,128)(2,1)}, bf16[256,2048]{1,0:T(8,128)(2,1)}, u32[]{:S(2)}, u32[]{:S(2)}) collective-permute-start(bf16[256,2048]{1,0:T(8,128)(2,1)} %collective-permute-done.10.refs_9_), channel_id=1, source_target_pairs={{0,2},{1,5},{2,0},{3,7},{4,6},{5,1},{6,4},{7,3},{8,10},{9,13},{10,... | collective-permute-start | bytes 3145736 | tf_op jit(solution)/shard_map/ppermute | solution.py:58
  147.4 26.4 %collective-permute-start.19 = (bf16[512,2048]{1,0:T(8,128)(2,1)}, bf16[512,2048]{1,0:T(8,128)(2,1)}, u32[]{:S(2)}, u32[]{:S(2)}) collective-permute-start(bf16[512,2048]{1,0:T(8,128)(2,1)} %slice_add_fusion.4), channel_id=1, source_target_pairs={{0,2},{1,5},{2,0},{3,7},{4,6},{5,1},{6,4},{7,3},{8,10},{9,13},{10,... | collective-permute-start | bytes 6291464 | tf_op jit(solution)/shard_map/ppermute | solution.py:58
  149.0 24.8 %collective-permute-start.17 = (bf16[512,2048]{1,0:T(8,128)(2,1)}, bf16[512,2048]{1,0:T(8,128)(2,1)}, u32[]{:S(2)}, u32[]{:S(2)}) collective-permute-start(bf16[512,2048]{1,0:T(8,128)(2,1)} %back.12), channel_id=1, source_target_pairs={{0,1},{1,0},{2,3},{3,2},{4,5},{5,4},{6,7},{7,6},{8,9},{9,8},{10,11... | collective-permute-start | bytes 6291464 | tf_op jit(solution)/shard_map/ppermute | solution.py:42
  151.5 318.6 %reduce-scatter.4.cloned.1.call-start = ((), (), s32[]{:S(2)}) async-start(), calls=%async_computation.5 | async-start | bytes 9830400 | tf_op jit(solution)/shard_map/reduce_scatter | solution.py:691
  208.3 14.9 %collective-permute-start.20 = (bf16[256,2048]{1,0:T(8,128)(2,1)S(1)}, bf16[256,2048]{1,0:T(8,128)(2,1)S(1)}, u32[]{:S(2)}, u32[]{:S(2)}) collective-permute-start(bf16[256,2048]{1,0:T(8,128)(2,1)S(1)} %slice.186), channel_id=1, source_target_pairs={{0,4},{1,3},{2,6},{3,1},{4,0},{5,7},{6,2},{7,5},{8,12},{9,11},{10,... | collective-permute-start | bytes 3145736 | tf_op jit(solution)/shard_map/ppermute | solution.py:54
  226.9 25.6 %collective-permute-start.22 = (bf16[256,2048]{1,0:T(8,128)(2,1)S(1)}, bf16[256,2048]{1,0:T(8,128)(2,1)S(1)}, u32[]{:S(2)}, u32[]{:S(2)}) collective-permute-start(bf16[256,2048]{1,0:T(8,128)(2,1)S(1)} %multiply_convert_fusion.refs_0_), channel_id=1, source_target_pairs={{0,2},{1,5},{2,0},{3,7},{4,6},{5,1},{6,4},{7,3},{8,10},{9,13},{10,... | collective-permute-start | bytes 3145736 | tf_op jit(solution)/shard_map/ppermute | solution.py:58
  228.4 24.1 %collective-permute-start.21 = (bf16[256,2048]{1,0:T(8,128)(2,1)S(1)}, bf16[256,2048]{1,0:T(8,128)(2,1)S(1)}, u32[]{:S(2)}, u32[]{:S(2)}) collective-permute-start(bf16[256,2048]{1,0:T(8,128)(2,1)S(1)} %multiply_convert_fusion.refs_0_), channel_id=1, source_target_pairs={{0,4},{1,3},{2,6},{3,1},{4,0},{5,7},{6,2},{7,5},{8,12},{9,11},{10,... | collective-permute-start | bytes 3145736 | tf_op jit(solution)/shard_map/ppermute | solution.py:54
  229.9 24.7 %collective-permute-start.24 = (bf16[256,2048]{1,0:T(8,128)(2,1)S(1)}, bf16[256,2048]{1,0:T(8,128)(2,1)S(1)}, u32[]{:S(2)}, u32[]{:S(2)}) collective-permute-start(bf16[256,2048]{1,0:T(8,128)(2,1)S(1)} %multiply_convert_fusion.refs_0_), channel_id=1, source_target_pairs={{0,1},{1,0},{2,3},{3,2},{4,5},{5,4},{6,7},{7,6},{8,9},{9,8},{10,11... | collective-permute-start | bytes 3145736 | tf_op jit(solution)/shard_map/ppermute | solution.py:42
  253.1 14.8 %collective-permute-start.23 = (bf16[256,2048]{1,0:T(8,128)(2,1)S(1)}, bf16[256,2048]{1,0:T(8,128)(2,1)S(1)}, u32[]{:S(2)}, u32[]{:S(2)}) collective-permute-start(bf16[256,2048]{1,0:T(8,128)(2,1)S(1)} %collective-permute-done.21.refs_1_), channel_id=1, source_target_pairs={{0,2},{1,5},{2,0},{3,7},{4,6},{5,1},{6,4},{7,3},{8,10},{9,13},{10,... | collective-permute-start | bytes 3145736 | tf_op jit(solution)/shard_map/ppermute | solution.py:58
  324.1 221.6 %reduce-scatter.6.cloned.1.call-start = ((), (), s32[]{:S(2)}) async-start(), calls=%async_computation.6 | async-start | bytes 5898240 | tf_op jit(solution)/shard_map/reduce_scatter | solution.py:691
  360.5 14.8 %collective-permute-start.28 = (bf16[1024,2048]{1,0:T(8,128)(2,1)}, bf16[1024,2048]{1,0:T(8,128)(2,1)S(1)}, u32[]{:S(2)}, u32[]{:S(2)}) collective-permute-start(bf16[1024,2048]{1,0:T(8,128)(2,1)} %back.15), channel_id=1, source_target_pairs={{0,1},{1,0},{2,3},{3,2},{4,5},{5,4},{6,7},{7,6},{8,9},{9,8},{10,11... | collective-permute-start | bytes 12582920 | tf_op jit(solution)/shard_map/ppermute | solution.py:42
  379.9 26.4 %collective-permute-start.29 = (bf16[512,2048]{1,0:T(8,128)(2,1)}, bf16[512,2048]{1,0:T(8,128)(2,1)}, u32[]{:S(2)}, u32[]{:S(2)}) collective-permute-start(bf16[512,2048]{1,0:T(8,128)(2,1)} %slice_add_fusion.2), channel_id=1, source_target_pairs={{0,2},{1,5},{2,0},{3,7},{4,6},{5,1},{6,4},{7,3},{8,10},{9,13},{10,... | collective-permute-start | bytes 6291464 | tf_op jit(solution)/shard_map/ppermute | solution.py:58
  409.7 14.9 %collective-permute-start.30 = (bf16[256,2048]{1,0:T(8,128)(2,1)S(1)}, bf16[256,2048]{1,0:T(8,128)(2,1)S(1)}, u32[]{:S(2)}, u32[]{:S(2)}) collective-permute-start(bf16[256,2048]{1,0:T(8,128)(2,1)S(1)} %slice.193), channel_id=1, source_target_pairs={{0,4},{1,3},{2,6},{3,1},{4,0},{5,7},{6,2},{7,5},{8,12},{9,11},{10,... | collective-permute-start | bytes 3145736 | tf_op jit(solution)/shard_map/ppermute | solution.py:54
  429.8 25.2 %collective-permute-start.32 = (bf16[256,2048]{1,0:T(8,128)(2,1)}, bf16[256,2048]{1,0:T(8,128)(2,1)}, u32[]{:S(2)}, u32[]{:S(2)}) collective-permute-start(bf16[256,2048]{1,0:T(8,128)(2,1)} %get-tuple-element.93.refs_0_), channel_id=1, source_target_pairs={{0,2},{1,5},{2,0},{3,7},{4,6},{5,1},{6,4},{7,3},{8,10},{9,13},{10,... | collective-permute-start | bytes 3145736 | tf_op jit(solution)/shard_map/ppermute | solution.py:58
  431.2 23.8 %collective-permute-start.31 = (bf16[256,2048]{1,0:T(8,128)(2,1)}, bf16[256,2048]{1,0:T(8,128)(2,1)}, u32[]{:S(2)}, u32[]{:S(2)}) collective-permute-start(bf16[256,2048]{1,0:T(8,128)(2,1)} %get-tuple-element.93.refs_0_), channel_id=1, source_target_pairs={{0,4},{1,3},{2,6},{3,1},{4,0},{5,7},{6,2},{7,5},{8,12},{9,11},{10,... | collective-permute-start | bytes 3145736 | tf_op jit(solution)/shard_map/ppermute | solution.py:54
  431.4 239.6 %reduce-scatter.8.cloned.1.call-start = ((), (), s32[]{:S(2)}) async-start(), calls=%async_computation.7 | async-start | bytes 3276800 | tf_op jit(solution)/shard_map/reduce_scatter | solution.py:743
  455.6 14.5 %collective-permute-start.37 = (bf16[256,2048]{1,0:T(8,128)(2,1)}, bf16[256,2048]{1,0:T(8,128)(2,1)}, u32[]{:S(2)}, u32[]{:S(2)}) collective-permute-start(bf16[256,2048]{1,0:T(8,128)(2,1)} %get-tuple-element.93.refs_0_), channel_id=1, source_target_pairs={{0,1},{1,0},{2,3},{3,2},{4,5},{5,4},{6,7},{7,6},{8,9},{9,8},{10,11... | collective-permute-start | bytes 3145736 | tf_op jit(solution)/shard_map/ppermute | solution.py:42
  455.7 16.3 %collective-permute-start.38 = (bf16[256,2048]{1,0:T(8,128)(2,1)}, bf16[256,2048]{1,0:T(8,128)(2,1)}, u32[]{:S(2)}, u32[]{:S(2)}) collective-permute-start(bf16[256,2048]{1,0:T(8,128)(2,1)} %collective-permute-done.31.refs_1_), channel_id=1, source_target_pairs={{0,1},{1,0},{2,3},{3,2},{4,5},{5,4},{6,7},{7,6},{8,9},{9,8},{10,11... | collective-permute-start | bytes 3145736 | tf_op jit(solution)/shard_map/ppermute | solution.py:42
  456.1 15.9 %collective-permute-start.36 = (bf16[256,2048]{1,0:T(8,128)(2,1)}, bf16[256,2048]{1,0:T(8,128)(2,1)}, u32[]{:S(2)}, u32[]{:S(2)}) collective-permute-start(bf16[256,2048]{1,0:T(8,128)(2,1)} %collective-permute-done.31.refs_1_), channel_id=1, source_target_pairs={{0,2},{1,5},{2,0},{3,7},{4,6},{5,1},{6,4},{7,3},{8,10},{9,13},{10,... | collective-permute-start | bytes 3145736 | tf_op jit(solution)/shard_map/ppermute | solution.py:58
  459.6 12.4 %collective-permute-start.39 = (bf16[256,2048]{1,0:T(8,128)(2,1)}, bf16[256,2048]{1,0:T(8,128)(2,1)}, u32[]{:S(2)}, u32[]{:S(2)}) collective-permute-start(bf16[256,2048]{1,0:T(8,128)(2,1)} %collective-permute-done.32.refs_2_), channel_id=1, source_target_pairs={{0,1},{1,0},{2,3},{3,2},{4,5},{5,4},{6,7},{7,6},{8,9},{9,8},{10,11... | collective-permute-start | bytes 3145736 | tf_op jit(solution)/shard_map/ppermute | solution.py:42
  469.6 51.0 %collective-permute-start.35 = (bf16[512,2048]{1,0:T(8,128)(2,1)}, bf16[512,2048]{1,0:T(8,128)(2,1)}, u32[]{:S(2)}, u32[]{:S(2)}) collective-permute-start(bf16[512,2048]{1,0:T(8,128)(2,1)} %pad_maximum_fusion.6), channel_id=1, source_target_pairs={{0,2},{2,0},{1,3},{3,1},{4,6},{6,4},{5,7},{7,5},{8,10},{10,8},{9,1... | collective-permute-start | bytes 6291464 | tf_op jit(solution)/shard_map/ppermute | solution.py:46
  470.1 54.4 %collective-permute-start.42 = (bf16[512,1920]{1,0:T(8,128)(2,1)}, bf16[512,1920]{1,0:T(8,128)(2,1)S(1)}, u32[]{:S(2)}, u32[]{:S(2)}) collective-permute-start(bf16[512,1920]{1,0:T(8,128)(2,1)} %reduce-scatter.4.cloned.1.call-done), channel_id=1, source_target_pairs={{0,4},{4,0},{1,5},{5,1},{2,6},{6,2},{3,7},{7,3},{8,12},{12,8},{9,1... | collective-permute-start | bytes 5898248 | tf_op jit(solution)/shard_map/ppermute | solution.py:50
  529.3 9.6 %collective-permute-start.44 = (bf16[512,2048]{1,0:T(8,128)(2,1)}, bf16[512,2048]{1,0:T(8,128)(2,1)S(1)}, u32[]{:S(2)}, u32[]{:S(2)}) collective-permute-start(bf16[512,2048]{1,0:T(8,128)(2,1)} %back.21), channel_id=1, source_target_pairs={{0,1},{1,0},{2,3},{3,2},{4,5},{5,4},{6,7},{7,6},{8,9},{9,8},{10,11... | collective-permute-start | bytes 6291464 | tf_op jit(solution)/shard_map/ppermute | solution.py:42
  545.7 34.0 %collective-permute-start.45 = (bf16[512,2048]{1,0:T(8,128)(2,1)}, bf16[512,2048]{1,0:T(8,128)(2,1)}, u32[]{:S(2)}, u32[]{:S(2)}) collective-permute-start(bf16[512,2048]{1,0:T(8,128)(2,1)} %slice_add_fusion), channel_id=1, source_target_pairs={{0,2},{1,5},{2,0},{3,7},{4,6},{5,1},{6,4},{7,3},{8,10},{9,13},{10,... | collective-permute-start | bytes 6291464 | tf_op jit(solution)/shard_map/ppermute | solution.py:58
  547.2 32.5 %collective-permute-start.43 = (bf16[512,2048]{1,0:T(8,128)(2,1)}, bf16[512,2048]{1,0:T(8,128)(2,1)}, u32[]{:S(2)}, u32[]{:S(2)}) collective-permute-start(bf16[512,2048]{1,0:T(8,128)(2,1)} %back.20), channel_id=1, source_target_pairs={{0,1},{1,0},{2,3},{3,2},{4,5},{5,4},{6,7},{7,6},{8,9},{9,8},{10,11... | collective-permute-start | bytes 6291464 | tf_op jit(solution)/shard_map/ppermute | solution.py:42
  549.5 26.4 %collective-permute-start.41 = (bf16[256,2048]{1,0:T(8,128)(2,1)}, bf16[256,2048]{1,0:T(8,128)(2,1)}, u32[]{:S(2)}, u32[]{:S(2)}) collective-permute-start(bf16[256,2048]{1,0:T(8,128)(2,1)} %slice.250), channel_id=1, source_target_pairs={{0,4},{4,0},{1,5},{5,1},{2,6},{6,2},{3,7},{7,3},{8,12},{12,8},{9,1... | collective-permute-start | bytes 3145736 | tf_op jit(solution)/shard_map/ppermute | solution.py:50
  583.4 21.3 %collective-permute-start.46 = (bf16[256,2048]{1,0:T(8,128)(2,1)}, bf16[256,2048]{1,0:T(8,128)(2,1)}, u32[]{:S(2)}, u32[]{:S(2)}) collective-permute-start(bf16[256,2048]{1,0:T(8,128)(2,1)} %slice.205), channel_id=1, source_target_pairs={{0,4},{1,3},{2,6},{3,1},{4,0},{5,7},{6,2},{7,5},{8,12},{9,11},{10,... | collective-permute-start | bytes 3145736 | tf_op jit(solution)/shard_map/ppermute | solution.py:54
  610.3 55.8 %collective-permute-start.50 = (bf16[256,2048]{1,0:T(8,128)(2,1)}, bf16[256,2048]{1,0:T(8,128)(2,1)}, u32[]{:S(2)}, u32[]{:S(2)}) collective-permute-start(bf16[256,2048]{1,0:T(8,128)(2,1)} %fusion.6), channel_id=1, source_target_pairs={{0,2},{2,0},{1,3},{3,1},{4,6},{6,4},{5,7},{7,5},{8,10},{10,8},{9,1... | collective-permute-start | bytes 3145736 | tf_op jit(solution)/shard_map/ppermute | solution.py:46
  611.8 38.4 %collective-permute-start.47 = (bf16[256,2048]{1,0:T(8,128)(2,1)}, bf16[256,2048]{1,0:T(8,128)(2,1)}, u32[]{:S(2)}, u32[]{:S(2)}) collective-permute-start(bf16[256,2048]{1,0:T(8,128)(2,1)} %add_convert_fusion), channel_id=1, source_target_pairs={{0,2},{2,0},{1,3},{3,1},{4,6},{6,4},{5,7},{7,5},{8,10},{10,8},{9,1... | collective-permute-start | bytes 3145736 | tf_op jit(solution)/shard_map/ppermute | solution.py:46
  612.9 58.1 %collective-permute-start.53 = (bf16[512,1152]{1,0:T(8,128)(2,1)}, bf16[512,1152]{1,0:T(8,128)(2,1)}, u32[]{:S(2)}, u32[]{:S(2)}) collective-permute-start(bf16[512,1152]{1,0:T(8,128)(2,1)} %reduce-scatter.6.cloned.1.call-done), channel_id=1, source_target_pairs={{0,4},{4,0},{1,5},{5,1},{2,6},{6,2},{3,7},{7,3},{8,12},{12,8},{9,1... | collective-permute-start | bytes 3538952 | tf_op jit(solution)/shard_map/ppermute | solution.py:50
  618.2 90.9 %collective-permute-start.48 = (bf16[256,2048]{1,0:T(8,128)(2,1)}, bf16[256,2048]{1,0:T(8,128)(2,1)}, u32[]{:S(2)}, u32[]{:S(2)}) collective-permute-start(bf16[256,2048]{1,0:T(8,128)(2,1)} %add_convert_fusion), channel_id=1, source_target_pairs={{0,1},{1,0},{2,3},{3,2},{4,5},{5,4},{6,7},{7,6},{8,9},{9,8},{10,11... | collective-permute-start | bytes 3145736 | tf_op jit(solution)/shard_map/ppermute | solution.py:42
  642.4 74.4 %collective-permute-start.51 = (bf16[256,2048]{1,0:T(8,128)(2,1)}, bf16[256,2048]{1,0:T(8,128)(2,1)}, u32[]{:S(2)}, u32[]{:S(2)}) collective-permute-start(bf16[256,2048]{1,0:T(8,128)(2,1)} %fusion.6), channel_id=1, source_target_pairs={{0,1},{1,0},{2,3},{3,2},{4,5},{5,4},{6,7},{7,6},{8,9},{9,8},{10,11... | collective-permute-start | bytes 3145736 | tf_op jit(solution)/shard_map/ppermute | solution.py:42
  650.3 58.8 %collective-permute-start.49 = (bf16[256,2048]{1,0:T(8,128)(2,1)}, bf16[256,2048]{1,0:T(8,128)(2,1)}, u32[]{:S(2)}, u32[]{:S(2)}) collective-permute-start(bf16[256,2048]{1,0:T(8,128)(2,1)} %collective-permute-done.47), channel_id=1, source_target_pairs={{0,1},{1,0},{2,3},{3,2},{4,5},{5,4},{6,7},{7,6},{8,9},{9,8},{10,11... | collective-permute-start | bytes 3145736 | tf_op jit(solution)/shard_map/ppermute | solution.py:42
  666.2 50.6 %collective-permute-start.52 = (bf16[256,2048]{1,0:T(8,128)(2,1)}, bf16[256,2048]{1,0:T(8,128)(2,1)}, u32[]{:S(2)}, u32[]{:S(2)}) collective-permute-start(bf16[256,2048]{1,0:T(8,128)(2,1)} %collective-permute-done.50), channel_id=1, source_target_pairs={{0,1},{1,0},{2,3},{3,2},{4,5},{5,4},{6,7},{7,6},{8,9},{9,8},{10,11... | collective-permute-start | bytes 3145736 | tf_op jit(solution)/shard_map/ppermute | solution.py:42
  688.4 16.1 %collective-permute-start.54 = (bf16[512,640]{1,0:T(8,128)(2,1)S(1)}, bf16[512,640]{1,0:T(8,128)(2,1)S(1)}, u32[]{:S(2)}, u32[]{:S(2)}) collective-permute-start(bf16[512,640]{1,0:T(8,128)(2,1)S(1)} %copy-done.42), channel_id=1, source_target_pairs={{0,4},{4,0},{1,5},{5,1},{2,6},{6,2},{3,7},{7,3},{8,12},{12,8},{9,1... | collective-permute-start | bytes 1966088 | tf_op jit(solution)/shard_map/ppermute | solution.py:50
  (69 other events, 767.1 us)
Sparse Core Ops, SparseCore 0:
  69.4 138.7 all-gather.2
  209.8 87.6 all-gather.4
  324.2 133.4 reduce-scatter.3
  459.9 85.7 reduce-scatter.5
  563.7 51.3 reduce-scatter.7

commit v6 on v5

--- a/solution.py
+++ b/solution.py
@@ -14,7 +14,7 @@
 MASKED = -1e30
 LOG2_E = 1.4426950408889634
 BLOCK = 256
-SPLIT = (5, 3)
+SPLIT = (1, 1)
 VMEM = 56 * 2**20
 
 F32 = jnp.float32
@@ -476,33 +476,42 @@
     )(place, first, qkv, d_heads, heads, qkv, start, cos, sin)
 
 
-def sum_cores(terms, pieces=2, *held):
+def sum_cores(terms, pieces=2):
     sent = [back_product(terms, 2 * pieces - 1 - at, 2 * pieces) for at in range(pieces)]
-    arrived = [swap_core(after(piece, *held)) for piece in sent]
+    arrived = [swap_core(piece) for piece in sent]
+    return add_blocks(back_product(terms, 0, 2), arrived)
+
+
+def add_blocks(mine, arrived):
+    rows = mine.shape[0] // 4
+    each = 4 // len(arrived)
+    blocks = []
+    for at in range(4):
+        other = arrived[len(arrived) - 1 - at // each]
+        begin = (at % each) * rows
+        blocks.append(mine[at * rows : (at + 1) * rows] + other[begin : begin + rows])
+    return blocks
+
+
+def sum_first(blocks, early=()):
+    own, along_a, along_b, both = blocks
+    along_a = along_a + after(swap_second(both), *early)
+    return (own, *lax.optimization_barrier((along_a, along_b)))
+
+
+def sum_last(own, along_a, along_b, beside=()):
+    from_a = after(swap_first(along_a), *beside)
+    return own.astype(F32) + swap_second(along_b).astype(F32) + from_a.astype(F32)
+
+
+def sum_wide(terms, between, beside):
+    arrived = swap_core(back_product(terms, 1, 2))
     mine = back_product(terms, 0, 2)
-    rows = mine.shape[0] // 2
-    if pieces == 1:
-        return mine[rows:] + arrived[0][rows:], mine[:rows] + arrived[0][:rows]
-    return mine[rows:] + arrived[0], mine[:rows] + arrived[1]
-
-
-def y_first(far, near, core):
-    rows = near.shape[0] // 2
-    first, second = near[rows:], far[:rows]
-    return (
-        jnp.concatenate([jnp.where(core == 0, second, first), far[rows:]]),
-        jnp.concatenate([near[:rows], jnp.where(core == 0, first, second)]),
-    )
-
-
-def sum_pairs(far, near, *behind):
-    return near + after(swap_second(far), *behind)
-
-
-def sum_last(near, *beside):
-    rows = near.shape[0] // 2
-    near = after(near, *beside)
-    return near[:rows].astype(F32) + swap_first(near[rows:]).astype(F32)
+    rows = mine.shape[0] // 4
+    far, near = mine[2 * rows :] + arrived[2 * rows :], mine[: 2 * rows] + arrived[: 2 * rows]
+    near = after(near + swap_second(far), *between)
+    from_a = after(swap_first(near[rows:]), *beside)
+    return near[:rows].astype(F32) + from_a.astype(F32)
 
 
 def share_rows(own, beside=()):
@@ -673,75 +682,80 @@
         for shard in (first_shard, after(ffn_shards[1], heads))
     ]
     heads = after(heads, *cot)
-    attn_sum = sum_last(
-        sum_pairs(*sum_cores([(heads, 0, attn_full, 0, q_width)])), ffn_full[0]
-    )
+    attn_blocks = sum_cores([(heads, 0, attn_full, 0, q_width)])
+    attn_sum = sum_last(*sum_first(attn_blocks), beside=ffn_full[:1])
     hidden = tokens_own + attn_sum
     normed_two = share_rows((hidden * inv_rms(hidden) * gain_two).astype(BF16))
 
     acts = []
     grad_parts = []
-    for part, chunk in enumerate(chunks):
+
+    def chunk_grads(part, held=()):
+        chunk = chunks[part]
+        act = after(acts[part], *held)
+        grad_parts.append(weight_grads(normed_two, act, 2 * chunk, 0, cot, act, chunk, 2))
+
+    last = len(chunks) - 1
+    for part in range(len(chunks)):
         normed_two = (after(normed_two[0], *grad_parts), *normed_two[1:])
         acts.append(ffn_chunk(normed_two, cot, ffn_full[part]))
-        grad_parts.append(
-            weight_grads(normed_two, acts[part], 2 * chunk, 0, cot, acts[part], chunk, 2)
-        )
+        if part < last:
+            chunk_grads(part)
+    d_norm_terms = [
+        (acts[part], 0, ffn_full[part], 0, 2 * chunk) for part, chunk in enumerate(chunks)
+    ]
+    ffn_terms = [(acts[part], 2, ffn_full[part], 2, chunk) for part, chunk in enumerate(chunks)]
+    ffn_sent = [back_product(ffn_terms, at, 4) for at in (3, 2)]
+    ffn_mine = back_product(ffn_terms, 0, 2)
+    chunk_grads(last)
     reduced = [
         lax.psum_scatter(part, "fsdp", scatter_dimension=0, tiled=True) for part in grad_parts
     ]
-    d_norm_terms = [
-        (acts[part], 0, ffn_full[part], 0, 2 * chunk) for part, chunk in enumerate(chunks)
-    ]
-    ffn_terms = [
-        (acts[part], 2, ffn_full[part], 2, chunk) for part, chunk in enumerate(chunks)
-    ]
-    d_normed_two = sum_last(sum_pairs(*sum_cores(d_norm_terms, 1)), *grad_parts)
+    d_normed_two = sum_wide(d_norm_terms, grad_parts, ffn_sent[:1])
     d_hidden = cot_own + rms_back(hidden, gain_two, d_normed_two)
-    ffn_sent = [back_product(ffn_terms, at, 4) for at in (3, 2)]
-    ffn_mine = back_product(ffn_terms, 0, 2)
     d_own = d_hidden.astype(BF16)
-    d_one, d_two, ffn_mine, *ffn_sent = lax.optimization_barrier(
-        (swap_first(d_own), swap_second(d_own), ffn_mine, *ffn_sent)
+    ffn_own, ffn_a, ffn_b, ffn_both = add_blocks(ffn_mine, [swap_core(piece) for piece in ffn_sent])
+    ffn_x, ffn_y = jnp.where(core == 0, ffn_a, ffn_b), jnp.where(core == 0, ffn_b, ffn_a)
+    d_one, d_two, ffn_own, ffn_x, ffn_y, ffn_both = lax.optimization_barrier(
+        (swap_first(d_own), swap_second(d_own), ffn_own, ffn_x, ffn_y, ffn_both)
     )
     d_early = [swap_core(part) for part in (d_own, d_one, d_two)]
-    arrived = [swap_core(piece) for piece in ffn_sent]
-    half_rows = ffn_mine.shape[0] // 2
-    ffn_far, ffn_near = y_first(
-        ffn_mine[half_rows:] + arrived[0], ffn_mine[:half_rows] + arrived[1], core
-    )
-    d_last = after(swap_second(d_one), *d_early, ffn_far, ffn_near, reduced[0])
+    d_last = after(swap_second(d_one), *d_early, reduced[0])
     d_attn = (d_own, d_one, d_two, d_last, *d_early, swap_core(d_last))
 
     d_heads = front_product(d_attn, attn_full, q_width, 0)
-    other_reduced = [swap_x(reduced[0])]
+    other_reduced = [swap_x(after(reduced[0], d_last))]
     d_qkv = attend_back(qkv, depth, d_heads, heads, place, first, start_column, cos, sin)
-    ffn_near = ffn_near + after(swap_y(ffn_far), d_qkv)
-    d_qkv = after(d_qkv, ffn_near, other_reduced[0])
-    ffn_sum = ffn_near[:own_rows].astype(F32) + swap_x(ffn_near[own_rows:]).astype(F32)
-    result_own = (hidden + ffn_sum).astype(BF16)
-    normed_far, normed_near = sum_cores(
+    y_both, y_own, d_qkv, other_reduced[0] = lax.optimization_barrier(
+        (swap_y(ffn_both), swap_y(ffn_y), d_qkv, other_reduced[0])
+    )
+    ffn_x, ffn_own, d_qkv = lax.optimization_barrier((ffn_x + y_both, ffn_own + y_own, d_qkv))
+    result_own = (hidden + (ffn_own.astype(F32) + swap_x(ffn_x).astype(F32))).astype(BF16)
+    result_beside = swap_y(result_own)
+    normed_blocks = sum_cores(
         [
             (d_qkv, 0, attn_full, 1, q_width),
             (d_qkv, q_width // 128, attn_full, 2 * q_width // 128, 128),
         ]
     )
-    normed_far = after(normed_far, *reduced[1:])
     attn_grad = weight_grads(
-        d_attn, heads, q_width, 0, (qkv,), d_qkv, q_width + 128, 0
-    )
-    d_normed = sum_last(sum_pairs(normed_far, normed_near), attn_grad, result_own)
+        d_attn, heads, q_width, 0, (qkv,), after(d_qkv, result_own), q_width + 128, 0
+    )
+    d_normed = sum_last(*sum_first(normed_blocks, [attn_grad]), beside=reduced[1:])
     tokens_grad_own = (d_hidden + rms_back(tokens_own, gain_one, d_normed)).astype(BF16)
     for part in range(1, len(chunks)):
-        reduced[part] = after(reduced[part], attn_grad, tokens_grad_own)
+        reduced[part] = after(reduced[part], tokens_grad_own)
         other_reduced.append(swap_x(reduced[part]))
-    tokens_grad_beside = swap_y(tokens_grad_own)
+    attn_reduced = lax.psum_scatter(attn_grad, "fsdp", scatter_dimension=0, tiled=True)
+    attn_reduced = after(attn_reduced, tokens_grad_own)
+    tokens_grad_beside = after(swap_y(tokens_grad_own), attn_reduced)
     tokens_grad = share_in_ctx(tokens_grad_own, tokens_grad_beside, y, core)
-    result_own = after(result_own, tokens_grad_own)
-    result = share_in_ctx(result_own, swap_y(result_own), y, core)
-
-    attn_reduced = lax.psum_scatter(attn_grad, "fsdp", scatter_dimension=0, tiled=True)
-    attn_reduced = after(attn_reduced, tokens_grad_beside, *other_reduced)
+    result_own, result_beside, _ = lax.optimization_barrier(
+        (result_own, result_beside, tokens_grad_own)
+    )
+    result = share_in_ctx(result_own, result_beside, y, core)
+
+    attn_late = after(attn_reduced, tokens_grad_beside)
 
     def gain_part(pairs):
         return sum(jnp.sum(mine.astype(F32) * grad.astype(F32), axis=1) for mine, grad in pairs)
@@ -749,7 +763,7 @@
     gain_sums = sum_all(
         jnp.stack(
             [
-                gain_part([(attn_shard[:, q_width:], attn_reduced[:, q_width:])]),
+                gain_part([(attn_shard[:, q_width:], attn_late[:, q_width:])]),
                 gain_part(
                     [
                         (ffn_shards[part][:, : 2 * chunk], reduced[part][:, : 2 * chunk])
@@ -774,7 +788,9 @@
             axis=1,
         )
 
-    attn_low, attn_high = both_halves(attn_reduced, swap_x(attn_reduced), ctx)
+    attn_low, attn_high = both_halves(
+        attn_reduced, swap_x(after(attn_reduced, *other_reduced[1:])), ctx
+    )
 
     def attn_out(begin, end):
         return jnp.concatenate([attn_low[:, begin:end], attn_high[:, begin:end]], axis=1)

time: 741 us -> 694 us (0.937)
  starting transfers between devices: 83.6 us -> 44.7 us
  waiting for transfers between devices: 233 us -> 249 us
  other arithmetic: 97 us -> 84.2 us
  Pallas kernels: 265 us -> 253 us
    ppermute x28, starting transfers between devices: 45.2 us -> 5.8 us  [swap_core(): return lax.ppermute(v, 'tp', CORE)]
    ppermute x5, waiting for transfers between devices: 26.2 us -> 56.9 us  [swap_x(): return lax.ppermute(v, 'ctx', PAIR)]
    all_gather x2, waiting for transfers between devices: 31.3 us -> 18.6 us  [shards(): lax.all_gather(shard, 'fsdp', axis=0, tiled=True)]
    add x8, other arithmetic: 27.8 us -> 18.6 us  [the longest x2 5.27 us: sum_first(): along_a = along_a + after(swap_second(both), *early)]
    ppermute x28, waiting for transfers between devices: 15.8 us -> 8.14 us  [swap_core(): return lax.ppermute(v, 'tp', CORE)]
    ppermute x11 -> x13, waiting for transfers between devices: 76.7 us -> 81.9 us  [swap_second(): return lax.ppermute(v, ('ctx', 'tp'), SECOND)]
    ppermute x11 -> x13, starting transfers between devices: 13.5 us -> 15.9 us  [swap_second(): return lax.ppermute(v, ('ctx', 'tp'), SECOND)]
  transfers between devices with their start and end apart: 63 -> 66, of which waited for: 25 -> 27; matrix products, arithmetic and copies ran while one was open for 16% -> 15% of each run, Pallas kernels for 36% -> 37%
where the time goes in v6:
time: 694 us; the launch traced here: 687 us
  Pallas kernels  253 us (36%)
  waiting for transfers between devices  249 us (36%)
  other arithmetic  84.2 us (12%)
  starting transfers between devices  44.7 us (6%)
  local copies, waits for them, and re-layouts  40.6 us (6%)
  between operations  15.1 us (2%)
    ppermute x13, waiting for transfers between devices, swap_second(): return lax.ppermute(v, ('ctx', 'tp'), SECOND)  81.9 us
    pallas_call x11, Pallas kernels, back_product(): pl.pallas_call(back_kernel, out_shape=jax.ShapeDtypeStruct((rows, depth),...  75.5 us
    ppermute x5, waiting for transfers between devices, swap_x(): return lax.ppermute(v, 'ctx', PAIR)  56.9 us
    pallas_call x3, Pallas kernels, weight_grads(): pl.pallas_call(functools.partial(grads_kernel, len(x), len(y)), out_shape...  51.2 us
    pallas_call x2, Pallas kernels, ffn_chunk(): pl.pallas_call(functools.partial(ffn_kernel, len(x)), out_shape=jax.Shape...  43.5 us
    ppermute x7, waiting for transfers between devices, swap_first(): return lax.ppermute(v, ('ctx', 'tp'), FIRST)  41.6 us
    pallas_call x1, Pallas kernels, attend_back(): pl.pallas_call(attend_back_kernel, out_shape=jax.ShapeDtypeStruct((rows,...  35.1 us
    ppermute x3, waiting for transfers between devices, ring_over(): pieces.append(lax.ppermute(sent, 'fsdp', cycle))  30.8 us
  transfers between devices with their start and end apart: 66, of which 27 were waited for; matrix products, arithmetic and copies ran while one was open for 15% of the time, Pallas kernels for 37%

profile of v6, /device:TPU:0, one launch (start us, length us, event | category | flops | bytes accessed | tf_op | source)
XLA Modules:
  0.0 686.9 jit_solution(18230250991411535844)
XLA Ops:
  21.9 5.6 negate_select_fusion
  27.5 4.9 collective-permute-done
  34.7 16.2 %collective-permute-done.2 = bf16[528,640]{1,0:T(8,128)(2,1)} collective-permute-done((bf16[528,640]{1,0:T(8,128)(2,1)}, bf16[528,640]{1,0:T(8,128)(2,1)}, u32[]{:S(2)}, u32[]{:S(2)}) %collective-permute-start.2) | collective-permute-done | bytes 675872 | tf_op jit(solution)/shard_map/ppermute | solution.py:530
  58.8 9.6 %collective-permute-done.3 = bf16[528,640]{1,0:T(8,128)(2,1)} collective-permute-done((bf16[528,640]{1,0:T(8,128)(2,1)}, bf16[528,640]{1,0:T(8,128)(2,1)}, u32[]{:S(2)}, u32[]{:S(2)}) %collective-permute-start.3) | collective-permute-done | bytes 675872 | tf_op jit(solution)/shard_map/ppermute | solution.py:530
  79.5 15.3 %qkv.1.q_ref.kv_ref.refs_8_ = bf16[2048,2432]{1,0:T(8,128)(2,1)} custom-call(bf16[256,2048]{1,0:T(8,128)(2,1)} %copy-done.32, bf16[256,2048]{1,0:T(8,128)(2,1)} %copy-done.48, bf16[256,2048]{1,0:T(8,128)(2,1)} %collective-permute-done.4.refs_2_, bf16[256,2048]{1,0:T(8,128)(2,1)} %collective-permute-done.5.refs_3_, ...), custom_call_target="tpu_custom_call" | custom-call | flops 1 | bytes 1 | tf_op jit(solution)/shard_map/qkv/pallas_call | solution.py:141
  94.9 7.8 %collective-permute-done.11.refs_10_ = bf16[256,2048]{1,0:T(8,128)(2,1)S(1)} collective-permute-done((bf16[256,2048]{1,0:T(8,128)(2,1)}, bf16[256,2048]{1,0:T(8,128)(2,1)S(1)}, u32[]{:S(2)}, u32[]{:S(2)}) %collective-permute-start.11) | collective-permute-done | bytes 1048608 | tf_op jit(solution)/shard_map/ppermute | solution.py:58
  105.9 22.7 %attend.1.refs_0_.h_ref.refs_9_ = f32[2048,384]{1,0:T(8,128)} custom-call(s32[8]{0:T(128)} %select_reduce_fusion.2.place, s32[8]{0:T(128)} %and_select_fusion.2.first, bf16[2048,2432]{1,0:T(8,128)(2,1)} %qkv.1.q_ref.kv_ref.refs_8_, bf16[2048,2432]{1,0:T(8,128)(2,1)} %qkv.1.q_ref.kv_ref.refs_8_, s32[2048,1]{1,0:T(8,128)} %copy.28.start_ref), custom_call_target="tpu_custom_call" | custom-call | flops 1 | bytes 1 | tf_op jit(solution)/shard_map/attend/pallas_call | solution.py:358
  131.6 3.8 back.13
  137.2 3.5 back.12
  141.0 4.2 back.11
  148.3 13.5 %collective-permute-done.19 = bf16[256,2048]{1,0:T(8,128)(2,1)S(1)} collective-permute-done((bf16[256,2048]{1,0:T(8,128)(2,1)S(1)}, bf16[256,2048]{1,0:T(8,128)(2,1)S(1)}, u32[]{:S(2)}, u32[]{:S(2)}) %collective-permute-start.19) | collective-permute-done | bytes 1048608 | tf_op jit(solution)/shard_map/ppermute | solution.py:58
  166.0 23.8 %collective-permute-done.21 = bf16[256,2048]{1,0:T(8,128)(2,1)S(1)} collective-permute-done((bf16[256,2048]{1,0:T(8,128)(2,1)S(1)}, bf16[256,2048]{1,0:T(8,128)(2,1)S(1)}, u32[]{:S(2)}, u32[]{:S(2)}) %collective-permute-start.21) | collective-permute-done | bytes 1048608 | tf_op jit(solution)/shard_map/ppermute | solution.py:54
  189.8 3.3 multiply_reduce_fusion.3
  195.6 22.9 %collective-permute-done.23.refs_2_ = bf16[256,2048]{1,0:T(8,128)(2,1)S(1)} collective-permute-done((bf16[256,2048]{1,0:T(8,128)(2,1)S(1)}, bf16[256,2048]{1,0:T(8,128)(2,1)S(1)}, u32[]{:S(2)}, u32[]{:S(2)}) %collective-permute-start.23) | collective-permute-done | bytes 1048608 | tf_op jit(solution)/shard_map/ppermute | solution.py:58
  222.8 11.1 %collective-permute-done.24.refs_3_ = bf16[256,2048]{1,0:T(8,128)(2,1)S(1)} collective-permute-done((bf16[256,2048]{1,0:T(8,128)(2,1)S(1)}, bf16[256,2048]{1,0:T(8,128)(2,1)S(1)}, u32[]{:S(2)}, u32[]{:S(2)}) %collective-permute-start.24) | collective-permute-done | bytes 1048608 | tf_op jit(solution)/shard_map/ppermute | solution.py:58
  236.7 21.8 %ffn.2.refs_16_.refs_17_.refs_0_ = bf16[2048,1536]{1,0:T(8,128)(2,1)} custom-call(bf16[256,2048]{1,0:T(8,128)(2,1)} %copy-done.1, bf16[256,2048]{1,0:T(8,128)(2,1)} %copy-done.7, bf16[256,2048]{1,0:T(8,128)(2,1)} %copy-done.6, bf16[256,2048]{1,0:T(8,128)(2,1)} %copy-done.11, bf16[256,2048]{1,0:T(8,128)(2,1)} %copy-done.8, bf16[256,2048]{1,0:T(8,128)(2,1)} %copy-done.10, ...), custom_call_target="tpu_custom_call" | custom-call | flops 1 | bytes 1 | tf_op jit(solution)/shard_map/ffn/pallas_call | solution.py:180
  258.5 19.3 %weight_grads.3 = bf16[2048,1536]{1,0:T(8,128)(2,1)} custom-call(bf16[256,2048]{1,0:T(8,128)(2,1)} %copy-done.1, bf16[256,2048]{1,0:T(8,128)(2,1)} %copy-done.7, bf16[256,2048]{1,0:T(8,128)(2,1)} %copy-done.6, bf16[256,2048]{1,0:T(8,128)(2,1)} %copy-done.11, bf16[256,2048]{1,0:T(8,128)(2,1)} %copy-done.8, bf16[256,2048]{1,0:T(8,128)(2,1)} %copy-done.10, ...), custom_call_target="tpu_custom_call" | custom-call | flops 1 | bytes 1 | tf_op jit(solution)/shard_map/weight_grads/pallas_call | solution.py:216
  278.3 18.6 %all-gather.5.cloned.1.call-done.refs_16_.refs_3_ = bf16[2048,1536]{1,0:T(8,128)(2,1)} async-done(((bf16[512,1536]{1,0:T(8,128)(2,1)}), bf16[2048,1536]{1,0:T(8,128)(2,1)}) %all-gather.5.cloned.1.call-update) | async-done | bytes 6291472 | tf_op jit(solution)/shard_map/all_gather | solution.py:681
  296.9 21.7 %ffn.3.refs_1_.refs_16_.refs_17_ = bf16[2048,1536]{1,0:T(8,128)(2,1)} custom-call(bf16[256,2048]{1,0:T(8,128)(2,1)} %copy-done.1, bf16[256,2048]{1,0:T(8,128)(2,1)} %copy-done.7, bf16[256,2048]{1,0:T(8,128)(2,1)} %copy-done.6, bf16[256,2048]{1,0:T(8,128)(2,1)} %copy-done.11, bf16[256,2048]{1,0:T(8,128)(2,1)} %copy-done.8, bf16[256,2048]{1,0:T(8,128)(2,1)} %copy-done.10, ...), custom_call_target="tpu_custom_call" | custom-call | flops 1 | bytes 1 | tf_op jit(solution)/shard_map/ffn/pallas_call | solution.py:180
  318.6 14.5 %back.15 = bf16[1024,2048]{1,0:T(8,128)(2,1)} custom-call(bf16[2048,1536]{1,0:T(8,128)(2,1)} %ffn.2.refs_16_.refs_17_.refs_0_, bf16[2048,1536]{1,0:T(8,128)(2,1)} %ffn.3.refs_1_.refs_16_.refs_17_, bf16[2048,1536]{1,0:T(8,128)(2,1)} %all-gather.3.cloned.1.call-done.refs_16_.refs_2_, bf16[2048,1536]{1,0:T(8,128)(2,1)} %all-gather.5.cloned.1.call-done.refs_16_.refs_3_), custom_call_target="tpu_custom_call" | custom-call | flops 1 | bytes 1 | tf_op jit(solution)/shard_map/back/pallas_call | solution.py:252
  333.2 14.5 %back.14 = bf16[1024,2048]{1,0:T(8,128)(2,1)} custom-call(bf16[2048,1536]{1,0:T(8,128)(2,1)} %ffn.2.refs_16_.refs_17_.refs_0_, bf16[2048,1536]{1,0:T(8,128)(2,1)} %ffn.3.refs_1_.refs_16_.refs_17_, bf16[2048,1536]{1,0:T(8,128)(2,1)} %all-gather.3.cloned.1.call-done.refs_16_.refs_2_, bf16[2048,1536]{1,0:T(8,128)(2,1)} %all-gather.5.cloned.1.call-done.refs_16_.refs_3_), custom_call_target="tpu_custom_call" | custom-call | flops 1 | bytes 1 | tf_op jit(solution)/shard_map/back/pallas_call | solution.py:252
  347.7 4.6 slice_add_fusion
  353.9 19.4 %weight_grads.4 = bf16[2048,1536]{1,0:T(8,128)(2,1)} custom-call(bf16[256,2048]{1,0:T(8,128)(2,1)} %copy-done.1, bf16[256,2048]{1,0:T(8,128)(2,1)} %copy-done.7, bf16[256,2048]{1,0:T(8,128)(2,1)} %copy-done.6, bf16[256,2048]{1,0:T(8,128)(2,1)} %copy-done.11, bf16[256,2048]{1,0:T(8,128)(2,1)} %copy-done.8, bf16[256,2048]{1,0:T(8,128)(2,1)} %copy-done.10, ...), custom_call_target="tpu_custom_call" | custom-call | flops 1 | bytes 1 | tf_op jit(solution)/shard_map/weight_grads/pallas_call | solution.py:216
  373.5 5.2 collective-permute-done.30
  378.7 3.2 fusion.8
  383.6 6.3 back.18
  389.9 6.4 back.16
  397.3 3.3 fusion.25
  403.7 8.7 %back.17 = bf16[1024,2048]{1,0:T(8,128)(2,1)} custom-call(bf16[2048,1536]{1,0:T(8,128)(2,1)} %ffn.2.refs_16_.refs_17_.refs_0_, bf16[2048,1536]{1,0:T(8,128)(2,1)} %ffn.3.refs_1_.refs_16_.refs_17_, bf16[2048,1536]{1,0:T(8,128)(2,1)} %all-gather.3.cloned.1.call-done.refs_16_.refs_2_, bf16[2048,1536]{1,0:T(8,128)(2,1)} %all-gather.5.cloned.1.call-done.refs_16_.refs_3_), custom_call_target="tpu_custom_call" | custom-call | flops 1 | bytes 1 | tf_op jit(solution)/shard_map/back/pallas_call | solution.py:252
  412.4 5.2 broadcast_select_fusion
  417.6 8.5 %collective-permute-done.33.refs_2_ = bf16[256,2048]{1,0:T(8,128)(2,1)} collective-permute-done((bf16[256,2048]{1,0:T(8,128)(2,1)S(1)}, bf16[256,2048]{1,0:T(8,128)(2,1)}, u32[]{:S(2)}, u32[]{:S(2)}) %collective-permute-start.33) | collective-permute-done | bytes 1048608 | tf_op jit(solution)/shard_map/ppermute | solution.py:58
  431.5 10.2 %collective-permute-done.38.refs_3_ = bf16[256,2048]{1,0:T(8,128)(2,1)} collective-permute-done((bf16[256,2048]{1,0:T(8,128)(2,1)}, bf16[256,2048]{1,0:T(8,128)(2,1)}, u32[]{:S(2)}, u32[]{:S(2)}) %collective-permute-start.38) | collective-permute-done | bytes 1048608 | tf_op jit(solution)/shard_map/ppermute | solution.py:58
  447.0 9.6 %front.1.d_ref = bf16[2048,256]{1,0:T(8,128)(2,1)} custom-call(bf16[256,2048]{1,0:T(8,128)(2,1)} %copy-done.13, bf16[256,2048]{1,0:T(8,128)(2,1)} %collective-permute-done.32.refs_1_, bf16[256,2048]{1,0:T(8,128)(2,1)} %collective-permute-done.33.refs_2_, bf16[256,2048]{1,0:T(8,128)(2,1)} %collective-permute-done.38.refs_3_, bf16[256,2048]{1,0:T(8,128)(2,1)} %copy-done.26, ...), custom_call_target="tpu_custom_call" | custom-call | flops 1 | bytes 1 | tf_op jit(solution)/shard_map/front/pallas_call | solution.py:277
  456.6 35.1 %attend_back.1.refs_0_.refs_1_.refs_10_ = bf16[2048,384]{1,0:T(8,128)(2,1)} custom-call(s32[8]{0:T(128)} %select_reduce_fusion.2.place, s32[8]{0:T(128)} %and_select_fusion.2.first, bf16[2048,2432]{1,0:T(8,128)(2,1)} %qkv.1.q_ref.kv_ref.refs_8_, bf16[2048,256]{1,0:T(8,128)(2,1)} %front.1.d_ref, f32[2048,384]{1,0:T(8,128)} %attend.1.refs_0_.h_ref.refs_9_, ...), custom_call_target="tpu_custom_call" | custom-call | flops 1 | bytes 1 | tf_op jit(solution)/shard_map/attend_back/pallas_call | solution.py:455
  495.0 4.1 back.21
  499.4 4.1 back.20
  504.3 5.5 back.19
  514.3 15.4 %collective-permute-done.44 = bf16[256,2048]{1,0:T(8,128)(2,1)S(1)} collective-permute-done((bf16[256,2048]{1,0:T(8,128)(2,1)S(1)}, bf16[256,2048]{1,0:T(8,128)(2,1)S(1)}, u32[]{:S(2)}, u32[]{:S(2)}) %collective-permute-start.44) | collective-permute-done | bytes 1048608 | tf_op jit(solution)/shard_map/ppermute | solution.py:50
  531.1 12.6 %weight_grads.5 = bf16[2048,640]{1,0:T(8,128)(2,1)} custom-call(bf16[256,2048]{1,0:T(8,128)(2,1)} %copy-done.13, bf16[256,2048]{1,0:T(8,128)(2,1)} %collective-permute-done.32.refs_1_, bf16[256,2048]{1,0:T(8,128)(2,1)} %collective-permute-done.33.refs_2_, bf16[256,2048]{1,0:T(8,128)(2,1)} %collective-permute-done.38.refs_3_, bf16[256,2048]{1,0:T(8,128)(2,1)} %copy-done.26, ...), custom_call_target="tpu_custom_call" | custom-call | flops 1 | bytes 1 | tf_op jit(solution)/shard_map/weight_grads/pallas_call | solution.py:216
  543.7 3.1 fusion.10
  550.4 3.5 select_convert_fusion.3
  554.5 17.7 %collective-permute-done.50 = bf16[256,2048]{1,0:T(8,128)(2,1)} collective-permute-done((bf16[256,2048]{1,0:T(8,128)(2,1)}, bf16[256,2048]{1,0:T(8,128)(2,1)}, u32[]{:S(2)}, u32[]{:S(2)}) %collective-permute-start.50) | collective-permute-done | bytes 1048608 | tf_op jit(solution)/shard_map/ppermute | solution.py:54
  573.9 3.6 fusion.2
  577.6 4.7 fusion.6
  582.2 11.3 %collective-permute-done.45 = bf16[256,2048]{1,0:T(8,128)(2,1)} collective-permute-done((bf16[256,2048]{1,0:T(8,128)(2,1)}, bf16[256,2048]{1,0:T(8,128)(2,1)}, u32[]{:S(2)}, u32[]{:S(2)}) %collective-permute-start.45) | collective-permute-done | bytes 1048608 | tf_op jit(solution)/shard_map/ppermute | solution.py:46
  606.9 28.4 %collective-permute-done.56 = bf16[512,1536]{1,0:T(8,128)(2,1)S(1)} collective-permute-done((bf16[512,1536]{1,0:T(8,128)(2,1)S(1)}, bf16[512,1536]{1,0:T(8,128)(2,1)S(1)}, u32[]{:S(2)}, u32[]{:S(2)}) %collective-permute-start.56) | collective-permute-done | bytes 1572896 | tf_op jit(solution)/shard_map/ppermute | solution.py:50
  642.6 4.1 pad_maximum_fusion.3
  653.9 13.2 %collective-permute-done.60 = f32[2,512]{1,0:T(2,128)S(1)} collective-permute-done((f32[2,512]{1,0:T(2,128)S(1)}, f32[2,512]{1,0:T(2,128)S(1)}, u32[]{:S(2)}, u32[]{:S(2)}) %collective-permute-start.60) | collective-permute-done | bytes 4128 | tf_op jit(solution)/shard_map/ppermute | solution.py:50
  (329 shorter events, 136.3 us)
Async XLA Ops:
  7.2 182.6 %all-gather.3.cloned.1.call-start = ((), (), s32[]{:S(2)}) async-start(), calls=%async_computation.3 | async-start | bytes 7864320 | tf_op jit(solution)/shard_map/all_gather | solution.py:681
  11.9 20.5 %collective-permute-start = (bf16[528,640]{1,0:T(8,128)(2,1)}, bf16[528,640]{1,0:T(8,128)(2,1)}, u32[]{:S(2)}, u32[]{:S(2)}) collective-permute-start(bf16[528,640]{1,0:T(8,128)(2,1)} %fusion.12), channel_id=1, source_target_pairs={{0,8},{8,16},{16,24},{24,0},{1,9},{9,17},{17,25},{25,1},{2,10},{10... | collective-permute-start | bytes 2027528 | tf_op jit(solution)/shard_map/ppermute | solution.py:530
  16.3 16.2 %collective-permute-start.1 = (bf16[256,2048]{1,0:T(8,128)(2,1)S(1)}, bf16[256,2048]{1,0:T(8,128)(2,1)S(1)}, u32[]{:S(2)}, u32[]{:S(2)}) collective-permute-start(bf16[256,2048]{1,0:T(8,128)(2,1)S(1)} %constant_dynamic-slice_fusion.11.refs_0_), channel_id=1, source_target_pairs={{0,4},{1,3},{2,6},{3,1},{4,0},{5,7},{6,2},{7,5},{8,12},{9,11},{10,... | collective-permute-start | bytes 3145736 | tf_op jit(solution)/shard_map/ppermute | solution.py:54
  32.5 18.5 %collective-permute-start.2 = (bf16[528,640]{1,0:T(8,128)(2,1)}, bf16[528,640]{1,0:T(8,128)(2,1)}, u32[]{:S(2)}, u32[]{:S(2)}) collective-permute-start(bf16[528,640]{1,0:T(8,128)(2,1)} %collective-permute-done), channel_id=1, source_target_pairs={{0,8},{8,16},{16,24},{24,0},{1,9},{9,17},{17,25},{25,1},{2,10},{10... | collective-permute-start | bytes 2027528 | tf_op jit(solution)/shard_map/ppermute | solution.py:530
  32.7 25.2 %collective-permute-start.4 = (bf16[256,2048]{1,0:T(8,128)(2,1)S(1)}, bf16[256,2048]{1,0:T(8,128)(2,1)}, u32[]{:S(2)}, u32[]{:S(2)}) collective-permute-start(bf16[256,2048]{1,0:T(8,128)(2,1)S(1)} %constant_dynamic-slice_fusion.11.refs_0_), channel_id=1, source_target_pairs={{0,2},{1,5},{2,0},{3,7},{4,6},{5,1},{6,4},{7,3},{8,10},{9,13},{10,... | collective-permute-start | bytes 3145736 | tf_op jit(solution)/shard_map/ppermute | solution.py:58
  34.2 24.6 %collective-permute-start.5 = (bf16[256,2048]{1,0:T(8,128)(2,1)S(1)}, bf16[256,2048]{1,0:T(8,128)(2,1)}, u32[]{:S(2)}, u32[]{:S(2)}) collective-permute-start(bf16[256,2048]{1,0:T(8,128)(2,1)S(1)} %collective-permute-done.1.refs_1_), channel_id=1, source_target_pairs={{0,2},{1,5},{2,0},{3,7},{4,6},{5,1},{6,4},{7,3},{8,10},{9,13},{10,... | collective-permute-start | bytes 3145736 | tf_op jit(solution)/shard_map/ppermute | solution.py:58
  50.9 17.6 %collective-permute-start.3 = (bf16[528,640]{1,0:T(8,128)(2,1)}, bf16[528,640]{1,0:T(8,128)(2,1)}, u32[]{:S(2)}, u32[]{:S(2)}) collective-permute-start(bf16[528,640]{1,0:T(8,128)(2,1)} %collective-permute-done.2), channel_id=1, source_target_pairs={{0,8},{8,16},{16,24},{24,0},{1,9},{9,17},{17,25},{25,1},{2,10},{10... | collective-permute-start | bytes 2027528 | tf_op jit(solution)/shard_map/ppermute | solution.py:530
  68.5 228.4 %all-gather.5.cloned.1.call-start = ((), (), s32[]{:S(2)}) async-start(), calls=%async_computation.4 | async-start | bytes 7864320 | tf_op jit(solution)/shard_map/all_gather | solution.py:681
  77.0 25.6 %collective-permute-start.11 = (bf16[256,2048]{1,0:T(8,128)(2,1)}, bf16[256,2048]{1,0:T(8,128)(2,1)S(1)}, u32[]{:S(2)}, u32[]{:S(2)}) collective-permute-start(bf16[256,2048]{1,0:T(8,128)(2,1)} %constant_dynamic-slice_fusion.6.refs_8_), channel_id=1, source_target_pairs={{0,2},{1,5},{2,0},{3,7},{4,6},{5,1},{6,4},{7,3},{8,10},{9,13},{10,... | collective-permute-start | bytes 3145736 | tf_op jit(solution)/shard_map/ppermute | solution.py:58
  78.3 24.4 %collective-permute-start.10 = (bf16[256,2048]{1,0:T(8,128)(2,1)}, bf16[256,2048]{1,0:T(8,128)(2,1)S(1)}, u32[]{:S(2)}, u32[]{:S(2)}) collective-permute-start(bf16[256,2048]{1,0:T(8,128)(2,1)} %constant_dynamic-slice_fusion.6.refs_8_), channel_id=1, source_target_pairs={{0,4},{1,3},{2,6},{3,1},{4,0},{5,7},{6,2},{7,5},{8,12},{9,11},{10,... | collective-permute-start | bytes 3145736 | tf_op jit(solution)/shard_map/ppermute | solution.py:54
  79.5 49.1 %collective-permute-start.13 = (bf16[256,2048]{1,0:T(8,128)(2,1)}, bf16[256,2048]{1,0:T(8,128)(2,1)S(1)}, u32[]{:S(2)}, u32[]{:S(2)}) collective-permute-start(bf16[256,2048]{1,0:T(8,128)(2,1)} %constant_dynamic-slice_fusion.6.refs_8_), channel_id=1, source_target_pairs={{0,1},{1,0},{2,3},{3,2},{4,5},{5,4},{6,7},{7,6},{8,9},{9,8},{10,11... | collective-permute-start | bytes 3145736 | tf_op jit(solution)/shard_map/ppermute | solution.py:42
  102.7 26.0 %collective-permute-start.15 = (bf16[256,2048]{1,0:T(8,128)(2,1)S(1)}, bf16[256,2048]{1,0:T(8,128)(2,1)}, u32[]{:S(2)}, u32[]{:S(2)}) collective-permute-start(bf16[256,2048]{1,0:T(8,128)(2,1)S(1)} %collective-permute-done.11.refs_10_), channel_id=1, source_target_pairs={{0,1},{1,0},{2,3},{3,2},{4,5},{5,4},{6,7},{7,6},{8,9},{9,8},{10,11... | collective-permute-start | bytes 3145736 | tf_op jit(solution)/shard_map/ppermute | solution.py:42
  103.5 25.2 %collective-permute-start.14 = (bf16[256,2048]{1,0:T(8,128)(2,1)S(1)}, bf16[256,2048]{1,0:T(8,128)(2,1)}, u32[]{:S(2)}, u32[]{:S(2)}) collective-permute-start(bf16[256,2048]{1,0:T(8,128)(2,1)S(1)} %collective-permute-done.10.refs_9_), channel_id=1, source_target_pairs={{0,1},{1,0},{2,3},{3,2},{4,5},{5,4},{6,7},{7,6},{8,9},{9,8},{10,11... | collective-permute-start | bytes 3145736 | tf_op jit(solution)/shard_map/ppermute | solution.py:42
  103.5 25.2 %collective-permute-start.12 = (bf16[256,2048]{1,0:T(8,128)(2,1)S(1)}, bf16[256,2048]{1,0:T(8,128)(2,1)}, u32[]{:S(2)}, u32[]{:S(2)}) collective-permute-start(bf16[256,2048]{1,0:T(8,128)(2,1)S(1)} %collective-permute-done.10.refs_9_), channel_id=1, source_target_pairs={{0,2},{1,5},{2,0},{3,7},{4,6},{5,1},{6,4},{7,3},{8,10},{9,13},{10,... | collective-permute-start | bytes 3145736 | tf_op jit(solution)/shard_map/ppermute | solution.py:58
  136.9 304.9 %reduce-scatter.4.cloned.1.call-start = ((), (), s32[]{:S(2)}) async-start(), calls=%async_computation.5 | async-start | bytes 7864320 | tf_op jit(solution)/shard_map/reduce_scatter | solution.py:712
  140.6 21.2 %collective-permute-start.17 = (bf16[512,2048]{1,0:T(8,128)(2,1)}, bf16[512,2048]{1,0:T(8,128)(2,1)S(1)}, u32[]{:S(2)}, u32[]{:S(2)}) collective-permute-start(bf16[512,2048]{1,0:T(8,128)(2,1)} %back.12), channel_id=1, source_target_pairs={{0,1},{1,0},{2,3},{3,2},{4,5},{5,4},{6,7},{7,6},{8,9},{9,8},{10,11... | collective-permute-start | bytes 6291464 | tf_op jit(solution)/shard_map/ppermute | solution.py:42
  146.9 14.9 %collective-permute-start.19 = (bf16[256,2048]{1,0:T(8,128)(2,1)S(1)}, bf16[256,2048]{1,0:T(8,128)(2,1)S(1)}, u32[]{:S(2)}, u32[]{:S(2)}) collective-permute-start(bf16[256,2048]{1,0:T(8,128)(2,1)S(1)} %get-tuple-element.142), channel_id=1, source_target_pairs={{0,2},{1,5},{2,0},{3,7},{4,6},{5,1},{6,4},{7,3},{8,10},{9,13},{10,... | collective-permute-start | bytes 3145736 | tf_op jit(solution)/shard_map/ppermute | solution.py:58
  164.0 25.8 %collective-permute-start.21 = (bf16[256,2048]{1,0:T(8,128)(2,1)S(1)}, bf16[256,2048]{1,0:T(8,128)(2,1)S(1)}, u32[]{:S(2)}, u32[]{:S(2)}) collective-permute-start(bf16[256,2048]{1,0:T(8,128)(2,1)S(1)} %fusion.11), channel_id=1, source_target_pairs={{0,4},{1,3},{2,6},{3,1},{4,0},{5,7},{6,2},{7,5},{8,12},{9,11},{10,... | collective-permute-start | bytes 3145736 | tf_op jit(solution)/shard_map/ppermute | solution.py:54
  165.5 24.3 %collective-permute-start.20 = (bf16[256,2048]{1,0:T(8,128)(2,1)S(1)}, bf16[256,2048]{1,0:T(8,128)(2,1)}, u32[]{:S(2)}, u32[]{:S(2)}) collective-permute-start(bf16[256,2048]{1,0:T(8,128)(2,1)S(1)} %get-tuple-element.85), channel_id=1, source_target_pairs={{0,2},{1,5},{2,0},{3,7},{4,6},{5,1},{6,4},{7,3},{8,10},{9,13},{10,... | collective-permute-start | bytes 3145736 | tf_op jit(solution)/shard_map/ppermute | solution.py:58
  193.4 25.2 %collective-permute-start.23 = (bf16[256,2048]{1,0:T(8,128)(2,1)S(1)}, bf16[256,2048]{1,0:T(8,128)(2,1)S(1)}, u32[]{:S(2)}, u32[]{:S(2)}) collective-permute-start(bf16[256,2048]{1,0:T(8,128)(2,1)S(1)} %multiply_convert_fusion.refs_0_), channel_id=1, source_target_pairs={{0,2},{1,5},{2,0},{3,7},{4,6},{5,1},{6,4},{7,3},{8,10},{9,13},{10,... | collective-permute-start | bytes 3145736 | tf_op jit(solution)/shard_map/ppermute | solution.py:58
  194.2 24.4 %collective-permute-start.22 = (bf16[256,2048]{1,0:T(8,128)(2,1)S(1)}, bf16[256,2048]{1,0:T(8,128)(2,1)S(1)}, u32[]{:S(2)}, u32[]{:S(2)}) collective-permute-start(bf16[256,2048]{1,0:T(8,128)(2,1)S(1)} %multiply_convert_fusion.refs_0_), channel_id=1, source_target_pairs={{0,4},{1,3},{2,6},{3,1},{4,0},{5,7},{6,2},{7,5},{8,12},{9,11},{10,... | collective-permute-start | bytes 3145736 | tf_op jit(solution)/shard_map/ppermute | solution.py:54
  195.6 25.2 %collective-permute-start.25 = (bf16[256,2048]{1,0:T(8,128)(2,1)S(1)}, bf16[256,2048]{1,0:T(8,128)(2,1)S(1)}, u32[]{:S(2)}, u32[]{:S(2)}) collective-permute-start(bf16[256,2048]{1,0:T(8,128)(2,1)S(1)} %multiply_convert_fusion.refs_0_), channel_id=1, source_target_pairs={{0,1},{1,0},{2,3},{3,2},{4,5},{5,4},{6,7},{7,6},{8,9},{9,8},{10,11... | collective-permute-start | bytes 3145736 | tf_op jit(solution)/shard_map/ppermute | solution.py:42
  219.1 14.8 %collective-permute-start.24 = (bf16[256,2048]{1,0:T(8,128)(2,1)S(1)}, bf16[256,2048]{1,0:T(8,128)(2,1)S(1)}, u32[]{:S(2)}, u32[]{:S(2)}) collective-permute-start(bf16[256,2048]{1,0:T(8,128)(2,1)S(1)} %collective-permute-done.22.refs_1_), channel_id=1, source_target_pairs={{0,2},{1,5},{2,0},{3,7},{4,6},{5,1},{6,4},{7,3},{8,10},{9,13},{10,... | collective-permute-start | bytes 3145736 | tf_op jit(solution)/shard_map/ppermute | solution.py:58
  277.8 276.6 %reduce-scatter.6.cloned.1.call-start = ((), (), s32[]{:S(2)}) async-start(), calls=%async_computation.6 | async-start | bytes 7864320 | tf_op jit(solution)/shard_map/reduce_scatter | solution.py:712
  333.1 14.5 %collective-permute-start.29 = (bf16[1024,2048]{1,0:T(8,128)(2,1)}, bf16[1024,2048]{1,0:T(8,128)(2,1)S(1)}, u32[]{:S(2)}, u32[]{:S(2)}) collective-permute-start(bf16[1024,2048]{1,0:T(8,128)(2,1)} %back.15), channel_id=1, source_target_pairs={{0,1},{1,0},{2,3},{3,2},{4,5},{5,4},{6,7},{7,6},{8,9},{9,8},{10,11... | collective-permute-start | bytes 12582920 | tf_op jit(solution)/shard_map/ppermute | solution.py:42
  352.3 26.4 %collective-permute-start.30 = (bf16[512,2048]{1,0:T(8,128)(2,1)}, bf16[512,2048]{1,0:T(8,128)(2,1)}, u32[]{:S(2)}, u32[]{:S(2)}) collective-permute-start(bf16[512,2048]{1,0:T(8,128)(2,1)} %slice_add_fusion), channel_id=1, source_target_pairs={{0,2},{1,5},{2,0},{3,7},{4,6},{5,1},{6,4},{7,3},{8,10},{9,13},{10,... | collective-permute-start | bytes 6291464 | tf_op jit(solution)/shard_map/ppermute | solution.py:58
  373.3 267.9 %reduce-scatter.8.cloned.1.call-start = ((), (), s32[]{:S(2)}) async-start(), calls=%async_computation.7 | async-start | bytes 3276800 | tf_op jit(solution)/shard_map/reduce_scatter | solution.py:749
  381.9 14.9 %collective-permute-start.31 = (bf16[256,2048]{1,0:T(8,128)(2,1)S(1)}, bf16[256,2048]{1,0:T(8,128)(2,1)S(1)}, u32[]{:S(2)}, u32[]{:S(2)}) collective-permute-start(bf16[256,2048]{1,0:T(8,128)(2,1)S(1)} %slice.221), channel_id=1, source_target_pairs={{0,4},{1,3},{2,6},{3,1},{4,0},{5,7},{6,2},{7,5},{8,12},{9,11},{10,... | collective-permute-start | bytes 3145736 | tf_op jit(solution)/shard_map/ppermute | solution.py:54
  389.8 22.5 %collective-permute-start.34 = (bf16[512,2048]{1,0:T(8,128)(2,1)}, bf16[512,2048]{1,0:T(8,128)(2,1)}, u32[]{:S(2)}, u32[]{:S(2)}) collective-permute-start(bf16[512,2048]{1,0:T(8,128)(2,1)} %back.18), channel_id=1, source_target_pairs={{0,1},{1,0},{2,3},{3,2},{4,5},{5,4},{6,7},{7,6},{8,9},{9,8},{10,11... | collective-permute-start | bytes 6291464 | tf_op jit(solution)/shard_map/ppermute | solution.py:42
  396.3 16.1 %collective-permute-start.35 = (bf16[512,2048]{1,0:T(8,128)(2,1)}, bf16[512,2048]{1,0:T(8,128)(2,1)}, u32[]{:S(2)}, u32[]{:S(2)}) collective-permute-start(bf16[512,2048]{1,0:T(8,128)(2,1)} %back.16), channel_id=1, source_target_pairs={{0,1},{1,0},{2,3},{3,2},{4,5},{5,4},{6,7},{7,6},{8,9},{9,8},{10,11... | collective-permute-start | bytes 6291464 | tf_op jit(solution)/shard_map/ppermute | solution.py:42
  400.7 25.5 %collective-permute-start.33 = (bf16[256,2048]{1,0:T(8,128)(2,1)S(1)}, bf16[256,2048]{1,0:T(8,128)(2,1)}, u32[]{:S(2)}, u32[]{:S(2)}) collective-permute-start(bf16[256,2048]{1,0:T(8,128)(2,1)S(1)} %get-tuple-element.127.refs_0_), channel_id=1, source_target_pairs={{0,2},{1,5},{2,0},{3,7},{4,6},{5,1},{6,4},{7,3},{8,10},{9,13},{10,... | collective-permute-start | bytes 3145736 | tf_op jit(solution)/shard_map/ppermute | solution.py:58
  402.2 23.9 %collective-permute-start.32 = (bf16[256,2048]{1,0:T(8,128)(2,1)S(1)}, bf16[256,2048]{1,0:T(8,128)(2,1)}, u32[]{:S(2)}, u32[]{:S(2)}) collective-permute-start(bf16[256,2048]{1,0:T(8,128)(2,1)S(1)} %get-tuple-element.127.refs_0_), channel_id=1, source_target_pairs={{0,4},{1,3},{2,6},{3,1},{4,0},{5,7},{6,2},{7,5},{8,12},{9,11},{10,... | collective-permute-start | bytes 3145736 | tf_op jit(solution)/shard_map/ppermute | solution.py:54
  426.7 15.1 %collective-permute-start.38 = (bf16[256,2048]{1,0:T(8,128)(2,1)}, bf16[256,2048]{1,0:T(8,128)(2,1)}, u32[]{:S(2)}, u32[]{:S(2)}) collective-permute-start(bf16[256,2048]{1,0:T(8,128)(2,1)} %collective-permute-done.32.refs_1_), channel_id=1, source_target_pairs={{0,2},{1,5},{2,0},{3,7},{4,6},{5,1},{6,4},{7,3},{8,10},{9,13},{10,... | collective-permute-start | bytes 3145736 | tf_op jit(solution)/shard_map/ppermute | solution.py:58
  441.8 50.9 %collective-permute-start.43 = (bf16[512,1536]{1,0:T(8,128)(2,1)}, bf16[512,1536]{1,0:T(8,128)(2,1)S(1)}, u32[]{:S(2)}, u32[]{:S(2)}) collective-permute-start(bf16[512,1536]{1,0:T(8,128)(2,1)} %reduce-scatter.4.cloned.1.call-done), channel_id=1, source_target_pairs={{0,4},{4,0},{1,5},{5,1},{2,6},{6,2},{3,7},{7,3},{8,12},{12,8},{9,1... | collective-permute-start | bytes 4718600 | tf_op jit(solution)/shard_map/ppermute | solution.py:50
  443.2 48.5 %collective-permute-start.36 = (bf16[256,2048]{1,0:T(8,128)(2,1)}, bf16[256,2048]{1,0:T(8,128)(2,1)S(1)}, u32[]{:S(2)}, u32[]{:S(2)}) collective-permute-start(bf16[256,2048]{1,0:T(8,128)(2,1)} %get-tuple-element.97), channel_id=1, source_target_pairs={{0,2},{2,0},{1,3},{3,1},{4,6},{6,4},{5,7},{7,5},{8,10},{10,8},{9,1... | collective-permute-start | bytes 3145736 | tf_op jit(solution)/shard_map/ppermute | solution.py:46
  444.6 47.1 %collective-permute-start.37 = (bf16[256,2048]{1,0:T(8,128)(2,1)}, bf16[256,2048]{1,0:T(8,128)(2,1)S(1)}, u32[]{:S(2)}, u32[]{:S(2)}) collective-permute-start(bf16[256,2048]{1,0:T(8,128)(2,1)} %get-tuple-element.98), channel_id=1, source_target_pairs={{0,2},{2,0},{1,3},{3,1},{4,6},{6,4},{5,7},{7,5},{8,10},{10,8},{9,1... | collective-permute-start | bytes 3145736 | tf_op jit(solution)/shard_map/ppermute | solution.py:46
  503.4 40.3 %collective-permute-start.46 = (bf16[512,2048]{1,0:T(8,128)(2,1)}, bf16[512,2048]{1,0:T(8,128)(2,1)}, u32[]{:S(2)}, u32[]{:S(2)}) collective-permute-start(bf16[512,2048]{1,0:T(8,128)(2,1)} %back.20), channel_id=1, source_target_pairs={{0,1},{1,0},{2,3},{3,2},{4,5},{5,4},{6,7},{7,6},{8,9},{9,8},{10,11... | collective-permute-start | bytes 6291464 | tf_op jit(solution)/shard_map/ppermute | solution.py:42
  503.7 26.0 %collective-permute-start.44 = (bf16[256,2048]{1,0:T(8,128)(2,1)S(1)}, bf16[256,2048]{1,0:T(8,128)(2,1)S(1)}, u32[]{:S(2)}, u32[]{:S(2)}) collective-permute-start(bf16[256,2048]{1,0:T(8,128)(2,1)S(1)} %add.408), channel_id=1, source_target_pairs={{0,4},{4,0},{1,5},{5,1},{2,6},{6,2},{3,7},{7,3},{8,12},{12,8},{9,1... | collective-permute-start | bytes 3145736 | tf_op jit(solution)/shard_map/ppermute | solution.py:50
  512.9 30.8 %collective-permute-start.48 = (bf16[256,2048]{1,0:T(8,128)(2,1)}, bf16[256,2048]{1,0:T(8,128)(2,1)}, u32[]{:S(2)}, u32[]{:S(2)}) collective-permute-start(bf16[256,2048]{1,0:T(8,128)(2,1)} %get-tuple-element.138), channel_id=1, source_target_pairs={{0,2},{1,5},{2,0},{3,7},{4,6},{5,1},{6,4},{7,3},{8,10},{9,13},{10,... | collective-permute-start | bytes 3145736 | tf_op jit(solution)/shard_map/ppermute | solution.py:58
  546.8 25.4 %collective-permute-start.50 = (bf16[256,2048]{1,0:T(8,128)(2,1)}, bf16[256,2048]{1,0:T(8,128)(2,1)}, u32[]{:S(2)}, u32[]{:S(2)}) collective-permute-start(bf16[256,2048]{1,0:T(8,128)(2,1)} %fusion.10), channel_id=1, source_target_pairs={{0,4},{1,3},{2,6},{3,1},{4,0},{5,7},{6,2},{7,5},{8,12},{9,11},{10,... | collective-permute-start | bytes 3145736 | tf_op jit(solution)/shard_map/ppermute | solution.py:54
  547.5 26.4 %collective-permute-start.49 = (bf16[256,2048]{1,0:T(8,128)(2,1)}, bf16[256,2048]{1,0:T(8,128)(2,1)}, u32[]{:S(2)}, u32[]{:S(2)}) collective-permute-start(bf16[256,2048]{1,0:T(8,128)(2,1)} %get-tuple-element.112), channel_id=1, source_target_pairs={{0,2},{1,5},{2,0},{3,7},{4,6},{5,1},{6,4},{7,3},{8,10},{9,13},{10,... | collective-permute-start | bytes 3145736 | tf_op jit(solution)/shard_map/ppermute | solution.py:58
  553.9 39.6 %collective-permute-start.45 = (bf16[256,2048]{1,0:T(8,128)(2,1)}, bf16[256,2048]{1,0:T(8,128)(2,1)}, u32[]{:S(2)}, u32[]{:S(2)}) collective-permute-start(bf16[256,2048]{1,0:T(8,128)(2,1)} %add_convert_fusion), channel_id=1, source_target_pairs={{0,2},{2,0},{1,3},{3,1},{4,6},{6,4},{5,7},{7,5},{8,10},{10,8},{9,1... | collective-permute-start | bytes 3145736 | tf_op jit(solution)/shard_map/ppermute | solution.py:46
  597.3 75.5 %collective-permute-start.54 = (bf16[256,2048]{1,0:T(8,128)(2,1)}, bf16[256,2048]{1,0:T(8,128)(2,1)}, u32[]{:S(2)}, u32[]{:S(2)}) collective-permute-start(bf16[256,2048]{1,0:T(8,128)(2,1)} %fusion.6), channel_id=1, source_target_pairs={{0,1},{1,0},{2,3},{3,2},{4,5},{5,4},{6,7},{7,6},{8,9},{9,8},{10,11... | collective-permute-start | bytes 3145736 | tf_op jit(solution)/shard_map/ppermute | solution.py:42
  597.3 43.9 %collective-permute-start.53 = (bf16[256,2048]{1,0:T(8,128)(2,1)}, bf16[256,2048]{1,0:T(8,128)(2,1)}, u32[]{:S(2)}, u32[]{:S(2)}) collective-permute-start(bf16[256,2048]{1,0:T(8,128)(2,1)} %fusion.6), channel_id=1, source_target_pairs={{0,2},{2,0},{1,3},{3,1},{4,6},{6,4},{5,7},{7,5},{8,10},{10,8},{9,1... | collective-permute-start | bytes 3145736 | tf_op jit(solution)/shard_map/ppermute | solution.py:46
  598.8 36.5 %collective-permute-start.56 = (bf16[512,1536]{1,0:T(8,128)(2,1)S(1)}, bf16[512,1536]{1,0:T(8,128)(2,1)S(1)}, u32[]{:S(2)}, u32[]{:S(2)}) collective-permute-start(bf16[512,1536]{1,0:T(8,128)(2,1)S(1)} %copy-done.23), channel_id=1, source_target_pairs={{0,4},{4,0},{1,5},{5,1},{2,6},{6,2},{3,7},{7,3},{8,12},{12,8},{9,1... | collective-permute-start | bytes 4718600 | tf_op jit(solution)/shard_map/ppermute | solution.py:50
  649.8 23.0 %collective-permute-start.55 = (bf16[256,2048]{1,0:T(8,128)(2,1)}, bf16[256,2048]{1,0:T(8,128)(2,1)S(1)}, u32[]{:S(2)}, u32[]{:S(2)}) collective-permute-start(bf16[256,2048]{1,0:T(8,128)(2,1)} %collective-permute-done.53), channel_id=1, source_target_pairs={{0,1},{1,0},{2,3},{3,2},{4,5},{5,4},{6,7},{7,6},{8,9},{9,8},{10,11... | collective-permute-start | bytes 3145736 | tf_op jit(solution)/shard_map/ppermute | solution.py:42
  650.0 18.3 %collective-permute-start.57 = (bf16[512,640]{1,0:T(8,128)(2,1)S(1)}, bf16[512,640]{1,0:T(8,128)(2,1)S(1)}, u32[]{:S(2)}, u32[]{:S(2)}) collective-permute-start(bf16[512,640]{1,0:T(8,128)(2,1)S(1)} %copy-done.46), channel_id=1, source_target_pairs={{0,4},{4,0},{1,5},{5,1},{2,6},{6,2},{3,7},{7,3},{8,12},{12,8},{9,1... | collective-permute-start | bytes 1966088 | tf_op jit(solution)/shard_map/ppermute | solution.py:50
  650.5 16.6 %collective-permute-start.60 = (f32[2,512]{1,0:T(2,128)S(1)}, f32[2,512]{1,0:T(2,128)S(1)}, u32[]{:S(2)}, u32[]{:S(2)}) collective-permute-start(f32[2,512]{1,0:T(2,128)S(1)} %fusion.36), channel_id=1, source_target_pairs={{0,4},{4,0},{1,5},{5,1},{2,6},{6,2},{3,7},{7,3},{8,12},{12,8},{9,1... | collective-permute-start | bytes 12296 | tf_op jit(solution)/shard_map/ppermute | solution.py:50
  (78 other events, 803.6 us)
Sparse Core Ops, SparseCore 0:
  68.6 113.0 all-gather.2
  183.3 113.5 all-gather.4
  299.2 108.9 reduce-scatter.3
  410.4 111.2 reduce-scatter.5
  554.6 50.5 reduce-scatter.7

commit v7 on v6

--- a/solution.py
+++ b/solution.py
@@ -224,15 +224,14 @@
         ],
         out_specs=pl.BlockSpec((step, width), lambda i: (i, 0)),
         compiler_params=params(),
-        cost_estimate=cost(),
+        cost_estimate=cost(20),
         name="weight_grads",
     )(*x, *y, a, b)
 
 
-def back_kernel(*refs):
+def back_kernel(count, *refs):
     o_ref = refs[-1]
-    count = (len(refs) - 1) // 2
-    total = None
+    total = refs[2 * count][...].astype(F32) if len(refs) > 2 * count + 1 else None
     for part in range(count):
         term = lax.dot_general(
             refs[part][...].astype(BF16),
@@ -244,25 +243,26 @@
     o_ref[...] = total.astype(BF16)
 
 
-def back_product(terms, part, parts):
+def back_product(terms, part=0, parts=1, plus=()):
     rows = terms[0][0].shape[0] // parts
     depth = terms[0][2].shape[0]
     step = min(512, rows)
     ahead = part * (rows // step)
     return pl.pallas_call(
-        back_kernel,
+        functools.partial(back_kernel, len(terms)),
         out_shape=jax.ShapeDtypeStruct((rows, depth), BF16),
         grid=(rows // step,),
         in_specs=[
             pl.BlockSpec((step, term[4]), lambda i, column=term[1]: (i + ahead, column))
             for term in terms
         ]
-        + [pl.BlockSpec((depth, term[4]), lambda i, column=term[3]: (0, column)) for term in terms],
+        + [pl.BlockSpec((depth, term[4]), lambda i, column=term[3]: (0, column)) for term in terms]
+        + [pl.BlockSpec((step, depth), lambda i: (i + ahead, 0))] * len(plus),
         out_specs=pl.BlockSpec((step, depth), lambda i: (i, 0)),
         compiler_params=params(),
         cost_estimate=cost(),
         name="back",
-    )(*[term[0] for term in terms], *[term[2] for term in terms])
+    )(*[term[0] for term in terms], *[term[2] for term in terms], *plus)
 
 
 def front_kernel(count, *refs):
@@ -504,11 +504,15 @@
     return own.astype(F32) + swap_second(along_b).astype(F32) + from_a.astype(F32)
 
 
-def sum_wide(terms, between, beside):
-    arrived = swap_core(back_product(terms, 1, 2))
-    mine = back_product(terms, 0, 2)
+def halves_of_cores(terms, plus):
+    arrived = swap_core(back_product(terms, 1, 2, plus))
+    mine = back_product(terms, 0, 2, plus)
     rows = mine.shape[0] // 4
-    far, near = mine[2 * rows :] + arrived[2 * rows :], mine[: 2 * rows] + arrived[: 2 * rows]
+    return mine[2 * rows :] + arrived[2 * rows :], mine[: 2 * rows] + arrived[: 2 * rows]
+
+
+def sum_wide(far, near, between, beside):
+    rows = near.shape[0] // 2
     near = after(near + swap_second(far), *between)
     from_a = after(swap_first(near[rows:]), *beside)
     return near[:rows].astype(F32) + from_a.astype(F32)
@@ -689,6 +693,7 @@
 
     acts = []
     grad_parts = []
+    d_norm_partial = ()
 
     def chunk_grads(part, held=()):
         chunk = chunks[part]
@@ -697,21 +702,21 @@
 
     last = len(chunks) - 1
     for part in range(len(chunks)):
-        normed_two = (after(normed_two[0], *grad_parts), *normed_two[1:])
+        normed_two = (after(normed_two[0], *grad_parts, *d_norm_partial), *normed_two[1:])
         acts.append(ffn_chunk(normed_two, cot, ffn_full[part]))
+        d_norm_term = (acts[part], 0, ffn_full[part], 0, 2 * chunks[part])
         if part < last:
             chunk_grads(part)
-    d_norm_terms = [
-        (acts[part], 0, ffn_full[part], 0, 2 * chunk) for part, chunk in enumerate(chunks)
-    ]
+            d_norm_partial = (back_product([d_norm_term], plus=d_norm_partial),)
     ffn_terms = [(acts[part], 2, ffn_full[part], 2, chunk) for part, chunk in enumerate(chunks)]
     ffn_sent = [back_product(ffn_terms, at, 4) for at in (3, 2)]
     ffn_mine = back_product(ffn_terms, 0, 2)
+    d_norm_far, d_norm_near = halves_of_cores([d_norm_term], d_norm_partial)
     chunk_grads(last)
     reduced = [
         lax.psum_scatter(part, "fsdp", scatter_dimension=0, tiled=True) for part in grad_parts
     ]
-    d_normed_two = sum_wide(d_norm_terms, grad_parts, ffn_sent[:1])
+    d_normed_two = sum_wide(d_norm_far, d_norm_near, grad_parts, ffn_sent[:1])
     d_hidden = cot_own + rms_back(hidden, gain_two, d_normed_two)
     d_own = d_hidden.astype(BF16)
     ffn_own, ffn_a, ffn_b, ffn_both = add_blocks(ffn_mine, [swap_core(piece) for piece in ffn_sent])
@@ -730,8 +735,7 @@
         (swap_y(ffn_both), swap_y(ffn_y), d_qkv, other_reduced[0])
     )
     ffn_x, ffn_own, d_qkv = lax.optimization_barrier((ffn_x + y_both, ffn_own + y_own, d_qkv))
-    result_own = (hidden + (ffn_own.astype(F32) + swap_x(ffn_x).astype(F32))).astype(BF16)
-    result_beside = swap_y(result_own)
+    ffn_far = swap_x(ffn_x)
     normed_blocks = sum_cores(
         [
             (d_qkv, 0, attn_full, 1, q_width),
@@ -739,23 +743,29 @@
         ]
     )
     attn_grad = weight_grads(
-        d_attn, heads, q_width, 0, (qkv,), after(d_qkv, result_own), q_width + 128, 0
-    )
-    d_normed = sum_last(*sum_first(normed_blocks, [attn_grad]), beside=reduced[1:])
+        d_attn, heads, q_width, 0, (qkv,), after(d_qkv, normed_blocks[3]), q_width + 128, 0
+    )
+    ffn_far = after(ffn_far, attn_grad)
+    result_own = (hidden + (ffn_own.astype(F32) + ffn_far.astype(F32))).astype(BF16)
+    result_beside = swap_y(result_own)
+    normed_first = sum_first(normed_blocks, [attn_grad, result_own])
+    d_normed = sum_last(*normed_first, beside=[result_beside])
     tokens_grad_own = (d_hidden + rms_back(tokens_own, gain_one, d_normed)).astype(BF16)
     for part in range(1, len(chunks)):
         reduced[part] = after(reduced[part], tokens_grad_own)
         other_reduced.append(swap_x(reduced[part]))
     attn_reduced = lax.psum_scatter(attn_grad, "fsdp", scatter_dimension=0, tiled=True)
     attn_reduced = after(attn_reduced, tokens_grad_own)
-    tokens_grad_beside = after(swap_y(tokens_grad_own), attn_reduced)
+    tokens_grad_beside, other_reduced[1:] = lax.optimization_barrier(
+        (swap_y(tokens_grad_own), other_reduced[1:], attn_reduced)
+    )[:2]
     tokens_grad = share_in_ctx(tokens_grad_own, tokens_grad_beside, y, core)
     result_own, result_beside, _ = lax.optimization_barrier(
-        (result_own, result_beside, tokens_grad_own)
+        (result_own, result_beside, tokens_grad_beside)
     )
     result = share_in_ctx(result_own, result_beside, y, core)
 
-    attn_late = after(attn_reduced, tokens_grad_beside)
+    attn_late = after(attn_reduced, tokens_grad)
 
     def gain_part(pairs):
         return sum(jnp.sum(mine.astype(F32) * grad.astype(F32), axis=1) for mine, grad in pairs)
@@ -788,9 +798,7 @@
             axis=1,
         )
 
-    attn_low, attn_high = both_halves(
-        attn_reduced, swap_x(after(attn_reduced, *other_reduced[1:])), ctx
-    )
+    attn_low, attn_high = both_halves(attn_reduced, swap_x(attn_reduced), ctx)
 
     def attn_out(begin, end):
         return jnp.concatenate([attn_low[:, begin:end], attn_high[:, begin:end]], axis=1)

time: 694 us -> 681 us (0.981)
  waiting for transfers between devices: 249 us -> 226 us
  starting transfers between devices: 44.7 us -> 55.6 us
    ppermute x5, waiting for transfers between devices: 56.9 us -> 24.1 us  [swap_x(): return lax.ppermute(v, 'ctx', PAIR)]
    ppermute x5, waiting for transfers between devices: 11.3 us -> 35.5 us  [swap_y(): return lax.ppermute(v, 'tp', ACROSS)]
    ppermute x13, waiting for transfers between devices: 81.9 us -> 100 us  [swap_second(): return lax.ppermute(v, ('ctx', 'tp'), SECOND)]
    ppermute x7, waiting for transfers between devices: 41.6 us -> 24.3 us  [swap_first(): return lax.ppermute(v, ('ctx', 'tp'), FIRST)]
    all_gather x2, waiting for transfers between devices: 18.6 us -> 6.24 us  [shards(): lax.all_gather(shard, 'fsdp', axis=0, tiled=True)]
    reduce_scatter x1, starting transfers between devices: 0.21 us -> 12.3 us  [shards(): lax.psum_scatter(attn_grad, 'fsdp', scatter_dimension=0, tiled=True)]
    pallas_call x11 -> x12, Pallas kernels: 75.5 us -> 78.6 us  [back_product(): pl.pallas_call(functools.partial(back_kernel, len(terms)), out_shape=jax....]
  transfers between devices with their start and end apart: 66 -> 66, of which waited for: 27 -> 29; matrix products, arithmetic and copies ran while one was open for 15% -> 16% of each run, Pallas kernels for 37% -> 38%
where the time goes in v7:
time: 681 us; the launch traced here: 672 us
  Pallas kernels  256 us (38%)
  waiting for transfers between devices  226 us (33%)
  other arithmetic  83.4 us (12%)
  starting transfers between devices  55.6 us (8%)
  local copies, waits for them, and re-layouts  35.2 us (5%)
  between operations  15.1 us (2%)
    ppermute x13, waiting for transfers between devices, swap_second(): return lax.ppermute(v, ('ctx', 'tp'), SECOND)  100 us
    pallas_call x12, Pallas kernels, back_product(): pl.pallas_call(functools.partial(back_kernel, len(terms)), out_shape=jax....  78.6 us
    pallas_call x3, Pallas kernels, weight_grads(): pl.pallas_call(functools.partial(grads_kernel, len(x), len(y)), out_shape...  51.4 us
    pallas_call x2, Pallas kernels, ffn_chunk(): pl.pallas_call(functools.partial(ffn_kernel, len(x)), out_shape=jax.Shape...  43.5 us
    ppermute x5, waiting for transfers between devices, swap_y(): return lax.ppermute(v, 'tp', ACROSS)  35.5 us
    pallas_call x1, Pallas kernels, attend_back(): pl.pallas_call(attend_back_kernel, out_shape=jax.ShapeDtypeStruct((rows,...  35.2 us
    ppermute x3, waiting for transfers between devices, ring_over(): pieces.append(lax.ppermute(sent, 'fsdp', cycle))  26.6 us
    ppermute x7, waiting for transfers between devices, swap_first(): return lax.ppermute(v, ('ctx', 'tp'), FIRST)  24.3 us
  transfers between devices with their start and end apart: 66, of which 29 were waited for; matrix products, arithmetic and copies ran while one was open for 16% of the time, Pallas kernels for 38%

profile of v7, /device:TPU:0, one launch (start us, length us, event | category | flops | bytes accessed | tf_op | source)
XLA Modules:
  0.0 671.6 jit_solution(11295172580704017017)
XLA Ops:
  21.8 5.6 negate_select_fusion
  27.4 4.7 collective-permute-done
  35.9 14.4 %collective-permute-done.2 = bf16[528,640]{1,0:T(8,128)(2,1)} collective-permute-done((bf16[528,640]{1,0:T(8,128)(2,1)S(1)}, bf16[528,640]{1,0:T(8,128)(2,1)}, u32[]{:S(2)}, u32[]{:S(2)}) %collective-permute-start.2) | collective-permute-done | bytes 675872 | tf_op jit(solution)/shard_map/ppermute | solution.py:534
  55.3 4.8 collective-permute-done.5.refs_3_
  60.2 7.4 %collective-permute-done.3 = bf16[528,640]{1,0:T(8,128)(2,1)} collective-permute-done((bf16[528,640]{1,0:T(8,128)(2,1)}, bf16[528,640]{1,0:T(8,128)(2,1)}, u32[]{:S(2)}, u32[]{:S(2)}) %collective-permute-start.3) | collective-permute-done | bytes 675872 | tf_op jit(solution)/shard_map/ppermute | solution.py:534
  77.7 15.3 %qkv.1.q_ref.kv_ref.refs_8_ = bf16[2048,2432]{1,0:T(8,128)(2,1)} custom-call(bf16[256,2048]{1,0:T(8,128)(2,1)} %constant_dynamic-slice_fusion.11.refs_0_, bf16[256,2048]{1,0:T(8,128)(2,1)} %collective-permute-done.1.refs_1_, bf16[256,2048]{1,0:T(8,128)(2,1)} %collective-permute-done.4.refs_2_, bf16[256,2048]{1,0:T(8,128)(2,1)} %collective-permute-done.5.refs_3_, ...), custom_call_target="tpu_custom_call" | custom-call | flops 1 | bytes 1 | tf_op jit(solution)/shard_map/qkv/pallas_call | solution.py:141
  93.1 7.7 %collective-permute-done.11.refs_10_ = bf16[256,2048]{1,0:T(8,128)(2,1)S(1)} collective-permute-done((bf16[256,2048]{1,0:T(8,128)(2,1)S(1)}, bf16[256,2048]{1,0:T(8,128)(2,1)S(1)}, u32[]{:S(2)}, u32[]{:S(2)}) %collective-permute-start.11) | collective-permute-done | bytes 1048608 | tf_op jit(solution)/shard_map/ppermute | solution.py:58
  103.8 22.7 %attend.1.refs_0_.h_ref.refs_9_ = f32[2048,384]{1,0:T(8,128)} custom-call(s32[8]{0:T(128)} %select_reduce_fusion.2.place, s32[8]{0:T(128)} %and_select_fusion.2.first, bf16[2048,2432]{1,0:T(8,128)(2,1)} %qkv.1.q_ref.kv_ref.refs_8_, bf16[2048,2432]{1,0:T(8,128)(2,1)} %qkv.1.q_ref.kv_ref.refs_8_, s32[2048,1]{1,0:T(8,128)} %copy.28.start_ref), custom_call_target="tpu_custom_call" | custom-call | flops 1 | bytes 1 | tf_op jit(solution)/shard_map/attend/pallas_call | solution.py:358
  129.5 3.8 back.14
  133.5 3.5 back.13
  138.9 4.2 back.12
  147.0 13.4 %collective-permute-done.19 = bf16[256,2048]{1,0:T(8,128)(2,1)S(1)} collective-permute-done((bf16[256,2048]{1,0:T(8,128)(2,1)S(1)}, bf16[256,2048]{1,0:T(8,128)(2,1)S(1)}, u32[]{:S(2)}, u32[]{:S(2)}) %collective-permute-start.19) | collective-permute-done | bytes 1048608 | tf_op jit(solution)/shard_map/ppermute | solution.py:58
  164.2 23.7 %collective-permute-done.21 = bf16[256,2048]{1,0:T(8,128)(2,1)S(1)} collective-permute-done((bf16[256,2048]{1,0:T(8,128)(2,1)S(1)}, bf16[256,2048]{1,0:T(8,128)(2,1)S(1)}, u32[]{:S(2)}, u32[]{:S(2)}) %collective-permute-start.21) | collective-permute-done | bytes 1048608 | tf_op jit(solution)/shard_map/ppermute | solution.py:54
  187.9 3.5 multiply_reduce_fusion.3
  193.7 23.1 %collective-permute-done.23.refs_2_ = bf16[256,2048]{1,0:T(8,128)(2,1)S(1)} collective-permute-done((bf16[256,2048]{1,0:T(8,128)(2,1)S(1)}, bf16[256,2048]{1,0:T(8,128)(2,1)S(1)}, u32[]{:S(2)}, u32[]{:S(2)}) %collective-permute-start.23) | collective-permute-done | bytes 1048608 | tf_op jit(solution)/shard_map/ppermute | solution.py:58
  221.0 11.1 %collective-permute-done.24.refs_3_ = bf16[256,2048]{1,0:T(8,128)(2,1)S(1)} collective-permute-done((bf16[256,2048]{1,0:T(8,128)(2,1)S(1)}, bf16[256,2048]{1,0:T(8,128)(2,1)S(1)}, u32[]{:S(2)}, u32[]{:S(2)}) %collective-permute-start.24) | collective-permute-done | bytes 1048608 | tf_op jit(solution)/shard_map/ppermute | solution.py:58
  235.0 21.8 %ffn.2.refs_16_.refs_17_.refs_0_ = bf16[2048,1536]{1,0:T(8,128)(2,1)} custom-call(bf16[256,2048]{1,0:T(8,128)(2,1)} %copy-done.2, bf16[256,2048]{1,0:T(8,128)(2,1)} %copy-done.18, bf16[256,2048]{1,0:T(8,128)(2,1)} %copy-done.17, bf16[256,2048]{1,0:T(8,128)(2,1)} %copy-done.24, bf16[256,2048]{1,0:T(8,128)(2,1)} %copy-done.20, bf16[256,2048]{1,0:T(8,128)(2,1)} %copy-done.23, ...), custom_call_target="tpu_custom_call" | custom-call | flops 1 | bytes 1 | tf_op jit(solution)/shard_map/ffn/pallas_call | solution.py:180
  256.8 19.3 %weight_grads.3 = bf16[2048,1536]{1,0:T(8,128)(2,1)} custom-call(bf16[256,2048]{1,0:T(8,128)(2,1)} %copy-done.2, bf16[256,2048]{1,0:T(8,128)(2,1)} %copy-done.18, bf16[256,2048]{1,0:T(8,128)(2,1)} %copy-done.17, bf16[256,2048]{1,0:T(8,128)(2,1)} %copy-done.24, bf16[256,2048]{1,0:T(8,128)(2,1)} %copy-done.20, bf16[256,2048]{1,0:T(8,128)(2,1)} %copy-done.23, ...), custom_call_target="tpu_custom_call" | custom-call | flops 20000000000 | bytes 1 | tf_op jit(solution)/shard_map/weight_grads/pallas_call | solution.py:216
  276.5 13.4 %back.15.refs_2_ = bf16[2048,2048]{1,0:T(8,128)(2,1)} custom-call(bf16[2048,1536]{1,0:T(8,128)(2,1)} %ffn.2.refs_16_.refs_17_.refs_0_, bf16[2048,1536]{1,0:T(8,128)(2,1)} %all-gather.3.cloned.1.call-done.refs_16_.refs_1_.refs_2_), custom_call_target="tpu_custom_call" | custom-call | flops 1 | bytes 1 | tf_op jit(solution)/shard_map/back/pallas_call | solution.py:251
  289.8 6.2 all-gather.5.cloned.1.call-done.refs_16_.refs_1_.refs_3_
  296.1 21.8 %ffn.3.refs_0_.refs_16_.refs_17_.refs_1_ = bf16[2048,1536]{1,0:T(8,128)(2,1)} custom-call(bf16[256,2048]{1,0:T(8,128)(2,1)} %copy-done.2, bf16[256,2048]{1,0:T(8,128)(2,1)} %copy-done.18, bf16[256,2048]{1,0:T(8,128)(2,1)} %copy-done.17, bf16[256,2048]{1,0:T(8,128)(2,1)} %copy-done.24, bf16[256,2048]{1,0:T(8,128)(2,1)} %copy-done.20, ...), custom_call_target="tpu_custom_call" | custom-call | flops 1 | bytes 1 | tf_op jit(solution)/shard_map/ffn/pallas_call | solution.py:180
  317.8 9.3 %back.17 = bf16[1024,2048]{1,0:T(8,128)(2,1)} custom-call(bf16[2048,1536]{1,0:T(8,128)(2,1)} %ffn.3.refs_0_.refs_16_.refs_17_.refs_1_, bf16[2048,1536]{1,0:T(8,128)(2,1)} %all-gather.5.cloned.1.call-done.refs_16_.refs_1_.refs_3_, bf16[2048,2048]{1,0:T(8,128)(2,1)} %back.15.refs_2_), custom_call_target="tpu_custom_call" | custom-call | flops 1 | bytes 1 | tf_op jit(solution)/shard_map/back/pallas_call | solution.py:251
  327.2 9.6 %back.16 = bf16[1024,2048]{1,0:T(8,128)(2,1)} custom-call(bf16[2048,1536]{1,0:T(8,128)(2,1)} %ffn.3.refs_0_.refs_16_.refs_17_.refs_1_, bf16[2048,1536]{1,0:T(8,128)(2,1)} %all-gather.5.cloned.1.call-done.refs_16_.refs_1_.refs_3_, bf16[2048,2048]{1,0:T(8,128)(2,1)} %back.15.refs_2_), custom_call_target="tpu_custom_call" | custom-call | flops 1 | bytes 1 | tf_op jit(solution)/shard_map/back/pallas_call | solution.py:251
  336.8 4.6 slice_add_fusion
  343.0 19.4 %weight_grads.4 = bf16[2048,1536]{1,0:T(8,128)(2,1)} custom-call(bf16[256,2048]{1,0:T(8,128)(2,1)} %copy-done.2, bf16[256,2048]{1,0:T(8,128)(2,1)} %copy-done.18, bf16[256,2048]{1,0:T(8,128)(2,1)} %copy-done.17, bf16[256,2048]{1,0:T(8,128)(2,1)} %copy-done.24, bf16[256,2048]{1,0:T(8,128)(2,1)} %copy-done.20, bf16[256,2048]{1,0:T(8,128)(2,1)} %copy-done.23, ...), custom_call_target="tpu_custom_call" | custom-call | flops 20000000000 | bytes 1 | tf_op jit(solution)/shard_map/weight_grads/pallas_call | solution.py:216
  362.4 12.3 %reduce-scatter.8.cloned.1.call-start = ((), (), s32[]{:S(2)}) async-start(), calls=%async_computation.7 | async-start | bytes 3276800 | tf_op jit(solution)/shard_map/reduce_scatter | solution.py:757
  374.8 3.2 fusion.8
  379.6 6.3 back.20
  385.8 6.3 back.18
  393.4 3.3 fusion.25
  398.6 8.7 %back.19 = bf16[1024,2048]{1,0:T(8,128)(2,1)} custom-call(bf16[2048,1536]{1,0:T(8,128)(2,1)} %ffn.2.refs_16_.refs_17_.refs_0_, bf16[2048,1536]{1,0:T(8,128)(2,1)} %ffn.3.refs_0_.refs_16_.refs_17_.refs_1_, bf16[2048,1536]{1,0:T(8,128)(2,1)} %all-gather.3.cloned.1.call-done.refs_16_.refs_1_.refs_2_, ...), custom_call_target="tpu_custom_call" | custom-call | flops 1 | bytes 1 | tf_op jit(solution)/shard_map/back/pallas_call | solution.py:251
  407.3 5.1 broadcast_select_fusion
  412.5 9.4 %collective-permute-done.33.refs_2_ = bf16[256,2048]{1,0:T(8,128)(2,1)} collective-permute-done((bf16[256,2048]{1,0:T(8,128)(2,1)S(1)}, bf16[256,2048]{1,0:T(8,128)(2,1)}, u32[]{:S(2)}, u32[]{:S(2)}) %collective-permute-start.33) | collective-permute-done | bytes 1048608 | tf_op jit(solution)/shard_map/ppermute | solution.py:58
  427.2 10.3 %collective-permute-done.38.refs_3_ = bf16[256,2048]{1,0:T(8,128)(2,1)} collective-permute-done((bf16[256,2048]{1,0:T(8,128)(2,1)}, bf16[256,2048]{1,0:T(8,128)(2,1)}, u32[]{:S(2)}, u32[]{:S(2)}) %collective-permute-start.38) | collective-permute-done | bytes 1048608 | tf_op jit(solution)/shard_map/ppermute | solution.py:58
  442.9 9.6 %front.1.d_ref = bf16[2048,256]{1,0:T(8,128)(2,1)} custom-call(bf16[256,2048]{1,0:T(8,128)(2,1)} %copy-done.16, bf16[256,2048]{1,0:T(8,128)(2,1)} %collective-permute-done.32.refs_1_, bf16[256,2048]{1,0:T(8,128)(2,1)} %collective-permute-done.33.refs_2_, bf16[256,2048]{1,0:T(8,128)(2,1)} %collective-permute-done.38.refs_3_, bf16[256,2048]{1,0:T(8,128)(2,1)} %copy-done.43, ...), custom_call_target="tpu_custom_call" | custom-call | flops 1 | bytes 1 | tf_op jit(solution)/shard_map/front/pallas_call | solution.py:277
  452.5 35.2 %attend_back.1.refs_0_.refs_1_.refs_10_ = bf16[2048,384]{1,0:T(8,128)(2,1)} custom-call(s32[8]{0:T(128)} %select_reduce_fusion.2.place, s32[8]{0:T(128)} %and_select_fusion.2.first, bf16[2048,2432]{1,0:T(8,128)(2,1)} %qkv.1.q_ref.kv_ref.refs_8_, bf16[2048,256]{1,0:T(8,128)(2,1)} %front.1.d_ref, f32[2048,384]{1,0:T(8,128)} %attend.1.refs_0_.h_ref.refs_9_, ...), custom_call_target="tpu_custom_call" | custom-call | flops 1 | bytes 1 | tf_op jit(solution)/shard_map/attend_back/pallas_call | solution.py:455
  491.8 4.1 back.22
  496.0 4.1 back.23
  500.1 5.4 back.21
  510.3 12.7 %weight_grads.5 = bf16[2048,640]{1,0:T(8,128)(2,1)} custom-call(bf16[256,2048]{1,0:T(8,128)(2,1)} %copy-done.16, bf16[256,2048]{1,0:T(8,128)(2,1)} %collective-permute-done.32.refs_1_, bf16[256,2048]{1,0:T(8,128)(2,1)} %collective-permute-done.33.refs_2_, bf16[256,2048]{1,0:T(8,128)(2,1)} %collective-permute-done.38.refs_3_, bf16[256,2048]{1,0:T(8,128)(2,1)} %copy-done.43, ...), custom_call_target="tpu_custom_call" | custom-call | flops 20000000000 | bytes 1 | tf_op jit(solution)/shard_map/weight_grads/pallas_call | solution.py:216
  523.0 8.8 %collective-permute-done.44 = bf16[256,2048]{1,0:T(8,128)(2,1)} collective-permute-done((bf16[256,2048]{1,0:T(8,128)(2,1)}, bf16[256,2048]{1,0:T(8,128)(2,1)}, u32[]{:S(2)}, u32[]{:S(2)}) %collective-permute-start.44) | collective-permute-done | bytes 1048608 | tf_op jit(solution)/shard_map/ppermute | solution.py:50
  535.6 3.2 fusion.10
  540.5 20.4 %collective-permute-done.46 = bf16[256,2048]{1,0:T(8,128)(2,1)} collective-permute-done((bf16[256,2048]{1,0:T(8,128)(2,1)}, bf16[256,2048]{1,0:T(8,128)(2,1)}, u32[]{:S(2)}, u32[]{:S(2)}) %collective-permute-start.46) | collective-permute-done | bytes 1048608 | tf_op jit(solution)/shard_map/ppermute | solution.py:46
  560.9 20.4 %collective-permute-done.49 = bf16[256,2048]{1,0:T(8,128)(2,1)} collective-permute-done((bf16[256,2048]{1,0:T(8,128)(2,1)}, bf16[256,2048]{1,0:T(8,128)(2,1)}, u32[]{:S(2)}, u32[]{:S(2)}) %collective-permute-start.49) | collective-permute-done | bytes 1048608 | tf_op jit(solution)/shard_map/ppermute | solution.py:58
  581.4 3.6 fusion.2
  585.0 4.5 fusion.6
  599.5 13.5 %collective-permute-done.51 = bf16[256,2048]{1,0:T(8,128)(2,1)} collective-permute-done((bf16[256,2048]{1,0:T(8,128)(2,1)}, bf16[256,2048]{1,0:T(8,128)(2,1)}, u32[]{:S(2)}, u32[]{:S(2)}) %collective-permute-start.51) | collective-permute-done | bytes 1048608 | tf_op jit(solution)/shard_map/ppermute | solution.py:46
  613.0 15.3 %collective-permute-done.52 = bf16[512,1536]{1,0:T(8,128)(2,1)} collective-permute-done((bf16[512,1536]{1,0:T(8,128)(2,1)}, bf16[512,1536]{1,0:T(8,128)(2,1)}, u32[]{:S(2)}, u32[]{:S(2)}) %collective-permute-start.52) | collective-permute-done | bytes 1572896 | tf_op jit(solution)/shard_map/ppermute | solution.py:50
  (328 shorter events, 136.4 us)
Async XLA Ops:
  7.2 180.8 %all-gather.3.cloned.1.call-start = ((), (), s32[]{:S(2)}) async-start(), calls=%async_computation.3 | async-start | bytes 7864320 | tf_op jit(solution)/shard_map/all_gather | solution.py:685
  11.8 20.3 %collective-permute-start = (bf16[528,640]{1,0:T(8,128)(2,1)S(1)}, bf16[528,640]{1,0:T(8,128)(2,1)S(1)}, u32[]{:S(2)}, u32[]{:S(2)}) collective-permute-start(bf16[528,640]{1,0:T(8,128)(2,1)S(1)} %fusion.12), channel_id=1, source_target_pairs={{0,8},{8,16},{16,24},{24,0},{1,9},{9,17},{17,25},{25,1},{2,10},{10... | collective-permute-start | bytes 2027528 | tf_op jit(solution)/shard_map/ppermute | solution.py:534
  17.1 15.1 %collective-permute-start.1 = (bf16[256,2048]{1,0:T(8,128)(2,1)}, bf16[256,2048]{1,0:T(8,128)(2,1)}, u32[]{:S(2)}, u32[]{:S(2)}) collective-permute-start(bf16[256,2048]{1,0:T(8,128)(2,1)} %constant_dynamic-slice_fusion.11.refs_0_), channel_id=1, source_target_pairs={{0,4},{1,3},{2,6},{3,1},{4,0},{5,7},{6,2},{7,5},{8,12},{9,11},{10,... | collective-permute-start | bytes 3145736 | tf_op jit(solution)/shard_map/ppermute | solution.py:54
  32.3 18.0 %collective-permute-start.2 = (bf16[528,640]{1,0:T(8,128)(2,1)S(1)}, bf16[528,640]{1,0:T(8,128)(2,1)}, u32[]{:S(2)}, u32[]{:S(2)}) collective-permute-start(bf16[528,640]{1,0:T(8,128)(2,1)S(1)} %collective-permute-done), channel_id=1, source_target_pairs={{0,8},{8,16},{16,24},{24,0},{1,9},{9,17},{17,25},{25,1},{2,10},{10... | collective-permute-start | bytes 2027528 | tf_op jit(solution)/shard_map/ppermute | solution.py:534
  33.8 21.5 %collective-permute-start.4 = (bf16[256,2048]{1,0:T(8,128)(2,1)}, bf16[256,2048]{1,0:T(8,128)(2,1)}, u32[]{:S(2)}, u32[]{:S(2)}) collective-permute-start(bf16[256,2048]{1,0:T(8,128)(2,1)} %constant_dynamic-slice_fusion.11.refs_0_), channel_id=1, source_target_pairs={{0,2},{1,5},{2,0},{3,7},{4,6},{5,1},{6,4},{7,3},{8,10},{9,13},{10,... | collective-permute-start | bytes 3145736 | tf_op jit(solution)/shard_map/ppermute | solution.py:58
  35.4 24.8 %collective-permute-start.5 = (bf16[256,2048]{1,0:T(8,128)(2,1)}, bf16[256,2048]{1,0:T(8,128)(2,1)}, u32[]{:S(2)}, u32[]{:S(2)}) collective-permute-start(bf16[256,2048]{1,0:T(8,128)(2,1)} %collective-permute-done.1.refs_1_), channel_id=1, source_target_pairs={{0,2},{1,5},{2,0},{3,7},{4,6},{5,1},{6,4},{7,3},{8,10},{9,13},{10,... | collective-permute-start | bytes 3145736 | tf_op jit(solution)/shard_map/ppermute | solution.py:58
  50.3 17.3 %collective-permute-start.3 = (bf16[528,640]{1,0:T(8,128)(2,1)}, bf16[528,640]{1,0:T(8,128)(2,1)}, u32[]{:S(2)}, u32[]{:S(2)}) collective-permute-start(bf16[528,640]{1,0:T(8,128)(2,1)} %collective-permute-done.2), channel_id=1, source_target_pairs={{0,8},{8,16},{16,24},{24,0},{1,9},{9,17},{17,25},{25,1},{2,10},{10... | collective-permute-start | bytes 2027528 | tf_op jit(solution)/shard_map/ppermute | solution.py:534
  67.7 228.4 %all-gather.5.cloned.1.call-start = ((), (), s32[]{:S(2)}) async-start(), calls=%async_computation.4 | async-start | bytes 7864320 | tf_op jit(solution)/shard_map/all_gather | solution.py:685
  75.2 25.6 %collective-permute-start.11 = (bf16[256,2048]{1,0:T(8,128)(2,1)S(1)}, bf16[256,2048]{1,0:T(8,128)(2,1)S(1)}, u32[]{:S(2)}, u32[]{:S(2)}) collective-permute-start(bf16[256,2048]{1,0:T(8,128)(2,1)S(1)} %constant_dynamic-slice_fusion.6.refs_8_), channel_id=1, source_target_pairs={{0,2},{1,5},{2,0},{3,7},{4,6},{5,1},{6,4},{7,3},{8,10},{9,13},{10,... | collective-permute-start | bytes 3145736 | tf_op jit(solution)/shard_map/ppermute | solution.py:58
  76.6 24.2 %collective-permute-start.10 = (bf16[256,2048]{1,0:T(8,128)(2,1)S(1)}, bf16[256,2048]{1,0:T(8,128)(2,1)}, u32[]{:S(2)}, u32[]{:S(2)}) collective-permute-start(bf16[256,2048]{1,0:T(8,128)(2,1)S(1)} %constant_dynamic-slice_fusion.6.refs_8_), channel_id=1, source_target_pairs={{0,4},{1,3},{2,6},{3,1},{4,0},{5,7},{6,2},{7,5},{8,12},{9,11},{10,... | collective-permute-start | bytes 3145736 | tf_op jit(solution)/shard_map/ppermute | solution.py:54
  77.7 48.8 %collective-permute-start.13 = (bf16[256,2048]{1,0:T(8,128)(2,1)S(1)}, bf16[256,2048]{1,0:T(8,128)(2,1)}, u32[]{:S(2)}, u32[]{:S(2)}) collective-permute-start(bf16[256,2048]{1,0:T(8,128)(2,1)S(1)} %constant_dynamic-slice_fusion.6.refs_8_), channel_id=1, source_target_pairs={{0,1},{1,0},{2,3},{3,2},{4,5},{5,4},{6,7},{7,6},{8,9},{9,8},{10,11... | collective-permute-start | bytes 3145736 | tf_op jit(solution)/shard_map/ppermute | solution.py:42
  100.8 25.7 %collective-permute-start.15 = (bf16[256,2048]{1,0:T(8,128)(2,1)S(1)}, bf16[256,2048]{1,0:T(8,128)(2,1)}, u32[]{:S(2)}, u32[]{:S(2)}) collective-permute-start(bf16[256,2048]{1,0:T(8,128)(2,1)S(1)} %collective-permute-done.11.refs_10_), channel_id=1, source_target_pairs={{0,1},{1,0},{2,3},{3,2},{4,5},{5,4},{6,7},{7,6},{8,9},{9,8},{10,11... | collective-permute-start | bytes 3145736 | tf_op jit(solution)/shard_map/ppermute | solution.py:42
  101.4 25.1 %collective-permute-start.14 = (bf16[256,2048]{1,0:T(8,128)(2,1)}, bf16[256,2048]{1,0:T(8,128)(2,1)}, u32[]{:S(2)}, u32[]{:S(2)}) collective-permute-start(bf16[256,2048]{1,0:T(8,128)(2,1)} %collective-permute-done.10.refs_9_), channel_id=1, source_target_pairs={{0,1},{1,0},{2,3},{3,2},{4,5},{5,4},{6,7},{7,6},{8,9},{9,8},{10,11... | collective-permute-start | bytes 3145736 | tf_op jit(solution)/shard_map/ppermute | solution.py:42
  101.4 25.1 %collective-permute-start.12 = (bf16[256,2048]{1,0:T(8,128)(2,1)}, bf16[256,2048]{1,0:T(8,128)(2,1)}, u32[]{:S(2)}, u32[]{:S(2)}) collective-permute-start(bf16[256,2048]{1,0:T(8,128)(2,1)} %collective-permute-done.10.refs_9_), channel_id=1, source_target_pairs={{0,2},{1,5},{2,0},{3,7},{4,6},{5,1},{6,4},{7,3},{8,10},{9,13},{10,... | collective-permute-start | bytes 3145736 | tf_op jit(solution)/shard_map/ppermute | solution.py:58
  137.0 23.4 %collective-permute-start.17 = (bf16[512,2048]{1,0:T(8,128)(2,1)}, bf16[512,2048]{1,0:T(8,128)(2,1)}, u32[]{:S(2)}, u32[]{:S(2)}) collective-permute-start(bf16[512,2048]{1,0:T(8,128)(2,1)} %back.13), channel_id=1, source_target_pairs={{0,1},{1,0},{2,3},{3,2},{4,5},{5,4},{6,7},{7,6},{8,9},{9,8},{10,11... | collective-permute-start | bytes 6291464 | tf_op jit(solution)/shard_map/ppermute | solution.py:42
  138.6 298.9 %reduce-scatter.4.cloned.1.call-start = ((), (), s32[]{:S(2)}) async-start(), calls=%async_computation.5 | async-start | bytes 7864320 | tf_op jit(solution)/shard_map/reduce_scatter | solution.py:717
  145.5 14.9 %collective-permute-start.19 = (bf16[256,2048]{1,0:T(8,128)(2,1)S(1)}, bf16[256,2048]{1,0:T(8,128)(2,1)S(1)}, u32[]{:S(2)}, u32[]{:S(2)}) collective-permute-start(bf16[256,2048]{1,0:T(8,128)(2,1)S(1)} %get-tuple-element.144), channel_id=1, source_target_pairs={{0,2},{1,5},{2,0},{3,7},{4,6},{5,1},{6,4},{7,3},{8,10},{9,13},{10,... | collective-permute-start | bytes 3145736 | tf_op jit(solution)/shard_map/ppermute | solution.py:58
  162.1 25.8 %collective-permute-start.21 = (bf16[256,2048]{1,0:T(8,128)(2,1)S(1)}, bf16[256,2048]{1,0:T(8,128)(2,1)S(1)}, u32[]{:S(2)}, u32[]{:S(2)}) collective-permute-start(bf16[256,2048]{1,0:T(8,128)(2,1)S(1)} %fusion.11), channel_id=1, source_target_pairs={{0,4},{1,3},{2,6},{3,1},{4,0},{5,7},{6,2},{7,5},{8,12},{9,11},{10,... | collective-permute-start | bytes 3145736 | tf_op jit(solution)/shard_map/ppermute | solution.py:54
  163.7 24.3 %collective-permute-start.20 = (bf16[256,2048]{1,0:T(8,128)(2,1)S(1)}, bf16[256,2048]{1,0:T(8,128)(2,1)}, u32[]{:S(2)}, u32[]{:S(2)}) collective-permute-start(bf16[256,2048]{1,0:T(8,128)(2,1)S(1)} %get-tuple-element.86), channel_id=1, source_target_pairs={{0,2},{1,5},{2,0},{3,7},{4,6},{5,1},{6,4},{7,3},{8,10},{9,13},{10,... | collective-permute-start | bytes 3145736 | tf_op jit(solution)/shard_map/ppermute | solution.py:58
  191.7 25.1 %collective-permute-start.23 = (bf16[256,2048]{1,0:T(8,128)(2,1)S(1)}, bf16[256,2048]{1,0:T(8,128)(2,1)S(1)}, u32[]{:S(2)}, u32[]{:S(2)}) collective-permute-start(bf16[256,2048]{1,0:T(8,128)(2,1)S(1)} %multiply_convert_fusion.refs_0_), channel_id=1, source_target_pairs={{0,2},{1,5},{2,0},{3,7},{4,6},{5,1},{6,4},{7,3},{8,10},{9,13},{10,... | collective-permute-start | bytes 3145736 | tf_op jit(solution)/shard_map/ppermute | solution.py:58
  192.3 24.6 %collective-permute-start.22 = (bf16[256,2048]{1,0:T(8,128)(2,1)S(1)}, bf16[256,2048]{1,0:T(8,128)(2,1)S(1)}, u32[]{:S(2)}, u32[]{:S(2)}) collective-permute-start(bf16[256,2048]{1,0:T(8,128)(2,1)S(1)} %multiply_convert_fusion.refs_0_), channel_id=1, source_target_pairs={{0,4},{1,3},{2,6},{3,1},{4,0},{5,7},{6,2},{7,5},{8,12},{9,11},{10,... | collective-permute-start | bytes 3145736 | tf_op jit(solution)/shard_map/ppermute | solution.py:54
  193.7 25.1 %collective-permute-start.25 = (bf16[256,2048]{1,0:T(8,128)(2,1)S(1)}, bf16[256,2048]{1,0:T(8,128)(2,1)S(1)}, u32[]{:S(2)}, u32[]{:S(2)}) collective-permute-start(bf16[256,2048]{1,0:T(8,128)(2,1)S(1)} %multiply_convert_fusion.refs_0_), channel_id=1, source_target_pairs={{0,1},{1,0},{2,3},{3,2},{4,5},{5,4},{6,7},{7,6},{8,9},{9,8},{10,11... | collective-permute-start | bytes 3145736 | tf_op jit(solution)/shard_map/ppermute | solution.py:42
  217.4 14.8 %collective-permute-start.24 = (bf16[256,2048]{1,0:T(8,128)(2,1)S(1)}, bf16[256,2048]{1,0:T(8,128)(2,1)S(1)}, u32[]{:S(2)}, u32[]{:S(2)}) collective-permute-start(bf16[256,2048]{1,0:T(8,128)(2,1)S(1)} %collective-permute-done.22.refs_1_), channel_id=1, source_target_pairs={{0,2},{1,5},{2,0},{3,7},{4,6},{5,1},{6,4},{7,3},{8,10},{9,13},{10,... | collective-permute-start | bytes 3145736 | tf_op jit(solution)/shard_map/ppermute | solution.py:58
  276.1 314.5 %reduce-scatter.6.cloned.1.call-start = ((), (), s32[]{:S(2)}) async-start(), calls=%async_computation.6 | async-start | bytes 7864320 | tf_op jit(solution)/shard_map/reduce_scatter | solution.py:717
  341.4 33.3 %collective-permute-start.30 = (bf16[512,2048]{1,0:T(8,128)(2,1)}, bf16[512,2048]{1,0:T(8,128)(2,1)}, u32[]{:S(2)}, u32[]{:S(2)}) collective-permute-start(bf16[512,2048]{1,0:T(8,128)(2,1)} %slice_add_fusion), channel_id=1, source_target_pairs={{0,2},{1,5},{2,0},{3,7},{4,6},{5,1},{6,4},{7,3},{8,10},{9,13},{10,... | collective-permute-start | bytes 6291464 | tf_op jit(solution)/shard_map/ppermute | solution.py:58
  362.4 235.5 %reduce-scatter.8.cloned.1.call-start = ((), (), s32[]{:S(2)}) async-start(), calls=%async_computation.7 | async-start | bytes 3276800 | tf_op jit(solution)/shard_map/reduce_scatter | solution.py:757
  378.0 14.9 %collective-permute-start.31 = (bf16[256,2048]{1,0:T(8,128)(2,1)S(1)}, bf16[256,2048]{1,0:T(8,128)(2,1)S(1)}, u32[]{:S(2)}, u32[]{:S(2)}) collective-permute-start(bf16[256,2048]{1,0:T(8,128)(2,1)S(1)} %slice.221), channel_id=1, source_target_pairs={{0,4},{1,3},{2,6},{3,1},{4,0},{5,7},{6,2},{7,5},{8,12},{9,11},{10,... | collective-permute-start | bytes 3145736 | tf_op jit(solution)/shard_map/ppermute | solution.py:54
  385.8 21.5 %collective-permute-start.34 = (bf16[512,2048]{1,0:T(8,128)(2,1)}, bf16[512,2048]{1,0:T(8,128)(2,1)}, u32[]{:S(2)}, u32[]{:S(2)}) collective-permute-start(bf16[512,2048]{1,0:T(8,128)(2,1)} %back.20), channel_id=1, source_target_pairs={{0,1},{1,0},{2,3},{3,2},{4,5},{5,4},{6,7},{7,6},{8,9},{9,8},{10,11... | collective-permute-start | bytes 6291464 | tf_op jit(solution)/shard_map/ppermute | solution.py:42
  392.1 15.2 %collective-permute-start.35 = (bf16[512,2048]{1,0:T(8,128)(2,1)}, bf16[512,2048]{1,0:T(8,128)(2,1)}, u32[]{:S(2)}, u32[]{:S(2)}) collective-permute-start(bf16[512,2048]{1,0:T(8,128)(2,1)} %back.18), channel_id=1, source_target_pairs={{0,1},{1,0},{2,3},{3,2},{4,5},{5,4},{6,7},{7,6},{8,9},{9,8},{10,11... | collective-permute-start | bytes 6291464 | tf_op jit(solution)/shard_map/ppermute | solution.py:42
  396.7 25.2 %collective-permute-start.33 = (bf16[256,2048]{1,0:T(8,128)(2,1)S(1)}, bf16[256,2048]{1,0:T(8,128)(2,1)}, u32[]{:S(2)}, u32[]{:S(2)}) collective-permute-start(bf16[256,2048]{1,0:T(8,128)(2,1)S(1)} %get-tuple-element.129.refs_0_), channel_id=1, source_target_pairs={{0,2},{1,5},{2,0},{3,7},{4,6},{5,1},{6,4},{7,3},{8,10},{9,13},{10,... | collective-permute-start | bytes 3145736 | tf_op jit(solution)/shard_map/ppermute | solution.py:58
  397.0 24.8 %collective-permute-start.32 = (bf16[256,2048]{1,0:T(8,128)(2,1)S(1)}, bf16[256,2048]{1,0:T(8,128)(2,1)}, u32[]{:S(2)}, u32[]{:S(2)}) collective-permute-start(bf16[256,2048]{1,0:T(8,128)(2,1)S(1)} %get-tuple-element.129.refs_0_), channel_id=1, source_target_pairs={{0,4},{1,3},{2,6},{3,1},{4,0},{5,7},{6,2},{7,5},{8,12},{9,11},{10,... | collective-permute-start | bytes 3145736 | tf_op jit(solution)/shard_map/ppermute | solution.py:54
  422.4 15.1 %collective-permute-start.38 = (bf16[256,2048]{1,0:T(8,128)(2,1)}, bf16[256,2048]{1,0:T(8,128)(2,1)}, u32[]{:S(2)}, u32[]{:S(2)}) collective-permute-start(bf16[256,2048]{1,0:T(8,128)(2,1)} %collective-permute-done.32.refs_1_), channel_id=1, source_target_pairs={{0,2},{1,5},{2,0},{3,7},{4,6},{5,1},{6,4},{7,3},{8,10},{9,13},{10,... | collective-permute-start | bytes 3145736 | tf_op jit(solution)/shard_map/ppermute | solution.py:58
  437.5 50.2 %collective-permute-start.43 = (bf16[512,1536]{1,0:T(8,128)(2,1)}, bf16[512,1536]{1,0:T(8,128)(2,1)S(1)}, u32[]{:S(2)}, u32[]{:S(2)}) collective-permute-start(bf16[512,1536]{1,0:T(8,128)(2,1)} %reduce-scatter.4.cloned.1.call-done), channel_id=1, source_target_pairs={{0,4},{4,0},{1,5},{5,1},{2,6},{6,2},{3,7},{7,3},{8,12},{12,8},{9,1... | collective-permute-start | bytes 4718600 | tf_op jit(solution)/shard_map/ppermute | solution.py:50
  439.0 48.7 %collective-permute-start.36 = (bf16[256,2048]{1,0:T(8,128)(2,1)}, bf16[256,2048]{1,0:T(8,128)(2,1)S(1)}, u32[]{:S(2)}, u32[]{:S(2)}) collective-permute-start(bf16[256,2048]{1,0:T(8,128)(2,1)} %get-tuple-element.98), channel_id=1, source_target_pairs={{0,2},{2,0},{1,3},{3,1},{4,6},{6,4},{5,7},{7,5},{8,10},{10,8},{9,1... | collective-permute-start | bytes 3145736 | tf_op jit(solution)/shard_map/ppermute | solution.py:46
  440.1 47.6 %collective-permute-start.37 = (bf16[256,2048]{1,0:T(8,128)(2,1)}, bf16[256,2048]{1,0:T(8,128)(2,1)S(1)}, u32[]{:S(2)}, u32[]{:S(2)}) collective-permute-start(bf16[256,2048]{1,0:T(8,128)(2,1)} %get-tuple-element.99), channel_id=1, source_target_pairs={{0,2},{2,0},{1,3},{3,1},{4,6},{6,4},{5,7},{7,5},{8,10},{10,8},{9,1... | collective-permute-start | bytes 3145736 | tf_op jit(solution)/shard_map/ppermute | solution.py:46
  505.5 26.3 %collective-permute-start.44 = (bf16[256,2048]{1,0:T(8,128)(2,1)}, bf16[256,2048]{1,0:T(8,128)(2,1)}, u32[]{:S(2)}, u32[]{:S(2)}) collective-permute-start(bf16[256,2048]{1,0:T(8,128)(2,1)} %add.408), channel_id=1, source_target_pairs={{0,4},{4,0},{1,5},{5,1},{2,6},{6,2},{3,7},{7,3},{8,12},{12,8},{9,1... | collective-permute-start | bytes 3145736 | tf_op jit(solution)/shard_map/ppermute | solution.py:50
  506.1 29.5 %collective-permute-start.47 = (bf16[512,2048]{1,0:T(8,128)(2,1)}, bf16[512,2048]{1,0:T(8,128)(2,1)}, u32[]{:S(2)}, u32[]{:S(2)}) collective-permute-start(bf16[512,2048]{1,0:T(8,128)(2,1)} %back.23), channel_id=1, source_target_pairs={{0,1},{1,0},{2,3},{3,2},{4,5},{5,4},{6,7},{7,6},{8,9},{9,8},{10,11... | collective-permute-start | bytes 6291464 | tf_op jit(solution)/shard_map/ppermute | solution.py:42
  509.2 26.4 %collective-permute-start.48 = (bf16[256,2048]{1,0:T(8,128)(2,1)}, bf16[256,2048]{1,0:T(8,128)(2,1)}, u32[]{:S(2)}, u32[]{:S(2)}) collective-permute-start(bf16[256,2048]{1,0:T(8,128)(2,1)} %get-tuple-element.140), channel_id=1, source_target_pairs={{0,2},{1,5},{2,0},{3,7},{4,6},{5,1},{6,4},{7,3},{8,10},{9,13},{10,... | collective-permute-start | bytes 3145736 | tf_op jit(solution)/shard_map/ppermute | solution.py:58
  534.5 26.4 %collective-permute-start.46 = (bf16[256,2048]{1,0:T(8,128)(2,1)}, bf16[256,2048]{1,0:T(8,128)(2,1)}, u32[]{:S(2)}, u32[]{:S(2)}) collective-permute-start(bf16[256,2048]{1,0:T(8,128)(2,1)} %add_convert_fusion), channel_id=1, source_target_pairs={{0,2},{2,0},{1,3},{3,1},{4,6},{6,4},{5,7},{7,5},{8,10},{10,8},{9,1... | collective-permute-start | bytes 3145736 | tf_op jit(solution)/shard_map/ppermute | solution.py:46
  538.8 22.1 %collective-permute-start.50 = (bf16[256,2048]{1,0:T(8,128)(2,1)}, bf16[256,2048]{1,0:T(8,128)(2,1)}, u32[]{:S(2)}, u32[]{:S(2)}) collective-permute-start(bf16[256,2048]{1,0:T(8,128)(2,1)} %fusion.10), channel_id=1, source_target_pairs={{0,4},{1,3},{2,6},{3,1},{4,0},{5,7},{6,2},{7,5},{8,12},{9,11},{10,... | collective-permute-start | bytes 3145736 | tf_op jit(solution)/shard_map/ppermute | solution.py:54
  539.5 41.9 %collective-permute-start.49 = (bf16[256,2048]{1,0:T(8,128)(2,1)}, bf16[256,2048]{1,0:T(8,128)(2,1)}, u32[]{:S(2)}, u32[]{:S(2)}) collective-permute-start(bf16[256,2048]{1,0:T(8,128)(2,1)} %get-tuple-element.114), channel_id=1, source_target_pairs={{0,2},{1,5},{2,0},{3,7},{4,6},{5,1},{6,4},{7,3},{8,10},{9,13},{10,... | collective-permute-start | bytes 3145736 | tf_op jit(solution)/shard_map/ppermute | solution.py:58
  589.5 23.5 %collective-permute-start.51 = (bf16[256,2048]{1,0:T(8,128)(2,1)}, bf16[256,2048]{1,0:T(8,128)(2,1)}, u32[]{:S(2)}, u32[]{:S(2)}) collective-permute-start(bf16[256,2048]{1,0:T(8,128)(2,1)} %fusion.6), channel_id=1, source_target_pairs={{0,2},{2,0},{1,3},{3,1},{4,6},{6,4},{5,7},{7,5},{8,10},{10,8},{9,1... | collective-permute-start | bytes 3145736 | tf_op jit(solution)/shard_map/ppermute | solution.py:46
  590.6 37.6 %collective-permute-start.52 = (bf16[512,1536]{1,0:T(8,128)(2,1)}, bf16[512,1536]{1,0:T(8,128)(2,1)}, u32[]{:S(2)}, u32[]{:S(2)}) collective-permute-start(bf16[512,1536]{1,0:T(8,128)(2,1)} %reduce-scatter.6.cloned.1.call-done), channel_id=1, source_target_pairs={{0,4},{4,0},{1,5},{5,1},{2,6},{6,2},{3,7},{7,3},{8,12},{12,8},{9,1... | collective-permute-start | bytes 4718600 | tf_op jit(solution)/shard_map/ppermute | solution.py:50
  596.4 50.7 %collective-permute-start.55 = (bf16[256,2048]{1,0:T(8,128)(2,1)}, bf16[256,2048]{1,0:T(8,128)(2,1)}, u32[]{:S(2)}, u32[]{:S(2)}) collective-permute-start(bf16[256,2048]{1,0:T(8,128)(2,1)} %fusion.6), channel_id=1, source_target_pairs={{0,1},{1,0},{2,3},{3,2},{4,5},{5,4},{6,7},{7,6},{8,9},{9,8},{10,11... | collective-permute-start | bytes 3145736 | tf_op jit(solution)/shard_map/ppermute | solution.py:42
  597.9 44.6 %collective-permute-start.57 = (bf16[512,640]{1,0:T(8,128)(2,1)}, bf16[512,640]{1,0:T(8,128)(2,1)S(1)}, u32[]{:S(2)}, u32[]{:S(2)}) collective-permute-start(bf16[512,640]{1,0:T(8,128)(2,1)} %reduce-scatter.8.cloned.1.call-done), channel_id=1, source_target_pairs={{0,4},{4,0},{1,5},{5,1},{2,6},{6,2},{3,7},{7,3},{8,12},{12,8},{9,1... | collective-permute-start | bytes 1966088 | tf_op jit(solution)/shard_map/ppermute | solution.py:50
  628.3 18.8 %collective-permute-start.56 = (bf16[256,2048]{1,0:T(8,128)(2,1)}, bf16[256,2048]{1,0:T(8,128)(2,1)S(1)}, u32[]{:S(2)}, u32[]{:S(2)}) collective-permute-start(bf16[256,2048]{1,0:T(8,128)(2,1)} %collective-permute-done.51), channel_id=1, source_target_pairs={{0,1},{1,0},{2,3},{3,2},{4,5},{5,4},{6,7},{7,6},{8,9},{9,8},{10,11... | collective-permute-start | bytes 3145736 | tf_op jit(solution)/shard_map/ppermute | solution.py:42
  628.3 26.3 %collective-permute-start.53 = (bf16[256,2048]{1,0:T(8,128)(2,1)}, bf16[256,2048]{1,0:T(8,128)(2,1)S(1)}, u32[]{:S(2)}, u32[]{:S(2)}) collective-permute-start(bf16[256,2048]{1,0:T(8,128)(2,1)} %add_convert_fusion), channel_id=1, source_target_pairs={{0,1},{1,0},{2,3},{3,2},{4,5},{5,4},{6,7},{7,6},{8,9},{9,8},{10,11... | collective-permute-start | bytes 3145736 | tf_op jit(solution)/shard_map/ppermute | solution.py:42
  628.8 25.8 %collective-permute-start.54 = (bf16[256,2048]{1,0:T(8,128)(2,1)}, bf16[256,2048]{1,0:T(8,128)(2,1)S(1)}, u32[]{:S(2)}, u32[]{:S(2)}) collective-permute-start(bf16[256,2048]{1,0:T(8,128)(2,1)} %collective-permute-done.46), channel_id=1, source_target_pairs={{0,1},{1,0},{2,3},{3,2},{4,5},{5,4},{6,7},{7,6},{8,9},{9,8},{10,11... | collective-permute-start | bytes 3145736 | tf_op jit(solution)/shard_map/ppermute | solution.py:42
  (77 other events, 836.0 us)
Sparse Core Ops, SparseCore 0:
  67.8 113.0 all-gather.2
  182.5 113.5 all-gather.4
  298.4 108.9 reduce-scatter.3
  409.5 111.2 reduce-scatter.5
  532.0 50.0 reduce-scatter.7

commit v8 on v7

--- a/solution.py
+++ b/solution.py
@@ -79,6 +79,30 @@
     weighted = grad * gain
     inner = jnp.mean(weighted * hidden, axis=-1, keepdims=True)
     return scale * weighted - hidden * (scale * scale * scale) * inner
+
+
+def norm_back_kernel(count, *refs):
+    hidden_ref, gain_ref, kept_ref, o_ref = refs[count:]
+    grad = sum(ref[...].astype(F32) for ref in refs[:count])
+    back = rms_back(hidden_ref[...].astype(F32), gain_ref[...], grad)
+    o_ref[...] = (kept_ref[...].astype(F32) + back).astype(BF16)
+
+
+def norm_back(parts, hidden, gain, kept):
+    rows, depth = hidden.shape
+    step = min(64, rows)
+    block = pl.BlockSpec((step, depth), lambda i: (i, 0))
+    return pl.pallas_call(
+        functools.partial(norm_back_kernel, len(parts)),
+        out_shape=jax.ShapeDtypeStruct((rows, depth), BF16),
+        grid=(rows // step,),
+        in_specs=[block] * (len(parts) + 1)
+        + [pl.BlockSpec((1, depth), lambda i: (0, 0)), block],
+        out_specs=block,
+        compiler_params=params(),
+        cost_estimate=cost(),
+        name="norm_back",
+    )(*parts, hidden, gain, kept)
 
 
 def turn_lanes(u, first):
@@ -243,7 +267,7 @@
     o_ref[...] = total.astype(BF16)
 
 
-def back_product(terms, part=0, parts=1, plus=()):
+def back_product(terms, part=0, parts=1, plus=(), work=0):
     rows = terms[0][0].shape[0] // parts
     depth = terms[0][2].shape[0]
     step = min(512, rows)
@@ -260,7 +284,7 @@
         + [pl.BlockSpec((step, depth), lambda i: (i + ahead, 0))] * len(plus),
         out_specs=pl.BlockSpec((step, depth), lambda i: (i, 0)),
         compiler_params=params(),
-        cost_estimate=cost(),
+        cost_estimate=cost(work),
         name="back",
     )(*[term[0] for term in terms], *[term[2] for term in terms], *plus)
 
@@ -499,9 +523,8 @@
     return (own, *lax.optimization_barrier((along_a, along_b)))
 
 
-def sum_last(own, along_a, along_b, beside=()):
-    from_a = after(swap_first(along_a), *beside)
-    return own.astype(F32) + swap_second(along_b).astype(F32) + from_a.astype(F32)
+def last_parts(own, along_a, along_b, beside=()):
+    return own, swap_second(along_b), after(swap_first(along_a), *beside)
 
 
 def halves_of_cores(terms, plus):
@@ -511,11 +534,12 @@
     return mine[2 * rows :] + arrived[2 * rows :], mine[: 2 * rows] + arrived[: 2 * rows]
 
 
-def sum_wide(far, near, between, beside):
-    rows = near.shape[0] // 2
-    near = after(near + swap_second(far), *between)
-    from_a = after(swap_first(near[rows:]), *beside)
-    return near[:rows].astype(F32) + from_a.astype(F32)
+def wide_first(far, near, between):
+    return after(near + swap_second(far), *between)
+
+
+def wide_last(near, beside):
+    return near, after(swap_first(near[near.shape[0] // 2 :]), *beside)
 
 
 def share_rows(own, beside=()):
@@ -554,12 +578,6 @@
     four = jnp.where(y == 1, four[:, ::-1], four)
     four = jnp.where(core == 1, four[::-1], four)
     return four.transpose(1, 0, 2, 3).reshape(-1, own.shape[1])
-
-
-def sum_all(v):
-    v = v + swap_core(v)
-    v = v + swap_y(v)
-    return v + swap_x(v)
 
 
 def both_halves(own, other, ctx):
@@ -687,7 +705,8 @@
     ]
     heads = after(heads, *cot)
     attn_blocks = sum_cores([(heads, 0, attn_full, 0, q_width)])
-    attn_sum = sum_last(*sum_first(attn_blocks), beside=ffn_full[:1])
+    attn_parts = last_parts(*sum_first(attn_blocks), beside=ffn_full[:1])
+    attn_sum = sum(part.astype(F32) for part in attn_parts)
     hidden = tokens_own + attn_sum
     normed_two = share_rows((hidden * inv_rms(hidden) * gain_two).astype(BF16))
 
@@ -709,16 +728,21 @@
             chunk_grads(part)
             d_norm_partial = (back_product([d_norm_term], plus=d_norm_partial),)
     ffn_terms = [(acts[part], 2, ffn_full[part], 2, chunk) for part, chunk in enumerate(chunks)]
-    ffn_sent = [back_product(ffn_terms, at, 4) for at in (3, 2)]
-    ffn_mine = back_product(ffn_terms, 0, 2)
     d_norm_far, d_norm_near = halves_of_cores([d_norm_term], d_norm_partial)
-    chunk_grads(last)
+    chunk_grads(last, (d_norm_far,))
     reduced = [
         lax.psum_scatter(part, "fsdp", scatter_dimension=0, tiled=True) for part in grad_parts
     ]
-    d_normed_two = sum_wide(d_norm_far, d_norm_near, grad_parts, ffn_sent[:1])
-    d_hidden = cot_own + rms_back(hidden, gain_two, d_normed_two)
-    d_own = d_hidden.astype(BF16)
+    d_norm_near = wide_first(d_norm_far, d_norm_near, grad_parts)
+
+    def ffn_rows(part, parts, held):
+        (act, *rest), *others = ffn_terms
+        return back_product([(after(act, held), *rest), *others], part, parts, work=7)
+
+    ffn_sent = [ffn_rows(3, 4, d_norm_near)]
+    d_own = norm_back(wide_last(d_norm_near, ffn_sent), hidden, gain_two, cot_low)
+    ffn_sent.append(ffn_rows(2, 4, d_own))
+    ffn_mine = ffn_rows(0, 2, d_own)
     ffn_own, ffn_a, ffn_b, ffn_both = add_blocks(ffn_mine, [swap_core(piece) for piece in ffn_sent])
     ffn_x, ffn_y = jnp.where(core == 0, ffn_a, ffn_b), jnp.where(core == 0, ffn_b, ffn_a)
     d_one, d_two, ffn_own, ffn_x, ffn_y, ffn_both = lax.optimization_barrier(
@@ -749,42 +773,34 @@
     result_own = (hidden + (ffn_own.astype(F32) + ffn_far.astype(F32))).astype(BF16)
     result_beside = swap_y(result_own)
     normed_first = sum_first(normed_blocks, [attn_grad, result_own])
-    d_normed = sum_last(*normed_first, beside=[result_beside])
-    tokens_grad_own = (d_hidden + rms_back(tokens_own, gain_one, d_normed)).astype(BF16)
     for part in range(1, len(chunks)):
-        reduced[part] = after(reduced[part], tokens_grad_own)
+        reduced[part] = after(reduced[part], normed_first[1])
         other_reduced.append(swap_x(reduced[part]))
+    normed_parts = last_parts(*normed_first, beside=[result_beside, *other_reduced[1:]])
+    tokens_grad_own = norm_back(normed_parts, tokens_low, gain_one, d_own)
     attn_reduced = lax.psum_scatter(attn_grad, "fsdp", scatter_dimension=0, tiled=True)
     attn_reduced = after(attn_reduced, tokens_grad_own)
-    tokens_grad_beside, other_reduced[1:] = lax.optimization_barrier(
-        (swap_y(tokens_grad_own), other_reduced[1:], attn_reduced)
-    )[:2]
-    tokens_grad = share_in_ctx(tokens_grad_own, tokens_grad_beside, y, core)
+    other_attn = swap_x(attn_reduced)
     result_own, result_beside, _ = lax.optimization_barrier(
-        (result_own, result_beside, tokens_grad_beside)
+        (result_own, result_beside, tokens_grad_own)
     )
     result = share_in_ctx(result_own, result_beside, y, core)
-
-    attn_late = after(attn_reduced, tokens_grad)
 
     def gain_part(pairs):
         return sum(jnp.sum(mine.astype(F32) * grad.astype(F32), axis=1) for mine, grad in pairs)
 
-    gain_sums = sum_all(
-        jnp.stack(
-            [
-                gain_part([(attn_shard[:, q_width:], attn_late[:, q_width:])]),
-                gain_part(
-                    [
-                        (ffn_shards[part][:, : 2 * chunk], reduced[part][:, : 2 * chunk])
-                        for part, chunk in enumerate(chunks)
-                    ]
-                ),
-            ]
-        )
-    )
-    attn_gain_grad = gain_sums[0] / attn_gain.astype(F32)
-    ffn_gain_grad = gain_sums[1] / ffn_gain.astype(F32)
+    gain_sums = jnp.stack(
+        [
+            gain_part([(attn_shard[:, q_width:], attn_reduced[:, q_width:])]),
+            gain_part(
+                [
+                    (ffn_shards[part][:, : 2 * chunk], reduced[part][:, : 2 * chunk])
+                    for part, chunk in enumerate(chunks)
+                ]
+            ),
+        ]
+    )
+    gain_sums = gain_sums + swap_core(gain_sums)
 
     halves = [both_halves(mine, other, ctx) for mine, other in zip(reduced, other_reduced)]
 
@@ -798,7 +814,16 @@
             axis=1,
         )
 
-    attn_low, attn_high = both_halves(attn_reduced, swap_x(attn_reduced), ctx)
+    ffn_grads = [ffn_out(which) for which in range(3)]
+    tokens_grad_beside, gain_sums, other_attn, result, *ffn_grads = lax.optimization_barrier(
+        (swap_y(tokens_grad_own), gain_sums, other_attn, result, *ffn_grads)
+    )
+    tokens_grad = share_in_ctx(tokens_grad_own, tokens_grad_beside, y, core)
+    gain_sums = gain_sums + swap_y(gain_sums)
+    gain_sums = gain_sums + swap_x(gain_sums)
+    attn_gain_grad = gain_sums[0] / attn_gain.astype(F32)
+    ffn_gain_grad = gain_sums[1] / ffn_gain.astype(F32)
+    attn_low, attn_high = both_halves(attn_reduced, other_attn, ctx)
 
     def attn_out(begin, end):
         return jnp.concatenate([attn_low[:, begin:end], attn_high[:, begin:end]], axis=1)
@@ -812,9 +837,7 @@
         attn_out(k_end, k_end + kv_width),
         attn_out(0, q_width),
         attn_gain_grad,
-        ffn_out(0),
-        ffn_out(1),
-        ffn_out(2),
+        *ffn_grads,
         ffn_gain_grad,
     )
 

time: 681 us -> 674 us (0.990)
  Pallas kernels: 256 us -> 266 us
  other arithmetic: 83.4 us -> 76.3 us
    ppermute x13, waiting for transfers between devices: 100 us -> 46.4 us  [swap_second(): return lax.ppermute(v, ('ctx', 'tp'), SECOND)]
    ppermute x7, waiting for transfers between devices: 24.3 us -> 69 us  [swap_first(): return lax.ppermute(v, ('ctx', 'tp'), FIRST)]
    ppermute x5, waiting for transfers between devices: 24.1 us -> 50.7 us  [swap_x(): return lax.ppermute(v, 'ctx', PAIR)]
    ppermute x5, waiting for transfers between devices: 35.5 us -> 15.2 us  [swap_y(): return lax.ppermute(v, 'tp', ACROSS)]
    reduce_scatter x1, starting transfers between devices: 12.3 us -> 0.04 us  [shards(): lax.psum_scatter(attn_grad, 'fsdp', scatter_dimension=0, tiled=True)]
    pallas_call x0 -> x2, Pallas kernels: none -> 9.82 us  [norm_back(): pl.pallas_call(functools.partial(norm_back_kernel, len(parts)), out_shape...]
    convert_element_type x2 -> x1, other arithmetic: 7.82 us -> 0.66 us  [shards(): gain_two = gains[1].astype(F32)[None]]
  transfers between devices with their start and end apart: 66 -> 66, of which waited for: 29 -> 25; matrix products, arithmetic and copies ran while one was open for 16% -> 13% of each run, Pallas kernels for 38% -> 40%
where the time goes in v8:
time: 674 us; the launch traced here: 665 us
  Pallas kernels  266 us (39%)
  waiting for transfers between devices  222 us (33%)
  other arithmetic  76.3 us (11%)
  starting transfers between devices  50.5 us (7%)
  local copies, waits for them, and re-layouts  35.5 us (5%)
  between operations  15.1 us (2%)
    pallas_call x12, Pallas kernels, back_product(): pl.pallas_call(functools.partial(back_kernel, len(terms)), out_shape=jax....  79.1 us
    ppermute x7, waiting for transfers between devices, swap_first(): return lax.ppermute(v, ('ctx', 'tp'), FIRST)  69 us
    pallas_call x3, Pallas kernels, weight_grads(): pl.pallas_call(functools.partial(grads_kernel, len(x), len(y)), out_shape...  51 us
    ppermute x5, waiting for transfers between devices, swap_x(): return lax.ppermute(v, 'ctx', PAIR)  50.7 us
    ppermute x13, waiting for transfers between devices, swap_second(): return lax.ppermute(v, ('ctx', 'tp'), SECOND)  46.4 us
    pallas_call x2, Pallas kernels, ffn_chunk(): pl.pallas_call(functools.partial(ffn_kernel, len(x)), out_shape=jax.Shape...  43.5 us
    pallas_call x1, Pallas kernels, attend_back(): pl.pallas_call(attend_back_kernel, out_shape=jax.ShapeDtypeStruct((rows,...  35 us
    ppermute x3, waiting for transfers between devices, ring_over(): pieces.append(lax.ppermute(sent, 'fsdp', cycle))  30.9 us
  transfers between devices with their start and end apart: 66, of which 25 were waited for; matrix products, arithmetic and copies ran while one was open for 13% of the time, Pallas kernels for 40%

profile of v8, /device:TPU:0, one launch (start us, length us, event | category | flops | bytes accessed | tf_op | source)
XLA Modules:
  0.0 665.4 jit_solution(9757099854105877245)
XLA Ops:
  20.7 5.6 negate_select_fusion
  26.3 5.7 collective-permute-done
  34.6 15.9 %collective-permute-done.2 = bf16[528,640]{1,0:T(8,128)(2,1)} collective-permute-done((bf16[528,640]{1,0:T(8,128)(2,1)}, bf16[528,640]{1,0:T(8,128)(2,1)}, u32[]{:S(2)}, u32[]{:S(2)}) %collective-permute-start.2) | collective-permute-done | bytes 675872 | tf_op jit(solution)/shard_map/ppermute | solution.py:558
  58.7 9.3 %collective-permute-done.3 = bf16[528,640]{1,0:T(8,128)(2,1)} collective-permute-done((bf16[528,640]{1,0:T(8,128)(2,1)}, bf16[528,640]{1,0:T(8,128)(2,1)}, u32[]{:S(2)}, u32[]{:S(2)}) %collective-permute-start.3) | collective-permute-done | bytes 675872 | tf_op jit(solution)/shard_map/ppermute | solution.py:558
  79.8 15.3 %qkv.1.q_ref.kv_ref.refs_8_ = bf16[2048,2432]{1,0:T(8,128)(2,1)} custom-call(bf16[256,2048]{1,0:T(8,128)(2,1)} %copy-done.6, bf16[256,2048]{1,0:T(8,128)(2,1)} %collective-permute-done.1.refs_1_, bf16[256,2048]{1,0:T(8,128)(2,1)} %collective-permute-done.4.refs_2_, bf16[256,2048]{1,0:T(8,128)(2,1)} %collective-permute-done.5.refs_3_, ...), custom_call_target="tpu_custom_call" | custom-call | flops 1 | bytes 1 | tf_op jit(solution)/shard_map/qkv/pallas_call | solution.py:165
  95.2 7.6 %collective-permute-done.10.refs_9_ = bf16[256,2048]{1,0:T(8,128)(2,1)S(1)} collective-permute-done((bf16[256,2048]{1,0:T(8,128)(2,1)S(1)}, bf16[256,2048]{1,0:T(8,128)(2,1)S(1)}, u32[]{:S(2)}, u32[]{:S(2)}) %collective-permute-start.10) | collective-permute-done | bytes 1048608 | tf_op jit(solution)/shard_map/ppermute | solution.py:54
  105.7 22.7 %attend.1.refs_0_.h_ref.refs_9_ = f32[2048,384]{1,0:T(8,128)} custom-call(s32[8]{0:T(128)} %select_reduce_fusion.2.place, s32[8]{0:T(128)} %and_select_fusion.2.first, bf16[2048,2432]{1,0:T(8,128)(2,1)} %qkv.1.q_ref.kv_ref.refs_8_, bf16[2048,2432]{1,0:T(8,128)(2,1)} %qkv.1.q_ref.kv_ref.refs_8_, s32[2048,1]{1,0:T(8,128)} %copy.28.start_ref), custom_call_target="tpu_custom_call" | custom-call | flops 1 | bytes 1 | tf_op jit(solution)/shard_map/attend/pallas_call | solution.py:382
  131.4 3.8 back.14
  135.7 3.5 back.13
  140.8 4.3 back.12
  149.1 13.3 %collective-permute-done.19 = bf16[256,2048]{1,0:T(8,128)(2,1)S(1)} collective-permute-done((bf16[256,2048]{1,0:T(8,128)(2,1)S(1)}, bf16[256,2048]{1,0:T(8,128)(2,1)S(1)}, u32[]{:S(2)}, u32[]{:S(2)}) %collective-permute-start.19) | collective-permute-done | bytes 1048608 | tf_op jit(solution)/shard_map/ppermute | solution.py:58
  165.9 24.0 %collective-permute-done.21 = bf16[256,2048]{1,0:T(8,128)(2,1)} collective-permute-done((bf16[256,2048]{1,0:T(8,128)(2,1)S(1)}, bf16[256,2048]{1,0:T(8,128)(2,1)}, u32[]{:S(2)}, u32[]{:S(2)}) %collective-permute-start.21) | collective-permute-done | bytes 1048608 | tf_op jit(solution)/shard_map/ppermute | solution.py:54
  189.8 3.3 multiply_reduce_fusion.2
  195.5 23.1 %collective-permute-done.22.refs_1_ = bf16[256,2048]{1,0:T(8,128)(2,1)S(1)} collective-permute-done((bf16[256,2048]{1,0:T(8,128)(2,1)S(1)}, bf16[256,2048]{1,0:T(8,128)(2,1)S(1)}, u32[]{:S(2)}, u32[]{:S(2)}) %collective-permute-start.22) | collective-permute-done | bytes 1048608 | tf_op jit(solution)/shard_map/ppermute | solution.py:54
  220.8 12.7 %collective-permute-done.24.refs_3_ = bf16[256,2048]{1,0:T(8,128)(2,1)S(1)} collective-permute-done((bf16[256,2048]{1,0:T(8,128)(2,1)S(1)}, bf16[256,2048]{1,0:T(8,128)(2,1)S(1)}, u32[]{:S(2)}, u32[]{:S(2)}) %collective-permute-start.24) | collective-permute-done | bytes 1048608 | tf_op jit(solution)/shard_map/ppermute | solution.py:58
  237.3 21.8 %ffn.2.refs_16_.refs_17_.refs_0_ = bf16[2048,1536]{1,0:T(8,128)(2,1)} custom-call(bf16[256,2048]{1,0:T(8,128)(2,1)} %copy-done.5, bf16[256,2048]{1,0:T(8,128)(2,1)} %copy-done.21, bf16[256,2048]{1,0:T(8,128)(2,1)} %copy-done.22, bf16[256,2048]{1,0:T(8,128)(2,1)} %copy-done.24, bf16[256,2048]{1,0:T(8,128)(2,1)} %copy-done.23, bf16[256,2048]{1,0:T(8,128)(2,1)} %copy-done.25, ...), custom_call_target="tpu_custom_call" | custom-call | flops 1 | bytes 1 | tf_op jit(solution)/shard_map/ffn/pallas_call | solution.py:204
  259.1 19.4 %weight_grads.3 = bf16[2048,1536]{1,0:T(8,128)(2,1)} custom-call(bf16[256,2048]{1,0:T(8,128)(2,1)} %copy-done.5, bf16[256,2048]{1,0:T(8,128)(2,1)} %copy-done.21, bf16[256,2048]{1,0:T(8,128)(2,1)} %copy-done.22, bf16[256,2048]{1,0:T(8,128)(2,1)} %copy-done.24, bf16[256,2048]{1,0:T(8,128)(2,1)} %copy-done.23, bf16[256,2048]{1,0:T(8,128)(2,1)} %copy-done.25, ...), custom_call_target="tpu_custom_call" | custom-call | flops 20000000000 | bytes 1 | tf_op jit(solution)/shard_map/weight_grads/pallas_call | solution.py:240
  279.0 13.4 %back.15.refs_2_ = bf16[2048,2048]{1,0:T(8,128)(2,1)} custom-call(bf16[2048,1536]{1,0:T(8,128)(2,1)} %ffn.2.refs_16_.refs_17_.refs_0_, bf16[2048,1536]{1,0:T(8,128)(2,1)} %all-gather.3.cloned.1.call-done.refs_16_.refs_1_.refs_2_), custom_call_target="tpu_custom_call" | custom-call | flops 1 | bytes 1 | tf_op jit(solution)/shard_map/back/pallas_call | solution.py:275
  292.4 4.1 all-gather.5.cloned.1.call-done.refs_16_.refs_1_.refs_3_
  296.5 21.7 %ffn.3.refs_0_.refs_16_.refs_17_.refs_1_ = bf16[2048,1536]{1,0:T(8,128)(2,1)} custom-call(bf16[256,2048]{1,0:T(8,128)(2,1)} %copy-done.5, bf16[256,2048]{1,0:T(8,128)(2,1)} %copy-done.21, bf16[256,2048]{1,0:T(8,128)(2,1)} %copy-done.22, bf16[256,2048]{1,0:T(8,128)(2,1)} %copy-done.24, bf16[256,2048]{1,0:T(8,128)(2,1)} %copy-done.23, ...), custom_call_target="tpu_custom_call" | custom-call | flops 1 | bytes 1 | tf_op jit(solution)/shard_map/ffn/pallas_call | solution.py:204
  318.2 9.3 %back.17 = bf16[1024,2048]{1,0:T(8,128)(2,1)} custom-call(bf16[2048,1536]{1,0:T(8,128)(2,1)} %ffn.3.refs_0_.refs_16_.refs_17_.refs_1_, bf16[2048,1536]{1,0:T(8,128)(2,1)} %all-gather.5.cloned.1.call-done.refs_16_.refs_1_.refs_3_, bf16[2048,2048]{1,0:T(8,128)(2,1)} %back.15.refs_2_), custom_call_target="tpu_custom_call" | custom-call | flops 1 | bytes 1 | tf_op jit(solution)/shard_map/back/pallas_call | solution.py:275
  327.6 9.7 %back.16 = bf16[1024,2048]{1,0:T(8,128)(2,1)} custom-call(bf16[2048,1536]{1,0:T(8,128)(2,1)} %ffn.3.refs_0_.refs_16_.refs_17_.refs_1_, bf16[2048,1536]{1,0:T(8,128)(2,1)} %all-gather.5.cloned.1.call-done.refs_16_.refs_1_.refs_3_, bf16[2048,2048]{1,0:T(8,128)(2,1)} %back.15.refs_2_), custom_call_target="tpu_custom_call" | custom-call | flops 1 | bytes 1 | tf_op jit(solution)/shard_map/back/pallas_call | solution.py:275
  337.2 3.3 slice_add_fusion
  342.2 19.2 %weight_grads.4 = bf16[2048,1536]{1,0:T(8,128)(2,1)} custom-call(bf16[256,2048]{1,0:T(8,128)(2,1)} %copy-done.5, bf16[256,2048]{1,0:T(8,128)(2,1)} %copy-done.21, bf16[256,2048]{1,0:T(8,128)(2,1)} %copy-done.22, bf16[256,2048]{1,0:T(8,128)(2,1)} %copy-done.24, bf16[256,2048]{1,0:T(8,128)(2,1)} %copy-done.23, bf16[256,2048]{1,0:T(8,128)(2,1)} %copy-done.25, ...), custom_call_target="tpu_custom_call" | custom-call | flops 20000000000 | bytes 1 | tf_op jit(solution)/shard_map/weight_grads/pallas_call | solution.py:240
  361.5 5.3 collective-permute-done.30
  371.7 6.3 back.18
  378.0 7.0 %collective-permute-done.31.refs_1_ = bf16[256,2048]{1,0:T(8,128)(2,1)S(1)} collective-permute-done((bf16[256,2048]{1,0:T(8,128)(2,1)S(1)}, bf16[256,2048]{1,0:T(8,128)(2,1)S(1)}, u32[]{:S(2)}, u32[]{:S(2)}) %collective-permute-start.31) | collective-permute-done | bytes 1048608 | tf_op jit(solution)/shard_map/ppermute | solution.py:54
  385.9 4.9 norm_back.2.refs_0_.refs_5_
  390.8 6.4 back.20
  400.2 8.7 %back.19 = bf16[1024,2048]{1,0:T(8,128)(2,1)} custom-call(bf16[2048,1536]{1,0:T(8,128)(2,1)} %ffn.2.refs_16_.refs_17_.refs_0_, bf16[2048,1536]{1,0:T(8,128)(2,1)} %ffn.3.refs_0_.refs_16_.refs_17_.refs_1_, bf16[2048,1536]{1,0:T(8,128)(2,1)} %all-gather.3.cloned.1.call-done.refs_16_.refs_1_.refs_2_, ...), custom_call_target="tpu_custom_call" | custom-call | flops 7000000000 | bytes 1 | tf_op jit(solution)/shard_map/back/pallas_call | solution.py:275
  410.2 4.8 broadcast_select_fusion
  415.0 7.4 %collective-permute-done.32.refs_1_ = bf16[256,2048]{1,0:T(8,128)(2,1)S(1)} collective-permute-done((bf16[256,2048]{1,0:T(8,128)(2,1)S(1)}, bf16[256,2048]{1,0:T(8,128)(2,1)S(1)}, u32[]{:S(2)}, u32[]{:S(2)}) %collective-permute-start.32) | collective-permute-done | bytes 1048608 | tf_op jit(solution)/shard_map/ppermute | solution.py:54
  425.1 12.5 %collective-permute-done.38.refs_3_ = bf16[256,2048]{1,0:T(8,128)(2,1)S(1)} collective-permute-done((bf16[256,2048]{1,0:T(8,128)(2,1)S(1)}, bf16[256,2048]{1,0:T(8,128)(2,1)S(1)}, u32[]{:S(2)}, u32[]{:S(2)}) %collective-permute-start.38) | collective-permute-done | bytes 1048608 | tf_op jit(solution)/shard_map/ppermute | solution.py:58
  445.0 9.6 %front.1.d_ref = bf16[2048,256]{1,0:T(8,128)(2,1)} custom-call(bf16[256,2048]{1,0:T(8,128)(2,1)} %norm_back.2.refs_0_.refs_5_, bf16[256,2048]{1,0:T(8,128)(2,1)} %copy-done.44, bf16[256,2048]{1,0:T(8,128)(2,1)} %copy-done.45, bf16[256,2048]{1,0:T(8,128)(2,1)} %copy-done.47, bf16[256,2048]{1,0:T(8,128)(2,1)} %copy-done.46, bf16[256,2048]{1,0:T(8,128)(2,1)} %copy-done.48, ...), custom_call_target="tpu_custom_call" | custom-call | flops 1 | bytes 1 | tf_op jit(solution)/shard_map/front/pallas_call | solution.py:301
  454.6 35.0 %attend_back.1.refs_0_.refs_1_.refs_10_ = bf16[2048,384]{1,0:T(8,128)(2,1)} custom-call(s32[8]{0:T(128)} %select_reduce_fusion.2.place, s32[8]{0:T(128)} %and_select_fusion.2.first, bf16[2048,2432]{1,0:T(8,128)(2,1)} %qkv.1.q_ref.kv_ref.refs_8_, bf16[2048,256]{1,0:T(8,128)(2,1)} %front.1.d_ref, f32[2048,384]{1,0:T(8,128)} %attend.1.refs_0_.h_ref.refs_9_, ...), custom_call_target="tpu_custom_call" | custom-call | flops 1 | bytes 1 | tf_op jit(solution)/shard_map/attend_back/pallas_call | solution.py:479
  492.5 4.2 back.23
  497.2 4.1 back.22
  501.3 5.6 back.21
  507.7 3.7 slice_add_fusion.2
  513.2 12.4 %weight_grads.5 = bf16[2048,640]{1,0:T(8,128)(2,1)} custom-call(bf16[256,2048]{1,0:T(8,128)(2,1)} %norm_back.2.refs_0_.refs_5_, bf16[256,2048]{1,0:T(8,128)(2,1)} %copy-done.44, bf16[256,2048]{1,0:T(8,128)(2,1)} %copy-done.45, bf16[256,2048]{1,0:T(8,128)(2,1)} %copy-done.47, bf16[256,2048]{1,0:T(8,128)(2,1)} %copy-done.46, bf16[256,2048]{1,0:T(8,128)(2,1)} %copy-done.48, ...), custom_call_target="tpu_custom_call" | custom-call | flops 20000000000 | bytes 1 | tf_op jit(solution)/shard_map/weight_grads/pallas_call | solution.py:240
  525.6 7.9 %collective-permute-done.47 = bf16[256,2048]{1,0:T(8,128)(2,1)} collective-permute-done((bf16[256,2048]{1,0:T(8,128)(2,1)}, bf16[256,2048]{1,0:T(8,128)(2,1)}, u32[]{:S(2)}, u32[]{:S(2)}) %collective-permute-start.47) | collective-permute-done | bytes 1048608 | tf_op jit(solution)/shard_map/ppermute | solution.py:50
  538.1 4.2 fusion.4
  547.5 15.2 %collective-permute-done.50 = bf16[256,2048]{1,0:T(8,128)(2,1)} collective-permute-done((bf16[256,2048]{1,0:T(8,128)(2,1)}, bf16[256,2048]{1,0:T(8,128)(2,1)}, u32[]{:S(2)}, u32[]{:S(2)}) %collective-permute-start.50) | collective-permute-done | bytes 1048608 | tf_op jit(solution)/shard_map/ppermute | solution.py:46
  562.6 33.2 %collective-permute-done.51 = bf16[512,1536]{1,0:T(8,128)(2,1)} collective-permute-done((bf16[512,1536]{1,0:T(8,128)(2,1)}, bf16[512,1536]{1,0:T(8,128)(2,1)}, u32[]{:S(2)}, u32[]{:S(2)}) %collective-permute-start.51) | collective-permute-done | bytes 1572896 | tf_op jit(solution)/shard_map/ppermute | solution.py:50
  595.8 4.9 norm_back.3
  600.9 6.1 collective-permute-start.57
  624.7 5.4 fusion
  632.5 7.3 %collective-permute-done.54 = bf16[512,640]{1,0:T(8,128)(2,1)S(1)} collective-permute-done((bf16[512,640]{1,0:T(8,128)(2,1)}, bf16[512,640]{1,0:T(8,128)(2,1)S(1)}, u32[]{:S(2)}, u32[]{:S(2)}) %collective-permute-start.54) | collective-permute-done | bytes 655392 | tf_op jit(solution)/shard_map/ppermute | solution.py:50
  (325 shorter events, 136.5 us)
Async XLA Ops:
  7.2 182.7 %all-gather.3.cloned.1.call-start = ((), (), s32[]{:S(2)}) async-start(), calls=%async_computation.3 | async-start | bytes 7864320 | tf_op jit(solution)/shard_map/all_gather | solution.py:703
  11.7 20.3 %collective-permute-start = (bf16[528,640]{1,0:T(8,128)(2,1)S(1)}, bf16[528,640]{1,0:T(8,128)(2,1)}, u32[]{:S(2)}, u32[]{:S(2)}) collective-permute-start(bf16[528,640]{1,0:T(8,128)(2,1)S(1)} %fusion.6), channel_id=1, source_target_pairs={{0,8},{8,16},{16,24},{24,0},{1,9},{9,17},{17,25},{25,1},{2,10},{10... | collective-permute-start | bytes 2027528 | tf_op jit(solution)/shard_map/ppermute | solution.py:558
  16.0 16.0 %collective-permute-start.1 = (bf16[256,2048]{1,0:T(8,128)(2,1)S(1)}, bf16[256,2048]{1,0:T(8,128)(2,1)}, u32[]{:S(2)}, u32[]{:S(2)}) collective-permute-start(bf16[256,2048]{1,0:T(8,128)(2,1)S(1)} %constant_dynamic-slice_fusion.11.refs_0_.refs_3_), channel_id=1, source_target_pairs={{0,4},{1,3},{2,6},{3,1},{4,0},{5,7},{6,2},{7,5},{8,12},{9,11},{10,... | collective-permute-start | bytes 3145736 | tf_op jit(solution)/shard_map/ppermute | solution.py:54
  32.0 18.5 %collective-permute-start.2 = (bf16[528,640]{1,0:T(8,128)(2,1)}, bf16[528,640]{1,0:T(8,128)(2,1)}, u32[]{:S(2)}, u32[]{:S(2)}) collective-permute-start(bf16[528,640]{1,0:T(8,128)(2,1)} %collective-permute-done), channel_id=1, source_target_pairs={{0,8},{8,16},{16,24},{24,0},{1,9},{9,17},{17,25},{25,1},{2,10},{10... | collective-permute-start | bytes 2027528 | tf_op jit(solution)/shard_map/ppermute | solution.py:558
  32.6 23.9 %collective-permute-start.4 = (bf16[256,2048]{1,0:T(8,128)(2,1)S(1)}, bf16[256,2048]{1,0:T(8,128)(2,1)}, u32[]{:S(2)}, u32[]{:S(2)}) collective-permute-start(bf16[256,2048]{1,0:T(8,128)(2,1)S(1)} %constant_dynamic-slice_fusion.11.refs_0_.refs_3_), channel_id=1, source_target_pairs={{0,2},{1,5},{2,0},{3,7},{4,6},{5,1},{6,4},{7,3},{8,10},{9,13},{10,... | collective-permute-start | bytes 3145736 | tf_op jit(solution)/shard_map/ppermute | solution.py:58
  34.1 24.6 %collective-permute-start.5 = (bf16[256,2048]{1,0:T(8,128)(2,1)}, bf16[256,2048]{1,0:T(8,128)(2,1)}, u32[]{:S(2)}, u32[]{:S(2)}) collective-permute-start(bf16[256,2048]{1,0:T(8,128)(2,1)} %collective-permute-done.1.refs_1_), channel_id=1, source_target_pairs={{0,2},{1,5},{2,0},{3,7},{4,6},{5,1},{6,4},{7,3},{8,10},{9,13},{10,... | collective-permute-start | bytes 3145736 | tf_op jit(solution)/shard_map/ppermute | solution.py:58
  50.5 17.6 %collective-permute-start.3 = (bf16[528,640]{1,0:T(8,128)(2,1)}, bf16[528,640]{1,0:T(8,128)(2,1)}, u32[]{:S(2)}, u32[]{:S(2)}) collective-permute-start(bf16[528,640]{1,0:T(8,128)(2,1)} %collective-permute-done.2), channel_id=1, source_target_pairs={{0,8},{8,16},{16,24},{24,0},{1,9},{9,17},{17,25},{25,1},{2,10},{10... | collective-permute-start | bytes 2027528 | tf_op jit(solution)/shard_map/ppermute | solution.py:558
  68.1 228.4 %all-gather.5.cloned.1.call-start = ((), (), s32[]{:S(2)}) async-start(), calls=%async_computation.4 | async-start | bytes 7864320 | tf_op jit(solution)/shard_map/all_gather | solution.py:703
  77.3 25.4 %collective-permute-start.10 = (bf16[256,2048]{1,0:T(8,128)(2,1)S(1)}, bf16[256,2048]{1,0:T(8,128)(2,1)S(1)}, u32[]{:S(2)}, u32[]{:S(2)}) collective-permute-start(bf16[256,2048]{1,0:T(8,128)(2,1)S(1)} %constant_dynamic-slice_fusion.6.refs_8_.refs_4_), channel_id=1, source_target_pairs={{0,4},{1,3},{2,6},{3,1},{4,0},{5,7},{6,2},{7,5},{8,12},{9,11},{10,... | collective-permute-start | bytes 3145736 | tf_op jit(solution)/shard_map/ppermute | solution.py:54
  78.7 24.2 %collective-permute-start.11 = (bf16[256,2048]{1,0:T(8,128)(2,1)S(1)}, bf16[256,2048]{1,0:T(8,128)(2,1)}, u32[]{:S(2)}, u32[]{:S(2)}) collective-permute-start(bf16[256,2048]{1,0:T(8,128)(2,1)S(1)} %constant_dynamic-slice_fusion.6.refs_8_.refs_4_), channel_id=1, source_target_pairs={{0,2},{1,5},{2,0},{3,7},{4,6},{5,1},{6,4},{7,3},{8,10},{9,13},{10,... | collective-permute-start | bytes 3145736 | tf_op jit(solution)/shard_map/ppermute | solution.py:58
  79.8 48.6 %collective-permute-start.13 = (bf16[256,2048]{1,0:T(8,128)(2,1)S(1)}, bf16[256,2048]{1,0:T(8,128)(2,1)}, u32[]{:S(2)}, u32[]{:S(2)}) collective-permute-start(bf16[256,2048]{1,0:T(8,128)(2,1)S(1)} %constant_dynamic-slice_fusion.6.refs_8_.refs_4_), channel_id=1, source_target_pairs={{0,1},{1,0},{2,3},{3,2},{4,5},{5,4},{6,7},{7,6},{8,9},{9,8},{10,11... | collective-permute-start | bytes 3145736 | tf_op jit(solution)/shard_map/ppermute | solution.py:42
  102.8 25.6 %collective-permute-start.12 = (bf16[256,2048]{1,0:T(8,128)(2,1)S(1)}, bf16[256,2048]{1,0:T(8,128)(2,1)}, u32[]{:S(2)}, u32[]{:S(2)}) collective-permute-start(bf16[256,2048]{1,0:T(8,128)(2,1)S(1)} %collective-permute-done.10.refs_9_), channel_id=1, source_target_pairs={{0,2},{1,5},{2,0},{3,7},{4,6},{5,1},{6,4},{7,3},{8,10},{9,13},{10,... | collective-permute-start | bytes 3145736 | tf_op jit(solution)/shard_map/ppermute | solution.py:58
  103.9 24.6 %collective-permute-start.14 = (bf16[256,2048]{1,0:T(8,128)(2,1)S(1)}, bf16[256,2048]{1,0:T(8,128)(2,1)}, u32[]{:S(2)}, u32[]{:S(2)}) collective-permute-start(bf16[256,2048]{1,0:T(8,128)(2,1)S(1)} %collective-permute-done.10.refs_9_), channel_id=1, source_target_pairs={{0,1},{1,0},{2,3},{3,2},{4,5},{5,4},{6,7},{7,6},{8,9},{9,8},{10,11... | collective-permute-start | bytes 3145736 | tf_op jit(solution)/shard_map/ppermute | solution.py:42
  104.3 24.2 %collective-permute-start.15 = (bf16[256,2048]{1,0:T(8,128)(2,1)}, bf16[256,2048]{1,0:T(8,128)(2,1)}, u32[]{:S(2)}, u32[]{:S(2)}) collective-permute-start(bf16[256,2048]{1,0:T(8,128)(2,1)} %collective-permute-done.11.refs_10_), channel_id=1, source_target_pairs={{0,1},{1,0},{2,3},{3,2},{4,5},{5,4},{6,7},{7,6},{8,9},{9,8},{10,11... | collective-permute-start | bytes 3145736 | tf_op jit(solution)/shard_map/ppermute | solution.py:42
  139.1 23.2 %collective-permute-start.17 = (bf16[512,2048]{1,0:T(8,128)(2,1)}, bf16[512,2048]{1,0:T(8,128)(2,1)S(1)}, u32[]{:S(2)}, u32[]{:S(2)}) collective-permute-start(bf16[512,2048]{1,0:T(8,128)(2,1)} %back.13), channel_id=1, source_target_pairs={{0,1},{1,0},{2,3},{3,2},{4,5},{5,4},{6,7},{7,6},{8,9},{9,8},{10,11... | collective-permute-start | bytes 6291464 | tf_op jit(solution)/shard_map/ppermute | solution.py:42
  140.6 299.0 %reduce-scatter.4.cloned.1.call-start = ((), (), s32[]{:S(2)}) async-start(), calls=%async_computation.5 | async-start | bytes 7864320 | tf_op jit(solution)/shard_map/reduce_scatter | solution.py:734
  147.5 14.9 %collective-permute-start.19 = (bf16[256,2048]{1,0:T(8,128)(2,1)S(1)}, bf16[256,2048]{1,0:T(8,128)(2,1)S(1)}, u32[]{:S(2)}, u32[]{:S(2)}) collective-permute-start(bf16[256,2048]{1,0:T(8,128)(2,1)S(1)} %get-tuple-element.156), channel_id=1, source_target_pairs={{0,2},{1,5},{2,0},{3,7},{4,6},{5,1},{6,4},{7,3},{8,10},{9,13},{10,... | collective-permute-start | bytes 3145736 | tf_op jit(solution)/shard_map/ppermute | solution.py:58
  163.8 26.1 %collective-permute-start.21 = (bf16[256,2048]{1,0:T(8,128)(2,1)S(1)}, bf16[256,2048]{1,0:T(8,128)(2,1)}, u32[]{:S(2)}, u32[]{:S(2)}) collective-permute-start(bf16[256,2048]{1,0:T(8,128)(2,1)S(1)} %fusion.5), channel_id=1, source_target_pairs={{0,4},{1,3},{2,6},{3,1},{4,0},{5,7},{6,2},{7,5},{8,12},{9,11},{10,... | collective-permute-start | bytes 3145736 | tf_op jit(solution)/shard_map/ppermute | solution.py:54
  165.3 24.6 %collective-permute-start.20 = (bf16[256,2048]{1,0:T(8,128)(2,1)S(1)}, bf16[256,2048]{1,0:T(8,128)(2,1)}, u32[]{:S(2)}, u32[]{:S(2)}) collective-permute-start(bf16[256,2048]{1,0:T(8,128)(2,1)S(1)} %get-tuple-element.93), channel_id=1, source_target_pairs={{0,2},{1,5},{2,0},{3,7},{4,6},{5,1},{6,4},{7,3},{8,10},{9,13},{10,... | collective-permute-start | bytes 3145736 | tf_op jit(solution)/shard_map/ppermute | solution.py:58
  193.4 25.2 %collective-permute-start.22 = (bf16[256,2048]{1,0:T(8,128)(2,1)S(1)}, bf16[256,2048]{1,0:T(8,128)(2,1)S(1)}, u32[]{:S(2)}, u32[]{:S(2)}) collective-permute-start(bf16[256,2048]{1,0:T(8,128)(2,1)S(1)} %multiply_convert_fusion.refs_0_), channel_id=1, source_target_pairs={{0,4},{1,3},{2,6},{3,1},{4,0},{5,7},{6,2},{7,5},{8,12},{9,11},{10,... | collective-permute-start | bytes 3145736 | tf_op jit(solution)/shard_map/ppermute | solution.py:54
  194.2 24.4 %collective-permute-start.23 = (bf16[256,2048]{1,0:T(8,128)(2,1)S(1)}, bf16[256,2048]{1,0:T(8,128)(2,1)S(1)}, u32[]{:S(2)}, u32[]{:S(2)}) collective-permute-start(bf16[256,2048]{1,0:T(8,128)(2,1)S(1)} %multiply_convert_fusion.refs_0_), channel_id=1, source_target_pairs={{0,2},{1,5},{2,0},{3,7},{4,6},{5,1},{6,4},{7,3},{8,10},{9,13},{10,... | collective-permute-start | bytes 3145736 | tf_op jit(solution)/shard_map/ppermute | solution.py:58
  195.5 25.3 %collective-permute-start.25 = (bf16[256,2048]{1,0:T(8,128)(2,1)S(1)}, bf16[256,2048]{1,0:T(8,128)(2,1)S(1)}, u32[]{:S(2)}, u32[]{:S(2)}) collective-permute-start(bf16[256,2048]{1,0:T(8,128)(2,1)S(1)} %multiply_convert_fusion.refs_0_), channel_id=1, source_target_pairs={{0,1},{1,0},{2,3},{3,2},{4,5},{5,4},{6,7},{7,6},{8,9},{9,8},{10,11... | collective-permute-start | bytes 3145736 | tf_op jit(solution)/shard_map/ppermute | solution.py:42
  218.6 14.9 %collective-permute-start.24 = (bf16[256,2048]{1,0:T(8,128)(2,1)S(1)}, bf16[256,2048]{1,0:T(8,128)(2,1)S(1)}, u32[]{:S(2)}, u32[]{:S(2)}) collective-permute-start(bf16[256,2048]{1,0:T(8,128)(2,1)S(1)} %collective-permute-done.22.refs_1_), channel_id=1, source_target_pairs={{0,2},{1,5},{2,0},{3,7},{4,6},{5,1},{6,4},{7,3},{8,10},{9,13},{10,... | collective-permute-start | bytes 3145736 | tf_op jit(solution)/shard_map/ppermute | solution.py:58
  220.2 13.2 %collective-permute-start.26 = (bf16[256,2048]{1,0:T(8,128)(2,1)S(1)}, bf16[256,2048]{1,0:T(8,128)(2,1)S(1)}, u32[]{:S(2)}, u32[]{:S(2)}) collective-permute-start(bf16[256,2048]{1,0:T(8,128)(2,1)S(1)} %collective-permute-done.22.refs_1_), channel_id=1, source_target_pairs={{0,1},{1,0},{2,3},{3,2},{4,5},{5,4},{6,7},{7,6},{8,9},{9,8},{10,11... | collective-permute-start | bytes 3145736 | tf_op jit(solution)/shard_map/ppermute | solution.py:42
  220.3 13.2 %collective-permute-start.27 = (bf16[256,2048]{1,0:T(8,128)(2,1)S(1)}, bf16[256,2048]{1,0:T(8,128)(2,1)S(1)}, u32[]{:S(2)}, u32[]{:S(2)}) collective-permute-start(bf16[256,2048]{1,0:T(8,128)(2,1)S(1)} %collective-permute-done.23.refs_2_), channel_id=1, source_target_pairs={{0,1},{1,0},{2,3},{3,2},{4,5},{5,4},{6,7},{7,6},{8,9},{9,8},{10,11... | collective-permute-start | bytes 3145736 | tf_op jit(solution)/shard_map/ppermute | solution.py:42
  278.5 264.2 %reduce-scatter.6.cloned.1.call-start = ((), (), s32[]{:S(2)}) async-start(), calls=%async_computation.6 | async-start | bytes 7864320 | tf_op jit(solution)/shard_map/reduce_scatter | solution.py:734
  340.6 26.2 %collective-permute-start.30 = (bf16[512,2048]{1,0:T(8,128)(2,1)S(1)}, bf16[512,2048]{1,0:T(8,128)(2,1)}, u32[]{:S(2)}, u32[]{:S(2)}) collective-permute-start(bf16[512,2048]{1,0:T(8,128)(2,1)S(1)} %slice_add_fusion), channel_id=1, source_target_pairs={{0,2},{1,5},{2,0},{3,7},{4,6},{5,1},{6,4},{7,3},{8,10},{9,13},{10,... | collective-permute-start | bytes 6291464 | tf_op jit(solution)/shard_map/ppermute | solution.py:58
  361.5 261.4 %reduce-scatter.8.cloned.1.call-start = ((), (), s32[]{:S(2)}) async-start(), calls=%async_computation.7 | async-start | bytes 3276800 | tf_op jit(solution)/shard_map/reduce_scatter | solution.py:781
  370.1 14.9 %collective-permute-start.31 = (bf16[256,2048]{1,0:T(8,128)(2,1)S(1)}, bf16[256,2048]{1,0:T(8,128)(2,1)S(1)}, u32[]{:S(2)}, u32[]{:S(2)}) collective-permute-start(bf16[256,2048]{1,0:T(8,128)(2,1)S(1)} %slice.217), channel_id=1, source_target_pairs={{0,4},{1,3},{2,6},{3,1},{4,0},{5,7},{6,2},{7,5},{8,12},{9,11},{10,... | collective-permute-start | bytes 3145736 | tf_op jit(solution)/shard_map/ppermute | solution.py:54
  378.0 30.9 %collective-permute-start.35 = (bf16[512,2048]{1,0:T(8,128)(2,1)}, bf16[512,2048]{1,0:T(8,128)(2,1)S(1)}, u32[]{:S(2)}, u32[]{:S(2)}) collective-permute-start(bf16[512,2048]{1,0:T(8,128)(2,1)} %back.18), channel_id=1, source_target_pairs={{0,1},{1,0},{2,3},{3,2},{4,5},{5,4},{6,7},{7,6},{8,9},{9,8},{10,11... | collective-permute-start | bytes 6291464 | tf_op jit(solution)/shard_map/ppermute | solution.py:42
  397.2 25.2 %collective-permute-start.32 = (bf16[256,2048]{1,0:T(8,128)(2,1)S(1)}, bf16[256,2048]{1,0:T(8,128)(2,1)S(1)}, u32[]{:S(2)}, u32[]{:S(2)}) collective-permute-start(bf16[256,2048]{1,0:T(8,128)(2,1)S(1)} %copy-done.7), channel_id=1, source_target_pairs={{0,4},{1,3},{2,6},{3,1},{4,0},{5,7},{6,2},{7,5},{8,12},{9,11},{10,... | collective-permute-start | bytes 3145736 | tf_op jit(solution)/shard_map/ppermute | solution.py:54
  398.7 24.0 %collective-permute-start.33 = (bf16[256,2048]{1,0:T(8,128)(2,1)S(1)}, bf16[256,2048]{1,0:T(8,128)(2,1)S(1)}, u32[]{:S(2)}, u32[]{:S(2)}) collective-permute-start(bf16[256,2048]{1,0:T(8,128)(2,1)S(1)} %copy-done.7), channel_id=1, source_target_pairs={{0,2},{1,5},{2,0},{3,7},{4,6},{5,1},{6,4},{7,3},{8,10},{9,13},{10,... | collective-permute-start | bytes 3145736 | tf_op jit(solution)/shard_map/ppermute | solution.py:58
  400.2 24.9 %collective-permute-start.39 = (bf16[256,2048]{1,0:T(8,128)(2,1)S(1)}, bf16[256,2048]{1,0:T(8,128)(2,1)S(1)}, u32[]{:S(2)}, u32[]{:S(2)}) collective-permute-start(bf16[256,2048]{1,0:T(8,128)(2,1)S(1)} %copy-done.7), channel_id=1, source_target_pairs={{0,1},{1,0},{2,3},{3,2},{4,5},{5,4},{6,7},{7,6},{8,9},{9,8},{10,11... | collective-permute-start | bytes 3145736 | tf_op jit(solution)/shard_map/ppermute | solution.py:42
  422.8 14.8 %collective-permute-start.38 = (bf16[256,2048]{1,0:T(8,128)(2,1)S(1)}, bf16[256,2048]{1,0:T(8,128)(2,1)S(1)}, u32[]{:S(2)}, u32[]{:S(2)}) collective-permute-start(bf16[256,2048]{1,0:T(8,128)(2,1)S(1)} %collective-permute-done.32.refs_1_), channel_id=1, source_target_pairs={{0,2},{1,5},{2,0},{3,7},{4,6},{5,1},{6,4},{7,3},{8,10},{9,13},{10,... | collective-permute-start | bytes 3145736 | tf_op jit(solution)/shard_map/ppermute | solution.py:58
  424.7 14.8 %collective-permute-start.41 = (bf16[256,2048]{1,0:T(8,128)(2,1)S(1)}, bf16[256,2048]{1,0:T(8,128)(2,1)}, u32[]{:S(2)}, u32[]{:S(2)}) collective-permute-start(bf16[256,2048]{1,0:T(8,128)(2,1)S(1)} %collective-permute-done.33.refs_2_), channel_id=1, source_target_pairs={{0,1},{1,0},{2,3},{3,2},{4,5},{5,4},{6,7},{7,6},{8,9},{9,8},{10,11... | collective-permute-start | bytes 3145736 | tf_op jit(solution)/shard_map/ppermute | solution.py:42
  439.6 50.0 %collective-permute-start.43 = (bf16[512,1536]{1,0:T(8,128)(2,1)}, bf16[512,1536]{1,0:T(8,128)(2,1)S(1)}, u32[]{:S(2)}, u32[]{:S(2)}) collective-permute-start(bf16[512,1536]{1,0:T(8,128)(2,1)} %reduce-scatter.4.cloned.1.call-done), channel_id=1, source_target_pairs={{0,4},{4,0},{1,5},{5,1},{2,6},{6,2},{3,7},{7,3},{8,12},{12,8},{9,1... | collective-permute-start | bytes 4718600 | tf_op jit(solution)/shard_map/ppermute | solution.py:50
  441.1 48.5 %collective-permute-start.36 = (bf16[256,2048]{1,0:T(8,128)(2,1)}, bf16[256,2048]{1,0:T(8,128)(2,1)S(1)}, u32[]{:S(2)}, u32[]{:S(2)}) collective-permute-start(bf16[256,2048]{1,0:T(8,128)(2,1)} %get-tuple-element.108), channel_id=1, source_target_pairs={{0,2},{2,0},{1,3},{3,1},{4,6},{6,4},{5,7},{7,5},{8,10},{10,8},{9,1... | collective-permute-start | bytes 3145736 | tf_op jit(solution)/shard_map/ppermute | solution.py:46
  442.9 46.7 %collective-permute-start.37 = (bf16[256,2048]{1,0:T(8,128)(2,1)}, bf16[256,2048]{1,0:T(8,128)(2,1)S(1)}, u32[]{:S(2)}, u32[]{:S(2)}) collective-permute-start(bf16[256,2048]{1,0:T(8,128)(2,1)} %get-tuple-element.109), channel_id=1, source_target_pairs={{0,2},{2,0},{1,3},{3,1},{4,6},{6,4},{5,7},{7,5},{8,10},{10,8},{9,1... | collective-permute-start | bytes 3145736 | tf_op jit(solution)/shard_map/ppermute | solution.py:46
  506.9 31.2 %collective-permute-start.44 = (bf16[512,2048]{1,0:T(8,128)(2,1)}, bf16[512,2048]{1,0:T(8,128)(2,1)}, u32[]{:S(2)}, u32[]{:S(2)}) collective-permute-start(bf16[512,2048]{1,0:T(8,128)(2,1)} %back.22), channel_id=1, source_target_pairs={{0,1},{1,0},{2,3},{3,2},{4,5},{5,4},{6,7},{7,6},{8,9},{9,8},{10,11... | collective-permute-start | bytes 6291464 | tf_op jit(solution)/shard_map/ppermute | solution.py:42
  507.2 26.3 %collective-permute-start.47 = (bf16[256,2048]{1,0:T(8,128)(2,1)}, bf16[256,2048]{1,0:T(8,128)(2,1)}, u32[]{:S(2)}, u32[]{:S(2)}) collective-permute-start(bf16[256,2048]{1,0:T(8,128)(2,1)} %add.380), channel_id=1, source_target_pairs={{0,4},{4,0},{1,5},{5,1},{2,6},{6,2},{3,7},{7,3},{8,12},{12,8},{9,1... | collective-permute-start | bytes 3145736 | tf_op jit(solution)/shard_map/ppermute | solution.py:50
  511.4 26.7 %collective-permute-start.46 = (bf16[256,2048]{1,0:T(8,128)(2,1)}, bf16[256,2048]{1,0:T(8,128)(2,1)}, u32[]{:S(2)}, u32[]{:S(2)}) collective-permute-start(bf16[256,2048]{1,0:T(8,128)(2,1)} %get-tuple-element.150), channel_id=1, source_target_pairs={{0,2},{1,5},{2,0},{3,7},{4,6},{5,1},{6,4},{7,3},{8,10},{9,13},{10,... | collective-permute-start | bytes 3145736 | tf_op jit(solution)/shard_map/ppermute | solution.py:58
  536.2 26.4 %collective-permute-start.50 = (bf16[256,2048]{1,0:T(8,128)(2,1)}, bf16[256,2048]{1,0:T(8,128)(2,1)}, u32[]{:S(2)}, u32[]{:S(2)}) collective-permute-start(bf16[256,2048]{1,0:T(8,128)(2,1)} %add_convert_fusion), channel_id=1, source_target_pairs={{0,2},{2,0},{1,3},{3,1},{4,6},{6,4},{5,7},{7,5},{8,10},{10,8},{9,1... | collective-permute-start | bytes 3145736 | tf_op jit(solution)/shard_map/ppermute | solution.py:46
  542.3 20.4 %collective-permute-start.49 = (bf16[256,2048]{1,0:T(8,128)(2,1)}, bf16[256,2048]{1,0:T(8,128)(2,1)}, u32[]{:S(2)}, u32[]{:S(2)}) collective-permute-start(bf16[256,2048]{1,0:T(8,128)(2,1)} %get-tuple-element.125), channel_id=1, source_target_pairs={{0,4},{1,3},{2,6},{3,1},{4,0},{5,7},{6,2},{7,5},{8,12},{9,11},{10,... | collective-permute-start | bytes 3145736 | tf_op jit(solution)/shard_map/ppermute | solution.py:54
  542.7 53.1 %collective-permute-start.51 = (bf16[512,1536]{1,0:T(8,128)(2,1)}, bf16[512,1536]{1,0:T(8,128)(2,1)}, u32[]{:S(2)}, u32[]{:S(2)}) collective-permute-start(bf16[512,1536]{1,0:T(8,128)(2,1)} %reduce-scatter.6.cloned.1.call-done), channel_id=1, source_target_pairs={{0,4},{4,0},{1,5},{5,1},{2,6},{6,2},{3,7},{7,3},{8,12},{12,8},{9,1... | collective-permute-start | bytes 4718600 | tf_op jit(solution)/shard_map/ppermute | solution.py:50
  544.3 51.5 %collective-permute-start.48 = (bf16[256,2048]{1,0:T(8,128)(2,1)}, bf16[256,2048]{1,0:T(8,128)(2,1)}, u32[]{:S(2)}, u32[]{:S(2)}) collective-permute-start(bf16[256,2048]{1,0:T(8,128)(2,1)} %get-tuple-element.124), channel_id=1, source_target_pairs={{0,2},{1,5},{2,0},{3,7},{4,6},{5,1},{6,4},{7,3},{8,10},{9,13},{10,... | collective-permute-start | bytes 3145736 | tf_op jit(solution)/shard_map/ppermute | solution.py:58
  600.7 31.8 %collective-permute-start.52 = (bf16[256,2048]{1,0:T(8,128)(2,1)}, bf16[256,2048]{1,0:T(8,128)(2,1)}, u32[]{:S(2)}, u32[]{:S(2)}) collective-permute-start(bf16[256,2048]{1,0:T(8,128)(2,1)} %norm_back.3), channel_id=1, source_target_pairs={{0,2},{2,0},{1,3},{3,1},{4,6},{6,4},{5,7},{7,5},{8,10},{10,8},{9,1... | collective-permute-start | bytes 3145736 | tf_op jit(solution)/shard_map/ppermute | solution.py:46
  600.9 50.7 %collective-permute-start.57 = (bf16[256,2048]{1,0:T(8,128)(2,1)}, bf16[256,2048]{1,0:T(8,128)(2,1)}, u32[]{:S(2)}, u32[]{:S(2)}) collective-permute-start(bf16[256,2048]{1,0:T(8,128)(2,1)} %norm_back.3), channel_id=1, source_target_pairs={{0,1},{1,0},{2,3},{3,2},{4,5},{5,4},{6,7},{7,6},{8,9},{9,8},{10,11... | collective-permute-start | bytes 3145736 | tf_op jit(solution)/shard_map/ppermute | solution.py:42
  622.9 16.9 %collective-permute-start.54 = (bf16[512,640]{1,0:T(8,128)(2,1)}, bf16[512,640]{1,0:T(8,128)(2,1)S(1)}, u32[]{:S(2)}, u32[]{:S(2)}) collective-permute-start(bf16[512,640]{1,0:T(8,128)(2,1)} %reduce-scatter.8.cloned.1.call-done), channel_id=1, source_target_pairs={{0,4},{4,0},{1,5},{5,1},{2,6},{6,2},{3,7},{7,3},{8,12},{12,8},{9,1... | collective-permute-start | bytes 1966088 | tf_op jit(solution)/shard_map/ppermute | solution.py:50
  (78 other events, 1058.6 us)
Sparse Core Ops, SparseCore 0:
  68.2 113.0 all-gather.2
  182.9 113.5 all-gather.4
  298.8 108.9 reduce-scatter.3
  409.9 111.2 reduce-scatter.5
  538.1 51.3 reduce-scatter.7

commit v9 on v8

--- a/solution.py
+++ b/solution.py
@@ -774,7 +774,7 @@
     result_beside = swap_y(result_own)
     normed_first = sum_first(normed_blocks, [attn_grad, result_own])
     for part in range(1, len(chunks)):
-        reduced[part] = after(reduced[part], normed_first[1])
+        reduced[part] = after(reduced[part], attn_grad)
         other_reduced.append(swap_x(reduced[part]))
     normed_parts = last_parts(*normed_first, beside=[result_beside, *other_reduced[1:]])
     tokens_grad_own = norm_back(normed_parts, tokens_low, gain_one, d_own)
@@ -801,7 +801,10 @@
         ]
     )
     gain_sums = gain_sums + swap_core(gain_sums)
-
+    gain_sums = gain_sums + swap_y(gain_sums)
+    gain_sums = gain_sums + swap_x(gain_sums)
+
+    other_reduced[-1] = after(other_reduced[-1], attn_reduced)
     halves = [both_halves(mine, other, ctx) for mine, other in zip(reduced, other_reduced)]
 
     def ffn_out(which):
@@ -819,8 +822,6 @@
         (swap_y(tokens_grad_own), gain_sums, other_attn, result, *ffn_grads)
     )
     tokens_grad = share_in_ctx(tokens_grad_own, tokens_grad_beside, y, core)
-    gain_sums = gain_sums + swap_y(gain_sums)
-    gain_sums = gain_sums + swap_x(gain_sums)
     attn_gain_grad = gain_sums[0] / attn_gain.astype(F32)
     ffn_gain_grad = gain_sums[1] / ffn_gain.astype(F32)
     attn_low, attn_high = both_halves(attn_reduced, other_attn, ctx)

time: 674 us -> 669 us (level)
  other arithmetic: 76.3 us -> 68.3 us
    ppermute x5, waiting for transfers between devices: 50.7 us -> 23.7 us  [swap_x(): return lax.ppermute(v, 'ctx', PAIR)]
    ppermute x7, waiting for transfers between devices: 69 us -> 91.7 us  [swap_first(): return lax.ppermute(v, ('ctx', 'tp'), FIRST)]
    ppermute x5, waiting for transfers between devices: 15.2 us -> 22.8 us  [swap_y(): return lax.ppermute(v, 'tp', ACROSS)]
    unnamed x121 -> x133, local copies, waits for them, and re-layouts: 11.4 us -> 14 us
  transfers between devices with their start and end apart: 66 -> 66, of which waited for: 25 -> 27; matrix products, arithmetic and copies ran while one was open for 13% -> 13% of each run, Pallas kernels for 40% -> 40%
where the time goes in v9:
time: 669 us; the launch traced here: 661 us
  Pallas kernels  264 us (39%)
  waiting for transfers between devices  226 us (34%)
  other arithmetic  68.3 us (10%)
  starting transfers between devices  46.1 us (7%)
  local copies, waits for them, and re-layouts  40.8 us (6%)
  between operations  15.1 us (2%)
    ppermute x7, waiting for transfers between devices, swap_first(): return lax.ppermute(v, ('ctx', 'tp'), FIRST)  91.7 us
    pallas_call x12, Pallas kernels, back_product(): pl.pallas_call(functools.partial(back_kernel, len(terms)), out_shape=jax....  79.1 us
    pallas_call x3, Pallas kernels, weight_grads(): pl.pallas_call(functools.partial(grads_kernel, len(x), len(y)), out_shape...  51.1 us
    ppermute x13, waiting for transfers between devices, swap_second(): return lax.ppermute(v, ('ctx', 'tp'), SECOND)  46.6 us
    pallas_call x2, Pallas kernels, ffn_chunk(): pl.pallas_call(functools.partial(ffn_kernel, len(x)), out_shape=jax.Shape...  43.5 us
    pallas_call x1, Pallas kernels, attend_back(): pl.pallas_call(attend_back_kernel, out_shape=jax.ShapeDtypeStruct((rows,...  33.7 us
    ppermute x3, waiting for transfers between devices, ring_over(): pieces.append(lax.ppermute(sent, 'fsdp', cycle))  30.9 us
    ppermute x5, waiting for transfers between devices, swap_x(): return lax.ppermute(v, 'ctx', PAIR)  23.7 us
  transfers between devices with their start and end apart: 66, of which 27 were waited for; matrix products, arithmetic and copies ran while one was open for 13% of the time, Pallas kernels for 40%

profile of v9, /device:TPU:0, one launch (start us, length us, event | category | flops | bytes accessed | tf_op | source)
XLA Modules:
  0.0 660.5 jit_solution(7178473923434506982)
XLA Ops:
  11.7 3.0 collective-permute-start
  20.7 5.6 negate_select_fusion
  26.4 5.6 collective-permute-done
  34.6 15.9 %collective-permute-done.2 = bf16[528,640]{1,0:T(8,128)(2,1)} collective-permute-done((bf16[528,640]{1,0:T(8,128)(2,1)}, bf16[528,640]{1,0:T(8,128)(2,1)}, u32[]{:S(2)}, u32[]{:S(2)}) %collective-permute-start.2) | collective-permute-done | bytes 675872 | tf_op jit(solution)/shard_map/ppermute | solution.py:558
  58.7 9.3 %collective-permute-done.3 = bf16[528,640]{1,0:T(8,128)(2,1)} collective-permute-done((bf16[528,640]{1,0:T(8,128)(2,1)}, bf16[528,640]{1,0:T(8,128)(2,1)}, u32[]{:S(2)}, u32[]{:S(2)}) %collective-permute-start.3) | collective-permute-done | bytes 675872 | tf_op jit(solution)/shard_map/ppermute | solution.py:558
  79.8 15.3 %qkv.1.q_ref.kv_ref.refs_8_ = bf16[2048,2432]{1,0:T(8,128)(2,1)} custom-call(bf16[256,2048]{1,0:T(8,128)(2,1)} %copy-done.7, bf16[256,2048]{1,0:T(8,128)(2,1)} %collective-permute-done.1.refs_1_, bf16[256,2048]{1,0:T(8,128)(2,1)} %collective-permute-done.4.refs_2_, bf16[256,2048]{1,0:T(8,128)(2,1)} %collective-permute-done.5.refs_3_, ...), custom_call_target="tpu_custom_call" | custom-call | flops 1 | bytes 1 | tf_op jit(solution)/shard_map/qkv/pallas_call | solution.py:165
  95.2 7.6 %collective-permute-done.10.refs_9_ = bf16[256,2048]{1,0:T(8,128)(2,1)S(1)} collective-permute-done((bf16[256,2048]{1,0:T(8,128)(2,1)S(1)}, bf16[256,2048]{1,0:T(8,128)(2,1)S(1)}, u32[]{:S(2)}, u32[]{:S(2)}) %collective-permute-start.10) | collective-permute-done | bytes 1048608 | tf_op jit(solution)/shard_map/ppermute | solution.py:54
  105.7 21.8 %attend.1.refs_0_.h_ref.refs_9_ = f32[2048,384]{1,0:T(8,128)} custom-call(s32[8]{0:T(128)} %select_reduce_fusion.2.place, s32[8]{0:T(128)} %and_select_fusion.2.first, bf16[2048,2432]{1,0:T(8,128)(2,1)} %qkv.1.q_ref.kv_ref.refs_8_, bf16[2048,2432]{1,0:T(8,128)(2,1)} %qkv.1.q_ref.kv_ref.refs_8_, s32[2048,1]{1,0:T(8,128)} %copy.28.start_ref), custom_call_target="tpu_custom_call" | custom-call | flops 1 | bytes 1 | tf_op jit(solution)/shard_map/attend/pallas_call | solution.py:382
  130.6 3.8 back.14
  134.8 3.5 back.13
  140.0 4.3 back.12
  148.2 13.3 %collective-permute-done.19 = bf16[256,2048]{1,0:T(8,128)(2,1)S(1)} collective-permute-done((bf16[256,2048]{1,0:T(8,128)(2,1)S(1)}, bf16[256,2048]{1,0:T(8,128)(2,1)S(1)}, u32[]{:S(2)}, u32[]{:S(2)}) %collective-permute-start.19) | collective-permute-done | bytes 1048608 | tf_op jit(solution)/shard_map/ppermute | solution.py:58
  165.0 23.9 %collective-permute-done.21 = bf16[256,2048]{1,0:T(8,128)(2,1)} collective-permute-done((bf16[256,2048]{1,0:T(8,128)(2,1)S(1)}, bf16[256,2048]{1,0:T(8,128)(2,1)}, u32[]{:S(2)}, u32[]{:S(2)}) %collective-permute-start.21) | collective-permute-done | bytes 1048608 | tf_op jit(solution)/shard_map/ppermute | solution.py:54
  189.0 3.4 multiply_reduce_fusion.2
  194.6 23.3 %collective-permute-done.22.refs_1_ = bf16[256,2048]{1,0:T(8,128)(2,1)S(1)} collective-permute-done((bf16[256,2048]{1,0:T(8,128)(2,1)S(1)}, bf16[256,2048]{1,0:T(8,128)(2,1)S(1)}, u32[]{:S(2)}, u32[]{:S(2)}) %collective-permute-start.22) | collective-permute-done | bytes 1048608 | tf_op jit(solution)/shard_map/ppermute | solution.py:54
  219.8 12.9 %collective-permute-done.24.refs_3_ = bf16[256,2048]{1,0:T(8,128)(2,1)S(1)} collective-permute-done((bf16[256,2048]{1,0:T(8,128)(2,1)S(1)}, bf16[256,2048]{1,0:T(8,128)(2,1)S(1)}, u32[]{:S(2)}, u32[]{:S(2)}) %collective-permute-start.24) | collective-permute-done | bytes 1048608 | tf_op jit(solution)/shard_map/ppermute | solution.py:58
  236.6 21.8 %ffn.2.refs_16_.refs_17_.refs_0_ = bf16[2048,1536]{1,0:T(8,128)(2,1)} custom-call(bf16[256,2048]{1,0:T(8,128)(2,1)} %copy-done.6, bf16[256,2048]{1,0:T(8,128)(2,1)} %copy-done.21, bf16[256,2048]{1,0:T(8,128)(2,1)} %copy-done.22, bf16[256,2048]{1,0:T(8,128)(2,1)} %copy-done.24, bf16[256,2048]{1,0:T(8,128)(2,1)} %copy-done.23, bf16[256,2048]{1,0:T(8,128)(2,1)} %copy-done.25, ...), custom_call_target="tpu_custom_call" | custom-call | flops 1 | bytes 1 | tf_op jit(solution)/shard_map/ffn/pallas_call | solution.py:204
  258.4 19.2 %weight_grads.3 = bf16[2048,1536]{1,0:T(8,128)(2,1)} custom-call(bf16[256,2048]{1,0:T(8,128)(2,1)} %copy-done.6, bf16[256,2048]{1,0:T(8,128)(2,1)} %copy-done.21, bf16[256,2048]{1,0:T(8,128)(2,1)} %copy-done.22, bf16[256,2048]{1,0:T(8,128)(2,1)} %copy-done.24, bf16[256,2048]{1,0:T(8,128)(2,1)} %copy-done.23, bf16[256,2048]{1,0:T(8,128)(2,1)} %copy-done.25, ...), custom_call_target="tpu_custom_call" | custom-call | flops 20000000000 | bytes 1 | tf_op jit(solution)/shard_map/weight_grads/pallas_call | solution.py:240
  278.1 13.4 %back.15.refs_2_ = bf16[2048,2048]{1,0:T(8,128)(2,1)} custom-call(bf16[2048,1536]{1,0:T(8,128)(2,1)} %ffn.2.refs_16_.refs_17_.refs_0_, bf16[2048,1536]{1,0:T(8,128)(2,1)} %all-gather.3.cloned.1.call-done.refs_16_.refs_1_.refs_2_), custom_call_target="tpu_custom_call" | custom-call | flops 1 | bytes 1 | tf_op jit(solution)/shard_map/back/pallas_call | solution.py:275
  291.5 5.0 all-gather.5.cloned.1.call-done.refs_16_.refs_1_.refs_3_
  296.5 21.7 %ffn.3.refs_0_.refs_16_.refs_17_.refs_1_ = bf16[2048,1536]{1,0:T(8,128)(2,1)} custom-call(bf16[256,2048]{1,0:T(8,128)(2,1)} %copy-done.6, bf16[256,2048]{1,0:T(8,128)(2,1)} %copy-done.21, bf16[256,2048]{1,0:T(8,128)(2,1)} %copy-done.22, bf16[256,2048]{1,0:T(8,128)(2,1)} %copy-done.24, bf16[256,2048]{1,0:T(8,128)(2,1)} %copy-done.23, ...), custom_call_target="tpu_custom_call" | custom-call | flops 1 | bytes 1 | tf_op jit(solution)/shard_map/ffn/pallas_call | solution.py:204
  318.2 9.3 %back.17 = bf16[1024,2048]{1,0:T(8,128)(2,1)} custom-call(bf16[2048,1536]{1,0:T(8,128)(2,1)} %ffn.3.refs_0_.refs_16_.refs_17_.refs_1_, bf16[2048,1536]{1,0:T(8,128)(2,1)} %all-gather.5.cloned.1.call-done.refs_16_.refs_1_.refs_3_, bf16[2048,2048]{1,0:T(8,128)(2,1)} %back.15.refs_2_), custom_call_target="tpu_custom_call" | custom-call | flops 1 | bytes 1 | tf_op jit(solution)/shard_map/back/pallas_call | solution.py:275
  327.5 9.7 %back.16 = bf16[1024,2048]{1,0:T(8,128)(2,1)} custom-call(bf16[2048,1536]{1,0:T(8,128)(2,1)} %ffn.3.refs_0_.refs_16_.refs_17_.refs_1_, bf16[2048,1536]{1,0:T(8,128)(2,1)} %all-gather.5.cloned.1.call-done.refs_16_.refs_1_.refs_3_, bf16[2048,2048]{1,0:T(8,128)(2,1)} %back.15.refs_2_), custom_call_target="tpu_custom_call" | custom-call | flops 1 | bytes 1 | tf_op jit(solution)/shard_map/back/pallas_call | solution.py:275
  337.2 3.3 slice_add_fusion
  342.2 19.3 %weight_grads.4 = bf16[2048,1536]{1,0:T(8,128)(2,1)} custom-call(bf16[256,2048]{1,0:T(8,128)(2,1)} %copy-done.6, bf16[256,2048]{1,0:T(8,128)(2,1)} %copy-done.21, bf16[256,2048]{1,0:T(8,128)(2,1)} %copy-done.22, bf16[256,2048]{1,0:T(8,128)(2,1)} %copy-done.24, bf16[256,2048]{1,0:T(8,128)(2,1)} %copy-done.23, bf16[256,2048]{1,0:T(8,128)(2,1)} %copy-done.25, ...), custom_call_target="tpu_custom_call" | custom-call | flops 20000000000 | bytes 1 | tf_op jit(solution)/shard_map/weight_grads/pallas_call | solution.py:240
  361.6 5.2 collective-permute-done.30
  366.8 3.2 fusion.2.refs_0_
  371.7 6.3 back.18
  378.0 7.0 %collective-permute-done.31.refs_1_ = bf16[256,2048]{1,0:T(8,128)(2,1)S(1)} collective-permute-done((bf16[256,2048]{1,0:T(8,128)(2,1)S(1)}, bf16[256,2048]{1,0:T(8,128)(2,1)S(1)}, u32[]{:S(2)}, u32[]{:S(2)}) %collective-permute-start.31) | collective-permute-done | bytes 1048608 | tf_op jit(solution)/shard_map/ppermute | solution.py:54
  385.9 4.9 norm_back.2.refs_0_.refs_5_
  390.8 6.4 back.20
  400.2 8.7 %back.19 = bf16[1024,2048]{1,0:T(8,128)(2,1)} custom-call(bf16[2048,1536]{1,0:T(8,128)(2,1)} %ffn.2.refs_16_.refs_17_.refs_0_, bf16[2048,1536]{1,0:T(8,128)(2,1)} %ffn.3.refs_0_.refs_16_.refs_17_.refs_1_, bf16[2048,1536]{1,0:T(8,128)(2,1)} %all-gather.3.cloned.1.call-done.refs_16_.refs_1_.refs_2_, ...), custom_call_target="tpu_custom_call" | custom-call | flops 7000000000 | bytes 1 | tf_op jit(solution)/shard_map/back/pallas_call | solution.py:275
  410.2 4.8 broadcast_select_fusion
  415.0 7.5 %collective-permute-done.32.refs_1_ = bf16[256,2048]{1,0:T(8,128)(2,1)S(1)} collective-permute-done((bf16[256,2048]{1,0:T(8,128)(2,1)S(1)}, bf16[256,2048]{1,0:T(8,128)(2,1)S(1)}, u32[]{:S(2)}, u32[]{:S(2)}) %collective-permute-start.32) | collective-permute-done | bytes 1048608 | tf_op jit(solution)/shard_map/ppermute | solution.py:54
  425.1 12.5 %collective-permute-done.38.refs_3_ = bf16[256,2048]{1,0:T(8,128)(2,1)S(1)} collective-permute-done((bf16[256,2048]{1,0:T(8,128)(2,1)S(1)}, bf16[256,2048]{1,0:T(8,128)(2,1)S(1)}, u32[]{:S(2)}, u32[]{:S(2)}) %collective-permute-start.38) | collective-permute-done | bytes 1048608 | tf_op jit(solution)/shard_map/ppermute | solution.py:58
  444.9 9.6 %front.1.d_ref = bf16[2048,256]{1,0:T(8,128)(2,1)} custom-call(bf16[256,2048]{1,0:T(8,128)(2,1)} %norm_back.2.refs_0_.refs_5_, bf16[256,2048]{1,0:T(8,128)(2,1)} %copy-done.50, bf16[256,2048]{1,0:T(8,128)(2,1)} %copy-done.51, bf16[256,2048]{1,0:T(8,128)(2,1)} %copy-done.53, bf16[256,2048]{1,0:T(8,128)(2,1)} %copy-done.52, bf16[256,2048]{1,0:T(8,128)(2,1)} %copy-done.54, ...), custom_call_target="tpu_custom_call" | custom-call | flops 1 | bytes 1 | tf_op jit(solution)/shard_map/front/pallas_call | solution.py:301
  454.6 33.7 %attend_back.1.refs_0_.refs_1_.refs_10_ = bf16[2048,384]{1,0:T(8,128)(2,1)} custom-call(s32[8]{0:T(128)} %select_reduce_fusion.2.place, s32[8]{0:T(128)} %and_select_fusion.2.first, bf16[2048,2432]{1,0:T(8,128)(2,1)} %qkv.1.q_ref.kv_ref.refs_8_, bf16[2048,256]{1,0:T(8,128)(2,1)} %front.1.d_ref, f32[2048,384]{1,0:T(8,128)} %attend.1.refs_0_.h_ref.refs_9_, ...), custom_call_target="tpu_custom_call" | custom-call | flops 1 | bytes 1 | tf_op jit(solution)/shard_map/attend_back/pallas_call | solution.py:479
  492.3 4.1 back.23
  496.4 5.6 back.21
  502.0 4.2 back.22
  510.5 12.6 %weight_grads.5 = bf16[2048,640]{1,0:T(8,128)(2,1)} custom-call(bf16[256,2048]{1,0:T(8,128)(2,1)} %norm_back.2.refs_0_.refs_5_, bf16[256,2048]{1,0:T(8,128)(2,1)} %copy-done.50, bf16[256,2048]{1,0:T(8,128)(2,1)} %copy-done.51, bf16[256,2048]{1,0:T(8,128)(2,1)} %copy-done.53, bf16[256,2048]{1,0:T(8,128)(2,1)} %copy-done.52, bf16[256,2048]{1,0:T(8,128)(2,1)} %copy-done.54, ...), custom_call_target="tpu_custom_call" | custom-call | flops 20000000000 | bytes 1 | tf_op jit(solution)/shard_map/weight_grads/pallas_call | solution.py:240
  523.1 10.0 %collective-permute-done.47 = bf16[256,2048]{1,0:T(8,128)(2,1)} collective-permute-done((bf16[256,2048]{1,0:T(8,128)(2,1)}, bf16[256,2048]{1,0:T(8,128)(2,1)}, u32[]{:S(2)}, u32[]{:S(2)}) %collective-permute-start.47) | collective-permute-done | bytes 1048608 | tf_op jit(solution)/shard_map/ppermute | solution.py:50
  537.9 4.0 fusion.4
  546.1 16.1 %collective-permute-done.50 = bf16[256,2048]{1,0:T(8,128)(2,1)} collective-permute-done((bf16[256,2048]{1,0:T(8,128)(2,1)}, bf16[256,2048]{1,0:T(8,128)(2,1)}, u32[]{:S(2)}, u32[]{:S(2)}) %collective-permute-start.50) | collective-permute-done | bytes 1048608 | tf_op jit(solution)/shard_map/ppermute | solution.py:46
  562.2 13.0 %collective-permute-done.51 = bf16[512,1536]{1,0:T(8,128)(2,1)} collective-permute-done((bf16[512,1536]{1,0:T(8,128)(2,1)}, bf16[512,1536]{1,0:T(8,128)(2,1)}, u32[]{:S(2)}, u32[]{:S(2)}) %collective-permute-start.51) | collective-permute-done | bytes 1572896 | tf_op jit(solution)/shard_map/ppermute | solution.py:50
  575.2 22.5 %collective-permute-done.49.refs_2_ = bf16[256,2048]{1,0:T(8,128)(2,1)} collective-permute-done((bf16[256,2048]{1,0:T(8,128)(2,1)}, bf16[256,2048]{1,0:T(8,128)(2,1)}, u32[]{:S(2)}, u32[]{:S(2)}) %collective-permute-start.49) | collective-permute-done | bytes 1048608 | tf_op jit(solution)/shard_map/ppermute | solution.py:54
  597.7 4.9 norm_back.3
  630.2 5.6 collective-permute-done.54
  (337 shorter events, 138.0 us)
Async XLA Ops:
  7.2 181.8 %all-gather.3.cloned.1.call-start = ((), (), s32[]{:S(2)}) async-start(), calls=%async_computation.3 | async-start | bytes 7864320 | tf_op jit(solution)/shard_map/all_gather | solution.py:703
  11.7 20.3 %collective-permute-start = (bf16[528,640]{1,0:T(8,128)(2,1)S(1)}, bf16[528,640]{1,0:T(8,128)(2,1)}, u32[]{:S(2)}, u32[]{:S(2)}) collective-permute-start(bf16[528,640]{1,0:T(8,128)(2,1)S(1)} %fusion.6), channel_id=1, source_target_pairs={{0,8},{8,16},{16,24},{24,0},{1,9},{9,17},{17,25},{25,1},{2,10},{10... | collective-permute-start | bytes 2027528 | tf_op jit(solution)/shard_map/ppermute | solution.py:558
  16.0 16.0 %collective-permute-start.1 = (bf16[256,2048]{1,0:T(8,128)(2,1)S(1)}, bf16[256,2048]{1,0:T(8,128)(2,1)}, u32[]{:S(2)}, u32[]{:S(2)}) collective-permute-start(bf16[256,2048]{1,0:T(8,128)(2,1)S(1)} %constant_dynamic-slice_fusion.11.refs_0_.refs_3_), channel_id=1, source_target_pairs={{0,4},{1,3},{2,6},{3,1},{4,0},{5,7},{6,2},{7,5},{8,12},{9,11},{10,... | collective-permute-start | bytes 3145736 | tf_op jit(solution)/shard_map/ppermute | solution.py:54
  32.0 18.5 %collective-permute-start.2 = (bf16[528,640]{1,0:T(8,128)(2,1)}, bf16[528,640]{1,0:T(8,128)(2,1)}, u32[]{:S(2)}, u32[]{:S(2)}) collective-permute-start(bf16[528,640]{1,0:T(8,128)(2,1)} %collective-permute-done), channel_id=1, source_target_pairs={{0,8},{8,16},{16,24},{24,0},{1,9},{9,17},{17,25},{25,1},{2,10},{10... | collective-permute-start | bytes 2027528 | tf_op jit(solution)/shard_map/ppermute | solution.py:558
  32.6 23.8 %collective-permute-start.4 = (bf16[256,2048]{1,0:T(8,128)(2,1)S(1)}, bf16[256,2048]{1,0:T(8,128)(2,1)}, u32[]{:S(2)}, u32[]{:S(2)}) collective-permute-start(bf16[256,2048]{1,0:T(8,128)(2,1)S(1)} %constant_dynamic-slice_fusion.11.refs_0_.refs_3_), channel_id=1, source_target_pairs={{0,2},{1,5},{2,0},{3,7},{4,6},{5,1},{6,4},{7,3},{8,10},{9,13},{10,... | collective-permute-start | bytes 3145736 | tf_op jit(solution)/shard_map/ppermute | solution.py:58
  34.1 24.6 %collective-permute-start.5 = (bf16[256,2048]{1,0:T(8,128)(2,1)}, bf16[256,2048]{1,0:T(8,128)(2,1)}, u32[]{:S(2)}, u32[]{:S(2)}) collective-permute-start(bf16[256,2048]{1,0:T(8,128)(2,1)} %collective-permute-done.1.refs_1_), channel_id=1, source_target_pairs={{0,2},{1,5},{2,0},{3,7},{4,6},{5,1},{6,4},{7,3},{8,10},{9,13},{10,... | collective-permute-start | bytes 3145736 | tf_op jit(solution)/shard_map/ppermute | solution.py:58
  50.5 17.6 %collective-permute-start.3 = (bf16[528,640]{1,0:T(8,128)(2,1)}, bf16[528,640]{1,0:T(8,128)(2,1)}, u32[]{:S(2)}, u32[]{:S(2)}) collective-permute-start(bf16[528,640]{1,0:T(8,128)(2,1)} %collective-permute-done.2), channel_id=1, source_target_pairs={{0,8},{8,16},{16,24},{24,0},{1,9},{9,17},{17,25},{25,1},{2,10},{10... | collective-permute-start | bytes 2027528 | tf_op jit(solution)/shard_map/ppermute | solution.py:558
  68.1 228.4 %all-gather.5.cloned.1.call-start = ((), (), s32[]{:S(2)}) async-start(), calls=%async_computation.4 | async-start | bytes 7864320 | tf_op jit(solution)/shard_map/all_gather | solution.py:703
  77.3 25.4 %collective-permute-start.10 = (bf16[256,2048]{1,0:T(8,128)(2,1)S(1)}, bf16[256,2048]{1,0:T(8,128)(2,1)S(1)}, u32[]{:S(2)}, u32[]{:S(2)}) collective-permute-start(bf16[256,2048]{1,0:T(8,128)(2,1)S(1)} %constant_dynamic-slice_fusion.6.refs_8_.refs_4_), channel_id=1, source_target_pairs={{0,4},{1,3},{2,6},{3,1},{4,0},{5,7},{6,2},{7,5},{8,12},{9,11},{10,... | collective-permute-start | bytes 3145736 | tf_op jit(solution)/shard_map/ppermute | solution.py:54
  78.6 24.2 %collective-permute-start.11 = (bf16[256,2048]{1,0:T(8,128)(2,1)S(1)}, bf16[256,2048]{1,0:T(8,128)(2,1)}, u32[]{:S(2)}, u32[]{:S(2)}) collective-permute-start(bf16[256,2048]{1,0:T(8,128)(2,1)S(1)} %constant_dynamic-slice_fusion.6.refs_8_.refs_4_), channel_id=1, source_target_pairs={{0,2},{1,5},{2,0},{3,7},{4,6},{5,1},{6,4},{7,3},{8,10},{9,13},{10,... | collective-permute-start | bytes 3145736 | tf_op jit(solution)/shard_map/ppermute | solution.py:58
  79.8 47.8 %collective-permute-start.13 = (bf16[256,2048]{1,0:T(8,128)(2,1)S(1)}, bf16[256,2048]{1,0:T(8,128)(2,1)}, u32[]{:S(2)}, u32[]{:S(2)}) collective-permute-start(bf16[256,2048]{1,0:T(8,128)(2,1)S(1)} %constant_dynamic-slice_fusion.6.refs_8_.refs_4_), channel_id=1, source_target_pairs={{0,1},{1,0},{2,3},{3,2},{4,5},{5,4},{6,7},{7,6},{8,9},{9,8},{10,11... | collective-permute-start | bytes 3145736 | tf_op jit(solution)/shard_map/ppermute | solution.py:42
  102.8 24.7 %collective-permute-start.12 = (bf16[256,2048]{1,0:T(8,128)(2,1)S(1)}, bf16[256,2048]{1,0:T(8,128)(2,1)}, u32[]{:S(2)}, u32[]{:S(2)}) collective-permute-start(bf16[256,2048]{1,0:T(8,128)(2,1)S(1)} %collective-permute-done.10.refs_9_), channel_id=1, source_target_pairs={{0,2},{1,5},{2,0},{3,7},{4,6},{5,1},{6,4},{7,3},{8,10},{9,13},{10,... | collective-permute-start | bytes 3145736 | tf_op jit(solution)/shard_map/ppermute | solution.py:58
  103.8 23.7 %collective-permute-start.14 = (bf16[256,2048]{1,0:T(8,128)(2,1)S(1)}, bf16[256,2048]{1,0:T(8,128)(2,1)}, u32[]{:S(2)}, u32[]{:S(2)}) collective-permute-start(bf16[256,2048]{1,0:T(8,128)(2,1)S(1)} %collective-permute-done.10.refs_9_), channel_id=1, source_target_pairs={{0,1},{1,0},{2,3},{3,2},{4,5},{5,4},{6,7},{7,6},{8,9},{9,8},{10,11... | collective-permute-start | bytes 3145736 | tf_op jit(solution)/shard_map/ppermute | solution.py:42
  104.3 23.3 %collective-permute-start.15 = (bf16[256,2048]{1,0:T(8,128)(2,1)}, bf16[256,2048]{1,0:T(8,128)(2,1)}, u32[]{:S(2)}, u32[]{:S(2)}) collective-permute-start(bf16[256,2048]{1,0:T(8,128)(2,1)} %collective-permute-done.11.refs_10_), channel_id=1, source_target_pairs={{0,1},{1,0},{2,3},{3,2},{4,5},{5,4},{6,7},{7,6},{8,9},{9,8},{10,11... | collective-permute-start | bytes 3145736 | tf_op jit(solution)/shard_map/ppermute | solution.py:42
  138.2 23.2 %collective-permute-start.17 = (bf16[512,2048]{1,0:T(8,128)(2,1)}, bf16[512,2048]{1,0:T(8,128)(2,1)S(1)}, u32[]{:S(2)}, u32[]{:S(2)}) collective-permute-start(bf16[512,2048]{1,0:T(8,128)(2,1)} %back.13), channel_id=1, source_target_pairs={{0,1},{1,0},{2,3},{3,2},{4,5},{5,4},{6,7},{7,6},{8,9},{9,8},{10,11... | collective-permute-start | bytes 6291464 | tf_op jit(solution)/shard_map/ppermute | solution.py:42
  139.7 299.8 %reduce-scatter.4.cloned.1.call-start = ((), (), s32[]{:S(2)}) async-start(), calls=%async_computation.5 | async-start | bytes 7864320 | tf_op jit(solution)/shard_map/reduce_scatter | solution.py:734
  146.6 14.9 %collective-permute-start.19 = (bf16[256,2048]{1,0:T(8,128)(2,1)S(1)}, bf16[256,2048]{1,0:T(8,128)(2,1)S(1)}, u32[]{:S(2)}, u32[]{:S(2)}) collective-permute-start(bf16[256,2048]{1,0:T(8,128)(2,1)S(1)} %get-tuple-element.158), channel_id=1, source_target_pairs={{0,2},{1,5},{2,0},{3,7},{4,6},{5,1},{6,4},{7,3},{8,10},{9,13},{10,... | collective-permute-start | bytes 3145736 | tf_op jit(solution)/shard_map/ppermute | solution.py:58
  162.9 26.1 %collective-permute-start.21 = (bf16[256,2048]{1,0:T(8,128)(2,1)S(1)}, bf16[256,2048]{1,0:T(8,128)(2,1)}, u32[]{:S(2)}, u32[]{:S(2)}) collective-permute-start(bf16[256,2048]{1,0:T(8,128)(2,1)S(1)} %fusion.5), channel_id=1, source_target_pairs={{0,4},{1,3},{2,6},{3,1},{4,0},{5,7},{6,2},{7,5},{8,12},{9,11},{10,... | collective-permute-start | bytes 3145736 | tf_op jit(solution)/shard_map/ppermute | solution.py:54
  164.4 24.6 %collective-permute-start.20 = (bf16[256,2048]{1,0:T(8,128)(2,1)S(1)}, bf16[256,2048]{1,0:T(8,128)(2,1)}, u32[]{:S(2)}, u32[]{:S(2)}) collective-permute-start(bf16[256,2048]{1,0:T(8,128)(2,1)S(1)} %get-tuple-element.94), channel_id=1, source_target_pairs={{0,2},{1,5},{2,0},{3,7},{4,6},{5,1},{6,4},{7,3},{8,10},{9,13},{10,... | collective-permute-start | bytes 3145736 | tf_op jit(solution)/shard_map/ppermute | solution.py:58
  192.6 25.3 %collective-permute-start.22 = (bf16[256,2048]{1,0:T(8,128)(2,1)S(1)}, bf16[256,2048]{1,0:T(8,128)(2,1)S(1)}, u32[]{:S(2)}, u32[]{:S(2)}) collective-permute-start(bf16[256,2048]{1,0:T(8,128)(2,1)S(1)} %multiply_convert_fusion.refs_0_), channel_id=1, source_target_pairs={{0,4},{1,3},{2,6},{3,1},{4,0},{5,7},{6,2},{7,5},{8,12},{9,11},{10,... | collective-permute-start | bytes 3145736 | tf_op jit(solution)/shard_map/ppermute | solution.py:54
  193.4 24.5 %collective-permute-start.23 = (bf16[256,2048]{1,0:T(8,128)(2,1)S(1)}, bf16[256,2048]{1,0:T(8,128)(2,1)S(1)}, u32[]{:S(2)}, u32[]{:S(2)}) collective-permute-start(bf16[256,2048]{1,0:T(8,128)(2,1)S(1)} %multiply_convert_fusion.refs_0_), channel_id=1, source_target_pairs={{0,2},{1,5},{2,0},{3,7},{4,6},{5,1},{6,4},{7,3},{8,10},{9,13},{10,... | collective-permute-start | bytes 3145736 | tf_op jit(solution)/shard_map/ppermute | solution.py:58
  194.6 25.2 %collective-permute-start.25 = (bf16[256,2048]{1,0:T(8,128)(2,1)S(1)}, bf16[256,2048]{1,0:T(8,128)(2,1)S(1)}, u32[]{:S(2)}, u32[]{:S(2)}) collective-permute-start(bf16[256,2048]{1,0:T(8,128)(2,1)S(1)} %multiply_convert_fusion.refs_0_), channel_id=1, source_target_pairs={{0,1},{1,0},{2,3},{3,2},{4,5},{5,4},{6,7},{7,6},{8,9},{9,8},{10,11... | collective-permute-start | bytes 3145736 | tf_op jit(solution)/shard_map/ppermute | solution.py:42
  217.9 14.9 %collective-permute-start.24 = (bf16[256,2048]{1,0:T(8,128)(2,1)S(1)}, bf16[256,2048]{1,0:T(8,128)(2,1)S(1)}, u32[]{:S(2)}, u32[]{:S(2)}) collective-permute-start(bf16[256,2048]{1,0:T(8,128)(2,1)S(1)} %collective-permute-done.22.refs_1_), channel_id=1, source_target_pairs={{0,2},{1,5},{2,0},{3,7},{4,6},{5,1},{6,4},{7,3},{8,10},{9,13},{10,... | collective-permute-start | bytes 3145736 | tf_op jit(solution)/shard_map/ppermute | solution.py:58
  219.3 13.5 %collective-permute-start.26 = (bf16[256,2048]{1,0:T(8,128)(2,1)S(1)}, bf16[256,2048]{1,0:T(8,128)(2,1)S(1)}, u32[]{:S(2)}, u32[]{:S(2)}) collective-permute-start(bf16[256,2048]{1,0:T(8,128)(2,1)S(1)} %collective-permute-done.22.refs_1_), channel_id=1, source_target_pairs={{0,1},{1,0},{2,3},{3,2},{4,5},{5,4},{6,7},{7,6},{8,9},{9,8},{10,11... | collective-permute-start | bytes 3145736 | tf_op jit(solution)/shard_map/ppermute | solution.py:42
  219.3 13.5 %collective-permute-start.27 = (bf16[256,2048]{1,0:T(8,128)(2,1)S(1)}, bf16[256,2048]{1,0:T(8,128)(2,1)S(1)}, u32[]{:S(2)}, u32[]{:S(2)}) collective-permute-start(bf16[256,2048]{1,0:T(8,128)(2,1)S(1)} %collective-permute-done.23.refs_2_), channel_id=1, source_target_pairs={{0,1},{1,0},{2,3},{3,2},{4,5},{5,4},{6,7},{7,6},{8,9},{9,8},{10,11... | collective-permute-start | bytes 3145736 | tf_op jit(solution)/shard_map/ppermute | solution.py:42
  277.7 259.9 %reduce-scatter.6.cloned.1.call-start = ((), (), s32[]{:S(2)}) async-start(), calls=%async_computation.6 | async-start | bytes 7864320 | tf_op jit(solution)/shard_map/reduce_scatter | solution.py:734
  340.6 26.2 %collective-permute-start.30 = (bf16[512,2048]{1,0:T(8,128)(2,1)S(1)}, bf16[512,2048]{1,0:T(8,128)(2,1)}, u32[]{:S(2)}, u32[]{:S(2)}) collective-permute-start(bf16[512,2048]{1,0:T(8,128)(2,1)S(1)} %slice_add_fusion), channel_id=1, source_target_pairs={{0,2},{1,5},{2,0},{3,7},{4,6},{5,1},{6,4},{7,3},{8,10},{9,13},{10,... | collective-permute-start | bytes 6291464 | tf_op jit(solution)/shard_map/ppermute | solution.py:58
  361.5 257.9 %reduce-scatter.8.cloned.1.call-start = ((), (), s32[]{:S(2)}) async-start(), calls=%async_computation.7 | async-start | bytes 3276800 | tf_op jit(solution)/shard_map/reduce_scatter | solution.py:781
  370.1 14.9 %collective-permute-start.31 = (bf16[256,2048]{1,0:T(8,128)(2,1)S(1)}, bf16[256,2048]{1,0:T(8,128)(2,1)S(1)}, u32[]{:S(2)}, u32[]{:S(2)}) collective-permute-start(bf16[256,2048]{1,0:T(8,128)(2,1)S(1)} %slice.217), channel_id=1, source_target_pairs={{0,4},{1,3},{2,6},{3,1},{4,0},{5,7},{6,2},{7,5},{8,12},{9,11},{10,... | collective-permute-start | bytes 3145736 | tf_op jit(solution)/shard_map/ppermute | solution.py:54
  378.0 30.9 %collective-permute-start.35 = (bf16[512,2048]{1,0:T(8,128)(2,1)}, bf16[512,2048]{1,0:T(8,128)(2,1)S(1)}, u32[]{:S(2)}, u32[]{:S(2)}) collective-permute-start(bf16[512,2048]{1,0:T(8,128)(2,1)} %back.18), channel_id=1, source_target_pairs={{0,1},{1,0},{2,3},{3,2},{4,5},{5,4},{6,7},{7,6},{8,9},{9,8},{10,11... | collective-permute-start | bytes 6291464 | tf_op jit(solution)/shard_map/ppermute | solution.py:42
  397.2 25.2 %collective-permute-start.32 = (bf16[256,2048]{1,0:T(8,128)(2,1)S(1)}, bf16[256,2048]{1,0:T(8,128)(2,1)S(1)}, u32[]{:S(2)}, u32[]{:S(2)}) collective-permute-start(bf16[256,2048]{1,0:T(8,128)(2,1)S(1)} %copy-done.8), channel_id=1, source_target_pairs={{0,4},{1,3},{2,6},{3,1},{4,0},{5,7},{6,2},{7,5},{8,12},{9,11},{10,... | collective-permute-start | bytes 3145736 | tf_op jit(solution)/shard_map/ppermute | solution.py:54
  398.7 24.0 %collective-permute-start.33 = (bf16[256,2048]{1,0:T(8,128)(2,1)S(1)}, bf16[256,2048]{1,0:T(8,128)(2,1)S(1)}, u32[]{:S(2)}, u32[]{:S(2)}) collective-permute-start(bf16[256,2048]{1,0:T(8,128)(2,1)S(1)} %copy-done.8), channel_id=1, source_target_pairs={{0,2},{1,5},{2,0},{3,7},{4,6},{5,1},{6,4},{7,3},{8,10},{9,13},{10,... | collective-permute-start | bytes 3145736 | tf_op jit(solution)/shard_map/ppermute | solution.py:58
  400.2 24.9 %collective-permute-start.39 = (bf16[256,2048]{1,0:T(8,128)(2,1)S(1)}, bf16[256,2048]{1,0:T(8,128)(2,1)S(1)}, u32[]{:S(2)}, u32[]{:S(2)}) collective-permute-start(bf16[256,2048]{1,0:T(8,128)(2,1)S(1)} %copy-done.8), channel_id=1, source_target_pairs={{0,1},{1,0},{2,3},{3,2},{4,5},{5,4},{6,7},{7,6},{8,9},{9,8},{10,11... | collective-permute-start | bytes 3145736 | tf_op jit(solution)/shard_map/ppermute | solution.py:42
  422.7 14.8 %collective-permute-start.38 = (bf16[256,2048]{1,0:T(8,128)(2,1)S(1)}, bf16[256,2048]{1,0:T(8,128)(2,1)S(1)}, u32[]{:S(2)}, u32[]{:S(2)}) collective-permute-start(bf16[256,2048]{1,0:T(8,128)(2,1)S(1)} %collective-permute-done.32.refs_1_), channel_id=1, source_target_pairs={{0,2},{1,5},{2,0},{3,7},{4,6},{5,1},{6,4},{7,3},{8,10},{9,13},{10,... | collective-permute-start | bytes 3145736 | tf_op jit(solution)/shard_map/ppermute | solution.py:58
  424.7 14.8 %collective-permute-start.41 = (bf16[256,2048]{1,0:T(8,128)(2,1)S(1)}, bf16[256,2048]{1,0:T(8,128)(2,1)}, u32[]{:S(2)}, u32[]{:S(2)}) collective-permute-start(bf16[256,2048]{1,0:T(8,128)(2,1)S(1)} %collective-permute-done.33.refs_2_), channel_id=1, source_target_pairs={{0,1},{1,0},{2,3},{3,2},{4,5},{5,4},{6,7},{7,6},{8,9},{9,8},{10,11... | collective-permute-start | bytes 3145736 | tf_op jit(solution)/shard_map/ppermute | solution.py:42
  439.5 49.9 %collective-permute-start.43 = (bf16[512,1536]{1,0:T(8,128)(2,1)}, bf16[512,1536]{1,0:T(8,128)(2,1)S(1)}, u32[]{:S(2)}, u32[]{:S(2)}) collective-permute-start(bf16[512,1536]{1,0:T(8,128)(2,1)} %reduce-scatter.4.cloned.1.call-done), channel_id=1, source_target_pairs={{0,4},{4,0},{1,5},{5,1},{2,6},{6,2},{3,7},{7,3},{8,12},{12,8},{9,1... | collective-permute-start | bytes 4718600 | tf_op jit(solution)/shard_map/ppermute | solution.py:50
  441.1 47.2 %collective-permute-start.36 = (bf16[256,2048]{1,0:T(8,128)(2,1)}, bf16[256,2048]{1,0:T(8,128)(2,1)S(1)}, u32[]{:S(2)}, u32[]{:S(2)}) collective-permute-start(bf16[256,2048]{1,0:T(8,128)(2,1)} %get-tuple-element.109), channel_id=1, source_target_pairs={{0,2},{2,0},{1,3},{3,1},{4,6},{6,4},{5,7},{7,5},{8,10},{10,8},{9,1... | collective-permute-start | bytes 3145736 | tf_op jit(solution)/shard_map/ppermute | solution.py:46
  442.9 46.5 %collective-permute-start.37 = (bf16[256,2048]{1,0:T(8,128)(2,1)}, bf16[256,2048]{1,0:T(8,128)(2,1)S(1)}, u32[]{:S(2)}, u32[]{:S(2)}) collective-permute-start(bf16[256,2048]{1,0:T(8,128)(2,1)} %get-tuple-element.110), channel_id=1, source_target_pairs={{0,2},{2,0},{1,3},{3,1},{4,6},{6,4},{5,7},{7,5},{8,10},{10,8},{9,1... | collective-permute-start | bytes 3145736 | tf_op jit(solution)/shard_map/ppermute | solution.py:46
  506.2 31.8 %collective-permute-start.44 = (bf16[512,2048]{1,0:T(8,128)(2,1)}, bf16[512,2048]{1,0:T(8,128)(2,1)}, u32[]{:S(2)}, u32[]{:S(2)}) collective-permute-start(bf16[512,2048]{1,0:T(8,128)(2,1)} %back.22), channel_id=1, source_target_pairs={{0,1},{1,0},{2,3},{3,2},{4,5},{5,4},{6,7},{7,6},{8,9},{9,8},{10,11... | collective-permute-start | bytes 6291464 | tf_op jit(solution)/shard_map/ppermute | solution.py:42
  506.7 26.3 %collective-permute-start.47 = (bf16[256,2048]{1,0:T(8,128)(2,1)}, bf16[256,2048]{1,0:T(8,128)(2,1)}, u32[]{:S(2)}, u32[]{:S(2)}) collective-permute-start(bf16[256,2048]{1,0:T(8,128)(2,1)} %add.380), channel_id=1, source_target_pairs={{0,4},{4,0},{1,5},{5,1},{2,6},{6,2},{3,7},{7,3},{8,12},{12,8},{9,1... | collective-permute-start | bytes 3145736 | tf_op jit(solution)/shard_map/ppermute | solution.py:50
  508.7 29.2 %collective-permute-start.46 = (bf16[256,2048]{1,0:T(8,128)(2,1)}, bf16[256,2048]{1,0:T(8,128)(2,1)}, u32[]{:S(2)}, u32[]{:S(2)}) collective-permute-start(bf16[256,2048]{1,0:T(8,128)(2,1)} %get-tuple-element.152), channel_id=1, source_target_pairs={{0,2},{1,5},{2,0},{3,7},{4,6},{5,1},{6,4},{7,3},{8,10},{9,13},{10,... | collective-permute-start | bytes 3145736 | tf_op jit(solution)/shard_map/ppermute | solution.py:58
  535.7 26.4 %collective-permute-start.50 = (bf16[256,2048]{1,0:T(8,128)(2,1)}, bf16[256,2048]{1,0:T(8,128)(2,1)}, u32[]{:S(2)}, u32[]{:S(2)}) collective-permute-start(bf16[256,2048]{1,0:T(8,128)(2,1)} %add_convert_fusion), channel_id=1, source_target_pairs={{0,2},{2,0},{1,3},{3,1},{4,6},{6,4},{5,7},{7,5},{8,10},{10,8},{9,1... | collective-permute-start | bytes 3145736 | tf_op jit(solution)/shard_map/ppermute | solution.py:46
  537.5 37.6 %collective-permute-start.51 = (bf16[512,1536]{1,0:T(8,128)(2,1)}, bf16[512,1536]{1,0:T(8,128)(2,1)}, u32[]{:S(2)}, u32[]{:S(2)}) collective-permute-start(bf16[512,1536]{1,0:T(8,128)(2,1)} %reduce-scatter.6.cloned.1.call-done), channel_id=1, source_target_pairs={{0,4},{4,0},{1,5},{5,1},{2,6},{6,2},{3,7},{7,3},{8,12},{12,8},{9,1... | collective-permute-start | bytes 4718600 | tf_op jit(solution)/shard_map/ppermute | solution.py:50
  542.0 55.7 %collective-permute-start.49 = (bf16[256,2048]{1,0:T(8,128)(2,1)}, bf16[256,2048]{1,0:T(8,128)(2,1)}, u32[]{:S(2)}, u32[]{:S(2)}) collective-permute-start(bf16[256,2048]{1,0:T(8,128)(2,1)} %get-tuple-element.126), channel_id=1, source_target_pairs={{0,4},{1,3},{2,6},{3,1},{4,0},{5,7},{6,2},{7,5},{8,12},{9,11},{10,... | collective-permute-start | bytes 3145736 | tf_op jit(solution)/shard_map/ppermute | solution.py:54
  543.6 54.0 %collective-permute-start.48 = (bf16[256,2048]{1,0:T(8,128)(2,1)}, bf16[256,2048]{1,0:T(8,128)(2,1)}, u32[]{:S(2)}, u32[]{:S(2)}) collective-permute-start(bf16[256,2048]{1,0:T(8,128)(2,1)} %get-tuple-element.125), channel_id=1, source_target_pairs={{0,2},{1,5},{2,0},{3,7},{4,6},{5,1},{6,4},{7,3},{8,10},{9,13},{10,... | collective-permute-start | bytes 3145736 | tf_op jit(solution)/shard_map/ppermute | solution.py:58
  610.0 29.5 %collective-permute-start.52 = (bf16[256,2048]{1,0:T(8,128)(2,1)S(1)}, bf16[256,2048]{1,0:T(8,128)(2,1)}, u32[]{:S(2)}, u32[]{:S(2)}) collective-permute-start(bf16[256,2048]{1,0:T(8,128)(2,1)S(1)} %copy-done.31), channel_id=1, source_target_pairs={{0,2},{2,0},{1,3},{3,1},{4,6},{6,4},{5,7},{7,5},{8,10},{10,8},{9,1... | collective-permute-start | bytes 3145736 | tf_op jit(solution)/shard_map/ppermute | solution.py:46
  611.8 34.9 %collective-permute-start.59 = (bf16[256,2048]{1,0:T(8,128)(2,1)S(1)}, bf16[256,2048]{1,0:T(8,128)(2,1)}, u32[]{:S(2)}, u32[]{:S(2)}) collective-permute-start(bf16[256,2048]{1,0:T(8,128)(2,1)S(1)} %copy-done.31), channel_id=1, source_target_pairs={{0,1},{1,0},{2,3},{3,2},{4,5},{5,4},{6,7},{7,6},{8,9},{9,8},{10,11... | collective-permute-start | bytes 3145736 | tf_op jit(solution)/shard_map/ppermute | solution.py:42
  619.5 20.0 %collective-permute-start.56 = (bf16[512,640]{1,0:T(8,128)(2,1)}, bf16[512,640]{1,0:T(8,128)(2,1)S(1)}, u32[]{:S(2)}, u32[]{:S(2)}) collective-permute-start(bf16[512,640]{1,0:T(8,128)(2,1)} %reduce-scatter.8.cloned.1.call-done), channel_id=1, source_target_pairs={{0,4},{4,0},{1,5},{5,1},{2,6},{6,2},{3,7},{7,3},{8,12},{12,8},{9,1... | collective-permute-start | bytes 1966088 | tf_op jit(solution)/shard_map/ppermute | solution.py:50
  (84 other events, 1052.4 us)
Sparse Core Ops, SparseCore 0:
  68.2 113.0 all-gather.2
  182.8 113.5 all-gather.4
  298.8 108.9 reduce-scatter.3
  409.9 111.2 reduce-scatter.5
  533.2 50.1 reduce-scatter.7

commit v10 on v9

--- a/solution.py
+++ b/solution.py
@@ -14,7 +14,7 @@
 MASKED = -1e30
 LOG2_E = 1.4426950408889634
 BLOCK = 256
-SPLIT = (1, 1)
+SPLIT = (5, 3)
 VMEM = 56 * 2**20
 
 F32 = jnp.float32
@@ -705,10 +705,12 @@
     ]
     heads = after(heads, *cot)
     attn_blocks = sum_cores([(heads, 0, attn_full, 0, q_width)])
-    attn_parts = last_parts(*sum_first(attn_blocks), beside=ffn_full[:1])
+    attn_parts = last_parts(*sum_first(attn_blocks))
     attn_sum = sum(part.astype(F32) for part in attn_parts)
     hidden = tokens_own + attn_sum
-    normed_two = share_rows((hidden * inv_rms(hidden) * gain_two).astype(BF16))
+    normed_two = share_rows(
+        (hidden * inv_rms(hidden) * gain_two).astype(BF16), [(), ffn_full[:1]]
+    )
 
     acts = []
     grad_parts = []

time: 669 us -> 675 us (level)
  waiting for transfers between devices: 226 us -> 203 us
  Pallas kernels: 264 us -> 274 us
  other arithmetic: 68.3 us -> 77.8 us
    ppermute x5, waiting for transfers between devices: 23.7 us -> 9.89 us  [swap_x(): return lax.ppermute(v, 'ctx', PAIR)]
    ppermute x28, starting transfers between devices: 6.35 us -> 14.6 us  [swap_core(): return lax.ppermute(v, 'tp', CORE)]
    ppermute x13, waiting for transfers between devices: 46.6 us -> 53.8 us  [swap_second(): return lax.ppermute(v, ('ctx', 'tp'), SECOND)]
    pallas_call x2, Pallas kernels: 43.5 us -> 50.3 us  [ffn_chunk(): pl.pallas_call(functools.partial(ffn_kernel, len(x)), out_shape=jax.Shape...]
    unnamed x133 -> x129, local copies, waits for them, and re-layouts: 14 us -> 13.5 us
  transfers between devices with their start and end apart: 66 -> 66, of which waited for: 27 -> 26; matrix products, arithmetic and copies ran while one was open for 13% -> 14% of each run, Pallas kernels for 40% -> 41%
where the time goes in v10:
time: 675 us; the launch traced here: 665 us
  Pallas kernels  274 us (41%)
  waiting for transfers between devices  203 us (30%)
  other arithmetic  77.8 us (12%)
  starting transfers between devices  51.1 us (8%)
  local copies, waits for them, and re-layouts  43 us (6%)
  between operations  15.1 us (2%)
    ppermute x7, waiting for transfers between devices, swap_first(): return lax.ppermute(v, ('ctx', 'tp'), FIRST)  88.3 us
    pallas_call x12, Pallas kernels, back_product(): pl.pallas_call(functools.partial(back_kernel, len(terms)), out_shape=jax....  80.6 us
    ppermute x13, waiting for transfers between devices, swap_second(): return lax.ppermute(v, ('ctx', 'tp'), SECOND)  53.8 us
    pallas_call x3, Pallas kernels, weight_grads(): pl.pallas_call(functools.partial(grads_kernel, len(x), len(y)), out_shape...  53.4 us
    pallas_call x2, Pallas kernels, ffn_chunk(): pl.pallas_call(functools.partial(ffn_kernel, len(x)), out_shape=jax.Shape...  50.3 us
    pallas_call x1, Pallas kernels, attend_back(): pl.pallas_call(attend_back_kernel, out_shape=jax.ShapeDtypeStruct((rows,...  33.6 us
    ppermute x3, waiting for transfers between devices, ring_over(): pieces.append(lax.ppermute(sent, 'fsdp', cycle))  26.5 us
    pallas_call x1, Pallas kernels, attend(): pl.pallas_call(attend_kernel, out_shape=jax.ShapeDtypeStruct((rows, q_wid...  21.8 us
  transfers between devices with their start and end apart: 66, of which 26 were waited for; matrix products, arithmetic and copies ran while one was open for 14% of the time, Pallas kernels for 41%

profile of v10, /device:TPU:0, one launch (start us, length us, event | category | flops | bytes accessed | tf_op | source)
XLA Modules:
  0.0 664.7 jit_solution(3302217291108670202)
XLA Ops:
  23.8 5.6 negate_select_fusion
  29.4 3.3 collective-permute-done
  36.2 15.0 %collective-permute-done.2 = bf16[528,640]{1,0:T(8,128)(2,1)} collective-permute-done((bf16[528,640]{1,0:T(8,128)(2,1)}, bf16[528,640]{1,0:T(8,128)(2,1)}, u32[]{:S(2)}, u32[]{:S(2)}) %collective-permute-start.2) | collective-permute-done | bytes 675872 | tf_op jit(solution)/shard_map/ppermute | solution.py:558
  55.3 5.3 collective-permute-done.5.refs_3_
  60.6 8.2 %collective-permute-done.3 = bf16[528,640]{1,0:T(8,128)(2,1)} collective-permute-done((bf16[528,640]{1,0:T(8,128)(2,1)}, bf16[528,640]{1,0:T(8,128)(2,1)}, u32[]{:S(2)}, u32[]{:S(2)}) %collective-permute-start.3) | collective-permute-done | bytes 675872 | tf_op jit(solution)/shard_map/ppermute | solution.py:558
  80.6 15.3 %qkv.1.q_ref.kv_ref.refs_8_ = bf16[2048,2432]{1,0:T(8,128)(2,1)} custom-call(bf16[256,2048]{1,0:T(8,128)(2,1)} %constant_dynamic-slice_fusion.11.refs_0_.refs_3_, bf16[256,2048]{1,0:T(8,128)(2,1)} %collective-permute-done.1.refs_1_, bf16[256,2048]{1,0:T(8,128)(2,1)} %collective-permute-done.4.refs_2_, bf16[256,2048]{1,0:T(8,128)(2,1)} %collective-permute-done.5.refs_3_, ...), custom_call_target="tpu_custom_call" | custom-call | flops 1 | bytes 1 | tf_op jit(solution)/shard_map/qkv/pallas_call | solution.py:165
  95.9 7.7 %collective-permute-done.10.refs_9_ = bf16[256,2048]{1,0:T(8,128)(2,1)} collective-permute-done((bf16[256,2048]{1,0:T(8,128)(2,1)S(1)}, bf16[256,2048]{1,0:T(8,128)(2,1)}, u32[]{:S(2)}, u32[]{:S(2)}) %collective-permute-start.10) | collective-permute-done | bytes 1048608 | tf_op jit(solution)/shard_map/ppermute | solution.py:54
  106.5 21.8 %attend.1.refs_0_.h_ref.refs_9_ = f32[2048,384]{1,0:T(8,128)} custom-call(s32[8]{0:T(128)} %select_reduce_fusion.2.place, s32[8]{0:T(128)} %and_select_fusion.2.first, bf16[2048,2432]{1,0:T(8,128)(2,1)} %qkv.1.q_ref.kv_ref.refs_8_, bf16[2048,2432]{1,0:T(8,128)(2,1)} %qkv.1.q_ref.kv_ref.refs_8_, s32[2048,1]{1,0:T(8,128)} %copy.28.start_ref), custom_call_target="tpu_custom_call" | custom-call | flops 1 | bytes 1 | tf_op jit(solution)/shard_map/attend/pallas_call | solution.py:382
  131.4 3.5 back.14
  135.2 3.5 back.13
  138.8 4.2 back.12
  148.6 12.3 %collective-permute-done.19 = bf16[256,2048]{1,0:T(8,128)(2,1)} collective-permute-done((bf16[256,2048]{1,0:T(8,128)(2,1)}, bf16[256,2048]{1,0:T(8,128)(2,1)}, u32[]{:S(2)}, u32[]{:S(2)}) %collective-permute-start.19) | collective-permute-done | bytes 1048608 | tf_op jit(solution)/shard_map/ppermute | solution.py:58
  167.4 21.1 %collective-permute-done.21 = bf16[256,2048]{1,0:T(8,128)(2,1)S(1)} collective-permute-done((bf16[256,2048]{1,0:T(8,128)(2,1)}, bf16[256,2048]{1,0:T(8,128)(2,1)S(1)}, u32[]{:S(2)}, u32[]{:S(2)}) %collective-permute-start.21) | collective-permute-done | bytes 1048608 | tf_op jit(solution)/shard_map/ppermute | solution.py:54
  189.8 3.3 multiply_reduce_fusion.1
  196.2 22.9 %collective-permute-done.22.refs_1_ = bf16[256,2048]{1,0:T(8,128)(2,1)S(1)} collective-permute-done((bf16[256,2048]{1,0:T(8,128)(2,1)S(1)}, bf16[256,2048]{1,0:T(8,128)(2,1)S(1)}, u32[]{:S(2)}, u32[]{:S(2)}) %collective-permute-start.22) | collective-permute-done | bytes 1048608 | tf_op jit(solution)/shard_map/ppermute | solution.py:54
  220.9 13.2 %collective-permute-done.24.refs_3_ = bf16[256,2048]{1,0:T(8,128)(2,1)S(1)} collective-permute-done((bf16[256,2048]{1,0:T(8,128)(2,1)S(1)}, bf16[256,2048]{1,0:T(8,128)(2,1)S(1)}, u32[]{:S(2)}, u32[]{:S(2)}) %collective-permute-start.24) | collective-permute-done | bytes 1048608 | tf_op jit(solution)/shard_map/ppermute | solution.py:58
  240.0 29.3 %ffn.2.refs_16_.refs_17_.refs_0_ = bf16[2048,1920]{1,0:T(8,128)(2,1)} custom-call(bf16[256,2048]{1,0:T(8,128)(2,1)} %copy-done.9, bf16[256,2048]{1,0:T(8,128)(2,1)} %copy-done.20, bf16[256,2048]{1,0:T(8,128)(2,1)} %copy-done.21, bf16[256,2048]{1,0:T(8,128)(2,1)} %copy-done.23, bf16[256,2048]{1,0:T(8,128)(2,1)} %copy-done.22, bf16[256,2048]{1,0:T(8,128)(2,1)} %copy-done.24, ...), custom_call_target="tpu_custom_call" | custom-call | flops 1 | bytes 1 | tf_op jit(solution)/shard_map/ffn/pallas_call | solution.py:204
  269.2 24.1 %weight_grads.3 = bf16[2048,1920]{1,0:T(8,128)(2,1)} custom-call(bf16[256,2048]{1,0:T(8,128)(2,1)} %copy-done.9, bf16[256,2048]{1,0:T(8,128)(2,1)} %copy-done.20, bf16[256,2048]{1,0:T(8,128)(2,1)} %copy-done.21, bf16[256,2048]{1,0:T(8,128)(2,1)} %copy-done.23, bf16[256,2048]{1,0:T(8,128)(2,1)} %copy-done.22, bf16[256,2048]{1,0:T(8,128)(2,1)} %copy-done.24, ...), custom_call_target="tpu_custom_call" | custom-call | flops 20000000000 | bytes 1 | tf_op jit(solution)/shard_map/weight_grads/pallas_call | solution.py:240
  293.9 16.1 %back.15.refs_2_ = bf16[2048,2048]{1,0:T(8,128)(2,1)} custom-call(bf16[2048,1920]{1,0:T(8,128)(2,1)} %ffn.2.refs_16_.refs_17_.refs_0_, bf16[2048,1920]{1,0:T(8,128)(2,1)} %all-gather.3.cloned.1.call-done.refs_16_.refs_1_.refs_2_), custom_call_target="tpu_custom_call" | custom-call | flops 1 | bytes 1 | tf_op jit(solution)/shard_map/back/pallas_call | solution.py:275
  309.9 21.0 %ffn.3.refs_0_.refs_16_.refs_17_.refs_1_ = bf16[2048,1152]{1,0:T(8,128)(2,1)} custom-call(bf16[256,2048]{1,0:T(8,128)(2,1)} %copy-done.9, bf16[256,2048]{1,0:T(8,128)(2,1)} %copy-done.20, bf16[256,2048]{1,0:T(8,128)(2,1)} %copy-done.21, bf16[256,2048]{1,0:T(8,128)(2,1)} %copy-done.23, bf16[256,2048]{1,0:T(8,128)(2,1)} %copy-done.22, ...), custom_call_target="tpu_custom_call" | custom-call | flops 1 | bytes 1 | tf_op jit(solution)/shard_map/ffn/pallas_call | solution.py:204
  330.9 7.8 %back.17 = bf16[1024,2048]{1,0:T(8,128)(2,1)} custom-call(bf16[2048,1152]{1,0:T(8,128)(2,1)} %ffn.3.refs_0_.refs_16_.refs_17_.refs_1_, bf16[2048,1152]{1,0:T(8,128)(2,1)} %all-gather.5.cloned.1.call-done.refs_16_.refs_1_.refs_3_, bf16[2048,2048]{1,0:T(8,128)(2,1)} %back.15.refs_2_), custom_call_target="tpu_custom_call" | custom-call | flops 1 | bytes 1 | tf_op jit(solution)/shard_map/back/pallas_call | solution.py:275
  338.9 8.2 %back.16 = bf16[1024,2048]{1,0:T(8,128)(2,1)} custom-call(bf16[2048,1152]{1,0:T(8,128)(2,1)} %ffn.3.refs_0_.refs_16_.refs_17_.refs_1_, bf16[2048,1152]{1,0:T(8,128)(2,1)} %all-gather.5.cloned.1.call-done.refs_16_.refs_1_.refs_3_, bf16[2048,2048]{1,0:T(8,128)(2,1)} %back.15.refs_2_), custom_call_target="tpu_custom_call" | custom-call | flops 1 | bytes 1 | tf_op jit(solution)/shard_map/back/pallas_call | solution.py:275
  347.1 3.3 slice_add_fusion
  351.6 16.5 %weight_grads.4 = bf16[2048,1152]{1,0:T(8,128)(2,1)} custom-call(bf16[256,2048]{1,0:T(8,128)(2,1)} %copy-done.9, bf16[256,2048]{1,0:T(8,128)(2,1)} %copy-done.20, bf16[256,2048]{1,0:T(8,128)(2,1)} %copy-done.21, bf16[256,2048]{1,0:T(8,128)(2,1)} %copy-done.23, bf16[256,2048]{1,0:T(8,128)(2,1)} %copy-done.22, bf16[256,2048]{1,0:T(8,128)(2,1)} %copy-done.24, ...), custom_call_target="tpu_custom_call" | custom-call | flops 20000000000 | bytes 1 | tf_op jit(solution)/shard_map/weight_grads/pallas_call | solution.py:240
  368.1 8.6 %collective-permute-done.30 = bf16[512,2048]{1,0:T(8,128)(2,1)} collective-permute-done((bf16[512,2048]{1,0:T(8,128)(2,1)S(1)}, bf16[512,2048]{1,0:T(8,128)(2,1)}, u32[]{:S(2)}, u32[]{:S(2)}) %collective-permute-start.30) | collective-permute-done | bytes 2097184 | tf_op jit(solution)/shard_map/ppermute | solution.py:58
  376.7 3.2 fusion.2.refs_0_
  380.7 6.8 %back.18 = bf16[512,2048]{1,0:T(8,128)(2,1)} custom-call(bf16[2048,1920]{1,0:T(8,128)(2,1)} %ffn.2.refs_16_.refs_17_.refs_0_, bf16[2048,1152]{1,0:T(8,128)(2,1)} %ffn.3.refs_0_.refs_16_.refs_17_.refs_1_, bf16[2048,1920]{1,0:T(8,128)(2,1)} %all-gather.3.cloned.1.call-done.refs_16_.refs_1_.refs_2_, ...), custom_call_target="tpu_custom_call" | custom-call | flops 7000000000 | bytes 1 | tf_op jit(solution)/shard_map/back/pallas_call | solution.py:275
  387.6 7.3 %collective-permute-done.31.refs_1_ = bf16[256,2048]{1,0:T(8,128)(2,1)S(1)} collective-permute-done((bf16[256,2048]{1,0:T(8,128)(2,1)S(1)}, bf16[256,2048]{1,0:T(8,128)(2,1)S(1)}, u32[]{:S(2)}, u32[]{:S(2)}) %collective-permute-start.31) | collective-permute-done | bytes 1048608 | tf_op jit(solution)/shard_map/ppermute | solution.py:54
  395.8 4.8 norm_back.2.refs_0_.refs_5_
  400.7 6.8 %back.20 = bf16[512,2048]{1,0:T(8,128)(2,1)} custom-call(bf16[2048,1920]{1,0:T(8,128)(2,1)} %ffn.2.refs_16_.refs_17_.refs_0_, bf16[2048,1152]{1,0:T(8,128)(2,1)} %ffn.3.refs_0_.refs_16_.refs_17_.refs_1_, bf16[2048,1920]{1,0:T(8,128)(2,1)} %all-gather.3.cloned.1.call-done.refs_16_.refs_1_.refs_2_, ...), custom_call_target="tpu_custom_call" | custom-call | flops 7000000000 | bytes 1 | tf_op jit(solution)/shard_map/back/pallas_call | solution.py:275
  411.1 10.0 %back.19 = bf16[1024,2048]{1,0:T(8,128)(2,1)} custom-call(bf16[2048,1920]{1,0:T(8,128)(2,1)} %ffn.2.refs_16_.refs_17_.refs_0_, bf16[2048,1152]{1,0:T(8,128)(2,1)} %ffn.3.refs_0_.refs_16_.refs_17_.refs_1_, bf16[2048,1920]{1,0:T(8,128)(2,1)} %all-gather.3.cloned.1.call-done.refs_16_.refs_1_.refs_2_, ...), custom_call_target="tpu_custom_call" | custom-call | flops 7000000000 | bytes 1 | tf_op jit(solution)/shard_map/back/pallas_call | solution.py:275
  421.0 5.1 broadcast_select_fusion
  426.1 7.8 %collective-permute-done.32.refs_1_ = bf16[256,2048]{1,0:T(8,128)(2,1)S(1)} collective-permute-done((bf16[256,2048]{1,0:T(8,128)(2,1)S(1)}, bf16[256,2048]{1,0:T(8,128)(2,1)S(1)}, u32[]{:S(2)}, u32[]{:S(2)}) %collective-permute-start.32) | collective-permute-done | bytes 1048608 | tf_op jit(solution)/shard_map/ppermute | solution.py:54
  435.6 13.2 %collective-permute-done.38.refs_3_ = bf16[256,2048]{1,0:T(8,128)(2,1)S(1)} collective-permute-done((bf16[256,2048]{1,0:T(8,128)(2,1)S(1)}, bf16[256,2048]{1,0:T(8,128)(2,1)S(1)}, u32[]{:S(2)}, u32[]{:S(2)}) %collective-permute-start.38) | collective-permute-done | bytes 1048608 | tf_op jit(solution)/shard_map/ppermute | solution.py:58
  456.0 9.6 %front.1.d_ref = bf16[2048,256]{1,0:T(8,128)(2,1)} custom-call(bf16[256,2048]{1,0:T(8,128)(2,1)} %norm_back.2.refs_0_.refs_5_, bf16[256,2048]{1,0:T(8,128)(2,1)} %copy-done.45, bf16[256,2048]{1,0:T(8,128)(2,1)} %copy-done.46, bf16[256,2048]{1,0:T(8,128)(2,1)} %copy-done.48, bf16[256,2048]{1,0:T(8,128)(2,1)} %copy-done.47, bf16[256,2048]{1,0:T(8,128)(2,1)} %copy-done.49, ...), custom_call_target="tpu_custom_call" | custom-call | flops 1 | bytes 1 | tf_op jit(solution)/shard_map/front/pallas_call | solution.py:301
  465.6 33.6 %attend_back.1.refs_0_.refs_1_.refs_10_ = bf16[2048,384]{1,0:T(8,128)(2,1)} custom-call(s32[8]{0:T(128)} %select_reduce_fusion.2.place, s32[8]{0:T(128)} %and_select_fusion.2.first, bf16[2048,2432]{1,0:T(8,128)(2,1)} %qkv.1.q_ref.kv_ref.refs_8_, bf16[2048,256]{1,0:T(8,128)(2,1)} %front.1.d_ref, f32[2048,384]{1,0:T(8,128)} %attend.1.refs_0_.h_ref.refs_9_, ...), custom_call_target="tpu_custom_call" | custom-call | flops 1 | bytes 1 | tf_op jit(solution)/shard_map/attend_back/pallas_call | solution.py:479
  503.4 4.1 back.23
  507.5 5.4 back.21
  512.9 4.3 back.22
  520.9 12.7 %weight_grads.5 = bf16[2048,640]{1,0:T(8,128)(2,1)} custom-call(bf16[256,2048]{1,0:T(8,128)(2,1)} %norm_back.2.refs_0_.refs_5_, bf16[256,2048]{1,0:T(8,128)(2,1)} %copy-done.45, bf16[256,2048]{1,0:T(8,128)(2,1)} %copy-done.46, bf16[256,2048]{1,0:T(8,128)(2,1)} %copy-done.48, bf16[256,2048]{1,0:T(8,128)(2,1)} %copy-done.47, bf16[256,2048]{1,0:T(8,128)(2,1)} %copy-done.49, ...), custom_call_target="tpu_custom_call" | custom-call | flops 20000000000 | bytes 1 | tf_op jit(solution)/shard_map/weight_grads/pallas_call | solution.py:240
  534.5 9.5 %collective-permute-done.47 = bf16[256,2048]{1,0:T(8,128)(2,1)} collective-permute-done((bf16[256,2048]{1,0:T(8,128)(2,1)}, bf16[256,2048]{1,0:T(8,128)(2,1)}, u32[]{:S(2)}, u32[]{:S(2)}) %collective-permute-start.47) | collective-permute-done | bytes 1048608 | tf_op jit(solution)/shard_map/ppermute | solution.py:50
  554.2 4.6 select_convert_fusion.1
  558.8 11.5 %collective-permute-done.50 = bf16[256,2048]{1,0:T(8,128)(2,1)} collective-permute-done((bf16[256,2048]{1,0:T(8,128)(2,1)}, bf16[256,2048]{1,0:T(8,128)(2,1)}, u32[]{:S(2)}, u32[]{:S(2)}) %collective-permute-start.50) | collective-permute-done | bytes 1048608 | tf_op jit(solution)/shard_map/ppermute | solution.py:46
  570.3 21.5 %collective-permute-done.49.refs_2_ = bf16[256,2048]{1,0:T(8,128)(2,1)} collective-permute-done((bf16[256,2048]{1,0:T(8,128)(2,1)S(1)}, bf16[256,2048]{1,0:T(8,128)(2,1)}, u32[]{:S(2)}, u32[]{:S(2)}) %collective-permute-start.49) | collective-permute-done | bytes 1048608 | tf_op jit(solution)/shard_map/ppermute | solution.py:54
  592.4 4.9 norm_back.3
  597.3 9.4 %collective-permute-start.57 = (bf16[256,2048]{1,0:T(8,128)(2,1)}, bf16[256,2048]{1,0:T(8,128)(2,1)S(1)}, u32[]{:S(2)}, u32[]{:S(2)}) collective-permute-start(bf16[256,2048]{1,0:T(8,128)(2,1)} %add_convert_fusion), channel_id=1, source_target_pairs={{0,1},{1,0},{2,3},{3,2},{4,5},{5,4},{6,7},{7,6},{8,9},{9,8},{10,11... | collective-permute-start | bytes 3145736 | tf_op jit(solution)/shard_map/ppermute | solution.py:42
  606.8 3.9 fusion.20
  634.0 5.6 collective-permute-done.54
  (335 shorter events, 143.0 us)
Async XLA Ops:
  7.2 228.9 %all-gather.3.cloned.1.call-start = ((), (), s32[]{:S(2)}) async-start(), calls=%async_computation.3 | async-start | bytes 9830400 | tf_op jit(solution)/shard_map/all_gather | solution.py:703
  12.2 20.5 %collective-permute-start = (bf16[528,640]{1,0:T(8,128)(2,1)}, bf16[528,640]{1,0:T(8,128)(2,1)}, u32[]{:S(2)}, u32[]{:S(2)}) collective-permute-start(bf16[528,640]{1,0:T(8,128)(2,1)} %fusion.6), channel_id=1, source_target_pairs={{0,8},{8,16},{16,24},{24,0},{1,9},{9,17},{17,25},{25,1},{2,10},{10... | collective-permute-start | bytes 2027528 | tf_op jit(solution)/shard_map/ppermute | solution.py:558
  17.5 15.2 %collective-permute-start.1 = (bf16[256,2048]{1,0:T(8,128)(2,1)}, bf16[256,2048]{1,0:T(8,128)(2,1)}, u32[]{:S(2)}, u32[]{:S(2)}) collective-permute-start(bf16[256,2048]{1,0:T(8,128)(2,1)} %constant_dynamic-slice_fusion.11.refs_0_.refs_3_), channel_id=1, source_target_pairs={{0,4},{1,3},{2,6},{3,1},{4,0},{5,7},{6,2},{7,5},{8,12},{9,11},{10,... | collective-permute-start | bytes 3145736 | tf_op jit(solution)/shard_map/ppermute | solution.py:54
  32.7 18.5 %collective-permute-start.2 = (bf16[528,640]{1,0:T(8,128)(2,1)}, bf16[528,640]{1,0:T(8,128)(2,1)}, u32[]{:S(2)}, u32[]{:S(2)}) collective-permute-start(bf16[528,640]{1,0:T(8,128)(2,1)} %collective-permute-done), channel_id=1, source_target_pairs={{0,8},{8,16},{16,24},{24,0},{1,9},{9,17},{17,25},{25,1},{2,10},{10... | collective-permute-start | bytes 2027528 | tf_op jit(solution)/shard_map/ppermute | solution.py:558
  34.2 21.1 %collective-permute-start.4 = (bf16[256,2048]{1,0:T(8,128)(2,1)}, bf16[256,2048]{1,0:T(8,128)(2,1)}, u32[]{:S(2)}, u32[]{:S(2)}) collective-permute-start(bf16[256,2048]{1,0:T(8,128)(2,1)} %constant_dynamic-slice_fusion.11.refs_0_.refs_3_), channel_id=1, source_target_pairs={{0,2},{1,5},{2,0},{3,7},{4,6},{5,1},{6,4},{7,3},{8,10},{9,13},{10,... | collective-permute-start | bytes 3145736 | tf_op jit(solution)/shard_map/ppermute | solution.py:58
  35.7 24.8 %collective-permute-start.5 = (bf16[256,2048]{1,0:T(8,128)(2,1)}, bf16[256,2048]{1,0:T(8,128)(2,1)}, u32[]{:S(2)}, u32[]{:S(2)}) collective-permute-start(bf16[256,2048]{1,0:T(8,128)(2,1)} %collective-permute-done.1.refs_1_), channel_id=1, source_target_pairs={{0,2},{1,5},{2,0},{3,7},{4,6},{5,1},{6,4},{7,3},{8,10},{9,13},{10,... | collective-permute-start | bytes 3145736 | tf_op jit(solution)/shard_map/ppermute | solution.py:58
  51.2 17.6 %collective-permute-start.3 = (bf16[528,640]{1,0:T(8,128)(2,1)}, bf16[528,640]{1,0:T(8,128)(2,1)}, u32[]{:S(2)}, u32[]{:S(2)}) collective-permute-start(bf16[528,640]{1,0:T(8,128)(2,1)} %collective-permute-done.2), channel_id=1, source_target_pairs={{0,8},{8,16},{16,24},{24,0},{1,9},{9,17},{17,25},{25,1},{2,10},{10... | collective-permute-start | bytes 2027528 | tf_op jit(solution)/shard_map/ppermute | solution.py:558
  68.8 241.1 %all-gather.5.cloned.1.call-start = ((), (), s32[]{:S(2)}) async-start(), calls=%async_computation.4 | async-start | bytes 5898240 | tf_op jit(solution)/shard_map/all_gather | solution.py:703
  78.0 25.5 %collective-permute-start.10 = (bf16[256,2048]{1,0:T(8,128)(2,1)S(1)}, bf16[256,2048]{1,0:T(8,128)(2,1)}, u32[]{:S(2)}, u32[]{:S(2)}) collective-permute-start(bf16[256,2048]{1,0:T(8,128)(2,1)S(1)} %constant_dynamic-slice_fusion.6.refs_8_.refs_4_), channel_id=1, source_target_pairs={{0,4},{1,3},{2,6},{3,1},{4,0},{5,7},{6,2},{7,5},{8,12},{9,11},{10,... | collective-permute-start | bytes 3145736 | tf_op jit(solution)/shard_map/ppermute | solution.py:54
  79.3 24.2 %collective-permute-start.11 = (bf16[256,2048]{1,0:T(8,128)(2,1)S(1)}, bf16[256,2048]{1,0:T(8,128)(2,1)}, u32[]{:S(2)}, u32[]{:S(2)}) collective-permute-start(bf16[256,2048]{1,0:T(8,128)(2,1)S(1)} %constant_dynamic-slice_fusion.6.refs_8_.refs_4_), channel_id=1, source_target_pairs={{0,2},{1,5},{2,0},{3,7},{4,6},{5,1},{6,4},{7,3},{8,10},{9,13},{10,... | collective-permute-start | bytes 3145736 | tf_op jit(solution)/shard_map/ppermute | solution.py:58
  80.5 47.8 %collective-permute-start.13 = (bf16[256,2048]{1,0:T(8,128)(2,1)S(1)}, bf16[256,2048]{1,0:T(8,128)(2,1)}, u32[]{:S(2)}, u32[]{:S(2)}) collective-permute-start(bf16[256,2048]{1,0:T(8,128)(2,1)S(1)} %constant_dynamic-slice_fusion.6.refs_8_.refs_4_), channel_id=1, source_target_pairs={{0,1},{1,0},{2,3},{3,2},{4,5},{5,4},{6,7},{7,6},{8,9},{9,8},{10,11... | collective-permute-start | bytes 3145736 | tf_op jit(solution)/shard_map/ppermute | solution.py:42
  103.5 24.8 %collective-permute-start.12 = (bf16[256,2048]{1,0:T(8,128)(2,1)}, bf16[256,2048]{1,0:T(8,128)(2,1)}, u32[]{:S(2)}, u32[]{:S(2)}) collective-permute-start(bf16[256,2048]{1,0:T(8,128)(2,1)} %collective-permute-done.10.refs_9_), channel_id=1, source_target_pairs={{0,2},{1,5},{2,0},{3,7},{4,6},{5,1},{6,4},{7,3},{8,10},{9,13},{10,... | collective-permute-start | bytes 3145736 | tf_op jit(solution)/shard_map/ppermute | solution.py:58
  104.6 23.7 %collective-permute-start.14 = (bf16[256,2048]{1,0:T(8,128)(2,1)}, bf16[256,2048]{1,0:T(8,128)(2,1)}, u32[]{:S(2)}, u32[]{:S(2)}) collective-permute-start(bf16[256,2048]{1,0:T(8,128)(2,1)} %collective-permute-done.10.refs_9_), channel_id=1, source_target_pairs={{0,1},{1,0},{2,3},{3,2},{4,5},{5,4},{6,7},{7,6},{8,9},{9,8},{10,11... | collective-permute-start | bytes 3145736 | tf_op jit(solution)/shard_map/ppermute | solution.py:42
  105.0 23.3 %collective-permute-start.15 = (bf16[256,2048]{1,0:T(8,128)(2,1)}, bf16[256,2048]{1,0:T(8,128)(2,1)}, u32[]{:S(2)}, u32[]{:S(2)}) collective-permute-start(bf16[256,2048]{1,0:T(8,128)(2,1)} %collective-permute-done.11.refs_10_), channel_id=1, source_target_pairs={{0,1},{1,0},{2,3},{3,2},{4,5},{5,4},{6,7},{7,6},{8,9},{9,8},{10,11... | collective-permute-start | bytes 3145736 | tf_op jit(solution)/shard_map/ppermute | solution.py:42
  138.7 22.2 %collective-permute-start.17 = (bf16[512,2048]{1,0:T(8,128)(2,1)}, bf16[512,2048]{1,0:T(8,128)(2,1)}, u32[]{:S(2)}, u32[]{:S(2)}) collective-permute-start(bf16[512,2048]{1,0:T(8,128)(2,1)} %back.13), channel_id=1, source_target_pairs={{0,1},{1,0},{2,3},{3,2},{4,5},{5,4},{6,7},{7,6},{8,9},{9,8},{10,11... | collective-permute-start | bytes 6291464 | tf_op jit(solution)/shard_map/ppermute | solution.py:42
  145.8 15.1 %collective-permute-start.19 = (bf16[256,2048]{1,0:T(8,128)(2,1)}, bf16[256,2048]{1,0:T(8,128)(2,1)}, u32[]{:S(2)}, u32[]{:S(2)}) collective-permute-start(bf16[256,2048]{1,0:T(8,128)(2,1)} %get-tuple-element.156), channel_id=1, source_target_pairs={{0,2},{1,5},{2,0},{3,7},{4,6},{5,1},{6,4},{7,3},{8,10},{9,13},{10,... | collective-permute-start | bytes 3145736 | tf_op jit(solution)/shard_map/ppermute | solution.py:58
  163.9 25.9 %collective-permute-start.20 = (bf16[256,2048]{1,0:T(8,128)(2,1)S(1)}, bf16[256,2048]{1,0:T(8,128)(2,1)}, u32[]{:S(2)}, u32[]{:S(2)}) collective-permute-start(bf16[256,2048]{1,0:T(8,128)(2,1)S(1)} %get-tuple-element.93), channel_id=1, source_target_pairs={{0,2},{1,5},{2,0},{3,7},{4,6},{5,1},{6,4},{7,3},{8,10},{9,13},{10,... | collective-permute-start | bytes 3145736 | tf_op jit(solution)/shard_map/ppermute | solution.py:58
  165.4 23.1 %collective-permute-start.21 = (bf16[256,2048]{1,0:T(8,128)(2,1)}, bf16[256,2048]{1,0:T(8,128)(2,1)S(1)}, u32[]{:S(2)}, u32[]{:S(2)}) collective-permute-start(bf16[256,2048]{1,0:T(8,128)(2,1)} %fusion.5), channel_id=1, source_target_pairs={{0,4},{1,3},{2,6},{3,1},{4,0},{5,7},{6,2},{7,5},{8,12},{9,11},{10,... | collective-permute-start | bytes 3145736 | tf_op jit(solution)/shard_map/ppermute | solution.py:54
  167.1 283.6 %reduce-scatter.4.cloned.1.call-start = ((), (), s32[]{:S(2)}) async-start(), calls=%async_computation.5 | async-start | bytes 9830400 | tf_op jit(solution)/shard_map/reduce_scatter | solution.py:736
  193.4 25.8 %collective-permute-start.22 = (bf16[256,2048]{1,0:T(8,128)(2,1)S(1)}, bf16[256,2048]{1,0:T(8,128)(2,1)S(1)}, u32[]{:S(2)}, u32[]{:S(2)}) collective-permute-start(bf16[256,2048]{1,0:T(8,128)(2,1)S(1)} %multiply_convert_fusion.refs_0_), channel_id=1, source_target_pairs={{0,4},{1,3},{2,6},{3,1},{4,0},{5,7},{6,2},{7,5},{8,12},{9,11},{10,... | collective-permute-start | bytes 3145736 | tf_op jit(solution)/shard_map/ppermute | solution.py:54
  194.4 25.0 %collective-permute-start.23 = (bf16[256,2048]{1,0:T(8,128)(2,1)S(1)}, bf16[256,2048]{1,0:T(8,128)(2,1)S(1)}, u32[]{:S(2)}, u32[]{:S(2)}) collective-permute-start(bf16[256,2048]{1,0:T(8,128)(2,1)S(1)} %multiply_convert_fusion.refs_0_), channel_id=1, source_target_pairs={{0,2},{1,5},{2,0},{3,7},{4,6},{5,1},{6,4},{7,3},{8,10},{9,13},{10,... | collective-permute-start | bytes 3145736 | tf_op jit(solution)/shard_map/ppermute | solution.py:58
  195.7 25.2 %collective-permute-start.25 = (bf16[256,2048]{1,0:T(8,128)(2,1)S(1)}, bf16[256,2048]{1,0:T(8,128)(2,1)S(1)}, u32[]{:S(2)}, u32[]{:S(2)}) collective-permute-start(bf16[256,2048]{1,0:T(8,128)(2,1)S(1)} %multiply_convert_fusion.refs_0_), channel_id=1, source_target_pairs={{0,1},{1,0},{2,3},{3,2},{4,5},{5,4},{6,7},{7,6},{8,9},{9,8},{10,11... | collective-permute-start | bytes 3145736 | tf_op jit(solution)/shard_map/ppermute | solution.py:42
  219.3 14.8 %collective-permute-start.24 = (bf16[256,2048]{1,0:T(8,128)(2,1)S(1)}, bf16[256,2048]{1,0:T(8,128)(2,1)S(1)}, u32[]{:S(2)}, u32[]{:S(2)}) collective-permute-start(bf16[256,2048]{1,0:T(8,128)(2,1)S(1)} %collective-permute-done.22.refs_1_), channel_id=1, source_target_pairs={{0,2},{1,5},{2,0},{3,7},{4,6},{5,1},{6,4},{7,3},{8,10},{9,13},{10,... | collective-permute-start | bytes 3145736 | tf_op jit(solution)/shard_map/ppermute | solution.py:58
  220.4 15.7 %collective-permute-start.27 = (bf16[256,2048]{1,0:T(8,128)(2,1)S(1)}, bf16[256,2048]{1,0:T(8,128)(2,1)}, u32[]{:S(2)}, u32[]{:S(2)}) collective-permute-start(bf16[256,2048]{1,0:T(8,128)(2,1)S(1)} %collective-permute-done.23.refs_2_), channel_id=1, source_target_pairs={{0,1},{1,0},{2,3},{3,2},{4,5},{5,4},{6,7},{7,6},{8,9},{9,8},{10,11... | collective-permute-start | bytes 3145736 | tf_op jit(solution)/shard_map/ppermute | solution.py:42
  293.4 240.3 %reduce-scatter.6.cloned.1.call-start = ((), (), s32[]{:S(2)}) async-start(), calls=%async_computation.6 | async-start | bytes 5898240 | tf_op jit(solution)/shard_map/reduce_scatter | solution.py:736
  350.5 26.2 %collective-permute-start.30 = (bf16[512,2048]{1,0:T(8,128)(2,1)S(1)}, bf16[512,2048]{1,0:T(8,128)(2,1)}, u32[]{:S(2)}, u32[]{:S(2)}) collective-permute-start(bf16[512,2048]{1,0:T(8,128)(2,1)S(1)} %slice_add_fusion), channel_id=1, source_target_pairs={{0,2},{1,5},{2,0},{3,7},{4,6},{5,1},{6,4},{7,3},{8,10},{9,13},{10,... | collective-permute-start | bytes 6291464 | tf_op jit(solution)/shard_map/ppermute | solution.py:58
  380.0 14.9 %collective-permute-start.31 = (bf16[256,2048]{1,0:T(8,128)(2,1)S(1)}, bf16[256,2048]{1,0:T(8,128)(2,1)S(1)}, u32[]{:S(2)}, u32[]{:S(2)}) collective-permute-start(bf16[256,2048]{1,0:T(8,128)(2,1)S(1)} %slice.217), channel_id=1, source_target_pairs={{0,4},{1,3},{2,6},{3,1},{4,0},{5,7},{6,2},{7,5},{8,12},{9,11},{10,... | collective-permute-start | bytes 3145736 | tf_op jit(solution)/shard_map/ppermute | solution.py:54
  387.6 33.5 %collective-permute-start.35 = (bf16[512,2048]{1,0:T(8,128)(2,1)}, bf16[512,2048]{1,0:T(8,128)(2,1)}, u32[]{:S(2)}, u32[]{:S(2)}) collective-permute-start(bf16[512,2048]{1,0:T(8,128)(2,1)} %back.18), channel_id=1, source_target_pairs={{0,1},{1,0},{2,3},{3,2},{4,5},{5,4},{6,7},{7,6},{8,9},{9,8},{10,11... | collective-permute-start | bytes 6291464 | tf_op jit(solution)/shard_map/ppermute | solution.py:42
  407.5 214.2 %reduce-scatter.8.cloned.1.call-start = ((), (), s32[]{:S(2)}) async-start(), calls=%async_computation.7 | async-start | bytes 3276800 | tf_op jit(solution)/shard_map/reduce_scatter | solution.py:783
  408.7 25.2 %collective-permute-start.32 = (bf16[256,2048]{1,0:T(8,128)(2,1)S(1)}, bf16[256,2048]{1,0:T(8,128)(2,1)S(1)}, u32[]{:S(2)}, u32[]{:S(2)}) collective-permute-start(bf16[256,2048]{1,0:T(8,128)(2,1)S(1)} %copy-done.10), channel_id=1, source_target_pairs={{0,4},{1,3},{2,6},{3,1},{4,0},{5,7},{6,2},{7,5},{8,12},{9,11},{10,... | collective-permute-start | bytes 3145736 | tf_op jit(solution)/shard_map/ppermute | solution.py:54
  409.3 24.6 %collective-permute-start.33 = (bf16[256,2048]{1,0:T(8,128)(2,1)S(1)}, bf16[256,2048]{1,0:T(8,128)(2,1)S(1)}, u32[]{:S(2)}, u32[]{:S(2)}) collective-permute-start(bf16[256,2048]{1,0:T(8,128)(2,1)S(1)} %copy-done.10), channel_id=1, source_target_pairs={{0,2},{1,5},{2,0},{3,7},{4,6},{5,1},{6,4},{7,3},{8,10},{9,13},{10,... | collective-permute-start | bytes 3145736 | tf_op jit(solution)/shard_map/ppermute | solution.py:58
  411.1 24.5 %collective-permute-start.39 = (bf16[256,2048]{1,0:T(8,128)(2,1)S(1)}, bf16[256,2048]{1,0:T(8,128)(2,1)S(1)}, u32[]{:S(2)}, u32[]{:S(2)}) collective-permute-start(bf16[256,2048]{1,0:T(8,128)(2,1)S(1)} %copy-done.10), channel_id=1, source_target_pairs={{0,1},{1,0},{2,3},{3,2},{4,5},{5,4},{6,7},{7,6},{8,9},{9,8},{10,11... | collective-permute-start | bytes 3145736 | tf_op jit(solution)/shard_map/ppermute | solution.py:42
  433.9 14.9 %collective-permute-start.38 = (bf16[256,2048]{1,0:T(8,128)(2,1)S(1)}, bf16[256,2048]{1,0:T(8,128)(2,1)S(1)}, u32[]{:S(2)}, u32[]{:S(2)}) collective-permute-start(bf16[256,2048]{1,0:T(8,128)(2,1)S(1)} %collective-permute-done.32.refs_1_), channel_id=1, source_target_pairs={{0,2},{1,5},{2,0},{3,7},{4,6},{5,1},{6,4},{7,3},{8,10},{9,13},{10,... | collective-permute-start | bytes 3145736 | tf_op jit(solution)/shard_map/ppermute | solution.py:58
  435.1 15.7 %collective-permute-start.41 = (bf16[256,2048]{1,0:T(8,128)(2,1)S(1)}, bf16[256,2048]{1,0:T(8,128)(2,1)}, u32[]{:S(2)}, u32[]{:S(2)}) collective-permute-start(bf16[256,2048]{1,0:T(8,128)(2,1)S(1)} %collective-permute-done.33.refs_2_), channel_id=1, source_target_pairs={{0,1},{1,0},{2,3},{3,2},{4,5},{5,4},{6,7},{7,6},{8,9},{9,8},{10,11... | collective-permute-start | bytes 3145736 | tf_op jit(solution)/shard_map/ppermute | solution.py:42
  450.7 49.7 %collective-permute-start.43 = (bf16[512,1920]{1,0:T(8,128)(2,1)}, bf16[512,1920]{1,0:T(8,128)(2,1)S(1)}, u32[]{:S(2)}, u32[]{:S(2)}) collective-permute-start(bf16[512,1920]{1,0:T(8,128)(2,1)} %reduce-scatter.4.cloned.1.call-done), channel_id=1, source_target_pairs={{0,4},{4,0},{1,5},{5,1},{2,6},{6,2},{3,7},{7,3},{8,12},{12,8},{9,1... | collective-permute-start | bytes 5898248 | tf_op jit(solution)/shard_map/ppermute | solution.py:50
  452.1 47.1 %collective-permute-start.36 = (bf16[256,2048]{1,0:T(8,128)(2,1)}, bf16[256,2048]{1,0:T(8,128)(2,1)S(1)}, u32[]{:S(2)}, u32[]{:S(2)}) collective-permute-start(bf16[256,2048]{1,0:T(8,128)(2,1)} %get-tuple-element.107), channel_id=1, source_target_pairs={{0,2},{2,0},{1,3},{3,1},{4,6},{6,4},{5,7},{7,5},{8,10},{10,8},{9,1... | collective-permute-start | bytes 3145736 | tf_op jit(solution)/shard_map/ppermute | solution.py:46
  452.5 47.9 %collective-permute-start.37 = (bf16[256,2048]{1,0:T(8,128)(2,1)}, bf16[256,2048]{1,0:T(8,128)(2,1)S(1)}, u32[]{:S(2)}, u32[]{:S(2)}) collective-permute-start(bf16[256,2048]{1,0:T(8,128)(2,1)} %get-tuple-element.108), channel_id=1, source_target_pairs={{0,2},{2,0},{1,3},{3,1},{4,6},{6,4},{5,7},{7,5},{8,10},{10,8},{9,1... | collective-permute-start | bytes 3145736 | tf_op jit(solution)/shard_map/ppermute | solution.py:46
  517.2 29.9 %collective-permute-start.44 = (bf16[512,2048]{1,0:T(8,128)(2,1)}, bf16[512,2048]{1,0:T(8,128)(2,1)}, u32[]{:S(2)}, u32[]{:S(2)}) collective-permute-start(bf16[512,2048]{1,0:T(8,128)(2,1)} %back.22), channel_id=1, source_target_pairs={{0,1},{1,0},{2,3},{3,2},{4,5},{5,4},{6,7},{7,6},{8,9},{9,8},{10,11... | collective-permute-start | bytes 6291464 | tf_op jit(solution)/shard_map/ppermute | solution.py:42
  517.6 26.3 %collective-permute-start.47 = (bf16[256,2048]{1,0:T(8,128)(2,1)}, bf16[256,2048]{1,0:T(8,128)(2,1)}, u32[]{:S(2)}, u32[]{:S(2)}) collective-permute-start(bf16[256,2048]{1,0:T(8,128)(2,1)} %add.380), channel_id=1, source_target_pairs={{0,4},{4,0},{1,5},{5,1},{2,6},{6,2},{3,7},{7,3},{8,12},{12,8},{9,1... | collective-permute-start | bytes 3145736 | tf_op jit(solution)/shard_map/ppermute | solution.py:50
  519.9 27.1 %collective-permute-start.46 = (bf16[256,2048]{1,0:T(8,128)(2,1)}, bf16[256,2048]{1,0:T(8,128)(2,1)}, u32[]{:S(2)}, u32[]{:S(2)}) collective-permute-start(bf16[256,2048]{1,0:T(8,128)(2,1)} %get-tuple-element.150), channel_id=1, source_target_pairs={{0,2},{1,5},{2,0},{3,7},{4,6},{5,1},{6,4},{7,3},{8,10},{9,13},{10,... | collective-permute-start | bytes 3145736 | tf_op jit(solution)/shard_map/ppermute | solution.py:58
  533.7 36.6 %collective-permute-start.51 = (bf16[512,1152]{1,0:T(8,128)(2,1)}, bf16[512,1152]{1,0:T(8,128)(2,1)}, u32[]{:S(2)}, u32[]{:S(2)}) collective-permute-start(bf16[512,1152]{1,0:T(8,128)(2,1)} %reduce-scatter.6.cloned.1.call-done), channel_id=1, source_target_pairs={{0,4},{4,0},{1,5},{5,1},{2,6},{6,2},{3,7},{7,3},{8,12},{12,8},{9,1... | collective-permute-start | bytes 3538952 | tf_op jit(solution)/shard_map/ppermute | solution.py:50
  546.7 23.6 %collective-permute-start.50 = (bf16[256,2048]{1,0:T(8,128)(2,1)}, bf16[256,2048]{1,0:T(8,128)(2,1)}, u32[]{:S(2)}, u32[]{:S(2)}) collective-permute-start(bf16[256,2048]{1,0:T(8,128)(2,1)} %add_convert_fusion), channel_id=1, source_target_pairs={{0,2},{2,0},{1,3},{3,1},{4,6},{6,4},{5,7},{7,5},{8,10},{10,8},{9,1... | collective-permute-start | bytes 3145736 | tf_op jit(solution)/shard_map/ppermute | solution.py:46
  550.2 41.6 %collective-permute-start.49 = (bf16[256,2048]{1,0:T(8,128)(2,1)S(1)}, bf16[256,2048]{1,0:T(8,128)(2,1)}, u32[]{:S(2)}, u32[]{:S(2)}) collective-permute-start(bf16[256,2048]{1,0:T(8,128)(2,1)S(1)} %get-tuple-element.124), channel_id=1, source_target_pairs={{0,4},{1,3},{2,6},{3,1},{4,0},{5,7},{6,2},{7,5},{8,12},{9,11},{10,... | collective-permute-start | bytes 3145736 | tf_op jit(solution)/shard_map/ppermute | solution.py:54
  551.5 41.0 %collective-permute-start.48 = (bf16[256,2048]{1,0:T(8,128)(2,1)}, bf16[256,2048]{1,0:T(8,128)(2,1)}, u32[]{:S(2)}, u32[]{:S(2)}) collective-permute-start(bf16[256,2048]{1,0:T(8,128)(2,1)} %get-tuple-element.123), channel_id=1, source_target_pairs={{0,2},{1,5},{2,0},{3,7},{4,6},{5,1},{6,4},{7,3},{8,10},{9,13},{10,... | collective-permute-start | bytes 3145736 | tf_op jit(solution)/shard_map/ppermute | solution.py:58
  597.3 18.7 %collective-permute-start.57 = (bf16[256,2048]{1,0:T(8,128)(2,1)}, bf16[256,2048]{1,0:T(8,128)(2,1)S(1)}, u32[]{:S(2)}, u32[]{:S(2)}) collective-permute-start(bf16[256,2048]{1,0:T(8,128)(2,1)} %add_convert_fusion), channel_id=1, source_target_pairs={{0,1},{1,0},{2,3},{3,2},{4,5},{5,4},{6,7},{7,6},{8,9},{9,8},{10,11... | collective-permute-start | bytes 3145736 | tf_op jit(solution)/shard_map/ppermute | solution.py:42
  613.6 29.7 %collective-permute-start.52 = (bf16[256,2048]{1,0:T(8,128)(2,1)}, bf16[256,2048]{1,0:T(8,128)(2,1)}, u32[]{:S(2)}, u32[]{:S(2)}) collective-permute-start(bf16[256,2048]{1,0:T(8,128)(2,1)} %norm_back.3), channel_id=1, source_target_pairs={{0,2},{2,0},{1,3},{3,1},{4,6},{6,4},{5,7},{7,5},{8,10},{10,8},{9,1... | collective-permute-start | bytes 3145736 | tf_op jit(solution)/shard_map/ppermute | solution.py:46
  614.0 36.9 %collective-permute-start.59 = (bf16[256,2048]{1,0:T(8,128)(2,1)}, bf16[256,2048]{1,0:T(8,128)(2,1)}, u32[]{:S(2)}, u32[]{:S(2)}) collective-permute-start(bf16[256,2048]{1,0:T(8,128)(2,1)} %norm_back.3), channel_id=1, source_target_pairs={{0,1},{1,0},{2,3},{3,2},{4,5},{5,4},{6,7},{7,6},{8,9},{9,8},{10,11... | collective-permute-start | bytes 3145736 | tf_op jit(solution)/shard_map/ppermute | solution.py:42
  621.7 21.6 %collective-permute-start.56 = (bf16[512,640]{1,0:T(8,128)(2,1)}, bf16[512,640]{1,0:T(8,128)(2,1)S(1)}, u32[]{:S(2)}, u32[]{:S(2)}) collective-permute-start(bf16[512,640]{1,0:T(8,128)(2,1)} %reduce-scatter.8.cloned.1.call-done), channel_id=1, source_target_pairs={{0,4},{4,0},{1,5},{5,1},{2,6},{6,2},{3,7},{7,3},{8,12},{12,8},{9,1... | collective-permute-start | bytes 1966088 | tf_op jit(solution)/shard_map/ppermute | solution.py:50
  (82 other events, 868.4 us)
Sparse Core Ops, SparseCore 0:
  68.9 138.7 all-gather.2
  209.9 87.6 all-gather.4
  299.8 134.6 reduce-scatter.3
  436.7 85.7 reduce-scatter.5
  533.8 49.6 reduce-scatter.7

commit v11 on v9

--- a/solution.py
+++ b/solution.py
@@ -776,16 +776,25 @@
     for part in range(1, len(chunks)):
         reduced[part] = after(reduced[part], attn_grad)
         other_reduced.append(swap_x(reduced[part]))
-    normed_parts = last_parts(*normed_first, beside=[result_beside, *other_reduced[1:]])
+    halves = [both_halves(mine, other, ctx) for mine, other in zip(reduced, other_reduced)]
+
+    def ffn_out(which):
+        return jnp.concatenate(
+            [
+                halves[part][side][:, which * chunk : (which + 1) * chunk]
+                for side in range(2)
+                for part, chunk in enumerate(chunks)
+            ],
+            axis=1,
+        )
+
+    ffn_grads = [ffn_out(which) for which in range(3)]
+    result = share_in_ctx(result_own, result_beside, y, core)
+    normed_parts = last_parts(*normed_first, beside=[result, *ffn_grads])
     tokens_grad_own = norm_back(normed_parts, tokens_low, gain_one, d_own)
     attn_reduced = lax.psum_scatter(attn_grad, "fsdp", scatter_dimension=0, tiled=True)
     attn_reduced = after(attn_reduced, tokens_grad_own)
     other_attn = swap_x(attn_reduced)
-    result_own, result_beside, _ = lax.optimization_barrier(
-        (result_own, result_beside, tokens_grad_own)
-    )
-    result = share_in_ctx(result_own, result_beside, y, core)
-
     def gain_part(pairs):
         return sum(jnp.sum(mine.astype(F32) * grad.astype(F32), axis=1) for mine, grad in pairs)
 
@@ -804,20 +813,6 @@
     gain_sums = gain_sums + swap_y(gain_sums)
     gain_sums = gain_sums + swap_x(gain_sums)
 
-    other_reduced[-1] = after(other_reduced[-1], attn_reduced)
-    halves = [both_halves(mine, other, ctx) for mine, other in zip(reduced, other_reduced)]
-
-    def ffn_out(which):
-        return jnp.concatenate(
-            [
-                halves[part][side][:, which * chunk : (which + 1) * chunk]
-                for side in range(2)
-                for part, chunk in enumerate(chunks)
-            ],
-            axis=1,
-        )
-
-    ffn_grads = [ffn_out(which) for which in range(3)]
     tokens_grad_beside, gain_sums, other_attn, result, *ffn_grads = lax.optimization_barrier(
         (swap_y(tokens_grad_own), gain_sums, other_attn, result, *ffn_grads)
     )

time: 669 us -> 657 us (0.982)
  waiting for transfers between devices: 226 us -> 193 us
  starting transfers between devices: 46.1 us -> 63.4 us
    ppermute x7, waiting for transfers between devices: 91.7 us -> 73.6 us  [swap_first(): return lax.ppermute(v, ('ctx', 'tp'), FIRST)]
    ppermute x28, starting transfers between devices: 6.35 us -> 21.9 us  [swap_core(): return lax.ppermute(v, 'tp', CORE)]
    ppermute x5, waiting for transfers between devices: 23.7 us -> 12.8 us  [swap_x(): return lax.ppermute(v, 'ctx', PAIR)]
    unnamed x133 -> x137, local copies, waits for them, and re-layouts: 14 us -> 14.1 us
  transfers between devices with their start and end apart: 66 -> 66, of which waited for: 27 -> 26; matrix products, arithmetic and copies ran while one was open for 13% -> 14% of each run, Pallas kernels for 40% -> 41%
where the time goes in v11:
time: 657 us; the launch traced here: 649 us
  Pallas kernels  266 us (40%)
  waiting for transfers between devices  193 us (29%)
  other arithmetic  70.8 us (11%)
  starting transfers between devices  63.4 us (10%)
  local copies, waits for them, and re-layouts  40.3 us (6%)
  between operations  15.2 us (2%)
    pallas_call x12, Pallas kernels, back_product(): pl.pallas_call(functools.partial(back_kernel, len(terms)), out_shape=jax....  79 us
    ppermute x7, waiting for transfers between devices, swap_first(): return lax.ppermute(v, ('ctx', 'tp'), FIRST)  73.6 us
    pallas_call x3, Pallas kernels, weight_grads(): pl.pallas_call(functools.partial(grads_kernel, len(x), len(y)), out_shape...  50.9 us
    ppermute x13, waiting for transfers between devices, swap_second(): return lax.ppermute(v, ('ctx', 'tp'), SECOND)  46.4 us
    pallas_call x2, Pallas kernels, ffn_chunk(): pl.pallas_call(functools.partial(ffn_kernel, len(x)), out_shape=jax.Shape...  43.5 us
    pallas_call x1, Pallas kernels, attend_back(): pl.pallas_call(attend_back_kernel, out_shape=jax.ShapeDtypeStruct((rows,...  35 us
    ppermute x3, waiting for transfers between devices, ring_over(): pieces.append(lax.ppermute(sent, 'fsdp', cycle))  30.9 us
    pallas_call x1, Pallas kernels, attend(): pl.pallas_call(attend_kernel, out_shape=jax.ShapeDtypeStruct((rows, q_wid...  22.7 us
  transfers between devices with their start and end apart: 66, of which 26 were waited for; matrix products, arithmetic and copies ran while one was open for 14% of the time, Pallas kernels for 41%

profile of v11, /device:TPU:0, one launch (start us, length us, event | category | flops | bytes accessed | tf_op | source)
XLA Modules:
  0.0 648.6 jit_solution(3823629737518272571)
XLA Ops:
  20.7 5.6 negate_select_fusion
  26.3 5.7 collective-permute-done
  34.6 15.9 %collective-permute-done.2 = bf16[528,640]{1,0:T(8,128)(2,1)} collective-permute-done((bf16[528,640]{1,0:T(8,128)(2,1)}, bf16[528,640]{1,0:T(8,128)(2,1)}, u32[]{:S(2)}, u32[]{:S(2)}) %collective-permute-start.2) | collective-permute-done | bytes 675872 | tf_op jit(solution)/shard_map/ppermute | solution.py:558
  58.7 9.3 %collective-permute-done.3 = bf16[528,640]{1,0:T(8,128)(2,1)} collective-permute-done((bf16[528,640]{1,0:T(8,128)(2,1)}, bf16[528,640]{1,0:T(8,128)(2,1)}, u32[]{:S(2)}, u32[]{:S(2)}) %collective-permute-start.3) | collective-permute-done | bytes 675872 | tf_op jit(solution)/shard_map/ppermute | solution.py:558
  79.8 15.3 %qkv.1.q_ref.kv_ref.refs_8_ = bf16[2048,2432]{1,0:T(8,128)(2,1)} custom-call(bf16[256,2048]{1,0:T(8,128)(2,1)} %copy-done.9, bf16[256,2048]{1,0:T(8,128)(2,1)} %collective-permute-done.1.refs_1_, bf16[256,2048]{1,0:T(8,128)(2,1)} %collective-permute-done.4.refs_2_, bf16[256,2048]{1,0:T(8,128)(2,1)} %collective-permute-done.5.refs_3_, ...), custom_call_target="tpu_custom_call" | custom-call | flops 1 | bytes 1 | tf_op jit(solution)/shard_map/qkv/pallas_call | solution.py:165
  95.2 7.6 %collective-permute-done.10.refs_9_ = bf16[256,2048]{1,0:T(8,128)(2,1)S(1)} collective-permute-done((bf16[256,2048]{1,0:T(8,128)(2,1)S(1)}, bf16[256,2048]{1,0:T(8,128)(2,1)S(1)}, u32[]{:S(2)}, u32[]{:S(2)}) %collective-permute-start.10) | collective-permute-done | bytes 1048608 | tf_op jit(solution)/shard_map/ppermute | solution.py:54
  105.7 22.7 %attend.1.refs_0_.h_ref.refs_9_ = f32[2048,384]{1,0:T(8,128)} custom-call(s32[8]{0:T(128)} %select_reduce_fusion.2.place, s32[8]{0:T(128)} %and_select_fusion.2.first, bf16[2048,2432]{1,0:T(8,128)(2,1)} %qkv.1.q_ref.kv_ref.refs_8_, bf16[2048,2432]{1,0:T(8,128)(2,1)} %qkv.1.q_ref.kv_ref.refs_8_, s32[2048,1]{1,0:T(8,128)} %copy.28.start_ref), custom_call_target="tpu_custom_call" | custom-call | flops 1 | bytes 1 | tf_op jit(solution)/shard_map/attend/pallas_call | solution.py:382
  131.4 3.8 back.14
  135.6 3.5 back.13
  140.8 4.3 back.12
  149.0 13.3 %collective-permute-done.19 = bf16[256,2048]{1,0:T(8,128)(2,1)S(1)} collective-permute-done((bf16[256,2048]{1,0:T(8,128)(2,1)S(1)}, bf16[256,2048]{1,0:T(8,128)(2,1)S(1)}, u32[]{:S(2)}, u32[]{:S(2)}) %collective-permute-start.19) | collective-permute-done | bytes 1048608 | tf_op jit(solution)/shard_map/ppermute | solution.py:58
  165.9 24.0 %collective-permute-done.21 = bf16[256,2048]{1,0:T(8,128)(2,1)} collective-permute-done((bf16[256,2048]{1,0:T(8,128)(2,1)S(1)}, bf16[256,2048]{1,0:T(8,128)(2,1)}, u32[]{:S(2)}, u32[]{:S(2)}) %collective-permute-start.21) | collective-permute-done | bytes 1048608 | tf_op jit(solution)/shard_map/ppermute | solution.py:54
  189.8 3.3 multiply_reduce_fusion.2
  195.4 23.1 %collective-permute-done.22.refs_1_ = bf16[256,2048]{1,0:T(8,128)(2,1)S(1)} collective-permute-done((bf16[256,2048]{1,0:T(8,128)(2,1)S(1)}, bf16[256,2048]{1,0:T(8,128)(2,1)S(1)}, u32[]{:S(2)}, u32[]{:S(2)}) %collective-permute-start.22) | collective-permute-done | bytes 1048608 | tf_op jit(solution)/shard_map/ppermute | solution.py:54
  220.7 12.7 %collective-permute-done.24.refs_3_ = bf16[256,2048]{1,0:T(8,128)(2,1)S(1)} collective-permute-done((bf16[256,2048]{1,0:T(8,128)(2,1)S(1)}, bf16[256,2048]{1,0:T(8,128)(2,1)S(1)}, u32[]{:S(2)}, u32[]{:S(2)}) %collective-permute-start.24) | collective-permute-done | bytes 1048608 | tf_op jit(solution)/shard_map/ppermute | solution.py:58
  237.2 21.8 %ffn.2.refs_16_.refs_17_.refs_0_ = bf16[2048,1536]{1,0:T(8,128)(2,1)} custom-call(bf16[256,2048]{1,0:T(8,128)(2,1)} %copy-done.8, bf16[256,2048]{1,0:T(8,128)(2,1)} %copy-done.24, bf16[256,2048]{1,0:T(8,128)(2,1)} %copy-done.25, bf16[256,2048]{1,0:T(8,128)(2,1)} %copy-done.27, bf16[256,2048]{1,0:T(8,128)(2,1)} %copy-done.26, bf16[256,2048]{1,0:T(8,128)(2,1)} %copy-done.29, ...), custom_call_target="tpu_custom_call" | custom-call | flops 1 | bytes 1 | tf_op jit(solution)/shard_map/ffn/pallas_call | solution.py:204
  259.1 19.2 %weight_grads.3 = bf16[2048,1536]{1,0:T(8,128)(2,1)} custom-call(bf16[256,2048]{1,0:T(8,128)(2,1)} %copy-done.8, bf16[256,2048]{1,0:T(8,128)(2,1)} %copy-done.24, bf16[256,2048]{1,0:T(8,128)(2,1)} %copy-done.25, bf16[256,2048]{1,0:T(8,128)(2,1)} %copy-done.27, bf16[256,2048]{1,0:T(8,128)(2,1)} %copy-done.26, bf16[256,2048]{1,0:T(8,128)(2,1)} %copy-done.29, ...), custom_call_target="tpu_custom_call" | custom-call | flops 20000000000 | bytes 1 | tf_op jit(solution)/shard_map/weight_grads/pallas_call | solution.py:240
  278.8 13.4 %back.15.refs_2_ = bf16[2048,2048]{1,0:T(8,128)(2,1)} custom-call(bf16[2048,1536]{1,0:T(8,128)(2,1)} %ffn.2.refs_16_.refs_17_.refs_0_, bf16[2048,1536]{1,0:T(8,128)(2,1)} %all-gather.3.cloned.1.call-done.refs_16_.refs_1_.refs_2_), custom_call_target="tpu_custom_call" | custom-call | flops 1 | bytes 1 | tf_op jit(solution)/shard_map/back/pallas_call | solution.py:275
  292.2 4.3 all-gather.5.cloned.1.call-done.refs_16_.refs_1_.refs_3_
  296.5 21.7 %ffn.3.refs_0_.refs_16_.refs_17_.refs_1_ = bf16[2048,1536]{1,0:T(8,128)(2,1)} custom-call(bf16[256,2048]{1,0:T(8,128)(2,1)} %copy-done.8, bf16[256,2048]{1,0:T(8,128)(2,1)} %copy-done.24, bf16[256,2048]{1,0:T(8,128)(2,1)} %copy-done.25, bf16[256,2048]{1,0:T(8,128)(2,1)} %copy-done.27, bf16[256,2048]{1,0:T(8,128)(2,1)} %copy-done.26, ...), custom_call_target="tpu_custom_call" | custom-call | flops 1 | bytes 1 | tf_op jit(solution)/shard_map/ffn/pallas_call | solution.py:204
  318.2 9.3 %back.17 = bf16[1024,2048]{1,0:T(8,128)(2,1)} custom-call(bf16[2048,1536]{1,0:T(8,128)(2,1)} %ffn.3.refs_0_.refs_16_.refs_17_.refs_1_, bf16[2048,1536]{1,0:T(8,128)(2,1)} %all-gather.5.cloned.1.call-done.refs_16_.refs_1_.refs_3_, bf16[2048,2048]{1,0:T(8,128)(2,1)} %back.15.refs_2_), custom_call_target="tpu_custom_call" | custom-call | flops 1 | bytes 1 | tf_op jit(solution)/shard_map/back/pallas_call | solution.py:275
  327.5 9.6 %back.16 = bf16[1024,2048]{1,0:T(8,128)(2,1)} custom-call(bf16[2048,1536]{1,0:T(8,128)(2,1)} %ffn.3.refs_0_.refs_16_.refs_17_.refs_1_, bf16[2048,1536]{1,0:T(8,128)(2,1)} %all-gather.5.cloned.1.call-done.refs_16_.refs_1_.refs_3_, bf16[2048,2048]{1,0:T(8,128)(2,1)} %back.15.refs_2_), custom_call_target="tpu_custom_call" | custom-call | flops 1 | bytes 1 | tf_op jit(solution)/shard_map/back/pallas_call | solution.py:275
  337.1 3.3 slice_add_fusion
  342.1 19.2 %weight_grads.4 = bf16[2048,1536]{1,0:T(8,128)(2,1)} custom-call(bf16[256,2048]{1,0:T(8,128)(2,1)} %copy-done.8, bf16[256,2048]{1,0:T(8,128)(2,1)} %copy-done.24, bf16[256,2048]{1,0:T(8,128)(2,1)} %copy-done.25, bf16[256,2048]{1,0:T(8,128)(2,1)} %copy-done.27, bf16[256,2048]{1,0:T(8,128)(2,1)} %copy-done.26, bf16[256,2048]{1,0:T(8,128)(2,1)} %copy-done.29, ...), custom_call_target="tpu_custom_call" | custom-call | flops 20000000000 | bytes 1 | tf_op jit(solution)/shard_map/weight_grads/pallas_call | solution.py:240
  361.4 5.3 collective-permute-done.30
  366.6 3.2 fusion.2.refs_0_
  371.6 6.3 back.18
  377.8 6.9 %collective-permute-done.31.refs_1_ = bf16[256,2048]{1,0:T(8,128)(2,1)S(1)} collective-permute-done((bf16[256,2048]{1,0:T(8,128)(2,1)S(1)}, bf16[256,2048]{1,0:T(8,128)(2,1)S(1)}, u32[]{:S(2)}, u32[]{:S(2)}) %collective-permute-start.31) | collective-permute-done | bytes 1048608 | tf_op jit(solution)/shard_map/ppermute | solution.py:54
  385.8 4.9 norm_back.2.refs_0_.refs_5_
  390.7 6.4 back.20
  400.1 8.7 %back.19 = bf16[1024,2048]{1,0:T(8,128)(2,1)} custom-call(bf16[2048,1536]{1,0:T(8,128)(2,1)} %ffn.2.refs_16_.refs_17_.refs_0_, bf16[2048,1536]{1,0:T(8,128)(2,1)} %ffn.3.refs_0_.refs_16_.refs_17_.refs_1_, bf16[2048,1536]{1,0:T(8,128)(2,1)} %all-gather.3.cloned.1.call-done.refs_16_.refs_1_.refs_2_, ...), custom_call_target="tpu_custom_call" | custom-call | flops 7000000000 | bytes 1 | tf_op jit(solution)/shard_map/back/pallas_call | solution.py:275
  410.1 4.8 broadcast_select_fusion
  414.8 7.5 %collective-permute-done.32.refs_1_ = bf16[256,2048]{1,0:T(8,128)(2,1)S(1)} collective-permute-done((bf16[256,2048]{1,0:T(8,128)(2,1)S(1)}, bf16[256,2048]{1,0:T(8,128)(2,1)S(1)}, u32[]{:S(2)}, u32[]{:S(2)}) %collective-permute-start.32) | collective-permute-done | bytes 1048608 | tf_op jit(solution)/shard_map/ppermute | solution.py:54
  425.0 12.5 %collective-permute-done.38.refs_3_ = bf16[256,2048]{1,0:T(8,128)(2,1)S(1)} collective-permute-done((bf16[256,2048]{1,0:T(8,128)(2,1)S(1)}, bf16[256,2048]{1,0:T(8,128)(2,1)S(1)}, u32[]{:S(2)}, u32[]{:S(2)}) %collective-permute-start.38) | collective-permute-done | bytes 1048608 | tf_op jit(solution)/shard_map/ppermute | solution.py:58
  444.9 9.6 %front.1.d_ref = bf16[2048,256]{1,0:T(8,128)(2,1)} custom-call(bf16[256,2048]{1,0:T(8,128)(2,1)} %norm_back.2.refs_0_.refs_5_, bf16[256,2048]{1,0:T(8,128)(2,1)} %copy-done.49, bf16[256,2048]{1,0:T(8,128)(2,1)} %copy-done.50, bf16[256,2048]{1,0:T(8,128)(2,1)} %copy-done.52, bf16[256,2048]{1,0:T(8,128)(2,1)} %copy-done.51, bf16[256,2048]{1,0:T(8,128)(2,1)} %copy-done.53, ...), custom_call_target="tpu_custom_call" | custom-call | flops 1 | bytes 1 | tf_op jit(solution)/shard_map/front/pallas_call | solution.py:301
  454.5 35.0 %attend_back.1.refs_0_.refs_1_.refs_10_ = bf16[2048,384]{1,0:T(8,128)(2,1)} custom-call(s32[8]{0:T(128)} %select_reduce_fusion.2.place, s32[8]{0:T(128)} %and_select_fusion.2.first, bf16[2048,2432]{1,0:T(8,128)(2,1)} %qkv.1.q_ref.kv_ref.refs_8_, bf16[2048,256]{1,0:T(8,128)(2,1)} %front.1.d_ref, f32[2048,384]{1,0:T(8,128)} %attend.1.refs_0_.h_ref.refs_9_, ...), custom_call_target="tpu_custom_call" | custom-call | flops 1 | bytes 1 | tf_op jit(solution)/shard_map/attend_back/pallas_call | solution.py:479
  492.4 4.1 back.23
  496.6 5.6 back.21
  502.2 4.2 back.22
  513.5 12.4 %weight_grads.5 = bf16[2048,640]{1,0:T(8,128)(2,1)} custom-call(bf16[256,2048]{1,0:T(8,128)(2,1)} %norm_back.2.refs_0_.refs_5_, bf16[256,2048]{1,0:T(8,128)(2,1)} %copy-done.49, bf16[256,2048]{1,0:T(8,128)(2,1)} %copy-done.50, bf16[256,2048]{1,0:T(8,128)(2,1)} %copy-done.52, bf16[256,2048]{1,0:T(8,128)(2,1)} %copy-done.51, bf16[256,2048]{1,0:T(8,128)(2,1)} %copy-done.53, ...), custom_call_target="tpu_custom_call" | custom-call | flops 20000000000 | bytes 1 | tf_op jit(solution)/shard_map/weight_grads/pallas_call | solution.py:240
  525.9 6.9 %collective-permute-done.47 = bf16[256,2048]{1,0:T(8,128)(2,1)} collective-permute-done((bf16[256,2048]{1,0:T(8,128)(2,1)}, bf16[256,2048]{1,0:T(8,128)(2,1)}, u32[]{:S(2)}, u32[]{:S(2)}) %collective-permute-start.47) | collective-permute-done | bytes 1048608 | tf_op jit(solution)/shard_map/ppermute | solution.py:50
  542.0 3.8 fusion.4
  547.2 15.4 %collective-permute-done.50 = bf16[256,2048]{1,0:T(8,128)(2,1)} collective-permute-done((bf16[256,2048]{1,0:T(8,128)(2,1)}, bf16[256,2048]{1,0:T(8,128)(2,1)}, u32[]{:S(2)}, u32[]{:S(2)}) %collective-permute-start.50) | collective-permute-done | bytes 1048608 | tf_op jit(solution)/shard_map/ppermute | solution.py:46
  564.5 5.9 collective-permute-done.53
  588.2 4.5 collective-permute-done.49.refs_2_
  594.8 5.3 norm_back.3
  604.6 8.6 %collective-permute-start.55 = (f32[2,512]{1,0:T(2,128)S(1)}, f32[2,512]{1,0:T(2,128)S(1)}, u32[]{:S(2)}, u32[]{:S(2)}) collective-permute-start(f32[2,512]{1,0:T(2,128)S(1)} %pad_maximum_fusion.11), channel_id=1, source_target_pairs={{0,1},{1,0},{2,3},{3,2},{4,5},{5,4},{6,7},{7,6},{8,9},{9,8},{10,11... | collective-permute-start | bytes 12296 | tf_op jit(solution)/shard_map/ppermute | solution.py:42
  619.6 7.0 %collective-permute-start.59 = (bf16[256,2048]{1,0:T(8,128)(2,1)S(1)}, bf16[256,2048]{1,0:T(8,128)(2,1)S(1)}, u32[]{:S(2)}, u32[]{:S(2)}) collective-permute-start(bf16[256,2048]{1,0:T(8,128)(2,1)S(1)} %copy-done.34), channel_id=1, source_target_pairs={{0,1},{1,0},{2,3},{3,2},{4,5},{5,4},{6,7},{7,6},{8,9},{9,8},{10,11... | collective-permute-start | bytes 3145736 | tf_op jit(solution)/shard_map/ppermute | solution.py:42
  (341 shorter events, 147.0 us)
Async XLA Ops:
  7.2 182.6 %all-gather.3.cloned.1.call-start = ((), (), s32[]{:S(2)}) async-start(), calls=%async_computation.3 | async-start | bytes 7864320 | tf_op jit(solution)/shard_map/all_gather | solution.py:703
  11.7 20.3 %collective-permute-start = (bf16[528,640]{1,0:T(8,128)(2,1)S(1)}, bf16[528,640]{1,0:T(8,128)(2,1)}, u32[]{:S(2)}, u32[]{:S(2)}) collective-permute-start(bf16[528,640]{1,0:T(8,128)(2,1)S(1)} %fusion.6), channel_id=1, source_target_pairs={{0,8},{8,16},{16,24},{24,0},{1,9},{9,17},{17,25},{25,1},{2,10},{10... | collective-permute-start | bytes 2027528 | tf_op jit(solution)/shard_map/ppermute | solution.py:558
  16.0 16.0 %collective-permute-start.1 = (bf16[256,2048]{1,0:T(8,128)(2,1)S(1)}, bf16[256,2048]{1,0:T(8,128)(2,1)}, u32[]{:S(2)}, u32[]{:S(2)}) collective-permute-start(bf16[256,2048]{1,0:T(8,128)(2,1)S(1)} %constant_dynamic-slice_fusion.11.refs_0_.refs_3_), channel_id=1, source_target_pairs={{0,4},{1,3},{2,6},{3,1},{4,0},{5,7},{6,2},{7,5},{8,12},{9,11},{10,... | collective-permute-start | bytes 3145736 | tf_op jit(solution)/shard_map/ppermute | solution.py:54
  32.0 18.5 %collective-permute-start.2 = (bf16[528,640]{1,0:T(8,128)(2,1)}, bf16[528,640]{1,0:T(8,128)(2,1)}, u32[]{:S(2)}, u32[]{:S(2)}) collective-permute-start(bf16[528,640]{1,0:T(8,128)(2,1)} %collective-permute-done), channel_id=1, source_target_pairs={{0,8},{8,16},{16,24},{24,0},{1,9},{9,17},{17,25},{25,1},{2,10},{10... | collective-permute-start | bytes 2027528 | tf_op jit(solution)/shard_map/ppermute | solution.py:558
  32.6 23.8 %collective-permute-start.4 = (bf16[256,2048]{1,0:T(8,128)(2,1)S(1)}, bf16[256,2048]{1,0:T(8,128)(2,1)}, u32[]{:S(2)}, u32[]{:S(2)}) collective-permute-start(bf16[256,2048]{1,0:T(8,128)(2,1)S(1)} %constant_dynamic-slice_fusion.11.refs_0_.refs_3_), channel_id=1, source_target_pairs={{0,2},{1,5},{2,0},{3,7},{4,6},{5,1},{6,4},{7,3},{8,10},{9,13},{10,... | collective-permute-start | bytes 3145736 | tf_op jit(solution)/shard_map/ppermute | solution.py:58
  34.1 24.6 %collective-permute-start.5 = (bf16[256,2048]{1,0:T(8,128)(2,1)}, bf16[256,2048]{1,0:T(8,128)(2,1)}, u32[]{:S(2)}, u32[]{:S(2)}) collective-permute-start(bf16[256,2048]{1,0:T(8,128)(2,1)} %collective-permute-done.1.refs_1_), channel_id=1, source_target_pairs={{0,2},{1,5},{2,0},{3,7},{4,6},{5,1},{6,4},{7,3},{8,10},{9,13},{10,... | collective-permute-start | bytes 3145736 | tf_op jit(solution)/shard_map/ppermute | solution.py:58
  50.5 17.6 %collective-permute-start.3 = (bf16[528,640]{1,0:T(8,128)(2,1)}, bf16[528,640]{1,0:T(8,128)(2,1)}, u32[]{:S(2)}, u32[]{:S(2)}) collective-permute-start(bf16[528,640]{1,0:T(8,128)(2,1)} %collective-permute-done.2), channel_id=1, source_target_pairs={{0,8},{8,16},{16,24},{24,0},{1,9},{9,17},{17,25},{25,1},{2,10},{10... | collective-permute-start | bytes 2027528 | tf_op jit(solution)/shard_map/ppermute | solution.py:558
  68.0 228.4 %all-gather.5.cloned.1.call-start = ((), (), s32[]{:S(2)}) async-start(), calls=%async_computation.4 | async-start | bytes 7864320 | tf_op jit(solution)/shard_map/all_gather | solution.py:703
  77.3 25.4 %collective-permute-start.10 = (bf16[256,2048]{1,0:T(8,128)(2,1)S(1)}, bf16[256,2048]{1,0:T(8,128)(2,1)S(1)}, u32[]{:S(2)}, u32[]{:S(2)}) collective-permute-start(bf16[256,2048]{1,0:T(8,128)(2,1)S(1)} %constant_dynamic-slice_fusion.6.refs_8_.refs_4_), channel_id=1, source_target_pairs={{0,4},{1,3},{2,6},{3,1},{4,0},{5,7},{6,2},{7,5},{8,12},{9,11},{10,... | collective-permute-start | bytes 3145736 | tf_op jit(solution)/shard_map/ppermute | solution.py:54
  78.7 24.2 %collective-permute-start.11 = (bf16[256,2048]{1,0:T(8,128)(2,1)S(1)}, bf16[256,2048]{1,0:T(8,128)(2,1)}, u32[]{:S(2)}, u32[]{:S(2)}) collective-permute-start(bf16[256,2048]{1,0:T(8,128)(2,1)S(1)} %constant_dynamic-slice_fusion.6.refs_8_.refs_4_), channel_id=1, source_target_pairs={{0,2},{1,5},{2,0},{3,7},{4,6},{5,1},{6,4},{7,3},{8,10},{9,13},{10,... | collective-permute-start | bytes 3145736 | tf_op jit(solution)/shard_map/ppermute | solution.py:58
  79.8 48.6 %collective-permute-start.13 = (bf16[256,2048]{1,0:T(8,128)(2,1)S(1)}, bf16[256,2048]{1,0:T(8,128)(2,1)}, u32[]{:S(2)}, u32[]{:S(2)}) collective-permute-start(bf16[256,2048]{1,0:T(8,128)(2,1)S(1)} %constant_dynamic-slice_fusion.6.refs_8_.refs_4_), channel_id=1, source_target_pairs={{0,1},{1,0},{2,3},{3,2},{4,5},{5,4},{6,7},{7,6},{8,9},{9,8},{10,11... | collective-permute-start | bytes 3145736 | tf_op jit(solution)/shard_map/ppermute | solution.py:42
  102.8 25.6 %collective-permute-start.12 = (bf16[256,2048]{1,0:T(8,128)(2,1)S(1)}, bf16[256,2048]{1,0:T(8,128)(2,1)}, u32[]{:S(2)}, u32[]{:S(2)}) collective-permute-start(bf16[256,2048]{1,0:T(8,128)(2,1)S(1)} %collective-permute-done.10.refs_9_), channel_id=1, source_target_pairs={{0,2},{1,5},{2,0},{3,7},{4,6},{5,1},{6,4},{7,3},{8,10},{9,13},{10,... | collective-permute-start | bytes 3145736 | tf_op jit(solution)/shard_map/ppermute | solution.py:58
  103.8 24.6 %collective-permute-start.14 = (bf16[256,2048]{1,0:T(8,128)(2,1)S(1)}, bf16[256,2048]{1,0:T(8,128)(2,1)}, u32[]{:S(2)}, u32[]{:S(2)}) collective-permute-start(bf16[256,2048]{1,0:T(8,128)(2,1)S(1)} %collective-permute-done.10.refs_9_), channel_id=1, source_target_pairs={{0,1},{1,0},{2,3},{3,2},{4,5},{5,4},{6,7},{7,6},{8,9},{9,8},{10,11... | collective-permute-start | bytes 3145736 | tf_op jit(solution)/shard_map/ppermute | solution.py:42
  104.2 24.2 %collective-permute-start.15 = (bf16[256,2048]{1,0:T(8,128)(2,1)}, bf16[256,2048]{1,0:T(8,128)(2,1)}, u32[]{:S(2)}, u32[]{:S(2)}) collective-permute-start(bf16[256,2048]{1,0:T(8,128)(2,1)} %collective-permute-done.11.refs_10_), channel_id=1, source_target_pairs={{0,1},{1,0},{2,3},{3,2},{4,5},{5,4},{6,7},{7,6},{8,9},{9,8},{10,11... | collective-permute-start | bytes 3145736 | tf_op jit(solution)/shard_map/ppermute | solution.py:42
  139.1 23.2 %collective-permute-start.17 = (bf16[512,2048]{1,0:T(8,128)(2,1)}, bf16[512,2048]{1,0:T(8,128)(2,1)S(1)}, u32[]{:S(2)}, u32[]{:S(2)}) collective-permute-start(bf16[512,2048]{1,0:T(8,128)(2,1)} %back.13), channel_id=1, source_target_pairs={{0,1},{1,0},{2,3},{3,2},{4,5},{5,4},{6,7},{7,6},{8,9},{9,8},{10,11... | collective-permute-start | bytes 6291464 | tf_op jit(solution)/shard_map/ppermute | solution.py:42
  140.6 298.9 %reduce-scatter.4.cloned.1.call-start = ((), (), s32[]{:S(2)}) async-start(), calls=%async_computation.5 | async-start | bytes 7864320 | tf_op jit(solution)/shard_map/reduce_scatter | solution.py:734
  147.5 14.9 %collective-permute-start.19 = (bf16[256,2048]{1,0:T(8,128)(2,1)S(1)}, bf16[256,2048]{1,0:T(8,128)(2,1)S(1)}, u32[]{:S(2)}, u32[]{:S(2)}) collective-permute-start(bf16[256,2048]{1,0:T(8,128)(2,1)S(1)} %get-tuple-element.152), channel_id=1, source_target_pairs={{0,2},{1,5},{2,0},{3,7},{4,6},{5,1},{6,4},{7,3},{8,10},{9,13},{10,... | collective-permute-start | bytes 3145736 | tf_op jit(solution)/shard_map/ppermute | solution.py:58
  163.7 26.1 %collective-permute-start.21 = (bf16[256,2048]{1,0:T(8,128)(2,1)S(1)}, bf16[256,2048]{1,0:T(8,128)(2,1)}, u32[]{:S(2)}, u32[]{:S(2)}) collective-permute-start(bf16[256,2048]{1,0:T(8,128)(2,1)S(1)} %fusion.5), channel_id=1, source_target_pairs={{0,4},{1,3},{2,6},{3,1},{4,0},{5,7},{6,2},{7,5},{8,12},{9,11},{10,... | collective-permute-start | bytes 3145736 | tf_op jit(solution)/shard_map/ppermute | solution.py:54
  165.2 24.6 %collective-permute-start.20 = (bf16[256,2048]{1,0:T(8,128)(2,1)S(1)}, bf16[256,2048]{1,0:T(8,128)(2,1)}, u32[]{:S(2)}, u32[]{:S(2)}) collective-permute-start(bf16[256,2048]{1,0:T(8,128)(2,1)S(1)} %get-tuple-element.91), channel_id=1, source_target_pairs={{0,2},{1,5},{2,0},{3,7},{4,6},{5,1},{6,4},{7,3},{8,10},{9,13},{10,... | collective-permute-start | bytes 3145736 | tf_op jit(solution)/shard_map/ppermute | solution.py:58
  193.4 25.2 %collective-permute-start.22 = (bf16[256,2048]{1,0:T(8,128)(2,1)S(1)}, bf16[256,2048]{1,0:T(8,128)(2,1)S(1)}, u32[]{:S(2)}, u32[]{:S(2)}) collective-permute-start(bf16[256,2048]{1,0:T(8,128)(2,1)S(1)} %multiply_convert_fusion.refs_0_), channel_id=1, source_target_pairs={{0,4},{1,3},{2,6},{3,1},{4,0},{5,7},{6,2},{7,5},{8,12},{9,11},{10,... | collective-permute-start | bytes 3145736 | tf_op jit(solution)/shard_map/ppermute | solution.py:54
  194.2 24.4 %collective-permute-start.23 = (bf16[256,2048]{1,0:T(8,128)(2,1)S(1)}, bf16[256,2048]{1,0:T(8,128)(2,1)S(1)}, u32[]{:S(2)}, u32[]{:S(2)}) collective-permute-start(bf16[256,2048]{1,0:T(8,128)(2,1)S(1)} %multiply_convert_fusion.refs_0_), channel_id=1, source_target_pairs={{0,2},{1,5},{2,0},{3,7},{4,6},{5,1},{6,4},{7,3},{8,10},{9,13},{10,... | collective-permute-start | bytes 3145736 | tf_op jit(solution)/shard_map/ppermute | solution.py:58
  195.4 25.3 %collective-permute-start.25 = (bf16[256,2048]{1,0:T(8,128)(2,1)S(1)}, bf16[256,2048]{1,0:T(8,128)(2,1)S(1)}, u32[]{:S(2)}, u32[]{:S(2)}) collective-permute-start(bf16[256,2048]{1,0:T(8,128)(2,1)S(1)} %multiply_convert_fusion.refs_0_), channel_id=1, source_target_pairs={{0,1},{1,0},{2,3},{3,2},{4,5},{5,4},{6,7},{7,6},{8,9},{9,8},{10,11... | collective-permute-start | bytes 3145736 | tf_op jit(solution)/shard_map/ppermute | solution.py:42
  218.6 14.9 %collective-permute-start.24 = (bf16[256,2048]{1,0:T(8,128)(2,1)S(1)}, bf16[256,2048]{1,0:T(8,128)(2,1)S(1)}, u32[]{:S(2)}, u32[]{:S(2)}) collective-permute-start(bf16[256,2048]{1,0:T(8,128)(2,1)S(1)} %collective-permute-done.22.refs_1_), channel_id=1, source_target_pairs={{0,2},{1,5},{2,0},{3,7},{4,6},{5,1},{6,4},{7,3},{8,10},{9,13},{10,... | collective-permute-start | bytes 3145736 | tf_op jit(solution)/shard_map/ppermute | solution.py:58
  278.3 254.4 %reduce-scatter.6.cloned.1.call-start = ((), (), s32[]{:S(2)}) async-start(), calls=%async_computation.6 | async-start | bytes 7864320 | tf_op jit(solution)/shard_map/reduce_scatter | solution.py:734
  340.4 26.2 %collective-permute-start.30 = (bf16[512,2048]{1,0:T(8,128)(2,1)S(1)}, bf16[512,2048]{1,0:T(8,128)(2,1)}, u32[]{:S(2)}, u32[]{:S(2)}) collective-permute-start(bf16[512,2048]{1,0:T(8,128)(2,1)S(1)} %slice_add_fusion), channel_id=1, source_target_pairs={{0,2},{1,5},{2,0},{3,7},{4,6},{5,1},{6,4},{7,3},{8,10},{9,13},{10,... | collective-permute-start | bytes 6291464 | tf_op jit(solution)/shard_map/ppermute | solution.py:58
  361.3 241.3 %reduce-scatter.8.cloned.1.call-start = ((), (), s32[]{:S(2)}) async-start(), calls=%async_computation.7 | async-start | bytes 3276800 | tf_op jit(solution)/shard_map/reduce_scatter | solution.py:795
  369.9 14.9 %collective-permute-start.31 = (bf16[256,2048]{1,0:T(8,128)(2,1)S(1)}, bf16[256,2048]{1,0:T(8,128)(2,1)S(1)}, u32[]{:S(2)}, u32[]{:S(2)}) collective-permute-start(bf16[256,2048]{1,0:T(8,128)(2,1)S(1)} %slice.217), channel_id=1, source_target_pairs={{0,4},{1,3},{2,6},{3,1},{4,0},{5,7},{6,2},{7,5},{8,12},{9,11},{10,... | collective-permute-start | bytes 3145736 | tf_op jit(solution)/shard_map/ppermute | solution.py:54
  377.8 30.9 %collective-permute-start.35 = (bf16[512,2048]{1,0:T(8,128)(2,1)}, bf16[512,2048]{1,0:T(8,128)(2,1)S(1)}, u32[]{:S(2)}, u32[]{:S(2)}) collective-permute-start(bf16[512,2048]{1,0:T(8,128)(2,1)} %back.18), channel_id=1, source_target_pairs={{0,1},{1,0},{2,3},{3,2},{4,5},{5,4},{6,7},{7,6},{8,9},{9,8},{10,11... | collective-permute-start | bytes 6291464 | tf_op jit(solution)/shard_map/ppermute | solution.py:42
  397.0 25.2 %collective-permute-start.32 = (bf16[256,2048]{1,0:T(8,128)(2,1)S(1)}, bf16[256,2048]{1,0:T(8,128)(2,1)S(1)}, u32[]{:S(2)}, u32[]{:S(2)}) collective-permute-start(bf16[256,2048]{1,0:T(8,128)(2,1)S(1)} %copy-done.10), channel_id=1, source_target_pairs={{0,4},{1,3},{2,6},{3,1},{4,0},{5,7},{6,2},{7,5},{8,12},{9,11},{10,... | collective-permute-start | bytes 3145736 | tf_op jit(solution)/shard_map/ppermute | solution.py:54
  398.6 24.0 %collective-permute-start.33 = (bf16[256,2048]{1,0:T(8,128)(2,1)S(1)}, bf16[256,2048]{1,0:T(8,128)(2,1)S(1)}, u32[]{:S(2)}, u32[]{:S(2)}) collective-permute-start(bf16[256,2048]{1,0:T(8,128)(2,1)S(1)} %copy-done.10), channel_id=1, source_target_pairs={{0,2},{1,5},{2,0},{3,7},{4,6},{5,1},{6,4},{7,3},{8,10},{9,13},{10,... | collective-permute-start | bytes 3145736 | tf_op jit(solution)/shard_map/ppermute | solution.py:58
  400.1 24.9 %collective-permute-start.39 = (bf16[256,2048]{1,0:T(8,128)(2,1)S(1)}, bf16[256,2048]{1,0:T(8,128)(2,1)S(1)}, u32[]{:S(2)}, u32[]{:S(2)}) collective-permute-start(bf16[256,2048]{1,0:T(8,128)(2,1)S(1)} %copy-done.10), channel_id=1, source_target_pairs={{0,1},{1,0},{2,3},{3,2},{4,5},{5,4},{6,7},{7,6},{8,9},{9,8},{10,11... | collective-permute-start | bytes 3145736 | tf_op jit(solution)/shard_map/ppermute | solution.py:42
  422.6 14.8 %collective-permute-start.38 = (bf16[256,2048]{1,0:T(8,128)(2,1)S(1)}, bf16[256,2048]{1,0:T(8,128)(2,1)S(1)}, u32[]{:S(2)}, u32[]{:S(2)}) collective-permute-start(bf16[256,2048]{1,0:T(8,128)(2,1)S(1)} %collective-permute-done.32.refs_1_), channel_id=1, source_target_pairs={{0,2},{1,5},{2,0},{3,7},{4,6},{5,1},{6,4},{7,3},{8,10},{9,13},{10,... | collective-permute-start | bytes 3145736 | tf_op jit(solution)/shard_map/ppermute | solution.py:58
  424.6 14.9 %collective-permute-start.41 = (bf16[256,2048]{1,0:T(8,128)(2,1)S(1)}, bf16[256,2048]{1,0:T(8,128)(2,1)}, u32[]{:S(2)}, u32[]{:S(2)}) collective-permute-start(bf16[256,2048]{1,0:T(8,128)(2,1)S(1)} %collective-permute-done.33.refs_2_), channel_id=1, source_target_pairs={{0,1},{1,0},{2,3},{3,2},{4,5},{5,4},{6,7},{7,6},{8,9},{9,8},{10,11... | collective-permute-start | bytes 3145736 | tf_op jit(solution)/shard_map/ppermute | solution.py:42
  439.4 50.1 %collective-permute-start.43 = (bf16[512,1536]{1,0:T(8,128)(2,1)}, bf16[512,1536]{1,0:T(8,128)(2,1)S(1)}, u32[]{:S(2)}, u32[]{:S(2)}) collective-permute-start(bf16[512,1536]{1,0:T(8,128)(2,1)} %reduce-scatter.4.cloned.1.call-done), channel_id=1, source_target_pairs={{0,4},{4,0},{1,5},{5,1},{2,6},{6,2},{3,7},{7,3},{8,12},{12,8},{9,1... | collective-permute-start | bytes 4718600 | tf_op jit(solution)/shard_map/ppermute | solution.py:50
  441.0 48.5 %collective-permute-start.36 = (bf16[256,2048]{1,0:T(8,128)(2,1)}, bf16[256,2048]{1,0:T(8,128)(2,1)S(1)}, u32[]{:S(2)}, u32[]{:S(2)}) collective-permute-start(bf16[256,2048]{1,0:T(8,128)(2,1)} %get-tuple-element.106), channel_id=1, source_target_pairs={{0,2},{2,0},{1,3},{3,1},{4,6},{6,4},{5,7},{7,5},{8,10},{10,8},{9,1... | collective-permute-start | bytes 3145736 | tf_op jit(solution)/shard_map/ppermute | solution.py:46
  442.8 46.7 %collective-permute-start.37 = (bf16[256,2048]{1,0:T(8,128)(2,1)}, bf16[256,2048]{1,0:T(8,128)(2,1)S(1)}, u32[]{:S(2)}, u32[]{:S(2)}) collective-permute-start(bf16[256,2048]{1,0:T(8,128)(2,1)} %get-tuple-element.107), channel_id=1, source_target_pairs={{0,2},{2,0},{1,3},{3,1},{4,6},{6,4},{5,7},{7,5},{8,10},{10,8},{9,1... | collective-permute-start | bytes 3145736 | tf_op jit(solution)/shard_map/ppermute | solution.py:46
  506.5 26.3 %collective-permute-start.47 = (bf16[256,2048]{1,0:T(8,128)(2,1)}, bf16[256,2048]{1,0:T(8,128)(2,1)}, u32[]{:S(2)}, u32[]{:S(2)}) collective-permute-start(bf16[256,2048]{1,0:T(8,128)(2,1)} %add.380), channel_id=1, source_target_pairs={{0,4},{4,0},{1,5},{5,1},{2,6},{6,2},{3,7},{7,3},{8,12},{12,8},{9,1... | collective-permute-start | bytes 3145736 | tf_op jit(solution)/shard_map/ppermute | solution.py:50
  507.0 35.0 %collective-permute-start.44 = (bf16[512,2048]{1,0:T(8,128)(2,1)}, bf16[512,2048]{1,0:T(8,128)(2,1)}, u32[]{:S(2)}, u32[]{:S(2)}) collective-permute-start(bf16[512,2048]{1,0:T(8,128)(2,1)} %back.22), channel_id=1, source_target_pairs={{0,1},{1,0},{2,3},{3,2},{4,5},{5,4},{6,7},{7,6},{8,9},{9,8},{10,11... | collective-permute-start | bytes 6291464 | tf_op jit(solution)/shard_map/ppermute | solution.py:42
  511.7 30.3 %collective-permute-start.46 = (bf16[256,2048]{1,0:T(8,128)(2,1)}, bf16[256,2048]{1,0:T(8,128)(2,1)}, u32[]{:S(2)}, u32[]{:S(2)}) collective-permute-start(bf16[256,2048]{1,0:T(8,128)(2,1)} %get-tuple-element.146), channel_id=1, source_target_pairs={{0,2},{1,5},{2,0},{3,7},{4,6},{5,1},{6,4},{7,3},{8,10},{9,13},{10,... | collective-permute-start | bytes 3145736 | tf_op jit(solution)/shard_map/ppermute | solution.py:58
  532.8 37.7 %collective-permute-start.53 = (bf16[512,1536]{1,0:T(8,128)(2,1)}, bf16[512,1536]{1,0:T(8,128)(2,1)}, u32[]{:S(2)}, u32[]{:S(2)}) collective-permute-start(bf16[512,1536]{1,0:T(8,128)(2,1)} %reduce-scatter.6.cloned.1.call-done), channel_id=1, source_target_pairs={{0,4},{4,0},{1,5},{5,1},{2,6},{6,2},{3,7},{7,3},{8,12},{12,8},{9,1... | collective-permute-start | bytes 4718600 | tf_op jit(solution)/shard_map/ppermute | solution.py:50
  536.2 26.4 %collective-permute-start.50 = (bf16[256,2048]{1,0:T(8,128)(2,1)}, bf16[256,2048]{1,0:T(8,128)(2,1)}, u32[]{:S(2)}, u32[]{:S(2)}) collective-permute-start(bf16[256,2048]{1,0:T(8,128)(2,1)} %add_convert_fusion), channel_id=1, source_target_pairs={{0,2},{2,0},{1,3},{3,1},{4,6},{6,4},{5,7},{7,5},{8,10},{10,8},{9,1... | collective-permute-start | bytes 3145736 | tf_op jit(solution)/shard_map/ppermute | solution.py:46
  541.9 39.5 %collective-permute-start.51 = (bf16[256,2048]{1,0:T(8,128)(2,1)}, bf16[256,2048]{1,0:T(8,128)(2,1)}, u32[]{:S(2)}, u32[]{:S(2)}) collective-permute-start(bf16[256,2048]{1,0:T(8,128)(2,1)} %add_convert_fusion), channel_id=1, source_target_pairs={{0,1},{1,0},{2,3},{3,2},{4,5},{5,4},{6,7},{7,6},{8,9},{9,8},{10,11... | collective-permute-start | bytes 3145736 | tf_op jit(solution)/shard_map/ppermute | solution.py:42
  545.8 47.0 %collective-permute-start.49 = (bf16[256,2048]{1,0:T(8,128)(2,1)S(1)}, bf16[256,2048]{1,0:T(8,128)(2,1)S(1)}, u32[]{:S(2)}, u32[]{:S(2)}) collective-permute-start(bf16[256,2048]{1,0:T(8,128)(2,1)S(1)} %get-tuple-element.123), channel_id=1, source_target_pairs={{0,4},{1,3},{2,6},{3,1},{4,0},{5,7},{6,2},{7,5},{8,12},{9,11},{10,... | collective-permute-start | bytes 3145736 | tf_op jit(solution)/shard_map/ppermute | solution.py:54
  546.9 45.8 %collective-permute-start.48 = (bf16[256,2048]{1,0:T(8,128)(2,1)S(1)}, bf16[256,2048]{1,0:T(8,128)(2,1)S(1)}, u32[]{:S(2)}, u32[]{:S(2)}) collective-permute-start(bf16[256,2048]{1,0:T(8,128)(2,1)S(1)} %copy-done.58), channel_id=1, source_target_pairs={{0,2},{1,5},{2,0},{3,7},{4,6},{5,1},{6,4},{7,3},{8,10},{9,13},{10,... | collective-permute-start | bytes 3145736 | tf_op jit(solution)/shard_map/ppermute | solution.py:58
  562.6 18.8 %collective-permute-start.52 = (bf16[256,2048]{1,0:T(8,128)(2,1)}, bf16[256,2048]{1,0:T(8,128)(2,1)S(1)}, u32[]{:S(2)}, u32[]{:S(2)}) collective-permute-start(bf16[256,2048]{1,0:T(8,128)(2,1)} %collective-permute-done.50), channel_id=1, source_target_pairs={{0,1},{1,0},{2,3},{3,2},{4,5},{5,4},{6,7},{7,6},{8,9},{9,8},{10,11... | collective-permute-start | bytes 3145736 | tf_op jit(solution)/shard_map/ppermute | solution.py:42
  600.1 26.6 %collective-permute-start.54 = (bf16[256,2048]{1,0:T(8,128)(2,1)}, bf16[256,2048]{1,0:T(8,128)(2,1)S(1)}, u32[]{:S(2)}, u32[]{:S(2)}) collective-permute-start(bf16[256,2048]{1,0:T(8,128)(2,1)} %norm_back.3), channel_id=1, source_target_pairs={{0,2},{2,0},{1,3},{3,1},{4,6},{6,4},{5,7},{7,5},{8,10},{10,8},{9,1... | collective-permute-start | bytes 3145736 | tf_op jit(solution)/shard_map/ppermute | solution.py:46
  602.7 24.0 %collective-permute-start.58 = (bf16[512,640]{1,0:T(8,128)(2,1)}, bf16[512,640]{1,0:T(8,128)(2,1)S(1)}, u32[]{:S(2)}, u32[]{:S(2)}) collective-permute-start(bf16[512,640]{1,0:T(8,128)(2,1)} %reduce-scatter.8.cloned.1.call-done), channel_id=1, source_target_pairs={{0,4},{4,0},{1,5},{5,1},{2,6},{6,2},{3,7},{7,3},{8,12},{12,8},{9,1... | collective-permute-start | bytes 1966088 | tf_op jit(solution)/shard_map/ppermute | solution.py:50
  619.6 16.3 %collective-permute-start.59 = (bf16[256,2048]{1,0:T(8,128)(2,1)S(1)}, bf16[256,2048]{1,0:T(8,128)(2,1)S(1)}, u32[]{:S(2)}, u32[]{:S(2)}) collective-permute-start(bf16[256,2048]{1,0:T(8,128)(2,1)S(1)} %copy-done.34), channel_id=1, source_target_pairs={{0,1},{1,0},{2,3},{3,2},{4,5},{5,4},{6,7},{7,6},{8,9},{9,8},{10,11... | collective-permute-start | bytes 3145736 | tf_op jit(solution)/shard_map/ppermute | solution.py:42
  (86 other events, 1101.0 us)
Sparse Core Ops, SparseCore 0:
  68.2 113.0 all-gather.2
  182.8 113.5 all-gather.4
  298.8 108.9 reduce-scatter.3
  409.9 111.2 reduce-scatter.5
  542.1 49.1 reduce-scatter.7

commit v12 on v11

--- a/solution.py
+++ b/solution.py
@@ -743,13 +743,13 @@
     d_own = norm_back(wide_last(d_norm_near, ffn_sent), hidden, gain_two, cot_low)
     ffn_sent.append(ffn_rows(2, 4, d_own))
     ffn_mine = ffn_rows(0, 2, d_own)
+    d_one, d_two, ffn_mine, ffn_sent[1] = lax.optimization_barrier(
+        (swap_first(d_own), swap_second(d_own), ffn_mine, ffn_sent[1])
+    )
     ffn_own, ffn_a, ffn_b, ffn_both = add_blocks(ffn_mine, [swap_core(piece) for piece in ffn_sent])
     ffn_x, ffn_y = jnp.where(core == 0, ffn_a, ffn_b), jnp.where(core == 0, ffn_b, ffn_a)
-    d_one, d_two, ffn_own, ffn_x, ffn_y, ffn_both = lax.optimization_barrier(
-        (swap_first(d_own), swap_second(d_own), ffn_own, ffn_x, ffn_y, ffn_both)
-    )
     d_early = [swap_core(part) for part in (d_own, d_one, d_two)]
-    d_last = after(swap_second(d_one), *d_early, reduced[0])
+    d_last = after(swap_second(d_one), *d_early, ffn_own, ffn_x, ffn_y, ffn_both, reduced[0])
     d_attn = (d_own, d_one, d_two, d_last, *d_early, swap_core(d_last))
 
     d_heads = front_product(d_attn, attn_full, q_width, 0)
@@ -776,7 +776,8 @@
     for part in range(1, len(chunks)):
         reduced[part] = after(reduced[part], attn_grad)
         other_reduced.append(swap_x(reduced[part]))
-    halves = [both_halves(mine, other, ctx) for mine, other in zip(reduced, other_reduced)]
+    late = [after(part, normed_first[1]) for part in other_reduced]
+    halves = [both_halves(mine, other, ctx) for mine, other in zip(reduced, late)]
 
     def ffn_out(which):
         return jnp.concatenate(

time: 657 us -> 654 us (level)
  waiting for transfers between devices: 193 us -> 221 us
  starting transfers between devices: 63.4 us -> 43.7 us
  local copies, waits for them, and re-layouts: 40.3 us -> 32.7 us
    ppermute x5, waiting for transfers between devices: 18.3 us -> 37.2 us  [swap_y(): return lax.ppermute(v, 'tp', ACROSS)]
    ppermute x28, starting transfers between devices: 21.9 us -> 6.57 us  [swap_core(): return lax.ppermute(v, 'tp', CORE)]
    ppermute x5, waiting for transfers between devices: 12.8 us -> 21.9 us  [swap_x(): return lax.ppermute(v, 'ctx', PAIR)]
    unnamed x137 -> x111, local copies, waits for them, and re-layouts: 14.1 us -> 8.62 us
  transfers between devices with their start and end apart: 66 -> 66, of which waited for: 26 -> 28; matrix products, arithmetic and copies ran while one was open for 14% -> 13% of each run, Pallas kernels for 41% -> 41%
where the time goes in v12:
time: 654 us; the launch traced here: 645 us
  Pallas kernels  264 us (40%)
  waiting for transfers between devices  221 us (34%)
  other arithmetic  68.4 us (10%)
  starting transfers between devices  43.7 us (7%)
  local copies, waits for them, and re-layouts  32.7 us (5%)
  between operations  15.2 us (2%)
    pallas_call x12, Pallas kernels, back_product(): pl.pallas_call(functools.partial(back_kernel, len(terms)), out_shape=jax....  79 us
    ppermute x7, waiting for transfers between devices, swap_first(): return lax.ppermute(v, ('ctx', 'tp'), FIRST)  76.3 us
    pallas_call x3, Pallas kernels, weight_grads(): pl.pallas_call(functools.partial(grads_kernel, len(x), len(y)), out_shape...  51.1 us
    pallas_call x2, Pallas kernels, ffn_chunk(): pl.pallas_call(functools.partial(ffn_kernel, len(x)), out_shape=jax.Shape...  43.5 us
    ppermute x13, waiting for transfers between devices, swap_second(): return lax.ppermute(v, ('ctx', 'tp'), SECOND)  40.4 us
    ppermute x5, waiting for transfers between devices, swap_y(): return lax.ppermute(v, 'tp', ACROSS)  37.2 us
    pallas_call x1, Pallas kernels, attend_back(): pl.pallas_call(attend_back_kernel, out_shape=jax.ShapeDtypeStruct((rows,...  33.7 us
    ppermute x3, waiting for transfers between devices, ring_over(): pieces.append(lax.ppermute(sent, 'fsdp', cycle))  30.9 us
  transfers between devices with their start and end apart: 66, of which 28 were waited for; matrix products, arithmetic and copies ran while one was open for 13% of the time, Pallas kernels for 41%

profile of v12, /device:TPU:0, one launch (start us, length us, event | category | flops | bytes accessed | tf_op | source)
XLA Modules:
  0.0 645.0 jit_solution(17369467707137982727)
XLA Ops:
  20.7 5.6 negate_select_fusion
  26.3 5.7 collective-permute-done
  34.6 15.9 %collective-permute-done.2 = bf16[528,640]{1,0:T(8,128)(2,1)} collective-permute-done((bf16[528,640]{1,0:T(8,128)(2,1)}, bf16[528,640]{1,0:T(8,128)(2,1)}, u32[]{:S(2)}, u32[]{:S(2)}) %collective-permute-start.2) | collective-permute-done | bytes 675872 | tf_op jit(solution)/shard_map/ppermute | solution.py:558
  58.7 9.3 %collective-permute-done.3 = bf16[528,640]{1,0:T(8,128)(2,1)} collective-permute-done((bf16[528,640]{1,0:T(8,128)(2,1)}, bf16[528,640]{1,0:T(8,128)(2,1)}, u32[]{:S(2)}, u32[]{:S(2)}) %collective-permute-start.3) | collective-permute-done | bytes 675872 | tf_op jit(solution)/shard_map/ppermute | solution.py:558
  79.8 15.3 %qkv.1.q_ref.kv_ref.refs_8_ = bf16[2048,2432]{1,0:T(8,128)(2,1)} custom-call(bf16[256,2048]{1,0:T(8,128)(2,1)} %copy-done.6, bf16[256,2048]{1,0:T(8,128)(2,1)} %collective-permute-done.1.refs_1_, bf16[256,2048]{1,0:T(8,128)(2,1)} %collective-permute-done.4.refs_2_, bf16[256,2048]{1,0:T(8,128)(2,1)} %collective-permute-done.5.refs_3_, ...), custom_call_target="tpu_custom_call" | custom-call | flops 1 | bytes 1 | tf_op jit(solution)/shard_map/qkv/pallas_call | solution.py:165
  95.2 7.6 %collective-permute-done.10.refs_9_ = bf16[256,2048]{1,0:T(8,128)(2,1)S(1)} collective-permute-done((bf16[256,2048]{1,0:T(8,128)(2,1)S(1)}, bf16[256,2048]{1,0:T(8,128)(2,1)S(1)}, u32[]{:S(2)}, u32[]{:S(2)}) %collective-permute-start.10) | collective-permute-done | bytes 1048608 | tf_op jit(solution)/shard_map/ppermute | solution.py:54
  105.7 21.8 %attend.1.refs_0_.h_ref.refs_9_ = f32[2048,384]{1,0:T(8,128)} custom-call(s32[8]{0:T(128)} %select_reduce_fusion.2.place, s32[8]{0:T(128)} %and_select_fusion.2.first, bf16[2048,2432]{1,0:T(8,128)(2,1)} %qkv.1.q_ref.kv_ref.refs_8_, bf16[2048,2432]{1,0:T(8,128)(2,1)} %qkv.1.q_ref.kv_ref.refs_8_, s32[2048,1]{1,0:T(8,128)} %copy.28.start_ref), custom_call_target="tpu_custom_call" | custom-call | flops 1 | bytes 1 | tf_op jit(solution)/shard_map/attend/pallas_call | solution.py:382
  130.5 3.8 back.14
  134.8 3.5 back.13
  139.9 4.2 back.12
  148.2 13.3 %collective-permute-done.19 = bf16[256,2048]{1,0:T(8,128)(2,1)S(1)} collective-permute-done((bf16[256,2048]{1,0:T(8,128)(2,1)S(1)}, bf16[256,2048]{1,0:T(8,128)(2,1)S(1)}, u32[]{:S(2)}, u32[]{:S(2)}) %collective-permute-start.19) | collective-permute-done | bytes 1048608 | tf_op jit(solution)/shard_map/ppermute | solution.py:58
  165.0 24.0 %collective-permute-done.21 = bf16[256,2048]{1,0:T(8,128)(2,1)} collective-permute-done((bf16[256,2048]{1,0:T(8,128)(2,1)S(1)}, bf16[256,2048]{1,0:T(8,128)(2,1)}, u32[]{:S(2)}, u32[]{:S(2)}) %collective-permute-start.21) | collective-permute-done | bytes 1048608 | tf_op jit(solution)/shard_map/ppermute | solution.py:54
  188.9 3.4 multiply_reduce_fusion.2
  194.6 23.3 %collective-permute-done.22.refs_1_ = bf16[256,2048]{1,0:T(8,128)(2,1)S(1)} collective-permute-done((bf16[256,2048]{1,0:T(8,128)(2,1)S(1)}, bf16[256,2048]{1,0:T(8,128)(2,1)S(1)}, u32[]{:S(2)}, u32[]{:S(2)}) %collective-permute-start.22) | collective-permute-done | bytes 1048608 | tf_op jit(solution)/shard_map/ppermute | solution.py:54
  219.8 12.9 %collective-permute-done.24.refs_3_ = bf16[256,2048]{1,0:T(8,128)(2,1)S(1)} collective-permute-done((bf16[256,2048]{1,0:T(8,128)(2,1)S(1)}, bf16[256,2048]{1,0:T(8,128)(2,1)S(1)}, u32[]{:S(2)}, u32[]{:S(2)}) %collective-permute-start.24) | collective-permute-done | bytes 1048608 | tf_op jit(solution)/shard_map/ppermute | solution.py:58
  236.6 21.8 %ffn.2.refs_16_.refs_17_.refs_0_ = bf16[2048,1536]{1,0:T(8,128)(2,1)} custom-call(bf16[256,2048]{1,0:T(8,128)(2,1)} %copy-done.5, bf16[256,2048]{1,0:T(8,128)(2,1)} %copy-done.20, bf16[256,2048]{1,0:T(8,128)(2,1)} %copy-done.21, bf16[256,2048]{1,0:T(8,128)(2,1)} %copy-done.23, bf16[256,2048]{1,0:T(8,128)(2,1)} %copy-done.22, bf16[256,2048]{1,0:T(8,128)(2,1)} %copy-done.24, ...), custom_call_target="tpu_custom_call" | custom-call | flops 1 | bytes 1 | tf_op jit(solution)/shard_map/ffn/pallas_call | solution.py:204
  258.4 19.3 %weight_grads.3 = bf16[2048,1536]{1,0:T(8,128)(2,1)} custom-call(bf16[256,2048]{1,0:T(8,128)(2,1)} %copy-done.5, bf16[256,2048]{1,0:T(8,128)(2,1)} %copy-done.20, bf16[256,2048]{1,0:T(8,128)(2,1)} %copy-done.21, bf16[256,2048]{1,0:T(8,128)(2,1)} %copy-done.23, bf16[256,2048]{1,0:T(8,128)(2,1)} %copy-done.22, bf16[256,2048]{1,0:T(8,128)(2,1)} %copy-done.24, ...), custom_call_target="tpu_custom_call" | custom-call | flops 20000000000 | bytes 1 | tf_op jit(solution)/shard_map/weight_grads/pallas_call | solution.py:240
  278.1 13.4 %back.15.refs_2_ = bf16[2048,2048]{1,0:T(8,128)(2,1)} custom-call(bf16[2048,1536]{1,0:T(8,128)(2,1)} %ffn.2.refs_16_.refs_17_.refs_0_, bf16[2048,1536]{1,0:T(8,128)(2,1)} %all-gather.3.cloned.1.call-done.refs_16_.refs_1_.refs_2_), custom_call_target="tpu_custom_call" | custom-call | flops 1 | bytes 1 | tf_op jit(solution)/shard_map/back/pallas_call | solution.py:275
  291.5 5.0 all-gather.5.cloned.1.call-done.refs_16_.refs_1_.refs_3_
  296.4 21.7 %ffn.3.refs_0_.refs_16_.refs_17_.refs_1_ = bf16[2048,1536]{1,0:T(8,128)(2,1)} custom-call(bf16[256,2048]{1,0:T(8,128)(2,1)} %copy-done.5, bf16[256,2048]{1,0:T(8,128)(2,1)} %copy-done.20, bf16[256,2048]{1,0:T(8,128)(2,1)} %copy-done.21, bf16[256,2048]{1,0:T(8,128)(2,1)} %copy-done.23, bf16[256,2048]{1,0:T(8,128)(2,1)} %copy-done.22, ...), custom_call_target="tpu_custom_call" | custom-call | flops 1 | bytes 1 | tf_op jit(solution)/shard_map/ffn/pallas_call | solution.py:204
  318.2 9.3 %back.17 = bf16[1024,2048]{1,0:T(8,128)(2,1)} custom-call(bf16[2048,1536]{1,0:T(8,128)(2,1)} %ffn.3.refs_0_.refs_16_.refs_17_.refs_1_, bf16[2048,1536]{1,0:T(8,128)(2,1)} %all-gather.5.cloned.1.call-done.refs_16_.refs_1_.refs_3_, bf16[2048,2048]{1,0:T(8,128)(2,1)} %back.15.refs_2_), custom_call_target="tpu_custom_call" | custom-call | flops 1 | bytes 1 | tf_op jit(solution)/shard_map/back/pallas_call | solution.py:275
  327.6 9.6 %back.16 = bf16[1024,2048]{1,0:T(8,128)(2,1)} custom-call(bf16[2048,1536]{1,0:T(8,128)(2,1)} %ffn.3.refs_0_.refs_16_.refs_17_.refs_1_, bf16[2048,1536]{1,0:T(8,128)(2,1)} %all-gather.5.cloned.1.call-done.refs_16_.refs_1_.refs_3_, bf16[2048,2048]{1,0:T(8,128)(2,1)} %back.15.refs_2_), custom_call_target="tpu_custom_call" | custom-call | flops 1 | bytes 1 | tf_op jit(solution)/shard_map/back/pallas_call | solution.py:275
  337.2 3.3 slice_add_fusion
  342.1 19.3 %weight_grads.4 = bf16[2048,1536]{1,0:T(8,128)(2,1)} custom-call(bf16[256,2048]{1,0:T(8,128)(2,1)} %copy-done.5, bf16[256,2048]{1,0:T(8,128)(2,1)} %copy-done.20, bf16[256,2048]{1,0:T(8,128)(2,1)} %copy-done.21, bf16[256,2048]{1,0:T(8,128)(2,1)} %copy-done.23, bf16[256,2048]{1,0:T(8,128)(2,1)} %copy-done.22, bf16[256,2048]{1,0:T(8,128)(2,1)} %copy-done.24, ...), custom_call_target="tpu_custom_call" | custom-call | flops 20000000000 | bytes 1 | tf_op jit(solution)/shard_map/weight_grads/pallas_call | solution.py:240
  361.5 5.2 collective-permute-done.30
  366.7 3.2 fusion.2.refs_0_
  371.6 6.3 back.18
  377.9 7.0 %collective-permute-done.31.refs_1_ = bf16[256,2048]{1,0:T(8,128)(2,1)S(1)} collective-permute-done((bf16[256,2048]{1,0:T(8,128)(2,1)S(1)}, bf16[256,2048]{1,0:T(8,128)(2,1)S(1)}, u32[]{:S(2)}, u32[]{:S(2)}) %collective-permute-start.31) | collective-permute-done | bytes 1048608 | tf_op jit(solution)/shard_map/ppermute | solution.py:54
  385.8 4.9 norm_back.2.refs_0_.refs_5_
  393.8 6.3 back.20
  400.1 8.8 %back.19 = bf16[1024,2048]{1,0:T(8,128)(2,1)} custom-call(bf16[2048,1536]{1,0:T(8,128)(2,1)} %ffn.2.refs_16_.refs_17_.refs_0_, bf16[2048,1536]{1,0:T(8,128)(2,1)} %ffn.3.refs_0_.refs_16_.refs_17_.refs_1_, bf16[2048,1536]{1,0:T(8,128)(2,1)} %all-gather.3.cloned.1.call-done.refs_16_.refs_1_.refs_2_, ...), custom_call_target="tpu_custom_call" | custom-call | flops 7000000000 | bytes 1 | tf_op jit(solution)/shard_map/back/pallas_call | solution.py:275
  408.9 7.3 %collective-permute-done.32.refs_1_ = bf16[256,2048]{1,0:T(8,128)(2,1)} collective-permute-done((bf16[256,2048]{1,0:T(8,128)(2,1)}, bf16[256,2048]{1,0:T(8,128)(2,1)}, u32[]{:S(2)}, u32[]{:S(2)}) %collective-permute-start.32) | collective-permute-done | bytes 1048608 | tf_op jit(solution)/shard_map/ppermute | solution.py:54
  420.5 4.8 broadcast_select_fusion
  425.3 6.5 %collective-permute-done.38.refs_3_ = bf16[256,2048]{1,0:T(8,128)(2,1)} collective-permute-done((bf16[256,2048]{1,0:T(8,128)(2,1)}, bf16[256,2048]{1,0:T(8,128)(2,1)}, u32[]{:S(2)}, u32[]{:S(2)}) %collective-permute-start.38) | collective-permute-done | bytes 1048608 | tf_op jit(solution)/shard_map/ppermute | solution.py:58
  437.3 9.6 %front.1.d_ref = bf16[2048,256]{1,0:T(8,128)(2,1)} custom-call(bf16[256,2048]{1,0:T(8,128)(2,1)} %norm_back.2.refs_0_.refs_5_, bf16[256,2048]{1,0:T(8,128)(2,1)} %collective-permute-done.32.refs_1_, bf16[256,2048]{1,0:T(8,128)(2,1)} %collective-permute-done.33.refs_2_, bf16[256,2048]{1,0:T(8,128)(2,1)} %collective-permute-done.38.refs_3_, ...), custom_call_target="tpu_custom_call" | custom-call | flops 1 | bytes 1 | tf_op jit(solution)/shard_map/front/pallas_call | solution.py:301
  446.9 33.7 %attend_back.1.refs_0_.refs_1_.refs_10_ = bf16[2048,384]{1,0:T(8,128)(2,1)} custom-call(s32[8]{0:T(128)} %select_reduce_fusion.2.place, s32[8]{0:T(128)} %and_select_fusion.2.first, bf16[2048,2432]{1,0:T(8,128)(2,1)} %qkv.1.q_ref.kv_ref.refs_8_, bf16[2048,256]{1,0:T(8,128)(2,1)} %front.1.d_ref, f32[2048,384]{1,0:T(8,128)} %attend.1.refs_0_.h_ref.refs_9_, ...), custom_call_target="tpu_custom_call" | custom-call | flops 1 | bytes 1 | tf_op jit(solution)/shard_map/attend_back/pallas_call | solution.py:479
  483.4 4.1 back.23
  487.5 4.2 back.22
  491.7 5.6 back.21
  498.3 3.1 slice_add_fusion.2
  502.0 12.6 %weight_grads.5 = bf16[2048,640]{1,0:T(8,128)(2,1)} custom-call(bf16[256,2048]{1,0:T(8,128)(2,1)} %norm_back.2.refs_0_.refs_5_, bf16[256,2048]{1,0:T(8,128)(2,1)} %collective-permute-done.32.refs_1_, bf16[256,2048]{1,0:T(8,128)(2,1)} %collective-permute-done.33.refs_2_, bf16[256,2048]{1,0:T(8,128)(2,1)} %collective-permute-done.38.refs_3_, ...), custom_call_target="tpu_custom_call" | custom-call | flops 20000000000 | bytes 1 | tf_op jit(solution)/shard_map/weight_grads/pallas_call | solution.py:240
  514.6 9.6 %collective-permute-done.47 = bf16[256,2048]{1,0:T(8,128)(2,1)} collective-permute-done((bf16[256,2048]{1,0:T(8,128)(2,1)}, bf16[256,2048]{1,0:T(8,128)(2,1)}, u32[]{:S(2)}, u32[]{:S(2)}) %collective-permute-start.47) | collective-permute-done | bytes 1048608 | tf_op jit(solution)/shard_map/ppermute | solution.py:50
  528.0 4.1 fusion.4
  535.6 17.6 %collective-permute-done.50 = bf16[256,2048]{1,0:T(8,128)(2,1)} collective-permute-done((bf16[256,2048]{1,0:T(8,128)(2,1)}, bf16[256,2048]{1,0:T(8,128)(2,1)}, u32[]{:S(2)}, u32[]{:S(2)}) %collective-permute-start.50) | collective-permute-done | bytes 1048608 | tf_op jit(solution)/shard_map/ppermute | solution.py:46
  555.4 9.6 %collective-permute-done.53 = bf16[512,1536]{1,0:T(8,128)(2,1)S(1)} collective-permute-done((bf16[512,1536]{1,0:T(8,128)(2,1)}, bf16[512,1536]{1,0:T(8,128)(2,1)S(1)}, u32[]{:S(2)}, u32[]{:S(2)}) %collective-permute-start.53) | collective-permute-done | bytes 1572896 | tf_op jit(solution)/shard_map/ppermute | solution.py:50
  580.3 7.2 %collective-permute-done.49.refs_2_ = bf16[256,2048]{1,0:T(8,128)(2,1)S(1)} collective-permute-done((bf16[256,2048]{1,0:T(8,128)(2,1)S(1)}, bf16[256,2048]{1,0:T(8,128)(2,1)S(1)}, u32[]{:S(2)}, u32[]{:S(2)}) %collective-permute-start.49) | collective-permute-done | bytes 1048608 | tf_op jit(solution)/shard_map/ppermute | solution.py:54
  589.4 5.2 norm_back.3
  601.7 18.6 %collective-permute-done.56 = f32[2,512]{1,0:T(2,128)S(1)} collective-permute-done((f32[2,512]{1,0:T(2,128)S(1)}, f32[2,512]{1,0:T(2,128)S(1)}, u32[]{:S(2)}, u32[]{:S(2)}) %collective-permute-start.56) | collective-permute-done | bytes 4128 | tf_op jit(solution)/shard_map/ppermute | solution.py:46
  (315 shorter events, 132.5 us)
Async XLA Ops:
  7.2 181.8 %all-gather.3.cloned.1.call-start = ((), (), s32[]{:S(2)}) async-start(), calls=%async_computation.3 | async-start | bytes 7864320 | tf_op jit(solution)/shard_map/all_gather | solution.py:703
  11.7 20.3 %collective-permute-start = (bf16[528,640]{1,0:T(8,128)(2,1)S(1)}, bf16[528,640]{1,0:T(8,128)(2,1)}, u32[]{:S(2)}, u32[]{:S(2)}) collective-permute-start(bf16[528,640]{1,0:T(8,128)(2,1)S(1)} %fusion.6), channel_id=1, source_target_pairs={{0,8},{8,16},{16,24},{24,0},{1,9},{9,17},{17,25},{25,1},{2,10},{10... | collective-permute-start | bytes 2027528 | tf_op jit(solution)/shard_map/ppermute | solution.py:558
  16.0 16.0 %collective-permute-start.1 = (bf16[256,2048]{1,0:T(8,128)(2,1)S(1)}, bf16[256,2048]{1,0:T(8,128)(2,1)}, u32[]{:S(2)}, u32[]{:S(2)}) collective-permute-start(bf16[256,2048]{1,0:T(8,128)(2,1)S(1)} %constant_dynamic-slice_fusion.11.refs_0_.refs_3_), channel_id=1, source_target_pairs={{0,4},{1,3},{2,6},{3,1},{4,0},{5,7},{6,2},{7,5},{8,12},{9,11},{10,... | collective-permute-start | bytes 3145736 | tf_op jit(solution)/shard_map/ppermute | solution.py:54
  32.0 18.5 %collective-permute-start.2 = (bf16[528,640]{1,0:T(8,128)(2,1)}, bf16[528,640]{1,0:T(8,128)(2,1)}, u32[]{:S(2)}, u32[]{:S(2)}) collective-permute-start(bf16[528,640]{1,0:T(8,128)(2,1)} %collective-permute-done), channel_id=1, source_target_pairs={{0,8},{8,16},{16,24},{24,0},{1,9},{9,17},{17,25},{25,1},{2,10},{10... | collective-permute-start | bytes 2027528 | tf_op jit(solution)/shard_map/ppermute | solution.py:558
  32.5 23.8 %collective-permute-start.4 = (bf16[256,2048]{1,0:T(8,128)(2,1)S(1)}, bf16[256,2048]{1,0:T(8,128)(2,1)}, u32[]{:S(2)}, u32[]{:S(2)}) collective-permute-start(bf16[256,2048]{1,0:T(8,128)(2,1)S(1)} %constant_dynamic-slice_fusion.11.refs_0_.refs_3_), channel_id=1, source_target_pairs={{0,2},{1,5},{2,0},{3,7},{4,6},{5,1},{6,4},{7,3},{8,10},{9,13},{10,... | collective-permute-start | bytes 3145736 | tf_op jit(solution)/shard_map/ppermute | solution.py:58
  34.1 24.6 %collective-permute-start.5 = (bf16[256,2048]{1,0:T(8,128)(2,1)}, bf16[256,2048]{1,0:T(8,128)(2,1)}, u32[]{:S(2)}, u32[]{:S(2)}) collective-permute-start(bf16[256,2048]{1,0:T(8,128)(2,1)} %collective-permute-done.1.refs_1_), channel_id=1, source_target_pairs={{0,2},{1,5},{2,0},{3,7},{4,6},{5,1},{6,4},{7,3},{8,10},{9,13},{10,... | collective-permute-start | bytes 3145736 | tf_op jit(solution)/shard_map/ppermute | solution.py:58
  50.5 17.6 %collective-permute-start.3 = (bf16[528,640]{1,0:T(8,128)(2,1)}, bf16[528,640]{1,0:T(8,128)(2,1)}, u32[]{:S(2)}, u32[]{:S(2)}) collective-permute-start(bf16[528,640]{1,0:T(8,128)(2,1)} %collective-permute-done.2), channel_id=1, source_target_pairs={{0,8},{8,16},{16,24},{24,0},{1,9},{9,17},{17,25},{25,1},{2,10},{10... | collective-permute-start | bytes 2027528 | tf_op jit(solution)/shard_map/ppermute | solution.py:558
  68.0 228.4 %all-gather.5.cloned.1.call-start = ((), (), s32[]{:S(2)}) async-start(), calls=%async_computation.4 | async-start | bytes 7864320 | tf_op jit(solution)/shard_map/all_gather | solution.py:703
  77.3 25.4 %collective-permute-start.10 = (bf16[256,2048]{1,0:T(8,128)(2,1)S(1)}, bf16[256,2048]{1,0:T(8,128)(2,1)S(1)}, u32[]{:S(2)}, u32[]{:S(2)}) collective-permute-start(bf16[256,2048]{1,0:T(8,128)(2,1)S(1)} %constant_dynamic-slice_fusion.6.refs_8_.refs_4_), channel_id=1, source_target_pairs={{0,4},{1,3},{2,6},{3,1},{4,0},{5,7},{6,2},{7,5},{8,12},{9,11},{10,... | collective-permute-start | bytes 3145736 | tf_op jit(solution)/shard_map/ppermute | solution.py:54
  78.6 24.2 %collective-permute-start.11 = (bf16[256,2048]{1,0:T(8,128)(2,1)S(1)}, bf16[256,2048]{1,0:T(8,128)(2,1)}, u32[]{:S(2)}, u32[]{:S(2)}) collective-permute-start(bf16[256,2048]{1,0:T(8,128)(2,1)S(1)} %constant_dynamic-slice_fusion.6.refs_8_.refs_4_), channel_id=1, source_target_pairs={{0,2},{1,5},{2,0},{3,7},{4,6},{5,1},{6,4},{7,3},{8,10},{9,13},{10,... | collective-permute-start | bytes 3145736 | tf_op jit(solution)/shard_map/ppermute | solution.py:58
  79.8 47.8 %collective-permute-start.13 = (bf16[256,2048]{1,0:T(8,128)(2,1)S(1)}, bf16[256,2048]{1,0:T(8,128)(2,1)}, u32[]{:S(2)}, u32[]{:S(2)}) collective-permute-start(bf16[256,2048]{1,0:T(8,128)(2,1)S(1)} %constant_dynamic-slice_fusion.6.refs_8_.refs_4_), channel_id=1, source_target_pairs={{0,1},{1,0},{2,3},{3,2},{4,5},{5,4},{6,7},{7,6},{8,9},{9,8},{10,11... | collective-permute-start | bytes 3145736 | tf_op jit(solution)/shard_map/ppermute | solution.py:42
  102.8 24.7 %collective-permute-start.12 = (bf16[256,2048]{1,0:T(8,128)(2,1)S(1)}, bf16[256,2048]{1,0:T(8,128)(2,1)}, u32[]{:S(2)}, u32[]{:S(2)}) collective-permute-start(bf16[256,2048]{1,0:T(8,128)(2,1)S(1)} %collective-permute-done.10.refs_9_), channel_id=1, source_target_pairs={{0,2},{1,5},{2,0},{3,7},{4,6},{5,1},{6,4},{7,3},{8,10},{9,13},{10,... | collective-permute-start | bytes 3145736 | tf_op jit(solution)/shard_map/ppermute | solution.py:58
  103.8 23.7 %collective-permute-start.14 = (bf16[256,2048]{1,0:T(8,128)(2,1)S(1)}, bf16[256,2048]{1,0:T(8,128)(2,1)}, u32[]{:S(2)}, u32[]{:S(2)}) collective-permute-start(bf16[256,2048]{1,0:T(8,128)(2,1)S(1)} %collective-permute-done.10.refs_9_), channel_id=1, source_target_pairs={{0,1},{1,0},{2,3},{3,2},{4,5},{5,4},{6,7},{7,6},{8,9},{9,8},{10,11... | collective-permute-start | bytes 3145736 | tf_op jit(solution)/shard_map/ppermute | solution.py:42
  104.2 23.3 %collective-permute-start.15 = (bf16[256,2048]{1,0:T(8,128)(2,1)}, bf16[256,2048]{1,0:T(8,128)(2,1)}, u32[]{:S(2)}, u32[]{:S(2)}) collective-permute-start(bf16[256,2048]{1,0:T(8,128)(2,1)} %collective-permute-done.11.refs_10_), channel_id=1, source_target_pairs={{0,1},{1,0},{2,3},{3,2},{4,5},{5,4},{6,7},{7,6},{8,9},{9,8},{10,11... | collective-permute-start | bytes 3145736 | tf_op jit(solution)/shard_map/ppermute | solution.py:42
  138.2 23.2 %collective-permute-start.17 = (bf16[512,2048]{1,0:T(8,128)(2,1)}, bf16[512,2048]{1,0:T(8,128)(2,1)S(1)}, u32[]{:S(2)}, u32[]{:S(2)}) collective-permute-start(bf16[512,2048]{1,0:T(8,128)(2,1)} %back.13), channel_id=1, source_target_pairs={{0,1},{1,0},{2,3},{3,2},{4,5},{5,4},{6,7},{7,6},{8,9},{9,8},{10,11... | collective-permute-start | bytes 6291464 | tf_op jit(solution)/shard_map/ppermute | solution.py:42
  139.7 292.2 %reduce-scatter.4.cloned.1.call-start = ((), (), s32[]{:S(2)}) async-start(), calls=%async_computation.5 | async-start | bytes 7864320 | tf_op jit(solution)/shard_map/reduce_scatter | solution.py:734
  146.6 14.9 %collective-permute-start.19 = (bf16[256,2048]{1,0:T(8,128)(2,1)S(1)}, bf16[256,2048]{1,0:T(8,128)(2,1)S(1)}, u32[]{:S(2)}, u32[]{:S(2)}) collective-permute-start(bf16[256,2048]{1,0:T(8,128)(2,1)S(1)} %get-tuple-element.152), channel_id=1, source_target_pairs={{0,2},{1,5},{2,0},{3,7},{4,6},{5,1},{6,4},{7,3},{8,10},{9,13},{10,... | collective-permute-start | bytes 3145736 | tf_op jit(solution)/shard_map/ppermute | solution.py:58
  162.9 26.1 %collective-permute-start.21 = (bf16[256,2048]{1,0:T(8,128)(2,1)S(1)}, bf16[256,2048]{1,0:T(8,128)(2,1)}, u32[]{:S(2)}, u32[]{:S(2)}) collective-permute-start(bf16[256,2048]{1,0:T(8,128)(2,1)S(1)} %fusion.5), channel_id=1, source_target_pairs={{0,4},{1,3},{2,6},{3,1},{4,0},{5,7},{6,2},{7,5},{8,12},{9,11},{10,... | collective-permute-start | bytes 3145736 | tf_op jit(solution)/shard_map/ppermute | solution.py:54
  164.4 24.6 %collective-permute-start.20 = (bf16[256,2048]{1,0:T(8,128)(2,1)S(1)}, bf16[256,2048]{1,0:T(8,128)(2,1)}, u32[]{:S(2)}, u32[]{:S(2)}) collective-permute-start(bf16[256,2048]{1,0:T(8,128)(2,1)S(1)} %get-tuple-element.91), channel_id=1, source_target_pairs={{0,2},{1,5},{2,0},{3,7},{4,6},{5,1},{6,4},{7,3},{8,10},{9,13},{10,... | collective-permute-start | bytes 3145736 | tf_op jit(solution)/shard_map/ppermute | solution.py:58
  192.6 25.3 %collective-permute-start.22 = (bf16[256,2048]{1,0:T(8,128)(2,1)S(1)}, bf16[256,2048]{1,0:T(8,128)(2,1)S(1)}, u32[]{:S(2)}, u32[]{:S(2)}) collective-permute-start(bf16[256,2048]{1,0:T(8,128)(2,1)S(1)} %multiply_convert_fusion.refs_0_), channel_id=1, source_target_pairs={{0,4},{1,3},{2,6},{3,1},{4,0},{5,7},{6,2},{7,5},{8,12},{9,11},{10,... | collective-permute-start | bytes 3145736 | tf_op jit(solution)/shard_map/ppermute | solution.py:54
  193.4 24.5 %collective-permute-start.23 = (bf16[256,2048]{1,0:T(8,128)(2,1)S(1)}, bf16[256,2048]{1,0:T(8,128)(2,1)S(1)}, u32[]{:S(2)}, u32[]{:S(2)}) collective-permute-start(bf16[256,2048]{1,0:T(8,128)(2,1)S(1)} %multiply_convert_fusion.refs_0_), channel_id=1, source_target_pairs={{0,2},{1,5},{2,0},{3,7},{4,6},{5,1},{6,4},{7,3},{8,10},{9,13},{10,... | collective-permute-start | bytes 3145736 | tf_op jit(solution)/shard_map/ppermute | solution.py:58
  194.6 25.2 %collective-permute-start.25 = (bf16[256,2048]{1,0:T(8,128)(2,1)S(1)}, bf16[256,2048]{1,0:T(8,128)(2,1)S(1)}, u32[]{:S(2)}, u32[]{:S(2)}) collective-permute-start(bf16[256,2048]{1,0:T(8,128)(2,1)S(1)} %multiply_convert_fusion.refs_0_), channel_id=1, source_target_pairs={{0,1},{1,0},{2,3},{3,2},{4,5},{5,4},{6,7},{7,6},{8,9},{9,8},{10,11... | collective-permute-start | bytes 3145736 | tf_op jit(solution)/shard_map/ppermute | solution.py:42
  217.9 14.9 %collective-permute-start.24 = (bf16[256,2048]{1,0:T(8,128)(2,1)S(1)}, bf16[256,2048]{1,0:T(8,128)(2,1)S(1)}, u32[]{:S(2)}, u32[]{:S(2)}) collective-permute-start(bf16[256,2048]{1,0:T(8,128)(2,1)S(1)} %collective-permute-done.22.refs_1_), channel_id=1, source_target_pairs={{0,2},{1,5},{2,0},{3,7},{4,6},{5,1},{6,4},{7,3},{8,10},{9,13},{10,... | collective-permute-start | bytes 3145736 | tf_op jit(solution)/shard_map/ppermute | solution.py:58
  277.7 249.7 %reduce-scatter.6.cloned.1.call-start = ((), (), s32[]{:S(2)}) async-start(), calls=%async_computation.6 | async-start | bytes 7864320 | tf_op jit(solution)/shard_map/reduce_scatter | solution.py:734
  340.5 26.2 %collective-permute-start.30 = (bf16[512,2048]{1,0:T(8,128)(2,1)S(1)}, bf16[512,2048]{1,0:T(8,128)(2,1)}, u32[]{:S(2)}, u32[]{:S(2)}) collective-permute-start(bf16[512,2048]{1,0:T(8,128)(2,1)S(1)} %slice_add_fusion), channel_id=1, source_target_pairs={{0,2},{1,5},{2,0},{3,7},{4,6},{5,1},{6,4},{7,3},{8,10},{9,13},{10,... | collective-permute-start | bytes 6291464 | tf_op jit(solution)/shard_map/ppermute | solution.py:58
  361.4 235.6 %reduce-scatter.8.cloned.1.call-start = ((), (), s32[]{:S(2)}) async-start(), calls=%async_computation.7 | async-start | bytes 3276800 | tf_op jit(solution)/shard_map/reduce_scatter | solution.py:796
  370.0 14.9 %collective-permute-start.31 = (bf16[256,2048]{1,0:T(8,128)(2,1)S(1)}, bf16[256,2048]{1,0:T(8,128)(2,1)S(1)}, u32[]{:S(2)}, u32[]{:S(2)}) collective-permute-start(bf16[256,2048]{1,0:T(8,128)(2,1)S(1)} %slice.217), channel_id=1, source_target_pairs={{0,4},{1,3},{2,6},{3,1},{4,0},{5,7},{6,2},{7,5},{8,12},{9,11},{10,... | collective-permute-start | bytes 3145736 | tf_op jit(solution)/shard_map/ppermute | solution.py:54
  377.9 40.1 %collective-permute-start.35 = (bf16[512,2048]{1,0:T(8,128)(2,1)}, bf16[512,2048]{1,0:T(8,128)(2,1)}, u32[]{:S(2)}, u32[]{:S(2)}) collective-permute-start(bf16[512,2048]{1,0:T(8,128)(2,1)} %back.18), channel_id=1, source_target_pairs={{0,1},{1,0},{2,3},{3,2},{4,5},{5,4},{6,7},{7,6},{8,9},{9,8},{10,11... | collective-permute-start | bytes 6291464 | tf_op jit(solution)/shard_map/ppermute | solution.py:42
  390.7 25.5 %collective-permute-start.32 = (bf16[256,2048]{1,0:T(8,128)(2,1)}, bf16[256,2048]{1,0:T(8,128)(2,1)}, u32[]{:S(2)}, u32[]{:S(2)}) collective-permute-start(bf16[256,2048]{1,0:T(8,128)(2,1)} %norm_back.2.refs_0_.refs_5_), channel_id=1, source_target_pairs={{0,4},{1,3},{2,6},{3,1},{4,0},{5,7},{6,2},{7,5},{8,12},{9,11},{10,... | collective-permute-start | bytes 3145736 | tf_op jit(solution)/shard_map/ppermute | solution.py:54
  392.3 23.9 %collective-permute-start.33 = (bf16[256,2048]{1,0:T(8,128)(2,1)}, bf16[256,2048]{1,0:T(8,128)(2,1)}, u32[]{:S(2)}, u32[]{:S(2)}) collective-permute-start(bf16[256,2048]{1,0:T(8,128)(2,1)} %norm_back.2.refs_0_.refs_5_), channel_id=1, source_target_pairs={{0,2},{1,5},{2,0},{3,7},{4,6},{5,1},{6,4},{7,3},{8,10},{9,13},{10,... | collective-permute-start | bytes 3145736 | tf_op jit(solution)/shard_map/ppermute | solution.py:58
  416.7 15.1 %collective-permute-start.38 = (bf16[256,2048]{1,0:T(8,128)(2,1)}, bf16[256,2048]{1,0:T(8,128)(2,1)}, u32[]{:S(2)}, u32[]{:S(2)}) collective-permute-start(bf16[256,2048]{1,0:T(8,128)(2,1)} %collective-permute-done.32.refs_1_), channel_id=1, source_target_pairs={{0,2},{1,5},{2,0},{3,7},{4,6},{5,1},{6,4},{7,3},{8,10},{9,13},{10,... | collective-permute-start | bytes 3145736 | tf_op jit(solution)/shard_map/ppermute | solution.py:58
  417.2 14.6 %collective-permute-start.40 = (bf16[256,2048]{1,0:T(8,128)(2,1)}, bf16[256,2048]{1,0:T(8,128)(2,1)}, u32[]{:S(2)}, u32[]{:S(2)}) collective-permute-start(bf16[256,2048]{1,0:T(8,128)(2,1)} %collective-permute-done.32.refs_1_), channel_id=1, source_target_pairs={{0,1},{1,0},{2,3},{3,2},{4,5},{5,4},{6,7},{7,6},{8,9},{9,8},{10,11... | collective-permute-start | bytes 3145736 | tf_op jit(solution)/shard_map/ppermute | solution.py:42
  418.0 13.9 %collective-permute-start.41 = (bf16[256,2048]{1,0:T(8,128)(2,1)}, bf16[256,2048]{1,0:T(8,128)(2,1)}, u32[]{:S(2)}, u32[]{:S(2)}) collective-permute-start(bf16[256,2048]{1,0:T(8,128)(2,1)} %collective-permute-done.33.refs_2_), channel_id=1, source_target_pairs={{0,1},{1,0},{2,3},{3,2},{4,5},{5,4},{6,7},{7,6},{8,9},{9,8},{10,11... | collective-permute-start | bytes 3145736 | tf_op jit(solution)/shard_map/ppermute | solution.py:42
  431.9 49.8 %collective-permute-start.43 = (bf16[512,1536]{1,0:T(8,128)(2,1)}, bf16[512,1536]{1,0:T(8,128)(2,1)S(1)}, u32[]{:S(2)}, u32[]{:S(2)}) collective-permute-start(bf16[512,1536]{1,0:T(8,128)(2,1)} %reduce-scatter.4.cloned.1.call-done), channel_id=1, source_target_pairs={{0,4},{4,0},{1,5},{5,1},{2,6},{6,2},{3,7},{7,3},{8,12},{12,8},{9,1... | collective-permute-start | bytes 4718600 | tf_op jit(solution)/shard_map/ppermute | solution.py:50
  433.4 47.2 %collective-permute-start.36 = (bf16[256,2048]{1,0:T(8,128)(2,1)}, bf16[256,2048]{1,0:T(8,128)(2,1)S(1)}, u32[]{:S(2)}, u32[]{:S(2)}) collective-permute-start(bf16[256,2048]{1,0:T(8,128)(2,1)} %get-tuple-element.150), channel_id=1, source_target_pairs={{0,2},{2,0},{1,3},{3,1},{4,6},{6,4},{5,7},{7,5},{8,10},{10,8},{9,1... | collective-permute-start | bytes 3145736 | tf_op jit(solution)/shard_map/ppermute | solution.py:46
  434.0 47.7 %collective-permute-start.37 = (bf16[256,2048]{1,0:T(8,128)(2,1)}, bf16[256,2048]{1,0:T(8,128)(2,1)S(1)}, u32[]{:S(2)}, u32[]{:S(2)}) collective-permute-start(bf16[256,2048]{1,0:T(8,128)(2,1)} %get-tuple-element.143), channel_id=1, source_target_pairs={{0,2},{2,0},{1,3},{3,1},{4,6},{6,4},{5,7},{7,5},{8,10},{10,8},{9,1... | collective-permute-start | bytes 3145736 | tf_op jit(solution)/shard_map/ppermute | solution.py:46
  497.3 30.7 %collective-permute-start.44 = (bf16[512,2048]{1,0:T(8,128)(2,1)}, bf16[512,2048]{1,0:T(8,128)(2,1)}, u32[]{:S(2)}, u32[]{:S(2)}) collective-permute-start(bf16[512,2048]{1,0:T(8,128)(2,1)} %back.22), channel_id=1, source_target_pairs={{0,1},{1,0},{2,3},{3,2},{4,5},{5,4},{6,7},{7,6},{8,9},{9,8},{10,11... | collective-permute-start | bytes 6291464 | tf_op jit(solution)/shard_map/ppermute | solution.py:42
  497.8 26.3 %collective-permute-start.47 = (bf16[256,2048]{1,0:T(8,128)(2,1)}, bf16[256,2048]{1,0:T(8,128)(2,1)}, u32[]{:S(2)}, u32[]{:S(2)}) collective-permute-start(bf16[256,2048]{1,0:T(8,128)(2,1)} %add.380), channel_id=1, source_target_pairs={{0,4},{4,0},{1,5},{5,1},{2,6},{6,2},{3,7},{7,3},{8,12},{12,8},{9,1... | collective-permute-start | bytes 3145736 | tf_op jit(solution)/shard_map/ppermute | solution.py:50
  501.5 26.5 %collective-permute-start.46 = (bf16[256,2048]{1,0:T(8,128)(2,1)}, bf16[256,2048]{1,0:T(8,128)(2,1)}, u32[]{:S(2)}, u32[]{:S(2)}) collective-permute-start(bf16[256,2048]{1,0:T(8,128)(2,1)} %get-tuple-element.146), channel_id=1, source_target_pairs={{0,2},{1,5},{2,0},{3,7},{4,6},{5,1},{6,4},{7,3},{8,10},{9,13},{10,... | collective-permute-start | bytes 3145736 | tf_op jit(solution)/shard_map/ppermute | solution.py:58
  526.8 26.4 %collective-permute-start.50 = (bf16[256,2048]{1,0:T(8,128)(2,1)}, bf16[256,2048]{1,0:T(8,128)(2,1)}, u32[]{:S(2)}, u32[]{:S(2)}) collective-permute-start(bf16[256,2048]{1,0:T(8,128)(2,1)} %add_convert_fusion), channel_id=1, source_target_pairs={{0,2},{2,0},{1,3},{3,1},{4,6},{6,4},{5,7},{7,5},{8,10},{10,8},{9,1... | collective-permute-start | bytes 3145736 | tf_op jit(solution)/shard_map/ppermute | solution.py:46
  527.3 46.1 %collective-permute-start.51 = (bf16[256,2048]{1,0:T(8,128)(2,1)}, bf16[256,2048]{1,0:T(8,128)(2,1)}, u32[]{:S(2)}, u32[]{:S(2)}) collective-permute-start(bf16[256,2048]{1,0:T(8,128)(2,1)} %add_convert_fusion), channel_id=1, source_target_pairs={{0,1},{1,0},{2,3},{3,2},{4,5},{5,4},{6,7},{7,6},{8,9},{9,8},{10,11... | collective-permute-start | bytes 3145736 | tf_op jit(solution)/shard_map/ppermute | solution.py:42
  527.4 37.6 %collective-permute-start.53 = (bf16[512,1536]{1,0:T(8,128)(2,1)}, bf16[512,1536]{1,0:T(8,128)(2,1)S(1)}, u32[]{:S(2)}, u32[]{:S(2)}) collective-permute-start(bf16[512,1536]{1,0:T(8,128)(2,1)} %reduce-scatter.6.cloned.1.call-done), channel_id=1, source_target_pairs={{0,4},{4,0},{1,5},{5,1},{2,6},{6,2},{3,7},{7,3},{8,12},{12,8},{9,1... | collective-permute-start | bytes 4718600 | tf_op jit(solution)/shard_map/ppermute | solution.py:50
  532.0 55.5 %collective-permute-start.49 = (bf16[256,2048]{1,0:T(8,128)(2,1)S(1)}, bf16[256,2048]{1,0:T(8,128)(2,1)S(1)}, u32[]{:S(2)}, u32[]{:S(2)}) collective-permute-start(bf16[256,2048]{1,0:T(8,128)(2,1)S(1)} %get-tuple-element.121), channel_id=1, source_target_pairs={{0,4},{1,3},{2,6},{3,1},{4,0},{5,7},{6,2},{7,5},{8,12},{9,11},{10,... | collective-permute-start | bytes 3145736 | tf_op jit(solution)/shard_map/ppermute | solution.py:54
  533.3 54.2 %collective-permute-start.48 = (bf16[256,2048]{1,0:T(8,128)(2,1)S(1)}, bf16[256,2048]{1,0:T(8,128)(2,1)S(1)}, u32[]{:S(2)}, u32[]{:S(2)}) collective-permute-start(bf16[256,2048]{1,0:T(8,128)(2,1)S(1)} %copy-done.45), channel_id=1, source_target_pairs={{0,2},{1,5},{2,0},{3,7},{4,6},{5,1},{6,4},{7,3},{8,10},{9,13},{10,... | collective-permute-start | bytes 3145736 | tf_op jit(solution)/shard_map/ppermute | solution.py:58
  554.9 18.5 %collective-permute-start.52 = (bf16[256,2048]{1,0:T(8,128)(2,1)}, bf16[256,2048]{1,0:T(8,128)(2,1)S(1)}, u32[]{:S(2)}, u32[]{:S(2)}) collective-permute-start(bf16[256,2048]{1,0:T(8,128)(2,1)} %collective-permute-done.50), channel_id=1, source_target_pairs={{0,1},{1,0},{2,3},{3,2},{4,5},{5,4},{6,7},{7,6},{8,9},{9,8},{10,11... | collective-permute-start | bytes 3145736 | tf_op jit(solution)/shard_map/ppermute | solution.py:42
  594.7 29.3 %collective-permute-start.54 = (bf16[256,2048]{1,0:T(8,128)(2,1)}, bf16[256,2048]{1,0:T(8,128)(2,1)}, u32[]{:S(2)}, u32[]{:S(2)}) collective-permute-start(bf16[256,2048]{1,0:T(8,128)(2,1)} %norm_back.3), channel_id=1, source_target_pairs={{0,2},{2,0},{1,3},{3,1},{4,6},{6,4},{5,7},{7,5},{8,10},{10,8},{9,1... | collective-permute-start | bytes 3145736 | tf_op jit(solution)/shard_map/ppermute | solution.py:46
  597.0 27.0 %collective-permute-start.58 = (bf16[512,640]{1,0:T(8,128)(2,1)}, bf16[512,640]{1,0:T(8,128)(2,1)S(1)}, u32[]{:S(2)}, u32[]{:S(2)}) collective-permute-start(bf16[512,640]{1,0:T(8,128)(2,1)} %reduce-scatter.8.cloned.1.call-done), channel_id=1, source_target_pairs={{0,4},{4,0},{1,5},{5,1},{2,6},{6,2},{3,7},{7,3},{8,12},{12,8},{9,1... | collective-permute-start | bytes 1966088 | tf_op jit(solution)/shard_map/ppermute | solution.py:50
  600.6 19.7 %collective-permute-start.56 = (f32[2,512]{1,0:T(2,128)S(1)}, f32[2,512]{1,0:T(2,128)S(1)}, u32[]{:S(2)}, u32[]{:S(2)}) collective-permute-start(f32[2,512]{1,0:T(2,128)S(1)} %fusion.18), channel_id=1, source_target_pairs={{0,2},{2,0},{1,3},{3,1},{4,6},{6,4},{5,7},{7,5},{8,10},{10,8},{9,1... | collective-permute-start | bytes 12296 | tf_op jit(solution)/shard_map/ppermute | solution.py:46
  (73 other events, 1037.0 us)
Sparse Core Ops, SparseCore 0:
  68.2 113.0 all-gather.2
  182.8 113.5 all-gather.4
  298.8 108.9 reduce-scatter.3
  409.9 111.2 reduce-scatter.5
  527.5 49.8 reduce-scatter.7

commit v13 on v12

--- a/solution.py
+++ b/solution.py
@@ -232,7 +232,7 @@
     o_ref[:, split:] = product(refs[x_count : x_count + y_count], b_ref)
 
 
-def weight_grads(x, a, a_width, a_column, y, b, b_width, b_column):
+def weight_grads(x, a, a_width, a_column, y, b, b_width, b_column, work=20):
     depth = x[0].shape[1]
     rows = a.shape[0]
     width = a_width + b_width
@@ -248,7 +248,7 @@
         ],
         out_specs=pl.BlockSpec((step, width), lambda i: (i, 0)),
         compiler_params=params(),
-        cost_estimate=cost(20),
+        cost_estimate=cost(work),
         name="weight_grads",
     )(*x, *y, a, b)
 
@@ -767,7 +767,7 @@
         ]
     )
     attn_grad = weight_grads(
-        d_attn, heads, q_width, 0, (qkv,), after(d_qkv, normed_blocks[3]), q_width + 128, 0
+        d_attn, heads, q_width, 0, (qkv,), after(d_qkv, normed_blocks[3]), q_width + 128, 0, 0
     )
     ffn_far = after(ffn_far, attn_grad)
     result_own = (hidden + (ffn_own.astype(F32) + ffn_far.astype(F32))).astype(BF16)

time: 654 us -> 651 us (level)
  waiting for transfers between devices: 221 us -> 212 us
  transfers between devices with their start and end apart: 66 -> 66, of which waited for: 28 -> 27; matrix products, arithmetic and copies ran while one was open for 13% -> 13% of each run, Pallas kernels for 41% -> 42%
where the time goes in v13:
time: 651 us; the launch traced here: 641 us
  Pallas kernels  267 us (41%)
  waiting for transfers between devices  212 us (33%)
  other arithmetic  68.7 us (11%)
  starting transfers between devices  44.5 us (7%)
  local copies, waits for them, and re-layouts  34 us (5%)
  between operations  15.2 us (2%)
    pallas_call x12, Pallas kernels, back_product(): pl.pallas_call(functools.partial(back_kernel, len(terms)), out_shape=jax....  78.9 us
    ppermute x7, waiting for transfers between devices, swap_first(): return lax.ppermute(v, ('ctx', 'tp'), FIRST)  76.2 us
    pallas_call x3, Pallas kernels, weight_grads(): pl.pallas_call(functools.partial(grads_kernel, len(x), len(y)), out_shape...  51.2 us
    pallas_call x2, Pallas kernels, ffn_chunk(): pl.pallas_call(functools.partial(ffn_kernel, len(x)), out_shape=jax.Shape...  43.5 us
    ppermute x13, waiting for transfers between devices, swap_second(): return lax.ppermute(v, ('ctx', 'tp'), SECOND)  37.4 us
    ppermute x5, waiting for transfers between devices, swap_y(): return lax.ppermute(v, 'tp', ACROSS)  35.8 us
    pallas_call x1, Pallas kernels, attend_back(): pl.pallas_call(attend_back_kernel, out_shape=jax.ShapeDtypeStruct((rows,...  35.2 us
    ppermute x3, waiting for transfers between devices, ring_over(): pieces.append(lax.ppermute(sent, 'fsdp', cycle))  30.9 us
  transfers between devices with their start and end apart: 66, of which 27 were waited for; matrix products, arithmetic and copies ran while one was open for 13% of the time, Pallas kernels for 42%

profile of v13, /device:TPU:0, one launch (start us, length us, event | category | flops | bytes accessed | tf_op | source)
XLA Modules:
  0.0 640.7 jit_solution(17255045849981687500)
XLA Ops:
  20.7 5.6 negate_select_fusion
  26.3 5.7 collective-permute-done
  34.6 15.9 %collective-permute-done.2 = bf16[528,640]{1,0:T(8,128)(2,1)} collective-permute-done((bf16[528,640]{1,0:T(8,128)(2,1)}, bf16[528,640]{1,0:T(8,128)(2,1)}, u32[]{:S(2)}, u32[]{:S(2)}) %collective-permute-start.2) | collective-permute-done | bytes 675872 | tf_op jit(solution)/shard_map/ppermute | solution.py:558
  58.7 9.3 %collective-permute-done.3 = bf16[528,640]{1,0:T(8,128)(2,1)} collective-permute-done((bf16[528,640]{1,0:T(8,128)(2,1)}, bf16[528,640]{1,0:T(8,128)(2,1)}, u32[]{:S(2)}, u32[]{:S(2)}) %collective-permute-start.3) | collective-permute-done | bytes 675872 | tf_op jit(solution)/shard_map/ppermute | solution.py:558
  79.8 15.3 %qkv.1.q_ref.kv_ref.refs_8_ = bf16[2048,2432]{1,0:T(8,128)(2,1)} custom-call(bf16[256,2048]{1,0:T(8,128)(2,1)} %copy-done.7, bf16[256,2048]{1,0:T(8,128)(2,1)} %collective-permute-done.1.refs_1_, bf16[256,2048]{1,0:T(8,128)(2,1)} %collective-permute-done.4.refs_2_, bf16[256,2048]{1,0:T(8,128)(2,1)} %collective-permute-done.5.refs_3_, ...), custom_call_target="tpu_custom_call" | custom-call | flops 1 | bytes 1 | tf_op jit(solution)/shard_map/qkv/pallas_call | solution.py:165
  95.2 7.6 %collective-permute-done.10.refs_9_ = bf16[256,2048]{1,0:T(8,128)(2,1)S(1)} collective-permute-done((bf16[256,2048]{1,0:T(8,128)(2,1)S(1)}, bf16[256,2048]{1,0:T(8,128)(2,1)S(1)}, u32[]{:S(2)}, u32[]{:S(2)}) %collective-permute-start.10) | collective-permute-done | bytes 1048608 | tf_op jit(solution)/shard_map/ppermute | solution.py:54
  105.7 22.7 %attend.1.refs_0_.h_ref.refs_9_ = f32[2048,384]{1,0:T(8,128)} custom-call(s32[8]{0:T(128)} %select_reduce_fusion.2.place, s32[8]{0:T(128)} %and_select_fusion.2.first, bf16[2048,2432]{1,0:T(8,128)(2,1)} %qkv.1.q_ref.kv_ref.refs_8_, bf16[2048,2432]{1,0:T(8,128)(2,1)} %qkv.1.q_ref.kv_ref.refs_8_, s32[2048,1]{1,0:T(8,128)} %copy.28.start_ref), custom_call_target="tpu_custom_call" | custom-call | flops 1 | bytes 1 | tf_op jit(solution)/shard_map/attend/pallas_call | solution.py:382
  131.4 3.8 back.14
  135.6 3.5 back.13
  140.8 4.2 back.12
  149.0 13.3 %collective-permute-done.19 = bf16[256,2048]{1,0:T(8,128)(2,1)S(1)} collective-permute-done((bf16[256,2048]{1,0:T(8,128)(2,1)S(1)}, bf16[256,2048]{1,0:T(8,128)(2,1)S(1)}, u32[]{:S(2)}, u32[]{:S(2)}) %collective-permute-start.19) | collective-permute-done | bytes 1048608 | tf_op jit(solution)/shard_map/ppermute | solution.py:58
  165.9 24.0 %collective-permute-done.21 = bf16[256,2048]{1,0:T(8,128)(2,1)} collective-permute-done((bf16[256,2048]{1,0:T(8,128)(2,1)S(1)}, bf16[256,2048]{1,0:T(8,128)(2,1)}, u32[]{:S(2)}, u32[]{:S(2)}) %collective-permute-start.21) | collective-permute-done | bytes 1048608 | tf_op jit(solution)/shard_map/ppermute | solution.py:54
  189.8 3.3 multiply_reduce_fusion.2
  195.4 23.1 %collective-permute-done.22.refs_1_ = bf16[256,2048]{1,0:T(8,128)(2,1)S(1)} collective-permute-done((bf16[256,2048]{1,0:T(8,128)(2,1)S(1)}, bf16[256,2048]{1,0:T(8,128)(2,1)S(1)}, u32[]{:S(2)}, u32[]{:S(2)}) %collective-permute-start.22) | collective-permute-done | bytes 1048608 | tf_op jit(solution)/shard_map/ppermute | solution.py:54
  220.8 12.7 %collective-permute-done.24.refs_3_ = bf16[256,2048]{1,0:T(8,128)(2,1)S(1)} collective-permute-done((bf16[256,2048]{1,0:T(8,128)(2,1)S(1)}, bf16[256,2048]{1,0:T(8,128)(2,1)S(1)}, u32[]{:S(2)}, u32[]{:S(2)}) %collective-permute-start.24) | collective-permute-done | bytes 1048608 | tf_op jit(solution)/shard_map/ppermute | solution.py:58
  237.3 21.8 %ffn.2.refs_16_.refs_17_.refs_0_ = bf16[2048,1536]{1,0:T(8,128)(2,1)} custom-call(bf16[256,2048]{1,0:T(8,128)(2,1)} %copy-done.6, bf16[256,2048]{1,0:T(8,128)(2,1)} %copy-done.22, bf16[256,2048]{1,0:T(8,128)(2,1)} %copy-done.23, bf16[256,2048]{1,0:T(8,128)(2,1)} %copy-done.26, bf16[256,2048]{1,0:T(8,128)(2,1)} %copy-done.24, bf16[256,2048]{1,0:T(8,128)(2,1)} %copy-done.27, ...), custom_call_target="tpu_custom_call" | custom-call | flops 1 | bytes 1 | tf_op jit(solution)/shard_map/ffn/pallas_call | solution.py:204
  259.1 19.3 %weight_grads.3 = bf16[2048,1536]{1,0:T(8,128)(2,1)} custom-call(bf16[256,2048]{1,0:T(8,128)(2,1)} %copy-done.6, bf16[256,2048]{1,0:T(8,128)(2,1)} %copy-done.22, bf16[256,2048]{1,0:T(8,128)(2,1)} %copy-done.23, bf16[256,2048]{1,0:T(8,128)(2,1)} %copy-done.26, bf16[256,2048]{1,0:T(8,128)(2,1)} %copy-done.24, bf16[256,2048]{1,0:T(8,128)(2,1)} %copy-done.27, ...), custom_call_target="tpu_custom_call" | custom-call | flops 20000000000 | bytes 1 | tf_op jit(solution)/shard_map/weight_grads/pallas_call | solution.py:240
  278.8 13.4 %back.15.refs_2_ = bf16[2048,2048]{1,0:T(8,128)(2,1)} custom-call(bf16[2048,1536]{1,0:T(8,128)(2,1)} %ffn.2.refs_16_.refs_17_.refs_0_, bf16[2048,1536]{1,0:T(8,128)(2,1)} %all-gather.3.cloned.1.call-done.refs_16_.refs_1_.refs_2_), custom_call_target="tpu_custom_call" | custom-call | flops 1 | bytes 1 | tf_op jit(solution)/shard_map/back/pallas_call | solution.py:275
  292.2 4.3 all-gather.5.cloned.1.call-done.refs_16_.refs_1_.refs_3_
  296.5 21.7 %ffn.3.refs_0_.refs_16_.refs_17_.refs_1_ = bf16[2048,1536]{1,0:T(8,128)(2,1)} custom-call(bf16[256,2048]{1,0:T(8,128)(2,1)} %copy-done.6, bf16[256,2048]{1,0:T(8,128)(2,1)} %copy-done.22, bf16[256,2048]{1,0:T(8,128)(2,1)} %copy-done.23, bf16[256,2048]{1,0:T(8,128)(2,1)} %copy-done.26, bf16[256,2048]{1,0:T(8,128)(2,1)} %copy-done.24, ...), custom_call_target="tpu_custom_call" | custom-call | flops 1 | bytes 1 | tf_op jit(solution)/shard_map/ffn/pallas_call | solution.py:204
  318.2 9.3 %back.17 = bf16[1024,2048]{1,0:T(8,128)(2,1)} custom-call(bf16[2048,1536]{1,0:T(8,128)(2,1)} %ffn.3.refs_0_.refs_16_.refs_17_.refs_1_, bf16[2048,1536]{1,0:T(8,128)(2,1)} %all-gather.5.cloned.1.call-done.refs_16_.refs_1_.refs_3_, bf16[2048,2048]{1,0:T(8,128)(2,1)} %back.15.refs_2_), custom_call_target="tpu_custom_call" | custom-call | flops 1 | bytes 1 | tf_op jit(solution)/shard_map/back/pallas_call | solution.py:275
  327.6 9.6 %back.16 = bf16[1024,2048]{1,0:T(8,128)(2,1)} custom-call(bf16[2048,1536]{1,0:T(8,128)(2,1)} %ffn.3.refs_0_.refs_16_.refs_17_.refs_1_, bf16[2048,1536]{1,0:T(8,128)(2,1)} %all-gather.5.cloned.1.call-done.refs_16_.refs_1_.refs_3_, bf16[2048,2048]{1,0:T(8,128)(2,1)} %back.15.refs_2_), custom_call_target="tpu_custom_call" | custom-call | flops 1 | bytes 1 | tf_op jit(solution)/shard_map/back/pallas_call | solution.py:275
  337.2 3.3 slice_add_fusion
  342.1 19.3 %weight_grads.4 = bf16[2048,1536]{1,0:T(8,128)(2,1)} custom-call(bf16[256,2048]{1,0:T(8,128)(2,1)} %copy-done.6, bf16[256,2048]{1,0:T(8,128)(2,1)} %copy-done.22, bf16[256,2048]{1,0:T(8,128)(2,1)} %copy-done.23, bf16[256,2048]{1,0:T(8,128)(2,1)} %copy-done.26, bf16[256,2048]{1,0:T(8,128)(2,1)} %copy-done.24, bf16[256,2048]{1,0:T(8,128)(2,1)} %copy-done.27, ...), custom_call_target="tpu_custom_call" | custom-call | flops 20000000000 | bytes 1 | tf_op jit(solution)/shard_map/weight_grads/pallas_call | solution.py:240
  361.5 5.2 collective-permute-done.30
  366.7 3.2 fusion.2.refs_0_
  371.6 6.2 back.18
  377.9 7.0 %collective-permute-done.31.refs_1_ = bf16[256,2048]{1,0:T(8,128)(2,1)S(1)} collective-permute-done((bf16[256,2048]{1,0:T(8,128)(2,1)S(1)}, bf16[256,2048]{1,0:T(8,128)(2,1)S(1)}, u32[]{:S(2)}, u32[]{:S(2)}) %collective-permute-start.31) | collective-permute-done | bytes 1048608 | tf_op jit(solution)/shard_map/ppermute | solution.py:54
  385.8 4.9 norm_back.2.refs_0_.refs_5_
  393.8 6.3 back.20
  400.1 8.7 %back.19 = bf16[1024,2048]{1,0:T(8,128)(2,1)} custom-call(bf16[2048,1536]{1,0:T(8,128)(2,1)} %ffn.2.refs_16_.refs_17_.refs_0_, bf16[2048,1536]{1,0:T(8,128)(2,1)} %ffn.3.refs_0_.refs_16_.refs_17_.refs_1_, bf16[2048,1536]{1,0:T(8,128)(2,1)} %all-gather.3.cloned.1.call-done.refs_16_.refs_1_.refs_2_, ...), custom_call_target="tpu_custom_call" | custom-call | flops 7000000000 | bytes 1 | tf_op jit(solution)/shard_map/back/pallas_call | solution.py:275
  408.8 7.3 %collective-permute-done.32.refs_1_ = bf16[256,2048]{1,0:T(8,128)(2,1)S(1)} collective-permute-done((bf16[256,2048]{1,0:T(8,128)(2,1)}, bf16[256,2048]{1,0:T(8,128)(2,1)S(1)}, u32[]{:S(2)}, u32[]{:S(2)}) %collective-permute-start.32) | collective-permute-done | bytes 1048608 | tf_op jit(solution)/shard_map/ppermute | solution.py:54
  418.0 4.8 collective-permute-done.34
  422.8 5.1 broadcast_select_fusion
  427.9 3.7 collective-permute-done.38.refs_3_
  437.0 9.6 %front.1.d_ref = bf16[2048,256]{1,0:T(8,128)(2,1)} custom-call(bf16[256,2048]{1,0:T(8,128)(2,1)} %norm_back.2.refs_0_.refs_5_, bf16[256,2048]{1,0:T(8,128)(2,1)} %copy-done.20, bf16[256,2048]{1,0:T(8,128)(2,1)} %copy-done.21, bf16[256,2048]{1,0:T(8,128)(2,1)} %collective-permute-done.38.refs_3_, bf16[256,2048]{1,0:T(8,128)(2,1)} %collective-permute-done.39.refs_4_, ...), custom_call_target="tpu_custom_call" | custom-call | flops 1 | bytes 1 | tf_op jit(solution)/shard_map/front/pallas_call | solution.py:301
  446.6 35.2 %attend_back.1.refs_0_.refs_1_.refs_10_ = bf16[2048,384]{1,0:T(8,128)(2,1)} custom-call(s32[8]{0:T(128)} %select_reduce_fusion.2.place, s32[8]{0:T(128)} %and_select_fusion.2.first, bf16[2048,2432]{1,0:T(8,128)(2,1)} %qkv.1.q_ref.kv_ref.refs_8_, bf16[2048,256]{1,0:T(8,128)(2,1)} %front.1.d_ref, f32[2048,384]{1,0:T(8,128)} %attend.1.refs_0_.h_ref.refs_9_, ...), custom_call_target="tpu_custom_call" | custom-call | flops 1 | bytes 1 | tf_op jit(solution)/shard_map/attend_back/pallas_call | solution.py:479
  485.0 4.1 back.23
  489.2 4.1 back.22
  494.3 5.6 back.21
  503.5 12.7 %weight_grads.5 = bf16[2048,640]{1,0:T(8,128)(2,1)} custom-call(bf16[256,2048]{1,0:T(8,128)(2,1)} %norm_back.2.refs_0_.refs_5_, bf16[256,2048]{1,0:T(8,128)(2,1)} %copy-done.20, bf16[256,2048]{1,0:T(8,128)(2,1)} %copy-done.21, bf16[256,2048]{1,0:T(8,128)(2,1)} %collective-permute-done.38.refs_3_, bf16[256,2048]{1,0:T(8,128)(2,1)} %collective-permute-done.39.refs_4_, ...), custom_call_target="tpu_custom_call" | custom-call | flops 1 | bytes 1 | tf_op jit(solution)/shard_map/weight_grads/pallas_call | solution.py:240
  516.2 3.9 collective-permute-done.47
  523.9 4.1 fusion.4
  531.6 17.6 %collective-permute-done.50 = bf16[256,2048]{1,0:T(8,128)(2,1)} collective-permute-done((bf16[256,2048]{1,0:T(8,128)(2,1)}, bf16[256,2048]{1,0:T(8,128)(2,1)}, u32[]{:S(2)}, u32[]{:S(2)}) %collective-permute-start.50) | collective-permute-done | bytes 1048608 | tf_op jit(solution)/shard_map/ppermute | solution.py:46
  551.4 9.6 %collective-permute-done.53 = bf16[512,1536]{1,0:T(8,128)(2,1)S(1)} collective-permute-done((bf16[512,1536]{1,0:T(8,128)(2,1)}, bf16[512,1536]{1,0:T(8,128)(2,1)S(1)}, u32[]{:S(2)}, u32[]{:S(2)}) %collective-permute-start.53) | collective-permute-done | bytes 1572896 | tf_op jit(solution)/shard_map/ppermute | solution.py:50
  576.2 7.2 %collective-permute-done.49.refs_2_ = bf16[256,2048]{1,0:T(8,128)(2,1)S(1)} collective-permute-done((bf16[256,2048]{1,0:T(8,128)(2,1)S(1)}, bf16[256,2048]{1,0:T(8,128)(2,1)S(1)}, u32[]{:S(2)}, u32[]{:S(2)}) %collective-permute-start.49) | collective-permute-done | bytes 1048608 | tf_op jit(solution)/shard_map/ppermute | solution.py:54
  585.4 5.2 norm_back.3
  597.9 18.2 %collective-permute-done.56 = f32[2,512]{1,0:T(2,128)S(1)} collective-permute-done((f32[2,512]{1,0:T(2,128)S(1)}, f32[2,512]{1,0:T(2,128)S(1)}, u32[]{:S(2)}, u32[]{:S(2)}) %collective-permute-start.56) | collective-permute-done | bytes 4128 | tf_op jit(solution)/shard_map/ppermute | solution.py:46
  (321 shorter events, 134.1 us)
Async XLA Ops:
  7.2 182.7 %all-gather.3.cloned.1.call-start = ((), (), s32[]{:S(2)}) async-start(), calls=%async_computation.3 | async-start | bytes 7864320 | tf_op jit(solution)/shard_map/all_gather | solution.py:703
  11.7 20.3 %collective-permute-start = (bf16[528,640]{1,0:T(8,128)(2,1)S(1)}, bf16[528,640]{1,0:T(8,128)(2,1)}, u32[]{:S(2)}, u32[]{:S(2)}) collective-permute-start(bf16[528,640]{1,0:T(8,128)(2,1)S(1)} %fusion.6), channel_id=1, source_target_pairs={{0,8},{8,16},{16,24},{24,0},{1,9},{9,17},{17,25},{25,1},{2,10},{10... | collective-permute-start | bytes 2027528 | tf_op jit(solution)/shard_map/ppermute | solution.py:558
  16.0 16.0 %collective-permute-start.1 = (bf16[256,2048]{1,0:T(8,128)(2,1)S(1)}, bf16[256,2048]{1,0:T(8,128)(2,1)}, u32[]{:S(2)}, u32[]{:S(2)}) collective-permute-start(bf16[256,2048]{1,0:T(8,128)(2,1)S(1)} %constant_dynamic-slice_fusion.11.refs_0_.refs_3_), channel_id=1, source_target_pairs={{0,4},{1,3},{2,6},{3,1},{4,0},{5,7},{6,2},{7,5},{8,12},{9,11},{10,... | collective-permute-start | bytes 3145736 | tf_op jit(solution)/shard_map/ppermute | solution.py:54
  32.0 18.5 %collective-permute-start.2 = (bf16[528,640]{1,0:T(8,128)(2,1)}, bf16[528,640]{1,0:T(8,128)(2,1)}, u32[]{:S(2)}, u32[]{:S(2)}) collective-permute-start(bf16[528,640]{1,0:T(8,128)(2,1)} %collective-permute-done), channel_id=1, source_target_pairs={{0,8},{8,16},{16,24},{24,0},{1,9},{9,17},{17,25},{25,1},{2,10},{10... | collective-permute-start | bytes 2027528 | tf_op jit(solution)/shard_map/ppermute | solution.py:558
  32.5 23.8 %collective-permute-start.4 = (bf16[256,2048]{1,0:T(8,128)(2,1)S(1)}, bf16[256,2048]{1,0:T(8,128)(2,1)}, u32[]{:S(2)}, u32[]{:S(2)}) collective-permute-start(bf16[256,2048]{1,0:T(8,128)(2,1)S(1)} %constant_dynamic-slice_fusion.11.refs_0_.refs_3_), channel_id=1, source_target_pairs={{0,2},{1,5},{2,0},{3,7},{4,6},{5,1},{6,4},{7,3},{8,10},{9,13},{10,... | collective-permute-start | bytes 3145736 | tf_op jit(solution)/shard_map/ppermute | solution.py:58
  34.1 24.6 %collective-permute-start.5 = (bf16[256,2048]{1,0:T(8,128)(2,1)}, bf16[256,2048]{1,0:T(8,128)(2,1)}, u32[]{:S(2)}, u32[]{:S(2)}) collective-permute-start(bf16[256,2048]{1,0:T(8,128)(2,1)} %collective-permute-done.1.refs_1_), channel_id=1, source_target_pairs={{0,2},{1,5},{2,0},{3,7},{4,6},{5,1},{6,4},{7,3},{8,10},{9,13},{10,... | collective-permute-start | bytes 3145736 | tf_op jit(solution)/shard_map/ppermute | solution.py:58
  50.5 17.6 %collective-permute-start.3 = (bf16[528,640]{1,0:T(8,128)(2,1)}, bf16[528,640]{1,0:T(8,128)(2,1)}, u32[]{:S(2)}, u32[]{:S(2)}) collective-permute-start(bf16[528,640]{1,0:T(8,128)(2,1)} %collective-permute-done.2), channel_id=1, source_target_pairs={{0,8},{8,16},{16,24},{24,0},{1,9},{9,17},{17,25},{25,1},{2,10},{10... | collective-permute-start | bytes 2027528 | tf_op jit(solution)/shard_map/ppermute | solution.py:558
  68.0 228.4 %all-gather.5.cloned.1.call-start = ((), (), s32[]{:S(2)}) async-start(), calls=%async_computation.4 | async-start | bytes 7864320 | tf_op jit(solution)/shard_map/all_gather | solution.py:703
  77.3 25.4 %collective-permute-start.10 = (bf16[256,2048]{1,0:T(8,128)(2,1)S(1)}, bf16[256,2048]{1,0:T(8,128)(2,1)S(1)}, u32[]{:S(2)}, u32[]{:S(2)}) collective-permute-start(bf16[256,2048]{1,0:T(8,128)(2,1)S(1)} %constant_dynamic-slice_fusion.6.refs_8_.refs_4_), channel_id=1, source_target_pairs={{0,4},{1,3},{2,6},{3,1},{4,0},{5,7},{6,2},{7,5},{8,12},{9,11},{10,... | collective-permute-start | bytes 3145736 | tf_op jit(solution)/shard_map/ppermute | solution.py:54
  78.6 24.2 %collective-permute-start.11 = (bf16[256,2048]{1,0:T(8,128)(2,1)S(1)}, bf16[256,2048]{1,0:T(8,128)(2,1)}, u32[]{:S(2)}, u32[]{:S(2)}) collective-permute-start(bf16[256,2048]{1,0:T(8,128)(2,1)S(1)} %constant_dynamic-slice_fusion.6.refs_8_.refs_4_), channel_id=1, source_target_pairs={{0,2},{1,5},{2,0},{3,7},{4,6},{5,1},{6,4},{7,3},{8,10},{9,13},{10,... | collective-permute-start | bytes 3145736 | tf_op jit(solution)/shard_map/ppermute | solution.py:58
  79.8 48.6 %collective-permute-start.13 = (bf16[256,2048]{1,0:T(8,128)(2,1)S(1)}, bf16[256,2048]{1,0:T(8,128)(2,1)}, u32[]{:S(2)}, u32[]{:S(2)}) collective-permute-start(bf16[256,2048]{1,0:T(8,128)(2,1)S(1)} %constant_dynamic-slice_fusion.6.refs_8_.refs_4_), channel_id=1, source_target_pairs={{0,1},{1,0},{2,3},{3,2},{4,5},{5,4},{6,7},{7,6},{8,9},{9,8},{10,11... | collective-permute-start | bytes 3145736 | tf_op jit(solution)/shard_map/ppermute | solution.py:42
  102.8 25.6 %collective-permute-start.12 = (bf16[256,2048]{1,0:T(8,128)(2,1)S(1)}, bf16[256,2048]{1,0:T(8,128)(2,1)}, u32[]{:S(2)}, u32[]{:S(2)}) collective-permute-start(bf16[256,2048]{1,0:T(8,128)(2,1)S(1)} %collective-permute-done.10.refs_9_), channel_id=1, source_target_pairs={{0,2},{1,5},{2,0},{3,7},{4,6},{5,1},{6,4},{7,3},{8,10},{9,13},{10,... | collective-permute-start | bytes 3145736 | tf_op jit(solution)/shard_map/ppermute | solution.py:58
  103.8 24.6 %collective-permute-start.14 = (bf16[256,2048]{1,0:T(8,128)(2,1)S(1)}, bf16[256,2048]{1,0:T(8,128)(2,1)}, u32[]{:S(2)}, u32[]{:S(2)}) collective-permute-start(bf16[256,2048]{1,0:T(8,128)(2,1)S(1)} %collective-permute-done.10.refs_9_), channel_id=1, source_target_pairs={{0,1},{1,0},{2,3},{3,2},{4,5},{5,4},{6,7},{7,6},{8,9},{9,8},{10,11... | collective-permute-start | bytes 3145736 | tf_op jit(solution)/shard_map/ppermute | solution.py:42
  104.2 24.2 %collective-permute-start.15 = (bf16[256,2048]{1,0:T(8,128)(2,1)}, bf16[256,2048]{1,0:T(8,128)(2,1)}, u32[]{:S(2)}, u32[]{:S(2)}) collective-permute-start(bf16[256,2048]{1,0:T(8,128)(2,1)} %collective-permute-done.11.refs_10_), channel_id=1, source_target_pairs={{0,1},{1,0},{2,3},{3,2},{4,5},{5,4},{6,7},{7,6},{8,9},{9,8},{10,11... | collective-permute-start | bytes 3145736 | tf_op jit(solution)/shard_map/ppermute | solution.py:42
  139.1 23.2 %collective-permute-start.17 = (bf16[512,2048]{1,0:T(8,128)(2,1)}, bf16[512,2048]{1,0:T(8,128)(2,1)S(1)}, u32[]{:S(2)}, u32[]{:S(2)}) collective-permute-start(bf16[512,2048]{1,0:T(8,128)(2,1)} %back.13), channel_id=1, source_target_pairs={{0,1},{1,0},{2,3},{3,2},{4,5},{5,4},{6,7},{7,6},{8,9},{9,8},{10,11... | collective-permute-start | bytes 6291464 | tf_op jit(solution)/shard_map/ppermute | solution.py:42
  140.6 291.1 %reduce-scatter.4.cloned.1.call-start = ((), (), s32[]{:S(2)}) async-start(), calls=%async_computation.5 | async-start | bytes 7864320 | tf_op jit(solution)/shard_map/reduce_scatter | solution.py:734
  147.5 14.9 %collective-permute-start.19 = (bf16[256,2048]{1,0:T(8,128)(2,1)S(1)}, bf16[256,2048]{1,0:T(8,128)(2,1)S(1)}, u32[]{:S(2)}, u32[]{:S(2)}) collective-permute-start(bf16[256,2048]{1,0:T(8,128)(2,1)S(1)} %get-tuple-element.152), channel_id=1, source_target_pairs={{0,2},{1,5},{2,0},{3,7},{4,6},{5,1},{6,4},{7,3},{8,10},{9,13},{10,... | collective-permute-start | bytes 3145736 | tf_op jit(solution)/shard_map/ppermute | solution.py:58
  163.7 26.1 %collective-permute-start.21 = (bf16[256,2048]{1,0:T(8,128)(2,1)S(1)}, bf16[256,2048]{1,0:T(8,128)(2,1)}, u32[]{:S(2)}, u32[]{:S(2)}) collective-permute-start(bf16[256,2048]{1,0:T(8,128)(2,1)S(1)} %fusion.5), channel_id=1, source_target_pairs={{0,4},{1,3},{2,6},{3,1},{4,0},{5,7},{6,2},{7,5},{8,12},{9,11},{10,... | collective-permute-start | bytes 3145736 | tf_op jit(solution)/shard_map/ppermute | solution.py:54
  165.2 24.6 %collective-permute-start.20 = (bf16[256,2048]{1,0:T(8,128)(2,1)S(1)}, bf16[256,2048]{1,0:T(8,128)(2,1)}, u32[]{:S(2)}, u32[]{:S(2)}) collective-permute-start(bf16[256,2048]{1,0:T(8,128)(2,1)S(1)} %get-tuple-element.91), channel_id=1, source_target_pairs={{0,2},{1,5},{2,0},{3,7},{4,6},{5,1},{6,4},{7,3},{8,10},{9,13},{10,... | collective-permute-start | bytes 3145736 | tf_op jit(solution)/shard_map/ppermute | solution.py:58
  193.4 25.2 %collective-permute-start.22 = (bf16[256,2048]{1,0:T(8,128)(2,1)S(1)}, bf16[256,2048]{1,0:T(8,128)(2,1)S(1)}, u32[]{:S(2)}, u32[]{:S(2)}) collective-permute-start(bf16[256,2048]{1,0:T(8,128)(2,1)S(1)} %multiply_convert_fusion.refs_0_), channel_id=1, source_target_pairs={{0,4},{1,3},{2,6},{3,1},{4,0},{5,7},{6,2},{7,5},{8,12},{9,11},{10,... | collective-permute-start | bytes 3145736 | tf_op jit(solution)/shard_map/ppermute | solution.py:54
  194.2 24.4 %collective-permute-start.23 = (bf16[256,2048]{1,0:T(8,128)(2,1)S(1)}, bf16[256,2048]{1,0:T(8,128)(2,1)S(1)}, u32[]{:S(2)}, u32[]{:S(2)}) collective-permute-start(bf16[256,2048]{1,0:T(8,128)(2,1)S(1)} %multiply_convert_fusion.refs_0_), channel_id=1, source_target_pairs={{0,2},{1,5},{2,0},{3,7},{4,6},{5,1},{6,4},{7,3},{8,10},{9,13},{10,... | collective-permute-start | bytes 3145736 | tf_op jit(solution)/shard_map/ppermute | solution.py:58
  195.4 25.3 %collective-permute-start.25 = (bf16[256,2048]{1,0:T(8,128)(2,1)S(1)}, bf16[256,2048]{1,0:T(8,128)(2,1)S(1)}, u32[]{:S(2)}, u32[]{:S(2)}) collective-permute-start(bf16[256,2048]{1,0:T(8,128)(2,1)S(1)} %multiply_convert_fusion.refs_0_), channel_id=1, source_target_pairs={{0,1},{1,0},{2,3},{3,2},{4,5},{5,4},{6,7},{7,6},{8,9},{9,8},{10,11... | collective-permute-start | bytes 3145736 | tf_op jit(solution)/shard_map/ppermute | solution.py:42
  218.6 14.9 %collective-permute-start.24 = (bf16[256,2048]{1,0:T(8,128)(2,1)S(1)}, bf16[256,2048]{1,0:T(8,128)(2,1)S(1)}, u32[]{:S(2)}, u32[]{:S(2)}) collective-permute-start(bf16[256,2048]{1,0:T(8,128)(2,1)S(1)} %collective-permute-done.22.refs_1_), channel_id=1, source_target_pairs={{0,2},{1,5},{2,0},{3,7},{4,6},{5,1},{6,4},{7,3},{8,10},{9,13},{10,... | collective-permute-start | bytes 3145736 | tf_op jit(solution)/shard_map/ppermute | solution.py:58
  278.4 245.0 %reduce-scatter.6.cloned.1.call-start = ((), (), s32[]{:S(2)}) async-start(), calls=%async_computation.6 | async-start | bytes 7864320 | tf_op jit(solution)/shard_map/reduce_scatter | solution.py:734
  340.5 26.2 %collective-permute-start.30 = (bf16[512,2048]{1,0:T(8,128)(2,1)S(1)}, bf16[512,2048]{1,0:T(8,128)(2,1)}, u32[]{:S(2)}, u32[]{:S(2)}) collective-permute-start(bf16[512,2048]{1,0:T(8,128)(2,1)S(1)} %slice_add_fusion), channel_id=1, source_target_pairs={{0,2},{1,5},{2,0},{3,7},{4,6},{5,1},{6,4},{7,3},{8,10},{9,13},{10,... | collective-permute-start | bytes 6291464 | tf_op jit(solution)/shard_map/ppermute | solution.py:58
  361.4 231.6 %reduce-scatter.8.cloned.1.call-start = ((), (), s32[]{:S(2)}) async-start(), calls=%async_computation.7 | async-start | bytes 3276800 | tf_op jit(solution)/shard_map/reduce_scatter | solution.py:796
  370.0 14.9 %collective-permute-start.31 = (bf16[256,2048]{1,0:T(8,128)(2,1)S(1)}, bf16[256,2048]{1,0:T(8,128)(2,1)S(1)}, u32[]{:S(2)}, u32[]{:S(2)}) collective-permute-start(bf16[256,2048]{1,0:T(8,128)(2,1)S(1)} %slice.217), channel_id=1, source_target_pairs={{0,4},{1,3},{2,6},{3,1},{4,0},{5,7},{6,2},{7,5},{8,12},{9,11},{10,... | collective-permute-start | bytes 3145736 | tf_op jit(solution)/shard_map/ppermute | solution.py:54
  377.9 40.1 %collective-permute-start.35 = (bf16[512,2048]{1,0:T(8,128)(2,1)}, bf16[512,2048]{1,0:T(8,128)(2,1)}, u32[]{:S(2)}, u32[]{:S(2)}) collective-permute-start(bf16[512,2048]{1,0:T(8,128)(2,1)} %back.18), channel_id=1, source_target_pairs={{0,1},{1,0},{2,3},{3,2},{4,5},{5,4},{6,7},{7,6},{8,9},{9,8},{10,11... | collective-permute-start | bytes 6291464 | tf_op jit(solution)/shard_map/ppermute | solution.py:42
  390.8 25.4 %collective-permute-start.32 = (bf16[256,2048]{1,0:T(8,128)(2,1)}, bf16[256,2048]{1,0:T(8,128)(2,1)S(1)}, u32[]{:S(2)}, u32[]{:S(2)}) collective-permute-start(bf16[256,2048]{1,0:T(8,128)(2,1)} %norm_back.2.refs_0_.refs_5_), channel_id=1, source_target_pairs={{0,4},{1,3},{2,6},{3,1},{4,0},{5,7},{6,2},{7,5},{8,12},{9,11},{10,... | collective-permute-start | bytes 3145736 | tf_op jit(solution)/shard_map/ppermute | solution.py:54
  392.3 23.8 %collective-permute-start.33 = (bf16[256,2048]{1,0:T(8,128)(2,1)}, bf16[256,2048]{1,0:T(8,128)(2,1)S(1)}, u32[]{:S(2)}, u32[]{:S(2)}) collective-permute-start(bf16[256,2048]{1,0:T(8,128)(2,1)} %norm_back.2.refs_0_.refs_5_), channel_id=1, source_target_pairs={{0,2},{1,5},{2,0},{3,7},{4,6},{5,1},{6,4},{7,3},{8,10},{9,13},{10,... | collective-permute-start | bytes 3145736 | tf_op jit(solution)/shard_map/ppermute | solution.py:58
  416.7 14.9 %collective-permute-start.38 = (bf16[256,2048]{1,0:T(8,128)(2,1)S(1)}, bf16[256,2048]{1,0:T(8,128)(2,1)}, u32[]{:S(2)}, u32[]{:S(2)}) collective-permute-start(bf16[256,2048]{1,0:T(8,128)(2,1)S(1)} %collective-permute-done.32.refs_1_), channel_id=1, source_target_pairs={{0,2},{1,5},{2,0},{3,7},{4,6},{5,1},{6,4},{7,3},{8,10},{9,13},{10,... | collective-permute-start | bytes 3145736 | tf_op jit(solution)/shard_map/ppermute | solution.py:58
  417.2 14.4 %collective-permute-start.40 = (bf16[256,2048]{1,0:T(8,128)(2,1)S(1)}, bf16[256,2048]{1,0:T(8,128)(2,1)}, u32[]{:S(2)}, u32[]{:S(2)}) collective-permute-start(bf16[256,2048]{1,0:T(8,128)(2,1)S(1)} %collective-permute-done.32.refs_1_), channel_id=1, source_target_pairs={{0,1},{1,0},{2,3},{3,2},{4,5},{5,4},{6,7},{7,6},{8,9},{9,8},{10,11... | collective-permute-start | bytes 3145736 | tf_op jit(solution)/shard_map/ppermute | solution.py:42
  418.0 13.6 %collective-permute-start.41 = (bf16[256,2048]{1,0:T(8,128)(2,1)S(1)}, bf16[256,2048]{1,0:T(8,128)(2,1)}, u32[]{:S(2)}, u32[]{:S(2)}) collective-permute-start(bf16[256,2048]{1,0:T(8,128)(2,1)S(1)} %collective-permute-done.33.refs_2_), channel_id=1, source_target_pairs={{0,1},{1,0},{2,3},{3,2},{4,5},{5,4},{6,7},{7,6},{8,9},{9,8},{10,11... | collective-permute-start | bytes 3145736 | tf_op jit(solution)/shard_map/ppermute | solution.py:42
  431.6 50.2 %collective-permute-start.43 = (bf16[512,1536]{1,0:T(8,128)(2,1)}, bf16[512,1536]{1,0:T(8,128)(2,1)S(1)}, u32[]{:S(2)}, u32[]{:S(2)}) collective-permute-start(bf16[512,1536]{1,0:T(8,128)(2,1)} %reduce-scatter.4.cloned.1.call-done), channel_id=1, source_target_pairs={{0,4},{4,0},{1,5},{5,1},{2,6},{6,2},{3,7},{7,3},{8,12},{12,8},{9,1... | collective-permute-start | bytes 4718600 | tf_op jit(solution)/shard_map/ppermute | solution.py:50
  433.2 48.6 %collective-permute-start.36 = (bf16[256,2048]{1,0:T(8,128)(2,1)}, bf16[256,2048]{1,0:T(8,128)(2,1)S(1)}, u32[]{:S(2)}, u32[]{:S(2)}) collective-permute-start(bf16[256,2048]{1,0:T(8,128)(2,1)} %get-tuple-element.150), channel_id=1, source_target_pairs={{0,2},{2,0},{1,3},{3,1},{4,6},{6,4},{5,7},{7,5},{8,10},{10,8},{9,1... | collective-permute-start | bytes 3145736 | tf_op jit(solution)/shard_map/ppermute | solution.py:46
  433.7 48.1 %collective-permute-start.37 = (bf16[256,2048]{1,0:T(8,128)(2,1)}, bf16[256,2048]{1,0:T(8,128)(2,1)S(1)}, u32[]{:S(2)}, u32[]{:S(2)}) collective-permute-start(bf16[256,2048]{1,0:T(8,128)(2,1)} %get-tuple-element.143), channel_id=1, source_target_pairs={{0,2},{2,0},{1,3},{3,1},{4,6},{6,4},{5,7},{7,5},{8,10},{10,8},{9,1... | collective-permute-start | bytes 3145736 | tf_op jit(solution)/shard_map/ppermute | solution.py:46
  493.4 30.6 %collective-permute-start.44 = (bf16[512,2048]{1,0:T(8,128)(2,1)}, bf16[512,2048]{1,0:T(8,128)(2,1)}, u32[]{:S(2)}, u32[]{:S(2)}) collective-permute-start(bf16[512,2048]{1,0:T(8,128)(2,1)} %back.22), channel_id=1, source_target_pairs={{0,1},{1,0},{2,3},{3,2},{4,5},{5,4},{6,7},{7,6},{8,9},{9,8},{10,11... | collective-permute-start | bytes 6291464 | tf_op jit(solution)/shard_map/ppermute | solution.py:42
  493.7 26.3 %collective-permute-start.47 = (bf16[256,2048]{1,0:T(8,128)(2,1)}, bf16[256,2048]{1,0:T(8,128)(2,1)}, u32[]{:S(2)}, u32[]{:S(2)}) collective-permute-start(bf16[256,2048]{1,0:T(8,128)(2,1)} %add.380), channel_id=1, source_target_pairs={{0,4},{4,0},{1,5},{5,1},{2,6},{6,2},{3,7},{7,3},{8,12},{12,8},{9,1... | collective-permute-start | bytes 3145736 | tf_op jit(solution)/shard_map/ppermute | solution.py:50
  503.1 20.8 %collective-permute-start.46 = (bf16[256,2048]{1,0:T(8,128)(2,1)}, bf16[256,2048]{1,0:T(8,128)(2,1)}, u32[]{:S(2)}, u32[]{:S(2)}) collective-permute-start(bf16[256,2048]{1,0:T(8,128)(2,1)} %get-tuple-element.146), channel_id=1, source_target_pairs={{0,2},{1,5},{2,0},{3,7},{4,6},{5,1},{6,4},{7,3},{8,10},{9,13},{10,... | collective-permute-start | bytes 3145736 | tf_op jit(solution)/shard_map/ppermute | solution.py:58
  522.8 26.4 %collective-permute-start.50 = (bf16[256,2048]{1,0:T(8,128)(2,1)}, bf16[256,2048]{1,0:T(8,128)(2,1)}, u32[]{:S(2)}, u32[]{:S(2)}) collective-permute-start(bf16[256,2048]{1,0:T(8,128)(2,1)} %add_convert_fusion), channel_id=1, source_target_pairs={{0,2},{2,0},{1,3},{3,1},{4,6},{6,4},{5,7},{7,5},{8,10},{10,8},{9,1... | collective-permute-start | bytes 3145736 | tf_op jit(solution)/shard_map/ppermute | solution.py:46
  523.3 46.1 %collective-permute-start.51 = (bf16[256,2048]{1,0:T(8,128)(2,1)}, bf16[256,2048]{1,0:T(8,128)(2,1)}, u32[]{:S(2)}, u32[]{:S(2)}) collective-permute-start(bf16[256,2048]{1,0:T(8,128)(2,1)} %add_convert_fusion), channel_id=1, source_target_pairs={{0,1},{1,0},{2,3},{3,2},{4,5},{5,4},{6,7},{7,6},{8,9},{9,8},{10,11... | collective-permute-start | bytes 3145736 | tf_op jit(solution)/shard_map/ppermute | solution.py:42
  523.4 37.6 %collective-permute-start.53 = (bf16[512,1536]{1,0:T(8,128)(2,1)}, bf16[512,1536]{1,0:T(8,128)(2,1)S(1)}, u32[]{:S(2)}, u32[]{:S(2)}) collective-permute-start(bf16[512,1536]{1,0:T(8,128)(2,1)} %reduce-scatter.6.cloned.1.call-done), channel_id=1, source_target_pairs={{0,4},{4,0},{1,5},{5,1},{2,6},{6,2},{3,7},{7,3},{8,12},{12,8},{9,1... | collective-permute-start | bytes 4718600 | tf_op jit(solution)/shard_map/ppermute | solution.py:50
  528.0 55.4 %collective-permute-start.49 = (bf16[256,2048]{1,0:T(8,128)(2,1)S(1)}, bf16[256,2048]{1,0:T(8,128)(2,1)S(1)}, u32[]{:S(2)}, u32[]{:S(2)}) collective-permute-start(bf16[256,2048]{1,0:T(8,128)(2,1)S(1)} %get-tuple-element.121), channel_id=1, source_target_pairs={{0,4},{1,3},{2,6},{3,1},{4,0},{5,7},{6,2},{7,5},{8,12},{9,11},{10,... | collective-permute-start | bytes 3145736 | tf_op jit(solution)/shard_map/ppermute | solution.py:54
  529.3 54.2 %collective-permute-start.48 = (bf16[256,2048]{1,0:T(8,128)(2,1)S(1)}, bf16[256,2048]{1,0:T(8,128)(2,1)S(1)}, u32[]{:S(2)}, u32[]{:S(2)}) collective-permute-start(bf16[256,2048]{1,0:T(8,128)(2,1)S(1)} %copy-done.48), channel_id=1, source_target_pairs={{0,2},{1,5},{2,0},{3,7},{4,6},{5,1},{6,4},{7,3},{8,10},{9,13},{10,... | collective-permute-start | bytes 3145736 | tf_op jit(solution)/shard_map/ppermute | solution.py:58
  550.9 18.5 %collective-permute-start.52 = (bf16[256,2048]{1,0:T(8,128)(2,1)}, bf16[256,2048]{1,0:T(8,128)(2,1)S(1)}, u32[]{:S(2)}, u32[]{:S(2)}) collective-permute-start(bf16[256,2048]{1,0:T(8,128)(2,1)} %collective-permute-done.50), channel_id=1, source_target_pairs={{0,1},{1,0},{2,3},{3,2},{4,5},{5,4},{6,7},{7,6},{8,9},{9,8},{10,11... | collective-permute-start | bytes 3145736 | tf_op jit(solution)/shard_map/ppermute | solution.py:42
  590.7 29.1 %collective-permute-start.54 = (bf16[256,2048]{1,0:T(8,128)(2,1)}, bf16[256,2048]{1,0:T(8,128)(2,1)}, u32[]{:S(2)}, u32[]{:S(2)}) collective-permute-start(bf16[256,2048]{1,0:T(8,128)(2,1)} %norm_back.3), channel_id=1, source_target_pairs={{0,2},{2,0},{1,3},{3,1},{4,6},{6,4},{5,7},{7,5},{8,10},{10,8},{9,1... | collective-permute-start | bytes 3145736 | tf_op jit(solution)/shard_map/ppermute | solution.py:46
  593.0 26.8 %collective-permute-start.58 = (bf16[512,640]{1,0:T(8,128)(2,1)}, bf16[512,640]{1,0:T(8,128)(2,1)S(1)}, u32[]{:S(2)}, u32[]{:S(2)}) collective-permute-start(bf16[512,640]{1,0:T(8,128)(2,1)} %reduce-scatter.8.cloned.1.call-done), channel_id=1, source_target_pairs={{0,4},{4,0},{1,5},{5,1},{2,6},{6,2},{3,7},{7,3},{8,12},{12,8},{9,1... | collective-permute-start | bytes 1966088 | tf_op jit(solution)/shard_map/ppermute | solution.py:50
  596.8 19.3 %collective-permute-start.56 = (f32[2,512]{1,0:T(2,128)S(1)}, f32[2,512]{1,0:T(2,128)S(1)}, u32[]{:S(2)}, u32[]{:S(2)}) collective-permute-start(f32[2,512]{1,0:T(2,128)S(1)} %fusion.18), channel_id=1, source_target_pairs={{0,2},{2,0},{1,3},{3,1},{4,6},{6,4},{5,7},{7,5},{8,10},{10,8},{9,1... | collective-permute-start | bytes 12296 | tf_op jit(solution)/shard_map/ppermute | solution.py:46
  (76 other events, 1084.4 us)
Sparse Core Ops, SparseCore 0:
  68.2 113.0 all-gather.2
  182.8 113.5 all-gather.4
  298.8 108.9 reduce-scatter.3
  409.9 111.2 reduce-scatter.5
  524.0 52.6 reduce-scatter.7

commit v14 on v13

--- a/solution.py
+++ b/solution.py
@@ -812,12 +812,12 @@
     )
     gain_sums = gain_sums + swap_core(gain_sums)
     gain_sums = gain_sums + swap_y(gain_sums)
-    gain_sums = gain_sums + swap_x(gain_sums)
 
     tokens_grad_beside, gain_sums, other_attn, result, *ffn_grads = lax.optimization_barrier(
         (swap_y(tokens_grad_own), gain_sums, other_attn, result, *ffn_grads)
     )
     tokens_grad = share_in_ctx(tokens_grad_own, tokens_grad_beside, y, core)
+    gain_sums = gain_sums + swap_x(gain_sums)
     attn_gain_grad = gain_sums[0] / attn_gain.astype(F32)
     ffn_gain_grad = gain_sums[1] / ffn_gain.astype(F32)
     attn_low, attn_high = both_halves(attn_reduced, other_attn, ctx)

time: 651 us -> 647 us (level)
  transfers between devices with their start and end apart: 66 -> 66, of which waited for: 27 -> 26; matrix products, arithmetic and copies ran while one was open for 13% -> 13% of each run, Pallas kernels for 42% -> 42%
where the time goes in v14:
time: 647 us; the launch traced here: 638 us
  Pallas kernels  267 us (41%)
  waiting for transfers between devices  209 us (32%)
  other arithmetic  68.7 us (11%)
  starting transfers between devices  44.5 us (7%)
  local copies, waits for them, and re-layouts  34 us (5%)
  between operations  15.2 us (2%)
    pallas_call x12, Pallas kernels, back_product(): pl.pallas_call(functools.partial(back_kernel, len(terms)), out_shape=jax....  78.9 us
    ppermute x7, waiting for transfers between devices, swap_first(): return lax.ppermute(v, ('ctx', 'tp'), FIRST)  76.2 us
    pallas_call x3, Pallas kernels, weight_grads(): pl.pallas_call(functools.partial(grads_kernel, len(x), len(y)), out_shape...  51.2 us
    pallas_call x2, Pallas kernels, ffn_chunk(): pl.pallas_call(functools.partial(ffn_kernel, len(x)), out_shape=jax.Shape...  43.5 us
    ppermute x13, waiting for transfers between devices, swap_second(): return lax.ppermute(v, ('ctx', 'tp'), SECOND)  37.4 us
    ppermute x5, waiting for transfers between devices, swap_y(): return lax.ppermute(v, 'tp', ACROSS)  35.7 us
    pallas_call x1, Pallas kernels, attend_back(): pl.pallas_call(attend_back_kernel, out_shape=jax.ShapeDtypeStruct((rows,...  35.2 us
    ppermute x3, waiting for transfers between devices, ring_over(): pieces.append(lax.ppermute(sent, 'fsdp', cycle))  30.9 us
  transfers between devices with their start and end apart: 66, of which 26 were waited for; matrix products, arithmetic and copies ran while one was open for 13% of the time, Pallas kernels for 42%

profile of v14, /device:TPU:0, one launch (start us, length us, event | category | flops | bytes accessed | tf_op | source)
XLA Modules:
  0.0 638.2 jit_solution(3697192978842997574)
XLA Ops:
  20.7 5.6 negate_select_fusion
  26.3 5.7 collective-permute-done
  34.6 15.9 %collective-permute-done.2 = bf16[528,640]{1,0:T(8,128)(2,1)} collective-permute-done((bf16[528,640]{1,0:T(8,128)(2,1)}, bf16[528,640]{1,0:T(8,128)(2,1)}, u32[]{:S(2)}, u32[]{:S(2)}) %collective-permute-start.2) | collective-permute-done | bytes 675872 | tf_op jit(solution)/shard_map/ppermute | solution.py:558
  58.7 9.3 %collective-permute-done.3 = bf16[528,640]{1,0:T(8,128)(2,1)} collective-permute-done((bf16[528,640]{1,0:T(8,128)(2,1)}, bf16[528,640]{1,0:T(8,128)(2,1)}, u32[]{:S(2)}, u32[]{:S(2)}) %collective-permute-start.3) | collective-permute-done | bytes 675872 | tf_op jit(solution)/shard_map/ppermute | solution.py:558
  79.8 15.3 %qkv.1.q_ref.kv_ref.refs_8_ = bf16[2048,2432]{1,0:T(8,128)(2,1)} custom-call(bf16[256,2048]{1,0:T(8,128)(2,1)} %copy-done.7, bf16[256,2048]{1,0:T(8,128)(2,1)} %collective-permute-done.1.refs_1_, bf16[256,2048]{1,0:T(8,128)(2,1)} %collective-permute-done.4.refs_2_, bf16[256,2048]{1,0:T(8,128)(2,1)} %collective-permute-done.5.refs_3_, ...), custom_call_target="tpu_custom_call" | custom-call | flops 1 | bytes 1 | tf_op jit(solution)/shard_map/qkv/pallas_call | solution.py:165
  95.2 7.6 %collective-permute-done.10.refs_9_ = bf16[256,2048]{1,0:T(8,128)(2,1)S(1)} collective-permute-done((bf16[256,2048]{1,0:T(8,128)(2,1)S(1)}, bf16[256,2048]{1,0:T(8,128)(2,1)S(1)}, u32[]{:S(2)}, u32[]{:S(2)}) %collective-permute-start.10) | collective-permute-done | bytes 1048608 | tf_op jit(solution)/shard_map/ppermute | solution.py:54
  105.7 22.7 %attend.1.refs_0_.h_ref.refs_9_ = f32[2048,384]{1,0:T(8,128)} custom-call(s32[8]{0:T(128)} %select_reduce_fusion.2.place, s32[8]{0:T(128)} %and_select_fusion.2.first, bf16[2048,2432]{1,0:T(8,128)(2,1)} %qkv.1.q_ref.kv_ref.refs_8_, bf16[2048,2432]{1,0:T(8,128)(2,1)} %qkv.1.q_ref.kv_ref.refs_8_, s32[2048,1]{1,0:T(8,128)} %copy.28.start_ref), custom_call_target="tpu_custom_call" | custom-call | flops 1 | bytes 1 | tf_op jit(solution)/shard_map/attend/pallas_call | solution.py:382
  131.4 3.8 back.14
  135.6 3.5 back.13
  140.8 4.2 back.12
  149.0 13.3 %collective-permute-done.19 = bf16[256,2048]{1,0:T(8,128)(2,1)S(1)} collective-permute-done((bf16[256,2048]{1,0:T(8,128)(2,1)S(1)}, bf16[256,2048]{1,0:T(8,128)(2,1)S(1)}, u32[]{:S(2)}, u32[]{:S(2)}) %collective-permute-start.19) | collective-permute-done | bytes 1048608 | tf_op jit(solution)/shard_map/ppermute | solution.py:58
  165.9 24.0 %collective-permute-done.21 = bf16[256,2048]{1,0:T(8,128)(2,1)} collective-permute-done((bf16[256,2048]{1,0:T(8,128)(2,1)S(1)}, bf16[256,2048]{1,0:T(8,128)(2,1)}, u32[]{:S(2)}, u32[]{:S(2)}) %collective-permute-start.21) | collective-permute-done | bytes 1048608 | tf_op jit(solution)/shard_map/ppermute | solution.py:54
  189.8 3.3 multiply_reduce_fusion.2
  195.4 23.1 %collective-permute-done.22.refs_1_ = bf16[256,2048]{1,0:T(8,128)(2,1)S(1)} collective-permute-done((bf16[256,2048]{1,0:T(8,128)(2,1)S(1)}, bf16[256,2048]{1,0:T(8,128)(2,1)S(1)}, u32[]{:S(2)}, u32[]{:S(2)}) %collective-permute-start.22) | collective-permute-done | bytes 1048608 | tf_op jit(solution)/shard_map/ppermute | solution.py:54
  220.8 12.7 %collective-permute-done.24.refs_3_ = bf16[256,2048]{1,0:T(8,128)(2,1)S(1)} collective-permute-done((bf16[256,2048]{1,0:T(8,128)(2,1)S(1)}, bf16[256,2048]{1,0:T(8,128)(2,1)S(1)}, u32[]{:S(2)}, u32[]{:S(2)}) %collective-permute-start.24) | collective-permute-done | bytes 1048608 | tf_op jit(solution)/shard_map/ppermute | solution.py:58
  237.3 21.8 %ffn.2.refs_16_.refs_17_.refs_0_ = bf16[2048,1536]{1,0:T(8,128)(2,1)} custom-call(bf16[256,2048]{1,0:T(8,128)(2,1)} %copy-done.6, bf16[256,2048]{1,0:T(8,128)(2,1)} %copy-done.22, bf16[256,2048]{1,0:T(8,128)(2,1)} %copy-done.23, bf16[256,2048]{1,0:T(8,128)(2,1)} %copy-done.26, bf16[256,2048]{1,0:T(8,128)(2,1)} %copy-done.24, bf16[256,2048]{1,0:T(8,128)(2,1)} %copy-done.27, ...), custom_call_target="tpu_custom_call" | custom-call | flops 1 | bytes 1 | tf_op jit(solution)/shard_map/ffn/pallas_call | solution.py:204
  259.1 19.3 %weight_grads.3 = bf16[2048,1536]{1,0:T(8,128)(2,1)} custom-call(bf16[256,2048]{1,0:T(8,128)(2,1)} %copy-done.6, bf16[256,2048]{1,0:T(8,128)(2,1)} %copy-done.22, bf16[256,2048]{1,0:T(8,128)(2,1)} %copy-done.23, bf16[256,2048]{1,0:T(8,128)(2,1)} %copy-done.26, bf16[256,2048]{1,0:T(8,128)(2,1)} %copy-done.24, bf16[256,2048]{1,0:T(8,128)(2,1)} %copy-done.27, ...), custom_call_target="tpu_custom_call" | custom-call | flops 20000000000 | bytes 1 | tf_op jit(solution)/shard_map/weight_grads/pallas_call | solution.py:240
  278.8 13.4 %back.15.refs_2_ = bf16[2048,2048]{1,0:T(8,128)(2,1)} custom-call(bf16[2048,1536]{1,0:T(8,128)(2,1)} %ffn.2.refs_16_.refs_17_.refs_0_, bf16[2048,1536]{1,0:T(8,128)(2,1)} %all-gather.3.cloned.1.call-done.refs_16_.refs_1_.refs_2_), custom_call_target="tpu_custom_call" | custom-call | flops 1 | bytes 1 | tf_op jit(solution)/shard_map/back/pallas_call | solution.py:275
  292.2 4.3 all-gather.5.cloned.1.call-done.refs_16_.refs_1_.refs_3_
  296.5 21.7 %ffn.3.refs_0_.refs_16_.refs_17_.refs_1_ = bf16[2048,1536]{1,0:T(8,128)(2,1)} custom-call(bf16[256,2048]{1,0:T(8,128)(2,1)} %copy-done.6, bf16[256,2048]{1,0:T(8,128)(2,1)} %copy-done.22, bf16[256,2048]{1,0:T(8,128)(2,1)} %copy-done.23, bf16[256,2048]{1,0:T(8,128)(2,1)} %copy-done.26, bf16[256,2048]{1,0:T(8,128)(2,1)} %copy-done.24, ...), custom_call_target="tpu_custom_call" | custom-call | flops 1 | bytes 1 | tf_op jit(solution)/shard_map/ffn/pallas_call | solution.py:204
  318.2 9.3 %back.17 = bf16[1024,2048]{1,0:T(8,128)(2,1)} custom-call(bf16[2048,1536]{1,0:T(8,128)(2,1)} %ffn.3.refs_0_.refs_16_.refs_17_.refs_1_, bf16[2048,1536]{1,0:T(8,128)(2,1)} %all-gather.5.cloned.1.call-done.refs_16_.refs_1_.refs_3_, bf16[2048,2048]{1,0:T(8,128)(2,1)} %back.15.refs_2_), custom_call_target="tpu_custom_call" | custom-call | flops 1 | bytes 1 | tf_op jit(solution)/shard_map/back/pallas_call | solution.py:275
  327.6 9.6 %back.16 = bf16[1024,2048]{1,0:T(8,128)(2,1)} custom-call(bf16[2048,1536]{1,0:T(8,128)(2,1)} %ffn.3.refs_0_.refs_16_.refs_17_.refs_1_, bf16[2048,1536]{1,0:T(8,128)(2,1)} %all-gather.5.cloned.1.call-done.refs_16_.refs_1_.refs_3_, bf16[2048,2048]{1,0:T(8,128)(2,1)} %back.15.refs_2_), custom_call_target="tpu_custom_call" | custom-call | flops 1 | bytes 1 | tf_op jit(solution)/shard_map/back/pallas_call | solution.py:275
  337.2 3.3 slice_add_fusion
  342.1 19.3 %weight_grads.4 = bf16[2048,1536]{1,0:T(8,128)(2,1)} custom-call(bf16[256,2048]{1,0:T(8,128)(2,1)} %copy-done.6, bf16[256,2048]{1,0:T(8,128)(2,1)} %copy-done.22, bf16[256,2048]{1,0:T(8,128)(2,1)} %copy-done.23, bf16[256,2048]{1,0:T(8,128)(2,1)} %copy-done.26, bf16[256,2048]{1,0:T(8,128)(2,1)} %copy-done.24, bf16[256,2048]{1,0:T(8,128)(2,1)} %copy-done.27, ...), custom_call_target="tpu_custom_call" | custom-call | flops 20000000000 | bytes 1 | tf_op jit(solution)/shard_map/weight_grads/pallas_call | solution.py:240
  361.5 5.2 collective-permute-done.30
  366.7 3.2 fusion.2.refs_0_
  371.6 6.2 back.18
  377.9 7.0 %collective-permute-done.31.refs_1_ = bf16[256,2048]{1,0:T(8,128)(2,1)S(1)} collective-permute-done((bf16[256,2048]{1,0:T(8,128)(2,1)S(1)}, bf16[256,2048]{1,0:T(8,128)(2,1)S(1)}, u32[]{:S(2)}, u32[]{:S(2)}) %collective-permute-start.31) | collective-permute-done | bytes 1048608 | tf_op jit(solution)/shard_map/ppermute | solution.py:54
  385.8 4.9 norm_back.2.refs_0_.refs_5_
  393.8 6.3 back.20
  400.1 8.7 %back.19 = bf16[1024,2048]{1,0:T(8,128)(2,1)} custom-call(bf16[2048,1536]{1,0:T(8,128)(2,1)} %ffn.2.refs_16_.refs_17_.refs_0_, bf16[2048,1536]{1,0:T(8,128)(2,1)} %ffn.3.refs_0_.refs_16_.refs_17_.refs_1_, bf16[2048,1536]{1,0:T(8,128)(2,1)} %all-gather.3.cloned.1.call-done.refs_16_.refs_1_.refs_2_, ...), custom_call_target="tpu_custom_call" | custom-call | flops 7000000000 | bytes 1 | tf_op jit(solution)/shard_map/back/pallas_call | solution.py:275
  408.8 7.3 %collective-permute-done.32.refs_1_ = bf16[256,2048]{1,0:T(8,128)(2,1)S(1)} collective-permute-done((bf16[256,2048]{1,0:T(8,128)(2,1)}, bf16[256,2048]{1,0:T(8,128)(2,1)S(1)}, u32[]{:S(2)}, u32[]{:S(2)}) %collective-permute-start.32) | collective-permute-done | bytes 1048608 | tf_op jit(solution)/shard_map/ppermute | solution.py:54
  418.0 4.8 collective-permute-done.34
  422.8 5.1 broadcast_select_fusion
  427.9 3.7 collective-permute-done.38.refs_3_
  437.0 9.6 %front.1.d_ref = bf16[2048,256]{1,0:T(8,128)(2,1)} custom-call(bf16[256,2048]{1,0:T(8,128)(2,1)} %norm_back.2.refs_0_.refs_5_, bf16[256,2048]{1,0:T(8,128)(2,1)} %copy-done.20, bf16[256,2048]{1,0:T(8,128)(2,1)} %copy-done.21, bf16[256,2048]{1,0:T(8,128)(2,1)} %collective-permute-done.38.refs_3_, bf16[256,2048]{1,0:T(8,128)(2,1)} %collective-permute-done.39.refs_4_, ...), custom_call_target="tpu_custom_call" | custom-call | flops 1 | bytes 1 | tf_op jit(solution)/shard_map/front/pallas_call | solution.py:301
  446.6 35.2 %attend_back.1.refs_0_.refs_1_.refs_10_ = bf16[2048,384]{1,0:T(8,128)(2,1)} custom-call(s32[8]{0:T(128)} %select_reduce_fusion.2.place, s32[8]{0:T(128)} %and_select_fusion.2.first, bf16[2048,2432]{1,0:T(8,128)(2,1)} %qkv.1.q_ref.kv_ref.refs_8_, bf16[2048,256]{1,0:T(8,128)(2,1)} %front.1.d_ref, f32[2048,384]{1,0:T(8,128)} %attend.1.refs_0_.h_ref.refs_9_, ...), custom_call_target="tpu_custom_call" | custom-call | flops 1 | bytes 1 | tf_op jit(solution)/shard_map/attend_back/pallas_call | solution.py:479
  485.0 4.1 back.23
  489.2 4.1 back.22
  494.3 5.6 back.21
  503.5 12.7 %weight_grads.5 = bf16[2048,640]{1,0:T(8,128)(2,1)} custom-call(bf16[256,2048]{1,0:T(8,128)(2,1)} %norm_back.2.refs_0_.refs_5_, bf16[256,2048]{1,0:T(8,128)(2,1)} %copy-done.20, bf16[256,2048]{1,0:T(8,128)(2,1)} %copy-done.21, bf16[256,2048]{1,0:T(8,128)(2,1)} %collective-permute-done.38.refs_3_, bf16[256,2048]{1,0:T(8,128)(2,1)} %collective-permute-done.39.refs_4_, ...), custom_call_target="tpu_custom_call" | custom-call | flops 1 | bytes 1 | tf_op jit(solution)/shard_map/weight_grads/pallas_call | solution.py:240
  516.2 3.9 collective-permute-done.47
  523.9 4.1 fusion.4
  531.6 17.6 %collective-permute-done.50 = bf16[256,2048]{1,0:T(8,128)(2,1)} collective-permute-done((bf16[256,2048]{1,0:T(8,128)(2,1)}, bf16[256,2048]{1,0:T(8,128)(2,1)}, u32[]{:S(2)}, u32[]{:S(2)}) %collective-permute-start.50) | collective-permute-done | bytes 1048608 | tf_op jit(solution)/shard_map/ppermute | solution.py:46
  551.4 9.6 %collective-permute-done.53 = bf16[512,1536]{1,0:T(8,128)(2,1)S(1)} collective-permute-done((bf16[512,1536]{1,0:T(8,128)(2,1)}, bf16[512,1536]{1,0:T(8,128)(2,1)S(1)}, u32[]{:S(2)}, u32[]{:S(2)}) %collective-permute-start.53) | collective-permute-done | bytes 1572896 | tf_op jit(solution)/shard_map/ppermute | solution.py:50
  576.2 7.2 %collective-permute-done.49.refs_2_ = bf16[256,2048]{1,0:T(8,128)(2,1)S(1)} collective-permute-done((bf16[256,2048]{1,0:T(8,128)(2,1)S(1)}, bf16[256,2048]{1,0:T(8,128)(2,1)S(1)}, u32[]{:S(2)}, u32[]{:S(2)}) %collective-permute-start.49) | collective-permute-done | bytes 1048608 | tf_op jit(solution)/shard_map/ppermute | solution.py:54
  585.4 5.2 norm_back.3
  597.9 18.1 %collective-permute-done.56 = f32[2,512]{1,0:T(2,128)S(1)} collective-permute-done((f32[2,512]{1,0:T(2,128)S(1)}, f32[2,512]{1,0:T(2,128)S(1)}, u32[]{:S(2)}, u32[]{:S(2)}) %collective-permute-start.56) | collective-permute-done | bytes 4128 | tf_op jit(solution)/shard_map/ppermute | solution.py:46
  (321 shorter events, 131.6 us)
Async XLA Ops:
  7.2 182.7 %all-gather.3.cloned.1.call-start = ((), (), s32[]{:S(2)}) async-start(), calls=%async_computation.3 | async-start | bytes 7864320 | tf_op jit(solution)/shard_map/all_gather | solution.py:703
  11.7 20.3 %collective-permute-start = (bf16[528,640]{1,0:T(8,128)(2,1)S(1)}, bf16[528,640]{1,0:T(8,128)(2,1)}, u32[]{:S(2)}, u32[]{:S(2)}) collective-permute-start(bf16[528,640]{1,0:T(8,128)(2,1)S(1)} %fusion.6), channel_id=1, source_target_pairs={{0,8},{8,16},{16,24},{24,0},{1,9},{9,17},{17,25},{25,1},{2,10},{10... | collective-permute-start | bytes 2027528 | tf_op jit(solution)/shard_map/ppermute | solution.py:558
  16.0 16.0 %collective-permute-start.1 = (bf16[256,2048]{1,0:T(8,128)(2,1)S(1)}, bf16[256,2048]{1,0:T(8,128)(2,1)}, u32[]{:S(2)}, u32[]{:S(2)}) collective-permute-start(bf16[256,2048]{1,0:T(8,128)(2,1)S(1)} %constant_dynamic-slice_fusion.11.refs_0_.refs_3_), channel_id=1, source_target_pairs={{0,4},{1,3},{2,6},{3,1},{4,0},{5,7},{6,2},{7,5},{8,12},{9,11},{10,... | collective-permute-start | bytes 3145736 | tf_op jit(solution)/shard_map/ppermute | solution.py:54
  32.0 18.5 %collective-permute-start.2 = (bf16[528,640]{1,0:T(8,128)(2,1)}, bf16[528,640]{1,0:T(8,128)(2,1)}, u32[]{:S(2)}, u32[]{:S(2)}) collective-permute-start(bf16[528,640]{1,0:T(8,128)(2,1)} %collective-permute-done), channel_id=1, source_target_pairs={{0,8},{8,16},{16,24},{24,0},{1,9},{9,17},{17,25},{25,1},{2,10},{10... | collective-permute-start | bytes 2027528 | tf_op jit(solution)/shard_map/ppermute | solution.py:558
  32.5 23.8 %collective-permute-start.4 = (bf16[256,2048]{1,0:T(8,128)(2,1)S(1)}, bf16[256,2048]{1,0:T(8,128)(2,1)}, u32[]{:S(2)}, u32[]{:S(2)}) collective-permute-start(bf16[256,2048]{1,0:T(8,128)(2,1)S(1)} %constant_dynamic-slice_fusion.11.refs_0_.refs_3_), channel_id=1, source_target_pairs={{0,2},{1,5},{2,0},{3,7},{4,6},{5,1},{6,4},{7,3},{8,10},{9,13},{10,... | collective-permute-start | bytes 3145736 | tf_op jit(solution)/shard_map/ppermute | solution.py:58
  34.1 24.6 %collective-permute-start.5 = (bf16[256,2048]{1,0:T(8,128)(2,1)}, bf16[256,2048]{1,0:T(8,128)(2,1)}, u32[]{:S(2)}, u32[]{:S(2)}) collective-permute-start(bf16[256,2048]{1,0:T(8,128)(2,1)} %collective-permute-done.1.refs_1_), channel_id=1, source_target_pairs={{0,2},{1,5},{2,0},{3,7},{4,6},{5,1},{6,4},{7,3},{8,10},{9,13},{10,... | collective-permute-start | bytes 3145736 | tf_op jit(solution)/shard_map/ppermute | solution.py:58
  50.5 17.6 %collective-permute-start.3 = (bf16[528,640]{1,0:T(8,128)(2,1)}, bf16[528,640]{1,0:T(8,128)(2,1)}, u32[]{:S(2)}, u32[]{:S(2)}) collective-permute-start(bf16[528,640]{1,0:T(8,128)(2,1)} %collective-permute-done.2), channel_id=1, source_target_pairs={{0,8},{8,16},{16,24},{24,0},{1,9},{9,17},{17,25},{25,1},{2,10},{10... | collective-permute-start | bytes 2027528 | tf_op jit(solution)/shard_map/ppermute | solution.py:558
  68.0 228.4 %all-gather.5.cloned.1.call-start = ((), (), s32[]{:S(2)}) async-start(), calls=%async_computation.4 | async-start | bytes 7864320 | tf_op jit(solution)/shard_map/all_gather | solution.py:703
  77.3 25.4 %collective-permute-start.10 = (bf16[256,2048]{1,0:T(8,128)(2,1)S(1)}, bf16[256,2048]{1,0:T(8,128)(2,1)S(1)}, u32[]{:S(2)}, u32[]{:S(2)}) collective-permute-start(bf16[256,2048]{1,0:T(8,128)(2,1)S(1)} %constant_dynamic-slice_fusion.6.refs_8_.refs_4_), channel_id=1, source_target_pairs={{0,4},{1,3},{2,6},{3,1},{4,0},{5,7},{6,2},{7,5},{8,12},{9,11},{10,... | collective-permute-start | bytes 3145736 | tf_op jit(solution)/shard_map/ppermute | solution.py:54
  78.6 24.2 %collective-permute-start.11 = (bf16[256,2048]{1,0:T(8,128)(2,1)S(1)}, bf16[256,2048]{1,0:T(8,128)(2,1)}, u32[]{:S(2)}, u32[]{:S(2)}) collective-permute-start(bf16[256,2048]{1,0:T(8,128)(2,1)S(1)} %constant_dynamic-slice_fusion.6.refs_8_.refs_4_), channel_id=1, source_target_pairs={{0,2},{1,5},{2,0},{3,7},{4,6},{5,1},{6,4},{7,3},{8,10},{9,13},{10,... | collective-permute-start | bytes 3145736 | tf_op jit(solution)/shard_map/ppermute | solution.py:58
  79.8 48.6 %collective-permute-start.13 = (bf16[256,2048]{1,0:T(8,128)(2,1)S(1)}, bf16[256,2048]{1,0:T(8,128)(2,1)}, u32[]{:S(2)}, u32[]{:S(2)}) collective-permute-start(bf16[256,2048]{1,0:T(8,128)(2,1)S(1)} %constant_dynamic-slice_fusion.6.refs_8_.refs_4_), channel_id=1, source_target_pairs={{0,1},{1,0},{2,3},{3,2},{4,5},{5,4},{6,7},{7,6},{8,9},{9,8},{10,11... | collective-permute-start | bytes 3145736 | tf_op jit(solution)/shard_map/ppermute | solution.py:42
  102.8 25.6 %collective-permute-start.12 = (bf16[256,2048]{1,0:T(8,128)(2,1)S(1)}, bf16[256,2048]{1,0:T(8,128)(2,1)}, u32[]{:S(2)}, u32[]{:S(2)}) collective-permute-start(bf16[256,2048]{1,0:T(8,128)(2,1)S(1)} %collective-permute-done.10.refs_9_), channel_id=1, source_target_pairs={{0,2},{1,5},{2,0},{3,7},{4,6},{5,1},{6,4},{7,3},{8,10},{9,13},{10,... | collective-permute-start | bytes 3145736 | tf_op jit(solution)/shard_map/ppermute | solution.py:58
  103.8 24.6 %collective-permute-start.14 = (bf16[256,2048]{1,0:T(8,128)(2,1)S(1)}, bf16[256,2048]{1,0:T(8,128)(2,1)}, u32[]{:S(2)}, u32[]{:S(2)}) collective-permute-start(bf16[256,2048]{1,0:T(8,128)(2,1)S(1)} %collective-permute-done.10.refs_9_), channel_id=1, source_target_pairs={{0,1},{1,0},{2,3},{3,2},{4,5},{5,4},{6,7},{7,6},{8,9},{9,8},{10,11... | collective-permute-start | bytes 3145736 | tf_op jit(solution)/shard_map/ppermute | solution.py:42
  104.2 24.2 %collective-permute-start.15 = (bf16[256,2048]{1,0:T(8,128)(2,1)}, bf16[256,2048]{1,0:T(8,128)(2,1)}, u32[]{:S(2)}, u32[]{:S(2)}) collective-permute-start(bf16[256,2048]{1,0:T(8,128)(2,1)} %collective-permute-done.11.refs_10_), channel_id=1, source_target_pairs={{0,1},{1,0},{2,3},{3,2},{4,5},{5,4},{6,7},{7,6},{8,9},{9,8},{10,11... | collective-permute-start | bytes 3145736 | tf_op jit(solution)/shard_map/ppermute | solution.py:42
  139.1 23.2 %collective-permute-start.17 = (bf16[512,2048]{1,0:T(8,128)(2,1)}, bf16[512,2048]{1,0:T(8,128)(2,1)S(1)}, u32[]{:S(2)}, u32[]{:S(2)}) collective-permute-start(bf16[512,2048]{1,0:T(8,128)(2,1)} %back.13), channel_id=1, source_target_pairs={{0,1},{1,0},{2,3},{3,2},{4,5},{5,4},{6,7},{7,6},{8,9},{9,8},{10,11... | collective-permute-start | bytes 6291464 | tf_op jit(solution)/shard_map/ppermute | solution.py:42
  140.6 291.1 %reduce-scatter.4.cloned.1.call-start = ((), (), s32[]{:S(2)}) async-start(), calls=%async_computation.5 | async-start | bytes 7864320 | tf_op jit(solution)/shard_map/reduce_scatter | solution.py:734
  147.5 14.9 %collective-permute-start.19 = (bf16[256,2048]{1,0:T(8,128)(2,1)S(1)}, bf16[256,2048]{1,0:T(8,128)(2,1)S(1)}, u32[]{:S(2)}, u32[]{:S(2)}) collective-permute-start(bf16[256,2048]{1,0:T(8,128)(2,1)S(1)} %get-tuple-element.152), channel_id=1, source_target_pairs={{0,2},{1,5},{2,0},{3,7},{4,6},{5,1},{6,4},{7,3},{8,10},{9,13},{10,... | collective-permute-start | bytes 3145736 | tf_op jit(solution)/shard_map/ppermute | solution.py:58
  163.7 26.1 %collective-permute-start.21 = (bf16[256,2048]{1,0:T(8,128)(2,1)S(1)}, bf16[256,2048]{1,0:T(8,128)(2,1)}, u32[]{:S(2)}, u32[]{:S(2)}) collective-permute-start(bf16[256,2048]{1,0:T(8,128)(2,1)S(1)} %fusion.5), channel_id=1, source_target_pairs={{0,4},{1,3},{2,6},{3,1},{4,0},{5,7},{6,2},{7,5},{8,12},{9,11},{10,... | collective-permute-start | bytes 3145736 | tf_op jit(solution)/shard_map/ppermute | solution.py:54
  165.2 24.6 %collective-permute-start.20 = (bf16[256,2048]{1,0:T(8,128)(2,1)S(1)}, bf16[256,2048]{1,0:T(8,128)(2,1)}, u32[]{:S(2)}, u32[]{:S(2)}) collective-permute-start(bf16[256,2048]{1,0:T(8,128)(2,1)S(1)} %get-tuple-element.91), channel_id=1, source_target_pairs={{0,2},{1,5},{2,0},{3,7},{4,6},{5,1},{6,4},{7,3},{8,10},{9,13},{10,... | collective-permute-start | bytes 3145736 | tf_op jit(solution)/shard_map/ppermute | solution.py:58
  193.4 25.2 %collective-permute-start.22 = (bf16[256,2048]{1,0:T(8,128)(2,1)S(1)}, bf16[256,2048]{1,0:T(8,128)(2,1)S(1)}, u32[]{:S(2)}, u32[]{:S(2)}) collective-permute-start(bf16[256,2048]{1,0:T(8,128)(2,1)S(1)} %multiply_convert_fusion.refs_0_), channel_id=1, source_target_pairs={{0,4},{1,3},{2,6},{3,1},{4,0},{5,7},{6,2},{7,5},{8,12},{9,11},{10,... | collective-permute-start | bytes 3145736 | tf_op jit(solution)/shard_map/ppermute | solution.py:54
  194.2 24.4 %collective-permute-start.23 = (bf16[256,2048]{1,0:T(8,128)(2,1)S(1)}, bf16[256,2048]{1,0:T(8,128)(2,1)S(1)}, u32[]{:S(2)}, u32[]{:S(2)}) collective-permute-start(bf16[256,2048]{1,0:T(8,128)(2,1)S(1)} %multiply_convert_fusion.refs_0_), channel_id=1, source_target_pairs={{0,2},{1,5},{2,0},{3,7},{4,6},{5,1},{6,4},{7,3},{8,10},{9,13},{10,... | collective-permute-start | bytes 3145736 | tf_op jit(solution)/shard_map/ppermute | solution.py:58
  195.4 25.3 %collective-permute-start.25 = (bf16[256,2048]{1,0:T(8,128)(2,1)S(1)}, bf16[256,2048]{1,0:T(8,128)(2,1)S(1)}, u32[]{:S(2)}, u32[]{:S(2)}) collective-permute-start(bf16[256,2048]{1,0:T(8,128)(2,1)S(1)} %multiply_convert_fusion.refs_0_), channel_id=1, source_target_pairs={{0,1},{1,0},{2,3},{3,2},{4,5},{5,4},{6,7},{7,6},{8,9},{9,8},{10,11... | collective-permute-start | bytes 3145736 | tf_op jit(solution)/shard_map/ppermute | solution.py:42
  218.6 14.9 %collective-permute-start.24 = (bf16[256,2048]{1,0:T(8,128)(2,1)S(1)}, bf16[256,2048]{1,0:T(8,128)(2,1)S(1)}, u32[]{:S(2)}, u32[]{:S(2)}) collective-permute-start(bf16[256,2048]{1,0:T(8,128)(2,1)S(1)} %collective-permute-done.22.refs_1_), channel_id=1, source_target_pairs={{0,2},{1,5},{2,0},{3,7},{4,6},{5,1},{6,4},{7,3},{8,10},{9,13},{10,... | collective-permute-start | bytes 3145736 | tf_op jit(solution)/shard_map/ppermute | solution.py:58
  278.4 245.0 %reduce-scatter.6.cloned.1.call-start = ((), (), s32[]{:S(2)}) async-start(), calls=%async_computation.6 | async-start | bytes 7864320 | tf_op jit(solution)/shard_map/reduce_scatter | solution.py:734
  340.5 26.2 %collective-permute-start.30 = (bf16[512,2048]{1,0:T(8,128)(2,1)S(1)}, bf16[512,2048]{1,0:T(8,128)(2,1)}, u32[]{:S(2)}, u32[]{:S(2)}) collective-permute-start(bf16[512,2048]{1,0:T(8,128)(2,1)S(1)} %slice_add_fusion), channel_id=1, source_target_pairs={{0,2},{1,5},{2,0},{3,7},{4,6},{5,1},{6,4},{7,3},{8,10},{9,13},{10,... | collective-permute-start | bytes 6291464 | tf_op jit(solution)/shard_map/ppermute | solution.py:58
  361.4 231.6 %reduce-scatter.8.cloned.1.call-start = ((), (), s32[]{:S(2)}) async-start(), calls=%async_computation.7 | async-start | bytes 3276800 | tf_op jit(solution)/shard_map/reduce_scatter | solution.py:796
  370.0 14.9 %collective-permute-start.31 = (bf16[256,2048]{1,0:T(8,128)(2,1)S(1)}, bf16[256,2048]{1,0:T(8,128)(2,1)S(1)}, u32[]{:S(2)}, u32[]{:S(2)}) collective-permute-start(bf16[256,2048]{1,0:T(8,128)(2,1)S(1)} %slice.217), channel_id=1, source_target_pairs={{0,4},{1,3},{2,6},{3,1},{4,0},{5,7},{6,2},{7,5},{8,12},{9,11},{10,... | collective-permute-start | bytes 3145736 | tf_op jit(solution)/shard_map/ppermute | solution.py:54
  377.9 40.1 %collective-permute-start.35 = (bf16[512,2048]{1,0:T(8,128)(2,1)}, bf16[512,2048]{1,0:T(8,128)(2,1)}, u32[]{:S(2)}, u32[]{:S(2)}) collective-permute-start(bf16[512,2048]{1,0:T(8,128)(2,1)} %back.18), channel_id=1, source_target_pairs={{0,1},{1,0},{2,3},{3,2},{4,5},{5,4},{6,7},{7,6},{8,9},{9,8},{10,11... | collective-permute-start | bytes 6291464 | tf_op jit(solution)/shard_map/ppermute | solution.py:42
  390.8 25.4 %collective-permute-start.32 = (bf16[256,2048]{1,0:T(8,128)(2,1)}, bf16[256,2048]{1,0:T(8,128)(2,1)S(1)}, u32[]{:S(2)}, u32[]{:S(2)}) collective-permute-start(bf16[256,2048]{1,0:T(8,128)(2,1)} %norm_back.2.refs_0_.refs_5_), channel_id=1, source_target_pairs={{0,4},{1,3},{2,6},{3,1},{4,0},{5,7},{6,2},{7,5},{8,12},{9,11},{10,... | collective-permute-start | bytes 3145736 | tf_op jit(solution)/shard_map/ppermute | solution.py:54
  392.3 23.8 %collective-permute-start.33 = (bf16[256,2048]{1,0:T(8,128)(2,1)}, bf16[256,2048]{1,0:T(8,128)(2,1)S(1)}, u32[]{:S(2)}, u32[]{:S(2)}) collective-permute-start(bf16[256,2048]{1,0:T(8,128)(2,1)} %norm_back.2.refs_0_.refs_5_), channel_id=1, source_target_pairs={{0,2},{1,5},{2,0},{3,7},{4,6},{5,1},{6,4},{7,3},{8,10},{9,13},{10,... | collective-permute-start | bytes 3145736 | tf_op jit(solution)/shard_map/ppermute | solution.py:58
  416.7 14.9 %collective-permute-start.38 = (bf16[256,2048]{1,0:T(8,128)(2,1)S(1)}, bf16[256,2048]{1,0:T(8,128)(2,1)}, u32[]{:S(2)}, u32[]{:S(2)}) collective-permute-start(bf16[256,2048]{1,0:T(8,128)(2,1)S(1)} %collective-permute-done.32.refs_1_), channel_id=1, source_target_pairs={{0,2},{1,5},{2,0},{3,7},{4,6},{5,1},{6,4},{7,3},{8,10},{9,13},{10,... | collective-permute-start | bytes 3145736 | tf_op jit(solution)/shard_map/ppermute | solution.py:58
  417.2 14.4 %collective-permute-start.40 = (bf16[256,2048]{1,0:T(8,128)(2,1)S(1)}, bf16[256,2048]{1,0:T(8,128)(2,1)}, u32[]{:S(2)}, u32[]{:S(2)}) collective-permute-start(bf16[256,2048]{1,0:T(8,128)(2,1)S(1)} %collective-permute-done.32.refs_1_), channel_id=1, source_target_pairs={{0,1},{1,0},{2,3},{3,2},{4,5},{5,4},{6,7},{7,6},{8,9},{9,8},{10,11... | collective-permute-start | bytes 3145736 | tf_op jit(solution)/shard_map/ppermute | solution.py:42
  431.6 50.2 %collective-permute-start.43 = (bf16[512,1536]{1,0:T(8,128)(2,1)}, bf16[512,1536]{1,0:T(8,128)(2,1)S(1)}, u32[]{:S(2)}, u32[]{:S(2)}) collective-permute-start(bf16[512,1536]{1,0:T(8,128)(2,1)} %reduce-scatter.4.cloned.1.call-done), channel_id=1, source_target_pairs={{0,4},{4,0},{1,5},{5,1},{2,6},{6,2},{3,7},{7,3},{8,12},{12,8},{9,1... | collective-permute-start | bytes 4718600 | tf_op jit(solution)/shard_map/ppermute | solution.py:50
  433.2 48.6 %collective-permute-start.36 = (bf16[256,2048]{1,0:T(8,128)(2,1)}, bf16[256,2048]{1,0:T(8,128)(2,1)S(1)}, u32[]{:S(2)}, u32[]{:S(2)}) collective-permute-start(bf16[256,2048]{1,0:T(8,128)(2,1)} %get-tuple-element.150), channel_id=1, source_target_pairs={{0,2},{2,0},{1,3},{3,1},{4,6},{6,4},{5,7},{7,5},{8,10},{10,8},{9,1... | collective-permute-start | bytes 3145736 | tf_op jit(solution)/shard_map/ppermute | solution.py:46
  433.7 48.1 %collective-permute-start.37 = (bf16[256,2048]{1,0:T(8,128)(2,1)}, bf16[256,2048]{1,0:T(8,128)(2,1)S(1)}, u32[]{:S(2)}, u32[]{:S(2)}) collective-permute-start(bf16[256,2048]{1,0:T(8,128)(2,1)} %get-tuple-element.143), channel_id=1, source_target_pairs={{0,2},{2,0},{1,3},{3,1},{4,6},{6,4},{5,7},{7,5},{8,10},{10,8},{9,1... | collective-permute-start | bytes 3145736 | tf_op jit(solution)/shard_map/ppermute | solution.py:46
  493.4 30.6 %collective-permute-start.44 = (bf16[512,2048]{1,0:T(8,128)(2,1)}, bf16[512,2048]{1,0:T(8,128)(2,1)}, u32[]{:S(2)}, u32[]{:S(2)}) collective-permute-start(bf16[512,2048]{1,0:T(8,128)(2,1)} %back.22), channel_id=1, source_target_pairs={{0,1},{1,0},{2,3},{3,2},{4,5},{5,4},{6,7},{7,6},{8,9},{9,8},{10,11... | collective-permute-start | bytes 6291464 | tf_op jit(solution)/shard_map/ppermute | solution.py:42
  493.7 26.3 %collective-permute-start.47 = (bf16[256,2048]{1,0:T(8,128)(2,1)}, bf16[256,2048]{1,0:T(8,128)(2,1)}, u32[]{:S(2)}, u32[]{:S(2)}) collective-permute-start(bf16[256,2048]{1,0:T(8,128)(2,1)} %add.380), channel_id=1, source_target_pairs={{0,4},{4,0},{1,5},{5,1},{2,6},{6,2},{3,7},{7,3},{8,12},{12,8},{9,1... | collective-permute-start | bytes 3145736 | tf_op jit(solution)/shard_map/ppermute | solution.py:50
  503.1 20.8 %collective-permute-start.46 = (bf16[256,2048]{1,0:T(8,128)(2,1)}, bf16[256,2048]{1,0:T(8,128)(2,1)}, u32[]{:S(2)}, u32[]{:S(2)}) collective-permute-start(bf16[256,2048]{1,0:T(8,128)(2,1)} %get-tuple-element.146), channel_id=1, source_target_pairs={{0,2},{1,5},{2,0},{3,7},{4,6},{5,1},{6,4},{7,3},{8,10},{9,13},{10,... | collective-permute-start | bytes 3145736 | tf_op jit(solution)/shard_map/ppermute | solution.py:58
  522.8 26.4 %collective-permute-start.50 = (bf16[256,2048]{1,0:T(8,128)(2,1)}, bf16[256,2048]{1,0:T(8,128)(2,1)}, u32[]{:S(2)}, u32[]{:S(2)}) collective-permute-start(bf16[256,2048]{1,0:T(8,128)(2,1)} %add_convert_fusion), channel_id=1, source_target_pairs={{0,2},{2,0},{1,3},{3,1},{4,6},{6,4},{5,7},{7,5},{8,10},{10,8},{9,1... | collective-permute-start | bytes 3145736 | tf_op jit(solution)/shard_map/ppermute | solution.py:46
  523.3 46.1 %collective-permute-start.51 = (bf16[256,2048]{1,0:T(8,128)(2,1)}, bf16[256,2048]{1,0:T(8,128)(2,1)}, u32[]{:S(2)}, u32[]{:S(2)}) collective-permute-start(bf16[256,2048]{1,0:T(8,128)(2,1)} %add_convert_fusion), channel_id=1, source_target_pairs={{0,1},{1,0},{2,3},{3,2},{4,5},{5,4},{6,7},{7,6},{8,9},{9,8},{10,11... | collective-permute-start | bytes 3145736 | tf_op jit(solution)/shard_map/ppermute | solution.py:42
  523.4 37.6 %collective-permute-start.53 = (bf16[512,1536]{1,0:T(8,128)(2,1)}, bf16[512,1536]{1,0:T(8,128)(2,1)S(1)}, u32[]{:S(2)}, u32[]{:S(2)}) collective-permute-start(bf16[512,1536]{1,0:T(8,128)(2,1)} %reduce-scatter.6.cloned.1.call-done), channel_id=1, source_target_pairs={{0,4},{4,0},{1,5},{5,1},{2,6},{6,2},{3,7},{7,3},{8,12},{12,8},{9,1... | collective-permute-start | bytes 4718600 | tf_op jit(solution)/shard_map/ppermute | solution.py:50
  528.0 55.4 %collective-permute-start.49 = (bf16[256,2048]{1,0:T(8,128)(2,1)S(1)}, bf16[256,2048]{1,0:T(8,128)(2,1)S(1)}, u32[]{:S(2)}, u32[]{:S(2)}) collective-permute-start(bf16[256,2048]{1,0:T(8,128)(2,1)S(1)} %get-tuple-element.121), channel_id=1, source_target_pairs={{0,4},{1,3},{2,6},{3,1},{4,0},{5,7},{6,2},{7,5},{8,12},{9,11},{10,... | collective-permute-start | bytes 3145736 | tf_op jit(solution)/shard_map/ppermute | solution.py:54
  529.3 54.2 %collective-permute-start.48 = (bf16[256,2048]{1,0:T(8,128)(2,1)S(1)}, bf16[256,2048]{1,0:T(8,128)(2,1)S(1)}, u32[]{:S(2)}, u32[]{:S(2)}) collective-permute-start(bf16[256,2048]{1,0:T(8,128)(2,1)S(1)} %copy-done.48), channel_id=1, source_target_pairs={{0,2},{1,5},{2,0},{3,7},{4,6},{5,1},{6,4},{7,3},{8,10},{9,13},{10,... | collective-permute-start | bytes 3145736 | tf_op jit(solution)/shard_map/ppermute | solution.py:58
  550.9 18.5 %collective-permute-start.52 = (bf16[256,2048]{1,0:T(8,128)(2,1)}, bf16[256,2048]{1,0:T(8,128)(2,1)S(1)}, u32[]{:S(2)}, u32[]{:S(2)}) collective-permute-start(bf16[256,2048]{1,0:T(8,128)(2,1)} %collective-permute-done.50), channel_id=1, source_target_pairs={{0,1},{1,0},{2,3},{3,2},{4,5},{5,4},{6,7},{7,6},{8,9},{9,8},{10,11... | collective-permute-start | bytes 3145736 | tf_op jit(solution)/shard_map/ppermute | solution.py:42
  590.7 25.4 %collective-permute-start.54 = (bf16[256,2048]{1,0:T(8,128)(2,1)}, bf16[256,2048]{1,0:T(8,128)(2,1)}, u32[]{:S(2)}, u32[]{:S(2)}) collective-permute-start(bf16[256,2048]{1,0:T(8,128)(2,1)} %norm_back.3), channel_id=1, source_target_pairs={{0,2},{2,0},{1,3},{3,1},{4,6},{6,4},{5,7},{7,5},{8,10},{10,8},{9,1... | collective-permute-start | bytes 3145736 | tf_op jit(solution)/shard_map/ppermute | solution.py:46
  593.0 23.1 %collective-permute-start.57 = (bf16[512,640]{1,0:T(8,128)(2,1)}, bf16[512,640]{1,0:T(8,128)(2,1)S(1)}, u32[]{:S(2)}, u32[]{:S(2)}) collective-permute-start(bf16[512,640]{1,0:T(8,128)(2,1)} %reduce-scatter.8.cloned.1.call-done), channel_id=1, source_target_pairs={{0,4},{4,0},{1,5},{5,1},{2,6},{6,2},{3,7},{7,3},{8,12},{12,8},{9,1... | collective-permute-start | bytes 1966088 | tf_op jit(solution)/shard_map/ppermute | solution.py:50
  596.8 19.3 %collective-permute-start.56 = (f32[2,512]{1,0:T(2,128)S(1)}, f32[2,512]{1,0:T(2,128)S(1)}, u32[]{:S(2)}, u32[]{:S(2)}) collective-permute-start(f32[2,512]{1,0:T(2,128)S(1)} %fusion.18), channel_id=1, source_target_pairs={{0,2},{2,0},{1,3},{3,1},{4,6},{6,4},{5,7},{7,5},{8,10},{10,8},{9,1... | collective-permute-start | bytes 12296 | tf_op jit(solution)/shard_map/ppermute | solution.py:46
  597.9 27.7 %collective-permute-start.58 = (bf16[256,2048]{1,0:T(8,128)(2,1)S(1)}, bf16[256,2048]{1,0:T(8,128)(2,1)S(1)}, u32[]{:S(2)}, u32[]{:S(2)}) collective-permute-start(bf16[256,2048]{1,0:T(8,128)(2,1)S(1)} %copy-done.34), channel_id=1, source_target_pairs={{0,1},{1,0},{2,3},{3,2},{4,5},{5,4},{6,7},{7,6},{8,9},{9,8},{10,11... | collective-permute-start | bytes 3145736 | tf_op jit(solution)/shard_map/ppermute | solution.py:42
  (76 other events, 1070.1 us)
Sparse Core Ops, SparseCore 0:
  68.2 113.0 all-gather.2
  182.8 113.5 all-gather.4
  298.8 108.9 reduce-scatter.3
  409.9 111.2 reduce-scatter.5
  524.0 52.6 reduce-scatter.7

commit v15 on v14

--- a/solution.py
+++ b/solution.py
@@ -90,7 +90,7 @@
 
 def norm_back(parts, hidden, gain, kept):
     rows, depth = hidden.shape
-    step = min(64, rows)
+    step = min(128, rows)
     block = pl.BlockSpec((step, depth), lambda i: (i, 0))
     return pl.pallas_call(
         functools.partial(norm_back_kernel, len(parts)),

time: 647 us -> 646 us (level)
  no operation moved by 1% of the time
where the time goes in v15:
time: 646 us; the launch traced here: 637 us
  Pallas kernels  266 us (41%)
  waiting for transfers between devices  209 us (32%)
  other arithmetic  68.7 us (11%)
  starting transfers between devices  44.3 us (7%)
  local copies, waits for them, and re-layouts  34 us (5%)
  between operations  15.2 us (2%)
    pallas_call x12, Pallas kernels, back_product(): pl.pallas_call(functools.partial(back_kernel, len(terms)), out_shape=jax....  79 us
    ppermute x7, waiting for transfers between devices, swap_first(): return lax.ppermute(v, ('ctx', 'tp'), FIRST)  76.2 us
    pallas_call x3, Pallas kernels, weight_grads(): pl.pallas_call(functools.partial(grads_kernel, len(x), len(y)), out_shape...  51.1 us
    pallas_call x2, Pallas kernels, ffn_chunk(): pl.pallas_call(functools.partial(ffn_kernel, len(x)), out_shape=jax.Shape...  43.5 us
    ppermute x13, waiting for transfers between devices, swap_second(): return lax.ppermute(v, ('ctx', 'tp'), SECOND)  37.4 us
    ppermute x5, waiting for transfers between devices, swap_y(): return lax.ppermute(v, 'tp', ACROSS)  35.9 us
    pallas_call x1, Pallas kernels, attend_back(): pl.pallas_call(attend_back_kernel, out_shape=jax.ShapeDtypeStruct((rows,...  35.2 us
    ppermute x3, waiting for transfers between devices, ring_over(): pieces.append(lax.ppermute(sent, 'fsdp', cycle))  30.9 us
  transfers between devices with their start and end apart: 66, of which 26 were waited for; matrix products, arithmetic and copies ran while one was open for 13% of the time, Pallas kernels for 42%

profile of v15, /device:TPU:0, one launch (start us, length us, event | category | flops | bytes accessed | tf_op | source)
XLA Modules:
  0.0 637.2 jit_solution(15628694310054784549)
XLA Ops:
  20.7 5.6 negate_select_fusion
  26.3 5.7 collective-permute-done
  34.6 15.9 %collective-permute-done.2 = bf16[528,640]{1,0:T(8,128)(2,1)} collective-permute-done((bf16[528,640]{1,0:T(8,128)(2,1)}, bf16[528,640]{1,0:T(8,128)(2,1)}, u32[]{:S(2)}, u32[]{:S(2)}) %collective-permute-start.2) | collective-permute-done | bytes 675872 | tf_op jit(solution)/shard_map/ppermute | solution.py:558
  58.7 9.3 %collective-permute-done.3 = bf16[528,640]{1,0:T(8,128)(2,1)} collective-permute-done((bf16[528,640]{1,0:T(8,128)(2,1)}, bf16[528,640]{1,0:T(8,128)(2,1)}, u32[]{:S(2)}, u32[]{:S(2)}) %collective-permute-start.3) | collective-permute-done | bytes 675872 | tf_op jit(solution)/shard_map/ppermute | solution.py:558
  79.8 15.3 %qkv.1.q_ref.kv_ref.refs_8_ = bf16[2048,2432]{1,0:T(8,128)(2,1)} custom-call(bf16[256,2048]{1,0:T(8,128)(2,1)} %copy-done.7, bf16[256,2048]{1,0:T(8,128)(2,1)} %collective-permute-done.1.refs_1_, bf16[256,2048]{1,0:T(8,128)(2,1)} %collective-permute-done.4.refs_2_, bf16[256,2048]{1,0:T(8,128)(2,1)} %collective-permute-done.5.refs_3_, ...), custom_call_target="tpu_custom_call" | custom-call | flops 1 | bytes 1 | tf_op jit(solution)/shard_map/qkv/pallas_call | solution.py:165
  95.2 7.6 %collective-permute-done.10.refs_9_ = bf16[256,2048]{1,0:T(8,128)(2,1)S(1)} collective-permute-done((bf16[256,2048]{1,0:T(8,128)(2,1)S(1)}, bf16[256,2048]{1,0:T(8,128)(2,1)S(1)}, u32[]{:S(2)}, u32[]{:S(2)}) %collective-permute-start.10) | collective-permute-done | bytes 1048608 | tf_op jit(solution)/shard_map/ppermute | solution.py:54
  105.7 22.7 %attend.1.refs_0_.h_ref.refs_9_ = f32[2048,384]{1,0:T(8,128)} custom-call(s32[8]{0:T(128)} %select_reduce_fusion.2.place, s32[8]{0:T(128)} %and_select_fusion.2.first, bf16[2048,2432]{1,0:T(8,128)(2,1)} %qkv.1.q_ref.kv_ref.refs_8_, bf16[2048,2432]{1,0:T(8,128)(2,1)} %qkv.1.q_ref.kv_ref.refs_8_, s32[2048,1]{1,0:T(8,128)} %copy.28.start_ref), custom_call_target="tpu_custom_call" | custom-call | flops 1 | bytes 1 | tf_op jit(solution)/shard_map/attend/pallas_call | solution.py:382
  131.4 3.8 back.14
  135.6 3.5 back.13
  140.8 4.2 back.12
  149.0 13.3 %collective-permute-done.19 = bf16[256,2048]{1,0:T(8,128)(2,1)S(1)} collective-permute-done((bf16[256,2048]{1,0:T(8,128)(2,1)S(1)}, bf16[256,2048]{1,0:T(8,128)(2,1)S(1)}, u32[]{:S(2)}, u32[]{:S(2)}) %collective-permute-start.19) | collective-permute-done | bytes 1048608 | tf_op jit(solution)/shard_map/ppermute | solution.py:58
  165.9 24.0 %collective-permute-done.21 = bf16[256,2048]{1,0:T(8,128)(2,1)} collective-permute-done((bf16[256,2048]{1,0:T(8,128)(2,1)S(1)}, bf16[256,2048]{1,0:T(8,128)(2,1)}, u32[]{:S(2)}, u32[]{:S(2)}) %collective-permute-start.21) | collective-permute-done | bytes 1048608 | tf_op jit(solution)/shard_map/ppermute | solution.py:54
  189.8 3.3 multiply_reduce_fusion.2
  195.4 23.1 %collective-permute-done.22.refs_1_ = bf16[256,2048]{1,0:T(8,128)(2,1)S(1)} collective-permute-done((bf16[256,2048]{1,0:T(8,128)(2,1)S(1)}, bf16[256,2048]{1,0:T(8,128)(2,1)S(1)}, u32[]{:S(2)}, u32[]{:S(2)}) %collective-permute-start.22) | collective-permute-done | bytes 1048608 | tf_op jit(solution)/shard_map/ppermute | solution.py:54
  220.8 12.7 %collective-permute-done.24.refs_3_ = bf16[256,2048]{1,0:T(8,128)(2,1)S(1)} collective-permute-done((bf16[256,2048]{1,0:T(8,128)(2,1)S(1)}, bf16[256,2048]{1,0:T(8,128)(2,1)S(1)}, u32[]{:S(2)}, u32[]{:S(2)}) %collective-permute-start.24) | collective-permute-done | bytes 1048608 | tf_op jit(solution)/shard_map/ppermute | solution.py:58
  237.3 21.8 %ffn.2.refs_16_.refs_17_.refs_0_ = bf16[2048,1536]{1,0:T(8,128)(2,1)} custom-call(bf16[256,2048]{1,0:T(8,128)(2,1)} %copy-done.6, bf16[256,2048]{1,0:T(8,128)(2,1)} %copy-done.22, bf16[256,2048]{1,0:T(8,128)(2,1)} %copy-done.23, bf16[256,2048]{1,0:T(8,128)(2,1)} %copy-done.26, bf16[256,2048]{1,0:T(8,128)(2,1)} %copy-done.24, bf16[256,2048]{1,0:T(8,128)(2,1)} %copy-done.27, ...), custom_call_target="tpu_custom_call" | custom-call | flops 1 | bytes 1 | tf_op jit(solution)/shard_map/ffn/pallas_call | solution.py:204
  259.1 19.3 %weight_grads.3 = bf16[2048,1536]{1,0:T(8,128)(2,1)} custom-call(bf16[256,2048]{1,0:T(8,128)(2,1)} %copy-done.6, bf16[256,2048]{1,0:T(8,128)(2,1)} %copy-done.22, bf16[256,2048]{1,0:T(8,128)(2,1)} %copy-done.23, bf16[256,2048]{1,0:T(8,128)(2,1)} %copy-done.26, bf16[256,2048]{1,0:T(8,128)(2,1)} %copy-done.24, bf16[256,2048]{1,0:T(8,128)(2,1)} %copy-done.27, ...), custom_call_target="tpu_custom_call" | custom-call | flops 20000000000 | bytes 1 | tf_op jit(solution)/shard_map/weight_grads/pallas_call | solution.py:240
  278.8 13.4 %back.15.refs_2_ = bf16[2048,2048]{1,0:T(8,128)(2,1)} custom-call(bf16[2048,1536]{1,0:T(8,128)(2,1)} %ffn.2.refs_16_.refs_17_.refs_0_, bf16[2048,1536]{1,0:T(8,128)(2,1)} %all-gather.3.cloned.1.call-done.refs_16_.refs_1_.refs_2_), custom_call_target="tpu_custom_call" | custom-call | flops 1 | bytes 1 | tf_op jit(solution)/shard_map/back/pallas_call | solution.py:275
  292.2 4.3 all-gather.5.cloned.1.call-done.refs_16_.refs_1_.refs_3_
  296.5 21.7 %ffn.3.refs_0_.refs_16_.refs_17_.refs_1_ = bf16[2048,1536]{1,0:T(8,128)(2,1)} custom-call(bf16[256,2048]{1,0:T(8,128)(2,1)} %copy-done.6, bf16[256,2048]{1,0:T(8,128)(2,1)} %copy-done.22, bf16[256,2048]{1,0:T(8,128)(2,1)} %copy-done.23, bf16[256,2048]{1,0:T(8,128)(2,1)} %copy-done.26, bf16[256,2048]{1,0:T(8,128)(2,1)} %copy-done.24, ...), custom_call_target="tpu_custom_call" | custom-call | flops 1 | bytes 1 | tf_op jit(solution)/shard_map/ffn/pallas_call | solution.py:204
  318.2 9.3 %back.17 = bf16[1024,2048]{1,0:T(8,128)(2,1)} custom-call(bf16[2048,1536]{1,0:T(8,128)(2,1)} %ffn.3.refs_0_.refs_16_.refs_17_.refs_1_, bf16[2048,1536]{1,0:T(8,128)(2,1)} %all-gather.5.cloned.1.call-done.refs_16_.refs_1_.refs_3_, bf16[2048,2048]{1,0:T(8,128)(2,1)} %back.15.refs_2_), custom_call_target="tpu_custom_call" | custom-call | flops 1 | bytes 1 | tf_op jit(solution)/shard_map/back/pallas_call | solution.py:275
  327.6 9.6 %back.16 = bf16[1024,2048]{1,0:T(8,128)(2,1)} custom-call(bf16[2048,1536]{1,0:T(8,128)(2,1)} %ffn.3.refs_0_.refs_16_.refs_17_.refs_1_, bf16[2048,1536]{1,0:T(8,128)(2,1)} %all-gather.5.cloned.1.call-done.refs_16_.refs_1_.refs_3_, bf16[2048,2048]{1,0:T(8,128)(2,1)} %back.15.refs_2_), custom_call_target="tpu_custom_call" | custom-call | flops 1 | bytes 1 | tf_op jit(solution)/shard_map/back/pallas_call | solution.py:275
  337.2 3.3 slice_add_fusion
  342.1 19.3 %weight_grads.4 = bf16[2048,1536]{1,0:T(8,128)(2,1)} custom-call(bf16[256,2048]{1,0:T(8,128)(2,1)} %copy-done.6, bf16[256,2048]{1,0:T(8,128)(2,1)} %copy-done.22, bf16[256,2048]{1,0:T(8,128)(2,1)} %copy-done.23, bf16[256,2048]{1,0:T(8,128)(2,1)} %copy-done.26, bf16[256,2048]{1,0:T(8,128)(2,1)} %copy-done.24, bf16[256,2048]{1,0:T(8,128)(2,1)} %copy-done.27, ...), custom_call_target="tpu_custom_call" | custom-call | flops 20000000000 | bytes 1 | tf_op jit(solution)/shard_map/weight_grads/pallas_call | solution.py:240
  361.5 5.2 collective-permute-done.30
  366.7 3.2 fusion.2.refs_0_
  371.6 6.2 back.18
  377.9 7.0 %collective-permute-done.31.refs_1_ = bf16[256,2048]{1,0:T(8,128)(2,1)S(1)} collective-permute-done((bf16[256,2048]{1,0:T(8,128)(2,1)S(1)}, bf16[256,2048]{1,0:T(8,128)(2,1)S(1)}, u32[]{:S(2)}, u32[]{:S(2)}) %collective-permute-start.31) | collective-permute-done | bytes 1048608 | tf_op jit(solution)/shard_map/ppermute | solution.py:54
  385.8 4.3 norm_back.2.refs_0_.refs_5_
  393.2 6.3 back.20
  399.4 8.8 %back.19 = bf16[1024,2048]{1,0:T(8,128)(2,1)} custom-call(bf16[2048,1536]{1,0:T(8,128)(2,1)} %ffn.2.refs_16_.refs_17_.refs_0_, bf16[2048,1536]{1,0:T(8,128)(2,1)} %ffn.3.refs_0_.refs_16_.refs_17_.refs_1_, bf16[2048,1536]{1,0:T(8,128)(2,1)} %all-gather.3.cloned.1.call-done.refs_16_.refs_1_.refs_2_, ...), custom_call_target="tpu_custom_call" | custom-call | flops 7000000000 | bytes 1 | tf_op jit(solution)/shard_map/back/pallas_call | solution.py:275
  408.2 7.3 %collective-permute-done.32.refs_1_ = bf16[256,2048]{1,0:T(8,128)(2,1)S(1)} collective-permute-done((bf16[256,2048]{1,0:T(8,128)(2,1)}, bf16[256,2048]{1,0:T(8,128)(2,1)S(1)}, u32[]{:S(2)}, u32[]{:S(2)}) %collective-permute-start.32) | collective-permute-done | bytes 1048608 | tf_op jit(solution)/shard_map/ppermute | solution.py:54
  417.3 4.8 collective-permute-done.34
  422.2 5.1 broadcast_select_fusion
  427.3 3.7 collective-permute-done.38.refs_3_
  436.4 9.6 %front.1.d_ref = bf16[2048,256]{1,0:T(8,128)(2,1)} custom-call(bf16[256,2048]{1,0:T(8,128)(2,1)} %norm_back.2.refs_0_.refs_5_, bf16[256,2048]{1,0:T(8,128)(2,1)} %copy-done.20, bf16[256,2048]{1,0:T(8,128)(2,1)} %copy-done.21, bf16[256,2048]{1,0:T(8,128)(2,1)} %collective-permute-done.38.refs_3_, bf16[256,2048]{1,0:T(8,128)(2,1)} %collective-permute-done.39.refs_4_, ...), custom_call_target="tpu_custom_call" | custom-call | flops 1 | bytes 1 | tf_op jit(solution)/shard_map/front/pallas_call | solution.py:301
  446.0 35.2 %attend_back.1.refs_0_.refs_1_.refs_10_ = bf16[2048,384]{1,0:T(8,128)(2,1)} custom-call(s32[8]{0:T(128)} %select_reduce_fusion.2.place, s32[8]{0:T(128)} %and_select_fusion.2.first, bf16[2048,2432]{1,0:T(8,128)(2,1)} %qkv.1.q_ref.kv_ref.refs_8_, bf16[2048,256]{1,0:T(8,128)(2,1)} %front.1.d_ref, f32[2048,384]{1,0:T(8,128)} %attend.1.refs_0_.h_ref.refs_9_, ...), custom_call_target="tpu_custom_call" | custom-call | flops 1 | bytes 1 | tf_op jit(solution)/shard_map/attend_back/pallas_call | solution.py:479
  484.4 4.2 back.23
  488.7 4.2 back.22
  493.7 5.6 back.21
  502.9 12.6 %weight_grads.5 = bf16[2048,640]{1,0:T(8,128)(2,1)} custom-call(bf16[256,2048]{1,0:T(8,128)(2,1)} %norm_back.2.refs_0_.refs_5_, bf16[256,2048]{1,0:T(8,128)(2,1)} %copy-done.20, bf16[256,2048]{1,0:T(8,128)(2,1)} %copy-done.21, bf16[256,2048]{1,0:T(8,128)(2,1)} %collective-permute-done.38.refs_3_, bf16[256,2048]{1,0:T(8,128)(2,1)} %collective-permute-done.39.refs_4_, ...), custom_call_target="tpu_custom_call" | custom-call | flops 1 | bytes 1 | tf_op jit(solution)/shard_map/weight_grads/pallas_call | solution.py:240
  515.5 4.0 collective-permute-done.47
  523.3 4.1 fusion.4
  531.0 17.6 %collective-permute-done.50 = bf16[256,2048]{1,0:T(8,128)(2,1)} collective-permute-done((bf16[256,2048]{1,0:T(8,128)(2,1)}, bf16[256,2048]{1,0:T(8,128)(2,1)}, u32[]{:S(2)}, u32[]{:S(2)}) %collective-permute-start.50) | collective-permute-done | bytes 1048608 | tf_op jit(solution)/shard_map/ppermute | solution.py:46
  550.8 9.5 %collective-permute-done.53 = bf16[512,1536]{1,0:T(8,128)(2,1)S(1)} collective-permute-done((bf16[512,1536]{1,0:T(8,128)(2,1)}, bf16[512,1536]{1,0:T(8,128)(2,1)S(1)}, u32[]{:S(2)}, u32[]{:S(2)}) %collective-permute-start.53) | collective-permute-done | bytes 1572896 | tf_op jit(solution)/shard_map/ppermute | solution.py:50
  575.6 7.2 %collective-permute-done.49.refs_2_ = bf16[256,2048]{1,0:T(8,128)(2,1)S(1)} collective-permute-done((bf16[256,2048]{1,0:T(8,128)(2,1)S(1)}, bf16[256,2048]{1,0:T(8,128)(2,1)S(1)}, u32[]{:S(2)}, u32[]{:S(2)}) %collective-permute-start.49) | collective-permute-done | bytes 1048608 | tf_op jit(solution)/shard_map/ppermute | solution.py:54
  584.8 4.8 norm_back.3
  596.8 18.3 %collective-permute-done.56 = f32[2,512]{1,0:T(2,128)S(1)} collective-permute-done((f32[2,512]{1,0:T(2,128)S(1)}, f32[2,512]{1,0:T(2,128)S(1)}, u32[]{:S(2)}, u32[]{:S(2)}) %collective-permute-start.56) | collective-permute-done | bytes 4128 | tf_op jit(solution)/shard_map/ppermute | solution.py:46
  (321 shorter events, 131.4 us)
Async XLA Ops:
  7.2 182.7 %all-gather.3.cloned.1.call-start = ((), (), s32[]{:S(2)}) async-start(), calls=%async_computation.3 | async-start | bytes 7864320 | tf_op jit(solution)/shard_map/all_gather | solution.py:703
  11.7 20.3 %collective-permute-start = (bf16[528,640]{1,0:T(8,128)(2,1)S(1)}, bf16[528,640]{1,0:T(8,128)(2,1)}, u32[]{:S(2)}, u32[]{:S(2)}) collective-permute-start(bf16[528,640]{1,0:T(8,128)(2,1)S(1)} %fusion.6), channel_id=1, source_target_pairs={{0,8},{8,16},{16,24},{24,0},{1,9},{9,17},{17,25},{25,1},{2,10},{10... | collective-permute-start | bytes 2027528 | tf_op jit(solution)/shard_map/ppermute | solution.py:558
  16.0 16.0 %collective-permute-start.1 = (bf16[256,2048]{1,0:T(8,128)(2,1)S(1)}, bf16[256,2048]{1,0:T(8,128)(2,1)}, u32[]{:S(2)}, u32[]{:S(2)}) collective-permute-start(bf16[256,2048]{1,0:T(8,128)(2,1)S(1)} %constant_dynamic-slice_fusion.11.refs_0_.refs_3_), channel_id=1, source_target_pairs={{0,4},{1,3},{2,6},{3,1},{4,0},{5,7},{6,2},{7,5},{8,12},{9,11},{10,... | collective-permute-start | bytes 3145736 | tf_op jit(solution)/shard_map/ppermute | solution.py:54
  32.0 18.5 %collective-permute-start.2 = (bf16[528,640]{1,0:T(8,128)(2,1)}, bf16[528,640]{1,0:T(8,128)(2,1)}, u32[]{:S(2)}, u32[]{:S(2)}) collective-permute-start(bf16[528,640]{1,0:T(8,128)(2,1)} %collective-permute-done), channel_id=1, source_target_pairs={{0,8},{8,16},{16,24},{24,0},{1,9},{9,17},{17,25},{25,1},{2,10},{10... | collective-permute-start | bytes 2027528 | tf_op jit(solution)/shard_map/ppermute | solution.py:558
  32.5 23.8 %collective-permute-start.4 = (bf16[256,2048]{1,0:T(8,128)(2,1)S(1)}, bf16[256,2048]{1,0:T(8,128)(2,1)}, u32[]{:S(2)}, u32[]{:S(2)}) collective-permute-start(bf16[256,2048]{1,0:T(8,128)(2,1)S(1)} %constant_dynamic-slice_fusion.11.refs_0_.refs_3_), channel_id=1, source_target_pairs={{0,2},{1,5},{2,0},{3,7},{4,6},{5,1},{6,4},{7,3},{8,10},{9,13},{10,... | collective-permute-start | bytes 3145736 | tf_op jit(solution)/shard_map/ppermute | solution.py:58
  34.1 24.6 %collective-permute-start.5 = (bf16[256,2048]{1,0:T(8,128)(2,1)}, bf16[256,2048]{1,0:T(8,128)(2,1)}, u32[]{:S(2)}, u32[]{:S(2)}) collective-permute-start(bf16[256,2048]{1,0:T(8,128)(2,1)} %collective-permute-done.1.refs_1_), channel_id=1, source_target_pairs={{0,2},{1,5},{2,0},{3,7},{4,6},{5,1},{6,4},{7,3},{8,10},{9,13},{10,... | collective-permute-start | bytes 3145736 | tf_op jit(solution)/shard_map/ppermute | solution.py:58
  50.5 17.6 %collective-permute-start.3 = (bf16[528,640]{1,0:T(8,128)(2,1)}, bf16[528,640]{1,0:T(8,128)(2,1)}, u32[]{:S(2)}, u32[]{:S(2)}) collective-permute-start(bf16[528,640]{1,0:T(8,128)(2,1)} %collective-permute-done.2), channel_id=1, source_target_pairs={{0,8},{8,16},{16,24},{24,0},{1,9},{9,17},{17,25},{25,1},{2,10},{10... | collective-permute-start | bytes 2027528 | tf_op jit(solution)/shard_map/ppermute | solution.py:558
  68.0 228.4 %all-gather.5.cloned.1.call-start = ((), (), s32[]{:S(2)}) async-start(), calls=%async_computation.4 | async-start | bytes 7864320 | tf_op jit(solution)/shard_map/all_gather | solution.py:703
  77.3 25.4 %collective-permute-start.10 = (bf16[256,2048]{1,0:T(8,128)(2,1)S(1)}, bf16[256,2048]{1,0:T(8,128)(2,1)S(1)}, u32[]{:S(2)}, u32[]{:S(2)}) collective-permute-start(bf16[256,2048]{1,0:T(8,128)(2,1)S(1)} %constant_dynamic-slice_fusion.6.refs_8_.refs_4_), channel_id=1, source_target_pairs={{0,4},{1,3},{2,6},{3,1},{4,0},{5,7},{6,2},{7,5},{8,12},{9,11},{10,... | collective-permute-start | bytes 3145736 | tf_op jit(solution)/shard_map/ppermute | solution.py:54
  78.6 24.2 %collective-permute-start.11 = (bf16[256,2048]{1,0:T(8,128)(2,1)S(1)}, bf16[256,2048]{1,0:T(8,128)(2,1)}, u32[]{:S(2)}, u32[]{:S(2)}) collective-permute-start(bf16[256,2048]{1,0:T(8,128)(2,1)S(1)} %constant_dynamic-slice_fusion.6.refs_8_.refs_4_), channel_id=1, source_target_pairs={{0,2},{1,5},{2,0},{3,7},{4,6},{5,1},{6,4},{7,3},{8,10},{9,13},{10,... | collective-permute-start | bytes 3145736 | tf_op jit(solution)/shard_map/ppermute | solution.py:58
  79.8 48.6 %collective-permute-start.13 = (bf16[256,2048]{1,0:T(8,128)(2,1)S(1)}, bf16[256,2048]{1,0:T(8,128)(2,1)}, u32[]{:S(2)}, u32[]{:S(2)}) collective-permute-start(bf16[256,2048]{1,0:T(8,128)(2,1)S(1)} %constant_dynamic-slice_fusion.6.refs_8_.refs_4_), channel_id=1, source_target_pairs={{0,1},{1,0},{2,3},{3,2},{4,5},{5,4},{6,7},{7,6},{8,9},{9,8},{10,11... | collective-permute-start | bytes 3145736 | tf_op jit(solution)/shard_map/ppermute | solution.py:42
  102.8 25.6 %collective-permute-start.12 = (bf16[256,2048]{1,0:T(8,128)(2,1)S(1)}, bf16[256,2048]{1,0:T(8,128)(2,1)}, u32[]{:S(2)}, u32[]{:S(2)}) collective-permute-start(bf16[256,2048]{1,0:T(8,128)(2,1)S(1)} %collective-permute-done.10.refs_9_), channel_id=1, source_target_pairs={{0,2},{1,5},{2,0},{3,7},{4,6},{5,1},{6,4},{7,3},{8,10},{9,13},{10,... | collective-permute-start | bytes 3145736 | tf_op jit(solution)/shard_map/ppermute | solution.py:58
  103.8 24.6 %collective-permute-start.14 = (bf16[256,2048]{1,0:T(8,128)(2,1)S(1)}, bf16[256,2048]{1,0:T(8,128)(2,1)}, u32[]{:S(2)}, u32[]{:S(2)}) collective-permute-start(bf16[256,2048]{1,0:T(8,128)(2,1)S(1)} %collective-permute-done.10.refs_9_), channel_id=1, source_target_pairs={{0,1},{1,0},{2,3},{3,2},{4,5},{5,4},{6,7},{7,6},{8,9},{9,8},{10,11... | collective-permute-start | bytes 3145736 | tf_op jit(solution)/shard_map/ppermute | solution.py:42
  104.2 24.2 %collective-permute-start.15 = (bf16[256,2048]{1,0:T(8,128)(2,1)}, bf16[256,2048]{1,0:T(8,128)(2,1)}, u32[]{:S(2)}, u32[]{:S(2)}) collective-permute-start(bf16[256,2048]{1,0:T(8,128)(2,1)} %collective-permute-done.11.refs_10_), channel_id=1, source_target_pairs={{0,1},{1,0},{2,3},{3,2},{4,5},{5,4},{6,7},{7,6},{8,9},{9,8},{10,11... | collective-permute-start | bytes 3145736 | tf_op jit(solution)/shard_map/ppermute | solution.py:42
  139.1 23.2 %collective-permute-start.17 = (bf16[512,2048]{1,0:T(8,128)(2,1)}, bf16[512,2048]{1,0:T(8,128)(2,1)S(1)}, u32[]{:S(2)}, u32[]{:S(2)}) collective-permute-start(bf16[512,2048]{1,0:T(8,128)(2,1)} %back.13), channel_id=1, source_target_pairs={{0,1},{1,0},{2,3},{3,2},{4,5},{5,4},{6,7},{7,6},{8,9},{9,8},{10,11... | collective-permute-start | bytes 6291464 | tf_op jit(solution)/shard_map/ppermute | solution.py:42
  140.6 290.4 %reduce-scatter.4.cloned.1.call-start = ((), (), s32[]{:S(2)}) async-start(), calls=%async_computation.5 | async-start | bytes 7864320 | tf_op jit(solution)/shard_map/reduce_scatter | solution.py:734
  147.5 14.9 %collective-permute-start.19 = (bf16[256,2048]{1,0:T(8,128)(2,1)S(1)}, bf16[256,2048]{1,0:T(8,128)(2,1)S(1)}, u32[]{:S(2)}, u32[]{:S(2)}) collective-permute-start(bf16[256,2048]{1,0:T(8,128)(2,1)S(1)} %get-tuple-element.152), channel_id=1, source_target_pairs={{0,2},{1,5},{2,0},{3,7},{4,6},{5,1},{6,4},{7,3},{8,10},{9,13},{10,... | collective-permute-start | bytes 3145736 | tf_op jit(solution)/shard_map/ppermute | solution.py:58
  163.7 26.1 %collective-permute-start.21 = (bf16[256,2048]{1,0:T(8,128)(2,1)S(1)}, bf16[256,2048]{1,0:T(8,128)(2,1)}, u32[]{:S(2)}, u32[]{:S(2)}) collective-permute-start(bf16[256,2048]{1,0:T(8,128)(2,1)S(1)} %fusion.5), channel_id=1, source_target_pairs={{0,4},{1,3},{2,6},{3,1},{4,0},{5,7},{6,2},{7,5},{8,12},{9,11},{10,... | collective-permute-start | bytes 3145736 | tf_op jit(solution)/shard_map/ppermute | solution.py:54
  165.2 24.6 %collective-permute-start.20 = (bf16[256,2048]{1,0:T(8,128)(2,1)S(1)}, bf16[256,2048]{1,0:T(8,128)(2,1)}, u32[]{:S(2)}, u32[]{:S(2)}) collective-permute-start(bf16[256,2048]{1,0:T(8,128)(2,1)S(1)} %get-tuple-element.91), channel_id=1, source_target_pairs={{0,2},{1,5},{2,0},{3,7},{4,6},{5,1},{6,4},{7,3},{8,10},{9,13},{10,... | collective-permute-start | bytes 3145736 | tf_op jit(solution)/shard_map/ppermute | solution.py:58
  193.4 25.2 %collective-permute-start.22 = (bf16[256,2048]{1,0:T(8,128)(2,1)S(1)}, bf16[256,2048]{1,0:T(8,128)(2,1)S(1)}, u32[]{:S(2)}, u32[]{:S(2)}) collective-permute-start(bf16[256,2048]{1,0:T(8,128)(2,1)S(1)} %multiply_convert_fusion.refs_0_), channel_id=1, source_target_pairs={{0,4},{1,3},{2,6},{3,1},{4,0},{5,7},{6,2},{7,5},{8,12},{9,11},{10,... | collective-permute-start | bytes 3145736 | tf_op jit(solution)/shard_map/ppermute | solution.py:54
  194.2 24.4 %collective-permute-start.23 = (bf16[256,2048]{1,0:T(8,128)(2,1)S(1)}, bf16[256,2048]{1,0:T(8,128)(2,1)S(1)}, u32[]{:S(2)}, u32[]{:S(2)}) collective-permute-start(bf16[256,2048]{1,0:T(8,128)(2,1)S(1)} %multiply_convert_fusion.refs_0_), channel_id=1, source_target_pairs={{0,2},{1,5},{2,0},{3,7},{4,6},{5,1},{6,4},{7,3},{8,10},{9,13},{10,... | collective-permute-start | bytes 3145736 | tf_op jit(solution)/shard_map/ppermute | solution.py:58
  195.4 25.3 %collective-permute-start.25 = (bf16[256,2048]{1,0:T(8,128)(2,1)S(1)}, bf16[256,2048]{1,0:T(8,128)(2,1)S(1)}, u32[]{:S(2)}, u32[]{:S(2)}) collective-permute-start(bf16[256,2048]{1,0:T(8,128)(2,1)S(1)} %multiply_convert_fusion.refs_0_), channel_id=1, source_target_pairs={{0,1},{1,0},{2,3},{3,2},{4,5},{5,4},{6,7},{7,6},{8,9},{9,8},{10,11... | collective-permute-start | bytes 3145736 | tf_op jit(solution)/shard_map/ppermute | solution.py:42
  218.6 14.9 %collective-permute-start.24 = (bf16[256,2048]{1,0:T(8,128)(2,1)S(1)}, bf16[256,2048]{1,0:T(8,128)(2,1)S(1)}, u32[]{:S(2)}, u32[]{:S(2)}) collective-permute-start(bf16[256,2048]{1,0:T(8,128)(2,1)S(1)} %collective-permute-done.22.refs_1_), channel_id=1, source_target_pairs={{0,2},{1,5},{2,0},{3,7},{4,6},{5,1},{6,4},{7,3},{8,10},{9,13},{10,... | collective-permute-start | bytes 3145736 | tf_op jit(solution)/shard_map/ppermute | solution.py:58
  278.4 244.3 %reduce-scatter.6.cloned.1.call-start = ((), (), s32[]{:S(2)}) async-start(), calls=%async_computation.6 | async-start | bytes 7864320 | tf_op jit(solution)/shard_map/reduce_scatter | solution.py:734
  340.5 26.2 %collective-permute-start.30 = (bf16[512,2048]{1,0:T(8,128)(2,1)S(1)}, bf16[512,2048]{1,0:T(8,128)(2,1)}, u32[]{:S(2)}, u32[]{:S(2)}) collective-permute-start(bf16[512,2048]{1,0:T(8,128)(2,1)S(1)} %slice_add_fusion), channel_id=1, source_target_pairs={{0,2},{1,5},{2,0},{3,7},{4,6},{5,1},{6,4},{7,3},{8,10},{9,13},{10,... | collective-permute-start | bytes 6291464 | tf_op jit(solution)/shard_map/ppermute | solution.py:58
  361.4 230.6 %reduce-scatter.8.cloned.1.call-start = ((), (), s32[]{:S(2)}) async-start(), calls=%async_computation.7 | async-start | bytes 3276800 | tf_op jit(solution)/shard_map/reduce_scatter | solution.py:796
  370.0 14.9 %collective-permute-start.31 = (bf16[256,2048]{1,0:T(8,128)(2,1)S(1)}, bf16[256,2048]{1,0:T(8,128)(2,1)S(1)}, u32[]{:S(2)}, u32[]{:S(2)}) collective-permute-start(bf16[256,2048]{1,0:T(8,128)(2,1)S(1)} %slice.217), channel_id=1, source_target_pairs={{0,4},{1,3},{2,6},{3,1},{4,0},{5,7},{6,2},{7,5},{8,12},{9,11},{10,... | collective-permute-start | bytes 3145736 | tf_op jit(solution)/shard_map/ppermute | solution.py:54
  377.9 39.5 %collective-permute-start.35 = (bf16[512,2048]{1,0:T(8,128)(2,1)}, bf16[512,2048]{1,0:T(8,128)(2,1)}, u32[]{:S(2)}, u32[]{:S(2)}) collective-permute-start(bf16[512,2048]{1,0:T(8,128)(2,1)} %back.18), channel_id=1, source_target_pairs={{0,1},{1,0},{2,3},{3,2},{4,5},{5,4},{6,7},{7,6},{8,9},{9,8},{10,11... | collective-permute-start | bytes 6291464 | tf_op jit(solution)/shard_map/ppermute | solution.py:42
  390.1 25.4 %collective-permute-start.32 = (bf16[256,2048]{1,0:T(8,128)(2,1)}, bf16[256,2048]{1,0:T(8,128)(2,1)S(1)}, u32[]{:S(2)}, u32[]{:S(2)}) collective-permute-start(bf16[256,2048]{1,0:T(8,128)(2,1)} %norm_back.2.refs_0_.refs_5_), channel_id=1, source_target_pairs={{0,4},{1,3},{2,6},{3,1},{4,0},{5,7},{6,2},{7,5},{8,12},{9,11},{10,... | collective-permute-start | bytes 3145736 | tf_op jit(solution)/shard_map/ppermute | solution.py:54
  391.7 23.8 %collective-permute-start.33 = (bf16[256,2048]{1,0:T(8,128)(2,1)}, bf16[256,2048]{1,0:T(8,128)(2,1)S(1)}, u32[]{:S(2)}, u32[]{:S(2)}) collective-permute-start(bf16[256,2048]{1,0:T(8,128)(2,1)} %norm_back.2.refs_0_.refs_5_), channel_id=1, source_target_pairs={{0,2},{1,5},{2,0},{3,7},{4,6},{5,1},{6,4},{7,3},{8,10},{9,13},{10,... | collective-permute-start | bytes 3145736 | tf_op jit(solution)/shard_map/ppermute | solution.py:58
  416.1 14.9 %collective-permute-start.38 = (bf16[256,2048]{1,0:T(8,128)(2,1)S(1)}, bf16[256,2048]{1,0:T(8,128)(2,1)}, u32[]{:S(2)}, u32[]{:S(2)}) collective-permute-start(bf16[256,2048]{1,0:T(8,128)(2,1)S(1)} %collective-permute-done.32.refs_1_), channel_id=1, source_target_pairs={{0,2},{1,5},{2,0},{3,7},{4,6},{5,1},{6,4},{7,3},{8,10},{9,13},{10,... | collective-permute-start | bytes 3145736 | tf_op jit(solution)/shard_map/ppermute | solution.py:58
  416.5 14.4 %collective-permute-start.40 = (bf16[256,2048]{1,0:T(8,128)(2,1)S(1)}, bf16[256,2048]{1,0:T(8,128)(2,1)}, u32[]{:S(2)}, u32[]{:S(2)}) collective-permute-start(bf16[256,2048]{1,0:T(8,128)(2,1)S(1)} %collective-permute-done.32.refs_1_), channel_id=1, source_target_pairs={{0,1},{1,0},{2,3},{3,2},{4,5},{5,4},{6,7},{7,6},{8,9},{9,8},{10,11... | collective-permute-start | bytes 3145736 | tf_op jit(solution)/shard_map/ppermute | solution.py:42
  431.0 50.2 %collective-permute-start.43 = (bf16[512,1536]{1,0:T(8,128)(2,1)}, bf16[512,1536]{1,0:T(8,128)(2,1)S(1)}, u32[]{:S(2)}, u32[]{:S(2)}) collective-permute-start(bf16[512,1536]{1,0:T(8,128)(2,1)} %reduce-scatter.4.cloned.1.call-done), channel_id=1, source_target_pairs={{0,4},{4,0},{1,5},{5,1},{2,6},{6,2},{3,7},{7,3},{8,12},{12,8},{9,1... | collective-permute-start | bytes 4718600 | tf_op jit(solution)/shard_map/ppermute | solution.py:50
  432.5 48.7 %collective-permute-start.36 = (bf16[256,2048]{1,0:T(8,128)(2,1)}, bf16[256,2048]{1,0:T(8,128)(2,1)S(1)}, u32[]{:S(2)}, u32[]{:S(2)}) collective-permute-start(bf16[256,2048]{1,0:T(8,128)(2,1)} %get-tuple-element.150), channel_id=1, source_target_pairs={{0,2},{2,0},{1,3},{3,1},{4,6},{6,4},{5,7},{7,5},{8,10},{10,8},{9,1... | collective-permute-start | bytes 3145736 | tf_op jit(solution)/shard_map/ppermute | solution.py:46
  433.1 48.1 %collective-permute-start.37 = (bf16[256,2048]{1,0:T(8,128)(2,1)}, bf16[256,2048]{1,0:T(8,128)(2,1)S(1)}, u32[]{:S(2)}, u32[]{:S(2)}) collective-permute-start(bf16[256,2048]{1,0:T(8,128)(2,1)} %get-tuple-element.143), channel_id=1, source_target_pairs={{0,2},{2,0},{1,3},{3,1},{4,6},{6,4},{5,7},{7,5},{8,10},{10,8},{9,1... | collective-permute-start | bytes 3145736 | tf_op jit(solution)/shard_map/ppermute | solution.py:46
  492.8 30.5 %collective-permute-start.44 = (bf16[512,2048]{1,0:T(8,128)(2,1)}, bf16[512,2048]{1,0:T(8,128)(2,1)}, u32[]{:S(2)}, u32[]{:S(2)}) collective-permute-start(bf16[512,2048]{1,0:T(8,128)(2,1)} %back.22), channel_id=1, source_target_pairs={{0,1},{1,0},{2,3},{3,2},{4,5},{5,4},{6,7},{7,6},{8,9},{9,8},{10,11... | collective-permute-start | bytes 6291464 | tf_op jit(solution)/shard_map/ppermute | solution.py:42
  493.2 26.3 %collective-permute-start.47 = (bf16[256,2048]{1,0:T(8,128)(2,1)}, bf16[256,2048]{1,0:T(8,128)(2,1)}, u32[]{:S(2)}, u32[]{:S(2)}) collective-permute-start(bf16[256,2048]{1,0:T(8,128)(2,1)} %add.380), channel_id=1, source_target_pairs={{0,4},{4,0},{1,5},{5,1},{2,6},{6,2},{3,7},{7,3},{8,12},{12,8},{9,1... | collective-permute-start | bytes 3145736 | tf_op jit(solution)/shard_map/ppermute | solution.py:50
  502.4 20.9 %collective-permute-start.46 = (bf16[256,2048]{1,0:T(8,128)(2,1)}, bf16[256,2048]{1,0:T(8,128)(2,1)}, u32[]{:S(2)}, u32[]{:S(2)}) collective-permute-start(bf16[256,2048]{1,0:T(8,128)(2,1)} %get-tuple-element.146), channel_id=1, source_target_pairs={{0,2},{1,5},{2,0},{3,7},{4,6},{5,1},{6,4},{7,3},{8,10},{9,13},{10,... | collective-permute-start | bytes 3145736 | tf_op jit(solution)/shard_map/ppermute | solution.py:58
  522.2 26.4 %collective-permute-start.50 = (bf16[256,2048]{1,0:T(8,128)(2,1)}, bf16[256,2048]{1,0:T(8,128)(2,1)}, u32[]{:S(2)}, u32[]{:S(2)}) collective-permute-start(bf16[256,2048]{1,0:T(8,128)(2,1)} %add_convert_fusion), channel_id=1, source_target_pairs={{0,2},{2,0},{1,3},{3,1},{4,6},{6,4},{5,7},{7,5},{8,10},{10,8},{9,1... | collective-permute-start | bytes 3145736 | tf_op jit(solution)/shard_map/ppermute | solution.py:46
  522.6 46.1 %collective-permute-start.51 = (bf16[256,2048]{1,0:T(8,128)(2,1)}, bf16[256,2048]{1,0:T(8,128)(2,1)}, u32[]{:S(2)}, u32[]{:S(2)}) collective-permute-start(bf16[256,2048]{1,0:T(8,128)(2,1)} %add_convert_fusion), channel_id=1, source_target_pairs={{0,1},{1,0},{2,3},{3,2},{4,5},{5,4},{6,7},{7,6},{8,9},{9,8},{10,11... | collective-permute-start | bytes 3145736 | tf_op jit(solution)/shard_map/ppermute | solution.py:42
  522.7 37.6 %collective-permute-start.53 = (bf16[512,1536]{1,0:T(8,128)(2,1)}, bf16[512,1536]{1,0:T(8,128)(2,1)S(1)}, u32[]{:S(2)}, u32[]{:S(2)}) collective-permute-start(bf16[512,1536]{1,0:T(8,128)(2,1)} %reduce-scatter.6.cloned.1.call-done), channel_id=1, source_target_pairs={{0,4},{4,0},{1,5},{5,1},{2,6},{6,2},{3,7},{7,3},{8,12},{12,8},{9,1... | collective-permute-start | bytes 4718600 | tf_op jit(solution)/shard_map/ppermute | solution.py:50
  527.5 55.3 %collective-permute-start.49 = (bf16[256,2048]{1,0:T(8,128)(2,1)S(1)}, bf16[256,2048]{1,0:T(8,128)(2,1)S(1)}, u32[]{:S(2)}, u32[]{:S(2)}) collective-permute-start(bf16[256,2048]{1,0:T(8,128)(2,1)S(1)} %get-tuple-element.121), channel_id=1, source_target_pairs={{0,4},{1,3},{2,6},{3,1},{4,0},{5,7},{6,2},{7,5},{8,12},{9,11},{10,... | collective-permute-start | bytes 3145736 | tf_op jit(solution)/shard_map/ppermute | solution.py:54
  528.6 54.2 %collective-permute-start.48 = (bf16[256,2048]{1,0:T(8,128)(2,1)S(1)}, bf16[256,2048]{1,0:T(8,128)(2,1)S(1)}, u32[]{:S(2)}, u32[]{:S(2)}) collective-permute-start(bf16[256,2048]{1,0:T(8,128)(2,1)S(1)} %copy-done.48), channel_id=1, source_target_pairs={{0,2},{1,5},{2,0},{3,7},{4,6},{5,1},{6,4},{7,3},{8,10},{9,13},{10,... | collective-permute-start | bytes 3145736 | tf_op jit(solution)/shard_map/ppermute | solution.py:58
  550.3 18.4 %collective-permute-start.52 = (bf16[256,2048]{1,0:T(8,128)(2,1)}, bf16[256,2048]{1,0:T(8,128)(2,1)S(1)}, u32[]{:S(2)}, u32[]{:S(2)}) collective-permute-start(bf16[256,2048]{1,0:T(8,128)(2,1)} %collective-permute-done.50), channel_id=1, source_target_pairs={{0,1},{1,0},{2,3},{3,2},{4,5},{5,4},{6,7},{7,6},{8,9},{9,8},{10,11... | collective-permute-start | bytes 3145736 | tf_op jit(solution)/shard_map/ppermute | solution.py:42
  589.6 25.5 %collective-permute-start.54 = (bf16[256,2048]{1,0:T(8,128)(2,1)}, bf16[256,2048]{1,0:T(8,128)(2,1)}, u32[]{:S(2)}, u32[]{:S(2)}) collective-permute-start(bf16[256,2048]{1,0:T(8,128)(2,1)} %norm_back.3), channel_id=1, source_target_pairs={{0,2},{2,0},{1,3},{3,1},{4,6},{6,4},{5,7},{7,5},{8,10},{10,8},{9,1... | collective-permute-start | bytes 3145736 | tf_op jit(solution)/shard_map/ppermute | solution.py:46
  592.0 23.1 %collective-permute-start.57 = (bf16[512,640]{1,0:T(8,128)(2,1)}, bf16[512,640]{1,0:T(8,128)(2,1)S(1)}, u32[]{:S(2)}, u32[]{:S(2)}) collective-permute-start(bf16[512,640]{1,0:T(8,128)(2,1)} %reduce-scatter.8.cloned.1.call-done), channel_id=1, source_target_pairs={{0,4},{4,0},{1,5},{5,1},{2,6},{6,2},{3,7},{7,3},{8,12},{12,8},{9,1... | collective-permute-start | bytes 1966088 | tf_op jit(solution)/shard_map/ppermute | solution.py:50
  595.6 19.5 %collective-permute-start.56 = (f32[2,512]{1,0:T(2,128)S(1)}, f32[2,512]{1,0:T(2,128)S(1)}, u32[]{:S(2)}, u32[]{:S(2)}) collective-permute-start(f32[2,512]{1,0:T(2,128)S(1)} %fusion.18), channel_id=1, source_target_pairs={{0,2},{2,0},{1,3},{3,1},{4,6},{6,4},{5,7},{7,5},{8,10},{10,8},{9,1... | collective-permute-start | bytes 12296 | tf_op jit(solution)/shard_map/ppermute | solution.py:46
  596.7 27.8 %collective-permute-start.58 = (bf16[256,2048]{1,0:T(8,128)(2,1)S(1)}, bf16[256,2048]{1,0:T(8,128)(2,1)S(1)}, u32[]{:S(2)}, u32[]{:S(2)}) collective-permute-start(bf16[256,2048]{1,0:T(8,128)(2,1)S(1)} %copy-done.34), channel_id=1, source_target_pairs={{0,1},{1,0},{2,3},{3,2},{4,5},{5,4},{6,7},{7,6},{8,9},{9,8},{10,11... | collective-permute-start | bytes 3145736 | tf_op jit(solution)/shard_map/ppermute | solution.py:42
  (76 other events, 1069.3 us)
Sparse Core Ops, SparseCore 0:
  68.2 113.0 all-gather.2
  182.8 113.5 all-gather.4
  298.8 108.9 reduce-scatter.3
  409.9 111.2 reduce-scatter.5
  524.0 52.6 reduce-scatter.7
